TPU v7x, 256 devices: a whole 4x4x8 slice. The times are simulated.
256 devices in a mesh: dp: 8 (over x, core), expert: 4 (over z_hi), shard: 8 (over y, z_lo).
Axes of the slice: x: 4, y: 4, z: 8 (z_hi: 4, z_lo: 2; z = z_hi * 2 + z_lo), core: 2. Of those that a mesh axis runs over, the one named last changes fastest.
Arguments:
- tokens: bfloat16 [4096, 4096], P(('dp', 'expert'), 'shard'), may hold values from -6 to 6
- expert_ids: int32 [4096, 2], P(('dp', 'expert')), may hold values from 0 to 3, all different within a row; in each aligned block of 128 rows (0 to 127, 128 to 255, ...) at most 80 rows name the same one
- gate_probs: float32 [4096, 2], P(('dp', 'expert')), may hold values from 0.1 to 1
- stacked_weights: bfloat16 [4, 3, 1536, 4096], P('expert', None, 'shard', 'dp'), may hold values from -0.09375 to 0.09375
- out_grad: bfloat16 [4096, 4096], P(('dp', 'expert'), 'shard'), may hold values from -6 to 6
Outputs:
- layer_output: bfloat16 [4096, 4096], P(('dp', 'expert'), 'shard')
- token_grad: bfloat16 [4096, 4096], P(('dp', 'expert'), 'shard')
- prob_grad: float32 [4096, 2], P(('dp', 'expert'))
- weight_grad: float32 [4, 3, 1536, 4096], P('expert', None, 'shard', 'dp')
Inputs may be any that keep to these rules, and one draw needn't show every extreme that they name: `expert_ids`: within each aligned block of 128 rows (the tokens of one index of dp and expert) no expert is named by more than 80 rows, a bound that some block reaches; the 2 ids of a row differ.
All inputs are finite; a program needn't handle non-finite values.
Results may differ from a plain program's by a relative error of at most 0.0065.
Values may be sent and summed in bfloat16 or wider, within the bound.
No kernel may reach another device: no remote copies, remote signals or barrier semaphores. Data moves between devices by JAX's collectives and lax.ppermute only.
A program may use at most 128 MiB of HBM per device.

v0:
```python
import jax
import jax.numpy as jnp
from jax import lax
from jax.experimental import pallas as pl
from jax.experimental.pallas import tpu as pltpu
from jax.sharding import Mesh, PartitionSpec as P

F32 = jnp.float32
BF16 = jnp.bfloat16
CAP = 80
TILE = 16
PARAMS = pltpu.CompilerParams(vmem_limit_bytes=48 * 1024 * 1024)


def nn(a, b):
    return lax.dot_general(a, b, (((1,), (0,)), ((), ())), preferred_element_type=F32)


def nt(a, b):
    return lax.dot_general(a, b, (((1,), (1,)), ((), ())), preferred_element_type=F32)


def tn(a, b):
    return lax.dot_general(a, b, (((0,), (0,)), ((), ())), preferred_element_type=F32)


def call(kernel, place, args, outs, scratch=(), spaces=None):
    whole = pl.BlockSpec(memory_space=pltpu.VMEM)
    return pl.pallas_call(
        kernel,
        out_shape=[jax.ShapeDtypeStruct(shape, kind) for shape, kind in outs],
        in_specs=[pl.BlockSpec(memory_space=pltpu.SMEM)] + (spaces or [whole] * len(args)),
        out_specs=[whole] * len(outs),
        scratch_shapes=list(scratch),
        compiler_params=PARAMS,
    )(place, *args)


def expert_rows(place, ids, k):
    expert = lax.rem(place[0] + k, 4)
    return ids[0:1, :] == expert, ids[1:2, :] == expert


def slots_kernel(place, ids, probs, tokens, grads, placing, *refs):
    outs, token_copy, grad_copy, sems = refs[0:4], refs[4], refs[5], refs[6]
    first = pltpu.make_async_copy(tokens, token_copy, sems.at[0])
    second = pltpu.make_async_copy(grads, grad_copy, sems.at[1])
    first.start()
    second.start()
    rows = ids.shape[1]
    before = (
        lax.broadcasted_iota(jnp.int32, (rows, rows), 0)
        < lax.broadcasted_iota(jnp.int32, (rows, rows), 1)
    ).astype(BF16)
    slot = lax.broadcasted_iota(jnp.int32, (CAP, rows), 0)
    scales = []
    for k in range(4):
        one, two = expert_rows(place, ids, k)
        named = jnp.logical_or(one, two)
        marks = jnp.broadcast_to(named, (8, rows)).astype(F32)
        position = nn(marks.astype(BF16), before)[0:1, :].astype(jnp.int32)
        weight = jnp.where(one, probs[0:1, :], probs[1:2, :])
        chosen = jnp.logical_and(
            jnp.broadcast_to(marks[0:1, :] > 0.5, (CAP, rows)),
            slot == jnp.broadcast_to(position, (CAP, rows)),
        )
        placing[k * CAP : (k + 1) * CAP, :] = chosen.astype(F32).astype(BF16)
        scales.append(jnp.sum(jnp.where(chosen, weight, 0.0), axis=1, keepdims=True))
    first.wait()
    second.wait()
    for k in range(4):
        hot = placing[k * CAP : (k + 1) * CAP, :]
        outs[k][0:CAP, :] = nn(hot, token_copy[...]).astype(BF16)
        outs[k][CAP : 2 * CAP, :] = (scales[k] * nn(hot, grad_copy[...])).astype(BF16)


def split_halves(total, keep, send, zl):
    part = keep.shape[-2]
    mine = pl.multiple_of(zl * part, 32)
    theirs = pl.multiple_of((1 - zl) * part, 32)
    for n in range(keep.shape[0]):
        keep[n] = total[n, pl.ds(mine, part), :]
        send[n] = total[n, pl.ds(theirs, part), :].astype(BF16)


def fetch(weights, joined, sems, names):
    half = weights.shape[3]
    copies = [
        pltpu.make_async_copy(
            weights.at[block, c, m],
            joined.at[n, block, pl.ds(c * half, half)],
            sems.at[n, block, c],
        )
        for n, m in enumerate(names)
        for block in range(4)
        for c in range(2)
    ]
    for copy in copies:
        copy.start()
    return copies


def project(rows, weights, y, total, joined, sems, names):
    for copy in fetch(weights, joined, sems, names):
        copy.wait()
    for n in range(len(names)):
        for j in range(4):
            share = nt(rows[j][...], joined[n, lax.rem(y - j + 4, 4)])
            total[n] = share if j == 0 else total[n] + share


def gate_up_kernel(place, *refs):
    rows, weights, keep, send, total, joined, sems = refs[0:4], *refs[4:10]
    project(rows, weights, place[2], total, joined, sems, (0, 1))
    split_halves(total, keep, send, place[3])


def back_kernel(place, *refs):
    rows, weights, keep, send, total, joined, sems = refs[0:4], *refs[4:10]
    project(rows, weights, place[2], total, joined, sems, (2,))
    split_halves(total, keep, send, place[3])


def pieces(values):
    high = values.astype(BF16)
    rest = values - high.astype(F32)
    middle = rest.astype(BF16)
    low = (rest - middle.astype(F32)).astype(BF16)
    return high, middle, low


def marked_rows(row):
    spot = lax.broadcasted_iota(jnp.int32, (TILE, row.shape[1]), 0)
    parts = [part.astype(F32) for part in pieces(row)]
    total = jnp.where(spot == 0, parts[0], 0.0)
    total += jnp.where(spot == 1, parts[1], 0.0)
    return (total + jnp.where(spot == 2, parts[2], 0.0)).astype(BF16)


def hidden_kernel(place, both, act, keep, far, out):
    gate, up = both[0], both[1]
    sigmoid = 1.0 / (1.0 + jnp.exp(-gate))
    swish = gate * sigmoid
    grad = keep[0] + far[0].astype(F32)
    part = grad.shape[0]
    out[0:part, :] = (grad * up * sigmoid * (1.0 + gate * (1.0 - sigmoid))).astype(BF16)
    out[part : 2 * part, :] = (grad * swish).astype(BF16)
    share = jnp.sum(act[0].astype(F32) * grad, axis=1, keepdims=True)
    out[2 * part :, :] = jnp.zeros((2 * TILE, out.shape[1]), BF16)
    shape = (CAP, 128)
    same = lax.broadcasted_iota(jnp.int32, shape, 0) == lax.broadcasted_iota(jnp.int32, shape, 1)
    for n in range(2):
        row = jnp.sum(
            jnp.where(same, share[n * CAP : (n + 1) * CAP, :], 0.0), axis=0, keepdims=True
        )
        out[2 * part + n * TILE : 2 * part + (n + 1) * TILE, 0:128] = marked_rows(row)


def join(target, mine, theirs, zl):
    part = mine.shape[-2]
    target[pl.ds(pl.multiple_of(zl * part, 32), part), :] = mine[...]
    target[pl.ds(pl.multiple_of((1 - zl) * part, 32), part), :] = theirs[...]


def join_hidden(joined, act, act_far, grad, grad_far, zl):
    part = act.shape[1]
    join(joined.at[2], act.at[0], act_far.at[0], zl)
    for n in range(2):
        span = pl.ds(n * part, part)
        join(joined.at[n], grad.at[span], grad_far.at[span], zl)


def share_kernel(place, act, act_far, grad, grad_far, weights, *refs):
    outs, joined, blocks, marks, sems = refs[0:4], *refs[4:8]
    copies = fetch(weights, blocks, sems, (2, 0, 1))
    part = act.shape[1]
    join_hidden(joined, act, act_far, grad, grad_far, place[3])
    marks[place[3]] = grad[2 * part :, 0:128]
    marks[1 - place[3]] = grad_far[2 * part :, 0:128]
    unit = 2 * CAP + TILE
    for n in range(3):
        for copy in copies[8 * n : 8 * n + 8]:
            copy.wait()
        if n == 1:
            continue
        for j in range(4):
            spot = lax.rem(place[2] - j + 4, 4)
            kind = outs[j].dtype
            if n == 0:
                acc = nn(joined[2], blocks[0, spot])
            else:
                acc = nn(joined[0], blocks[1, spot]) + nn(joined[1], blocks[2, spot])
            first = 0 if n == 0 else CAP
            for k in range(4):
                start = k * unit + first
                outs[j][start : start + CAP, :] = acc[k * CAP : (k + 1) * CAP, :].astype(kind)
    for j in range(4):
        for k in range(4):
            start = k * unit + 2 * CAP
            kind = outs[j].dtype
            rows = marks[k // 2, (k % 2) * TILE : (k % 2 + 1) * TILE, :]
            outs[j][start : start + TILE, :] = jnp.zeros((TILE, outs[j].shape[1]), kind)
            outs[j][start : start + TILE, 0:128] = rows.astype(kind)


def total_kernel(place, own, one, three, two, *outs):
    unit = 2 * CAP + TILE
    for k in range(4):
        span = pl.ds(k * unit, unit)
        total = own[span, :] + one[span, :].astype(F32)
        total += three[span, :].astype(F32) + two[span, :].astype(F32)
        outs[k][...] = total.astype(BF16)
        row = jnp.sum(total[2 * CAP :, 0:128], axis=0, keepdims=True)
        outs[k][2 * CAP :, 0:128] = marked_rows(row)


def weight_kernel(place, after, *refs):
    act, act_far, grad, grad_far = refs[0:4]
    rows, routed = refs[4:8], refs[8:12]
    out, joined, turned = refs[12:15]
    y, zl = place[2], place[3]
    half = out.shape[3]
    join_hidden(joined, act, act_far, grad, grad_far, zl)
    for j in range(4):
        spot = lax.rem(y - j + 4, 4)
        turned[0, spot] = rows[j][...]
        turned[1, spot] = routed[j][...]
    for i in range(4):
        for m in range(3):
            total = tn(joined[m], turned[1 if m == 2 else 0, i])
            for c in range(2):
                out[i, c, m] = total[c * half : (c + 1) * half, :].astype(BF16)


def column(row):
    rows = row.shape[1]
    shape = (rows, rows)
    same = lax.broadcasted_iota(jnp.int32, shape, 0) == lax.broadcasted_iota(jnp.int32, shape, 1)
    return jnp.sum(jnp.where(same, row, 0.0), axis=1, keepdims=True)


def owner_kernel(place, ids, probs, placing, *refs):
    blocks, layer, token, prob = refs[0:4], *refs[4:7]
    total = jnp.zeros(layer.shape, F32)
    grads = jnp.zeros(token.shape, F32)
    shares = [jnp.zeros((1, ids.shape[1]), F32) for _ in range(2)]
    for k in range(4):
        one, two = expert_rows(place, ids, k)
        hot = placing[k * CAP : (k + 1) * CAP, :]
        weight = jnp.where(one, probs[0:1, :], 0.0) + jnp.where(two, probs[1:2, :], 0.0)
        total += column(weight) * tn(hot, blocks[k][0:CAP, :])
        grads += tn(hot, blocks[k][CAP : 2 * CAP, :])
        found = nn(blocks[k][2 * CAP :, 0:128][:, 0:CAP], hot)
        share = jnp.sum(found, axis=0, keepdims=True)
        shares[0] += jnp.where(one, share, 0.0)
        shares[1] += jnp.where(two, share, 0.0)
    layer[...] = total.astype(BF16)
    token[...] = grads.astype(BF16)
    prob[...] = jnp.zeros(prob.shape, F32)
    for n in range(2):
        prob[n : n + 1, :] = shares[n] / probs[n : n + 1, :]


def shift(value, axis, step):
    return lax.ppermute(value, axis, [(i, (i + step) % 4) for i in range(4)])


def swap(value, axis):
    return lax.ppermute(value, axis, [(0, 1), (1, 0)])


def turn(value):
    return lax.ppermute(value, ("core", "zl"), [(2 * c + z, 2 * z + c) for c in range(2) for z in range(2)])


def body(tokens, expert_ids, gate_probs, stacked_weights, out_grad):
    rows, width = tokens.shape
    half = stacked_weights.shape[2]
    hidden = 2 * half
    slots = 4 * CAP
    part = slots // 2
    place = jnp.stack(
        [lax.axis_index(name) for name in ("expert", "x", "y", "zl")]
    ).astype(jnp.int32)
    ids, probs = expert_ids.T, gate_probs.T
    vmem = pl.BlockSpec(memory_space=pltpu.VMEM)
    hbm = pl.BlockSpec(memory_space=pl.ANY)

    weights = lax.all_gather(turn(stacked_weights[0]), ("x", "core"), axis=0, tiled=False)
    weights = weights.reshape(4, 2, 3, half, width)

    placing, *blocks = call(
        slots_kernel,
        place,
        [ids, probs, tokens, out_grad],
        [((slots, rows), BF16)] + [((2 * CAP, width), BF16)] * 4,
        [pltpu.VMEM((rows, width), BF16)] * 2 + [pltpu.SemaphoreType.DMA((2,))],
        [vmem, vmem, hbm, hbm],
    )
    blocks = [blocks[0]] + [shift(blocks[k], "expert", k) for k in (1, 2, 3)]
    token_rows = jnp.concatenate([block[:CAP] for block in blocks], axis=0)
    routed_rows = jnp.concatenate([block[CAP:] for block in blocks], axis=0)
    token_rows = [token_rows] + [shift(token_rows, "y", j) for j in (1, 3, 2)]
    routed_rows = [routed_rows] + [shift(routed_rows, "y", j) for j in (1, 3, 2)]
    token_rows[2:] = token_rows[:1:-1]
    routed_rows[2:] = routed_rows[:1:-1]

    def project_call(kernel, blocks, count):
        return call(
            kernel,
            place,
            blocks + [weights],
            [((count, part, hidden), F32), ((count, part, hidden), BF16)],
            [
                pltpu.VMEM((count, slots, hidden), F32),
                pltpu.VMEM((count, 4, hidden, width), BF16),
                pltpu.SemaphoreType.DMA((count, 4, 2)),
            ],
            [vmem] * 4 + [hbm],
        )

    keep, send = project_call(gate_up_kernel, token_rows, 2)
    both = keep + swap(send, "zl").astype(F32)
    gate, up = both[0:1], both[1:2]
    activation = (gate * jax.nn.sigmoid(gate) * up).astype(BF16)
    activation_far = swap(activation, "zl")
    keep, send = project_call(back_kernel, routed_rows, 1)
    hidden_grad = call(
        hidden_kernel,
        place,
        [both, activation, keep, swap(send, "zl")],
        [((2 * part + 2 * TILE, hidden), BF16)],
    )[0]
    pairs = [activation, activation_far, hidden_grad, swap(hidden_grad, "zl")]

    unit = 2 * CAP + TILE
    shares = call(
        share_kernel,
        place,
        pairs + [weights],
        [((4 * unit, width), F32)] + [((4 * unit, width), BF16)] * 3,
        [
            pltpu.VMEM((3, slots, hidden), BF16),
            pltpu.VMEM((3, 4, hidden, width), BF16),
            pltpu.VMEM((2, 2 * TILE, 128), BF16),
            pltpu.SemaphoreType.DMA((3, 4, 2)),
        ],
        [vmem] * 4 + [hbm],
    )
    arrived = [shift(shares[j], "y", -j) for j in (1, 3, 2)]
    terms = call(
        weight_kernel,
        place,
        [shares[3]] + pairs + token_rows + routed_rows,
        [((4, 2, 3, half, width), BF16)],
        [pltpu.VMEM((3, slots, hidden), BF16), pltpu.VMEM((2, 4, slots, width), BF16)],
        [hbm] + [vmem] * 12,
    )[0]
    weight_total = lax.psum_scatter(
        terms.reshape(8, 3, half, width), ("x", "core"), scatter_dimension=0, tiled=False
    )
    totals = call(total_kernel, place, [shares[0]] + arrived, [((unit, width), BF16)] * 4)
    returned = [totals[0]] + [shift(totals[k], "expert", -k) for k in (1, 2, 3)]
    weight_total, returned[1] = lax.optimization_barrier((weight_total, returned[1]))
    layer_output, token_grad, prob_grad = call(
        owner_kernel,
        place,
        [ids, probs, placing] + returned,
        [((rows, width), BF16), ((rows, width), BF16), ((8, rows), F32)],
    )
    weight_grad = turn(weight_total).astype(F32)[None]
    return layer_output, token_grad, prob_grad[0:2].T, weight_grad


def solution(mesh):
    split = Mesh(
        mesh.devices.reshape(4, 2, 4, 4, 2), ("x", "core", "expert", "y", "zl")
    )
    rows = P(("x", "core", "expert"), ("y", "zl"))
    pairs = P(("x", "core", "expert"), None)
    weights = P("expert", None, ("y", "zl"), ("x", "core"))
    return jax.shard_map(
        body,
        mesh=split,
        in_specs=(rows, pairs, pairs, weights, rows),
        out_specs=(rows, rows, pairs, weights),
        check_vma=False,
    )
```

profile of v0, /device:TPU:1, one launch (start us, length us, event | category | flops | bytes accessed | tf_op | source)
XLA Modules:
  0.0 187.0 jit_solution(11138201769370739646)
XLA Ops:
  7.2 4.9 %collective-permute-start.6 = (bf16[3,192,512]{2,1,0:T(8,128)(2,1)}, bf16[3,192,512]{2,1,0:T(8,128)(2,1)S(1)}, u32[]{:S(2)}, u32[]{:S(2)}) collective-permute-start(bf16[3,192,512]{2,1,0:T(8,128)(2,1)} %bitcast.23), channel_id=1, source_target_pairs={{0,0},{1,32},{32,1},{33,33},{2,2},{3,34},{34,3},{35,35},{4,4},{5,3... | collective-permute-start | bytes 1769480 | tf_op jit(solution)/shard_map/ppermute | solution.py:273
  12.2 7.8 %collective-permute-done.6 = bf16[3,192,512]{2,1,0:T(8,128)(2,1)S(1)} collective-permute-done((bf16[3,192,512]{2,1,0:T(8,128)(2,1)}, bf16[3,192,512]{2,1,0:T(8,128)(2,1)S(1)}, u32[]{:S(2)}, u32[]{:S(2)}) %collective-permute-start.6) | collective-permute-done | bytes 589856 | tf_op jit(solution)/shard_map/ppermute | solution.py:273
  19.9 0.8 copy-done.14
  20.9 0.9 copy-done.6
  21.8 0.9 copy-done.7
  22.7 0.7 copy-done.8
  23.4 0.7 copy-done.10
  24.1 1.5 shard_map.84
  25.5 3.4 %collective-permute-start = (bf16[160,512]{1,0:T(8,128)(2,1)S(1)}, bf16[160,512]{1,0:T(8,128)(2,1)S(1)}, u32[]{:S(2)}, u32[]{:S(2)}) collective-permute-start(bf16[160,512]{1,0:T(8,128)(2,1)S(1)} %get-tuple-element.28), channel_id=1, source_target_pairs={{0,8},{8,16},{16,24},{24,0},{1,9},{9,17},{17,25},{25,1},{2,10},{10... | collective-permute-start | bytes 491528 | tf_op jit(solution)/shard_map/ppermute | solution.py:265
  28.9 6.4 %collective-permute-start.1 = (bf16[160,512]{1,0:T(8,128)(2,1)S(1)}, bf16[160,512]{1,0:T(8,128)(2,1)S(1)}, u32[]{:S(2)}, u32[]{:S(2)}) collective-permute-start(bf16[160,512]{1,0:T(8,128)(2,1)S(1)} %get-tuple-element.29), channel_id=1, source_target_pairs={{0,16},{8,24},{16,0},{24,8},{1,17},{9,25},{17,1},{25,9},{2,18},{10... | collective-permute-start | bytes 491528 | tf_op jit(solution)/shard_map/ppermute | solution.py:265
  36.0 7.4 %collective-permute-done.1 = bf16[160,512]{1,0:T(8,128)(2,1)S(1)} collective-permute-done((bf16[160,512]{1,0:T(8,128)(2,1)S(1)}, bf16[160,512]{1,0:T(8,128)(2,1)S(1)}, u32[]{:S(2)}, u32[]{:S(2)}) %collective-permute-start.1) | collective-permute-done | bytes 163872 | tf_op jit(solution)/shard_map/ppermute | solution.py:265
  43.4 2.7 %collective-permute-done.2 = bf16[160,512]{1,0:T(8,128)(2,1)S(1)} collective-permute-done((bf16[160,512]{1,0:T(8,128)(2,1)S(1)}, bf16[160,512]{1,0:T(8,128)(2,1)S(1)}, u32[]{:S(2)}, u32[]{:S(2)}) %collective-permute-start.2) | collective-permute-done | bytes 163872 | tf_op jit(solution)/shard_map/ppermute | solution.py:265
  46.1 2.8 %collective-permute-start.5 = (bf16[320,512]{1,0:T(8,128)(2,1)S(1)}, bf16[320,512]{1,0:T(8,128)(2,1)S(1)}, u32[]{:S(2)}, u32[]{:S(2)}) collective-permute-start(bf16[320,512]{1,0:T(8,128)(2,1)S(1)} %pad_maximum_fusion.refs_0_.refs_4_), channel_id=1, source_target_pairs={{0,6},{2,0},{4,2},{6,4},{1,7},{3,1},{5,3},{7,5},{8,14},{10,8},{12,... | collective-permute-start | bytes 983048 | tf_op jit(solution)/shard_map/ppermute | solution.py:265
  49.2 0.7 collective-permute-start.3
  50.0 2.1 %collective-permute-start.11 = (bf16[320,512]{1,0:T(8,128)(2,1)S(1)}, bf16[320,512]{1,0:T(8,128)(2,1)S(1)}, u32[]{:S(2)}, u32[]{:S(2)}) collective-permute-start(bf16[320,512]{1,0:T(8,128)(2,1)S(1)} %pad_maximum_fusion.1.refs_0_.refs_8_), channel_id=1, source_target_pairs={{0,6},{2,0},{4,2},{6,4},{1,7},{3,1},{5,3},{7,5},{8,14},{10,8},{12,... | collective-permute-start | bytes 983048 | tf_op jit(solution)/shard_map/ppermute | solution.py:265
  52.0 1.4 collective-permute-start.10
  53.4 4.6 %collective-permute-done.5.refs_3_.refs_7_ = bf16[320,512]{1,0:T(8,128)(2,1)S(1)} collective-permute-done((bf16[320,512]{1,0:T(8,128)(2,1)S(1)}, bf16[320,512]{1,0:T(8,128)(2,1)S(1)}, u32[]{:S(2)}, u32[]{:S(2)}) %collective-permute-start.5) | collective-permute-done | bytes 327712 | tf_op jit(solution)/shard_map/ppermute | solution.py:265
  58.4 3.4 %collective-permute-done.3.refs_1_.refs_5_ = bf16[320,512]{1,0:T(8,128)(2,1)S(1)} collective-permute-done((bf16[320,512]{1,0:T(8,128)(2,1)S(1)}, bf16[320,512]{1,0:T(8,128)(2,1)S(1)}, u32[]{:S(2)}, u32[]{:S(2)}) %collective-permute-start.3) | collective-permute-done | bytes 327712 | tf_op jit(solution)/shard_map/ppermute | solution.py:265
  61.7 0.7 all-gather.3.cloned.1.call-done
  62.5 4.2 %shard_map.85 = (f32[2,160,384]{2,1,0:T(8,128)S(1)}, bf16[2,160,384]{2,1,0:T(8,128)(2,1)S(1)}) custom-call(s32[4]{0:T(128)S(1)} %pad_add_fusion.place, bf16[320,512]{1,0:T(8,128)(2,1)S(1)} %pad_maximum_fusion.refs_0_.refs_4_, bf16[320,512]{1,0:T(8,128)(2,1)S(1)} %collective-permute-done.3.refs_1_.refs_5_, ...), custom_call_target="tpu_custom_call" | custom-call | tf_op jit(solution)/shard_map/pallas_call | solution.py:29
  66.7 1.4 collective-permute-start.7
  68.0 0.8 collective-permute-done.9.refs_1_.refs_9_
  68.8 3.0 %shard_map.86 = (f32[1,160,384]{2,1,0:T(8,128)S(1)}, bf16[1,160,384]{2,1,0:T(8,128)(2,1)S(1)}) custom-call(s32[4]{0:T(128)S(1)} %pad_add_fusion.place, bf16[320,512]{1,0:T(8,128)(2,1)S(1)} %pad_maximum_fusion.1.refs_0_.refs_8_, bf16[320,512]{1,0:T(8,128)(2,1)S(1)} %collective-permute-done.9.refs_1_.refs_9_, ...), custom_call_target="tpu_custom_call" | custom-call | tf_op jit(solution)/shard_map/pallas_call | solution.py:29
  71.9 2.1 %collective-permute-done.7 = bf16[2,160,384]{2,1,0:T(8,128)(2,1)S(1)} collective-permute-done((bf16[2,160,384]{2,1,0:T(8,128)(2,1)S(1)}, bf16[2,160,384]{2,1,0:T(8,128)(2,1)S(1)}, u32[]{:S(2)}, u32[]{:S(2)}) %collective-permute-start.7) | collective-permute-done | bytes 245792 | tf_op jit(solution)/shard_map/ppermute | solution.py:269
  74.2 3.1 %collective-permute-done.12.far = bf16[1,160,384]{2,1,0:T(8,128)(2,1)S(1)} collective-permute-done((bf16[1,160,384]{2,1,0:T(8,128)(2,1)S(1)}, bf16[1,160,384]{2,1,0:T(8,128)(2,1)S(1)}, u32[]{:S(2)}, u32[]{:S(2)}) %collective-permute-start.12) | collective-permute-done | bytes 122912 | tf_op jit(solution)/shard_map/ppermute | solution.py:269
  77.2 0.8 shard_map.87.grad.refs_2_
  78.0 0.8 collective-permute-start.13
  78.8 0.8 collective-permute-start.8
  79.6 8.7 %collective-permute-done.8.act_far.refs_1_ = bf16[1,160,384]{2,1,0:T(8,128)(2,1)S(1)} collective-permute-done((bf16[1,160,384]{2,1,0:T(8,128)(2,1)S(1)}, bf16[1,160,384]{2,1,0:T(8,128)(2,1)S(1)}, u32[]{:S(2)}, u32[]{:S(2)}) %collective-permute-start.8) | collective-permute-done | bytes 122912 | tf_op jit(solution)/shard_map/ppermute | solution.py:269
  88.3 4.7 %shard_map.88 = (f32[704,512]{1,0:T(8,128)S(1)}, bf16[704,512]{1,0:T(8,128)(2,1)S(1)}, bf16[704,512]{1,0:T(8,128)(2,1)S(1)}, bf16[704,512]{1,0:T(8,128)(2,1)S(1)}) custom-call(s32[4]{0:T(128)S(1)} %pad_add_fusion.place, bf16[1,160,384]{2,1,0:T(8,128)(2,1)S(1)} %fusion.act.refs_0_, bf16[1,160,384]{2,1,0:T(8,128)(2,1)S(1)} %collective-permute-done.8.act_far.refs_1_, ...), custom_call_target="tpu_custom_call" | custom-call | tf_op jit(solution)/shard_map/pallas_call | solution.py:29
  93.1 5.6 %shard_map.90 = bf16[4,2,3,192,512]{4,3,2,1,0:T(8,128)(2,1)} custom-call(s32[4]{0:T(128)S(1)} %pad_add_fusion.place, bf16[704,512]{1,0:T(8,128)(2,1)S(1)} %get-tuple-element.37.after, bf16[1,160,384]{2,1,0:T(8,128)(2,1)S(1)} %fusion.act.refs_0_, bf16[1,160,384]{2,1,0:T(8,128)(2,1)S(1)} %collective-permute-done.8.act_far.refs_1_, ...), custom_call_target="tpu_custom_call" | custom-call | tf_op jit(solution)/shard_map/pallas_call | solution.py:29
  98.7 1.3 collective-permute-start.14
  100.0 0.5 collective-permute-start.16
  100.6 0.6 collective-permute-start.15
  101.2 14.2 %collective-permute-done.14.one = bf16[704,512]{1,0:T(8,128)(2,1)S(1)} collective-permute-done((bf16[704,512]{1,0:T(8,128)(2,1)}, bf16[704,512]{1,0:T(8,128)(2,1)S(1)}, u32[]{:S(2)}, u32[]{:S(2)}) %collective-permute-start.14) | collective-permute-done | bytes 720928 | tf_op jit(solution)/shard_map/ppermute | solution.py:265
  115.4 1.8 collective-permute-done.16.two
  117.2 18.2 %collective-permute-done.15.three = bf16[704,512]{1,0:T(8,128)(2,1)S(1)} collective-permute-done((bf16[704,512]{1,0:T(8,128)(2,1)S(1)}, bf16[704,512]{1,0:T(8,128)(2,1)S(1)}, u32[]{:S(2)}, u32[]{:S(2)}) %collective-permute-start.15) | collective-permute-done | bytes 720928 | tf_op jit(solution)/shard_map/ppermute | solution.py:265
  135.4 0.9 shard_map.89
  136.2 3.9 %collective-permute-start.17 = (bf16[176,512]{1,0:T(8,128)(2,1)S(1)}, bf16[176,512]{1,0:T(8,128)(2,1)S(1)}, u32[]{:S(2)}, u32[]{:S(2)}) collective-permute-start(bf16[176,512]{1,0:T(8,128)(2,1)S(1)} %get-tuple-element.40), channel_id=1, source_target_pairs={{0,24},{8,0},{16,8},{24,16},{1,25},{9,1},{17,9},{25,17},{2,26},{10... | collective-permute-start | bytes 540680 | tf_op jit(solution)/shard_map/ppermute | solution.py:265
  140.2 7.9 %collective-permute-done.17.refs_1_ = bf16[176,512]{1,0:T(8,128)(2,1)S(1)} collective-permute-done((bf16[176,512]{1,0:T(8,128)(2,1)S(1)}, bf16[176,512]{1,0:T(8,128)(2,1)S(1)}, u32[]{:S(2)}, u32[]{:S(2)}) %collective-permute-start.17) | collective-permute-done | bytes 180256 | tf_op jit(solution)/shard_map/ppermute | solution.py:265
  148.1 1.9 %collective-permute-start.20 = (bf16[3,192,512]{2,1,0:T(8,128)(2,1)}, bf16[3,192,512]{2,1,0:T(8,128)(2,1)S(1)}, u32[]{:S(2)}, u32[]{:S(2)}) collective-permute-start(bf16[3,192,512]{2,1,0:T(8,128)(2,1)} %bitcast.24), channel_id=1, source_target_pairs={{0,0},{1,32},{32,1},{33,33},{2,2},{3,34},{34,3},{35,35},{4,4},{5,3... | collective-permute-start | bytes 1769480 | tf_op jit(solution)/shard_map/ppermute | solution.py:273
  150.0 4.9 %collective-permute-start.18 = (bf16[176,512]{1,0:T(8,128)(2,1)S(1)}, bf16[176,512]{1,0:T(8,128)(2,1)S(1)}, u32[]{:S(2)}, u32[]{:S(2)}) collective-permute-start(bf16[176,512]{1,0:T(8,128)(2,1)S(1)} %get-tuple-element.42), channel_id=1, source_target_pairs={{0,16},{8,24},{16,0},{24,8},{1,17},{9,25},{17,1},{25,9},{2,18},{10... | collective-permute-start | bytes 540680 | tf_op jit(solution)/shard_map/ppermute | solution.py:265
  154.9 1.7 collective-permute-start.19
  156.6 17.5 %collective-permute-done.18.refs_2_ = bf16[176,512]{1,0:T(8,128)(2,1)S(1)} collective-permute-done((bf16[176,512]{1,0:T(8,128)(2,1)S(1)}, bf16[176,512]{1,0:T(8,128)(2,1)S(1)}, u32[]{:S(2)}, u32[]{:S(2)}) %collective-permute-start.18) | collective-permute-done | bytes 180256 | tf_op jit(solution)/shard_map/ppermute | solution.py:265
  174.1 2.6 %collective-permute-done.19.refs_3_ = bf16[176,512]{1,0:T(8,128)(2,1)S(1)} collective-permute-done((bf16[176,512]{1,0:T(8,128)(2,1)S(1)}, bf16[176,512]{1,0:T(8,128)(2,1)S(1)}, u32[]{:S(2)}, u32[]{:S(2)}) %collective-permute-start.19) | collective-permute-done | bytes 180256 | tf_op jit(solution)/shard_map/ppermute | solution.py:265
  176.7 1.7 shard_map.91
  178.4 0.6 slice_bitcast_fusion
  179.0 1.2 bitcast_convert_fusion
  (49 shorter events, 1.9 us)
Async XLA Ops:
  7.2 55.3 %all-gather.3.cloned.1.call-start = ((), (), s32[]{:S(2)}) async-start(), calls=%async_computation.2 | async-start | bytes 5308416 | tf_op jit(solution)/shard_map/all_gather | solution.py:289
  7.2 12.7 %collective-permute-start.6 = (bf16[3,192,512]{2,1,0:T(8,128)(2,1)}, bf16[3,192,512]{2,1,0:T(8,128)(2,1)S(1)}, u32[]{:S(2)}, u32[]{:S(2)}) collective-permute-start(bf16[3,192,512]{2,1,0:T(8,128)(2,1)} %bitcast.23), channel_id=1, source_target_pairs={{0,0},{1,32},{32,1},{33,33},{2,2},{3,34},{34,3},{35,35},{4,4},{5,3... | collective-permute-start | bytes 1769480 | tf_op jit(solution)/shard_map/ppermute | solution.py:273
  19.9 0.8 copy-start.14
  20.8 127.3 %reduce-scatter.2.cloned.1.call-start = ((), (), s32[]{:S(2)}) async-start(), calls=%async_computation.1 | async-start | bytes 5308416 | tf_op jit(solution)/shard_map/reduce_scatter | solution.py:359
  20.9 0.9 copy-start.6
  21.8 0.9 copy-start.7
  22.7 0.7 copy-start.8
  23.4 0.7 copy-start.10
  25.5 10.4 %collective-permute-start = (bf16[160,512]{1,0:T(8,128)(2,1)S(1)}, bf16[160,512]{1,0:T(8,128)(2,1)S(1)}, u32[]{:S(2)}, u32[]{:S(2)}) collective-permute-start(bf16[160,512]{1,0:T(8,128)(2,1)S(1)} %get-tuple-element.28), channel_id=1, source_target_pairs={{0,8},{8,16},{16,24},{24,0},{1,9},{9,17},{17,25},{25,1},{2,10},{10... | collective-permute-start | bytes 491528 | tf_op jit(solution)/shard_map/ppermute | solution.py:265
  28.9 14.4 %collective-permute-start.1 = (bf16[160,512]{1,0:T(8,128)(2,1)S(1)}, bf16[160,512]{1,0:T(8,128)(2,1)S(1)}, u32[]{:S(2)}, u32[]{:S(2)}) collective-permute-start(bf16[160,512]{1,0:T(8,128)(2,1)S(1)} %get-tuple-element.29), channel_id=1, source_target_pairs={{0,16},{8,24},{16,0},{24,8},{1,17},{9,25},{17,1},{25,9},{2,18},{10... | collective-permute-start | bytes 491528 | tf_op jit(solution)/shard_map/ppermute | solution.py:265
  35.3 10.7 %collective-permute-start.2 = (bf16[160,512]{1,0:T(8,128)(2,1)S(1)}, bf16[160,512]{1,0:T(8,128)(2,1)S(1)}, u32[]{:S(2)}, u32[]{:S(2)}) collective-permute-start(bf16[160,512]{1,0:T(8,128)(2,1)S(1)} %get-tuple-element.30), channel_id=1, source_target_pairs={{0,24},{8,0},{16,8},{24,16},{1,25},{9,1},{17,9},{25,17},{2,26},{10... | collective-permute-start | bytes 491528 | tf_op jit(solution)/shard_map/ppermute | solution.py:265
  46.1 11.9 %collective-permute-start.5 = (bf16[320,512]{1,0:T(8,128)(2,1)S(1)}, bf16[320,512]{1,0:T(8,128)(2,1)S(1)}, u32[]{:S(2)}, u32[]{:S(2)}) collective-permute-start(bf16[320,512]{1,0:T(8,128)(2,1)S(1)} %pad_maximum_fusion.refs_0_.refs_4_), channel_id=1, source_target_pairs={{0,6},{2,0},{4,2},{6,4},{1,7},{3,1},{5,3},{7,5},{8,14},{10,8},{12,... | collective-permute-start | bytes 983048 | tf_op jit(solution)/shard_map/ppermute | solution.py:265
  48.9 9.5 %collective-permute-start.4 = (bf16[320,512]{1,0:T(8,128)(2,1)S(1)}, bf16[320,512]{1,0:T(8,128)(2,1)S(1)}, u32[]{:S(2)}, u32[]{:S(2)}) collective-permute-start(bf16[320,512]{1,0:T(8,128)(2,1)S(1)} %pad_maximum_fusion.refs_0_.refs_4_), channel_id=1, source_target_pairs={{0,4},{2,6},{4,0},{6,2},{1,5},{3,7},{5,1},{7,3},{8,12},{10,14},{12... | collective-permute-start | bytes 983048 | tf_op jit(solution)/shard_map/ppermute | solution.py:265
  49.2 12.5 %collective-permute-start.3 = (bf16[320,512]{1,0:T(8,128)(2,1)S(1)}, bf16[320,512]{1,0:T(8,128)(2,1)S(1)}, u32[]{:S(2)}, u32[]{:S(2)}) collective-permute-start(bf16[320,512]{1,0:T(8,128)(2,1)S(1)} %pad_maximum_fusion.refs_0_.refs_4_), channel_id=1, source_target_pairs={{0,2},{2,4},{4,6},{6,0},{1,3},{3,5},{5,7},{7,1},{8,10},{10,12},{12... | collective-permute-start | bytes 983048 | tf_op jit(solution)/shard_map/ppermute | solution.py:265
  50.0 18.1 %collective-permute-start.11 = (bf16[320,512]{1,0:T(8,128)(2,1)S(1)}, bf16[320,512]{1,0:T(8,128)(2,1)S(1)}, u32[]{:S(2)}, u32[]{:S(2)}) collective-permute-start(bf16[320,512]{1,0:T(8,128)(2,1)S(1)} %pad_maximum_fusion.1.refs_0_.refs_8_), channel_id=1, source_target_pairs={{0,6},{2,0},{4,2},{6,4},{1,7},{3,1},{5,3},{7,5},{8,14},{10,8},{12,... | collective-permute-start | bytes 983048 | tf_op jit(solution)/shard_map/ppermute | solution.py:265
  52.0 16.0 %collective-permute-start.10 = (bf16[320,512]{1,0:T(8,128)(2,1)S(1)}, bf16[320,512]{1,0:T(8,128)(2,1)S(1)}, u32[]{:S(2)}, u32[]{:S(2)}) collective-permute-start(bf16[320,512]{1,0:T(8,128)(2,1)S(1)} %pad_maximum_fusion.1.refs_0_.refs_8_), channel_id=1, source_target_pairs={{0,4},{2,6},{4,0},{6,2},{1,5},{3,7},{5,1},{7,3},{8,12},{10,14},{12... | collective-permute-start | bytes 983048 | tf_op jit(solution)/shard_map/ppermute | solution.py:265
  58.0 10.8 %collective-permute-start.9 = (bf16[320,512]{1,0:T(8,128)(2,1)S(1)}, bf16[320,512]{1,0:T(8,128)(2,1)S(1)}, u32[]{:S(2)}, u32[]{:S(2)}) collective-permute-start(bf16[320,512]{1,0:T(8,128)(2,1)S(1)} %pad_maximum_fusion.1.refs_0_.refs_8_), channel_id=1, source_target_pairs={{0,2},{2,4},{4,6},{6,0},{1,3},{3,5},{5,7},{7,1},{8,10},{10,12},{12... | collective-permute-start | bytes 983048 | tf_op jit(solution)/shard_map/ppermute | solution.py:265
  66.7 7.4 %collective-permute-start.7 = (bf16[2,160,384]{2,1,0:T(8,128)(2,1)S(1)}, bf16[2,160,384]{2,1,0:T(8,128)(2,1)S(1)}, u32[]{:S(2)}, u32[]{:S(2)}) collective-permute-start(bf16[2,160,384]{2,1,0:T(8,128)(2,1)S(1)} %get-tuple-element.32), channel_id=1, source_target_pairs={{0,1},{1,0},{2,3},{3,2},{4,5},{5,4},{6,7},{7,6},{8,9},{9,8},{10,11... | collective-permute-start | bytes 737288 | tf_op jit(solution)/shard_map/ppermute | solution.py:269
  68.0 3.8 %copy-start = (bf16[320,512]{1,0:T(8,128)(2,1)}, bf16[320,512]{1,0:T(8,128)(2,1)S(1)}, u32[]{:S(2)}) copy-start(bf16[320,512]{1,0:T(8,128)(2,1)S(1)} %collective-permute-done.10.refs_2_.refs_10_) | copy-start | bytes 983044
  68.8 3.0 %copy-start.2 = (bf16[320,512]{1,0:T(8,128)(2,1)}, bf16[320,512]{1,0:T(8,128)(2,1)S(1)}, u32[]{:S(2)}) copy-start(bf16[320,512]{1,0:T(8,128)(2,1)S(1)} %collective-permute-done.9.refs_1_.refs_9_) | copy-start | bytes 983044
  71.8 5.4 %collective-permute-start.12 = (bf16[1,160,384]{2,1,0:T(8,128)(2,1)S(1)}, bf16[1,160,384]{2,1,0:T(8,128)(2,1)S(1)}, u32[]{:S(2)}, u32[]{:S(2)}) collective-permute-start(bf16[1,160,384]{2,1,0:T(8,128)(2,1)S(1)} %get-tuple-element.34), channel_id=1, source_target_pairs={{0,1},{1,0},{2,3},{3,2},{4,5},{5,4},{6,7},{7,6},{8,9},{9,8},{10,11... | collective-permute-start | bytes 368648 | tf_op jit(solution)/shard_map/ppermute | solution.py:269
  78.0 15.0 %copy-start.1 = (bf16[320,512]{1,0:T(8,128)(2,1)S(1)}, bf16[320,512]{1,0:T(8,128)(2,1)}, u32[]{:S(2)}) copy-start(bf16[320,512]{1,0:T(8,128)(2,1)} %copy-done) | copy-start | bytes 983044
  78.0 15.0 %copy-start.3 = (bf16[320,512]{1,0:T(8,128)(2,1)S(1)}, bf16[320,512]{1,0:T(8,128)(2,1)}, u32[]{:S(2)}) copy-start(bf16[320,512]{1,0:T(8,128)(2,1)} %copy-done.2) | copy-start | bytes 983044
  78.0 10.3 %collective-permute-start.13 = (bf16[352,384]{1,0:T(8,128)(2,1)S(1)}, bf16[352,384]{1,0:T(8,128)(2,1)S(1)}, u32[]{:S(2)}, u32[]{:S(2)}) collective-permute-start(bf16[352,384]{1,0:T(8,128)(2,1)S(1)} %shard_map.87.grad.refs_2_), channel_id=1, source_target_pairs={{0,1},{1,0},{2,3},{3,2},{4,5},{5,4},{6,7},{7,6},{8,9},{9,8},{10,11... | collective-permute-start | bytes 811016 | tf_op jit(solution)/shard_map/ppermute | solution.py:269
  78.8 9.5 %collective-permute-start.8 = (bf16[1,160,384]{2,1,0:T(8,128)(2,1)S(1)}, bf16[1,160,384]{2,1,0:T(8,128)(2,1)S(1)}, u32[]{:S(2)}, u32[]{:S(2)}) collective-permute-start(bf16[1,160,384]{2,1,0:T(8,128)(2,1)S(1)} %fusion.act.refs_0_), channel_id=1, source_target_pairs={{0,1},{1,0},{2,3},{3,2},{4,5},{5,4},{6,7},{7,6},{8,9},{9,8},{10,11... | collective-permute-start | bytes 368648 | tf_op jit(solution)/shard_map/ppermute | solution.py:269
  93.0 5.6 %copy-start.4 = (bf16[704,512]{1,0:T(8,128)(2,1)}, bf16[704,512]{1,0:T(8,128)(2,1)S(1)}, u32[]{:S(2)}) copy-start(bf16[704,512]{1,0:T(8,128)(2,1)S(1)} %get-tuple-element.37.after) | copy-start | bytes 2162692
  93.0 5.6 %copy-start.12 = (bf16[704,512]{1,0:T(8,128)(2,1)}, bf16[704,512]{1,0:T(8,128)(2,1)S(1)}, u32[]{:S(2)}) copy-start(bf16[704,512]{1,0:T(8,128)(2,1)S(1)} %get-tuple-element.38) | copy-start | bytes 2162692
  93.1 5.6 %copy-start.13 = (bf16[704,512]{1,0:T(8,128)(2,1)}, bf16[704,512]{1,0:T(8,128)(2,1)S(1)}, u32[]{:S(2)}) copy-start(bf16[704,512]{1,0:T(8,128)(2,1)S(1)} %get-tuple-element.36) | copy-start | bytes 2162692
  98.7 1.9 %copy-start.5 = (bf16[704,512]{1,0:T(8,128)(2,1)S(1)}, bf16[704,512]{1,0:T(8,128)(2,1)}, u32[]{:S(2)}) copy-start(bf16[704,512]{1,0:T(8,128)(2,1)} %copy-done.4) | copy-start | bytes 2162692
  98.7 16.7 %collective-permute-start.14 = (bf16[704,512]{1,0:T(8,128)(2,1)}, bf16[704,512]{1,0:T(8,128)(2,1)S(1)}, u32[]{:S(2)}, u32[]{:S(2)}) collective-permute-start(bf16[704,512]{1,0:T(8,128)(2,1)} %copy-done.13), channel_id=1, source_target_pairs={{0,6},{2,0},{4,2},{6,4},{1,7},{3,1},{5,3},{7,5},{8,14},{10,8},{12,... | collective-permute-start | bytes 2162696 | tf_op jit(solution)/shard_map/ppermute | solution.py:265
  100.0 17.2 %collective-permute-start.16 = (bf16[704,512]{1,0:T(8,128)(2,1)}, bf16[704,512]{1,0:T(8,128)(2,1)S(1)}, u32[]{:S(2)}, u32[]{:S(2)}) collective-permute-start(bf16[704,512]{1,0:T(8,128)(2,1)} %copy-done.12), channel_id=1, source_target_pairs={{0,4},{2,6},{4,0},{6,2},{1,5},{3,7},{5,1},{7,3},{8,12},{10,14},{12... | collective-permute-start | bytes 2162696 | tf_op jit(solution)/shard_map/ppermute | solution.py:265
  100.6 34.8 %collective-permute-start.15 = (bf16[704,512]{1,0:T(8,128)(2,1)S(1)}, bf16[704,512]{1,0:T(8,128)(2,1)S(1)}, u32[]{:S(2)}, u32[]{:S(2)}) collective-permute-start(bf16[704,512]{1,0:T(8,128)(2,1)S(1)} %copy-done.5), channel_id=1, source_target_pairs={{0,2},{2,4},{4,6},{6,0},{1,3},{3,5},{5,7},{7,1},{8,10},{10,12},{12... | collective-permute-start | bytes 2162696 | tf_op jit(solution)/shard_map/ppermute | solution.py:265
  135.4 41.3 %copy-start.9 = (s32[128,2]{0,1:T(2,128)S(1)}, s32[128,2]{0,1:T(2,128)}, u32[]{:S(2)}) copy-start(s32[128,2]{0,1:T(2,128)} %param.6) | copy-start | bytes 3076
  135.4 41.3 %copy-start.11 = (f32[128,2]{0,1:T(2,128)S(1)}, f32[128,2]{0,1:T(2,128)}, u32[]{:S(2)}) copy-start(f32[128,2]{0,1:T(2,128)} %param.7) | copy-start | bytes 3076
  136.2 11.8 %collective-permute-start.17 = (bf16[176,512]{1,0:T(8,128)(2,1)S(1)}, bf16[176,512]{1,0:T(8,128)(2,1)S(1)}, u32[]{:S(2)}, u32[]{:S(2)}) collective-permute-start(bf16[176,512]{1,0:T(8,128)(2,1)S(1)} %get-tuple-element.40), channel_id=1, source_target_pairs={{0,24},{8,0},{16,8},{24,16},{1,25},{9,1},{17,9},{25,17},{2,26},{10... | collective-permute-start | bytes 540680 | tf_op jit(solution)/shard_map/ppermute | solution.py:265
  148.1 30.9 %collective-permute-start.20 = (bf16[3,192,512]{2,1,0:T(8,128)(2,1)}, bf16[3,192,512]{2,1,0:T(8,128)(2,1)S(1)}, u32[]{:S(2)}, u32[]{:S(2)}) collective-permute-start(bf16[3,192,512]{2,1,0:T(8,128)(2,1)} %bitcast.24), channel_id=1, source_target_pairs={{0,0},{1,32},{32,1},{33,33},{2,2},{3,34},{34,3},{35,35},{4,4},{5,3... | collective-permute-start | bytes 1769480 | tf_op jit(solution)/shard_map/ppermute | solution.py:273
  150.0 24.1 %collective-permute-start.18 = (bf16[176,512]{1,0:T(8,128)(2,1)S(1)}, bf16[176,512]{1,0:T(8,128)(2,1)S(1)}, u32[]{:S(2)}, u32[]{:S(2)}) collective-permute-start(bf16[176,512]{1,0:T(8,128)(2,1)S(1)} %get-tuple-element.42), channel_id=1, source_target_pairs={{0,16},{8,24},{16,0},{24,8},{1,17},{9,25},{17,1},{25,9},{2,18},{10... | collective-permute-start | bytes 540680 | tf_op jit(solution)/shard_map/ppermute | solution.py:265
  154.9 21.8 %collective-permute-start.19 = (bf16[176,512]{1,0:T(8,128)(2,1)S(1)}, bf16[176,512]{1,0:T(8,128)(2,1)S(1)}, u32[]{:S(2)}, u32[]{:S(2)}) collective-permute-start(bf16[176,512]{1,0:T(8,128)(2,1)S(1)} %get-tuple-element.43), channel_id=1, source_target_pairs={{0,8},{8,16},{16,24},{24,0},{1,9},{9,17},{17,25},{25,1},{2,10},{10... | collective-permute-start | bytes 540680 | tf_op jit(solution)/shard_map/ppermute | solution.py:265
Sparse Core Ops, SparseCore 0:
  20.9 41.5 all-gather.2
  98.8 39.1 reduce-scatter.1
where the time goes:
time: 187 us
  waiting for transfers between devices  104 us (56%)
  starting transfers between devices  40.4 us (22%)
  Pallas kernels  22.3 us (12%)
  between operations  14.3 us (8%)
  local copies, waits for them, and re-layouts  4.63 us (2%)
    ppermute x15, waiting for transfers between devices, shift(): return lax.ppermute(value, axis, [(i, (i + step) % 4) for i in range(4)])  81.6 us
    ppermute x15, starting transfers between devices, shift(): return lax.ppermute(value, axis, [(i, (i + step) % 4) for i in range(4)])  30.4 us
    pallas_call x8, Pallas kernels, call(): pl.pallas_call(kernel, out_shape=[jax.ShapeDtypeStruct(shape, kind) for s...  22.3 us
    ppermute x4, waiting for transfers between devices, swap(): return lax.ppermute(value, axis, [(0, 1), (1, 0)])  13.9 us
    ppermute x2, waiting for transfers between devices, turn(): lax.ppermute(value, ('core', 'zl'), [(2 * c + z, 2 * z + c) for c in rang...  7.77 us
    ppermute x2, starting transfers between devices, turn(): lax.ppermute(value, ('core', 'zl'), [(2 * c + z, 2 * z + c) for c in rang...  6.84 us
    unnamed x30, local copies, waits for them, and re-layouts  4.02 us
  transfers between devices with their start and end apart: 23, of which 18 were waited for; matrix products, arithmetic and copies ran while one was open for 0% of the time, Pallas kernels for 6%

commit v1 on v0

v1 whole, which is shorter than its diff:
```python
import functools

import jax
import jax.numpy as jnp
from jax import lax
from jax.experimental import pallas as pl
from jax.experimental.pallas import tpu as pltpu
from jax.sharding import Mesh, PartitionSpec as P

F32 = jnp.float32
BF16 = jnp.bfloat16
CAP = 80
TILE = 16
PARAMS = pltpu.CompilerParams(vmem_limit_bytes=48 * 1024 * 1024)


def nn(a, b):
    return lax.dot_general(a, b, (((1,), (0,)), ((), ())), preferred_element_type=F32)


def nt(a, b):
    return lax.dot_general(a, b, (((1,), (1,)), ((), ())), preferred_element_type=F32)


def tn(a, b):
    return lax.dot_general(a, b, (((0,), (0,)), ((), ())), preferred_element_type=F32)


def call(kernel, place, args, outs, scratch=(), spaces=None):
    whole = pl.BlockSpec(memory_space=pltpu.VMEM)
    return list(pl.pallas_call(
        kernel,
        out_shape=[jax.ShapeDtypeStruct(shape, kind) for shape, kind in outs],
        in_specs=[pl.BlockSpec(memory_space=pltpu.SMEM)] + (spaces or [whole] * len(args)),
        out_specs=[whole] * len(outs),
        scratch_shapes=list(scratch),
        compiler_params=PARAMS,
    )(place, *args))


def expert_rows(place, ids, k):
    expert = lax.rem(place[0] + k, 4)
    return ids[0:1, :] == expert, ids[1:2, :] == expert


def slots_kernel(place, ids_far, probs_far, tokens, grads, placing, *refs):
    outs, ids, probs, token_copy, grad_copy, sems = refs[0:4], *refs[4:9]
    copies = [
        pltpu.make_async_copy(source, target, sems.at[n])
        for n, (source, target) in enumerate(
            [(ids_far, ids), (probs_far, probs), (tokens, token_copy), (grads, grad_copy)]
        )
    ]
    for copy in copies:
        copy.start()
    copies[0].wait()
    copies[1].wait()
    rows = ids.shape[1]
    before = (
        lax.broadcasted_iota(jnp.int32, (rows, rows), 0)
        < lax.broadcasted_iota(jnp.int32, (rows, rows), 1)
    ).astype(BF16)
    slot = lax.broadcasted_iota(jnp.int32, (CAP, rows), 0)
    scales = []
    for k in range(4):
        one, two = expert_rows(place, ids, k)
        named = jnp.logical_or(one, two)
        marks = jnp.broadcast_to(named, (8, rows)).astype(F32)
        position = nn(marks.astype(BF16), before)[0:1, :].astype(jnp.int32)
        weight = jnp.where(one, probs[0:1, :], probs[1:2, :])
        chosen = jnp.logical_and(
            jnp.broadcast_to(marks[0:1, :] > 0.5, (CAP, rows)),
            slot == jnp.broadcast_to(position, (CAP, rows)),
        )
        placing[k * CAP : (k + 1) * CAP, :] = chosen.astype(F32).astype(BF16)
        scales.append(jnp.sum(jnp.where(chosen, weight, 0.0), axis=1, keepdims=True))
    copies[2].wait()
    copies[3].wait()
    for k in range(4):
        hot = placing[k * CAP : (k + 1) * CAP, :]
        outs[k][0:CAP, :] = nn(hot, token_copy[...]).astype(BF16)
        outs[k][CAP : 2 * CAP, :] = (scales[k] * nn(hot, grad_copy[...])).astype(BF16)


def fetch(own, other, joined, sems, names, place):
    half, width = own[0].shape[1:]
    copies = []
    for i in range(4):
        spot = lax.rem(place[2] - place[1] + i + 4, 4)
        columns = pl.ds(pl.multiple_of(spot * width, width), width)
        for n, m in enumerate(names):
            for h, source in enumerate((own[i], other[i])):
                copies.append(
                    pltpu.make_async_copy(
                        source.at[m],
                        joined.at[pl.ds((2 * n + h) * half, half), columns],
                        sems.at[i, n, h],
                    )
                )
    for copy in copies:
        copy.start()
    return copies


def project_kernel(names, place, *refs):
    rows, own, other = refs[0:4], refs[4:8], refs[8:12]
    keep, send, joined, wide, total, sems = refs[12:18]
    width = rows[0].shape[1]
    copies = fetch(own, other, joined, sems, names, place)
    for j in range(4):
        wide[:, j * width : (j + 1) * width] = rows[j][...]
    for copy in copies:
        copy.wait()
    total[...] = nt(wide[...], joined[...])
    part = keep.shape[0]
    keep[...] = total[pl.ds(pl.multiple_of(place[3] * part, 32), part), :]
    send[...] = total[pl.ds(pl.multiple_of((1 - place[3]) * part, 32), part), :].astype(BF16)


def pieces(values):
    high = values.astype(BF16)
    rest = values - high.astype(F32)
    middle = rest.astype(BF16)
    low = (rest - middle.astype(F32)).astype(BF16)
    return high, middle, low


def marked_rows(row):
    spot = lax.broadcasted_iota(jnp.int32, (TILE, row.shape[1]), 0)
    parts = [part.astype(F32) for part in pieces(row)]
    total = jnp.where(spot == 0, parts[0], 0.0)
    total += jnp.where(spot == 1, parts[1], 0.0)
    return (total + jnp.where(spot == 2, parts[2], 0.0)).astype(BF16)


def hidden_kernel(place, both, act, keep, far, out):
    part, width = keep.shape
    gate, up = both[:, 0:width], both[:, width : 2 * width]
    sigmoid = 1.0 / (1.0 + jnp.exp(-gate))
    swish = gate * sigmoid
    grad = keep[...] + far[...].astype(F32)
    out[0:part, 0:width] = (
        grad * up * sigmoid * (1.0 + gate * (1.0 - sigmoid))
    ).astype(BF16)
    out[0:part, width : 2 * width] = (grad * swish).astype(BF16)
    share = jnp.sum(act[...].astype(F32) * grad, axis=1, keepdims=True)
    out[part:, :] = jnp.zeros((2 * TILE, out.shape[1]), BF16)
    shape = (CAP, 128)
    same = lax.broadcasted_iota(jnp.int32, shape, 0) == lax.broadcasted_iota(jnp.int32, shape, 1)
    for n in range(2):
        row = jnp.sum(
            jnp.where(same, share[n * CAP : (n + 1) * CAP, :], 0.0), axis=0, keepdims=True
        )
        out[part + n * TILE : part + (n + 1) * TILE, 0:128] = marked_rows(row)


def join(target, mine, theirs, zl):
    part = target.shape[0] // 2
    target[pl.ds(pl.multiple_of(zl * part, 32), part), :] = mine[0:part, :]
    target[pl.ds(pl.multiple_of((1 - zl) * part, 32), part), :] = theirs[0:part, :]


def share_kernel(place, act, act_far, grad, grad_far, pair, down, *refs):
    outs, acts, grads, marks = refs[0:4], *refs[4:7]
    part, width = act.shape[0], outs[0].shape[1]
    zl = place[3]
    join(acts, act, act_far, zl)
    join(grads, grad, grad_far, zl)
    marks[zl] = grad[part:, 0:128]
    marks[1 - zl] = grad_far[part:, 0:128]
    unit = 2 * CAP + TILE
    for j in (1, 3, 2, 0):
        kind = outs[j].dtype
        columns = slice(j * width, (j + 1) * width)
        out = nn(acts[...], down[:, columns])
        back = nn(grads[...], pair[:, columns])
        for k in range(4):
            start, rows = k * unit, slice(k * CAP, (k + 1) * CAP)
            outs[j][start : start + CAP, :] = out[rows, :].astype(kind)
            outs[j][start + CAP : start + 2 * CAP, :] = back[rows, :].astype(kind)
    for j in range(4):
        for k in range(4):
            start = k * unit + 2 * CAP
            kind = outs[j].dtype
            rows = marks[k // 2, (k % 2) * TILE : (k % 2 + 1) * TILE, :]
            outs[j][start : start + TILE, :] = jnp.zeros((TILE, outs[j].shape[1]), kind)
            outs[j][start : start + TILE, 0:128] = rows.astype(kind)


def total_kernel(place, own, one, three, two, *outs):
    unit = 2 * CAP + TILE
    for k in range(4):
        span = pl.ds(k * unit, unit)
        total = own[span, :] + one[span, :].astype(F32)
        total += three[span, :].astype(F32) + two[span, :].astype(F32)
        outs[k][...] = total.astype(BF16)
        row = jnp.sum(total[2 * CAP :, 0:128], axis=0, keepdims=True)
        outs[k][2 * CAP :, 0:128] = marked_rows(row)


def weight_kernel(place, act, act_far, grad, grad_far, *refs):
    rows, routed = refs[0:4], refs[4:8]
    keep, send, acts, grads, turned = refs[8:13]
    half = keep.shape[2]
    join(acts, act, act_far, place[3])
    join(grads, grad, grad_far, place[3])
    for j in range(4):
        spot = lax.rem(place[1] - place[2] + j + 4, 4)
        turned[0, spot] = rows[j][...]
        turned[1, spot] = routed[j][...]
    for i in range(4):
        pair = tn(grads[...], turned[0, i])
        down = tn(acts[...], turned[1, i])
        for m, total in enumerate((pair[0 : 2 * half], pair[2 * half :], down)):
            keep[i, m] = total[0:half, :]
            send[i, m] = total[half:, :].astype(BF16)


def sum_kernel(place, keep, far, *outs):
    for i in range(4):
        outs[i][...] = (keep[i] + far[i].astype(F32)).astype(outs[i].dtype)


def column(row):
    rows = row.shape[1]
    shape = (rows, rows)
    same = lax.broadcasted_iota(jnp.int32, shape, 0) == lax.broadcasted_iota(jnp.int32, shape, 1)
    return jnp.sum(jnp.where(same, row, 0.0), axis=1, keepdims=True)


def owner_kernel(place, ids, probs, placing, *refs):
    blocks, layer, token, prob = refs[0:4], *refs[4:7]
    total = jnp.zeros(layer.shape, F32)
    grads = jnp.zeros(token.shape, F32)
    shares = [jnp.zeros((1, ids.shape[1]), F32) for _ in range(2)]
    for k in range(4):
        one, two = expert_rows(place, ids, k)
        hot = placing[k * CAP : (k + 1) * CAP, :]
        weight = jnp.where(one, probs[0:1, :], 0.0) + jnp.where(two, probs[1:2, :], 0.0)
        total += column(weight) * tn(hot, blocks[k][0:CAP, :])
        grads += tn(hot, blocks[k][CAP : 2 * CAP, :])
        found = nn(blocks[k][2 * CAP :, 0:128][:, 0:CAP], hot)
        share = jnp.sum(found, axis=0, keepdims=True)
        shares[0] += jnp.where(one, share, 0.0)
        shares[1] += jnp.where(two, share, 0.0)
    layer[...] = total.astype(BF16)
    token[...] = grads.astype(BF16)
    prob[...] = jnp.zeros(prob.shape, F32)
    for n in range(2):
        prob[n : n + 1, :] = shares[n] / probs[n : n + 1, :]


def shift(value, axis, step):
    return lax.ppermute(value, axis, [(i, (i + step) % 4) for i in range(4)])


def swap(value, axis):
    return lax.ppermute(value, axis, [(0, 1), (1, 0)])


def turn(value):
    return lax.ppermute(value, ("core", "zl"), [(2 * c + z, 2 * z + c) for c in range(2) for z in range(2)])


def body(tokens, expert_ids, gate_probs, stacked_weights, out_grad):
    rows, width = tokens.shape
    half = stacked_weights.shape[2]
    hidden = 2 * half
    slots = 4 * CAP
    part = slots // 2
    place = jnp.stack(
        [lax.axis_index(name) for name in ("expert", "x", "y", "zl")]
    ).astype(jnp.int32)
    ids, probs = expert_ids.T, gate_probs.T
    vmem = pl.BlockSpec(memory_space=pltpu.VMEM)
    hbm = pl.BlockSpec(memory_space=pl.ANY)
    far = pl.BlockSpec(memory_space=pltpu.HBM)

    placing, *blocks = call(
        slots_kernel,
        place,
        [ids, probs, tokens, out_grad],
        [((slots, rows), BF16)] + [((2 * CAP, width), BF16)] * 4,
        [
            pltpu.VMEM(ids.shape, jnp.int32),
            pltpu.VMEM(probs.shape, F32),
            pltpu.VMEM((rows, width), BF16),
            pltpu.VMEM((rows, width), BF16),
            pltpu.SemaphoreType.DMA((4,)),
        ],
        [far, far, far, far],
    )

    own, placing = lax.optimization_barrier((turn(stacked_weights[0]), placing))
    own = [own] + [shift(own, "x", i) for i in (1, 3, 2)]
    own[2:] = own[:1:-1]
    other = [swap(block, "core") for block in own]
    blocks = [blocks[0]] + [shift(blocks[k], "expert", k) for k in (1, 2, 3)]
    token_rows = jnp.concatenate([block[:CAP] for block in blocks], axis=0)
    routed_rows = jnp.concatenate([block[CAP:] for block in blocks], axis=0)
    token_rows, other[1], other[3] = lax.optimization_barrier((token_rows, other[1], other[3]))
    token_rows = [token_rows] + [shift(token_rows, "y", j) for j in (1, 3, 2)]
    routed_rows = [routed_rows] + [shift(routed_rows, "y", j) for j in (1, 3, 2)]
    token_rows[2:] = token_rows[:1:-1]
    routed_rows[2:] = routed_rows[:1:-1]

    def project(names, blocks):
        wide = len(names) * hidden
        return call(
            functools.partial(project_kernel, names),
            place,
            blocks + own + other,
            [((part, wide), F32), ((part, wide), BF16), ((wide, 4 * width), BF16)],
            [
                pltpu.VMEM((slots, 4 * width), BF16),
                pltpu.VMEM((slots, wide), F32),
                pltpu.SemaphoreType.DMA((4, 2, 2)),
            ],
            [vmem] * 4 + [hbm] * 8,
        )

    keep, send, pair_weights = project((0, 1), token_rows)
    both = keep + swap(send, "zl").astype(F32)
    gate, up = both[:, :hidden], both[:, hidden:]
    activation = (gate * jax.nn.sigmoid(gate) * up).astype(BF16)
    activation_far = swap(activation, "zl")
    keep, send, down_weights = project((2,), routed_rows)
    send, activation_far = lax.optimization_barrier((swap(send, "zl"), activation_far))
    hidden_grad = call(
        hidden_kernel,
        place,
        [both, activation, keep, send],
        [((part + 2 * TILE, 2 * hidden), BF16)],
    )[0]
    pairs = [activation, activation_far, hidden_grad, swap(hidden_grad, "zl")]

    unit = 2 * CAP + TILE
    joined = [pltpu.VMEM((slots, hidden), BF16), pltpu.VMEM((slots, 2 * hidden), BF16)]
    shares = call(
        share_kernel,
        place,
        pairs + [pair_weights, down_weights],
        [((4 * unit, width), F32)] + [((4 * unit, width), BF16)] * 3,
        joined + [pltpu.VMEM((2, 2 * TILE, 128), BF16)],
    )
    arrived = [shift(shares[j], "y", -j) for j in (1, 3, 2)]
    shares[0], pairs[0] = lax.optimization_barrier((shares[0], pairs[0]))
    keep, send = call(
        weight_kernel,
        place,
        pairs + token_rows + routed_rows,
        [((4, 3, half, width), F32), ((4, 3, half, width), BF16)],
        joined + [pltpu.VMEM((2, 4, slots, width), BF16)],
    )
    sums = call(
        sum_kernel,
        place,
        [keep, swap(send, "core")],
        [((3, half, width), F32)] + [((3, half, width), BF16)] * 3,
    )
    sums = list(sums)
    sums[1], sums[3], arrived[0], arrived[1] = lax.optimization_barrier(
        (sums[1], sums[3], arrived[0], arrived[1])
    )
    sums[2], arrived[2] = lax.optimization_barrier((sums[2], arrived[2]))
    far_sums = [shift(sums[i], "x", -i) for i in (1, 3, 2)]
    totals = call(total_kernel, place, [shares[0]] + arrived, [((unit, width), BF16)] * 4)
    returned = [totals[0]] + [shift(totals[k], "expert", -k) for k in (1, 2, 3)]
    far_sums[2], returned[1], returned[3] = lax.optimization_barrier(
        (far_sums[2], returned[1], returned[3])
    )
    layer_output, token_grad, prob_grad = call(
        owner_kernel,
        place,
        [ids, probs, placing] + returned,
        [((rows, width), BF16), ((rows, width), BF16), ((8, rows), F32)],
    )
    weight_total = sums[0]
    for block in far_sums:
        weight_total = weight_total + block.astype(F32)
    weight_grad = turn(weight_total.astype(BF16)).astype(F32)[None]
    return layer_output, token_grad, prob_grad[0:2].T, weight_grad


def solution(mesh):
    split = Mesh(
        mesh.devices.reshape(4, 2, 4, 4, 2), ("x", "core", "expert", "y", "zl")
    )
    rows = P(("x", "core", "expert"), ("y", "zl"))
    pairs = P(("x", "core", "expert"), None)
    weights = P("expert", None, ("y", "zl"), ("x", "core"))
    return jax.shard_map(
        body,
        mesh=split,
        in_specs=(rows, pairs, pairs, weights, rows),
        out_specs=(rows, rows, pairs, weights),
        check_vma=False,
    )
```

time: 187 us -> 196 us (1.048)
  starting transfers between devices: 40.4 us -> 54.6 us
  between operations: 14.3 us -> 0.82 us
  waiting for transfers between devices: 104 us -> 112 us
    ppermute x15 -> x21, waiting for transfers between devices: 81.6 us -> 93.2 us  [shift(): return lax.ppermute(value, axis, [(i, (i + step) % 4) for i in range(4)])]
    ppermute x15 -> x21, starting transfers between devices: 30.4 us -> 40.6 us  [shift(): return lax.ppermute(value, axis, [(i, (i + step) % 4) for i in range(4)])]
    ppermute x2, waiting for transfers between devices: 7.77 us -> 3.3 us  [turn(): lax.ppermute(value, ('core', 'zl'), [(2 * c + z, 2 * z + c) for c in rang...]
    ppermute x4 -> x9, starting transfers between devices: 3 us -> 6.22 us  [swap(): return lax.ppermute(value, axis, [(0, 1), (1, 0)])]
    pallas_call x8 -> x9, Pallas kernels: 22.3 us -> 23.6 us  [call(): pl.pallas_call(kernel, out_shape=[jax.ShapeDtypeStruct(shape, kind) for s...]
    ppermute x4 -> x9, waiting for transfers between devices: 13.9 us -> 15 us  [swap(): return lax.ppermute(value, axis, [(0, 1), (1, 0)])]
    unnamed x30 -> x14, local copies, waits for them, and re-layouts: 4.02 us -> 3.18 us
  transfers between devices with their start and end apart: 23 -> 32, of which waited for: 18 -> 19; matrix products, arithmetic and copies ran while one was open for 0% -> 0% of each run, Pallas kernels for 6% -> 7%
where the time goes in v1:
time: 196 us
  waiting for transfers between devices  112 us (57%)
  starting transfers between devices  54.6 us (28%)
  Pallas kernels  23.6 us (12%)
  local copies, waits for them, and re-layouts  3.79 us (2%)
    ppermute x21, waiting for transfers between devices, shift(): return lax.ppermute(value, axis, [(i, (i + step) % 4) for i in range(4)])  93.2 us
    ppermute x21, starting transfers between devices, shift(): return lax.ppermute(value, axis, [(i, (i + step) % 4) for i in range(4)])  40.6 us
    pallas_call x9, Pallas kernels, call(): pl.pallas_call(kernel, out_shape=[jax.ShapeDtypeStruct(shape, kind) for s...  23.6 us
    ppermute x9, waiting for transfers between devices, swap(): return lax.ppermute(value, axis, [(0, 1), (1, 0)])  15 us
    ppermute x2, starting transfers between devices, turn(): lax.ppermute(value, ('core', 'zl'), [(2 * c + z, 2 * z + c) for c in rang...  7.76 us
    ppermute x9, starting transfers between devices, swap(): return lax.ppermute(value, axis, [(0, 1), (1, 0)])  6.22 us
  transfers between devices with their start and end apart: 32, of which 19 were waited for; matrix products, arithmetic and copies ran while one was open for 0% of the time, Pallas kernels for 7%

profile of v1, /device:TPU:1, one launch (start us, length us, event | category | flops | bytes accessed | tf_op | source)
XLA Modules:
  0.0 196.1 jit_solution(16348584168625658488)
XLA Ops:
  0.6 4.9 %collective-permute-start = (bf16[3,192,512]{2,1,0:T(8,128)(2,1)}, bf16[3,192,512]{2,1,0:T(8,128)(2,1)S(1)}, u32[]{:S(2)}, u32[]{:S(2)}) collective-permute-start(bf16[3,192,512]{2,1,0:T(8,128)(2,1)} %bitcast.16), channel_id=1, source_target_pairs={{0,0},{1,32},{32,1},{33,33},{2,2},{3,34},{34,3},{35,35},{4,4},{5,3... | collective-permute-start | bytes 1769480 | tf_op jit(solution)/shard_map/ppermute | solution.py:262
  5.7 0.9 copy-done.1
  6.6 0.9 copy-done.2
  8.8 1.5 shard_map.84
  10.3 3.3 %collective-permute-done.refs_4_ = bf16[3,192,512]{2,1,0:T(8,128)(2,1)S(1)} collective-permute-done((bf16[3,192,512]{2,1,0:T(8,128)(2,1)}, bf16[3,192,512]{2,1,0:T(8,128)(2,1)S(1)}, u32[]{:S(2)}, u32[]{:S(2)}) %collective-permute-start) | collective-permute-done | bytes 589856 | tf_op jit(solution)/shard_map/ppermute | solution.py:262
  13.6 2.5 %collective-permute-start.6 = (bf16[3,192,512]{2,1,0:T(8,128)(2,1)S(1)}, bf16[3,192,512]{2,1,0:T(8,128)(2,1)S(1)}, u32[]{:S(2)}, u32[]{:S(2)}) collective-permute-start(bf16[3,192,512]{2,1,0:T(8,128)(2,1)S(1)} %collective-permute-done.refs_4_), channel_id=1, source_target_pairs={{0,192},{64,0},{128,64},{192,128},{1,193},{65,1},{129,65},{193,129... | collective-permute-start | bytes 1769480 | tf_op jit(solution)/shard_map/ppermute | solution.py:254
  16.1 3.0 %collective-permute-start.1 = (bf16[160,512]{1,0:T(8,128)(2,1)S(1)}, bf16[160,512]{1,0:T(8,128)(2,1)S(1)}, u32[]{:S(2)}, u32[]{:S(2)}) collective-permute-start(bf16[160,512]{1,0:T(8,128)(2,1)S(1)} %get-tuple-element.53), channel_id=1, source_target_pairs={{0,8},{8,16},{16,24},{24,0},{1,9},{9,17},{17,25},{25,1},{2,10},{10... | collective-permute-start | bytes 491528 | tf_op jit(solution)/shard_map/ppermute | solution.py:254
  19.1 4.6 %collective-permute-start.2 = (bf16[160,512]{1,0:T(8,128)(2,1)S(1)}, bf16[160,512]{1,0:T(8,128)(2,1)S(1)}, u32[]{:S(2)}, u32[]{:S(2)}) collective-permute-start(bf16[160,512]{1,0:T(8,128)(2,1)S(1)} %get-tuple-element.54), channel_id=1, source_target_pairs={{0,16},{8,24},{16,0},{24,8},{1,17},{9,25},{17,1},{25,9},{2,18},{10... | collective-permute-start | bytes 491528 | tf_op jit(solution)/shard_map/ppermute | solution.py:254
  23.8 1.7 collective-permute-start.11
  25.8 5.1 %collective-permute-start.3 = (bf16[160,512]{1,0:T(8,128)(2,1)S(1)}, bf16[160,512]{1,0:T(8,128)(2,1)S(1)}, u32[]{:S(2)}, u32[]{:S(2)}) collective-permute-start(bf16[160,512]{1,0:T(8,128)(2,1)S(1)} %get-tuple-element.55), channel_id=1, source_target_pairs={{0,24},{8,0},{16,8},{24,16},{1,25},{9,1},{17,9},{25,17},{2,26},{10... | collective-permute-start | bytes 491528 | tf_op jit(solution)/shard_map/ppermute | solution.py:254
  30.9 9.9 %collective-permute-done.4.refs_5_ = bf16[3,192,512]{2,1,0:T(8,128)(2,1)S(1)} collective-permute-done((bf16[3,192,512]{2,1,0:T(8,128)(2,1)S(1)}, bf16[3,192,512]{2,1,0:T(8,128)(2,1)S(1)}, u32[]{:S(2)}, u32[]{:S(2)}) %collective-permute-start.4) | collective-permute-done | bytes 589856 | tf_op jit(solution)/shard_map/ppermute | solution.py:254
  41.6 1.2 collective-permute-done.5.refs_9_
  42.8 2.7 %collective-permute-start.10 = (bf16[320,512]{1,0:T(8,128)(2,1)S(1)}, bf16[320,512]{1,0:T(8,128)(2,1)S(1)}, u32[]{:S(2)}, u32[]{:S(2)}) collective-permute-start(bf16[320,512]{1,0:T(8,128)(2,1)S(1)} %pad_maximum_fusion.refs_0_), channel_id=1, source_target_pairs={{0,6},{2,0},{4,2},{6,4},{1,7},{3,1},{5,3},{7,5},{8,14},{10,8},{12,... | collective-permute-start | bytes 983048 | tf_op jit(solution)/shard_map/ppermute | solution.py:254
  45.9 0.7 collective-permute-start.8
  46.6 2.1 %collective-permute-start.17 = (bf16[320,512]{1,0:T(8,128)(2,1)S(1)}, bf16[320,512]{1,0:T(8,128)(2,1)S(1)}, u32[]{:S(2)}, u32[]{:S(2)}) collective-permute-start(bf16[320,512]{1,0:T(8,128)(2,1)S(1)} %pad_maximum_fusion.1.refs_0_.refs_4_), channel_id=1, source_target_pairs={{0,6},{2,0},{4,2},{6,4},{1,7},{3,1},{5,3},{7,5},{8,14},{10,8},{12,... | collective-permute-start | bytes 983048 | tf_op jit(solution)/shard_map/ppermute | solution.py:254
  48.7 1.4 collective-permute-start.16
  50.1 9.3 %collective-permute-done.10.refs_3_ = bf16[320,512]{1,0:T(8,128)(2,1)S(1)} collective-permute-done((bf16[320,512]{1,0:T(8,128)(2,1)S(1)}, bf16[320,512]{1,0:T(8,128)(2,1)S(1)}, u32[]{:S(2)}, u32[]{:S(2)}) %collective-permute-start.10) | collective-permute-done | bytes 327712 | tf_op jit(solution)/shard_map/ppermute | solution.py:254
  59.4 5.0 %collective-permute-done.8.refs_1_ = bf16[320,512]{1,0:T(8,128)(2,1)S(1)} collective-permute-done((bf16[320,512]{1,0:T(8,128)(2,1)S(1)}, bf16[320,512]{1,0:T(8,128)(2,1)S(1)}, u32[]{:S(2)}, u32[]{:S(2)}) %collective-permute-start.8) | collective-permute-done | bytes 327712 | tf_op jit(solution)/shard_map/ppermute | solution.py:254
  64.5 3.7 %shard_map.85 = (f32[160,768]{1,0:T(8,128)S(1)}, bf16[160,768]{1,0:T(8,128)(2,1)S(1)}, bf16[768,2048]{1,0:T(8,128)(2,1)}) custom-call(s32[4]{0:T(128)S(1)} %pad_add_fusion.place, bf16[320,512]{1,0:T(8,128)(2,1)S(1)} %pad_maximum_fusion.refs_0_, bf16[320,512]{1,0:T(8,128)(2,1)S(1)} %collective-permute-done.8.refs_1_, ...), custom_call_target="tpu_custom_call" | custom-call | tf_op jit(solution)/shard_map/pallas_call | solution.py:31
  68.1 0.9 collective-permute-start.14
  69.0 4.5 %collective-permute-done.17.refs_3_.refs_7_ = bf16[320,512]{1,0:T(8,128)(2,1)S(1)} collective-permute-done((bf16[320,512]{1,0:T(8,128)(2,1)S(1)}, bf16[320,512]{1,0:T(8,128)(2,1)S(1)}, u32[]{:S(2)}, u32[]{:S(2)}) %collective-permute-start.17) | collective-permute-done | bytes 327712 | tf_op jit(solution)/shard_map/ppermute | solution.py:254
  73.5 4.2 %collective-permute-done.15.refs_1_.refs_5_ = bf16[320,512]{1,0:T(8,128)(2,1)S(1)} collective-permute-done((bf16[320,512]{1,0:T(8,128)(2,1)S(1)}, bf16[320,512]{1,0:T(8,128)(2,1)S(1)}, u32[]{:S(2)}, u32[]{:S(2)}) %collective-permute-start.15) | collective-permute-done | bytes 327712 | tf_op jit(solution)/shard_map/ppermute | solution.py:254
  77.7 2.9 %shard_map.86 = (f32[160,384]{1,0:T(8,128)S(1)}, bf16[160,384]{1,0:T(8,128)(2,1)S(1)}, bf16[384,2048]{1,0:T(8,128)(2,1)}) custom-call(s32[4]{0:T(128)S(1)} %pad_add_fusion.place, bf16[320,512]{1,0:T(8,128)(2,1)S(1)} %pad_maximum_fusion.1.refs_0_.refs_4_, bf16[320,512]{1,0:T(8,128)(2,1)S(1)} %collective-permute-done.15.refs_1_.refs_5_, ...), custom_call_target="tpu_custom_call" | custom-call | tf_op jit(solution)/shard_map/pallas_call | solution.py:31
  81.4 1.0 collective-permute-start.19
  82.4 2.6 %collective-permute-done.18.far = bf16[160,384]{1,0:T(8,128)(2,1)S(1)} collective-permute-done((bf16[160,384]{1,0:T(8,128)(2,1)S(1)}, bf16[160,384]{1,0:T(8,128)(2,1)S(1)}, u32[]{:S(2)}, u32[]{:S(2)}) %collective-permute-start.18) | collective-permute-done | bytes 122912 | tf_op jit(solution)/shard_map/ppermute | solution.py:258
  85.0 2.6 %collective-permute-done.19.act_far = bf16[160,384]{1,0:T(8,128)(2,1)S(1)} collective-permute-done((bf16[160,384]{1,0:T(8,128)(2,1)S(1)}, bf16[160,384]{1,0:T(8,128)(2,1)S(1)}, u32[]{:S(2)}, u32[]{:S(2)}) %collective-permute-start.19) | collective-permute-done | bytes 122912 | tf_op jit(solution)/shard_map/ppermute | solution.py:258
  87.6 0.8 shard_map.87.grad
  89.0 6.5 %collective-permute-done.20.grad_far = bf16[192,768]{1,0:T(8,128)(2,1)S(1)} collective-permute-done((bf16[192,768]{1,0:T(8,128)(2,1)S(1)}, bf16[192,768]{1,0:T(8,128)(2,1)S(1)}, u32[]{:S(2)}, u32[]{:S(2)}) %collective-permute-start.20) | collective-permute-done | bytes 294944 | tf_op jit(solution)/shard_map/ppermute | solution.py:258
  95.5 3.8 %shard_map.88 = (f32[704,512]{1,0:T(8,128)S(1)}, bf16[704,512]{1,0:T(8,128)(2,1)S(1)}, bf16[704,512]{1,0:T(8,128)(2,1)S(1)}, bf16[704,512]{1,0:T(8,128)(2,1)S(1)}) custom-call(s32[4]{0:T(128)S(1)} %pad_add_fusion.place, bf16[160,384]{1,0:T(8,128)(2,1)S(1)} %fusion.act, bf16[160,384]{1,0:T(8,128)(2,1)S(1)} %collective-permute-done.19.act_far, ...), custom_call_target="tpu_custom_call" | custom-call | tf_op jit(solution)/shard_map/pallas_call | solution.py:31
  99.3 5.5 %shard_map.89 = (f32[4,3,192,512]{3,2,1,0:T(8,128)}, bf16[4,3,192,512]{3,2,1,0:T(8,128)(2,1)S(1)}) custom-call(s32[4]{0:T(128)S(1)} %pad_add_fusion.place, bf16[160,384]{1,0:T(8,128)(2,1)S(1)} %fusion.act, bf16[160,384]{1,0:T(8,128)(2,1)S(1)} %collective-permute-done.19.act_far, bf16[192,768]{1,0:T(8,128)(2,1)S(1)} %shard_map.87.grad, ...), custom_call_target="tpu_custom_call" | custom-call | tf_op jit(solution)/shard_map/pallas_call | solution.py:31
  104.8 2.4 %collective-permute-start.21 = (bf16[4,3,192,512]{3,2,1,0:T(8,128)(2,1)S(1)}, bf16[4,3,192,512]{3,2,1,0:T(8,128)(2,1)S(1)}, u32[]{:S(2)}, u32[]{:S(2)}) collective-permute-start(bf16[4,3,192,512]{3,2,1,0:T(8,128)(2,1)S(1)} %get-tuple-element.72), channel_id=1, source_target_pairs={{0,32},{32,0},{1,33},{33,1},{2,34},{34,2},{3,35},{35,3},{4,36},{36... | collective-permute-start | bytes 7077896 | tf_op jit(solution)/shard_map/ppermute | solution.py:258
  107.2 1.5 collective-permute-start.23
  109.2 2.1 %collective-permute-done.21.far = bf16[4,3,192,512]{3,2,1,0:T(8,128)(2,1)S(1)} collective-permute-done((bf16[4,3,192,512]{3,2,1,0:T(8,128)(2,1)S(1)}, bf16[4,3,192,512]{3,2,1,0:T(8,128)(2,1)S(1)}, u32[]{:S(2)}, u32[]{:S(2)}) %collective-permute-start.21) | collective-permute-done | bytes 2359328 | tf_op jit(solution)/shard_map/ppermute | solution.py:258
  111.3 2.9 %shard_map.90 = (f32[3,192,512]{2,1,0:T(8,128)S(1)}, bf16[3,192,512]{2,1,0:T(8,128)(2,1)S(1)}, bf16[3,192,512]{2,1,0:T(8,128)(2,1)S(1)}, bf16[3,192,512]{2,1,0:T(8,128)(2,1)S(1)}) custom-call(s32[4]{0:T(128)S(1)} %pad_add_fusion.place, f32[4,3,192,512]{3,2,1,0:T(8,128)} %get-tuple-element.71.keep, bf16[4,3,192,512]{3,2,1,0:T(8,128)(2,1)S(1)} %collective-permute-done.21.far), custom_call_target="tpu_custom_call" | custom-call | tf_op jit(solution)/shard_map/pallas_call | solution.py:31
  114.3 10.7 %collective-permute-done.22.one = bf16[704,512]{1,0:T(8,128)(2,1)S(1)} collective-permute-done((bf16[704,512]{1,0:T(8,128)(2,1)S(1)}, bf16[704,512]{1,0:T(8,128)(2,1)S(1)}, u32[]{:S(2)}, u32[]{:S(2)}) %collective-permute-start.22) | collective-permute-done | bytes 720928 | tf_op jit(solution)/shard_map/ppermute | solution.py:254
  124.9 16.7 %collective-permute-done.23.three = bf16[704,512]{1,0:T(8,128)(2,1)S(1)} collective-permute-done((bf16[704,512]{1,0:T(8,128)(2,1)S(1)}, bf16[704,512]{1,0:T(8,128)(2,1)S(1)}, u32[]{:S(2)}, u32[]{:S(2)}) %collective-permute-start.23) | collective-permute-done | bytes 720928 | tf_op jit(solution)/shard_map/ppermute | solution.py:254
  142.2 0.9 collective-permute-start.30
  143.1 0.9 shard_map.91
  143.9 6.1 %collective-permute-start.26 = (bf16[176,512]{1,0:T(8,128)(2,1)S(1)}, bf16[176,512]{1,0:T(8,128)(2,1)S(1)}, u32[]{:S(2)}, u32[]{:S(2)}) collective-permute-start(bf16[176,512]{1,0:T(8,128)(2,1)S(1)} %get-tuple-element.84), channel_id=1, source_target_pairs={{0,24},{8,0},{16,8},{24,16},{1,25},{9,1},{17,9},{25,17},{2,26},{10... | collective-permute-start | bytes 540680 | tf_op jit(solution)/shard_map/ppermute | solution.py:254
  150.0 5.5 %collective-permute-done.26.refs_1_ = bf16[176,512]{1,0:T(8,128)(2,1)S(1)} collective-permute-done((bf16[176,512]{1,0:T(8,128)(2,1)S(1)}, bf16[176,512]{1,0:T(8,128)(2,1)S(1)}, u32[]{:S(2)}, u32[]{:S(2)}) %collective-permute-start.26) | collective-permute-done | bytes 180256 | tf_op jit(solution)/shard_map/ppermute | solution.py:254
  155.6 5.7 %collective-permute-done.27.refs_3_ = bf16[176,512]{1,0:T(8,128)(2,1)S(1)} collective-permute-done((bf16[176,512]{1,0:T(8,128)(2,1)S(1)}, bf16[176,512]{1,0:T(8,128)(2,1)S(1)}, u32[]{:S(2)}, u32[]{:S(2)}) %collective-permute-start.27) | collective-permute-done | bytes 180256 | tf_op jit(solution)/shard_map/ppermute | solution.py:254
  161.3 6.8 %collective-permute-done.29 = bf16[3,192,512]{2,1,0:T(8,128)(2,1)S(1)} collective-permute-done((bf16[3,192,512]{2,1,0:T(8,128)(2,1)S(1)}, bf16[3,192,512]{2,1,0:T(8,128)(2,1)S(1)}, u32[]{:S(2)}, u32[]{:S(2)}) %collective-permute-start.29) | collective-permute-done | bytes 589856 | tf_op jit(solution)/shard_map/ppermute | solution.py:254
  168.1 2.9 %collective-permute-done.30 = bf16[3,192,512]{2,1,0:T(8,128)(2,1)S(1)} collective-permute-done((bf16[3,192,512]{2,1,0:T(8,128)(2,1)S(1)}, bf16[3,192,512]{2,1,0:T(8,128)(2,1)S(1)}, u32[]{:S(2)}, u32[]{:S(2)}) %collective-permute-start.30) | collective-permute-done | bytes 589856 | tf_op jit(solution)/shard_map/ppermute | solution.py:254
  171.3 2.8 %collective-permute-start.31 = (bf16[3,192,512]{2,1,0:T(8,128)(2,1)S(1)}, bf16[3,192,512]{2,1,0:T(8,128)(2,1)S(1)}, u32[]{:S(2)}, u32[]{:S(2)}) collective-permute-start(bf16[3,192,512]{2,1,0:T(8,128)(2,1)S(1)} %add_convert_fusion), channel_id=1, source_target_pairs={{0,0},{1,32},{32,1},{33,33},{2,2},{3,34},{34,3},{35,35},{4,4},{5,3... | collective-permute-start | bytes 1769480 | tf_op jit(solution)/shard_map/ppermute | solution.py:262
  174.2 6.8 %collective-permute-start.28 = (bf16[176,512]{1,0:T(8,128)(2,1)S(1)}, bf16[176,512]{1,0:T(8,128)(2,1)S(1)}, u32[]{:S(2)}, u32[]{:S(2)}) collective-permute-start(bf16[176,512]{1,0:T(8,128)(2,1)S(1)} %get-tuple-element.87), channel_id=1, source_target_pairs={{0,16},{8,24},{16,0},{24,8},{1,17},{9,25},{17,1},{25,9},{2,18},{10... | collective-permute-start | bytes 540680 | tf_op jit(solution)/shard_map/ppermute | solution.py:254
  181.0 11.7 %collective-permute-done.28.refs_2_ = bf16[176,512]{1,0:T(8,128)(2,1)S(1)} collective-permute-done((bf16[176,512]{1,0:T(8,128)(2,1)S(1)}, bf16[176,512]{1,0:T(8,128)(2,1)S(1)}, u32[]{:S(2)}, u32[]{:S(2)}) %collective-permute-start.28) | collective-permute-done | bytes 180256 | tf_op jit(solution)/shard_map/ppermute | solution.py:254
  192.7 1.7 shard_map.92
  194.9 1.2 bitcast_convert_fusion
  (51 shorter events, 6.4 us)
Async XLA Ops:
  0.6 13.0 %collective-permute-start = (bf16[3,192,512]{2,1,0:T(8,128)(2,1)}, bf16[3,192,512]{2,1,0:T(8,128)(2,1)S(1)}, u32[]{:S(2)}, u32[]{:S(2)}) collective-permute-start(bf16[3,192,512]{2,1,0:T(8,128)(2,1)} %bitcast.16), channel_id=1, source_target_pairs={{0,0},{1,32},{32,1},{33,33},{2,2},{3,34},{34,3},{35,35},{4,4},{5,3... | collective-permute-start | bytes 1769480 | tf_op jit(solution)/shard_map/ppermute | solution.py:262
  5.7 0.9 copy-start.1
  6.6 0.9 copy-start.2
  7.5 0.7 copy-start.3
  8.1 0.7 copy-start.4
  13.6 17.3 %collective-permute-start.6 = (bf16[3,192,512]{2,1,0:T(8,128)(2,1)S(1)}, bf16[3,192,512]{2,1,0:T(8,128)(2,1)S(1)}, u32[]{:S(2)}, u32[]{:S(2)}) collective-permute-start(bf16[3,192,512]{2,1,0:T(8,128)(2,1)S(1)} %collective-permute-done.refs_4_), channel_id=1, source_target_pairs={{0,192},{64,0},{128,64},{192,128},{1,193},{65,1},{129,65},{193,129... | collective-permute-start | bytes 1769480 | tf_op jit(solution)/shard_map/ppermute | solution.py:254
  16.1 24.7 %collective-permute-start.4 = (bf16[3,192,512]{2,1,0:T(8,128)(2,1)S(1)}, bf16[3,192,512]{2,1,0:T(8,128)(2,1)S(1)}, u32[]{:S(2)}, u32[]{:S(2)}) collective-permute-start(bf16[3,192,512]{2,1,0:T(8,128)(2,1)S(1)} %collective-permute-done.refs_4_), channel_id=1, source_target_pairs={{0,64},{64,128},{128,192},{192,0},{1,65},{65,129},{129,193},{193,1... | collective-permute-start | bytes 1769480 | tf_op jit(solution)/shard_map/ppermute | solution.py:254
  16.1 9.7 %collective-permute-start.1 = (bf16[160,512]{1,0:T(8,128)(2,1)S(1)}, bf16[160,512]{1,0:T(8,128)(2,1)S(1)}, u32[]{:S(2)}, u32[]{:S(2)}) collective-permute-start(bf16[160,512]{1,0:T(8,128)(2,1)S(1)} %get-tuple-element.53), channel_id=1, source_target_pairs={{0,8},{8,16},{16,24},{24,0},{1,9},{9,17},{17,25},{25,1},{2,10},{10... | collective-permute-start | bytes 491528 | tf_op jit(solution)/shard_map/ppermute | solution.py:254
  19.1 21.7 %collective-permute-start.2 = (bf16[160,512]{1,0:T(8,128)(2,1)S(1)}, bf16[160,512]{1,0:T(8,128)(2,1)S(1)}, u32[]{:S(2)}, u32[]{:S(2)}) collective-permute-start(bf16[160,512]{1,0:T(8,128)(2,1)S(1)} %get-tuple-element.54), channel_id=1, source_target_pairs={{0,16},{8,24},{16,0},{24,8},{1,17},{9,25},{17,1},{25,9},{2,18},{10... | collective-permute-start | bytes 491528 | tf_op jit(solution)/shard_map/ppermute | solution.py:254
  23.8 17.7 %collective-permute-start.11 = (bf16[3,192,512]{2,1,0:T(8,128)(2,1)S(1)}, bf16[3,192,512]{2,1,0:T(8,128)(2,1)S(1)}, u32[]{:S(2)}, u32[]{:S(2)}) collective-permute-start(bf16[3,192,512]{2,1,0:T(8,128)(2,1)S(1)} %collective-permute-done.refs_4_), channel_id=1, source_target_pairs={{0,128},{64,192},{128,0},{192,64},{1,129},{65,193},{129,1},{193,65... | collective-permute-start | bytes 1769480 | tf_op jit(solution)/shard_map/ppermute | solution.py:254
  25.8 15.8 %collective-permute-start.3 = (bf16[160,512]{1,0:T(8,128)(2,1)S(1)}, bf16[160,512]{1,0:T(8,128)(2,1)S(1)}, u32[]{:S(2)}, u32[]{:S(2)}) collective-permute-start(bf16[160,512]{1,0:T(8,128)(2,1)S(1)} %get-tuple-element.55), channel_id=1, source_target_pairs={{0,24},{8,0},{16,8},{24,16},{1,25},{9,1},{17,9},{25,17},{2,26},{10... | collective-permute-start | bytes 491528 | tf_op jit(solution)/shard_map/ppermute | solution.py:254
  30.9 10.7 %collective-permute-start.7 = (bf16[3,192,512]{2,1,0:T(8,128)(2,1)S(1)}, bf16[3,192,512]{2,1,0:T(8,128)(2,1)S(1)}, u32[]{:S(2)}, u32[]{:S(2)}) collective-permute-start(bf16[3,192,512]{2,1,0:T(8,128)(2,1)S(1)} %collective-permute-done.6.refs_7_), channel_id=1, source_target_pairs={{0,32},{32,0},{1,33},{33,1},{2,34},{34,2},{3,35},{35,3},{4,36},{36... | collective-permute-start | bytes 1769480 | tf_op jit(solution)/shard_map/ppermute | solution.py:258
  40.8 2.0 %collective-permute-start.5 = (bf16[3,192,512]{2,1,0:T(8,128)(2,1)S(1)}, bf16[3,192,512]{2,1,0:T(8,128)(2,1)S(1)}, u32[]{:S(2)}, u32[]{:S(2)}) collective-permute-start(bf16[3,192,512]{2,1,0:T(8,128)(2,1)S(1)} %collective-permute-done.4.refs_5_), channel_id=1, source_target_pairs={{0,32},{32,0},{1,33},{33,1},{2,34},{34,2},{3,35},{35,3},{4,36},{36... | collective-permute-start | bytes 1769480 | tf_op jit(solution)/shard_map/ppermute | solution.py:258
  40.9 5.8 %collective-permute-start.12 = (bf16[3,192,512]{2,1,0:T(8,128)(2,1)S(1)}, bf16[3,192,512]{2,1,0:T(8,128)(2,1)S(1)}, u32[]{:S(2)}, u32[]{:S(2)}) collective-permute-start(bf16[3,192,512]{2,1,0:T(8,128)(2,1)S(1)} %collective-permute-done.refs_4_), channel_id=1, source_target_pairs={{0,32},{32,0},{1,33},{33,1},{2,34},{34,2},{3,35},{35,3},{4,36},{36... | collective-permute-start | bytes 1769480 | tf_op jit(solution)/shard_map/ppermute | solution.py:258
  41.5 7.2 %collective-permute-start.13 = (bf16[3,192,512]{2,1,0:T(8,128)(2,1)S(1)}, bf16[3,192,512]{2,1,0:T(8,128)(2,1)S(1)}, u32[]{:S(2)}, u32[]{:S(2)}) collective-permute-start(bf16[3,192,512]{2,1,0:T(8,128)(2,1)S(1)} %collective-permute-done.11.refs_6_), channel_id=1, source_target_pairs={{0,32},{32,0},{1,33},{33,1},{2,34},{34,2},{3,35},{35,3},{4,36},{36... | collective-permute-start | bytes 1769480 | tf_op jit(solution)/shard_map/ppermute | solution.py:258
  41.6 22.8 %copy-start.6 = (bf16[3,192,512]{2,1,0:T(8,128)(2,1)}, bf16[3,192,512]{2,1,0:T(8,128)(2,1)S(1)}, u32[]{:S(2)}) copy-start(bf16[3,192,512]{2,1,0:T(8,128)(2,1)S(1)} %collective-permute-done.7.refs_11_) | copy-start | bytes 1769476
  42.8 16.6 %collective-permute-start.10 = (bf16[320,512]{1,0:T(8,128)(2,1)S(1)}, bf16[320,512]{1,0:T(8,128)(2,1)S(1)}, u32[]{:S(2)}, u32[]{:S(2)}) collective-permute-start(bf16[320,512]{1,0:T(8,128)(2,1)S(1)} %pad_maximum_fusion.refs_0_), channel_id=1, source_target_pairs={{0,6},{2,0},{4,2},{6,4},{1,7},{3,1},{5,3},{7,5},{8,14},{10,8},{12,... | collective-permute-start | bytes 983048 | tf_op jit(solution)/shard_map/ppermute | solution.py:254
  45.6 13.9 %collective-permute-start.9 = (bf16[320,512]{1,0:T(8,128)(2,1)S(1)}, bf16[320,512]{1,0:T(8,128)(2,1)S(1)}, u32[]{:S(2)}, u32[]{:S(2)}) collective-permute-start(bf16[320,512]{1,0:T(8,128)(2,1)S(1)} %pad_maximum_fusion.refs_0_), channel_id=1, source_target_pairs={{0,4},{2,6},{4,0},{6,2},{1,5},{3,7},{5,1},{7,3},{8,12},{10,14},{12... | collective-permute-start | bytes 983048 | tf_op jit(solution)/shard_map/ppermute | solution.py:254
  45.9 18.5 %collective-permute-start.8 = (bf16[320,512]{1,0:T(8,128)(2,1)S(1)}, bf16[320,512]{1,0:T(8,128)(2,1)S(1)}, u32[]{:S(2)}, u32[]{:S(2)}) collective-permute-start(bf16[320,512]{1,0:T(8,128)(2,1)S(1)} %pad_maximum_fusion.refs_0_), channel_id=1, source_target_pairs={{0,2},{2,4},{4,6},{6,0},{1,3},{3,5},{5,7},{7,1},{8,10},{10,12},{12... | collective-permute-start | bytes 983048 | tf_op jit(solution)/shard_map/ppermute | solution.py:254
  46.6 26.8 %collective-permute-start.17 = (bf16[320,512]{1,0:T(8,128)(2,1)S(1)}, bf16[320,512]{1,0:T(8,128)(2,1)S(1)}, u32[]{:S(2)}, u32[]{:S(2)}) collective-permute-start(bf16[320,512]{1,0:T(8,128)(2,1)S(1)} %pad_maximum_fusion.1.refs_0_.refs_4_), channel_id=1, source_target_pairs={{0,6},{2,0},{4,2},{6,4},{1,7},{3,1},{5,3},{7,5},{8,14},{10,8},{12,... | collective-permute-start | bytes 983048 | tf_op jit(solution)/shard_map/ppermute | solution.py:254
  48.7 24.8 %collective-permute-start.16 = (bf16[320,512]{1,0:T(8,128)(2,1)S(1)}, bf16[320,512]{1,0:T(8,128)(2,1)S(1)}, u32[]{:S(2)}, u32[]{:S(2)}) collective-permute-start(bf16[320,512]{1,0:T(8,128)(2,1)S(1)} %pad_maximum_fusion.1.refs_0_.refs_4_), channel_id=1, source_target_pairs={{0,4},{2,6},{4,0},{6,2},{1,5},{3,7},{5,1},{7,3},{8,12},{10,14},{12... | collective-permute-start | bytes 983048 | tf_op jit(solution)/shard_map/ppermute | solution.py:254
  59.4 18.2 %collective-permute-start.15 = (bf16[320,512]{1,0:T(8,128)(2,1)S(1)}, bf16[320,512]{1,0:T(8,128)(2,1)S(1)}, u32[]{:S(2)}, u32[]{:S(2)}) collective-permute-start(bf16[320,512]{1,0:T(8,128)(2,1)S(1)} %pad_maximum_fusion.1.refs_0_.refs_4_), channel_id=1, source_target_pairs={{0,2},{2,4},{4,6},{6,0},{1,3},{3,5},{5,7},{7,1},{8,10},{10,12},{12... | collective-permute-start | bytes 983048 | tf_op jit(solution)/shard_map/ppermute | solution.py:254
  68.1 13.1 %collective-permute-start.14 = (bf16[160,768]{1,0:T(8,128)(2,1)S(1)}, bf16[160,768]{1,0:T(8,128)(2,1)S(1)}, u32[]{:S(2)}, u32[]{:S(2)}) collective-permute-start(bf16[160,768]{1,0:T(8,128)(2,1)S(1)} %get-tuple-element.61), channel_id=1, source_target_pairs={{0,1},{1,0},{2,3},{3,2},{4,5},{5,4},{6,7},{7,6},{8,9},{9,8},{10,11... | collective-permute-start | bytes 737288 | tf_op jit(solution)/shard_map/ppermute | solution.py:258
  80.6 4.4 %collective-permute-start.18 = (bf16[160,384]{1,0:T(8,128)(2,1)S(1)}, bf16[160,384]{1,0:T(8,128)(2,1)S(1)}, u32[]{:S(2)}, u32[]{:S(2)}) collective-permute-start(bf16[160,384]{1,0:T(8,128)(2,1)S(1)} %get-tuple-element.62), channel_id=1, source_target_pairs={{0,1},{1,0},{2,3},{3,2},{4,5},{5,4},{6,7},{7,6},{8,9},{9,8},{10,11... | collective-permute-start | bytes 368648 | tf_op jit(solution)/shard_map/ppermute | solution.py:258
  81.3 14.2 %copy-start = (bf16[384,2048]{1,0:T(8,128)(2,1)S(1)}, bf16[384,2048]{1,0:T(8,128)(2,1)}, u32[]{:S(2)}) copy-start(bf16[384,2048]{1,0:T(8,128)(2,1)} %get-tuple-element.67.down) | copy-start | bytes 4718596
  81.4 6.2 %collective-permute-start.19 = (bf16[160,384]{1,0:T(8,128)(2,1)S(1)}, bf16[160,384]{1,0:T(8,128)(2,1)S(1)}, u32[]{:S(2)}, u32[]{:S(2)}) collective-permute-start(bf16[160,384]{1,0:T(8,128)(2,1)S(1)} %fusion.act), channel_id=1, source_target_pairs={{0,1},{1,0},{2,3},{3,2},{4,5},{5,4},{6,7},{7,6},{8,9},{9,8},{10,11... | collective-permute-start | bytes 368648 | tf_op jit(solution)/shard_map/ppermute | solution.py:258
  88.4 7.1 %collective-permute-start.20 = (bf16[192,768]{1,0:T(8,128)(2,1)S(1)}, bf16[192,768]{1,0:T(8,128)(2,1)S(1)}, u32[]{:S(2)}, u32[]{:S(2)}) collective-permute-start(bf16[192,768]{1,0:T(8,128)(2,1)S(1)} %shard_map.87.grad), channel_id=1, source_target_pairs={{0,1},{1,0},{2,3},{3,2},{4,5},{5,4},{6,7},{7,6},{8,9},{9,8},{10,11... | collective-permute-start | bytes 884744 | tf_op jit(solution)/shard_map/ppermute | solution.py:258
  104.8 6.5 %collective-permute-start.21 = (bf16[4,3,192,512]{3,2,1,0:T(8,128)(2,1)S(1)}, bf16[4,3,192,512]{3,2,1,0:T(8,128)(2,1)S(1)}, u32[]{:S(2)}, u32[]{:S(2)}) collective-permute-start(bf16[4,3,192,512]{3,2,1,0:T(8,128)(2,1)S(1)} %get-tuple-element.72), channel_id=1, source_target_pairs={{0,32},{32,0},{1,33},{33,1},{2,34},{34,2},{3,35},{35,3},{4,36},{36... | collective-permute-start | bytes 7077896 | tf_op jit(solution)/shard_map/ppermute | solution.py:258
  107.2 17.8 %collective-permute-start.22 = (bf16[704,512]{1,0:T(8,128)(2,1)S(1)}, bf16[704,512]{1,0:T(8,128)(2,1)S(1)}, u32[]{:S(2)}, u32[]{:S(2)}) collective-permute-start(bf16[704,512]{1,0:T(8,128)(2,1)S(1)} %get-tuple-element.75), channel_id=1, source_target_pairs={{0,6},{2,0},{4,2},{6,4},{1,7},{3,1},{5,3},{7,5},{8,14},{10,8},{12,... | collective-permute-start | bytes 2162696 | tf_op jit(solution)/shard_map/ppermute | solution.py:254
  107.2 34.4 %collective-permute-start.23 = (bf16[704,512]{1,0:T(8,128)(2,1)S(1)}, bf16[704,512]{1,0:T(8,128)(2,1)S(1)}, u32[]{:S(2)}, u32[]{:S(2)}) collective-permute-start(bf16[704,512]{1,0:T(8,128)(2,1)S(1)} %get-tuple-element.76), channel_id=1, source_target_pairs={{0,2},{2,4},{4,6},{6,0},{1,3},{3,5},{5,7},{7,1},{8,10},{10,12},{12... | collective-permute-start | bytes 2162696 | tf_op jit(solution)/shard_map/ppermute | solution.py:254
  108.6 33.0 %collective-permute-start.24 = (bf16[704,512]{1,0:T(8,128)(2,1)S(1)}, bf16[704,512]{1,0:T(8,128)(2,1)S(1)}, u32[]{:S(2)}, u32[]{:S(2)}) collective-permute-start(bf16[704,512]{1,0:T(8,128)(2,1)S(1)} %get-tuple-element.80), channel_id=1, source_target_pairs={{0,4},{2,6},{4,0},{6,2},{1,5},{3,7},{5,1},{7,3},{8,12},{10,14},{12... | collective-permute-start | bytes 2162696 | tf_op jit(solution)/shard_map/ppermute | solution.py:254
  141.6 19.7 %collective-permute-start.25 = (bf16[3,192,512]{2,1,0:T(8,128)(2,1)S(1)}, bf16[3,192,512]{2,1,0:T(8,128)(2,1)S(1)}, u32[]{:S(2)}, u32[]{:S(2)}) collective-permute-start(bf16[3,192,512]{2,1,0:T(8,128)(2,1)S(1)} %get-tuple-element.83), channel_id=1, source_target_pairs={{0,128},{64,192},{128,0},{192,64},{1,129},{65,193},{129,1},{193,65... | collective-permute-start | bytes 1769480 | tf_op jit(solution)/shard_map/ppermute | solution.py:254
  141.6 26.5 %collective-permute-start.29 = (bf16[3,192,512]{2,1,0:T(8,128)(2,1)S(1)}, bf16[3,192,512]{2,1,0:T(8,128)(2,1)S(1)}, u32[]{:S(2)}, u32[]{:S(2)}) collective-permute-start(bf16[3,192,512]{2,1,0:T(8,128)(2,1)S(1)} %get-tuple-element.93), channel_id=1, source_target_pairs={{0,192},{64,0},{128,64},{192,128},{1,193},{65,1},{129,65},{193,129... | collective-permute-start | bytes 1769480 | tf_op jit(solution)/shard_map/ppermute | solution.py:254
  142.2 28.8 %collective-permute-start.30 = (bf16[3,192,512]{2,1,0:T(8,128)(2,1)S(1)}, bf16[3,192,512]{2,1,0:T(8,128)(2,1)S(1)}, u32[]{:S(2)}, u32[]{:S(2)}) collective-permute-start(bf16[3,192,512]{2,1,0:T(8,128)(2,1)S(1)} %get-tuple-element.94), channel_id=1, source_target_pairs={{0,64},{64,128},{128,192},{192,0},{1,65},{65,129},{129,193},{193,1... | collective-permute-start | bytes 1769480 | tf_op jit(solution)/shard_map/ppermute | solution.py:254
  143.9 11.6 %collective-permute-start.26 = (bf16[176,512]{1,0:T(8,128)(2,1)S(1)}, bf16[176,512]{1,0:T(8,128)(2,1)S(1)}, u32[]{:S(2)}, u32[]{:S(2)}) collective-permute-start(bf16[176,512]{1,0:T(8,128)(2,1)S(1)} %get-tuple-element.84), channel_id=1, source_target_pairs={{0,24},{8,0},{16,8},{24,16},{1,25},{9,1},{17,9},{25,17},{2,26},{10... | collective-permute-start | bytes 540680 | tf_op jit(solution)/shard_map/ppermute | solution.py:254
  150.0 11.2 %collective-permute-start.27 = (bf16[176,512]{1,0:T(8,128)(2,1)S(1)}, bf16[176,512]{1,0:T(8,128)(2,1)S(1)}, u32[]{:S(2)}, u32[]{:S(2)}) collective-permute-start(bf16[176,512]{1,0:T(8,128)(2,1)S(1)} %get-tuple-element.85), channel_id=1, source_target_pairs={{0,8},{8,16},{16,24},{24,0},{1,9},{9,17},{17,25},{25,1},{2,10},{10... | collective-permute-start | bytes 540680 | tf_op jit(solution)/shard_map/ppermute | solution.py:254
  171.0 21.7 %copy-start.5 = (f32[128,2]{0,1:T(2,128)S(1)}, f32[128,2]{0,1:T(2,128)}, u32[]{:S(2)}) copy-start(f32[128,2]{0,1:T(2,128)} %param.7) | copy-start | bytes 3076
  171.3 23.6 %collective-permute-start.31 = (bf16[3,192,512]{2,1,0:T(8,128)(2,1)S(1)}, bf16[3,192,512]{2,1,0:T(8,128)(2,1)S(1)}, u32[]{:S(2)}, u32[]{:S(2)}) collective-permute-start(bf16[3,192,512]{2,1,0:T(8,128)(2,1)S(1)} %add_convert_fusion), channel_id=1, source_target_pairs={{0,0},{1,32},{32,1},{33,33},{2,2},{3,34},{34,3},{35,35},{4,4},{5,3... | collective-permute-start | bytes 1769480 | tf_op jit(solution)/shard_map/ppermute | solution.py:262
  174.2 18.5 %collective-permute-start.28 = (bf16[176,512]{1,0:T(8,128)(2,1)S(1)}, bf16[176,512]{1,0:T(8,128)(2,1)S(1)}, u32[]{:S(2)}, u32[]{:S(2)}) collective-permute-start(bf16[176,512]{1,0:T(8,128)(2,1)S(1)} %get-tuple-element.87), channel_id=1, source_target_pairs={{0,16},{8,24},{16,0},{24,8},{1,17},{9,25},{17,1},{25,9},{2,18},{10... | collective-permute-start | bytes 540680 | tf_op jit(solution)/shard_map/ppermute | solution.py:254

commit v2 on v1

--- a/solution.py
+++ b/solution.py
@@ -83,18 +83,18 @@
 
 
 def fetch(own, other, joined, sems, names, place):
-    half, width = own[0].shape[1:]
+    half, width = own.shape[2:]
     copies = []
-    for i in range(4):
-        spot = lax.rem(place[2] - place[1] + i + 4, 4)
+    for block in range(4):
+        spot = lax.rem(place[2] - place[1] + block + 4, 4)
         columns = pl.ds(pl.multiple_of(spot * width, width), width)
         for n, m in enumerate(names):
-            for h, source in enumerate((own[i], other[i])):
+            for h, source in enumerate((own, other)):
                 copies.append(
                     pltpu.make_async_copy(
-                        source.at[m],
+                        source.at[block, m],
                         joined.at[pl.ds((2 * n + h) * half, half), columns],
-                        sems.at[i, n, h],
+                        sems.at[block, n, h],
                     )
                 )
     for copy in copies:
@@ -102,13 +102,19 @@
     return copies
 
 
-def project_kernel(names, place, *refs):
-    rows, own, other = refs[0:4], refs[4:8], refs[8:12]
-    keep, send, joined, wide, total, sems = refs[12:18]
+def take_rows(target, source, second):
+    for k in range(4):
+        first = (2 * k + second) * CAP
+        target[k * CAP : (k + 1) * CAP, :] = source[first : first + CAP, :]
+
+
+def project_kernel(names, second, place, *refs):
+    rows, own, other = refs[0:4], refs[4], refs[5]
+    keep, send, joined, wide, total, sems = refs[6:12]
     width = rows[0].shape[1]
     copies = fetch(own, other, joined, sems, names, place)
     for j in range(4):
-        wide[:, j * width : (j + 1) * width] = rows[j][...]
+        take_rows(wide.at[:, pl.ds(j * width, width)], rows[j], second)
     for copy in copies:
         copy.wait()
     total[...] = nt(wide[...], joined[...])
@@ -125,12 +131,12 @@
     return high, middle, low
 
 
-def marked_rows(row):
+def marked_rows(row, first):
     spot = lax.broadcasted_iota(jnp.int32, (TILE, row.shape[1]), 0)
-    parts = [part.astype(F32) for part in pieces(row)]
-    total = jnp.where(spot == 0, parts[0], 0.0)
-    total += jnp.where(spot == 1, parts[1], 0.0)
-    return (total + jnp.where(spot == 2, parts[2], 0.0)).astype(BF16)
+    total = jnp.zeros(spot.shape, F32)
+    for n, part in enumerate(pieces(row)):
+        total += jnp.where(spot == first + n, part.astype(F32), 0.0)
+    return total
 
 
 def hidden_kernel(place, both, act, keep, far, out):
@@ -144,14 +150,16 @@
     ).astype(BF16)
     out[0:part, width : 2 * width] = (grad * swish).astype(BF16)
     share = jnp.sum(act[...].astype(F32) * grad, axis=1, keepdims=True)
-    out[part:, :] = jnp.zeros((2 * TILE, out.shape[1]), BF16)
+    out[part:, :] = jnp.zeros((TILE, out.shape[1]), BF16)
+    marks = jnp.zeros((TILE, 128), F32)
     shape = (CAP, 128)
     same = lax.broadcasted_iota(jnp.int32, shape, 0) == lax.broadcasted_iota(jnp.int32, shape, 1)
     for n in range(2):
         row = jnp.sum(
             jnp.where(same, share[n * CAP : (n + 1) * CAP, :], 0.0), axis=0, keepdims=True
         )
-        out[part + n * TILE : part + (n + 1) * TILE, 0:128] = marked_rows(row)
+        marks += marked_rows(row, 6 * place[3] + 3 * n)
+    out[part:, 0:128] = marks.astype(BF16)
 
 
 def join(target, mine, theirs, zl):
@@ -161,14 +169,13 @@
 
 
 def share_kernel(place, act, act_far, grad, grad_far, pair, down, *refs):
-    outs, acts, grads, marks = refs[0:4], *refs[4:7]
+    outs, acts, grads = refs[0:4], *refs[4:6]
     part, width = act.shape[0], outs[0].shape[1]
     zl = place[3]
     join(acts, act, act_far, zl)
     join(grads, grad, grad_far, zl)
-    marks[zl] = grad[part:, 0:128]
-    marks[1 - zl] = grad_far[part:, 0:128]
-    unit = 2 * CAP + TILE
+    marks = grad[part:, 0:128].astype(F32) + grad_far[part:, 0:128].astype(F32)
+    unit = 2 * CAP
     for j in (1, 3, 2, 0):
         kind = outs[j].dtype
         columns = slice(j * width, (j + 1) * width)
@@ -179,46 +186,46 @@
             outs[j][start : start + CAP, :] = out[rows, :].astype(kind)
             outs[j][start + CAP : start + 2 * CAP, :] = back[rows, :].astype(kind)
     for j in range(4):
-        for k in range(4):
-            start = k * unit + 2 * CAP
-            kind = outs[j].dtype
-            rows = marks[k // 2, (k % 2) * TILE : (k % 2 + 1) * TILE, :]
-            outs[j][start : start + TILE, :] = jnp.zeros((TILE, outs[j].shape[1]), kind)
-            outs[j][start : start + TILE, 0:128] = rows.astype(kind)
+        kind = outs[j].dtype
+        outs[j][4 * unit :, :] = jnp.zeros((TILE, width), kind)
+        outs[j][4 * unit :, 0:128] = marks.astype(kind)
 
 
 def total_kernel(place, own, one, three, two, *outs):
-    unit = 2 * CAP + TILE
+    unit = 2 * CAP
+
+    def total(span, columns):
+        value = own[span, columns] + one[span, columns].astype(F32)
+        return value + three[span, columns].astype(F32) + two[span, columns].astype(F32)
+
+    marks = total(slice(4 * unit, 4 * unit + TILE), slice(0, 128))
+    width = own.shape[1]
     for k in range(4):
-        span = pl.ds(k * unit, unit)
-        total = own[span, :] + one[span, :].astype(F32)
-        total += three[span, :].astype(F32) + two[span, :].astype(F32)
-        outs[k][...] = total.astype(BF16)
-        row = jnp.sum(total[2 * CAP :, 0:128], axis=0, keepdims=True)
-        outs[k][2 * CAP :, 0:128] = marked_rows(row)
-
-
-def weight_kernel(place, act, act_far, grad, grad_far, *refs):
-    rows, routed = refs[0:4], refs[4:8]
-    keep, send, acts, grads, turned = refs[8:13]
+        outs[k][0:unit, :] = total(slice(k * unit, (k + 1) * unit), slice(0, width)).astype(BF16)
+        row = jnp.sum(marks[3 * k : 3 * k + 3, :], axis=0, keepdims=True)
+        outs[k][unit:, :] = jnp.zeros((TILE, width), BF16)
+        outs[k][unit:, 0:128] = marked_rows(row, 0).astype(BF16)
+
+
+def weight_kernel(second, place, near, far, *refs):
+    rows, keep, send, joined, chosen = refs[0:4], *refs[4:8]
     half = keep.shape[2]
-    join(acts, act, act_far, place[3])
-    join(grads, grad, grad_far, place[3])
+    join(joined, near, far, place[3])
     for j in range(4):
-        spot = lax.rem(place[1] - place[2] + j + 4, 4)
-        turned[0, spot] = rows[j][...]
-        turned[1, spot] = routed[j][...]
+        block = lax.rem(place[1] - place[2] + j + 4, 4)
+        take_rows(chosen, rows[j], second)
+        total = tn(joined[...], chosen[...])
+        for m in range(keep.shape[1]):
+            keep[block, m] = total[2 * m * half : (2 * m + 1) * half, :]
+            send[block, m] = total[(2 * m + 1) * half : (2 * m + 2) * half, :].astype(BF16)
+
+
+def sum_kernel(place, pair, pair_far, down, down_far, *outs):
     for i in range(4):
-        pair = tn(grads[...], turned[0, i])
-        down = tn(acts[...], turned[1, i])
-        for m, total in enumerate((pair[0 : 2 * half], pair[2 * half :], down)):
-            keep[i, m] = total[0:half, :]
-            send[i, m] = total[half:, :].astype(BF16)
-
-
-def sum_kernel(place, keep, far, *outs):
-    for i in range(4):
-        outs[i][...] = (keep[i] + far[i].astype(F32)).astype(outs[i].dtype)
+        kind = outs[i].dtype
+        for m in range(2):
+            outs[i][m] = (pair[i, m] + pair_far[i, m].astype(F32)).astype(kind)
+        outs[i][2] = (down[i, 0] + down_far[i, 0].astype(F32)).astype(kind)
 
 
 def column(row):
@@ -292,83 +299,82 @@
     )
 
     own, placing = lax.optimization_barrier((turn(stacked_weights[0]), placing))
-    own = [own] + [shift(own, "x", i) for i in (1, 3, 2)]
-    own[2:] = own[:1:-1]
-    other = [swap(block, "core") for block in own]
+    near, back, across = [shift(own, "x", i) for i in (1, 3, 2)]
     blocks = [blocks[0]] + [shift(blocks[k], "expert", k) for k in (1, 2, 3)]
-    token_rows = jnp.concatenate([block[:CAP] for block in blocks], axis=0)
-    routed_rows = jnp.concatenate([block[CAP:] for block in blocks], axis=0)
-    token_rows, other[1], other[3] = lax.optimization_barrier((token_rows, other[1], other[3]))
-    token_rows = [token_rows] + [shift(token_rows, "y", j) for j in (1, 3, 2)]
-    routed_rows = [routed_rows] + [shift(routed_rows, "y", j) for j in (1, 3, 2)]
-    token_rows[2:] = token_rows[:1:-1]
-    routed_rows[2:] = routed_rows[:1:-1]
-
-    def project(names, blocks):
+    blocks[2], near, back = lax.optimization_barrier((blocks[2], near, back))
+    own = jnp.stack([own, near, across, back])
+    blocks = [jnp.concatenate(blocks, axis=0)]
+    blocks += [shift(blocks[0], "y", j) for j in (1, 3, 2)]
+    own, *blocks[1:] = lax.optimization_barrier((own, *blocks[1:]))
+    other = swap(own, "core")
+    blocks[2:] = blocks[:1:-1]
+
+    def project(names, second):
         wide = len(names) * hidden
         return call(
-            functools.partial(project_kernel, names),
+            functools.partial(project_kernel, names, second),
             place,
-            blocks + own + other,
+            blocks + [own, other],
             [((part, wide), F32), ((part, wide), BF16), ((wide, 4 * width), BF16)],
             [
                 pltpu.VMEM((slots, 4 * width), BF16),
                 pltpu.VMEM((slots, wide), F32),
                 pltpu.SemaphoreType.DMA((4, 2, 2)),
             ],
-            [vmem] * 4 + [hbm] * 8,
+            [vmem] * 4 + [hbm] * 2,
         )
 
-    keep, send, pair_weights = project((0, 1), token_rows)
+    keep, send, pair_weights = project((0, 1), 0)
     both = keep + swap(send, "zl").astype(F32)
     gate, up = both[:, :hidden], both[:, hidden:]
     activation = (gate * jax.nn.sigmoid(gate) * up).astype(BF16)
     activation_far = swap(activation, "zl")
-    keep, send, down_weights = project((2,), routed_rows)
+    keep, send, down_weights = project((2,), 1)
     send, activation_far = lax.optimization_barrier((swap(send, "zl"), activation_far))
     hidden_grad = call(
         hidden_kernel,
         place,
         [both, activation, keep, send],
-        [((part + 2 * TILE, 2 * hidden), BF16)],
+        [((part + TILE, 2 * hidden), BF16)],
     )[0]
-    pairs = [activation, activation_far, hidden_grad, swap(hidden_grad, "zl")]
+    hidden_far = swap(hidden_grad, "zl")
+
+    def weight_terms(near, far, second):
+        count = near.shape[1] // hidden
+        shape = (4, count, half, width)
+        return call(
+            functools.partial(weight_kernel, second),
+            place,
+            [near, far] + blocks,
+            [(shape, F32), (shape, BF16)],
+            [pltpu.VMEM((slots, near.shape[1]), BF16), pltpu.VMEM((slots, width), BF16)],
+        )
+
+    down_keep, down_send = weight_terms(activation, activation_far, 1)
+    hidden_far, down_keep = lax.optimization_barrier((hidden_far, down_keep))
 
     unit = 2 * CAP + TILE
-    joined = [pltpu.VMEM((slots, hidden), BF16), pltpu.VMEM((slots, 2 * hidden), BF16)]
     shares = call(
         share_kernel,
         place,
-        pairs + [pair_weights, down_weights],
-        [((4 * unit, width), F32)] + [((4 * unit, width), BF16)] * 3,
-        joined + [pltpu.VMEM((2, 2 * TILE, 128), BF16)],
+        [activation, activation_far, hidden_grad, hidden_far, pair_weights, down_weights],
+        [((8 * CAP + TILE, width), F32)] + [((8 * CAP + TILE, width), BF16)] * 3,
+        [pltpu.VMEM((slots, hidden), BF16), pltpu.VMEM((slots, 2 * hidden), BF16)],
     )
     arrived = [shift(shares[j], "y", -j) for j in (1, 3, 2)]
-    shares[0], pairs[0] = lax.optimization_barrier((shares[0], pairs[0]))
-    keep, send = call(
-        weight_kernel,
-        place,
-        pairs + token_rows + routed_rows,
-        [((4, 3, half, width), F32), ((4, 3, half, width), BF16)],
-        joined + [pltpu.VMEM((2, 4, slots, width), BF16)],
-    )
+    shares[0], hidden_grad = lax.optimization_barrier((shares[0], hidden_grad))
+    pair_keep, pair_send = weight_terms(hidden_grad, hidden_far, 0)
     sums = call(
         sum_kernel,
         place,
-        [keep, swap(send, "core")],
+        [pair_keep, swap(pair_send, "core"), down_keep, swap(down_send, "core")],
         [((3, half, width), F32)] + [((3, half, width), BF16)] * 3,
     )
-    sums = list(sums)
-    sums[1], sums[3], arrived[0], arrived[1] = lax.optimization_barrier(
-        (sums[1], sums[3], arrived[0], arrived[1])
-    )
-    sums[2], arrived[2] = lax.optimization_barrier((sums[2], arrived[2]))
+    sums[2], *arrived[:2] = lax.optimization_barrier((sums[2], *arrived[:2]))
     far_sums = [shift(sums[i], "x", -i) for i in (1, 3, 2)]
+    *far_sums, arrived[2] = lax.optimization_barrier((*far_sums, arrived[2]))
     totals = call(total_kernel, place, [shares[0]] + arrived, [((unit, width), BF16)] * 4)
     returned = [totals[0]] + [shift(totals[k], "expert", -k) for k in (1, 2, 3)]
-    far_sums[2], returned[1], returned[3] = lax.optimization_barrier(
-        (far_sums[2], returned[1], returned[3])
-    )
     layer_output, token_grad, prob_grad = call(
         owner_kernel,
         place,

time: 196 us -> 196 us (level)
  the two profiles are of different devices: /device:TPU:1 before, /device:TPU:25 now
where the time goes in v2:
time: 196 us
  waiting for transfers between devices  117 us (60%)
  starting transfers between devices  45.1 us (23%)
  Pallas kernels  24.1 us (12%)
  local copies, waits for them, and re-layouts  6.34 us (3%)
  other arithmetic  1.99 us (1%)
    ppermute x18, waiting for transfers between devices, shift(): return lax.ppermute(value, axis, [(i, (i + step) % 4) for i in range(4)])  98.7 us
    ppermute x18, starting transfers between devices, shift(): return lax.ppermute(value, axis, [(i, (i + step) % 4) for i in range(4)])  31.8 us
    pallas_call x10, Pallas kernels, call(): pl.pallas_call(kernel, out_shape=[jax.ShapeDtypeStruct(shape, kind) for s...  24.1 us
    ppermute x7, waiting for transfers between devices, swap(): return lax.ppermute(value, axis, [(0, 1), (1, 0)])  15.1 us
    ppermute x2, starting transfers between devices, turn(): lax.ppermute(value, ('core', 'zl'), [(2 * c + z, 2 * z + c) for c in rang...  7.46 us
    ppermute x7, starting transfers between devices, swap(): return lax.ppermute(value, axis, [(0, 1), (1, 0)])  5.82 us
    unnamed x19, local copies, waits for them, and re-layouts  5.77 us
  transfers between devices with their start and end apart: 27, of which 17 were waited for; matrix products, arithmetic and copies ran while one was open for 1% of the time, Pallas kernels for 6%

profile of v2, /device:TPU:25, one launch (start us, length us, event | category | flops | bytes accessed | tf_op | source)
XLA Modules:
  0.0 195.5 jit_solution(9958092424113594191)
XLA Ops:
  0.6 4.1 %collective-permute-start = (bf16[3,192,512]{2,1,0:T(8,128)(2,1)}, bf16[3,192,512]{2,1,0:T(8,128)(2,1)S(1)}, u32[]{:S(2)}, u32[]{:S(2)}) collective-permute-start(bf16[3,192,512]{2,1,0:T(8,128)(2,1)} %bitcast.24), channel_id=1, source_target_pairs={{0,0},{1,32},{32,1},{33,33},{2,2},{3,34},{34,3},{35,35},{4,4},{5,3... | collective-permute-start | bytes 1769480 | tf_op jit(solution)/shard_map/ppermute | solution.py:269
  4.8 0.9 copy-done.2
  5.7 0.9 copy-done.3
  6.6 0.7 copy-done.4
  8.0 1.5 shard_map.84
  9.5 3.3 %collective-permute-done = bf16[3,192,512]{2,1,0:T(8,128)(2,1)S(1)} collective-permute-done((bf16[3,192,512]{2,1,0:T(8,128)(2,1)}, bf16[3,192,512]{2,1,0:T(8,128)(2,1)S(1)}, u32[]{:S(2)}, u32[]{:S(2)}) %collective-permute-start) | collective-permute-done | bytes 589856 | tf_op jit(solution)/shard_map/ppermute | solution.py:269
  12.8 2.5 %collective-permute-start.4 = (bf16[3,192,512]{2,1,0:T(8,128)(2,1)S(1)}, bf16[3,192,512]{2,1,0:T(8,128)(2,1)S(1)}, u32[]{:S(2)}, u32[]{:S(2)}) collective-permute-start(bf16[3,192,512]{2,1,0:T(8,128)(2,1)S(1)} %collective-permute-done), channel_id=1, source_target_pairs={{0,192},{64,0},{128,64},{192,128},{1,193},{65,1},{129,65},{193,129... | collective-permute-start | bytes 1769480 | tf_op jit(solution)/shard_map/ppermute | solution.py:261
  15.3 3.0 %collective-permute-start.1 = (bf16[160,512]{1,0:T(8,128)(2,1)S(1)}, bf16[160,512]{1,0:T(8,128)(2,1)S(1)}, u32[]{:S(2)}, u32[]{:S(2)}) collective-permute-start(bf16[160,512]{1,0:T(8,128)(2,1)S(1)} %get-tuple-element.59), channel_id=1, source_target_pairs={{0,8},{8,16},{16,24},{24,0},{1,9},{9,17},{17,25},{25,1},{2,10},{10... | collective-permute-start | bytes 491528 | tf_op jit(solution)/shard_map/ppermute | solution.py:261
  18.3 4.6 %collective-permute-start.2 = (bf16[160,512]{1,0:T(8,128)(2,1)S(1)}, bf16[160,512]{1,0:T(8,128)(2,1)S(1)}, u32[]{:S(2)}, u32[]{:S(2)}) collective-permute-start(bf16[160,512]{1,0:T(8,128)(2,1)S(1)} %get-tuple-element.60), channel_id=1, source_target_pairs={{0,16},{8,24},{16,0},{24,8},{1,17},{9,25},{17,1},{25,9},{2,18},{10... | collective-permute-start | bytes 491528 | tf_op jit(solution)/shard_map/ppermute | solution.py:261
  22.9 2.4 %collective-permute-start.5 = (bf16[160,512]{1,0:T(8,128)(2,1)S(1)}, bf16[160,512]{1,0:T(8,128)(2,1)S(1)}, u32[]{:S(2)}, u32[]{:S(2)}) collective-permute-start(bf16[160,512]{1,0:T(8,128)(2,1)S(1)} %get-tuple-element.63), channel_id=1, source_target_pairs={{0,24},{8,0},{16,8},{24,16},{1,25},{9,1},{17,9},{25,17},{2,26},{10... | collective-permute-start | bytes 491528 | tf_op jit(solution)/shard_map/ppermute | solution.py:261
  25.4 1.8 collective-permute-start.6
  27.2 5.6 %collective-permute-done.2 = bf16[160,512]{1,0:T(8,128)(2,1)S(1)} collective-permute-done((bf16[160,512]{1,0:T(8,128)(2,1)S(1)}, bf16[160,512]{1,0:T(8,128)(2,1)S(1)}, u32[]{:S(2)}, u32[]{:S(2)}) %collective-permute-start.2) | collective-permute-done | bytes 163872 | tf_op jit(solution)/shard_map/ppermute | solution.py:261
  32.7 7.6 %collective-permute-done.3 = bf16[3,192,512]{2,1,0:T(8,128)(2,1)S(1)} collective-permute-done((bf16[3,192,512]{2,1,0:T(8,128)(2,1)S(1)}, bf16[3,192,512]{2,1,0:T(8,128)(2,1)S(1)}, u32[]{:S(2)}, u32[]{:S(2)}) %collective-permute-start.3) | collective-permute-done | bytes 589856 | tf_op jit(solution)/shard_map/ppermute | solution.py:261
  40.3 0.9 collective-permute-start.9
  41.2 2.7 %collective-permute-start.7 = (bf16[640,512]{1,0:T(8,128)(2,1)S(1)}, bf16[640,512]{1,0:T(8,128)(2,1)S(1)}, u32[]{:S(2)}, u32[]{:S(2)}) collective-permute-start(bf16[640,512]{1,0:T(8,128)(2,1)S(1)} %constant_dynamic-update-slice_fusion.refs_0_), channel_id=1, source_target_pairs={{0,2},{2,4},{4,6},{6,0},{1,3},{3,5},{5,7},{7,1},{8,10},{10,12},{12... | collective-permute-start | bytes 1966088 | tf_op jit(solution)/shard_map/ppermute | solution.py:261
  44.2 11.4 %collective-permute-done.9.refs_2_ = bf16[640,512]{1,0:T(8,128)(2,1)S(1)} collective-permute-done((bf16[640,512]{1,0:T(8,128)(2,1)S(1)}, bf16[640,512]{1,0:T(8,128)(2,1)S(1)}, u32[]{:S(2)}, u32[]{:S(2)}) %collective-permute-start.9) | collective-permute-done | bytes 655392 | tf_op jit(solution)/shard_map/ppermute | solution.py:261
  55.6 6.9 %collective-permute-done.8.refs_3_ = bf16[640,512]{1,0:T(8,128)(2,1)S(1)} collective-permute-done((bf16[640,512]{1,0:T(8,128)(2,1)S(1)}, bf16[640,512]{1,0:T(8,128)(2,1)S(1)}, u32[]{:S(2)}, u32[]{:S(2)}) %collective-permute-start.8) | collective-permute-done | bytes 655392 | tf_op jit(solution)/shard_map/ppermute | solution.py:261
  62.5 4.5 %collective-permute-done.10.refs_5_ = bf16[4,3,192,512]{3,2,1,0:T(8,128)(2,1)S(1)} collective-permute-done((bf16[4,3,192,512]{3,2,1,0:T(8,128)(2,1)S(1)}, bf16[4,3,192,512]{3,2,1,0:T(8,128)(2,1)S(1)}, u32[]{:S(2)}, u32[]{:S(2)}) %collective-permute-start.10) | collective-permute-done | bytes 2359328 | tf_op jit(solution)/shard_map/ppermute | solution.py:265
  67.1 1.4 copy-done.7
  68.5 3.9 %shard_map.85 = (f32[160,768]{1,0:T(8,128)S(1)}, bf16[160,768]{1,0:T(8,128)(2,1)S(1)}, bf16[768,2048]{1,0:T(8,128)(2,1)}) custom-call(s32[4]{0:T(128)S(1)} %pad_add_fusion.place, bf16[640,512]{1,0:T(8,128)(2,1)S(1)} %constant_dynamic-update-slice_fusion.refs_0_, bf16[640,512]{1,0:T(8,128)(2,1)S(1)} %collective-permute-done.7.refs_1_, ...), custom_call_target="tpu_custom_call" | custom-call | tf_op jit(solution)/shard_map/pallas_call | solution.py:31
  72.4 3.0 %shard_map.86 = (f32[160,384]{1,0:T(8,128)S(1)}, bf16[160,384]{1,0:T(8,128)(2,1)S(1)}, bf16[384,2048]{1,0:T(8,128)(2,1)S(1)}) custom-call(s32[4]{0:T(128)S(1)} %pad_add_fusion.place, bf16[640,512]{1,0:T(8,128)(2,1)S(1)} %constant_dynamic-update-slice_fusion.refs_0_, bf16[640,512]{1,0:T(8,128)(2,1)S(1)} %collective-permute-done.7.refs_1_, ...), custom_call_target="tpu_custom_call" | custom-call | tf_op jit(solution)/shard_map/pallas_call | solution.py:31
  75.5 1.5 collective-permute-start.12
  77.0 2.8 %collective-permute-done.11 = bf16[160,768]{1,0:T(8,128)(2,1)S(1)} collective-permute-done((bf16[160,768]{1,0:T(8,128)(2,1)S(1)}, bf16[160,768]{1,0:T(8,128)(2,1)S(1)}, u32[]{:S(2)}, u32[]{:S(2)}) %collective-permute-start.11) | collective-permute-done | bytes 245792 | tf_op jit(solution)/shard_map/ppermute | solution.py:265
  80.3 2.2 %collective-permute-done.12.far = bf16[160,384]{1,0:T(8,128)(2,1)S(1)} collective-permute-done((bf16[160,384]{1,0:T(8,128)(2,1)S(1)}, bf16[160,384]{1,0:T(8,128)(2,1)S(1)}, u32[]{:S(2)}, u32[]{:S(2)}) %collective-permute-start.12) | collective-permute-done | bytes 122912 | tf_op jit(solution)/shard_map/ppermute | solution.py:265
  82.5 1.6 collective-permute-done.13.far.act_far
  84.1 0.8 shard_map.87.grad.near
  85.1 1.6 shard_map.88
  86.7 1.1 copy-done.1
  87.9 2.5 %collective-permute-done.14.grad_far.far = bf16[176,768]{1,0:T(8,128)(2,1)S(1)} collective-permute-done((bf16[176,768]{1,0:T(8,128)(2,1)S(1)}, bf16[176,768]{1,0:T(8,128)(2,1)S(1)}, u32[]{:S(2)}, u32[]{:S(2)}) %collective-permute-start.14) | collective-permute-done | bytes 270368 | tf_op jit(solution)/shard_map/ppermute | solution.py:265
  90.4 3.8 %shard_map.89 = (f32[656,512]{1,0:T(8,128)S(1)}, bf16[656,512]{1,0:T(8,128)(2,1)S(1)}, bf16[656,512]{1,0:T(8,128)(2,1)S(1)}, bf16[656,512]{1,0:T(8,128)(2,1)S(1)}) custom-call(s32[4]{0:T(128)S(1)} %pad_add_fusion.place, bf16[160,384]{1,0:T(8,128)(2,1)S(1)} %fusion.act.near, bf16[160,384]{1,0:T(8,128)(2,1)S(1)} %collective-permute-done.13.far.act_far, ...), custom_call_target="tpu_custom_call" | custom-call | tf_op jit(solution)/shard_map/pallas_call | solution.py:31
  94.2 4.0 %shard_map.90 = (f32[4,2,192,512]{3,2,1,0:T(8,128)}, bf16[4,2,192,512]{3,2,1,0:T(8,128)(2,1)S(1)}) custom-call(s32[4]{0:T(128)S(1)} %pad_add_fusion.place, bf16[176,768]{1,0:T(8,128)(2,1)S(1)} %shard_map.87.grad.near, bf16[176,768]{1,0:T(8,128)(2,1)S(1)} %collective-permute-done.14.grad_far.far, ...), custom_call_target="tpu_custom_call" | custom-call | tf_op jit(solution)/shard_map/pallas_call | solution.py:31
  98.2 3.6 %collective-permute-start.15 = (bf16[4,2,192,512]{3,2,1,0:T(8,128)(2,1)S(1)}, bf16[4,2,192,512]{3,2,1,0:T(8,128)(2,1)S(1)}, u32[]{:S(2)}, u32[]{:S(2)}) collective-permute-start(bf16[4,2,192,512]{3,2,1,0:T(8,128)(2,1)S(1)} %get-tuple-element.84), channel_id=1, source_target_pairs={{0,32},{32,0},{1,33},{33,1},{2,34},{34,2},{3,35},{35,3},{4,36},{36... | collective-permute-start | bytes 4718600 | tf_op jit(solution)/shard_map/ppermute | solution.py:265
  102.3 2.2 %collective-permute-start.18 = (bf16[656,512]{1,0:T(8,128)(2,1)S(1)}, bf16[656,512]{1,0:T(8,128)(2,1)S(1)}, u32[]{:S(2)}, u32[]{:S(2)}) collective-permute-start(bf16[656,512]{1,0:T(8,128)(2,1)S(1)} %get-tuple-element.89), channel_id=1, source_target_pairs={{0,2},{2,4},{4,6},{6,0},{1,3},{3,5},{5,7},{7,1},{8,10},{10,12},{12... | collective-permute-start | bytes 2015240 | tf_op jit(solution)/shard_map/ppermute | solution.py:261
  104.5 1.5 collective-permute-done.16.down_far
  106.0 3.0 %shard_map.91 = (f32[3,192,512]{2,1,0:T(8,128)S(1)}, bf16[3,192,512]{2,1,0:T(8,128)(2,1)S(1)}, bf16[3,192,512]{2,1,0:T(8,128)(2,1)S(1)}, bf16[3,192,512]{2,1,0:T(8,128)(2,1)S(1)}) custom-call(s32[4]{0:T(128)S(1)} %pad_add_fusion.place, f32[4,2,192,512]{3,2,1,0:T(8,128)} %get-tuple-element.83.pair, ...), custom_call_target="tpu_custom_call" | custom-call | tf_op jit(solution)/shard_map/pallas_call | solution.py:31
  108.9 24.6 %collective-permute-done.17.one = bf16[656,512]{1,0:T(8,128)(2,1)S(1)} collective-permute-done((bf16[656,512]{1,0:T(8,128)(2,1)S(1)}, bf16[656,512]{1,0:T(8,128)(2,1)S(1)}, u32[]{:S(2)}, u32[]{:S(2)}) %collective-permute-start.17) | collective-permute-done | bytes 671776 | tf_op jit(solution)/shard_map/ppermute | solution.py:261
  133.6 2.7 %collective-permute-start.21 = (bf16[3,192,512]{2,1,0:T(8,128)(2,1)S(1)}, bf16[3,192,512]{2,1,0:T(8,128)(2,1)S(1)}, u32[]{:S(2)}, u32[]{:S(2)}) collective-permute-start(bf16[3,192,512]{2,1,0:T(8,128)(2,1)S(1)} %get-tuple-element.94), channel_id=1, source_target_pairs={{0,128},{64,192},{128,0},{192,64},{1,129},{65,193},{129,1},{193,65... | collective-permute-start | bytes 1769480 | tf_op jit(solution)/shard_map/ppermute | solution.py:261
  136.2 0.9 collective-permute-start.19
  137.7 10.8 %collective-permute-done.21 = bf16[3,192,512]{2,1,0:T(8,128)(2,1)S(1)} collective-permute-done((bf16[3,192,512]{2,1,0:T(8,128)(2,1)S(1)}, bf16[3,192,512]{2,1,0:T(8,128)(2,1)S(1)}, u32[]{:S(2)}, u32[]{:S(2)}) %collective-permute-start.21) | collective-permute-done | bytes 589856 | tf_op jit(solution)/shard_map/ppermute | solution.py:261
  148.6 13.9 %collective-permute-done.19 = bf16[3,192,512]{2,1,0:T(8,128)(2,1)S(1)} collective-permute-done((bf16[3,192,512]{2,1,0:T(8,128)(2,1)S(1)}, bf16[3,192,512]{2,1,0:T(8,128)(2,1)S(1)}, u32[]{:S(2)}, u32[]{:S(2)}) %collective-permute-start.19) | collective-permute-done | bytes 589856 | tf_op jit(solution)/shard_map/ppermute | solution.py:261
  163.3 3.4 %collective-permute-start.26 = (bf16[3,192,512]{2,1,0:T(8,128)(2,1)S(1)}, bf16[3,192,512]{2,1,0:T(8,128)(2,1)S(1)}, u32[]{:S(2)}, u32[]{:S(2)}) collective-permute-start(bf16[3,192,512]{2,1,0:T(8,128)(2,1)S(1)} %add_convert_fusion), channel_id=1, source_target_pairs={{0,0},{1,32},{32,1},{33,33},{2,2},{3,34},{34,3},{35,35},{4,4},{5,3... | collective-permute-start | bytes 1769480 | tf_op jit(solution)/shard_map/ppermute | solution.py:269
  166.7 0.8 shard_map.92
  167.5 1.8 collective-permute-start.23
  169.3 3.1 %collective-permute-start.24 = (bf16[176,512]{1,0:T(8,128)(2,1)S(1)}, bf16[176,512]{1,0:T(8,128)(2,1)S(1)}, u32[]{:S(2)}, u32[]{:S(2)}) collective-permute-start(bf16[176,512]{1,0:T(8,128)(2,1)S(1)} %get-tuple-element.99), channel_id=1, source_target_pairs={{0,16},{8,24},{16,0},{24,8},{1,17},{9,25},{17,1},{25,9},{2,18},{10... | collective-permute-start | bytes 540680 | tf_op jit(solution)/shard_map/ppermute | solution.py:261
  172.3 2.3 %collective-permute-start.25 = (bf16[176,512]{1,0:T(8,128)(2,1)S(1)}, bf16[176,512]{1,0:T(8,128)(2,1)S(1)}, u32[]{:S(2)}, u32[]{:S(2)}) collective-permute-start(bf16[176,512]{1,0:T(8,128)(2,1)S(1)} %get-tuple-element.100), channel_id=1, source_target_pairs={{0,8},{8,16},{16,24},{24,0},{1,9},{9,17},{17,25},{25,1},{2,10},{10... | collective-permute-start | bytes 540680 | tf_op jit(solution)/shard_map/ppermute | solution.py:261
  175.0 17.1 %collective-permute-done.24.refs_2_ = bf16[176,512]{1,0:T(8,128)(2,1)S(1)} collective-permute-done((bf16[176,512]{1,0:T(8,128)(2,1)S(1)}, bf16[176,512]{1,0:T(8,128)(2,1)S(1)}, u32[]{:S(2)}, u32[]{:S(2)}) %collective-permute-start.24) | collective-permute-done | bytes 180256 | tf_op jit(solution)/shard_map/ppermute | solution.py:261
  192.1 1.7 shard_map.93
  194.3 1.2 bitcast_convert_fusion
  (43 shorter events, 4.8 us)
Async XLA Ops:
  0.6 12.2 %collective-permute-start = (bf16[3,192,512]{2,1,0:T(8,128)(2,1)}, bf16[3,192,512]{2,1,0:T(8,128)(2,1)S(1)}, u32[]{:S(2)}, u32[]{:S(2)}) collective-permute-start(bf16[3,192,512]{2,1,0:T(8,128)(2,1)} %bitcast.24), channel_id=1, source_target_pairs={{0,0},{1,32},{32,1},{33,33},{2,2},{3,34},{34,3},{35,35},{4,4},{5,3... | collective-permute-start | bytes 1769480 | tf_op jit(solution)/shard_map/ppermute | solution.py:269
  4.8 0.9 copy-start.2
  5.7 0.9 copy-start.3
  6.6 0.7 copy-start.4
  7.3 0.7 copy-start.5
  12.8 19.9 %collective-permute-start.4 = (bf16[3,192,512]{2,1,0:T(8,128)(2,1)S(1)}, bf16[3,192,512]{2,1,0:T(8,128)(2,1)S(1)}, u32[]{:S(2)}, u32[]{:S(2)}) collective-permute-start(bf16[3,192,512]{2,1,0:T(8,128)(2,1)S(1)} %collective-permute-done), channel_id=1, source_target_pairs={{0,192},{64,0},{128,64},{192,128},{1,193},{65,1},{129,65},{193,129... | collective-permute-start | bytes 1769480 | tf_op jit(solution)/shard_map/ppermute | solution.py:261
  15.3 25.0 %collective-permute-start.3 = (bf16[3,192,512]{2,1,0:T(8,128)(2,1)S(1)}, bf16[3,192,512]{2,1,0:T(8,128)(2,1)S(1)}, u32[]{:S(2)}, u32[]{:S(2)}) collective-permute-start(bf16[3,192,512]{2,1,0:T(8,128)(2,1)S(1)} %collective-permute-done), channel_id=1, source_target_pairs={{0,64},{64,128},{128,192},{192,0},{1,65},{65,129},{129,193},{193,1... | collective-permute-start | bytes 1769480 | tf_op jit(solution)/shard_map/ppermute | solution.py:261
  15.3 10.0 %collective-permute-start.1 = (bf16[160,512]{1,0:T(8,128)(2,1)S(1)}, bf16[160,512]{1,0:T(8,128)(2,1)S(1)}, u32[]{:S(2)}, u32[]{:S(2)}) collective-permute-start(bf16[160,512]{1,0:T(8,128)(2,1)S(1)} %get-tuple-element.59), channel_id=1, source_target_pairs={{0,8},{8,16},{16,24},{24,0},{1,9},{9,17},{17,25},{25,1},{2,10},{10... | collective-permute-start | bytes 491528 | tf_op jit(solution)/shard_map/ppermute | solution.py:261
  18.3 14.5 %collective-permute-start.2 = (bf16[160,512]{1,0:T(8,128)(2,1)S(1)}, bf16[160,512]{1,0:T(8,128)(2,1)S(1)}, u32[]{:S(2)}, u32[]{:S(2)}) collective-permute-start(bf16[160,512]{1,0:T(8,128)(2,1)S(1)} %get-tuple-element.60), channel_id=1, source_target_pairs={{0,16},{8,24},{16,0},{24,8},{1,17},{9,25},{17,1},{25,9},{2,18},{10... | collective-permute-start | bytes 491528 | tf_op jit(solution)/shard_map/ppermute | solution.py:261
  22.9 17.4 %collective-permute-start.5 = (bf16[160,512]{1,0:T(8,128)(2,1)S(1)}, bf16[160,512]{1,0:T(8,128)(2,1)S(1)}, u32[]{:S(2)}, u32[]{:S(2)}) collective-permute-start(bf16[160,512]{1,0:T(8,128)(2,1)S(1)} %get-tuple-element.63), channel_id=1, source_target_pairs={{0,24},{8,0},{16,8},{24,16},{1,25},{9,1},{17,9},{25,17},{2,26},{10... | collective-permute-start | bytes 491528 | tf_op jit(solution)/shard_map/ppermute | solution.py:261
  25.4 18.5 %collective-permute-start.6 = (bf16[3,192,512]{2,1,0:T(8,128)(2,1)S(1)}, bf16[3,192,512]{2,1,0:T(8,128)(2,1)S(1)}, u32[]{:S(2)}, u32[]{:S(2)}) collective-permute-start(bf16[3,192,512]{2,1,0:T(8,128)(2,1)S(1)} %collective-permute-done), channel_id=1, source_target_pairs={{0,128},{64,192},{128,0},{192,64},{1,129},{65,193},{129,1},{193,65... | collective-permute-start | bytes 1769480 | tf_op jit(solution)/shard_map/ppermute | solution.py:261
  40.3 15.3 %collective-permute-start.9 = (bf16[640,512]{1,0:T(8,128)(2,1)S(1)}, bf16[640,512]{1,0:T(8,128)(2,1)S(1)}, u32[]{:S(2)}, u32[]{:S(2)}) collective-permute-start(bf16[640,512]{1,0:T(8,128)(2,1)S(1)} %constant_dynamic-update-slice_fusion.refs_0_), channel_id=1, source_target_pairs={{0,4},{2,6},{4,0},{6,2},{1,5},{3,7},{5,1},{7,3},{8,12},{10,14},{12... | collective-permute-start | bytes 1966088 | tf_op jit(solution)/shard_map/ppermute | solution.py:261
  41.2 21.3 %collective-permute-start.8 = (bf16[640,512]{1,0:T(8,128)(2,1)S(1)}, bf16[640,512]{1,0:T(8,128)(2,1)S(1)}, u32[]{:S(2)}, u32[]{:S(2)}) collective-permute-start(bf16[640,512]{1,0:T(8,128)(2,1)S(1)} %constant_dynamic-update-slice_fusion.refs_0_), channel_id=1, source_target_pairs={{0,6},{2,0},{4,2},{6,4},{1,7},{3,1},{5,3},{7,5},{8,14},{10,8},{12,... | collective-permute-start | bytes 1966088 | tf_op jit(solution)/shard_map/ppermute | solution.py:261
  41.2 21.3 %collective-permute-start.7 = (bf16[640,512]{1,0:T(8,128)(2,1)S(1)}, bf16[640,512]{1,0:T(8,128)(2,1)S(1)}, u32[]{:S(2)}, u32[]{:S(2)}) collective-permute-start(bf16[640,512]{1,0:T(8,128)(2,1)S(1)} %constant_dynamic-update-slice_fusion.refs_0_), channel_id=1, source_target_pairs={{0,2},{2,4},{4,6},{6,0},{1,3},{3,5},{5,7},{7,1},{8,10},{10,12},{12... | collective-permute-start | bytes 1966088 | tf_op jit(solution)/shard_map/ppermute | solution.py:261
  44.2 28.1 %copy-start = (bf16[4,3,192,512]{3,2,1,0:T(8,128)(2,1)}, bf16[4,3,192,512]{3,2,1,0:T(8,128)(2,1)S(1)}, u32[]{:S(2)}) copy-start(bf16[4,3,192,512]{3,2,1,0:T(8,128)(2,1)S(1)} %pad_maximum_fusion.refs_4_) | copy-start | bytes 7077892
  62.5 4.5 %collective-permute-start.10 = (bf16[4,3,192,512]{3,2,1,0:T(8,128)(2,1)S(1)}, bf16[4,3,192,512]{3,2,1,0:T(8,128)(2,1)S(1)}, u32[]{:S(2)}, u32[]{:S(2)}) collective-permute-start(bf16[4,3,192,512]{3,2,1,0:T(8,128)(2,1)S(1)} %pad_maximum_fusion.refs_4_), channel_id=1, source_target_pairs={{0,32},{32,0},{1,33},{33,1},{2,34},{34,2},{3,35},{35,3},{4,36},{36... | collective-permute-start | bytes 7077896 | tf_op jit(solution)/shard_map/ppermute | solution.py:265
  67.1 1.4 copy-start.7
  72.3 7.5 %collective-permute-start.11 = (bf16[160,768]{1,0:T(8,128)(2,1)S(1)}, bf16[160,768]{1,0:T(8,128)(2,1)S(1)}, u32[]{:S(2)}, u32[]{:S(2)}) collective-permute-start(bf16[160,768]{1,0:T(8,128)(2,1)S(1)} %get-tuple-element.71), channel_id=1, source_target_pairs={{0,1},{1,0},{2,3},{3,2},{4,5},{5,4},{6,7},{7,6},{8,9},{9,8},{10,11... | collective-permute-start | bytes 737288 | tf_op jit(solution)/shard_map/ppermute | solution.py:265
  75.5 7.0 %collective-permute-start.12 = (bf16[160,384]{1,0:T(8,128)(2,1)S(1)}, bf16[160,384]{1,0:T(8,128)(2,1)S(1)}, u32[]{:S(2)}, u32[]{:S(2)}) collective-permute-start(bf16[160,384]{1,0:T(8,128)(2,1)S(1)} %get-tuple-element.72), channel_id=1, source_target_pairs={{0,1},{1,0},{2,3},{3,2},{4,5},{5,4},{6,7},{7,6},{8,9},{9,8},{10,11... | collective-permute-start | bytes 368648 | tf_op jit(solution)/shard_map/ppermute | solution.py:265
  80.0 4.1 %collective-permute-start.13 = (bf16[160,384]{1,0:T(8,128)(2,1)S(1)}, bf16[160,384]{1,0:T(8,128)(2,1)S(1)}, u32[]{:S(2)}, u32[]{:S(2)}) collective-permute-start(bf16[160,384]{1,0:T(8,128)(2,1)S(1)} %fusion.act.near), channel_id=1, source_target_pairs={{0,1},{1,0},{2,3},{3,2},{4,5},{5,4},{6,7},{7,6},{8,9},{9,8},{10,11... | collective-permute-start | bytes 368648 | tf_op jit(solution)/shard_map/ppermute | solution.py:265
  84.8 5.6 %collective-permute-start.14 = (bf16[176,768]{1,0:T(8,128)(2,1)S(1)}, bf16[176,768]{1,0:T(8,128)(2,1)S(1)}, u32[]{:S(2)}, u32[]{:S(2)}) collective-permute-start(bf16[176,768]{1,0:T(8,128)(2,1)S(1)} %shard_map.87.grad.near), channel_id=1, source_target_pairs={{0,1},{1,0},{2,3},{3,2},{4,5},{5,4},{6,7},{7,6},{8,9},{9,8},{10,11... | collective-permute-start | bytes 811016 | tf_op jit(solution)/shard_map/ppermute | solution.py:265
  86.7 1.1 copy-start.1
  98.2 7.7 %collective-permute-start.15 = (bf16[4,2,192,512]{3,2,1,0:T(8,128)(2,1)S(1)}, bf16[4,2,192,512]{3,2,1,0:T(8,128)(2,1)S(1)}, u32[]{:S(2)}, u32[]{:S(2)}) collective-permute-start(bf16[4,2,192,512]{3,2,1,0:T(8,128)(2,1)S(1)} %get-tuple-element.84), channel_id=1, source_target_pairs={{0,32},{32,0},{1,33},{33,1},{2,34},{34,2},{3,35},{35,3},{4,36},{36... | collective-permute-start | bytes 4718600 | tf_op jit(solution)/shard_map/ppermute | solution.py:265
  101.8 4.2 %collective-permute-start.16 = (bf16[4,1,192,512]{3,2,1,0:T(8,128)(2,1)S(1)}, bf16[4,1,192,512]{3,2,1,0:T(8,128)(2,1)S(1)}, u32[]{:S(2)}, u32[]{:S(2)}) collective-permute-start(bf16[4,1,192,512]{3,2,1,0:T(8,128)(2,1)S(1)} %get-tuple-element.86), channel_id=1, source_target_pairs={{0,32},{32,0},{1,33},{33,1},{2,34},{34,2},{3,35},{35,3},{4,36},{36... | collective-permute-start | bytes 2359304 | tf_op jit(solution)/shard_map/ppermute | solution.py:265
  101.8 31.7 %collective-permute-start.17 = (bf16[656,512]{1,0:T(8,128)(2,1)S(1)}, bf16[656,512]{1,0:T(8,128)(2,1)S(1)}, u32[]{:S(2)}, u32[]{:S(2)}) collective-permute-start(bf16[656,512]{1,0:T(8,128)(2,1)S(1)} %get-tuple-element.88), channel_id=1, source_target_pairs={{0,6},{2,0},{4,2},{6,4},{1,7},{3,1},{5,3},{7,5},{8,14},{10,8},{12,... | collective-permute-start | bytes 2015240 | tf_op jit(solution)/shard_map/ppermute | solution.py:261
  102.3 31.3 %collective-permute-start.18 = (bf16[656,512]{1,0:T(8,128)(2,1)S(1)}, bf16[656,512]{1,0:T(8,128)(2,1)S(1)}, u32[]{:S(2)}, u32[]{:S(2)}) collective-permute-start(bf16[656,512]{1,0:T(8,128)(2,1)S(1)} %get-tuple-element.89), channel_id=1, source_target_pairs={{0,2},{2,4},{4,6},{6,0},{1,3},{3,5},{5,7},{7,1},{8,10},{10,12},{12... | collective-permute-start | bytes 2015240 | tf_op jit(solution)/shard_map/ppermute | solution.py:261
  104.5 33.3 %collective-permute-start.22 = (bf16[656,512]{1,0:T(8,128)(2,1)S(1)}, bf16[656,512]{1,0:T(8,128)(2,1)S(1)}, u32[]{:S(2)}, u32[]{:S(2)}) collective-permute-start(bf16[656,512]{1,0:T(8,128)(2,1)S(1)} %get-tuple-element.95), channel_id=1, source_target_pairs={{0,4},{2,6},{4,0},{6,2},{1,5},{3,7},{5,1},{7,3},{8,12},{10,14},{12... | collective-permute-start | bytes 2015240 | tf_op jit(solution)/shard_map/ppermute | solution.py:261
  133.6 15.0 %collective-permute-start.21 = (bf16[3,192,512]{2,1,0:T(8,128)(2,1)S(1)}, bf16[3,192,512]{2,1,0:T(8,128)(2,1)S(1)}, u32[]{:S(2)}, u32[]{:S(2)}) collective-permute-start(bf16[3,192,512]{2,1,0:T(8,128)(2,1)S(1)} %get-tuple-element.94), channel_id=1, source_target_pairs={{0,128},{64,192},{128,0},{192,64},{1,129},{65,193},{129,1},{193,65... | collective-permute-start | bytes 1769480 | tf_op jit(solution)/shard_map/ppermute | solution.py:261
  136.2 26.3 %collective-permute-start.19 = (bf16[3,192,512]{2,1,0:T(8,128)(2,1)S(1)}, bf16[3,192,512]{2,1,0:T(8,128)(2,1)S(1)}, u32[]{:S(2)}, u32[]{:S(2)}) collective-permute-start(bf16[3,192,512]{2,1,0:T(8,128)(2,1)S(1)} %get-tuple-element.92), channel_id=1, source_target_pairs={{0,192},{64,0},{128,64},{192,128},{1,193},{65,1},{129,65},{193,129... | collective-permute-start | bytes 1769480 | tf_op jit(solution)/shard_map/ppermute | solution.py:261
  137.2 25.8 %collective-permute-start.20 = (bf16[3,192,512]{2,1,0:T(8,128)(2,1)S(1)}, bf16[3,192,512]{2,1,0:T(8,128)(2,1)S(1)}, u32[]{:S(2)}, u32[]{:S(2)}) collective-permute-start(bf16[3,192,512]{2,1,0:T(8,128)(2,1)S(1)} %get-tuple-element.93), channel_id=1, source_target_pairs={{0,64},{64,128},{128,192},{192,0},{1,65},{65,129},{129,193},{193,1... | collective-permute-start | bytes 1769480 | tf_op jit(solution)/shard_map/ppermute | solution.py:261
  163.3 28.8 %copy-start.6 = (f32[128,2]{0,1:T(2,128)S(1)}, f32[128,2]{0,1:T(2,128)}, u32[]{:S(2)}) copy-start(f32[128,2]{0,1:T(2,128)} %param.7) | copy-start | bytes 3076
  163.3 31.0 %collective-permute-start.26 = (bf16[3,192,512]{2,1,0:T(8,128)(2,1)S(1)}, bf16[3,192,512]{2,1,0:T(8,128)(2,1)S(1)}, u32[]{:S(2)}, u32[]{:S(2)}) collective-permute-start(bf16[3,192,512]{2,1,0:T(8,128)(2,1)S(1)} %add_convert_fusion), channel_id=1, source_target_pairs={{0,0},{1,32},{32,1},{33,33},{2,2},{3,34},{34,3},{35,35},{4,4},{5,3... | collective-permute-start | bytes 1769480 | tf_op jit(solution)/shard_map/ppermute | solution.py:269
  167.5 7.5 %collective-permute-start.23 = (bf16[176,512]{1,0:T(8,128)(2,1)S(1)}, bf16[176,512]{1,0:T(8,128)(2,1)S(1)}, u32[]{:S(2)}, u32[]{:S(2)}) collective-permute-start(bf16[176,512]{1,0:T(8,128)(2,1)S(1)} %get-tuple-element.98), channel_id=1, source_target_pairs={{0,24},{8,0},{16,8},{24,16},{1,25},{9,1},{17,9},{25,17},{2,26},{10... | collective-permute-start | bytes 540680 | tf_op jit(solution)/shard_map/ppermute | solution.py:261
  169.3 22.8 %collective-permute-start.24 = (bf16[176,512]{1,0:T(8,128)(2,1)S(1)}, bf16[176,512]{1,0:T(8,128)(2,1)S(1)}, u32[]{:S(2)}, u32[]{:S(2)}) collective-permute-start(bf16[176,512]{1,0:T(8,128)(2,1)S(1)} %get-tuple-element.99), channel_id=1, source_target_pairs={{0,16},{8,24},{16,0},{24,8},{1,17},{9,25},{17,1},{25,9},{2,18},{10... | collective-permute-start | bytes 540680 | tf_op jit(solution)/shard_map/ppermute | solution.py:261
  172.3 19.7 %collective-permute-start.25 = (bf16[176,512]{1,0:T(8,128)(2,1)S(1)}, bf16[176,512]{1,0:T(8,128)(2,1)S(1)}, u32[]{:S(2)}, u32[]{:S(2)}) collective-permute-start(bf16[176,512]{1,0:T(8,128)(2,1)S(1)} %get-tuple-element.100), channel_id=1, source_target_pairs={{0,8},{8,16},{16,24},{24,0},{1,9},{9,17},{17,25},{25,1},{2,10},{10... | collective-permute-start | bytes 540680 | tf_op jit(solution)/shard_map/ppermute | solution.py:261

commit v3 on v2

--- a/solution.py
+++ b/solution.py
@@ -191,12 +191,12 @@
         outs[j][4 * unit :, 0:128] = marks.astype(kind)
 
 
-def total_kernel(place, own, one, three, two, *outs):
+def total_kernel(place, own, one, three, *outs):
     unit = 2 * CAP
 
     def total(span, columns):
         value = own[span, columns] + one[span, columns].astype(F32)
-        return value + three[span, columns].astype(F32) + two[span, columns].astype(F32)
+        return value + three[span, columns].astype(F32)
 
     marks = total(slice(4 * unit, 4 * unit + TILE), slice(0, 128))
     width = own.shape[1]
@@ -220,12 +220,15 @@
             send[block, m] = total[(2 * m + 1) * half : (2 * m + 2) * half, :].astype(BF16)
 
 
-def sum_kernel(place, pair, pair_far, down, down_far, *outs):
-    for i in range(4):
-        kind = outs[i].dtype
-        for m in range(2):
-            outs[i][m] = (pair[i, m] + pair_far[i, m].astype(F32)).astype(kind)
-        outs[i][2] = (down[i, 0] + down_far[i, 0].astype(F32)).astype(kind)
+def sum_kernel(place, pair, pair_far, down, down_far, own, one, two, three):
+    def total(i, m):
+        if m == 2:
+            return down[i, 0] + down_far[i, 0].astype(F32)
+        return pair[i, m] + pair_far[i, m].astype(F32)
+
+    for m in range(3):
+        for i, out in enumerate((own, one, two, three)):
+            out[m] = total(i, m).astype(out.dtype)
 
 
 def column(row):
@@ -261,6 +264,13 @@
     return lax.ppermute(value, axis, [(i, (i + step) % 4) for i in range(4)])
 
 
+def relay(value, axis):
+    steps = [(c, i, (i + (3 if c else 1)) % 4) for c in range(2) for i in range(4)]
+    if axis == "x":
+        return lax.ppermute(value, ("x", "core"), [(2 * i + c, 2 * j + c) for c, i, j in steps])
+    return lax.ppermute(value, ("core", axis), [(4 * c + i, 4 * c + j) for c, i, j in steps])
+
+
 def swap(value, axis):
     return lax.ppermute(value, axis, [(0, 1), (1, 0)])
 
@@ -299,15 +309,17 @@
     )
 
     own, placing = lax.optimization_barrier((turn(stacked_weights[0]), placing))
-    near, back, across = [shift(own, "x", i) for i in (1, 3, 2)]
+    first = lax.axis_index("core") == 0
+    near, back = shift(own, "x", 1), shift(own, "x", 3)
     blocks = [blocks[0]] + [shift(blocks[k], "expert", k) for k in (1, 2, 3)]
     blocks[2], near, back = lax.optimization_barrier((blocks[2], near, back))
+    across = relay(jnp.where(first, near, back), "x")
     own = jnp.stack([own, near, across, back])
     blocks = [jnp.concatenate(blocks, axis=0)]
-    blocks += [shift(blocks[0], "y", j) for j in (1, 3, 2)]
-    own, *blocks[1:] = lax.optimization_barrier((own, *blocks[1:]))
+    near, back = shift(blocks[0], "y", 1), shift(blocks[0], "y", 3)
+    own, near, back = lax.optimization_barrier((own, near, back))
     other = swap(own, "core")
-    blocks[2:] = blocks[:1:-1]
+    blocks += [near, relay(jnp.where(first, near, back), "y"), back]
 
     def project(names, second):
         wide = len(names) * hidden
@@ -353,35 +365,47 @@
     down_keep, down_send = weight_terms(activation, activation_far, 1)
     hidden_far, down_keep = lax.optimization_barrier((hidden_far, down_keep))
 
+    def halfway(passed, near, back):
+        passed = passed.astype(F32)
+        near = (near + jnp.where(first, 0.0, passed)).astype(BF16)
+        return near, (back + jnp.where(first, passed, 0.0)).astype(BF16)
+
     unit = 2 * CAP + TILE
     shares = call(
         share_kernel,
         place,
         [activation, activation_far, hidden_grad, hidden_far, pair_weights, down_weights],
-        [((8 * CAP + TILE, width), F32)] + [((8 * CAP + TILE, width), BF16)] * 3,
+        [((8 * CAP + TILE, width), kind) for kind in (F32, F32, BF16, F32)],
         [pltpu.VMEM((slots, hidden), BF16), pltpu.VMEM((slots, 2 * hidden), BF16)],
     )
-    arrived = [shift(shares[j], "y", -j) for j in (1, 3, 2)]
+    passed = relay(shares[2], "y")
     shares[0], hidden_grad = lax.optimization_barrier((shares[0], hidden_grad))
     pair_keep, pair_send = weight_terms(hidden_grad, hidden_far, 0)
-    sums = call(
+    pair_far = swap(pair_send, "core")
+    passed, pair_far = lax.optimization_barrier((passed, pair_far))
+    near, back = halfway(passed, shares[1], shares[3])
+    arrived = [shift(near, "y", -1), shift(back, "y", 1)]
+    mine, near, across, back = call(
         sum_kernel,
         place,
-        [pair_keep, swap(pair_send, "core"), down_keep, swap(down_send, "core")],
-        [((3, half, width), F32)] + [((3, half, width), BF16)] * 3,
-    )
-    sums[2], *arrived[:2] = lax.optimization_barrier((sums[2], *arrived[:2]))
-    far_sums = [shift(sums[i], "x", -i) for i in (1, 3, 2)]
-    *far_sums, arrived[2] = lax.optimization_barrier((*far_sums, arrived[2]))
+        [pair_keep, pair_far, down_keep, swap(down_send, "core")],
+        [((3, half, width), kind) for kind in (F32, F32, BF16, F32)],
+    )
+    near, back = halfway(relay(across, "x"), near, back)
+    near, back, *arrived = lax.optimization_barrier((near, back, *arrived))
+    far_sums = [shift(near, "x", -1), shift(back, "x", 1)]
     totals = call(total_kernel, place, [shares[0]] + arrived, [((unit, width), BF16)] * 4)
     returned = [totals[0]] + [shift(totals[k], "expert", -k) for k in (1, 2, 3)]
+    *far_sums, returned[1], returned[2], returned[3] = lax.optimization_barrier(
+        (*far_sums, *returned[1:])
+    )
     layer_output, token_grad, prob_grad = call(
         owner_kernel,
         place,
         [ids, probs, placing] + returned,
         [((rows, width), BF16), ((rows, width), BF16), ((8, rows), F32)],
     )
-    weight_total = sums[0]
+    weight_total = mine
     for block in far_sums:
         weight_total = weight_total + block.astype(F32)
     weight_grad = turn(weight_total.astype(BF16)).astype(F32)[None]

time: 196 us -> 170 us (0.87)
  the two profiles are of different devices: /device:TPU:25 before, /device:TPU:1 now
where the time goes in v3:
time: 170 us; the launch traced here: 168 us
  waiting for transfers between devices  82.5 us (49%)
  starting transfers between devices  48.1 us (28%)
  Pallas kernels  24.7 us (15%)
  local copies, waits for them, and re-layouts  8.69 us (5%)
  other arithmetic  2.94 us (2%)
    ppermute x14, waiting for transfers between devices, shift(): return lax.ppermute(value, axis, [(i, (i + step) % 4) for i in range(4)])  38.5 us
    ppermute x14, starting transfers between devices, shift(): return lax.ppermute(value, axis, [(i, (i + step) % 4) for i in range(4)])  26.6 us
    pallas_call x10, Pallas kernels, call(): pl.pallas_call(kernel, out_shape=[jax.ShapeDtypeStruct(shape, kind) for s...  24.7 us
    ppermute x2, waiting for transfers between devices, relay(): lax.ppermute(value, ('core', axis), [(4 * c + i, 4 * c + j) for c, i, j i...  19.5 us
    ppermute x2, starting transfers between devices, turn(): lax.ppermute(value, ('core', 'zl'), [(2 * c + z, 2 * z + c) for c in rang...  8.77 us
    ppermute x2, waiting for transfers between devices, turn(): lax.ppermute(value, ('core', 'zl'), [(2 * c + z, 2 * z + c) for c in rang...  8.58 us
    ppermute x7, waiting for transfers between devices, swap(): return lax.ppermute(value, axis, [(0, 1), (1, 0)])  8.38 us
    unnamed x25, local copies, waits for them, and re-layouts  8.11 us
  transfers between devices with their start and end apart: 27, of which 15 were waited for; matrix products, arithmetic and copies ran while one was open for 1% of the time, Pallas kernels for 5%

profile of v3, /device:TPU:1, one launch (start us, length us, event | category | flops | bytes accessed | tf_op | source)
XLA Modules:
  0.0 167.8 jit_solution(3603739525995163265)
XLA Ops:
  0.6 4.9 %collective-permute-start = (bf16[3,192,512]{2,1,0:T(8,128)(2,1)}, bf16[3,192,512]{2,1,0:T(8,128)(2,1)S(1)}, u32[]{:S(2)}, u32[]{:S(2)}) collective-permute-start(bf16[3,192,512]{2,1,0:T(8,128)(2,1)} %bitcast.24), channel_id=1, source_target_pairs={{0,0},{1,32},{32,1},{33,33},{2,2},{3,34},{34,3},{35,35},{4,4},{5,3... | collective-permute-start | bytes 1769480 | tf_op jit(solution)/shard_map/ppermute | solution.py:279
  5.7 0.9 copy-done.3
  6.6 0.9 copy-done.4
  8.8 1.5 shard_map.84
  10.3 3.3 %collective-permute-done = bf16[3,192,512]{2,1,0:T(8,128)(2,1)S(1)} collective-permute-done((bf16[3,192,512]{2,1,0:T(8,128)(2,1)}, bf16[3,192,512]{2,1,0:T(8,128)(2,1)S(1)}, u32[]{:S(2)}, u32[]{:S(2)}) %collective-permute-start) | collective-permute-done | bytes 589856 | tf_op jit(solution)/shard_map/ppermute | solution.py:279
  13.6 2.5 %collective-permute-start.4 = (bf16[3,192,512]{2,1,0:T(8,128)(2,1)S(1)}, bf16[3,192,512]{2,1,0:T(8,128)(2,1)S(1)}, u32[]{:S(2)}, u32[]{:S(2)}) collective-permute-start(bf16[3,192,512]{2,1,0:T(8,128)(2,1)S(1)} %collective-permute-done), channel_id=1, source_target_pairs={{0,192},{64,0},{128,64},{192,128},{1,193},{65,1},{129,65},{193,129... | collective-permute-start | bytes 1769480 | tf_op jit(solution)/shard_map/ppermute | solution.py:264
  16.1 3.0 %collective-permute-start.1 = (bf16[160,512]{1,0:T(8,128)(2,1)S(1)}, bf16[160,512]{1,0:T(8,128)(2,1)S(1)}, u32[]{:S(2)}, u32[]{:S(2)}) collective-permute-start(bf16[160,512]{1,0:T(8,128)(2,1)S(1)} %get-tuple-element.62), channel_id=1, source_target_pairs={{0,8},{8,16},{16,24},{24,0},{1,9},{9,17},{17,25},{25,1},{2,10},{10... | collective-permute-start | bytes 491528 | tf_op jit(solution)/shard_map/ppermute | solution.py:264
  19.1 4.6 %collective-permute-start.2 = (bf16[160,512]{1,0:T(8,128)(2,1)S(1)}, bf16[160,512]{1,0:T(8,128)(2,1)S(1)}, u32[]{:S(2)}, u32[]{:S(2)}) collective-permute-start(bf16[160,512]{1,0:T(8,128)(2,1)S(1)} %get-tuple-element.63), channel_id=1, source_target_pairs={{0,16},{8,24},{16,0},{24,8},{1,17},{9,25},{17,1},{25,9},{2,18},{10... | collective-permute-start | bytes 491528 | tf_op jit(solution)/shard_map/ppermute | solution.py:264
  23.8 2.4 %collective-permute-start.5 = (bf16[160,512]{1,0:T(8,128)(2,1)S(1)}, bf16[160,512]{1,0:T(8,128)(2,1)S(1)}, u32[]{:S(2)}, u32[]{:S(2)}) collective-permute-start(bf16[160,512]{1,0:T(8,128)(2,1)S(1)} %get-tuple-element.66), channel_id=1, source_target_pairs={{0,24},{8,0},{16,8},{24,16},{1,25},{9,1},{17,9},{25,17},{2,26},{10... | collective-permute-start | bytes 491528 | tf_op jit(solution)/shard_map/ppermute | solution.py:264
  26.2 7.4 %collective-permute-done.2 = bf16[160,512]{1,0:T(8,128)(2,1)S(1)} collective-permute-done((bf16[160,512]{1,0:T(8,128)(2,1)S(1)}, bf16[160,512]{1,0:T(8,128)(2,1)S(1)}, u32[]{:S(2)}, u32[]{:S(2)}) %collective-permute-start.2) | collective-permute-done | bytes 163872 | tf_op jit(solution)/shard_map/ppermute | solution.py:264
  33.6 3.8 %collective-permute-start.6 = (bf16[3,192,512]{2,1,0:T(8,128)(2,1)S(1)}, bf16[3,192,512]{2,1,0:T(8,128)(2,1)S(1)}, u32[]{:S(2)}, u32[]{:S(2)}) collective-permute-start(bf16[3,192,512]{2,1,0:T(8,128)(2,1)S(1)} %broadcast_select_fusion.1), channel_id=1, source_target_pairs={{0,64},{64,128},{128,192},{192,0},{32,224},{96,32},{160,96},{224,1... | collective-permute-start | bytes 1769480 | tf_op jit(solution)/shard_map/ppermute | solution.py:270
  37.4 2.9 %collective-permute-start.8 = (bf16[640,512]{1,0:T(8,128)(2,1)S(1)}, bf16[640,512]{1,0:T(8,128)(2,1)S(1)}, u32[]{:S(2)}, u32[]{:S(2)}) collective-permute-start(bf16[640,512]{1,0:T(8,128)(2,1)S(1)} %constant_dynamic-update-slice_fusion.refs_0_), channel_id=1, source_target_pairs={{0,6},{2,0},{4,2},{6,4},{1,7},{3,1},{5,3},{7,5},{8,14},{10,8},{12,... | collective-permute-start | bytes 1966088 | tf_op jit(solution)/shard_map/ppermute | solution.py:264
  40.3 3.9 %collective-permute-done.6 = bf16[3,192,512]{2,1,0:T(8,128)(2,1)S(1)} collective-permute-done((bf16[3,192,512]{2,1,0:T(8,128)(2,1)S(1)}, bf16[3,192,512]{2,1,0:T(8,128)(2,1)S(1)}, u32[]{:S(2)}, u32[]{:S(2)}) %collective-permute-start.6) | collective-permute-done | bytes 589856 | tf_op jit(solution)/shard_map/ppermute | solution.py:270
  44.5 5.2 %collective-permute-done.8.refs_3_ = bf16[640,512]{1,0:T(8,128)(2,1)S(1)} collective-permute-done((bf16[640,512]{1,0:T(8,128)(2,1)S(1)}, bf16[640,512]{1,0:T(8,128)(2,1)S(1)}, u32[]{:S(2)}, u32[]{:S(2)}) %collective-permute-start.8) | collective-permute-done | bytes 655392 | tf_op jit(solution)/shard_map/ppermute | solution.py:264
  49.8 3.4 %collective-permute-done.7.refs_1_ = bf16[640,512]{1,0:T(8,128)(2,1)S(1)} collective-permute-done((bf16[640,512]{1,0:T(8,128)(2,1)S(1)}, bf16[640,512]{1,0:T(8,128)(2,1)S(1)}, u32[]{:S(2)}, u32[]{:S(2)}) %collective-permute-start.7) | collective-permute-done | bytes 655392 | tf_op jit(solution)/shard_map/ppermute | solution.py:264
  53.3 9.7 %collective-permute-done.9.refs_2_ = bf16[640,512]{1,0:T(8,128)(2,1)S(1)} collective-permute-done((bf16[640,512]{1,0:T(8,128)(2,1)S(1)}, bf16[640,512]{1,0:T(8,128)(2,1)S(1)}, u32[]{:S(2)}, u32[]{:S(2)}) %collective-permute-start.9) | collective-permute-done | bytes 655392 | tf_op jit(solution)/shard_map/ppermute | solution.py:271
  63.1 1.4 copy-done.9
  64.5 3.8 %shard_map.85 = (f32[160,768]{1,0:T(8,128)S(1)}, bf16[160,768]{1,0:T(8,128)(2,1)S(1)}, bf16[768,2048]{1,0:T(8,128)(2,1)}) custom-call(s32[4]{0:T(128)S(1)} %pad_add_fusion.place, bf16[640,512]{1,0:T(8,128)(2,1)S(1)} %constant_dynamic-update-slice_fusion.refs_0_, bf16[640,512]{1,0:T(8,128)(2,1)S(1)} %collective-permute-done.7.refs_1_, ...), custom_call_target="tpu_custom_call" | custom-call | tf_op jit(solution)/shard_map/pallas_call | solution.py:31
  68.4 3.0 %shard_map.86 = (f32[160,384]{1,0:T(8,128)S(1)}, bf16[160,384]{1,0:T(8,128)(2,1)S(1)}, bf16[384,2048]{1,0:T(8,128)(2,1)S(1)}) custom-call(s32[4]{0:T(128)S(1)} %pad_add_fusion.place, bf16[640,512]{1,0:T(8,128)(2,1)S(1)} %constant_dynamic-update-slice_fusion.refs_0_, bf16[640,512]{1,0:T(8,128)(2,1)S(1)} %collective-permute-done.7.refs_1_, ...), custom_call_target="tpu_custom_call" | custom-call | tf_op jit(solution)/shard_map/pallas_call | solution.py:31
  71.5 1.2 copy-done.2
  72.7 1.4 collective-permute-start.12
  74.5 3.5 %collective-permute-done.12.far = bf16[160,384]{1,0:T(8,128)(2,1)S(1)} collective-permute-done((bf16[160,384]{1,0:T(8,128)(2,1)S(1)}, bf16[160,384]{1,0:T(8,128)(2,1)S(1)}, u32[]{:S(2)}, u32[]{:S(2)}) %collective-permute-start.12) | collective-permute-done | bytes 122912 | tf_op jit(solution)/shard_map/ppermute | solution.py:275
  78.0 2.3 %collective-permute-done.13.far.act_far = bf16[160,384]{1,0:T(8,128)(2,1)S(1)} collective-permute-done((bf16[160,384]{1,0:T(8,128)(2,1)S(1)}, bf16[160,384]{1,0:T(8,128)(2,1)S(1)}, u32[]{:S(2)}, u32[]{:S(2)}) %collective-permute-start.13) | collective-permute-done | bytes 122912 | tf_op jit(solution)/shard_map/ppermute | solution.py:275
  80.4 0.8 shard_map.87.grad.near
  81.2 1.6 shard_map.88
  82.9 1.1 copy-done.1
  84.0 2.5 %collective-permute-done.14.grad_far.far = bf16[176,768]{1,0:T(8,128)(2,1)S(1)} collective-permute-done((bf16[176,768]{1,0:T(8,128)(2,1)S(1)}, bf16[176,768]{1,0:T(8,128)(2,1)S(1)}, u32[]{:S(2)}, u32[]{:S(2)}) %collective-permute-start.14) | collective-permute-done | bytes 270368 | tf_op jit(solution)/shard_map/ppermute | solution.py:275
  86.5 4.2 %shard_map.89 = (f32[656,512]{1,0:T(8,128)S(1)}, f32[656,512]{1,0:T(8,128)S(1)}, bf16[656,512]{1,0:T(8,128)(2,1)S(1)}, f32[656,512]{1,0:T(8,128)S(1)}) custom-call(s32[4]{0:T(128)S(1)} %pad_add_fusion.place, bf16[160,384]{1,0:T(8,128)(2,1)S(1)} %fusion.8.act.near, bf16[160,384]{1,0:T(8,128)(2,1)S(1)} %collective-permute-done.13.far.act_far, ...), custom_call_target="tpu_custom_call" | custom-call | tf_op jit(solution)/shard_map/pallas_call | solution.py:31
  90.8 4.0 %shard_map.90 = (f32[4,2,192,512]{3,2,1,0:T(8,128)}, bf16[4,2,192,512]{3,2,1,0:T(8,128)(2,1)S(1)}) custom-call(s32[4]{0:T(128)S(1)} %pad_add_fusion.place, bf16[176,768]{1,0:T(8,128)(2,1)S(1)} %shard_map.87.grad.near, bf16[176,768]{1,0:T(8,128)(2,1)S(1)} %collective-permute-done.14.grad_far.far, ...), custom_call_target="tpu_custom_call" | custom-call | tf_op jit(solution)/shard_map/pallas_call | solution.py:31
  94.8 4.6 %collective-permute-start.16 = (bf16[4,2,192,512]{3,2,1,0:T(8,128)(2,1)S(1)}, bf16[4,2,192,512]{3,2,1,0:T(8,128)(2,1)S(1)}, u32[]{:S(2)}, u32[]{:S(2)}) collective-permute-start(bf16[4,2,192,512]{3,2,1,0:T(8,128)(2,1)S(1)} %get-tuple-element.87), channel_id=1, source_target_pairs={{0,32},{32,0},{1,33},{33,1},{2,34},{34,2},{3,35},{35,3},{4,36},{36... | collective-permute-start | bytes 4718600 | tf_op jit(solution)/shard_map/ppermute | solution.py:275
  99.5 9.8 %collective-permute-done.15 = bf16[656,512]{1,0:T(8,128)(2,1)S(1)} collective-permute-done((bf16[656,512]{1,0:T(8,128)(2,1)S(1)}, bf16[656,512]{1,0:T(8,128)(2,1)S(1)}, u32[]{:S(2)}, u32[]{:S(2)}) %collective-permute-start.15) | collective-permute-done | bytes 671776 | tf_op jit(solution)/shard_map/ppermute | solution.py:271
  109.3 1.2 copy-done.10
  110.5 3.3 %shard_map.91 = (f32[3,192,512]{2,1,0:T(8,128)S(1)}, f32[3,192,512]{2,1,0:T(8,128)S(1)}, bf16[3,192,512]{2,1,0:T(8,128)(2,1)S(1)}, f32[3,192,512]{2,1,0:T(8,128)S(1)}) custom-call(s32[4]{0:T(128)S(1)} %pad_add_fusion.place, f32[4,2,192,512]{3,2,1,0:T(8,128)} %get-tuple-element.85.pair, bf16[4,2,192,512]{3,2,1,0:T(8,128)(2,1)} %copy-done.10, ...), custom_call_target="tpu_custom_call" | custom-call | tf_op jit(solution)/shard_map/pallas_call | solution.py:31
  113.8 2.3 %collective-permute-start.18 = (bf16[3,192,512]{2,1,0:T(8,128)(2,1)S(1)}, bf16[3,192,512]{2,1,0:T(8,128)(2,1)S(1)}, u32[]{:S(2)}, u32[]{:S(2)}) collective-permute-start(bf16[3,192,512]{2,1,0:T(8,128)(2,1)S(1)} %get-tuple-element.92), channel_id=1, source_target_pairs={{0,64},{64,128},{128,192},{192,0},{32,224},{96,32},{160,96},{224,1... | collective-permute-start | bytes 1769480 | tf_op jit(solution)/shard_map/ppermute | solution.py:270
  116.6 2.7 %collective-permute-start.19 = (bf16[656,512]{1,0:T(8,128)(2,1)S(1)}, bf16[656,512]{1,0:T(8,128)(2,1)S(1)}, u32[]{:S(2)}, u32[]{:S(2)}) collective-permute-start(bf16[656,512]{1,0:T(8,128)(2,1)S(1)} %get-tuple-element.115), channel_id=1, source_target_pairs={{0,6},{2,0},{4,2},{6,4},{1,7},{3,1},{5,3},{7,5},{8,14},{10,8},{12,... | collective-permute-start | bytes 2015240 | tf_op jit(solution)/shard_map/ppermute | solution.py:264
  119.3 3.6 %collective-permute-done.18 = bf16[3,192,512]{2,1,0:T(8,128)(2,1)S(1)} collective-permute-done((bf16[3,192,512]{2,1,0:T(8,128)(2,1)S(1)}, bf16[3,192,512]{2,1,0:T(8,128)(2,1)S(1)}, u32[]{:S(2)}, u32[]{:S(2)}) %collective-permute-start.18) | collective-permute-done | bytes 589856 | tf_op jit(solution)/shard_map/ppermute | solution.py:270
  123.3 9.2 %collective-permute-done.20.three = bf16[656,512]{1,0:T(8,128)(2,1)S(1)} collective-permute-done((bf16[656,512]{1,0:T(8,128)(2,1)S(1)}, bf16[656,512]{1,0:T(8,128)(2,1)S(1)}, u32[]{:S(2)}, u32[]{:S(2)}) %collective-permute-start.20) | collective-permute-done | bytes 671776 | tf_op jit(solution)/shard_map/ppermute | solution.py:264
  132.5 1.2 collective-permute-start.21
  134.0 0.8 shard_map.92
  134.7 3.8 %collective-permute-start.23 = (bf16[176,512]{1,0:T(8,128)(2,1)S(1)}, bf16[176,512]{1,0:T(8,128)(2,1)S(1)}, u32[]{:S(2)}, u32[]{:S(2)}) collective-permute-start(bf16[176,512]{1,0:T(8,128)(2,1)S(1)} %get-tuple-element.102), channel_id=1, source_target_pairs={{0,24},{8,0},{16,8},{24,16},{1,25},{9,1},{17,9},{25,17},{2,26},{10... | collective-permute-start | bytes 540680 | tf_op jit(solution)/shard_map/ppermute | solution.py:264
  138.6 1.1 collective-permute-start.24
  139.7 2.1 %collective-permute-start.25 = (bf16[176,512]{1,0:T(8,128)(2,1)S(1)}, bf16[176,512]{1,0:T(8,128)(2,1)S(1)}, u32[]{:S(2)}, u32[]{:S(2)}) collective-permute-start(bf16[176,512]{1,0:T(8,128)(2,1)S(1)} %get-tuple-element.104), channel_id=1, source_target_pairs={{0,8},{8,16},{16,24},{24,0},{1,9},{9,17},{17,25},{25,1},{2,10},{10... | collective-permute-start | bytes 540680 | tf_op jit(solution)/shard_map/ppermute | solution.py:264
  141.8 9.1 %collective-permute-done.24.refs_2_ = bf16[176,512]{1,0:T(8,128)(2,1)S(1)} collective-permute-done((bf16[176,512]{1,0:T(8,128)(2,1)S(1)}, bf16[176,512]{1,0:T(8,128)(2,1)S(1)}, u32[]{:S(2)}, u32[]{:S(2)}) %collective-permute-start.24) | collective-permute-done | bytes 180256 | tf_op jit(solution)/shard_map/ppermute | solution.py:264
  150.9 4.0 %collective-permute-done.25.refs_3_ = bf16[176,512]{1,0:T(8,128)(2,1)S(1)} collective-permute-done((bf16[176,512]{1,0:T(8,128)(2,1)S(1)}, bf16[176,512]{1,0:T(8,128)(2,1)S(1)}, u32[]{:S(2)}, u32[]{:S(2)}) %collective-permute-start.25) | collective-permute-done | bytes 180256 | tf_op jit(solution)/shard_map/ppermute | solution.py:264
  155.3 3.8 %collective-permute-start.26 = (bf16[3,192,512]{2,1,0:T(8,128)(2,1)S(1)}, bf16[3,192,512]{2,1,0:T(8,128)(2,1)S(1)}, u32[]{:S(2)}, u32[]{:S(2)}) collective-permute-start(bf16[3,192,512]{2,1,0:T(8,128)(2,1)S(1)} %add_convert_fusion), channel_id=1, source_target_pairs={{0,0},{1,32},{32,1},{33,33},{2,2},{3,34},{34,3},{35,35},{4,4},{5,3... | collective-permute-start | bytes 1769480 | tf_op jit(solution)/shard_map/ppermute | solution.py:279
  159.1 1.7 %shard_map.93 = (bf16[128,512]{1,0:T(8,128)(2,1)}, bf16[128,512]{1,0:T(8,128)(2,1)}, f32[8,128]{1,0:T(8,128)S(1)}) custom-call(s32[4]{0:T(128)S(1)} %pad_add_fusion.place, s32[2,128]{1,0:T(2,128)S(1)} %bitcast.17, f32[2,128]{1,0:T(2,128)S(1)} %bitcast.19, bf16[320,128]{1,0:T(8,128)(2,1)S(1)} %get-tuple-element.60.placing, ...), custom_call_target="tpu_custom_call" | custom-call | tf_op jit(solution)/shard_map/pallas_call | solution.py:31
  161.4 5.3 %collective-permute-done.26 = bf16[3,192,512]{2,1,0:T(8,128)(2,1)S(1)} collective-permute-done((bf16[3,192,512]{2,1,0:T(8,128)(2,1)S(1)}, bf16[3,192,512]{2,1,0:T(8,128)(2,1)S(1)}, u32[]{:S(2)}, u32[]{:S(2)}) %collective-permute-start.26) | collective-permute-done | bytes 589856 | tf_op jit(solution)/shard_map/ppermute | solution.py:279
  166.7 1.2 bitcast_convert_fusion
  (53 shorter events, 4.8 us)
Async XLA Ops:
  0.6 13.0 %collective-permute-start = (bf16[3,192,512]{2,1,0:T(8,128)(2,1)}, bf16[3,192,512]{2,1,0:T(8,128)(2,1)S(1)}, u32[]{:S(2)}, u32[]{:S(2)}) collective-permute-start(bf16[3,192,512]{2,1,0:T(8,128)(2,1)} %bitcast.24), channel_id=1, source_target_pairs={{0,0},{1,32},{32,1},{33,33},{2,2},{3,34},{34,3},{35,35},{4,4},{5,3... | collective-permute-start | bytes 1769480 | tf_op jit(solution)/shard_map/ppermute | solution.py:279
  5.7 0.9 copy-start.3
  6.6 0.9 copy-start.4
  7.5 0.7 copy-start.5
  8.1 0.7 copy-start.7
  13.6 19.9 %collective-permute-start.4 = (bf16[3,192,512]{2,1,0:T(8,128)(2,1)S(1)}, bf16[3,192,512]{2,1,0:T(8,128)(2,1)S(1)}, u32[]{:S(2)}, u32[]{:S(2)}) collective-permute-start(bf16[3,192,512]{2,1,0:T(8,128)(2,1)S(1)} %collective-permute-done), channel_id=1, source_target_pairs={{0,192},{64,0},{128,64},{192,128},{1,193},{65,1},{129,65},{193,129... | collective-permute-start | bytes 1769480 | tf_op jit(solution)/shard_map/ppermute | solution.py:264
  16.1 17.4 %collective-permute-start.3 = (bf16[3,192,512]{2,1,0:T(8,128)(2,1)S(1)}, bf16[3,192,512]{2,1,0:T(8,128)(2,1)S(1)}, u32[]{:S(2)}, u32[]{:S(2)}) collective-permute-start(bf16[3,192,512]{2,1,0:T(8,128)(2,1)S(1)} %collective-permute-done), channel_id=1, source_target_pairs={{0,64},{64,128},{128,192},{192,0},{1,65},{65,129},{129,193},{193,1... | collective-permute-start | bytes 1769480 | tf_op jit(solution)/shard_map/ppermute | solution.py:264
  16.1 10.0 %collective-permute-start.1 = (bf16[160,512]{1,0:T(8,128)(2,1)S(1)}, bf16[160,512]{1,0:T(8,128)(2,1)S(1)}, u32[]{:S(2)}, u32[]{:S(2)}) collective-permute-start(bf16[160,512]{1,0:T(8,128)(2,1)S(1)} %get-tuple-element.62), channel_id=1, source_target_pairs={{0,8},{8,16},{16,24},{24,0},{1,9},{9,17},{17,25},{25,1},{2,10},{10... | collective-permute-start | bytes 491528 | tf_op jit(solution)/shard_map/ppermute | solution.py:264
  19.1 14.4 %collective-permute-start.2 = (bf16[160,512]{1,0:T(8,128)(2,1)S(1)}, bf16[160,512]{1,0:T(8,128)(2,1)S(1)}, u32[]{:S(2)}, u32[]{:S(2)}) collective-permute-start(bf16[160,512]{1,0:T(8,128)(2,1)S(1)} %get-tuple-element.63), channel_id=1, source_target_pairs={{0,16},{8,24},{16,0},{24,8},{1,17},{9,25},{17,1},{25,9},{2,18},{10... | collective-permute-start | bytes 491528 | tf_op jit(solution)/shard_map/ppermute | solution.py:264
  23.8 13.7 %collective-permute-start.5 = (bf16[160,512]{1,0:T(8,128)(2,1)S(1)}, bf16[160,512]{1,0:T(8,128)(2,1)S(1)}, u32[]{:S(2)}, u32[]{:S(2)}) collective-permute-start(bf16[160,512]{1,0:T(8,128)(2,1)S(1)} %get-tuple-element.66), channel_id=1, source_target_pairs={{0,24},{8,0},{16,8},{24,16},{1,25},{9,1},{17,9},{25,17},{2,26},{10... | collective-permute-start | bytes 491528 | tf_op jit(solution)/shard_map/ppermute | solution.py:264
  33.6 10.6 %collective-permute-start.6 = (bf16[3,192,512]{2,1,0:T(8,128)(2,1)S(1)}, bf16[3,192,512]{2,1,0:T(8,128)(2,1)S(1)}, u32[]{:S(2)}, u32[]{:S(2)}) collective-permute-start(bf16[3,192,512]{2,1,0:T(8,128)(2,1)S(1)} %broadcast_select_fusion.1), channel_id=1, source_target_pairs={{0,64},{64,128},{128,192},{192,0},{32,224},{96,32},{160,96},{224,1... | collective-permute-start | bytes 1769480 | tf_op jit(solution)/shard_map/ppermute | solution.py:270
  37.4 12.3 %collective-permute-start.8 = (bf16[640,512]{1,0:T(8,128)(2,1)S(1)}, bf16[640,512]{1,0:T(8,128)(2,1)S(1)}, u32[]{:S(2)}, u32[]{:S(2)}) collective-permute-start(bf16[640,512]{1,0:T(8,128)(2,1)S(1)} %constant_dynamic-update-slice_fusion.refs_0_), channel_id=1, source_target_pairs={{0,6},{2,0},{4,2},{6,4},{1,7},{3,1},{5,3},{7,5},{8,14},{10,8},{12,... | collective-permute-start | bytes 1966088 | tf_op jit(solution)/shard_map/ppermute | solution.py:264
  40.3 12.8 %collective-permute-start.7 = (bf16[640,512]{1,0:T(8,128)(2,1)S(1)}, bf16[640,512]{1,0:T(8,128)(2,1)S(1)}, u32[]{:S(2)}, u32[]{:S(2)}) collective-permute-start(bf16[640,512]{1,0:T(8,128)(2,1)S(1)} %constant_dynamic-update-slice_fusion.refs_0_), channel_id=1, source_target_pairs={{0,2},{2,4},{4,6},{6,0},{1,3},{3,5},{5,7},{7,1},{8,10},{10,12},{12... | collective-permute-start | bytes 1966088 | tf_op jit(solution)/shard_map/ppermute | solution.py:264
  44.5 23.8 %copy-start = (bf16[4,3,192,512]{3,2,1,0:T(8,128)(2,1)}, bf16[4,3,192,512]{3,2,1,0:T(8,128)(2,1)S(1)}, u32[]{:S(2)}) copy-start(bf16[4,3,192,512]{3,2,1,0:T(8,128)(2,1)S(1)} %pad_maximum_fusion.refs_4_) | copy-start | bytes 7077892
  53.2 9.9 %collective-permute-start.10 = (bf16[4,3,192,512]{3,2,1,0:T(8,128)(2,1)S(1)}, bf16[4,3,192,512]{3,2,1,0:T(8,128)(2,1)S(1)}, u32[]{:S(2)}, u32[]{:S(2)}) collective-permute-start(bf16[4,3,192,512]{3,2,1,0:T(8,128)(2,1)S(1)} %pad_maximum_fusion.refs_4_), channel_id=1, source_target_pairs={{0,32},{32,0},{1,33},{33,1},{2,34},{34,2},{3,35},{35,3},{4,36},{36... | collective-permute-start | bytes 7077896 | tf_op jit(solution)/shard_map/ppermute | solution.py:275
  53.2 9.8 %collective-permute-start.9 = (bf16[640,512]{1,0:T(8,128)(2,1)S(1)}, bf16[640,512]{1,0:T(8,128)(2,1)S(1)}, u32[]{:S(2)}, u32[]{:S(2)}) collective-permute-start(bf16[640,512]{1,0:T(8,128)(2,1)S(1)} %broadcast_select_fusion), channel_id=1, source_target_pairs={{0,2},{2,4},{4,6},{6,0},{32,38},{34,32},{36,34},{38,36},{1,3},{3,5... | collective-permute-start | bytes 1966088 | tf_op jit(solution)/shard_map/ppermute | solution.py:271
  63.1 1.4 copy-start.9
  68.3 5.8 %collective-permute-start.11 = (bf16[160,768]{1,0:T(8,128)(2,1)S(1)}, bf16[160,768]{1,0:T(8,128)(2,1)S(1)}, u32[]{:S(2)}, u32[]{:S(2)}) collective-permute-start(bf16[160,768]{1,0:T(8,128)(2,1)S(1)} %get-tuple-element.73), channel_id=1, source_target_pairs={{0,1},{1,0},{2,3},{3,2},{4,5},{5,4},{6,7},{7,6},{8,9},{9,8},{10,11... | collective-permute-start | bytes 737288 | tf_op jit(solution)/shard_map/ppermute | solution.py:275
  71.5 1.2 copy-start.2
  72.7 5.4 %collective-permute-start.12 = (bf16[160,384]{1,0:T(8,128)(2,1)S(1)}, bf16[160,384]{1,0:T(8,128)(2,1)S(1)}, u32[]{:S(2)}, u32[]{:S(2)}) collective-permute-start(bf16[160,384]{1,0:T(8,128)(2,1)S(1)} %get-tuple-element.74), channel_id=1, source_target_pairs={{0,1},{1,0},{2,3},{3,2},{4,5},{5,4},{6,7},{7,6},{8,9},{9,8},{10,11... | collective-permute-start | bytes 368648 | tf_op jit(solution)/shard_map/ppermute | solution.py:275
  74.3 6.1 %collective-permute-start.13 = (bf16[160,384]{1,0:T(8,128)(2,1)S(1)}, bf16[160,384]{1,0:T(8,128)(2,1)S(1)}, u32[]{:S(2)}, u32[]{:S(2)}) collective-permute-start(bf16[160,384]{1,0:T(8,128)(2,1)S(1)} %fusion.8.act.near), channel_id=1, source_target_pairs={{0,1},{1,0},{2,3},{3,2},{4,5},{5,4},{6,7},{7,6},{8,9},{9,8},{10,11... | collective-permute-start | bytes 368648 | tf_op jit(solution)/shard_map/ppermute | solution.py:275
  81.2 5.4 %collective-permute-start.14 = (bf16[176,768]{1,0:T(8,128)(2,1)S(1)}, bf16[176,768]{1,0:T(8,128)(2,1)S(1)}, u32[]{:S(2)}, u32[]{:S(2)}) collective-permute-start(bf16[176,768]{1,0:T(8,128)(2,1)S(1)} %shard_map.87.grad.near), channel_id=1, source_target_pairs={{0,1},{1,0},{2,3},{3,2},{4,5},{5,4},{6,7},{7,6},{8,9},{9,8},{10,11... | collective-permute-start | bytes 811016 | tf_op jit(solution)/shard_map/ppermute | solution.py:275
  82.8 1.2 copy-start.1
  94.8 14.6 %collective-permute-start.16 = (bf16[4,2,192,512]{3,2,1,0:T(8,128)(2,1)S(1)}, bf16[4,2,192,512]{3,2,1,0:T(8,128)(2,1)S(1)}, u32[]{:S(2)}, u32[]{:S(2)}) collective-permute-start(bf16[4,2,192,512]{3,2,1,0:T(8,128)(2,1)S(1)} %get-tuple-element.87), channel_id=1, source_target_pairs={{0,32},{32,0},{1,33},{33,1},{2,34},{34,2},{3,35},{35,3},{4,36},{36... | collective-permute-start | bytes 4718600 | tf_op jit(solution)/shard_map/ppermute | solution.py:275
  99.4 9.9 %collective-permute-start.17 = (bf16[4,1,192,512]{3,2,1,0:T(8,128)(2,1)S(1)}, bf16[4,1,192,512]{3,2,1,0:T(8,128)(2,1)S(1)}, u32[]{:S(2)}, u32[]{:S(2)}) collective-permute-start(bf16[4,1,192,512]{3,2,1,0:T(8,128)(2,1)S(1)} %get-tuple-element.90), channel_id=1, source_target_pairs={{0,32},{32,0},{1,33},{33,1},{2,34},{34,2},{3,35},{35,3},{4,36},{36... | collective-permute-start | bytes 2359304 | tf_op jit(solution)/shard_map/ppermute | solution.py:275
  99.4 9.9 %collective-permute-start.15 = (bf16[656,512]{1,0:T(8,128)(2,1)S(1)}, bf16[656,512]{1,0:T(8,128)(2,1)S(1)}, u32[]{:S(2)}, u32[]{:S(2)}) collective-permute-start(bf16[656,512]{1,0:T(8,128)(2,1)S(1)} %get-tuple-element.86), channel_id=1, source_target_pairs={{0,2},{2,4},{4,6},{6,0},{32,38},{34,32},{36,34},{38,36},{1,3},{3,5... | collective-permute-start | bytes 2015240 | tf_op jit(solution)/shard_map/ppermute | solution.py:271
  109.3 1.2 copy-start.10
  113.8 9.1 %collective-permute-start.18 = (bf16[3,192,512]{2,1,0:T(8,128)(2,1)S(1)}, bf16[3,192,512]{2,1,0:T(8,128)(2,1)S(1)}, u32[]{:S(2)}, u32[]{:S(2)}) collective-permute-start(bf16[3,192,512]{2,1,0:T(8,128)(2,1)S(1)} %get-tuple-element.92), channel_id=1, source_target_pairs={{0,64},{64,128},{128,192},{192,0},{32,224},{96,32},{160,96},{224,1... | collective-permute-start | bytes 1769480 | tf_op jit(solution)/shard_map/ppermute | solution.py:270
  116.5 16.0 %collective-permute-start.20 = (bf16[656,512]{1,0:T(8,128)(2,1)S(1)}, bf16[656,512]{1,0:T(8,128)(2,1)S(1)}, u32[]{:S(2)}, u32[]{:S(2)}) collective-permute-start(bf16[656,512]{1,0:T(8,128)(2,1)S(1)} %get-tuple-element.114), channel_id=1, source_target_pairs={{0,2},{2,4},{4,6},{6,0},{1,3},{3,5},{5,7},{7,1},{8,10},{10,12},{12... | collective-permute-start | bytes 2015240 | tf_op jit(solution)/shard_map/ppermute | solution.py:264
  116.6 15.9 %collective-permute-start.19 = (bf16[656,512]{1,0:T(8,128)(2,1)S(1)}, bf16[656,512]{1,0:T(8,128)(2,1)S(1)}, u32[]{:S(2)}, u32[]{:S(2)}) collective-permute-start(bf16[656,512]{1,0:T(8,128)(2,1)S(1)} %get-tuple-element.115), channel_id=1, source_target_pairs={{0,6},{2,0},{4,2},{6,4},{1,7},{3,1},{5,3},{7,5},{8,14},{10,8},{12,... | collective-permute-start | bytes 2015240 | tf_op jit(solution)/shard_map/ppermute | solution.py:264
  132.5 22.5 %collective-permute-start.21 = (bf16[3,192,512]{2,1,0:T(8,128)(2,1)S(1)}, bf16[3,192,512]{2,1,0:T(8,128)(2,1)S(1)}, u32[]{:S(2)}, u32[]{:S(2)}) collective-permute-start(bf16[3,192,512]{2,1,0:T(8,128)(2,1)S(1)} %get-tuple-element.100), channel_id=1, source_target_pairs={{0,192},{64,0},{128,64},{192,128},{1,193},{65,1},{129,65},{193,129... | collective-permute-start | bytes 1769480 | tf_op jit(solution)/shard_map/ppermute | solution.py:264
  133.7 21.3 %collective-permute-start.22 = (bf16[3,192,512]{2,1,0:T(8,128)(2,1)S(1)}, bf16[3,192,512]{2,1,0:T(8,128)(2,1)S(1)}, u32[]{:S(2)}, u32[]{:S(2)}) collective-permute-start(bf16[3,192,512]{2,1,0:T(8,128)(2,1)S(1)} %get-tuple-element.101), channel_id=1, source_target_pairs={{0,64},{64,128},{128,192},{192,0},{1,65},{65,129},{129,193},{193,1... | collective-permute-start | bytes 1769480 | tf_op jit(solution)/shard_map/ppermute | solution.py:264
  134.7 7.1 %collective-permute-start.23 = (bf16[176,512]{1,0:T(8,128)(2,1)S(1)}, bf16[176,512]{1,0:T(8,128)(2,1)S(1)}, u32[]{:S(2)}, u32[]{:S(2)}) collective-permute-start(bf16[176,512]{1,0:T(8,128)(2,1)S(1)} %get-tuple-element.102), channel_id=1, source_target_pairs={{0,24},{8,0},{16,8},{24,16},{1,25},{9,1},{17,9},{25,17},{2,26},{10... | collective-permute-start | bytes 540680 | tf_op jit(solution)/shard_map/ppermute | solution.py:264
  138.6 12.3 %collective-permute-start.24 = (bf16[176,512]{1,0:T(8,128)(2,1)S(1)}, bf16[176,512]{1,0:T(8,128)(2,1)S(1)}, u32[]{:S(2)}, u32[]{:S(2)}) collective-permute-start(bf16[176,512]{1,0:T(8,128)(2,1)S(1)} %get-tuple-element.103), channel_id=1, source_target_pairs={{0,16},{8,24},{16,0},{24,8},{1,17},{9,25},{17,1},{25,9},{2,18},{10... | collective-permute-start | bytes 540680 | tf_op jit(solution)/shard_map/ppermute | solution.py:264
  139.7 15.3 %collective-permute-start.25 = (bf16[176,512]{1,0:T(8,128)(2,1)S(1)}, bf16[176,512]{1,0:T(8,128)(2,1)S(1)}, u32[]{:S(2)}, u32[]{:S(2)}) collective-permute-start(bf16[176,512]{1,0:T(8,128)(2,1)S(1)} %get-tuple-element.104), channel_id=1, source_target_pairs={{0,8},{8,16},{16,24},{24,0},{1,9},{9,17},{17,25},{25,1},{2,10},{10... | collective-permute-start | bytes 540680 | tf_op jit(solution)/shard_map/ppermute | solution.py:264
  155.0 4.1 %copy-start.6 = (s32[128,2]{0,1:T(2,128)S(1)}, s32[128,2]{0,1:T(2,128)}, u32[]{:S(2)}) copy-start(s32[128,2]{0,1:T(2,128)} %param.6) | copy-start | bytes 3076
  155.0 4.1 %copy-start.8 = (f32[128,2]{0,1:T(2,128)S(1)}, f32[128,2]{0,1:T(2,128)}, u32[]{:S(2)}) copy-start(f32[128,2]{0,1:T(2,128)} %param.7) | copy-start | bytes 3076
  155.3 11.4 %collective-permute-start.26 = (bf16[3,192,512]{2,1,0:T(8,128)(2,1)S(1)}, bf16[3,192,512]{2,1,0:T(8,128)(2,1)S(1)}, u32[]{:S(2)}, u32[]{:S(2)}) collective-permute-start(bf16[3,192,512]{2,1,0:T(8,128)(2,1)S(1)} %add_convert_fusion), channel_id=1, source_target_pairs={{0,0},{1,32},{32,1},{33,33},{2,2},{3,34},{34,3},{35,35},{4,4},{5,3... | collective-permute-start | bytes 1769480 | tf_op jit(solution)/shard_map/ppermute | solution.py:279

commit v4 on v3

--- a/solution.py
+++ b/solution.py
@@ -83,16 +83,16 @@
 
 
 def fetch(own, other, joined, sems, names, place):
-    half, width = own.shape[2:]
+    half, width = own[0].shape[1:]
     copies = []
     for block in range(4):
         spot = lax.rem(place[2] - place[1] + block + 4, 4)
         columns = pl.ds(pl.multiple_of(spot * width, width), width)
         for n, m in enumerate(names):
-            for h, source in enumerate((own, other)):
+            for h, source in enumerate((own[block], other[block])):
                 copies.append(
                     pltpu.make_async_copy(
-                        source.at[block, m],
+                        source.at[m],
                         joined.at[pl.ds((2 * n + h) * half, half), columns],
                         sems.at[block, n, h],
                     )
@@ -109,8 +109,8 @@
 
 
 def project_kernel(names, second, place, *refs):
-    rows, own, other = refs[0:4], refs[4], refs[5]
-    keep, send, joined, wide, total, sems = refs[6:12]
+    rows, own, other = refs[0:4], refs[4:8], refs[8:12]
+    keep, send, joined, wide, total, sems = refs[12:18]
     width = rows[0].shape[1]
     copies = fetch(own, other, joined, sems, names, place)
     for j in range(4):
@@ -208,7 +208,8 @@
 
 
 def weight_kernel(second, place, near, far, *refs):
-    rows, keep, send, joined, chosen = refs[0:4], *refs[4:8]
+    rows, keep, joined, chosen = refs[0:4], refs[4], *refs[-2:]
+    sends = refs[5:-2]
     half = keep.shape[2]
     join(joined, near, far, place[3])
     for j in range(4):
@@ -217,18 +218,7 @@
         total = tn(joined[...], chosen[...])
         for m in range(keep.shape[1]):
             keep[block, m] = total[2 * m * half : (2 * m + 1) * half, :]
-            send[block, m] = total[(2 * m + 1) * half : (2 * m + 2) * half, :].astype(BF16)
-
-
-def sum_kernel(place, pair, pair_far, down, down_far, own, one, two, three):
-    def total(i, m):
-        if m == 2:
-            return down[i, 0] + down_far[i, 0].astype(F32)
-        return pair[i, m] + pair_far[i, m].astype(F32)
-
-    for m in range(3):
-        for i, out in enumerate((own, one, two, three)):
-            out[m] = total(i, m).astype(out.dtype)
+            sends[m][block] = total[(2 * m + 1) * half : (2 * m + 2) * half, :].astype(BF16)
 
 
 def column(row):
@@ -308,17 +298,17 @@
         [far, far, far, far],
     )
 
-    own, placing = lax.optimization_barrier((turn(stacked_weights[0]), placing))
+    blocks = [blocks[0]] + [shift(blocks[k], "expert", k) for k in (1, 2, 3)]
+    own, *blocks[1:] = lax.optimization_barrier((turn(stacked_weights[0]), *blocks[1:]))
     first = lax.axis_index("core") == 0
     near, back = shift(own, "x", 1), shift(own, "x", 3)
-    blocks = [blocks[0]] + [shift(blocks[k], "expert", k) for k in (1, 2, 3)]
-    blocks[2], near, back = lax.optimization_barrier((blocks[2], near, back))
-    across = relay(jnp.where(first, near, back), "x")
-    own = jnp.stack([own, near, across, back])
+    own = [own, near, relay(jnp.where(first, near, back), "x"), back]
     blocks = [jnp.concatenate(blocks, axis=0)]
     near, back = shift(blocks[0], "y", 1), shift(blocks[0], "y", 3)
-    own, near, back = lax.optimization_barrier((own, near, back))
-    other = swap(own, "core")
+    own[0], own[1], own[3], near, back = lax.optimization_barrier(
+        (own[0], own[1], own[3], near, back)
+    )
+    other = [swap(block, "core") for block in own]
     blocks += [near, relay(jnp.where(first, near, back), "y"), back]
 
     def project(names, second):
@@ -326,14 +316,14 @@
         return call(
             functools.partial(project_kernel, names, second),
             place,
-            blocks + [own, other],
+            blocks + own + other,
             [((part, wide), F32), ((part, wide), BF16), ((wide, 4 * width), BF16)],
             [
                 pltpu.VMEM((slots, 4 * width), BF16),
                 pltpu.VMEM((slots, wide), F32),
                 pltpu.SemaphoreType.DMA((4, 2, 2)),
             ],
-            [vmem] * 4 + [hbm] * 2,
+            [vmem] * 4 + [hbm] * 8,
         )
 
     keep, send, pair_weights = project((0, 1), 0)
@@ -358,7 +348,7 @@
             functools.partial(weight_kernel, second),
             place,
             [near, far] + blocks,
-            [(shape, F32), (shape, BF16)],
+            [(shape, F32)] + [((4, half, width), BF16)] * count,
             [pltpu.VMEM((slots, near.shape[1]), BF16), pltpu.VMEM((slots, width), BF16)],
         )
 
@@ -380,21 +370,23 @@
     )
     passed = relay(shares[2], "y")
     shares[0], hidden_grad = lax.optimization_barrier((shares[0], hidden_grad))
-    pair_keep, pair_send = weight_terms(hidden_grad, hidden_far, 0)
-    pair_far = swap(pair_send, "core")
-    passed, pair_far = lax.optimization_barrier((passed, pair_far))
+    pair_keep, *pair_send = weight_terms(hidden_grad, hidden_far, 0)
+    pair_far = [swap(send, "core") for send in pair_send]
     near, back = halfway(passed, shares[1], shares[3])
+    near, back, *pair_far = lax.optimization_barrier((near, back, *pair_far))
     arrived = [shift(near, "y", -1), shift(back, "y", 1)]
-    mine, near, across, back = call(
-        sum_kernel,
-        place,
-        [pair_keep, pair_far, down_keep, swap(down_send, "core")],
-        [((3, half, width), kind) for kind in (F32, F32, BF16, F32)],
-    )
-    near, back = halfway(relay(across, "x"), near, back)
-    near, back, *arrived = lax.optimization_barrier((near, back, *arrived))
+    down_far = swap(down_send, "core")
+
+    def both_cores(i):
+        kept = (pair_keep[i, 0], pair_keep[i, 1], down_keep[i, 0])
+        moved = (*pair_far, down_far)
+        return jnp.stack([near + far[i].astype(F32) for near, far in zip(kept, moved)])
+
+    passed = relay(both_cores(2).astype(BF16), "x")
+    totals = call(total_kernel, place, [shares[0]] + arrived, [((unit, width), BF16)] * 4)
+    passed, totals[0] = lax.optimization_barrier((passed, totals[0]))
+    near, back = halfway(passed, both_cores(1), both_cores(3))
     far_sums = [shift(near, "x", -1), shift(back, "x", 1)]
-    totals = call(total_kernel, place, [shares[0]] + arrived, [((unit, width), BF16)] * 4)
     returned = [totals[0]] + [shift(totals[k], "expert", -k) for k in (1, 2, 3)]
     *far_sums, returned[1], returned[2], returned[3] = lax.optimization_barrier(
         (*far_sums, *returned[1:])
@@ -405,7 +397,7 @@
         [ids, probs, placing] + returned,
         [((rows, width), BF16), ((rows, width), BF16), ((8, rows), F32)],
     )
-    weight_total = mine
+    weight_total = both_cores(0)
     for block in far_sums:
         weight_total = weight_total + block.astype(F32)
     weight_grad = turn(weight_total.astype(BF16)).astype(F32)[None]

time: 170 us -> 170 us (level)
  starting transfers between devices: 48.1 us -> 74.9 us
  waiting for transfers between devices: 82.5 us -> 62.4 us
  local copies, waits for them, and re-layouts: 8.69 us -> 3.82 us
  Pallas kernels: 24.7 us -> 22.7 us
  other arithmetic: 2.94 us -> 4.66 us
    ppermute x7 -> x11, starting transfers between devices: 6.57 us -> 26.1 us  [swap(): return lax.ppermute(value, axis, [(0, 1), (1, 0)])]
    ppermute x2, waiting for transfers between devices: 19.5 us -> 3.95 us  [relay(): lax.ppermute(value, ('core', axis), [(4 * c + i, 4 * c + j) for c, i, j i...]
    ppermute x2, waiting for transfers between devices: 7.5 us -> 0.01 us  [relay(): lax.ppermute(value, ('x', 'core'), [(2 * i + c, 2 * j + c) for c, i, j in...]
    ppermute x7 -> x11, waiting for transfers between devices: 8.38 us -> 15.1 us  [swap(): return lax.ppermute(value, axis, [(0, 1), (1, 0)])]
    ppermute x2, starting transfers between devices: 8.77 us -> 13.8 us  [turn(): lax.ppermute(value, ('core', 'zl'), [(2 * c + z, 2 * z + c) for c in rang...]
    unnamed x25 -> x29, local copies, waits for them, and re-layouts: 8.11 us -> 3.24 us
    ppermute x2, starting transfers between devices: 0.17 us -> 4.2 us  [relay(): lax.ppermute(value, ('core', axis), [(4 * c + i, 4 * c + j) for c, i, j i...]
    ppermute x2, waiting for transfers between devices: 8.58 us -> 5.27 us  [turn(): lax.ppermute(value, ('core', 'zl'), [(2 * c + z, 2 * z + c) for c in rang...]
  transfers between devices with their start and end apart: 27 -> 31, of which waited for: 15 -> 15; matrix products, arithmetic and copies ran while one was open for 1% -> 2% of each run, Pallas kernels for 5% -> 10%
where the time goes in v4:
time: 170 us; the launch traced here: 169 us
  starting transfers between devices  74.9 us (44%)
  waiting for transfers between devices  62.4 us (37%)
  Pallas kernels  22.7 us (13%)
  other arithmetic  4.66 us (3%)
  local copies, waits for them, and re-layouts  3.82 us (2%)
    ppermute x14, waiting for transfers between devices, shift(): return lax.ppermute(value, axis, [(i, (i + step) % 4) for i in range(4)])  38.1 us
    ppermute x14, starting transfers between devices, shift(): return lax.ppermute(value, axis, [(i, (i + step) % 4) for i in range(4)])  26.5 us
    ppermute x11, starting transfers between devices, swap(): return lax.ppermute(value, axis, [(0, 1), (1, 0)])  26.1 us
    pallas_call x9, Pallas kernels, call(): pl.pallas_call(kernel, out_shape=[jax.ShapeDtypeStruct(shape, kind) for s...  22.7 us
    ppermute x11, waiting for transfers between devices, swap(): return lax.ppermute(value, axis, [(0, 1), (1, 0)])  15.1 us
    ppermute x2, starting transfers between devices, turn(): lax.ppermute(value, ('core', 'zl'), [(2 * c + z, 2 * z + c) for c in rang...  13.8 us
    ppermute x2, waiting for transfers between devices, turn(): lax.ppermute(value, ('core', 'zl'), [(2 * c + z, 2 * z + c) for c in rang...  5.27 us
    ppermute x2, starting transfers between devices, relay(): lax.ppermute(value, ('x', 'core'), [(2 * i + c, 2 * j + c) for c, i, j in...  4.3 us
  transfers between devices with their start and end apart: 31, of which 15 were waited for; matrix products, arithmetic and copies ran while one was open for 2% of the time, Pallas kernels for 10%

profile of v4, /device:TPU:1, one launch (start us, length us, event | category | flops | bytes accessed | tf_op | source)
XLA Modules:
  0.0 169.4 jit_solution(5756525856878323707)
XLA Ops:
  0.6 4.9 %collective-permute-start = (bf16[3,192,512]{2,1,0:T(8,128)(2,1)}, bf16[3,192,512]{2,1,0:T(8,128)(2,1)}, u32[]{:S(2)}, u32[]{:S(2)}) collective-permute-start(bf16[3,192,512]{2,1,0:T(8,128)(2,1)} %bitcast.46), channel_id=1, source_target_pairs={{0,0},{1,32},{32,1},{33,33},{2,2},{3,34},{34,3},{35,35},{4,4},{5,3... | collective-permute-start | bytes 1769480 | tf_op jit(solution)/shard_map/ppermute | solution.py:269
  5.7 0.9 copy-done.6
  6.6 0.9 copy-done.7
  8.8 1.5 shard_map.84
  10.3 3.1 %collective-permute-start.1 = (bf16[160,512]{1,0:T(8,128)(2,1)S(1)}, bf16[160,512]{1,0:T(8,128)(2,1)S(1)}, u32[]{:S(2)}, u32[]{:S(2)}) collective-permute-start(bf16[160,512]{1,0:T(8,128)(2,1)S(1)} %get-tuple-element.59), channel_id=1, source_target_pairs={{0,8},{8,16},{16,24},{24,0},{1,9},{9,17},{17,25},{25,1},{2,10},{10... | collective-permute-start | bytes 491528 | tf_op jit(solution)/shard_map/ppermute | solution.py:254
  13.4 4.2 %collective-permute-start.2 = (bf16[160,512]{1,0:T(8,128)(2,1)S(1)}, bf16[160,512]{1,0:T(8,128)(2,1)S(1)}, u32[]{:S(2)}, u32[]{:S(2)}) collective-permute-start(bf16[160,512]{1,0:T(8,128)(2,1)S(1)} %get-tuple-element.60), channel_id=1, source_target_pairs={{0,16},{8,24},{16,0},{24,8},{1,17},{9,25},{17,1},{25,9},{2,18},{10... | collective-permute-start | bytes 491528 | tf_op jit(solution)/shard_map/ppermute | solution.py:254
  17.6 2.4 %collective-permute-start.3 = (bf16[160,512]{1,0:T(8,128)(2,1)S(1)}, bf16[160,512]{1,0:T(8,128)(2,1)S(1)}, u32[]{:S(2)}, u32[]{:S(2)}) collective-permute-start(bf16[160,512]{1,0:T(8,128)(2,1)S(1)} %get-tuple-element.61), channel_id=1, source_target_pairs={{0,24},{8,0},{16,8},{24,16},{1,25},{9,1},{17,9},{25,17},{2,26},{10... | collective-permute-start | bytes 491528 | tf_op jit(solution)/shard_map/ppermute | solution.py:254
  20.0 3.8 %collective-permute-done.1 = bf16[160,512]{1,0:T(8,128)(2,1)S(1)} collective-permute-done((bf16[160,512]{1,0:T(8,128)(2,1)S(1)}, bf16[160,512]{1,0:T(8,128)(2,1)S(1)}, u32[]{:S(2)}, u32[]{:S(2)}) %collective-permute-start.1) | collective-permute-done | bytes 163872 | tf_op jit(solution)/shard_map/ppermute | solution.py:254
  23.8 3.7 %collective-permute-done.2 = bf16[160,512]{1,0:T(8,128)(2,1)S(1)} collective-permute-done((bf16[160,512]{1,0:T(8,128)(2,1)S(1)}, bf16[160,512]{1,0:T(8,128)(2,1)S(1)}, u32[]{:S(2)}, u32[]{:S(2)}) %collective-permute-start.2) | collective-permute-done | bytes 163872 | tf_op jit(solution)/shard_map/ppermute | solution.py:254
  27.5 1.2 collective-permute-start.4
  28.7 1.4 collective-permute-start.5
  30.3 1.4 collective-permute-start.6
  31.6 1.5 collective-permute-start.7
  33.2 4.5 %collective-permute-done.4.refs_5_ = bf16[3,192,512]{2,1,0:T(8,128)(2,1)S(1)} collective-permute-done((bf16[3,192,512]{2,1,0:T(8,128)(2,1)}, bf16[3,192,512]{2,1,0:T(8,128)(2,1)S(1)}, u32[]{:S(2)}, u32[]{:S(2)}) %collective-permute-start.4) | collective-permute-done | bytes 589856 | tf_op jit(solution)/shard_map/ppermute | solution.py:254
  37.7 2.7 %collective-permute-start.9 = (bf16[3,192,512]{2,1,0:T(8,128)(2,1)S(1)}, bf16[3,192,512]{2,1,0:T(8,128)(2,1)S(1)}, u32[]{:S(2)}, u32[]{:S(2)}) collective-permute-start(bf16[3,192,512]{2,1,0:T(8,128)(2,1)S(1)} %broadcast_select_fusion.1), channel_id=1, source_target_pairs={{0,64},{64,128},{128,192},{192,0},{32,224},{96,32},{160,96},{224,1... | collective-permute-start | bytes 1769480 | tf_op jit(solution)/shard_map/ppermute | solution.py:260
  41.5 2.8 %collective-permute-start.8 = (bf16[640,512]{1,0:T(8,128)(2,1)S(1)}, bf16[640,512]{1,0:T(8,128)(2,1)S(1)}, u32[]{:S(2)}, u32[]{:S(2)}) collective-permute-start(bf16[640,512]{1,0:T(8,128)(2,1)S(1)} %broadcast_select_fusion), channel_id=1, source_target_pairs={{0,2},{2,4},{4,6},{6,0},{32,38},{34,32},{36,34},{38,36},{1,3},{3,5... | collective-permute-start | bytes 1966088 | tf_op jit(solution)/shard_map/ppermute | solution.py:261
  44.3 12.2 %collective-permute-start.10 = (bf16[3,192,512]{2,1,0:T(8,128)(2,1)}, bf16[3,192,512]{2,1,0:T(8,128)(2,1)S(1)}, u32[]{:S(2)}, u32[]{:S(2)}) collective-permute-start(bf16[3,192,512]{2,1,0:T(8,128)(2,1)} %collective-permute-done.refs_4_), channel_id=1, source_target_pairs={{0,32},{32,0},{1,33},{33,1},{2,34},{34,2},{3,35},{35,3},{4,36},{36... | collective-permute-start | bytes 1769480 | tf_op jit(solution)/shard_map/ppermute | solution.py:265
  57.0 4.7 %collective-permute-start.12 = (bf16[3,192,512]{2,1,0:T(8,128)(2,1)S(1)}, bf16[3,192,512]{2,1,0:T(8,128)(2,1)S(1)}, u32[]{:S(2)}, u32[]{:S(2)}) collective-permute-start(bf16[3,192,512]{2,1,0:T(8,128)(2,1)S(1)} %collective-permute-done.9.refs_6_), channel_id=1, source_target_pairs={{0,32},{32,0},{1,33},{33,1},{2,34},{34,2},{3,35},{35,3},{4,36},{36... | collective-permute-start | bytes 1769480 | tf_op jit(solution)/shard_map/ppermute | solution.py:265
  61.7 1.6 collective-permute-done.12.refs_10_
  63.4 4.3 %shard_map.85 = (f32[160,768]{1,0:T(8,128)S(1)}, bf16[160,768]{1,0:T(8,128)(2,1)S(1)}, bf16[768,2048]{1,0:T(8,128)(2,1)}) custom-call(s32[4]{0:T(128)S(1)} %pad_add_fusion.place, bf16[640,512]{1,0:T(8,128)(2,1)S(1)} %constant_dynamic-update-slice_fusion.refs_0_, bf16[640,512]{1,0:T(8,128)(2,1)} %copy-done, bf16[640,512]{1,0:T(8,128)(2,1)} %copy-done.4, ...), custom_call_target="tpu_custom_call" | custom-call | tf_op jit(solution)/shard_map/pallas_call | solution.py:31
  67.7 2.1 %collective-permute-start.14 = (bf16[160,768]{1,0:T(8,128)(2,1)S(1)}, bf16[160,768]{1,0:T(8,128)(2,1)S(1)}, u32[]{:S(2)}, u32[]{:S(2)}) collective-permute-start(bf16[160,768]{1,0:T(8,128)(2,1)S(1)} %get-tuple-element.72), channel_id=1, source_target_pairs={{0,1},{1,0},{2,3},{3,2},{4,5},{5,4},{6,7},{7,6},{8,9},{9,8},{10,11... | collective-permute-start | bytes 737288 | tf_op jit(solution)/shard_map/ppermute | solution.py:265
  69.7 3.8 %shard_map.86 = (f32[160,384]{1,0:T(8,128)S(1)}, bf16[160,384]{1,0:T(8,128)(2,1)S(1)}, bf16[384,2048]{1,0:T(8,128)(2,1)}) custom-call(s32[4]{0:T(128)S(1)} %pad_add_fusion.place, bf16[640,512]{1,0:T(8,128)(2,1)S(1)} %constant_dynamic-update-slice_fusion.refs_0_, bf16[640,512]{1,0:T(8,128)(2,1)} %copy-done, bf16[640,512]{1,0:T(8,128)(2,1)} %copy-done.4, ...), custom_call_target="tpu_custom_call" | custom-call | tf_op jit(solution)/shard_map/pallas_call | solution.py:31
  73.8 1.5 collective-permute-start.16
  75.4 3.6 %collective-permute-done.15.far = bf16[160,384]{1,0:T(8,128)(2,1)S(1)} collective-permute-done((bf16[160,384]{1,0:T(8,128)(2,1)S(1)}, bf16[160,384]{1,0:T(8,128)(2,1)S(1)}, u32[]{:S(2)}, u32[]{:S(2)}) %collective-permute-start.15) | collective-permute-done | bytes 122912 | tf_op jit(solution)/shard_map/ppermute | solution.py:265
  79.0 2.3 %collective-permute-done.16.far.act_far = bf16[160,384]{1,0:T(8,128)(2,1)S(1)} collective-permute-done((bf16[160,384]{1,0:T(8,128)(2,1)S(1)}, bf16[160,384]{1,0:T(8,128)(2,1)S(1)}, u32[]{:S(2)}, u32[]{:S(2)}) %collective-permute-start.16) | collective-permute-done | bytes 122912 | tf_op jit(solution)/shard_map/ppermute | solution.py:265
  81.3 1.6 shard_map.88
  82.9 3.8 %collective-permute-start.21 = (bf16[4,192,512]{2,1,0:T(8,128)(2,1)S(1)}, bf16[4,192,512]{2,1,0:T(8,128)(2,1)S(1)}, u32[]{:S(2)}, u32[]{:S(2)}) collective-permute-start(bf16[4,192,512]{2,1,0:T(8,128)(2,1)S(1)} %get-tuple-element.92), channel_id=1, source_target_pairs={{0,32},{32,0},{1,33},{33,1},{2,34},{34,2},{3,35},{35,3},{4,36},{36... | collective-permute-start | bytes 2359304 | tf_op jit(solution)/shard_map/ppermute | solution.py:265
  88.1 7.6 %collective-permute-done.17.grad_far.far = bf16[176,768]{1,0:T(8,128)(2,1)S(1)} collective-permute-done((bf16[176,768]{1,0:T(8,128)(2,1)S(1)}, bf16[176,768]{1,0:T(8,128)(2,1)S(1)}, u32[]{:S(2)}, u32[]{:S(2)}) %collective-permute-start.17) | collective-permute-done | bytes 270368 | tf_op jit(solution)/shard_map/ppermute | solution.py:265
  95.7 4.2 %shard_map.89 = (f32[656,512]{1,0:T(8,128)S(1)}, f32[656,512]{1,0:T(8,128)S(1)}, bf16[656,512]{1,0:T(8,128)(2,1)S(1)}, f32[656,512]{1,0:T(8,128)S(1)}) custom-call(s32[4]{0:T(128)S(1)} %pad_add_fusion.place, bf16[160,384]{1,0:T(8,128)(2,1)S(1)} %fusion.13.act.near, bf16[160,384]{1,0:T(8,128)(2,1)S(1)} %collective-permute-done.16.far.act_far, ...), custom_call_target="tpu_custom_call" | custom-call | tf_op jit(solution)/shard_map/pallas_call | solution.py:31
  99.9 1.4 collective-permute-start.18
  101.3 4.0 %shard_map.90 = (f32[4,2,192,512]{3,2,1,0:T(8,128)}, bf16[4,192,512]{2,1,0:T(8,128)(2,1)S(1)}, bf16[4,192,512]{2,1,0:T(8,128)(2,1)S(1)}) custom-call(s32[4]{0:T(128)S(1)} %pad_add_fusion.place, bf16[176,768]{1,0:T(8,128)(2,1)S(1)} %shard_map.87.grad.near, bf16[176,768]{1,0:T(8,128)(2,1)S(1)} %collective-permute-done.17.grad_far.far, ...), custom_call_target="tpu_custom_call" | custom-call | tf_op jit(solution)/shard_map/pallas_call | solution.py:31
  106.1 3.9 %collective-permute-done.18 = bf16[656,512]{1,0:T(8,128)(2,1)} collective-permute-done((bf16[656,512]{1,0:T(8,128)(2,1)S(1)}, bf16[656,512]{1,0:T(8,128)(2,1)}, u32[]{:S(2)}, u32[]{:S(2)}) %collective-permute-start.18) | collective-permute-done | bytes 671776 | tf_op jit(solution)/shard_map/ppermute | solution.py:261
  110.0 1.7 %fusion.3 = (bf16[656,512]{1,0:T(8,128)(2,1)S(1)}, bf16[656,512]{1,0:T(8,128)(2,1)S(1)}) fusion(f32[656,512]{1,0:T(8,128)S(1)} %get-tuple-element.86, bf16[656,512]{1,0:T(8,128)(2,1)} %collective-permute-done.18, pred[]{:T(512)S(6)} %eq.3, f32[656,512]{1,0:T(8,128)S(1)} %get-tuple-element.84), kind=kLoop, calls=%fused_computation.7 | loop fusion | flops 2351104 | bytes 4702209 | tf_op jit(solution)/shard_map/convert_element_type | solution.py:361
  111.8 2.3 %collective-permute-start.23 = (bf16[656,512]{1,0:T(8,128)(2,1)S(1)}, bf16[656,512]{1,0:T(8,128)(2,1)S(1)}, u32[]{:S(2)}, u32[]{:S(2)}) collective-permute-start(bf16[656,512]{1,0:T(8,128)(2,1)S(1)} %get-tuple-element.94), channel_id=1, source_target_pairs={{0,6},{2,0},{4,2},{6,4},{1,7},{3,1},{5,3},{7,5},{8,14},{10,8},{12,... | collective-permute-start | bytes 2015240 | tf_op jit(solution)/shard_map/ppermute | solution.py:254
  114.7 1.6 collective-permute-start.22
  116.2 11.8 %collective-permute-done.23.one = bf16[656,512]{1,0:T(8,128)(2,1)S(1)} collective-permute-done((bf16[656,512]{1,0:T(8,128)(2,1)S(1)}, bf16[656,512]{1,0:T(8,128)(2,1)S(1)}, u32[]{:S(2)}, u32[]{:S(2)}) %collective-permute-start.23) | collective-permute-done | bytes 671776 | tf_op jit(solution)/shard_map/ppermute | solution.py:254
  128.0 3.1 %collective-permute-done.24.three = bf16[656,512]{1,0:T(8,128)(2,1)S(1)} collective-permute-done((bf16[656,512]{1,0:T(8,128)(2,1)S(1)}, bf16[656,512]{1,0:T(8,128)(2,1)S(1)}, u32[]{:S(2)}, u32[]{:S(2)}) %collective-permute-start.24) | collective-permute-done | bytes 671776 | tf_op jit(solution)/shard_map/ppermute | solution.py:254
  132.2 1.3 collective-permute-start.25
  133.8 3.6 %collective-permute-start.27 = (bf16[176,512]{1,0:T(8,128)(2,1)S(1)}, bf16[176,512]{1,0:T(8,128)(2,1)S(1)}, u32[]{:S(2)}, u32[]{:S(2)}) collective-permute-start(bf16[176,512]{1,0:T(8,128)(2,1)S(1)} %get-tuple-element.99), channel_id=1, source_target_pairs={{0,24},{8,0},{16,8},{24,16},{1,25},{9,1},{17,9},{25,17},{2,26},{10... | collective-permute-start | bytes 540680 | tf_op jit(solution)/shard_map/ppermute | solution.py:254
  137.4 1.5 collective-permute-start.28
  138.9 2.4 %collective-permute-start.29 = (bf16[176,512]{1,0:T(8,128)(2,1)S(1)}, bf16[176,512]{1,0:T(8,128)(2,1)S(1)}, u32[]{:S(2)}, u32[]{:S(2)}) collective-permute-start(bf16[176,512]{1,0:T(8,128)(2,1)S(1)} %get-tuple-element.101), channel_id=1, source_target_pairs={{0,8},{8,16},{16,24},{24,0},{1,9},{9,17},{17,25},{25,1},{2,10},{10... | collective-permute-start | bytes 540680 | tf_op jit(solution)/shard_map/ppermute | solution.py:254
  141.2 3.1 %collective-permute-done.27.refs_1_ = bf16[176,512]{1,0:T(8,128)(2,1)S(1)} collective-permute-done((bf16[176,512]{1,0:T(8,128)(2,1)S(1)}, bf16[176,512]{1,0:T(8,128)(2,1)S(1)}, u32[]{:S(2)}, u32[]{:S(2)}) %collective-permute-start.27) | collective-permute-done | bytes 180256 | tf_op jit(solution)/shard_map/ppermute | solution.py:254
  144.4 3.9 %collective-permute-done.28.refs_2_ = bf16[176,512]{1,0:T(8,128)(2,1)S(1)} collective-permute-done((bf16[176,512]{1,0:T(8,128)(2,1)S(1)}, bf16[176,512]{1,0:T(8,128)(2,1)S(1)}, u32[]{:S(2)}, u32[]{:S(2)}) %collective-permute-start.28) | collective-permute-done | bytes 180256 | tf_op jit(solution)/shard_map/ppermute | solution.py:254
  148.3 3.3 %collective-permute-done.29.refs_3_ = bf16[176,512]{1,0:T(8,128)(2,1)S(1)} collective-permute-done((bf16[176,512]{1,0:T(8,128)(2,1)S(1)}, bf16[176,512]{1,0:T(8,128)(2,1)S(1)}, u32[]{:S(2)}, u32[]{:S(2)}) %collective-permute-start.29) | collective-permute-done | bytes 180256 | tf_op jit(solution)/shard_map/ppermute | solution.py:254
  151.9 8.8 %collective-permute-start.30 = (bf16[3,192,512]{2,1,0:T(8,128)(2,1)S(1)}, bf16[3,192,512]{2,1,0:T(8,128)(2,1)S(1)}, u32[]{:S(2)}, u32[]{:S(2)}) collective-permute-start(bf16[3,192,512]{2,1,0:T(8,128)(2,1)S(1)} %fusion.9), channel_id=1, source_target_pairs={{0,0},{1,32},{32,1},{33,33},{2,2},{3,34},{34,3},{35,35},{4,4},{5,3... | collective-permute-start | bytes 1769480 | tf_op jit(solution)/shard_map/ppermute | solution.py:269
  160.7 1.7 %shard_map.92 = (bf16[128,512]{1,0:T(8,128)(2,1)}, bf16[128,512]{1,0:T(8,128)(2,1)}, f32[8,128]{1,0:T(8,128)S(1)}) custom-call(s32[4]{0:T(128)S(1)} %pad_add_fusion.place, s32[2,128]{1,0:T(2,128)S(1)} %bitcast.43, f32[2,128]{1,0:T(2,128)S(1)} %bitcast.45, bf16[320,128]{1,0:T(8,128)(2,1)S(1)} %get-tuple-element.57.placing, ...), custom_call_target="tpu_custom_call" | custom-call | tf_op jit(solution)/shard_map/pallas_call | solution.py:31
  163.0 5.3 %collective-permute-done.30 = bf16[3,192,512]{2,1,0:T(8,128)(2,1)S(1)} collective-permute-done((bf16[3,192,512]{2,1,0:T(8,128)(2,1)S(1)}, bf16[3,192,512]{2,1,0:T(8,128)(2,1)S(1)}, u32[]{:S(2)}, u32[]{:S(2)}) %collective-permute-start.30) | collective-permute-done | bytes 589856 | tf_op jit(solution)/shard_map/ppermute | solution.py:269
  168.2 1.2 bitcast_convert_fusion
  (66 shorter events, 8.3 us)
Async XLA Ops:
  0.6 26.9 %collective-permute-start = (bf16[3,192,512]{2,1,0:T(8,128)(2,1)}, bf16[3,192,512]{2,1,0:T(8,128)(2,1)}, u32[]{:S(2)}, u32[]{:S(2)}) collective-permute-start(bf16[3,192,512]{2,1,0:T(8,128)(2,1)} %bitcast.46), channel_id=1, source_target_pairs={{0,0},{1,32},{32,1},{33,33},{2,2},{3,34},{34,3},{35,35},{4,4},{5,3... | collective-permute-start | bytes 1769480 | tf_op jit(solution)/shard_map/ppermute | solution.py:269
  5.7 0.9 copy-start.6
  6.6 0.9 copy-start.7
  7.5 0.7 copy-start.8
  8.2 0.7 copy-start.10
  10.3 13.5 %collective-permute-start.1 = (bf16[160,512]{1,0:T(8,128)(2,1)S(1)}, bf16[160,512]{1,0:T(8,128)(2,1)S(1)}, u32[]{:S(2)}, u32[]{:S(2)}) collective-permute-start(bf16[160,512]{1,0:T(8,128)(2,1)S(1)} %get-tuple-element.59), channel_id=1, source_target_pairs={{0,8},{8,16},{16,24},{24,0},{1,9},{9,17},{17,25},{25,1},{2,10},{10... | collective-permute-start | bytes 491528 | tf_op jit(solution)/shard_map/ppermute | solution.py:254
  13.4 14.1 %collective-permute-start.2 = (bf16[160,512]{1,0:T(8,128)(2,1)S(1)}, bf16[160,512]{1,0:T(8,128)(2,1)S(1)}, u32[]{:S(2)}, u32[]{:S(2)}) collective-permute-start(bf16[160,512]{1,0:T(8,128)(2,1)S(1)} %get-tuple-element.60), channel_id=1, source_target_pairs={{0,16},{8,24},{16,0},{24,8},{1,17},{9,25},{17,1},{25,9},{2,18},{10... | collective-permute-start | bytes 491528 | tf_op jit(solution)/shard_map/ppermute | solution.py:254
  17.6 9.9 %collective-permute-start.3 = (bf16[160,512]{1,0:T(8,128)(2,1)S(1)}, bf16[160,512]{1,0:T(8,128)(2,1)S(1)}, u32[]{:S(2)}, u32[]{:S(2)}) collective-permute-start(bf16[160,512]{1,0:T(8,128)(2,1)S(1)} %get-tuple-element.61), channel_id=1, source_target_pairs={{0,24},{8,0},{16,8},{24,16},{1,25},{9,1},{17,9},{25,17},{2,26},{10... | collective-permute-start | bytes 491528 | tf_op jit(solution)/shard_map/ppermute | solution.py:254
  27.5 10.2 %collective-permute-start.4 = (bf16[3,192,512]{2,1,0:T(8,128)(2,1)}, bf16[3,192,512]{2,1,0:T(8,128)(2,1)S(1)}, u32[]{:S(2)}, u32[]{:S(2)}) collective-permute-start(bf16[3,192,512]{2,1,0:T(8,128)(2,1)} %collective-permute-done.refs_4_), channel_id=1, source_target_pairs={{0,64},{64,128},{128,192},{192,0},{1,65},{65,129},{129,193},{193,1... | collective-permute-start | bytes 1769480 | tf_op jit(solution)/shard_map/ppermute | solution.py:254
  28.7 8.9 %collective-permute-start.5 = (bf16[3,192,512]{2,1,0:T(8,128)(2,1)}, bf16[3,192,512]{2,1,0:T(8,128)(2,1)S(1)}, u32[]{:S(2)}, u32[]{:S(2)}) collective-permute-start(bf16[3,192,512]{2,1,0:T(8,128)(2,1)} %collective-permute-done.refs_4_), channel_id=1, source_target_pairs={{0,192},{64,0},{128,64},{192,128},{1,193},{65,1},{129,65},{193,129... | collective-permute-start | bytes 1769480 | tf_op jit(solution)/shard_map/ppermute | solution.py:254
  30.3 11.1 %collective-permute-start.6 = (bf16[640,512]{1,0:T(8,128)(2,1)S(1)}, bf16[640,512]{1,0:T(8,128)(2,1)S(1)}, u32[]{:S(2)}, u32[]{:S(2)}) collective-permute-start(bf16[640,512]{1,0:T(8,128)(2,1)S(1)} %constant_dynamic-update-slice_fusion.refs_0_), channel_id=1, source_target_pairs={{0,2},{2,4},{4,6},{6,0},{1,3},{3,5},{5,7},{7,1},{8,10},{10,12},{12... | collective-permute-start | bytes 1966088 | tf_op jit(solution)/shard_map/ppermute | solution.py:254
  31.6 9.7 %collective-permute-start.7 = (bf16[640,512]{1,0:T(8,128)(2,1)S(1)}, bf16[640,512]{1,0:T(8,128)(2,1)S(1)}, u32[]{:S(2)}, u32[]{:S(2)}) collective-permute-start(bf16[640,512]{1,0:T(8,128)(2,1)S(1)} %constant_dynamic-update-slice_fusion.refs_0_), channel_id=1, source_target_pairs={{0,6},{2,0},{4,2},{6,4},{1,7},{3,1},{5,3},{7,5},{8,14},{10,8},{12,... | collective-permute-start | bytes 1966088 | tf_op jit(solution)/shard_map/ppermute | solution.py:254
  37.7 19.3 %collective-permute-start.9 = (bf16[3,192,512]{2,1,0:T(8,128)(2,1)S(1)}, bf16[3,192,512]{2,1,0:T(8,128)(2,1)S(1)}, u32[]{:S(2)}, u32[]{:S(2)}) collective-permute-start(bf16[3,192,512]{2,1,0:T(8,128)(2,1)S(1)} %broadcast_select_fusion.1), channel_id=1, source_target_pairs={{0,64},{64,128},{128,192},{192,0},{32,224},{96,32},{160,96},{224,1... | collective-permute-start | bytes 1769480 | tf_op jit(solution)/shard_map/ppermute | solution.py:260
  41.3 22.0 %copy-start = (bf16[640,512]{1,0:T(8,128)(2,1)}, bf16[640,512]{1,0:T(8,128)(2,1)S(1)}, u32[]{:S(2)}) copy-start(bf16[640,512]{1,0:T(8,128)(2,1)S(1)} %collective-permute-done.6.refs_1_) | copy-start | bytes 1966084
  41.4 22.0 %copy-start.2 = (bf16[640,512]{1,0:T(8,128)(2,1)}, bf16[640,512]{1,0:T(8,128)(2,1)S(1)}, u32[]{:S(2)}) copy-start(bf16[640,512]{1,0:T(8,128)(2,1)S(1)} %collective-permute-done.7.refs_3_) | copy-start | bytes 1966084
  41.5 20.3 %collective-permute-start.8 = (bf16[640,512]{1,0:T(8,128)(2,1)S(1)}, bf16[640,512]{1,0:T(8,128)(2,1)S(1)}, u32[]{:S(2)}, u32[]{:S(2)}) collective-permute-start(bf16[640,512]{1,0:T(8,128)(2,1)S(1)} %broadcast_select_fusion), channel_id=1, source_target_pairs={{0,2},{2,4},{4,6},{6,0},{32,38},{34,32},{36,34},{38,36},{1,3},{3,5... | collective-permute-start | bytes 1966088 | tf_op jit(solution)/shard_map/ppermute | solution.py:261
  44.3 17.5 %collective-permute-start.10 = (bf16[3,192,512]{2,1,0:T(8,128)(2,1)}, bf16[3,192,512]{2,1,0:T(8,128)(2,1)S(1)}, u32[]{:S(2)}, u32[]{:S(2)}) collective-permute-start(bf16[3,192,512]{2,1,0:T(8,128)(2,1)} %collective-permute-done.refs_4_), channel_id=1, source_target_pairs={{0,32},{32,0},{1,33},{33,1},{2,34},{34,2},{3,35},{35,3},{4,36},{36... | collective-permute-start | bytes 1769480 | tf_op jit(solution)/shard_map/ppermute | solution.py:265
  56.5 5.2 %collective-permute-start.11 = (bf16[3,192,512]{2,1,0:T(8,128)(2,1)S(1)}, bf16[3,192,512]{2,1,0:T(8,128)(2,1)S(1)}, u32[]{:S(2)}, u32[]{:S(2)}) collective-permute-start(bf16[3,192,512]{2,1,0:T(8,128)(2,1)S(1)} %collective-permute-done.4.refs_5_), channel_id=1, source_target_pairs={{0,32},{32,0},{1,33},{33,1},{2,34},{34,2},{3,35},{35,3},{4,36},{36... | collective-permute-start | bytes 1769480 | tf_op jit(solution)/shard_map/ppermute | solution.py:265
  56.5 5.2 %collective-permute-start.13 = (bf16[3,192,512]{2,1,0:T(8,128)(2,1)S(1)}, bf16[3,192,512]{2,1,0:T(8,128)(2,1)S(1)}, u32[]{:S(2)}, u32[]{:S(2)}) collective-permute-start(bf16[3,192,512]{2,1,0:T(8,128)(2,1)S(1)} %collective-permute-done.5.refs_7_), channel_id=1, source_target_pairs={{0,32},{32,0},{1,33},{33,1},{2,34},{34,2},{3,35},{35,3},{4,36},{36... | collective-permute-start | bytes 1769480 | tf_op jit(solution)/shard_map/ppermute | solution.py:265
  57.0 6.3 %collective-permute-start.12 = (bf16[3,192,512]{2,1,0:T(8,128)(2,1)S(1)}, bf16[3,192,512]{2,1,0:T(8,128)(2,1)S(1)}, u32[]{:S(2)}, u32[]{:S(2)}) collective-permute-start(bf16[3,192,512]{2,1,0:T(8,128)(2,1)S(1)} %collective-permute-done.9.refs_6_), channel_id=1, source_target_pairs={{0,32},{32,0},{1,33},{33,1},{2,34},{34,2},{3,35},{35,3},{4,36},{36... | collective-permute-start | bytes 1769480 | tf_op jit(solution)/shard_map/ppermute | solution.py:265
  61.7 1.6 copy-start.4
  67.7 6.0 %collective-permute-start.14 = (bf16[160,768]{1,0:T(8,128)(2,1)S(1)}, bf16[160,768]{1,0:T(8,128)(2,1)S(1)}, u32[]{:S(2)}, u32[]{:S(2)}) collective-permute-start(bf16[160,768]{1,0:T(8,128)(2,1)S(1)} %get-tuple-element.72), channel_id=1, source_target_pairs={{0,1},{1,0},{2,3},{3,2},{4,5},{5,4},{6,7},{7,6},{8,9},{9,8},{10,11... | collective-permute-start | bytes 737288 | tf_op jit(solution)/shard_map/ppermute | solution.py:265
  69.7 11.6 %copy-start.5 = (bf16[640,512]{1,0:T(8,128)(2,1)S(1)}, bf16[640,512]{1,0:T(8,128)(2,1)}, u32[]{:S(2)}) copy-start(bf16[640,512]{1,0:T(8,128)(2,1)} %copy-done.4) | copy-start | bytes 1966084
  73.6 7.8 %copy-start.1 = (bf16[640,512]{1,0:T(8,128)(2,1)S(1)}, bf16[640,512]{1,0:T(8,128)(2,1)}, u32[]{:S(2)}) copy-start(bf16[640,512]{1,0:T(8,128)(2,1)} %copy-done) | copy-start | bytes 1966084
  73.6 7.7 %copy-start.3 = (bf16[640,512]{1,0:T(8,128)(2,1)S(1)}, bf16[640,512]{1,0:T(8,128)(2,1)}, u32[]{:S(2)}) copy-start(bf16[640,512]{1,0:T(8,128)(2,1)} %copy-done.2) | copy-start | bytes 1966084
  73.6 5.4 %collective-permute-start.15 = (bf16[160,384]{1,0:T(8,128)(2,1)S(1)}, bf16[160,384]{1,0:T(8,128)(2,1)S(1)}, u32[]{:S(2)}, u32[]{:S(2)}) collective-permute-start(bf16[160,384]{1,0:T(8,128)(2,1)S(1)} %get-tuple-element.73), channel_id=1, source_target_pairs={{0,1},{1,0},{2,3},{3,2},{4,5},{5,4},{6,7},{7,6},{8,9},{9,8},{10,11... | collective-permute-start | bytes 368648 | tf_op jit(solution)/shard_map/ppermute | solution.py:265
  73.8 7.5 %collective-permute-start.16 = (bf16[160,384]{1,0:T(8,128)(2,1)S(1)}, bf16[160,384]{1,0:T(8,128)(2,1)S(1)}, u32[]{:S(2)}, u32[]{:S(2)}) collective-permute-start(bf16[160,384]{1,0:T(8,128)(2,1)S(1)} %fusion.13.act.near), channel_id=1, source_target_pairs={{0,1},{1,0},{2,3},{3,2},{4,5},{5,4},{6,7},{7,6},{8,9},{9,8},{10,11... | collective-permute-start | bytes 368648 | tf_op jit(solution)/shard_map/ppermute | solution.py:265
  82.9 22.9 %collective-permute-start.21 = (bf16[4,192,512]{2,1,0:T(8,128)(2,1)S(1)}, bf16[4,192,512]{2,1,0:T(8,128)(2,1)S(1)}, u32[]{:S(2)}, u32[]{:S(2)}) collective-permute-start(bf16[4,192,512]{2,1,0:T(8,128)(2,1)S(1)} %get-tuple-element.92), channel_id=1, source_target_pairs={{0,32},{32,0},{1,33},{33,1},{2,34},{34,2},{3,35},{35,3},{4,36},{36... | collective-permute-start | bytes 2359304 | tf_op jit(solution)/shard_map/ppermute | solution.py:265
  87.5 8.2 %collective-permute-start.17 = (bf16[176,768]{1,0:T(8,128)(2,1)S(1)}, bf16[176,768]{1,0:T(8,128)(2,1)S(1)}, u32[]{:S(2)}, u32[]{:S(2)}) collective-permute-start(bf16[176,768]{1,0:T(8,128)(2,1)S(1)} %shard_map.87.grad.near), channel_id=1, source_target_pairs={{0,1},{1,0},{2,3},{3,2},{4,5},{5,4},{6,7},{7,6},{8,9},{9,8},{10,11... | collective-permute-start | bytes 811016 | tf_op jit(solution)/shard_map/ppermute | solution.py:265
  99.9 10.1 %collective-permute-start.18 = (bf16[656,512]{1,0:T(8,128)(2,1)S(1)}, bf16[656,512]{1,0:T(8,128)(2,1)}, u32[]{:S(2)}, u32[]{:S(2)}) collective-permute-start(bf16[656,512]{1,0:T(8,128)(2,1)S(1)} %get-tuple-element.85), channel_id=1, source_target_pairs={{0,2},{2,4},{4,6},{6,0},{32,38},{34,32},{36,34},{38,36},{1,3},{3,5... | collective-permute-start | bytes 2015240 | tf_op jit(solution)/shard_map/ppermute | solution.py:261
  105.3 6.4 %collective-permute-start.19 = (bf16[4,192,512]{2,1,0:T(8,128)(2,1)S(1)}, bf16[4,192,512]{2,1,0:T(8,128)(2,1)S(1)}, u32[]{:S(2)}, u32[]{:S(2)}) collective-permute-start(bf16[4,192,512]{2,1,0:T(8,128)(2,1)S(1)} %get-tuple-element.87), channel_id=1, source_target_pairs={{0,32},{32,0},{1,33},{33,1},{2,34},{34,2},{3,35},{35,3},{4,36},{36... | collective-permute-start | bytes 2359304 | tf_op jit(solution)/shard_map/ppermute | solution.py:265
  105.3 6.4 %collective-permute-start.20 = (bf16[4,192,512]{2,1,0:T(8,128)(2,1)S(1)}, bf16[4,192,512]{2,1,0:T(8,128)(2,1)S(1)}, u32[]{:S(2)}, u32[]{:S(2)}) collective-permute-start(bf16[4,192,512]{2,1,0:T(8,128)(2,1)S(1)} %get-tuple-element.88), channel_id=1, source_target_pairs={{0,32},{32,0},{1,33},{33,1},{2,34},{34,2},{3,35},{35,3},{4,36},{36... | collective-permute-start | bytes 2359304 | tf_op jit(solution)/shard_map/ppermute | solution.py:265
  110.0 4.1 %copy-start.12 = (f32[4,2,192,512]{3,2,1,0:T(8,128)S(1)}, f32[4,2,192,512]{3,2,1,0:T(8,128)}, u32[]{:S(2)}) copy-start(f32[4,2,192,512]{3,2,1,0:T(8,128)} %get-tuple-element.83) | copy-start | bytes 9437188
  111.8 16.2 %collective-permute-start.23 = (bf16[656,512]{1,0:T(8,128)(2,1)S(1)}, bf16[656,512]{1,0:T(8,128)(2,1)S(1)}, u32[]{:S(2)}, u32[]{:S(2)}) collective-permute-start(bf16[656,512]{1,0:T(8,128)(2,1)S(1)} %get-tuple-element.94), channel_id=1, source_target_pairs={{0,6},{2,0},{4,2},{6,4},{1,7},{3,1},{5,3},{7,5},{8,14},{10,8},{12,... | collective-permute-start | bytes 2015240 | tf_op jit(solution)/shard_map/ppermute | solution.py:254
  114.1 17.0 %collective-permute-start.24 = (bf16[656,512]{1,0:T(8,128)(2,1)S(1)}, bf16[656,512]{1,0:T(8,128)(2,1)S(1)}, u32[]{:S(2)}, u32[]{:S(2)}) collective-permute-start(bf16[656,512]{1,0:T(8,128)(2,1)S(1)} %get-tuple-element.95), channel_id=1, source_target_pairs={{0,2},{2,4},{4,6},{6,0},{1,3},{3,5},{5,7},{7,1},{8,10},{10,12},{12... | collective-permute-start | bytes 2015240 | tf_op jit(solution)/shard_map/ppermute | solution.py:254
  114.7 17.2 %collective-permute-start.22 = (bf16[3,192,512]{2,1,0:T(8,128)(2,1)S(1)}, bf16[3,192,512]{2,1,0:T(8,128)(2,1)S(1)}, u32[]{:S(2)}, u32[]{:S(2)}) collective-permute-start(bf16[3,192,512]{2,1,0:T(8,128)(2,1)S(1)} %pad_maximum_fusion), channel_id=1, source_target_pairs={{0,64},{64,128},{128,192},{192,0},{32,224},{96,32},{160,96},{224,1... | collective-permute-start | bytes 1769480 | tf_op jit(solution)/shard_map/ppermute | solution.py:260
  132.2 19.3 %collective-permute-start.25 = (bf16[3,192,512]{2,1,0:T(8,128)(2,1)S(1)}, bf16[3,192,512]{2,1,0:T(8,128)(2,1)S(1)}, u32[]{:S(2)}, u32[]{:S(2)}) collective-permute-start(bf16[3,192,512]{2,1,0:T(8,128)(2,1)S(1)} %get-tuple-element.129), channel_id=1, source_target_pairs={{0,192},{64,0},{128,64},{192,128},{1,193},{65,1},{129,65},{193,129... | collective-permute-start | bytes 1769480 | tf_op jit(solution)/shard_map/ppermute | solution.py:254
  133.6 18.0 %collective-permute-start.26 = (bf16[3,192,512]{2,1,0:T(8,128)(2,1)S(1)}, bf16[3,192,512]{2,1,0:T(8,128)(2,1)S(1)}, u32[]{:S(2)}, u32[]{:S(2)}) collective-permute-start(bf16[3,192,512]{2,1,0:T(8,128)(2,1)S(1)} %get-tuple-element.128), channel_id=1, source_target_pairs={{0,64},{64,128},{128,192},{192,0},{1,65},{65,129},{129,193},{193,1... | collective-permute-start | bytes 1769480 | tf_op jit(solution)/shard_map/ppermute | solution.py:254
  133.8 10.6 %collective-permute-start.27 = (bf16[176,512]{1,0:T(8,128)(2,1)S(1)}, bf16[176,512]{1,0:T(8,128)(2,1)S(1)}, u32[]{:S(2)}, u32[]{:S(2)}) collective-permute-start(bf16[176,512]{1,0:T(8,128)(2,1)S(1)} %get-tuple-element.99), channel_id=1, source_target_pairs={{0,24},{8,0},{16,8},{24,16},{1,25},{9,1},{17,9},{25,17},{2,26},{10... | collective-permute-start | bytes 540680 | tf_op jit(solution)/shard_map/ppermute | solution.py:254
  137.4 10.9 %collective-permute-start.28 = (bf16[176,512]{1,0:T(8,128)(2,1)S(1)}, bf16[176,512]{1,0:T(8,128)(2,1)S(1)}, u32[]{:S(2)}, u32[]{:S(2)}) collective-permute-start(bf16[176,512]{1,0:T(8,128)(2,1)S(1)} %get-tuple-element.100), channel_id=1, source_target_pairs={{0,16},{8,24},{16,0},{24,8},{1,17},{9,25},{17,1},{25,9},{2,18},{10... | collective-permute-start | bytes 540680 | tf_op jit(solution)/shard_map/ppermute | solution.py:254
  138.9 12.7 %collective-permute-start.29 = (bf16[176,512]{1,0:T(8,128)(2,1)S(1)}, bf16[176,512]{1,0:T(8,128)(2,1)S(1)}, u32[]{:S(2)}, u32[]{:S(2)}) collective-permute-start(bf16[176,512]{1,0:T(8,128)(2,1)S(1)} %get-tuple-element.101), channel_id=1, source_target_pairs={{0,8},{8,16},{16,24},{24,0},{1,9},{9,17},{17,25},{25,1},{2,10},{10... | collective-permute-start | bytes 540680 | tf_op jit(solution)/shard_map/ppermute | solution.py:254
  151.6 9.1 %copy-start.9 = (s32[128,2]{0,1:T(2,128)S(1)}, s32[128,2]{0,1:T(2,128)}, u32[]{:S(2)}) copy-start(s32[128,2]{0,1:T(2,128)} %param.6) | copy-start | bytes 3076
  151.6 9.1 %copy-start.11 = (f32[128,2]{0,1:T(2,128)S(1)}, f32[128,2]{0,1:T(2,128)}, u32[]{:S(2)}) copy-start(f32[128,2]{0,1:T(2,128)} %param.7) | copy-start | bytes 3076
  151.9 16.4 %collective-permute-start.30 = (bf16[3,192,512]{2,1,0:T(8,128)(2,1)S(1)}, bf16[3,192,512]{2,1,0:T(8,128)(2,1)S(1)}, u32[]{:S(2)}, u32[]{:S(2)}) collective-permute-start(bf16[3,192,512]{2,1,0:T(8,128)(2,1)S(1)} %fusion.9), channel_id=1, source_target_pairs={{0,0},{1,32},{32,1},{33,33},{2,2},{3,34},{34,3},{35,35},{4,4},{5,3... | collective-permute-start | bytes 1769480 | tf_op jit(solution)/shard_map/ppermute | solution.py:269

commit v5 on v4

--- a/solution.py
+++ b/solution.py
@@ -299,7 +299,8 @@
     )
 
     blocks = [blocks[0]] + [shift(blocks[k], "expert", k) for k in (1, 2, 3)]
-    own, *blocks[1:] = lax.optimization_barrier((turn(stacked_weights[0]), *blocks[1:]))
+    own, blocks[0] = lax.optimization_barrier((stacked_weights[0], blocks[0]))
+    own = turn(own)
     first = lax.axis_index("core") == 0
     near, back = shift(own, "x", 1), shift(own, "x", 3)
     own = [own, near, relay(jnp.where(first, near, back), "x"), back]
@@ -383,14 +384,11 @@
         return jnp.stack([near + far[i].astype(F32) for near, far in zip(kept, moved)])
 
     passed = relay(both_cores(2).astype(BF16), "x")
-    totals = call(total_kernel, place, [shares[0]] + arrived, [((unit, width), BF16)] * 4)
-    passed, totals[0] = lax.optimization_barrier((passed, totals[0]))
+    passed, arrived[0] = lax.optimization_barrier((passed, arrived[0]))
     near, back = halfway(passed, both_cores(1), both_cores(3))
     far_sums = [shift(near, "x", -1), shift(back, "x", 1)]
+    totals = call(total_kernel, place, [shares[0]] + arrived, [((unit, width), BF16)] * 4)
     returned = [totals[0]] + [shift(totals[k], "expert", -k) for k in (1, 2, 3)]
-    *far_sums, returned[1], returned[2], returned[3] = lax.optimization_barrier(
-        (*far_sums, *returned[1:])
-    )
     layer_output, token_grad, prob_grad = call(
         owner_kernel,
         place,
@@ -400,7 +398,11 @@
     weight_total = both_cores(0)
     for block in far_sums:
         weight_total = weight_total + block.astype(F32)
-    weight_grad = turn(weight_total.astype(BF16)).astype(F32)[None]
+    weight_total = weight_total.astype(BF16).reshape(2, 3 * half // 2, width)
+    parts = [turn(weight_total[n]) for n in range(2)]
+    *parts, layer_output = lax.optimization_barrier((*parts, layer_output))
+    weight_grad = jnp.concatenate([part.astype(F32) for part in parts])
+    weight_grad = weight_grad.reshape(stacked_weights.shape)
     return layer_output, token_grad, prob_grad[0:2].T, weight_grad
 
 

time: 170 us -> 162 us (0.953)
  starting transfers between devices: 74.9 us -> 56.3 us
  waiting for transfers between devices: 62.4 us -> 73.7 us
    ppermute x11, starting transfers between devices: 26.1 us -> 7.69 us  [swap(): return lax.ppermute(value, axis, [(0, 1), (1, 0)])]
    ppermute x2, waiting for transfers between devices: 0.01 us -> 6.83 us  [relay(): lax.ppermute(value, ('x', 'core'), [(2 * i + c, 2 * j + c) for c, i, j in...]
    ppermute x2 -> x3, waiting for transfers between devices: 5.27 us -> 9.61 us  [turn(): lax.ppermute(value, ('core', 'zl'), [(2 * c + z, 2 * z + c) for c in rang...]
    ppermute x14, waiting for transfers between devices: 38.1 us -> 34.7 us  [shift(): return lax.ppermute(value, axis, [(i, (i + step) % 4) for i in range(4)])]
    ppermute x2, waiting for transfers between devices: 3.95 us -> 6.8 us  [relay(): lax.ppermute(value, ('core', axis), [(4 * c + i, 4 * c + j) for c, i, j i...]
    ppermute x2 -> x3, starting transfers between devices: 13.8 us -> 11.7 us  [turn(): lax.ppermute(value, ('core', 'zl'), [(2 * c + z, 2 * z + c) for c in rang...]
  transfers between devices with their start and end apart: 31 -> 32, of which waited for: 15 -> 21; matrix products, arithmetic and copies ran while one was open for 2% -> 2% of each run, Pallas kernels for 10% -> 9%
where the time goes in v5:
time: 162 us
  waiting for transfers between devices  73.7 us (45%)
  starting transfers between devices  56.3 us (35%)
  Pallas kernels  22.7 us (14%)
  local copies, waits for them, and re-layouts  4.7 us (3%)
  other arithmetic  3.42 us (2%)
    ppermute x14, waiting for transfers between devices, shift(): return lax.ppermute(value, axis, [(i, (i + step) % 4) for i in range(4)])  34.7 us
    ppermute x14, starting transfers between devices, shift(): return lax.ppermute(value, axis, [(i, (i + step) % 4) for i in range(4)])  26.8 us
    pallas_call x9, Pallas kernels, call(): pl.pallas_call(kernel, out_shape=[jax.ShapeDtypeStruct(shape, kind) for s...  22.7 us
    ppermute x11, waiting for transfers between devices, swap(): return lax.ppermute(value, axis, [(0, 1), (1, 0)])  15.7 us
    ppermute x3, starting transfers between devices, turn(): lax.ppermute(value, ('core', 'zl'), [(2 * c + z, 2 * z + c) for c in rang...  11.7 us
    ppermute x3, waiting for transfers between devices, turn(): lax.ppermute(value, ('core', 'zl'), [(2 * c + z, 2 * z + c) for c in rang...  9.61 us
    ppermute x11, starting transfers between devices, swap(): return lax.ppermute(value, axis, [(0, 1), (1, 0)])  7.69 us
    ppermute x2, waiting for transfers between devices, relay(): lax.ppermute(value, ('x', 'core'), [(2 * i + c, 2 * j + c) for c, i, j in...  6.83 us
  transfers between devices with their start and end apart: 32, of which 21 were waited for; matrix products, arithmetic and copies ran while one was open for 2% of the time, Pallas kernels for 9%

profile of v5, /device:TPU:1, one launch (start us, length us, event | category | flops | bytes accessed | tf_op | source)
XLA Modules:
  0.0 161.8 jit_solution(3366152525211255481)
XLA Ops:
  0.7 0.9 copy-done.6
  1.6 0.9 copy-done.7
  3.9 1.5 shard_map.84
  5.4 4.9 %collective-permute-start.3 = (bf16[3,192,512]{2,1,0:T(8,128)(2,1)}, bf16[3,192,512]{2,1,0:T(8,128)(2,1)}, u32[]{:S(2)}, u32[]{:S(2)}) collective-permute-start(bf16[3,192,512]{2,1,0:T(8,128)(2,1)} %bitcast.52), channel_id=1, source_target_pairs={{0,0},{1,32},{32,1},{33,33},{2,2},{3,34},{34,3},{35,35},{4,4},{5,3... | collective-permute-start | bytes 1769480 | tf_op jit(solution)/shard_map/ppermute | solution.py:269
  10.3 3.1 %collective-permute-start = (bf16[160,512]{1,0:T(8,128)(2,1)S(1)}, bf16[160,512]{1,0:T(8,128)(2,1)S(1)}, u32[]{:S(2)}, u32[]{:S(2)}) collective-permute-start(bf16[160,512]{1,0:T(8,128)(2,1)S(1)} %get-tuple-element.55), channel_id=1, source_target_pairs={{0,8},{8,16},{16,24},{24,0},{1,9},{9,17},{17,25},{25,1},{2,10},{10... | collective-permute-start | bytes 491528 | tf_op jit(solution)/shard_map/ppermute | solution.py:254
  13.4 4.2 %collective-permute-start.1 = (bf16[160,512]{1,0:T(8,128)(2,1)S(1)}, bf16[160,512]{1,0:T(8,128)(2,1)S(1)}, u32[]{:S(2)}, u32[]{:S(2)}) collective-permute-start(bf16[160,512]{1,0:T(8,128)(2,1)S(1)} %get-tuple-element.56), channel_id=1, source_target_pairs={{0,16},{8,24},{16,0},{24,8},{1,17},{9,25},{17,1},{25,9},{2,18},{10... | collective-permute-start | bytes 491528 | tf_op jit(solution)/shard_map/ppermute | solution.py:254
  17.6 2.4 %collective-permute-start.2 = (bf16[160,512]{1,0:T(8,128)(2,1)S(1)}, bf16[160,512]{1,0:T(8,128)(2,1)S(1)}, u32[]{:S(2)}, u32[]{:S(2)}) collective-permute-start(bf16[160,512]{1,0:T(8,128)(2,1)S(1)} %get-tuple-element.57), channel_id=1, source_target_pairs={{0,24},{8,0},{16,8},{24,16},{1,25},{9,1},{17,9},{25,17},{2,26},{10... | collective-permute-start | bytes 491528 | tf_op jit(solution)/shard_map/ppermute | solution.py:254
  20.0 2.8 %collective-permute-done.3.refs_4_ = bf16[3,192,512]{2,1,0:T(8,128)(2,1)} collective-permute-done((bf16[3,192,512]{2,1,0:T(8,128)(2,1)}, bf16[3,192,512]{2,1,0:T(8,128)(2,1)}, u32[]{:S(2)}, u32[]{:S(2)}) %collective-permute-start.3) | collective-permute-done | bytes 589856 | tf_op jit(solution)/shard_map/ppermute | solution.py:269
  22.8 1.2 collective-permute-start.4
  24.0 1.5 collective-permute-start.5
  25.5 7.9 %collective-permute-done = bf16[160,512]{1,0:T(8,128)(2,1)S(1)} collective-permute-done((bf16[160,512]{1,0:T(8,128)(2,1)S(1)}, bf16[160,512]{1,0:T(8,128)(2,1)S(1)}, u32[]{:S(2)}, u32[]{:S(2)}) %collective-permute-start) | collective-permute-done | bytes 163872 | tf_op jit(solution)/shard_map/ppermute | solution.py:254
  33.5 2.7 %collective-permute-done.1 = bf16[160,512]{1,0:T(8,128)(2,1)S(1)} collective-permute-done((bf16[160,512]{1,0:T(8,128)(2,1)S(1)}, bf16[160,512]{1,0:T(8,128)(2,1)S(1)}, u32[]{:S(2)}, u32[]{:S(2)}) %collective-permute-start.1) | collective-permute-done | bytes 163872 | tf_op jit(solution)/shard_map/ppermute | solution.py:254
  36.2 1.4 collective-permute-start.6
  37.6 1.5 collective-permute-start.7
  39.2 2.6 %collective-permute-start.9 = (bf16[3,192,512]{2,1,0:T(8,128)(2,1)S(1)}, bf16[3,192,512]{2,1,0:T(8,128)(2,1)S(1)}, u32[]{:S(2)}, u32[]{:S(2)}) collective-permute-start(bf16[3,192,512]{2,1,0:T(8,128)(2,1)S(1)} %broadcast_select_fusion.1), channel_id=1, source_target_pairs={{0,64},{64,128},{128,192},{192,0},{32,224},{96,32},{160,96},{224,1... | collective-permute-start | bytes 1769480 | tf_op jit(solution)/shard_map/ppermute | solution.py:260
  41.8 9.8 %collective-permute-done.6.refs_1_ = bf16[640,512]{1,0:T(8,128)(2,1)S(1)} collective-permute-done((bf16[640,512]{1,0:T(8,128)(2,1)S(1)}, bf16[640,512]{1,0:T(8,128)(2,1)S(1)}, u32[]{:S(2)}, u32[]{:S(2)}) %collective-permute-start.6) | collective-permute-done | bytes 655392 | tf_op jit(solution)/shard_map/ppermute | solution.py:254
  52.0 2.7 %collective-permute-start.8 = (bf16[640,512]{1,0:T(8,128)(2,1)S(1)}, bf16[640,512]{1,0:T(8,128)(2,1)S(1)}, u32[]{:S(2)}, u32[]{:S(2)}) collective-permute-start(bf16[640,512]{1,0:T(8,128)(2,1)S(1)} %broadcast_select_fusion), channel_id=1, source_target_pairs={{0,2},{2,4},{4,6},{6,0},{32,38},{34,32},{36,34},{38,36},{1,3},{3,5... | collective-permute-start | bytes 1966088 | tf_op jit(solution)/shard_map/ppermute | solution.py:261
  55.7 2.0 %collective-permute-done.10.refs_8_ = bf16[3,192,512]{2,1,0:T(8,128)(2,1)S(1)} collective-permute-done((bf16[3,192,512]{2,1,0:T(8,128)(2,1)}, bf16[3,192,512]{2,1,0:T(8,128)(2,1)S(1)}, u32[]{:S(2)}, u32[]{:S(2)}) %collective-permute-start.10) | collective-permute-done | bytes 589856 | tf_op jit(solution)/shard_map/ppermute | solution.py:265
  58.4 3.8 %collective-permute-done.8.refs_2_ = bf16[640,512]{1,0:T(8,128)(2,1)S(1)} collective-permute-done((bf16[640,512]{1,0:T(8,128)(2,1)S(1)}, bf16[640,512]{1,0:T(8,128)(2,1)S(1)}, u32[]{:S(2)}, u32[]{:S(2)}) %collective-permute-start.8) | collective-permute-done | bytes 655392 | tf_op jit(solution)/shard_map/ppermute | solution.py:261
  63.1 4.3 %shard_map.85 = (f32[160,768]{1,0:T(8,128)S(1)}, bf16[160,768]{1,0:T(8,128)(2,1)S(1)}, bf16[768,2048]{1,0:T(8,128)(2,1)}) custom-call(s32[4]{0:T(128)S(1)} %pad_add_fusion.place, bf16[640,512]{1,0:T(8,128)(2,1)S(1)} %constant_dynamic-update-slice_fusion.refs_0_, bf16[640,512]{1,0:T(8,128)(2,1)} %copy-done, bf16[640,512]{1,0:T(8,128)(2,1)} %copy-done.4, ...), custom_call_target="tpu_custom_call" | custom-call | tf_op jit(solution)/shard_map/pallas_call | solution.py:31
  67.7 3.8 %shard_map.86 = (f32[160,384]{1,0:T(8,128)S(1)}, bf16[160,384]{1,0:T(8,128)(2,1)S(1)}, bf16[384,2048]{1,0:T(8,128)(2,1)}) custom-call(s32[4]{0:T(128)S(1)} %pad_add_fusion.place, bf16[640,512]{1,0:T(8,128)(2,1)S(1)} %constant_dynamic-update-slice_fusion.refs_0_, bf16[640,512]{1,0:T(8,128)(2,1)} %copy-done, bf16[640,512]{1,0:T(8,128)(2,1)} %copy-done.4, ...), custom_call_target="tpu_custom_call" | custom-call | tf_op jit(solution)/shard_map/pallas_call | solution.py:31
  71.5 1.5 collective-permute-start.15
  74.1 2.8 %collective-permute-done.15.far = bf16[160,384]{1,0:T(8,128)(2,1)S(1)} collective-permute-done((bf16[160,384]{1,0:T(8,128)(2,1)S(1)}, bf16[160,384]{1,0:T(8,128)(2,1)S(1)}, u32[]{:S(2)}, u32[]{:S(2)}) %collective-permute-start.15) | collective-permute-done | bytes 122912 | tf_op jit(solution)/shard_map/ppermute | solution.py:265
  76.9 1.6 collective-permute-done.16.far.act_far
  78.5 1.6 shard_map.88
  80.1 4.0 %collective-permute-start.21 = (bf16[4,192,512]{2,1,0:T(8,128)(2,1)S(1)}, bf16[4,192,512]{2,1,0:T(8,128)(2,1)S(1)}, u32[]{:S(2)}, u32[]{:S(2)}) collective-permute-start(bf16[4,192,512]{2,1,0:T(8,128)(2,1)S(1)} %get-tuple-element.85), channel_id=1, source_target_pairs={{0,32},{32,0},{1,33},{33,1},{2,34},{34,2},{3,35},{35,3},{4,36},{36... | collective-permute-start | bytes 2359304 | tf_op jit(solution)/shard_map/ppermute | solution.py:265
  85.1 7.9 %collective-permute-done.17.grad_far.far = bf16[176,768]{1,0:T(8,128)(2,1)S(1)} collective-permute-done((bf16[176,768]{1,0:T(8,128)(2,1)S(1)}, bf16[176,768]{1,0:T(8,128)(2,1)S(1)}, u32[]{:S(2)}, u32[]{:S(2)}) %collective-permute-start.17) | collective-permute-done | bytes 270368 | tf_op jit(solution)/shard_map/ppermute | solution.py:265
  93.0 4.2 %shard_map.89 = (f32[656,512]{1,0:T(8,128)S(1)}, f32[656,512]{1,0:T(8,128)S(1)}, bf16[656,512]{1,0:T(8,128)(2,1)S(1)}, f32[656,512]{1,0:T(8,128)S(1)}) custom-call(s32[4]{0:T(128)S(1)} %pad_add_fusion.place, bf16[160,384]{1,0:T(8,128)(2,1)S(1)} %fusion.13.act.near, bf16[160,384]{1,0:T(8,128)(2,1)S(1)} %collective-permute-done.16.far.act_far, ...), custom_call_target="tpu_custom_call" | custom-call | tf_op jit(solution)/shard_map/pallas_call | solution.py:31
  97.3 2.3 %collective-permute-start.18 = (bf16[656,512]{1,0:T(8,128)(2,1)S(1)}, bf16[656,512]{1,0:T(8,128)(2,1)S(1)}, u32[]{:S(2)}, u32[]{:S(2)}) collective-permute-start(bf16[656,512]{1,0:T(8,128)(2,1)S(1)} %get-tuple-element.78), channel_id=1, source_target_pairs={{0,2},{2,4},{4,6},{6,0},{32,38},{34,32},{36,34},{38,36},{1,3},{3,5... | collective-permute-start | bytes 2015240 | tf_op jit(solution)/shard_map/ppermute | solution.py:261
  99.6 4.0 %shard_map.90 = (f32[4,2,192,512]{3,2,1,0:T(8,128)}, bf16[4,192,512]{2,1,0:T(8,128)(2,1)S(1)}, bf16[4,192,512]{2,1,0:T(8,128)(2,1)S(1)}) custom-call(s32[4]{0:T(128)S(1)} %pad_add_fusion.place, bf16[176,768]{1,0:T(8,128)(2,1)S(1)} %shard_map.87.grad.near, bf16[176,768]{1,0:T(8,128)(2,1)S(1)} %collective-permute-done.17.grad_far.far, ...), custom_call_target="tpu_custom_call" | custom-call | tf_op jit(solution)/shard_map/pallas_call | solution.py:31
  104.3 3.0 %collective-permute-done.18 = bf16[656,512]{1,0:T(8,128)(2,1)S(1)} collective-permute-done((bf16[656,512]{1,0:T(8,128)(2,1)S(1)}, bf16[656,512]{1,0:T(8,128)(2,1)S(1)}, u32[]{:S(2)}, u32[]{:S(2)}) %collective-permute-start.18) | collective-permute-done | bytes 671776 | tf_op jit(solution)/shard_map/ppermute | solution.py:261
  107.8 3.2 %collective-permute-start.23 = (bf16[656,512]{1,0:T(8,128)(2,1)S(1)}, bf16[656,512]{1,0:T(8,128)(2,1)S(1)}, u32[]{:S(2)}, u32[]{:S(2)}) collective-permute-start(bf16[656,512]{1,0:T(8,128)(2,1)S(1)} %get-tuple-element.86), channel_id=1, source_target_pairs={{0,6},{2,0},{4,2},{6,4},{1,7},{3,1},{5,3},{7,5},{8,14},{10,8},{12,... | collective-permute-start | bytes 2015240 | tf_op jit(solution)/shard_map/ppermute | solution.py:254
  111.6 2.6 %collective-permute-start.22 = (bf16[3,192,512]{2,1,0:T(8,128)(2,1)S(1)}, bf16[3,192,512]{2,1,0:T(8,128)(2,1)S(1)}, u32[]{:S(2)}, u32[]{:S(2)}) collective-permute-start(bf16[3,192,512]{2,1,0:T(8,128)(2,1)S(1)} %pad_maximum_fusion), channel_id=1, source_target_pairs={{0,64},{64,128},{128,192},{192,0},{32,224},{96,32},{160,96},{224,1... | collective-permute-start | bytes 1769480 | tf_op jit(solution)/shard_map/ppermute | solution.py:260
  114.1 6.8 %collective-permute-done.22 = bf16[3,192,512]{2,1,0:T(8,128)(2,1)S(1)} collective-permute-done((bf16[3,192,512]{2,1,0:T(8,128)(2,1)S(1)}, bf16[3,192,512]{2,1,0:T(8,128)(2,1)S(1)}, u32[]{:S(2)}, u32[]{:S(2)}) %collective-permute-start.22) | collective-permute-done | bytes 589856 | tf_op jit(solution)/shard_map/ppermute | solution.py:260
  121.0 3.7 %collective-permute-done.23.one = bf16[656,512]{1,0:T(8,128)(2,1)S(1)} collective-permute-done((bf16[656,512]{1,0:T(8,128)(2,1)S(1)}, bf16[656,512]{1,0:T(8,128)(2,1)S(1)}, u32[]{:S(2)}, u32[]{:S(2)}) %collective-permute-start.23) | collective-permute-done | bytes 671776 | tf_op jit(solution)/shard_map/ppermute | solution.py:254
  125.0 1.3 collective-permute-start.25
  126.3 1.5 collective-permute-start.24
  127.8 4.2 %collective-permute-done.28.three = bf16[656,512]{1,0:T(8,128)(2,1)S(1)} collective-permute-done((bf16[656,512]{1,0:T(8,128)(2,1)S(1)}, bf16[656,512]{1,0:T(8,128)(2,1)S(1)}, u32[]{:S(2)}, u32[]{:S(2)}) %collective-permute-start.28) | collective-permute-done | bytes 671776 | tf_op jit(solution)/shard_map/ppermute | solution.py:254
  132.8 2.3 %collective-permute-start.29 = (bf16[176,512]{1,0:T(8,128)(2,1)S(1)}, bf16[176,512]{1,0:T(8,128)(2,1)S(1)}, u32[]{:S(2)}, u32[]{:S(2)}) collective-permute-start(bf16[176,512]{1,0:T(8,128)(2,1)S(1)} %get-tuple-element.93), channel_id=1, source_target_pairs={{0,24},{8,0},{16,8},{24,16},{1,25},{9,1},{17,9},{25,17},{2,26},{10... | collective-permute-start | bytes 540680 | tf_op jit(solution)/shard_map/ppermute | solution.py:254
  135.1 3.1 %collective-permute-start.30 = (bf16[176,512]{1,0:T(8,128)(2,1)S(1)}, bf16[176,512]{1,0:T(8,128)(2,1)S(1)}, u32[]{:S(2)}, u32[]{:S(2)}) collective-permute-start(bf16[176,512]{1,0:T(8,128)(2,1)S(1)} %get-tuple-element.94), channel_id=1, source_target_pairs={{0,16},{8,24},{16,0},{24,8},{1,17},{9,25},{17,1},{25,9},{2,18},{10... | collective-permute-start | bytes 540680 | tf_op jit(solution)/shard_map/ppermute | solution.py:254
  138.4 1.1 collective-permute-done.25
  139.9 4.9 %collective-permute-start.26 = (bf16[288,512]{1,0:T(8,128)(2,1)S(1)}, bf16[288,512]{1,0:T(8,128)(2,1)S(1)}, u32[]{:S(2)}, u32[]{:S(2)}) collective-permute-start(bf16[288,512]{1,0:T(8,128)(2,1)S(1)} %get-tuple-element.121), channel_id=1, source_target_pairs={{0,0},{1,32},{32,1},{33,33},{2,2},{3,34},{34,3},{35,35},{4,4},{5,3... | collective-permute-start | bytes 884744 | tf_op jit(solution)/shard_map/ppermute | solution.py:269
  144.7 1.9 %collective-permute-start.27 = (bf16[288,512]{1,0:T(8,128)(2,1)S(1)}, bf16[288,512]{1,0:T(8,128)(2,1)S(1)}, u32[]{:S(2)}, u32[]{:S(2)}) collective-permute-start(bf16[288,512]{1,0:T(8,128)(2,1)S(1)} %get-tuple-element.120), channel_id=1, source_target_pairs={{0,0},{1,32},{32,1},{33,33},{2,2},{3,34},{34,3},{35,35},{4,4},{5,3... | collective-permute-start | bytes 884744 | tf_op jit(solution)/shard_map/ppermute | solution.py:269
  147.3 4.2 %collective-permute-done.31.refs_3_ = bf16[176,512]{1,0:T(8,128)(2,1)S(1)} collective-permute-done((bf16[176,512]{1,0:T(8,128)(2,1)S(1)}, bf16[176,512]{1,0:T(8,128)(2,1)S(1)}, u32[]{:S(2)}, u32[]{:S(2)}) %collective-permute-start.31) | collective-permute-done | bytes 180256 | tf_op jit(solution)/shard_map/ppermute | solution.py:254
  151.5 1.7 %shard_map.92 = (bf16[128,512]{1,0:T(8,128)(2,1)}, bf16[128,512]{1,0:T(8,128)(2,1)}, f32[8,128]{1,0:T(8,128)S(1)}) custom-call(s32[4]{0:T(128)S(1)} %pad_add_fusion.place, s32[2,128]{1,0:T(2,128)S(1)} %bitcast.47, f32[2,128]{1,0:T(2,128)S(1)} %bitcast.49, bf16[320,128]{1,0:T(8,128)(2,1)S(1)} %get-tuple-element.88.placing, ...), custom_call_target="tpu_custom_call" | custom-call | tf_op jit(solution)/shard_map/pallas_call | solution.py:31
  153.8 3.6 %collective-permute-done.26 = bf16[288,512]{1,0:T(8,128)(2,1)S(1)} collective-permute-done((bf16[288,512]{1,0:T(8,128)(2,1)S(1)}, bf16[288,512]{1,0:T(8,128)(2,1)S(1)}, u32[]{:S(2)}, u32[]{:S(2)}) %collective-permute-start.26) | collective-permute-done | bytes 294944 | tf_op jit(solution)/shard_map/ppermute | solution.py:269
  157.4 3.2 %collective-permute-done.27 = bf16[288,512]{1,0:T(8,128)(2,1)S(1)} collective-permute-done((bf16[288,512]{1,0:T(8,128)(2,1)S(1)}, bf16[288,512]{1,0:T(8,128)(2,1)S(1)}, u32[]{:S(2)}, u32[]{:S(2)}) %collective-permute-start.27) | collective-permute-done | bytes 294944 | tf_op jit(solution)/shard_map/ppermute | solution.py:269
  160.6 1.2 convert.14
  (70 shorter events, 11.5 us)
Async XLA Ops:
  0.7 0.9 copy-start.6
  1.6 0.9 copy-start.7
  2.5 0.7 copy-start.8
  3.2 0.7 copy-start.10
  5.4 17.4 %collective-permute-start.3 = (bf16[3,192,512]{2,1,0:T(8,128)(2,1)}, bf16[3,192,512]{2,1,0:T(8,128)(2,1)}, u32[]{:S(2)}, u32[]{:S(2)}) collective-permute-start(bf16[3,192,512]{2,1,0:T(8,128)(2,1)} %bitcast.52), channel_id=1, source_target_pairs={{0,0},{1,32},{32,1},{33,33},{2,2},{3,34},{34,3},{35,35},{4,4},{5,3... | collective-permute-start | bytes 1769480 | tf_op jit(solution)/shard_map/ppermute | solution.py:269
  10.3 23.1 %collective-permute-start = (bf16[160,512]{1,0:T(8,128)(2,1)S(1)}, bf16[160,512]{1,0:T(8,128)(2,1)S(1)}, u32[]{:S(2)}, u32[]{:S(2)}) collective-permute-start(bf16[160,512]{1,0:T(8,128)(2,1)S(1)} %get-tuple-element.55), channel_id=1, source_target_pairs={{0,8},{8,16},{16,24},{24,0},{1,9},{9,17},{17,25},{25,1},{2,10},{10... | collective-permute-start | bytes 491528 | tf_op jit(solution)/shard_map/ppermute | solution.py:254
  13.4 22.8 %collective-permute-start.1 = (bf16[160,512]{1,0:T(8,128)(2,1)S(1)}, bf16[160,512]{1,0:T(8,128)(2,1)S(1)}, u32[]{:S(2)}, u32[]{:S(2)}) collective-permute-start(bf16[160,512]{1,0:T(8,128)(2,1)S(1)} %get-tuple-element.56), channel_id=1, source_target_pairs={{0,16},{8,24},{16,0},{24,8},{1,17},{9,25},{17,1},{25,9},{2,18},{10... | collective-permute-start | bytes 491528 | tf_op jit(solution)/shard_map/ppermute | solution.py:254
  17.6 18.6 %collective-permute-start.2 = (bf16[160,512]{1,0:T(8,128)(2,1)S(1)}, bf16[160,512]{1,0:T(8,128)(2,1)S(1)}, u32[]{:S(2)}, u32[]{:S(2)}) collective-permute-start(bf16[160,512]{1,0:T(8,128)(2,1)S(1)} %get-tuple-element.57), channel_id=1, source_target_pairs={{0,24},{8,0},{16,8},{24,16},{1,25},{9,1},{17,9},{25,17},{2,26},{10... | collective-permute-start | bytes 491528 | tf_op jit(solution)/shard_map/ppermute | solution.py:254
  22.8 16.3 %collective-permute-start.4 = (bf16[3,192,512]{2,1,0:T(8,128)(2,1)}, bf16[3,192,512]{2,1,0:T(8,128)(2,1)S(1)}, u32[]{:S(2)}, u32[]{:S(2)}) collective-permute-start(bf16[3,192,512]{2,1,0:T(8,128)(2,1)} %collective-permute-done.3.refs_4_), channel_id=1, source_target_pairs={{0,64},{64,128},{128,192},{192,0},{1,65},{65,129},{129,193},{193,1... | collective-permute-start | bytes 1769480 | tf_op jit(solution)/shard_map/ppermute | solution.py:254
  24.0 15.1 %collective-permute-start.5 = (bf16[3,192,512]{2,1,0:T(8,128)(2,1)}, bf16[3,192,512]{2,1,0:T(8,128)(2,1)S(1)}, u32[]{:S(2)}, u32[]{:S(2)}) collective-permute-start(bf16[3,192,512]{2,1,0:T(8,128)(2,1)} %collective-permute-done.3.refs_4_), channel_id=1, source_target_pairs={{0,192},{64,0},{128,64},{192,128},{1,193},{65,1},{129,65},{193,129... | collective-permute-start | bytes 1769480 | tf_op jit(solution)/shard_map/ppermute | solution.py:254
  36.2 15.4 %collective-permute-start.6 = (bf16[640,512]{1,0:T(8,128)(2,1)S(1)}, bf16[640,512]{1,0:T(8,128)(2,1)S(1)}, u32[]{:S(2)}, u32[]{:S(2)}) collective-permute-start(bf16[640,512]{1,0:T(8,128)(2,1)S(1)} %constant_dynamic-update-slice_fusion.refs_0_), channel_id=1, source_target_pairs={{0,2},{2,4},{4,6},{6,0},{1,3},{3,5},{5,7},{7,1},{8,10},{10,12},{12... | collective-permute-start | bytes 1966088 | tf_op jit(solution)/shard_map/ppermute | solution.py:254
  37.6 14.3 %collective-permute-start.7 = (bf16[640,512]{1,0:T(8,128)(2,1)S(1)}, bf16[640,512]{1,0:T(8,128)(2,1)S(1)}, u32[]{:S(2)}, u32[]{:S(2)}) collective-permute-start(bf16[640,512]{1,0:T(8,128)(2,1)S(1)} %constant_dynamic-update-slice_fusion.refs_0_), channel_id=1, source_target_pairs={{0,6},{2,0},{4,2},{6,4},{1,7},{3,1},{5,3},{7,5},{8,14},{10,8},{12,... | collective-permute-start | bytes 1966088 | tf_op jit(solution)/shard_map/ppermute | solution.py:254
  39.2 16.0 %collective-permute-start.9 = (bf16[3,192,512]{2,1,0:T(8,128)(2,1)S(1)}, bf16[3,192,512]{2,1,0:T(8,128)(2,1)S(1)}, u32[]{:S(2)}, u32[]{:S(2)}) collective-permute-start(bf16[3,192,512]{2,1,0:T(8,128)(2,1)S(1)} %broadcast_select_fusion.1), channel_id=1, source_target_pairs={{0,64},{64,128},{128,192},{192,0},{32,224},{96,32},{160,96},{224,1... | collective-permute-start | bytes 1769480 | tf_op jit(solution)/shard_map/ppermute | solution.py:260
  51.6 10.6 %copy-start = (bf16[640,512]{1,0:T(8,128)(2,1)}, bf16[640,512]{1,0:T(8,128)(2,1)S(1)}, u32[]{:S(2)}) copy-start(bf16[640,512]{1,0:T(8,128)(2,1)S(1)} %collective-permute-done.6.refs_1_) | copy-start | bytes 1966084
  51.9 10.3 %copy-start.2 = (bf16[640,512]{1,0:T(8,128)(2,1)}, bf16[640,512]{1,0:T(8,128)(2,1)S(1)}, u32[]{:S(2)}) copy-start(bf16[640,512]{1,0:T(8,128)(2,1)S(1)} %collective-permute-done.7.refs_3_) | copy-start | bytes 1966084
  52.0 10.2 %collective-permute-start.8 = (bf16[640,512]{1,0:T(8,128)(2,1)S(1)}, bf16[640,512]{1,0:T(8,128)(2,1)S(1)}, u32[]{:S(2)}, u32[]{:S(2)}) collective-permute-start(bf16[640,512]{1,0:T(8,128)(2,1)S(1)} %broadcast_select_fusion), channel_id=1, source_target_pairs={{0,2},{2,4},{4,6},{6,0},{32,38},{34,32},{36,34},{38,36},{1,3},{3,5... | collective-permute-start | bytes 1966088 | tf_op jit(solution)/shard_map/ppermute | solution.py:261
  54.7 3.0 %collective-permute-start.10 = (bf16[3,192,512]{2,1,0:T(8,128)(2,1)}, bf16[3,192,512]{2,1,0:T(8,128)(2,1)S(1)}, u32[]{:S(2)}, u32[]{:S(2)}) collective-permute-start(bf16[3,192,512]{2,1,0:T(8,128)(2,1)} %collective-permute-done.3.refs_4_), channel_id=1, source_target_pairs={{0,32},{32,0},{1,33},{33,1},{2,34},{34,2},{3,35},{35,3},{4,36},{36... | collective-permute-start | bytes 1769480 | tf_op jit(solution)/shard_map/ppermute | solution.py:265
  54.7 3.0 %collective-permute-start.11 = (bf16[3,192,512]{2,1,0:T(8,128)(2,1)S(1)}, bf16[3,192,512]{2,1,0:T(8,128)(2,1)S(1)}, u32[]{:S(2)}, u32[]{:S(2)}) collective-permute-start(bf16[3,192,512]{2,1,0:T(8,128)(2,1)S(1)} %collective-permute-done.4.refs_5_), channel_id=1, source_target_pairs={{0,32},{32,0},{1,33},{33,1},{2,34},{34,2},{3,35},{35,3},{4,36},{36... | collective-permute-start | bytes 1769480 | tf_op jit(solution)/shard_map/ppermute | solution.py:265
  55.2 3.2 %collective-permute-start.13 = (bf16[3,192,512]{2,1,0:T(8,128)(2,1)S(1)}, bf16[3,192,512]{2,1,0:T(8,128)(2,1)S(1)}, u32[]{:S(2)}, u32[]{:S(2)}) collective-permute-start(bf16[3,192,512]{2,1,0:T(8,128)(2,1)S(1)} %collective-permute-done.5.refs_7_), channel_id=1, source_target_pairs={{0,32},{32,0},{1,33},{33,1},{2,34},{34,2},{3,35},{35,3},{4,36},{36... | collective-permute-start | bytes 1769480 | tf_op jit(solution)/shard_map/ppermute | solution.py:265
  55.2 7.0 %collective-permute-start.12 = (bf16[3,192,512]{2,1,0:T(8,128)(2,1)S(1)}, bf16[3,192,512]{2,1,0:T(8,128)(2,1)S(1)}, u32[]{:S(2)}, u32[]{:S(2)}) collective-permute-start(bf16[3,192,512]{2,1,0:T(8,128)(2,1)S(1)} %collective-permute-done.9.refs_6_), channel_id=1, source_target_pairs={{0,32},{32,0},{1,33},{33,1},{2,34},{34,2},{3,35},{35,3},{4,36},{36... | collective-permute-start | bytes 1769480 | tf_op jit(solution)/shard_map/ppermute | solution.py:265
  62.2 0.9 copy-start.4
  67.4 6.5 %collective-permute-start.14 = (bf16[160,768]{1,0:T(8,128)(2,1)S(1)}, bf16[160,768]{1,0:T(8,128)(2,1)S(1)}, u32[]{:S(2)}, u32[]{:S(2)}) collective-permute-start(bf16[160,768]{1,0:T(8,128)(2,1)S(1)} %get-tuple-element.65), channel_id=1, source_target_pairs={{0,1},{1,0},{2,3},{3,2},{4,5},{5,4},{6,7},{7,6},{8,9},{9,8},{10,11... | collective-permute-start | bytes 737288 | tf_op jit(solution)/shard_map/ppermute | solution.py:265
  67.7 10.8 %copy-start.5 = (bf16[640,512]{1,0:T(8,128)(2,1)S(1)}, bf16[640,512]{1,0:T(8,128)(2,1)}, u32[]{:S(2)}) copy-start(bf16[640,512]{1,0:T(8,128)(2,1)} %copy-done.4) | copy-start | bytes 1966084
  71.5 6.9 %copy-start.1 = (bf16[640,512]{1,0:T(8,128)(2,1)S(1)}, bf16[640,512]{1,0:T(8,128)(2,1)}, u32[]{:S(2)}) copy-start(bf16[640,512]{1,0:T(8,128)(2,1)} %copy-done) | copy-start | bytes 1966084
  71.5 6.9 %copy-start.3 = (bf16[640,512]{1,0:T(8,128)(2,1)S(1)}, bf16[640,512]{1,0:T(8,128)(2,1)}, u32[]{:S(2)}) copy-start(bf16[640,512]{1,0:T(8,128)(2,1)} %copy-done.2) | copy-start | bytes 1966084
  71.5 5.3 %collective-permute-start.15 = (bf16[160,384]{1,0:T(8,128)(2,1)S(1)}, bf16[160,384]{1,0:T(8,128)(2,1)S(1)}, u32[]{:S(2)}, u32[]{:S(2)}) collective-permute-start(bf16[160,384]{1,0:T(8,128)(2,1)S(1)} %get-tuple-element.66), channel_id=1, source_target_pairs={{0,1},{1,0},{2,3},{3,2},{4,5},{5,4},{6,7},{7,6},{8,9},{9,8},{10,11... | collective-permute-start | bytes 368648 | tf_op jit(solution)/shard_map/ppermute | solution.py:265
  74.0 4.4 %collective-permute-start.16 = (bf16[160,384]{1,0:T(8,128)(2,1)S(1)}, bf16[160,384]{1,0:T(8,128)(2,1)S(1)}, u32[]{:S(2)}, u32[]{:S(2)}) collective-permute-start(bf16[160,384]{1,0:T(8,128)(2,1)S(1)} %fusion.13.act.near), channel_id=1, source_target_pairs={{0,1},{1,0},{2,3},{3,2},{4,5},{5,4},{6,7},{7,6},{8,9},{9,8},{10,11... | collective-permute-start | bytes 368648 | tf_op jit(solution)/shard_map/ppermute | solution.py:265
  80.1 24.0 %collective-permute-start.21 = (bf16[4,192,512]{2,1,0:T(8,128)(2,1)S(1)}, bf16[4,192,512]{2,1,0:T(8,128)(2,1)S(1)}, u32[]{:S(2)}, u32[]{:S(2)}) collective-permute-start(bf16[4,192,512]{2,1,0:T(8,128)(2,1)S(1)} %get-tuple-element.85), channel_id=1, source_target_pairs={{0,32},{32,0},{1,33},{33,1},{2,34},{34,2},{3,35},{35,3},{4,36},{36... | collective-permute-start | bytes 2359304 | tf_op jit(solution)/shard_map/ppermute | solution.py:265
  84.8 8.2 %collective-permute-start.17 = (bf16[176,768]{1,0:T(8,128)(2,1)S(1)}, bf16[176,768]{1,0:T(8,128)(2,1)S(1)}, u32[]{:S(2)}, u32[]{:S(2)}) collective-permute-start(bf16[176,768]{1,0:T(8,128)(2,1)S(1)} %shard_map.87.grad.near), channel_id=1, source_target_pairs={{0,1},{1,0},{2,3},{3,2},{4,5},{5,4},{6,7},{7,6},{8,9},{9,8},{10,11... | collective-permute-start | bytes 811016 | tf_op jit(solution)/shard_map/ppermute | solution.py:265
  97.3 10.0 %collective-permute-start.18 = (bf16[656,512]{1,0:T(8,128)(2,1)S(1)}, bf16[656,512]{1,0:T(8,128)(2,1)S(1)}, u32[]{:S(2)}, u32[]{:S(2)}) collective-permute-start(bf16[656,512]{1,0:T(8,128)(2,1)S(1)} %get-tuple-element.78), channel_id=1, source_target_pairs={{0,2},{2,4},{4,6},{6,0},{32,38},{34,32},{36,34},{38,36},{1,3},{3,5... | collective-permute-start | bytes 2015240 | tf_op jit(solution)/shard_map/ppermute | solution.py:261
  103.6 4.2 %collective-permute-start.19 = (bf16[4,192,512]{2,1,0:T(8,128)(2,1)S(1)}, bf16[4,192,512]{2,1,0:T(8,128)(2,1)S(1)}, u32[]{:S(2)}, u32[]{:S(2)}) collective-permute-start(bf16[4,192,512]{2,1,0:T(8,128)(2,1)S(1)} %get-tuple-element.80), channel_id=1, source_target_pairs={{0,32},{32,0},{1,33},{33,1},{2,34},{34,2},{3,35},{35,3},{4,36},{36... | collective-permute-start | bytes 2359304 | tf_op jit(solution)/shard_map/ppermute | solution.py:265
  103.6 4.2 %collective-permute-start.20 = (bf16[4,192,512]{2,1,0:T(8,128)(2,1)S(1)}, bf16[4,192,512]{2,1,0:T(8,128)(2,1)S(1)}, u32[]{:S(2)}, u32[]{:S(2)}) collective-permute-start(bf16[4,192,512]{2,1,0:T(8,128)(2,1)S(1)} %get-tuple-element.81), channel_id=1, source_target_pairs={{0,32},{32,0},{1,33},{33,1},{2,34},{34,2},{3,35},{35,3},{4,36},{36... | collective-permute-start | bytes 2359304 | tf_op jit(solution)/shard_map/ppermute | solution.py:265
  107.3 3.7 %copy-start.12 = (f32[4,2,192,512]{3,2,1,0:T(8,128)S(1)}, f32[4,2,192,512]{3,2,1,0:T(8,128)}, u32[]{:S(2)}) copy-start(f32[4,2,192,512]{3,2,1,0:T(8,128)} %get-tuple-element.76) | copy-start | bytes 9437188
  107.8 16.9 %collective-permute-start.23 = (bf16[656,512]{1,0:T(8,128)(2,1)S(1)}, bf16[656,512]{1,0:T(8,128)(2,1)S(1)}, u32[]{:S(2)}, u32[]{:S(2)}) collective-permute-start(bf16[656,512]{1,0:T(8,128)(2,1)S(1)} %get-tuple-element.86), channel_id=1, source_target_pairs={{0,6},{2,0},{4,2},{6,4},{1,7},{3,1},{5,3},{7,5},{8,14},{10,8},{12,... | collective-permute-start | bytes 2015240 | tf_op jit(solution)/shard_map/ppermute | solution.py:254
  111.6 9.4 %collective-permute-start.22 = (bf16[3,192,512]{2,1,0:T(8,128)(2,1)S(1)}, bf16[3,192,512]{2,1,0:T(8,128)(2,1)S(1)}, u32[]{:S(2)}, u32[]{:S(2)}) collective-permute-start(bf16[3,192,512]{2,1,0:T(8,128)(2,1)S(1)} %pad_maximum_fusion), channel_id=1, source_target_pairs={{0,64},{64,128},{128,192},{192,0},{32,224},{96,32},{160,96},{224,1... | collective-permute-start | bytes 1769480 | tf_op jit(solution)/shard_map/ppermute | solution.py:260
  114.1 17.9 %collective-permute-start.28 = (bf16[656,512]{1,0:T(8,128)(2,1)S(1)}, bf16[656,512]{1,0:T(8,128)(2,1)S(1)}, u32[]{:S(2)}, u32[]{:S(2)}) collective-permute-start(bf16[656,512]{1,0:T(8,128)(2,1)S(1)} %get-tuple-element.91), channel_id=1, source_target_pairs={{0,2},{2,4},{4,6},{6,0},{1,3},{3,5},{5,7},{7,1},{8,10},{10,12},{12... | collective-permute-start | bytes 2015240 | tf_op jit(solution)/shard_map/ppermute | solution.py:254
  125.0 14.5 %collective-permute-start.25 = (bf16[3,192,512]{2,1,0:T(8,128)(2,1)S(1)}, bf16[3,192,512]{2,1,0:T(8,128)(2,1)S(1)}, u32[]{:S(2)}, u32[]{:S(2)}) collective-permute-start(bf16[3,192,512]{2,1,0:T(8,128)(2,1)S(1)} %get-tuple-element.123), channel_id=1, source_target_pairs={{0,64},{64,128},{128,192},{192,0},{1,65},{65,129},{129,193},{193,1... | collective-permute-start | bytes 1769480 | tf_op jit(solution)/shard_map/ppermute | solution.py:254
  126.3 13.2 %collective-permute-start.24 = (bf16[3,192,512]{2,1,0:T(8,128)(2,1)S(1)}, bf16[3,192,512]{2,1,0:T(8,128)(2,1)S(1)}, u32[]{:S(2)}, u32[]{:S(2)}) collective-permute-start(bf16[3,192,512]{2,1,0:T(8,128)(2,1)S(1)} %get-tuple-element.122), channel_id=1, source_target_pairs={{0,192},{64,0},{128,64},{192,128},{1,193},{65,1},{129,65},{193,129... | collective-permute-start | bytes 1769480 | tf_op jit(solution)/shard_map/ppermute | solution.py:254
  132.8 13.9 %collective-permute-start.29 = (bf16[176,512]{1,0:T(8,128)(2,1)S(1)}, bf16[176,512]{1,0:T(8,128)(2,1)S(1)}, u32[]{:S(2)}, u32[]{:S(2)}) collective-permute-start(bf16[176,512]{1,0:T(8,128)(2,1)S(1)} %get-tuple-element.93), channel_id=1, source_target_pairs={{0,24},{8,0},{16,8},{24,16},{1,25},{9,1},{17,9},{25,17},{2,26},{10... | collective-permute-start | bytes 540680 | tf_op jit(solution)/shard_map/ppermute | solution.py:254
  135.1 12.2 %collective-permute-start.30 = (bf16[176,512]{1,0:T(8,128)(2,1)S(1)}, bf16[176,512]{1,0:T(8,128)(2,1)S(1)}, u32[]{:S(2)}, u32[]{:S(2)}) collective-permute-start(bf16[176,512]{1,0:T(8,128)(2,1)S(1)} %get-tuple-element.94), channel_id=1, source_target_pairs={{0,16},{8,24},{16,0},{24,8},{1,17},{9,25},{17,1},{25,9},{2,18},{10... | collective-permute-start | bytes 540680 | tf_op jit(solution)/shard_map/ppermute | solution.py:254
  138.2 13.3 %collective-permute-start.31 = (bf16[176,512]{1,0:T(8,128)(2,1)S(1)}, bf16[176,512]{1,0:T(8,128)(2,1)S(1)}, u32[]{:S(2)}, u32[]{:S(2)}) collective-permute-start(bf16[176,512]{1,0:T(8,128)(2,1)S(1)} %get-tuple-element.95), channel_id=1, source_target_pairs={{0,8},{8,16},{16,24},{24,0},{1,9},{9,17},{17,25},{25,1},{2,10},{10... | collective-permute-start | bytes 540680 | tf_op jit(solution)/shard_map/ppermute | solution.py:254
  139.8 11.7 %copy-start.9 = (s32[128,2]{0,1:T(2,128)S(1)}, s32[128,2]{0,1:T(2,128)}, u32[]{:S(2)}) copy-start(s32[128,2]{0,1:T(2,128)} %param.6) | copy-start | bytes 3076
  139.8 11.7 %copy-start.11 = (f32[128,2]{0,1:T(2,128)S(1)}, f32[128,2]{0,1:T(2,128)}, u32[]{:S(2)}) copy-start(f32[128,2]{0,1:T(2,128)} %param.7) | copy-start | bytes 3076
  139.9 17.5 %collective-permute-start.26 = (bf16[288,512]{1,0:T(8,128)(2,1)S(1)}, bf16[288,512]{1,0:T(8,128)(2,1)S(1)}, u32[]{:S(2)}, u32[]{:S(2)}) collective-permute-start(bf16[288,512]{1,0:T(8,128)(2,1)S(1)} %get-tuple-element.121), channel_id=1, source_target_pairs={{0,0},{1,32},{32,1},{33,33},{2,2},{3,34},{34,3},{35,35},{4,4},{5,3... | collective-permute-start | bytes 884744 | tf_op jit(solution)/shard_map/ppermute | solution.py:269
  144.7 15.8 %collective-permute-start.27 = (bf16[288,512]{1,0:T(8,128)(2,1)S(1)}, bf16[288,512]{1,0:T(8,128)(2,1)S(1)}, u32[]{:S(2)}, u32[]{:S(2)}) collective-permute-start(bf16[288,512]{1,0:T(8,128)(2,1)S(1)} %get-tuple-element.120), channel_id=1, source_target_pairs={{0,0},{1,32},{32,1},{33,33},{2,2},{3,34},{34,3},{35,35},{4,4},{5,3... | collective-permute-start | bytes 884744 | tf_op jit(solution)/shard_map/ppermute | solution.py:269

commit v6 on v5

--- a/solution.py
+++ b/solution.py
@@ -39,22 +39,13 @@
 
 
 def expert_rows(place, ids, k):
-    expert = lax.rem(place[0] + k, 4)
+    expert = lax.rem(place[0] + k, 4).astype(F32)
     return ids[0:1, :] == expert, ids[1:2, :] == expert
 
 
-def slots_kernel(place, ids_far, probs_far, tokens, grads, placing, *refs):
-    outs, ids, probs, token_copy, grad_copy, sems = refs[0:4], *refs[4:9]
-    copies = [
-        pltpu.make_async_copy(source, target, sems.at[n])
-        for n, (source, target) in enumerate(
-            [(ids_far, ids), (probs_far, probs), (tokens, token_copy), (grads, grad_copy)]
-        )
-    ]
-    for copy in copies:
-        copy.start()
-    copies[0].wait()
-    copies[1].wait()
+def slots_kernel(place, small, wide, placing, *outs):
+    ids, probs = small.at[0:2], small.at[2:4]
+    width = wide.shape[1] // 2
     rows = ids.shape[1]
     before = (
         lax.broadcasted_iota(jnp.int32, (rows, rows), 0)
@@ -74,27 +65,25 @@
         )
         placing[k * CAP : (k + 1) * CAP, :] = chosen.astype(F32).astype(BF16)
         scales.append(jnp.sum(jnp.where(chosen, weight, 0.0), axis=1, keepdims=True))
-    copies[2].wait()
-    copies[3].wait()
     for k in range(4):
         hot = placing[k * CAP : (k + 1) * CAP, :]
-        outs[k][0:CAP, :] = nn(hot, token_copy[...]).astype(BF16)
-        outs[k][CAP : 2 * CAP, :] = (scales[k] * nn(hot, grad_copy[...])).astype(BF16)
-
-
-def fetch(own, other, joined, sems, names, place):
+        outs[k][0:CAP, :] = nn(hot, wide[:, 0:width]).astype(BF16)
+        outs[k][CAP : 2 * CAP, :] = (scales[k] * nn(hot, wide[:, width:])).astype(BF16)
+
+
+def fetch(own, other, joined, sems, place):
     half, width = own[0].shape[1:]
     copies = []
     for block in range(4):
         spot = lax.rem(place[2] - place[1] + block + 4, 4)
         columns = pl.ds(pl.multiple_of(spot * width, width), width)
-        for n, m in enumerate(names):
+        for m in range(3):
             for h, source in enumerate((own[block], other[block])):
                 copies.append(
                     pltpu.make_async_copy(
                         source.at[m],
-                        joined.at[pl.ds((2 * n + h) * half, half), columns],
-                        sems.at[block, n, h],
+                        joined.at[pl.ds((2 * m + h) * half, half), columns],
+                        sems.at[block, m, h],
                     )
                 )
     for copy in copies:
@@ -108,16 +97,19 @@
         target[k * CAP : (k + 1) * CAP, :] = source[first : first + CAP, :]
 
 
-def project_kernel(names, second, place, *refs):
+def project_kernel(place, *refs):
     rows, own, other = refs[0:4], refs[4:8], refs[8:12]
     keep, send, joined, wide, total, sems = refs[12:18]
     width = rows[0].shape[1]
-    copies = fetch(own, other, joined, sems, names, place)
-    for j in range(4):
-        take_rows(wide.at[:, pl.ds(j * width, width)], rows[j], second)
+    hidden = keep.shape[1] // 3
+    copies = fetch(own, other, joined, sems, place)
+    for second in range(2):
+        for j in range(4):
+            take_rows(wide.at[second, :, pl.ds(j * width, width)], rows[j], second)
     for copy in copies:
         copy.wait()
-    total[...] = nt(wide[...], joined[...])
+    total[:, 0 : 2 * hidden] = nt(wide[0], joined[0 : 2 * hidden, :])
+    total[:, 2 * hidden :] = nt(wide[1], joined[2 * hidden :, :])
     part = keep.shape[0]
     keep[...] = total[pl.ds(pl.multiple_of(place[3] * part, 32), part), :]
     send[...] = total[pl.ds(pl.multiple_of((1 - place[3]) * part, 32), part), :].astype(BF16)
@@ -139,17 +131,21 @@
     return total
 
 
-def hidden_kernel(place, both, act, keep, far, out):
-    part, width = keep.shape
-    gate, up = both[:, 0:width], both[:, width : 2 * width]
+def hidden_kernel(place, keep, far, out):
+    part, width = keep.shape[0], keep.shape[1] // 3
+    gate, up, grad = [
+        keep[:, n * width : (n + 1) * width] + far[:, n * width : (n + 1) * width].astype(F32)
+        for n in range(3)
+    ]
     sigmoid = 1.0 / (1.0 + jnp.exp(-gate))
     swish = gate * sigmoid
-    grad = keep[...] + far[...].astype(F32)
+    act = (swish * up).astype(BF16)
     out[0:part, 0:width] = (
         grad * up * sigmoid * (1.0 + gate * (1.0 - sigmoid))
     ).astype(BF16)
     out[0:part, width : 2 * width] = (grad * swish).astype(BF16)
-    share = jnp.sum(act[...].astype(F32) * grad, axis=1, keepdims=True)
+    out[0:part, 2 * width :] = act
+    share = jnp.sum(act.astype(F32) * grad, axis=1, keepdims=True)
     out[part:, :] = jnp.zeros((TILE, out.shape[1]), BF16)
     marks = jnp.zeros((TILE, 128), F32)
     shape = (CAP, 128)
@@ -168,19 +164,18 @@
     target[pl.ds(pl.multiple_of((1 - zl) * part, 32), part), :] = theirs[0:part, :]
 
 
-def share_kernel(place, act, act_far, grad, grad_far, pair, down, *refs):
-    outs, acts, grads = refs[0:4], *refs[4:6]
-    part, width = act.shape[0], outs[0].shape[1]
-    zl = place[3]
-    join(acts, act, act_far, zl)
-    join(grads, grad, grad_far, zl)
-    marks = grad[part:, 0:128].astype(F32) + grad_far[part:, 0:128].astype(F32)
+def share_kernel(place, near, far, weights, *refs):
+    outs, joined = refs[0:4], refs[4]
+    part, width = joined.shape[0] // 2, outs[0].shape[1]
+    hidden = near.shape[1] // 3
+    join(joined, near, far, place[3])
+    marks = near[part:, 0:128].astype(F32) + far[part:, 0:128].astype(F32)
     unit = 2 * CAP
     for j in (1, 3, 2, 0):
         kind = outs[j].dtype
         columns = slice(j * width, (j + 1) * width)
-        out = nn(acts[...], down[:, columns])
-        back = nn(grads[...], pair[:, columns])
+        out = nn(joined[:, 2 * hidden :], weights[2 * hidden :, columns])
+        back = nn(joined[:, 0 : 2 * hidden], weights[0 : 2 * hidden, columns])
         for k in range(4):
             start, rows = k * unit, slice(k * CAP, (k + 1) * CAP)
             outs[j][start : start + CAP, :] = out[rows, :].astype(kind)
@@ -207,18 +202,19 @@
         outs[k][unit:, 0:128] = marked_rows(row, 0).astype(BF16)
 
 
-def weight_kernel(second, place, near, far, *refs):
-    rows, keep, joined, chosen = refs[0:4], refs[4], *refs[-2:]
-    sends = refs[5:-2]
+def weight_kernel(place, near, far, *refs):
+    rows, keep, sends = refs[0:4], refs[4], refs[5:8]
+    joined, chosen = refs[8:10]
     half = keep.shape[2]
     join(joined, near, far, place[3])
     for j in range(4):
         block = lax.rem(place[1] - place[2] + j + 4, 4)
-        take_rows(chosen, rows[j], second)
-        total = tn(joined[...], chosen[...])
-        for m in range(keep.shape[1]):
-            keep[block, m] = total[2 * m * half : (2 * m + 1) * half, :]
-            sends[m][block] = total[(2 * m + 1) * half : (2 * m + 2) * half, :].astype(BF16)
+        for m, second in ((2, 1), (0, 0), (1, 0)):
+            if m != 1:
+                take_rows(chosen, rows[j], second)
+            total = tn(joined[:, 2 * m * half : 2 * (m + 1) * half], chosen[...])
+            keep[block, m] = total[0:half, :]
+            sends[m][block] = total[half:, :].astype(BF16)
 
 
 def column(row):
@@ -228,7 +224,8 @@
     return jnp.sum(jnp.where(same, row, 0.0), axis=1, keepdims=True)
 
 
-def owner_kernel(place, ids, probs, placing, *refs):
+def owner_kernel(place, small, placing, *refs):
+    ids, probs = small.at[0:2], small.at[2:4]
     blocks, layer, token, prob = refs[0:4], *refs[4:7]
     total = jnp.zeros(layer.shape, F32)
     grads = jnp.zeros(token.shape, F32)
@@ -276,31 +273,24 @@
     slots = 4 * CAP
     part = slots // 2
     place = jnp.stack(
-        [lax.axis_index(name) for name in ("expert", "x", "y", "zl")]
+        [lax.axis_index(name) for name in ("expert", "x", "y", "zl", "core")]
     ).astype(jnp.int32)
-    ids, probs = expert_ids.T, gate_probs.T
+    small = jnp.concatenate([expert_ids.T.astype(F32), gate_probs.T])
+    wide = jnp.concatenate([tokens, out_grad], axis=1)
     vmem = pl.BlockSpec(memory_space=pltpu.VMEM)
     hbm = pl.BlockSpec(memory_space=pl.ANY)
-    far = pl.BlockSpec(memory_space=pltpu.HBM)
 
     placing, *blocks = call(
         slots_kernel,
         place,
-        [ids, probs, tokens, out_grad],
+        [small, wide],
         [((slots, rows), BF16)] + [((2 * CAP, width), BF16)] * 4,
-        [
-            pltpu.VMEM(ids.shape, jnp.int32),
-            pltpu.VMEM(probs.shape, F32),
-            pltpu.VMEM((rows, width), BF16),
-            pltpu.VMEM((rows, width), BF16),
-            pltpu.SemaphoreType.DMA((4,)),
-        ],
-        [far, far, far, far],
     )
 
     blocks = [blocks[0]] + [shift(blocks[k], "expert", k) for k in (1, 2, 3)]
     own, blocks[0] = lax.optimization_barrier((stacked_weights[0], blocks[0]))
-    own = turn(own)
+    turned = lax.ppermute(own, ("core", "zl"), [(1, 2), (2, 1)])
+    own = jnp.where(place[4] == place[3], own, turned)
     first = lax.axis_index("core") == 0
     near, back = shift(own, "x", 1), shift(own, "x", 3)
     own = [own, near, relay(jnp.where(first, near, back), "x"), back]
@@ -312,49 +302,25 @@
     other = [swap(block, "core") for block in own]
     blocks += [near, relay(jnp.where(first, near, back), "y"), back]
 
-    def project(names, second):
-        wide = len(names) * hidden
-        return call(
-            functools.partial(project_kernel, names, second),
-            place,
-            blocks + own + other,
-            [((part, wide), F32), ((part, wide), BF16), ((wide, 4 * width), BF16)],
-            [
-                pltpu.VMEM((slots, 4 * width), BF16),
-                pltpu.VMEM((slots, wide), F32),
-                pltpu.SemaphoreType.DMA((4, 2, 2)),
-            ],
-            [vmem] * 4 + [hbm] * 8,
-        )
-
-    keep, send, pair_weights = project((0, 1), 0)
-    both = keep + swap(send, "zl").astype(F32)
-    gate, up = both[:, :hidden], both[:, hidden:]
-    activation = (gate * jax.nn.sigmoid(gate) * up).astype(BF16)
-    activation_far = swap(activation, "zl")
-    keep, send, down_weights = project((2,), 1)
-    send, activation_far = lax.optimization_barrier((swap(send, "zl"), activation_far))
-    hidden_grad = call(
+    keep, send, weights = call(
+        project_kernel,
+        place,
+        blocks + own + other,
+        [((part, 3 * hidden), F32), ((part, 3 * hidden), BF16), ((3 * hidden, 4 * width), BF16)],
+        [
+            pltpu.VMEM((2, slots, 4 * width), BF16),
+            pltpu.VMEM((slots, 3 * hidden), F32),
+            pltpu.SemaphoreType.DMA((4, 3, 2)),
+        ],
+        [vmem] * 4 + [hbm] * 8,
+    )
+    hidden_near = call(
         hidden_kernel,
         place,
-        [both, activation, keep, send],
-        [((part + TILE, 2 * hidden), BF16)],
+        [keep, swap(send, "zl")],
+        [((part + TILE, 3 * hidden), BF16)],
     )[0]
-    hidden_far = swap(hidden_grad, "zl")
-
-    def weight_terms(near, far, second):
-        count = near.shape[1] // hidden
-        shape = (4, count, half, width)
-        return call(
-            functools.partial(weight_kernel, second),
-            place,
-            [near, far] + blocks,
-            [(shape, F32)] + [((4, half, width), BF16)] * count,
-            [pltpu.VMEM((slots, near.shape[1]), BF16), pltpu.VMEM((slots, width), BF16)],
-        )
-
-    down_keep, down_send = weight_terms(activation, activation_far, 1)
-    hidden_far, down_keep = lax.optimization_barrier((hidden_far, down_keep))
+    hidden_far = swap(hidden_near, "zl")
 
     def halfway(passed, near, back):
         passed = passed.astype(F32)
@@ -365,26 +331,29 @@
     shares = call(
         share_kernel,
         place,
-        [activation, activation_far, hidden_grad, hidden_far, pair_weights, down_weights],
-        [((8 * CAP + TILE, width), kind) for kind in (F32, F32, BF16, F32)],
-        [pltpu.VMEM((slots, hidden), BF16), pltpu.VMEM((slots, 2 * hidden), BF16)],
+        [hidden_near, hidden_far, weights],
+        [((8 * CAP + TILE, width), F32)] + [((8 * CAP + TILE, width), BF16)] * 3,
+        [pltpu.VMEM((slots, 3 * hidden), BF16)],
     )
     passed = relay(shares[2], "y")
-    shares[0], hidden_grad = lax.optimization_barrier((shares[0], hidden_grad))
-    pair_keep, *pair_send = weight_terms(hidden_grad, hidden_far, 0)
-    pair_far = [swap(send, "core") for send in pair_send]
+    shares[0], hidden_near = lax.optimization_barrier((shares[0], hidden_near))
+    keep, *sends = call(
+        weight_kernel,
+        place,
+        [hidden_near, hidden_far] + blocks,
+        [((4, 3, half, width), F32)] + [((4, half, width), BF16)] * 3,
+        [pltpu.VMEM((slots, 3 * hidden), BF16), pltpu.VMEM((slots, width), BF16)],
+    )
+    moved = [swap(send, "core") for send in sends]
     near, back = halfway(passed, shares[1], shares[3])
-    near, back, *pair_far = lax.optimization_barrier((near, back, *pair_far))
+    near, back, *moved = lax.optimization_barrier((near, back, *moved))
     arrived = [shift(near, "y", -1), shift(back, "y", 1)]
-    down_far = swap(down_send, "core")
 
     def both_cores(i):
-        kept = (pair_keep[i, 0], pair_keep[i, 1], down_keep[i, 0])
-        moved = (*pair_far, down_far)
-        return jnp.stack([near + far[i].astype(F32) for near, far in zip(kept, moved)])
+        return jnp.stack([keep[i, m] + moved[m][i].astype(F32) for m in range(3)])
 
     passed = relay(both_cores(2).astype(BF16), "x")
-    passed, arrived[0] = lax.optimization_barrier((passed, arrived[0]))
+    passed, *arrived = lax.optimization_barrier((passed, *arrived))
     near, back = halfway(passed, both_cores(1), both_cores(3))
     far_sums = [shift(near, "x", -1), shift(back, "x", 1)]
     totals = call(total_kernel, place, [shares[0]] + arrived, [((unit, width), BF16)] * 4)
@@ -392,7 +361,7 @@
     layer_output, token_grad, prob_grad = call(
         owner_kernel,
         place,
-        [ids, probs, placing] + returned,
+        [small, placing] + returned,
         [((rows, width), BF16), ((rows, width), BF16), ((8, rows), F32)],
     )
     weight_total = both_cores(0)

time: 162 us -> 159 us (0.981)
  starting transfers between devices: 56.3 us -> 47.7 us
  waiting for transfers between devices: 73.7 us -> 79.4 us
  other arithmetic: 3.42 us -> 7.14 us
  Pallas kernels: 22.7 us -> 20 us
    ppermute x0 -> x1, waiting for transfers between devices: none -> 6.23 us  [body(): turned = lax.ppermute(own, ('core', 'zl'), [(1, 2), (2, 1)])]
    ppermute x3 -> x2, waiting for transfers between devices: 9.61 us -> 3.82 us  [turn(): lax.ppermute(value, ('core', 'zl'), [(2 * c + z, 2 * z + c) for c in rang...]
    ppermute x11 -> x9, waiting for transfers between devices: 15.7 us -> 21.5 us  [swap(): return lax.ppermute(value, axis, [(0, 1), (1, 0)])]
    ppermute x0 -> x1, starting transfers between devices: none -> 4.94 us  [body(): turned = lax.ppermute(own, ('core', 'zl'), [(1, 2), (2, 1)])]
    ppermute x2, starting transfers between devices: 4.97 us -> 1.1 us  [relay(): lax.ppermute(value, ('core', axis), [(4 * c + i, 4 * c + j) for c, i, j i...]
    ppermute x3 -> x2, starting transfers between devices: 11.7 us -> 7.9 us  [turn(): lax.ppermute(value, ('core', 'zl'), [(2 * c + z, 2 * z + c) for c in rang...]
    ppermute x11 -> x9, starting transfers between devices: 7.69 us -> 3.97 us  [swap(): return lax.ppermute(value, axis, [(0, 1), (1, 0)])]
    pallas_call x9 -> x7, Pallas kernels: 22.7 us -> 20 us  [call(): pl.pallas_call(kernel, out_shape=[jax.ShapeDtypeStruct(shape, kind) for s...]
  transfers between devices with their start and end apart: 32 -> 30, of which waited for: 21 -> 19; matrix products, arithmetic and copies ran while one was open for 2% -> 3% of each run, Pallas kernels for 9% -> 5%
where the time goes in v6:
time: 159 us
  waiting for transfers between devices  79.4 us (50%)
  starting transfers between devices  47.7 us (30%)
  Pallas kernels  20 us (13%)
  other arithmetic  7.14 us (4%)
  local copies, waits for them, and re-layouts  3.63 us (2%)
    ppermute x14, waiting for transfers between devices, shift(): return lax.ppermute(value, axis, [(i, (i + step) % 4) for i in range(4)])  32.7 us
    ppermute x14, starting transfers between devices, shift(): return lax.ppermute(value, axis, [(i, (i + step) % 4) for i in range(4)])  24.7 us
    ppermute x9, waiting for transfers between devices, swap(): return lax.ppermute(value, axis, [(0, 1), (1, 0)])  21.5 us
    pallas_call x7, Pallas kernels, call(): pl.pallas_call(kernel, out_shape=[jax.ShapeDtypeStruct(shape, kind) for s...  20 us
    ppermute x2, waiting for transfers between devices, relay(): lax.ppermute(value, ('core', axis), [(4 * c + i, 4 * c + j) for c, i, j i...  8.43 us
    ppermute x2, starting transfers between devices, turn(): lax.ppermute(value, ('core', 'zl'), [(2 * c + z, 2 * z + c) for c in rang...  7.9 us
    ppermute x2, waiting for transfers between devices, relay(): lax.ppermute(value, ('x', 'core'), [(2 * i + c, 2 * j + c) for c, i, j in...  6.83 us
    ppermute x1, waiting for transfers between devices, body(): turned = lax.ppermute(own, ('core', 'zl'), [(1, 2), (2, 1)])  6.23 us
  transfers between devices with their start and end apart: 30, of which 19 were waited for; matrix products, arithmetic and copies ran while one was open for 3% of the time, Pallas kernels for 5%

profile of v6, /device:TPU:1, one launch (start us, length us, event | category | flops | bytes accessed | tf_op | source)
XLA Modules:
  0.0 158.8 jit_solution(2426274818183292767)
XLA Ops:
  0.7 0.7 convert_bitcast_fusion
  1.4 0.7 pad_maximum_fusion.3.small
  2.1 1.0 pad_maximum_fusion.2.wide
  3.2 1.0 shard_map.84
  4.2 4.9 %collective-permute-start.3 = (bf16[3,192,512]{2,1,0:T(8,128)(2,1)}, bf16[3,192,512]{2,1,0:T(8,128)(2,1)S(1)}, u32[]{:S(2)}, u32[]{:S(2)}) collective-permute-start(bf16[3,192,512]{2,1,0:T(8,128)(2,1)} %bitcast.50), channel_id=1, source_target_pairs={{1,32},{32,1},{3,34},{34,3},{5,36},{36,5},{7,38},{38,7},{9,40},{40... | collective-permute-start | bytes 1769480 | tf_op jit(solution)/shard_map/ppermute | solution.py:292
  9.1 3.1 %collective-permute-start = (bf16[160,512]{1,0:T(8,128)(2,1)S(1)}, bf16[160,512]{1,0:T(8,128)(2,1)}, u32[]{:S(2)}, u32[]{:S(2)}) collective-permute-start(bf16[160,512]{1,0:T(8,128)(2,1)S(1)} %get-tuple-element.49), channel_id=1, source_target_pairs={{0,8},{8,16},{16,24},{24,0},{1,9},{9,17},{17,25},{25,1},{2,10},{10... | collective-permute-start | bytes 491528 | tf_op jit(solution)/shard_map/ppermute | solution.py:251
  12.2 4.2 %collective-permute-start.1 = (bf16[160,512]{1,0:T(8,128)(2,1)S(1)}, bf16[160,512]{1,0:T(8,128)(2,1)S(1)}, u32[]{:S(2)}, u32[]{:S(2)}) collective-permute-start(bf16[160,512]{1,0:T(8,128)(2,1)S(1)} %get-tuple-element.50), channel_id=1, source_target_pairs={{0,16},{8,24},{16,0},{24,8},{1,17},{9,25},{17,1},{25,9},{2,18},{10... | collective-permute-start | bytes 491528 | tf_op jit(solution)/shard_map/ppermute | solution.py:251
  16.4 2.4 %collective-permute-start.2 = (bf16[160,512]{1,0:T(8,128)(2,1)S(1)}, bf16[160,512]{1,0:T(8,128)(2,1)S(1)}, u32[]{:S(2)}, u32[]{:S(2)}) collective-permute-start(bf16[160,512]{1,0:T(8,128)(2,1)S(1)} %get-tuple-element.51), channel_id=1, source_target_pairs={{0,24},{8,0},{16,8},{24,16},{1,25},{9,1},{17,9},{25,17},{2,26},{10... | collective-permute-start | bytes 491528 | tf_op jit(solution)/shard_map/ppermute | solution.py:251
  18.8 6.2 %collective-permute-done.3 = bf16[3,192,512]{2,1,0:T(8,128)(2,1)S(1)} collective-permute-done((bf16[3,192,512]{2,1,0:T(8,128)(2,1)}, bf16[3,192,512]{2,1,0:T(8,128)(2,1)S(1)}, u32[]{:S(2)}, u32[]{:S(2)}) %collective-permute-start.3) | collective-permute-done | bytes 589856 | tf_op jit(solution)/shard_map/ppermute | solution.py:292
  25.1 2.6 %collective-permute-start.5 = (bf16[3,192,512]{2,1,0:T(8,128)(2,1)S(1)}, bf16[3,192,512]{2,1,0:T(8,128)(2,1)S(1)}, u32[]{:S(2)}, u32[]{:S(2)}) collective-permute-start(bf16[3,192,512]{2,1,0:T(8,128)(2,1)S(1)} %broadcast_select_fusion.2.refs_4_), channel_id=1, source_target_pairs={{0,192},{64,0},{128,64},{192,128},{1,193},{65,1},{129,65},{193,129... | collective-permute-start | bytes 1769480 | tf_op jit(solution)/shard_map/ppermute | solution.py:251
  27.7 2.9 %collective-permute-done = bf16[160,512]{1,0:T(8,128)(2,1)} collective-permute-done((bf16[160,512]{1,0:T(8,128)(2,1)S(1)}, bf16[160,512]{1,0:T(8,128)(2,1)}, u32[]{:S(2)}, u32[]{:S(2)}) %collective-permute-start) | collective-permute-done | bytes 163872 | tf_op jit(solution)/shard_map/ppermute | solution.py:251
  30.6 0.9 constant_dynamic-update-slice_fusion.2
  31.5 4.8 %collective-permute-done.1 = bf16[160,512]{1,0:T(8,128)(2,1)S(1)} collective-permute-done((bf16[160,512]{1,0:T(8,128)(2,1)S(1)}, bf16[160,512]{1,0:T(8,128)(2,1)S(1)}, u32[]{:S(2)}, u32[]{:S(2)}) %collective-permute-start.1) | collective-permute-done | bytes 163872 | tf_op jit(solution)/shard_map/ppermute | solution.py:251
  36.4 2.8 %collective-permute-start.7 = (bf16[640,512]{1,0:T(8,128)(2,1)S(1)}, bf16[640,512]{1,0:T(8,128)(2,1)S(1)}, u32[]{:S(2)}, u32[]{:S(2)}) collective-permute-start(bf16[640,512]{1,0:T(8,128)(2,1)S(1)} %constant_dynamic-update-slice_fusion.refs_0_), channel_id=1, source_target_pairs={{0,6},{2,0},{4,2},{6,4},{1,7},{3,1},{5,3},{7,5},{8,14},{10,8},{12,... | collective-permute-start | bytes 1966088 | tf_op jit(solution)/shard_map/ppermute | solution.py:251
  39.3 2.6 %collective-permute-start.9 = (bf16[3,192,512]{2,1,0:T(8,128)(2,1)S(1)}, bf16[3,192,512]{2,1,0:T(8,128)(2,1)S(1)}, u32[]{:S(2)}, u32[]{:S(2)}) collective-permute-start(bf16[3,192,512]{2,1,0:T(8,128)(2,1)S(1)} %broadcast_select_fusion.1), channel_id=1, source_target_pairs={{0,64},{64,128},{128,192},{192,0},{32,224},{96,32},{160,96},{224,1... | collective-permute-start | bytes 1769480 | tf_op jit(solution)/shard_map/ppermute | solution.py:257
  41.8 4.9 %collective-permute-done.7.refs_3_ = bf16[640,512]{1,0:T(8,128)(2,1)S(1)} collective-permute-done((bf16[640,512]{1,0:T(8,128)(2,1)S(1)}, bf16[640,512]{1,0:T(8,128)(2,1)S(1)}, u32[]{:S(2)}, u32[]{:S(2)}) %collective-permute-start.7) | collective-permute-done | bytes 655392 | tf_op jit(solution)/shard_map/ppermute | solution.py:251
  46.7 5.6 %collective-permute-done.6.refs_1_ = bf16[640,512]{1,0:T(8,128)(2,1)S(1)} collective-permute-done((bf16[640,512]{1,0:T(8,128)(2,1)S(1)}, bf16[640,512]{1,0:T(8,128)(2,1)S(1)}, u32[]{:S(2)}, u32[]{:S(2)}) %collective-permute-start.6) | collective-permute-done | bytes 655392 | tf_op jit(solution)/shard_map/ppermute | solution.py:251
  53.6 1.0 collective-permute-done.10.refs_8_
  54.6 1.9 %collective-permute-done.11.refs_9_ = bf16[3,192,512]{2,1,0:T(8,128)(2,1)S(1)} collective-permute-done((bf16[3,192,512]{2,1,0:T(8,128)(2,1)}, bf16[3,192,512]{2,1,0:T(8,128)(2,1)S(1)}, u32[]{:S(2)}, u32[]{:S(2)}) %collective-permute-start.11) | collective-permute-done | bytes 589856 | tf_op jit(solution)/shard_map/ppermute | solution.py:262
  56.5 5.4 %collective-permute-done.8.refs_2_ = bf16[640,512]{1,0:T(8,128)(2,1)S(1)} collective-permute-done((bf16[640,512]{1,0:T(8,128)(2,1)S(1)}, bf16[640,512]{1,0:T(8,128)(2,1)S(1)}, u32[]{:S(2)}, u32[]{:S(2)}) %collective-permute-start.8) | collective-permute-done | bytes 655392 | tf_op jit(solution)/shard_map/ppermute | solution.py:258
  61.9 0.8 copy-done.4
  62.8 5.9 %shard_map.85 = (f32[160,1152]{1,0:T(8,128)}, bf16[160,1152]{1,0:T(8,128)(2,1)S(1)}, bf16[1152,2048]{1,0:T(8,128)(2,1)}) custom-call(s32[5]{0:T(128)S(1)} %stack.48.place, bf16[640,512]{1,0:T(8,128)(2,1)S(1)} %constant_dynamic-update-slice_fusion.refs_0_, bf16[640,512]{1,0:T(8,128)(2,1)} %copy-done.2, bf16[640,512]{1,0:T(8,128)(2,1)} %copy-done.4, ...), custom_call_target="tpu_custom_call" | custom-call | tf_op jit(solution)/shard_map/pallas_call | solution.py:31
  68.9 8.6 %collective-permute-done.14.far = bf16[160,1152]{1,0:T(8,128)(2,1)S(1)} collective-permute-done((bf16[160,1152]{1,0:T(8,128)(2,1)S(1)}, bf16[160,1152]{1,0:T(8,128)(2,1)S(1)}, u32[]{:S(2)}, u32[]{:S(2)}) %collective-permute-start.14) | collective-permute-done | bytes 368672 | tf_op jit(solution)/shard_map/ppermute | solution.py:262
  77.5 1.1 copy-done.6
  78.6 0.9 shard_map.86.near
  79.5 2.0 %collective-permute-start.15 = (bf16[176,1152]{1,0:T(8,128)(2,1)S(1)}, bf16[176,1152]{1,0:T(8,128)(2,1)S(1)}, u32[]{:S(2)}, u32[]{:S(2)}) collective-permute-start(bf16[176,1152]{1,0:T(8,128)(2,1)S(1)} %shard_map.86.near), channel_id=1, source_target_pairs={{0,1},{1,0},{2,3},{3,2},{4,5},{5,4},{6,7},{7,6},{8,9},{9,8},{10,11... | collective-permute-start | bytes 1216520 | tf_op jit(solution)/shard_map/ppermute | solution.py:262
  81.5 9.4 %collective-permute-done.15.far = bf16[176,1152]{1,0:T(8,128)(2,1)S(1)} collective-permute-done((bf16[176,1152]{1,0:T(8,128)(2,1)S(1)}, bf16[176,1152]{1,0:T(8,128)(2,1)S(1)}, u32[]{:S(2)}, u32[]{:S(2)}) %collective-permute-start.15) | collective-permute-done | bytes 405536 | tf_op jit(solution)/shard_map/ppermute | solution.py:262
  90.9 4.4 %shard_map.87 = (f32[656,512]{1,0:T(8,128)S(1)}, bf16[656,512]{1,0:T(8,128)(2,1)S(1)}, bf16[656,512]{1,0:T(8,128)(2,1)S(1)}, bf16[656,512]{1,0:T(8,128)(2,1)S(1)}) custom-call(s32[5]{0:T(128)S(1)} %stack.48.place, bf16[176,1152]{1,0:T(8,128)(2,1)S(1)} %shard_map.86.near, bf16[176,1152]{1,0:T(8,128)(2,1)S(1)} %collective-permute-done.15.far, ...), custom_call_target="tpu_custom_call" | custom-call | tf_op jit(solution)/shard_map/pallas_call | solution.py:31
  95.3 1.0 collective-permute-start.16
  96.3 5.4 %shard_map.88 = (f32[4,3,192,512]{3,2,1,0:T(8,128)}, bf16[4,192,512]{2,1,0:T(8,128)(2,1)S(1)}, bf16[4,192,512]{2,1,0:T(8,128)(2,1)S(1)}, bf16[4,192,512]{2,1,0:T(8,128)(2,1)S(1)}) custom-call(s32[5]{0:T(128)S(1)} %stack.48.place, bf16[176,1152]{1,0:T(8,128)(2,1)S(1)} %shard_map.86.near, bf16[176,1152]{1,0:T(8,128)(2,1)S(1)} %collective-permute-done.15.far, ...), custom_call_target="tpu_custom_call" | custom-call | tf_op jit(solution)/shard_map/pallas_call | solution.py:31
  102.3 3.0 %collective-permute-done.16 = bf16[656,512]{1,0:T(8,128)(2,1)S(1)} collective-permute-done((bf16[656,512]{1,0:T(8,128)(2,1)S(1)}, bf16[656,512]{1,0:T(8,128)(2,1)S(1)}, u32[]{:S(2)}, u32[]{:S(2)}) %collective-permute-start.16) | collective-permute-done | bytes 671776 | tf_op jit(solution)/shard_map/ppermute | solution.py:258
  106.2 2.6 %collective-permute-start.21 = (bf16[656,512]{1,0:T(8,128)(2,1)S(1)}, bf16[656,512]{1,0:T(8,128)(2,1)S(1)}, u32[]{:S(2)}, u32[]{:S(2)}) collective-permute-start(bf16[656,512]{1,0:T(8,128)(2,1)S(1)} %get-tuple-element.73), channel_id=1, source_target_pairs={{0,6},{2,0},{4,2},{6,4},{1,7},{3,1},{5,3},{7,5},{8,14},{10,8},{12,... | collective-permute-start | bytes 2015240 | tf_op jit(solution)/shard_map/ppermute | solution.py:251
  108.8 1.6 %bitcast_add_fusion.7 = (f32[1,192,512]{2,1,0:T(8,128)S(1)}, f32[1,192,512]{2,1,0:T(8,128)S(1)}, bf16[1,192,512]{2,1,0:T(8,128)(2,1)S(1)}, f32[1,192,512]{2,1,0:T(8,128)S(1)}) fusion(f32[4,3,192,512]{3,2,1,0:T(8,128)} %get-tuple-element.63, bf16[4,192,512]{2,1,0:T(8,128)(2,1)S(1)} %collective-permute-done.18), kind=kLoop, calls=%fused_computation.30 | loop fusion | flops 884736 | bytes 3735552 | tf_op jit(solution)/shard_map/add | solution.py:353
  110.4 0.6 bitcast_add_fusion.8
  111.2 2.6 %collective-permute-start.20 = (bf16[3,192,512]{2,1,0:T(8,128)(2,1)S(1)}, bf16[3,192,512]{2,1,0:T(8,128)(2,1)S(1)}, u32[]{:S(2)}, u32[]{:S(2)}) collective-permute-start(bf16[3,192,512]{2,1,0:T(8,128)(2,1)S(1)} %pad_maximum_fusion), channel_id=1, source_target_pairs={{0,64},{64,128},{128,192},{192,0},{32,224},{96,32},{160,96},{224,1... | collective-permute-start | bytes 1769480 | tf_op jit(solution)/shard_map/ppermute | solution.py:257
  113.7 6.8 %collective-permute-done.20 = bf16[3,192,512]{2,1,0:T(8,128)(2,1)S(1)} collective-permute-done((bf16[3,192,512]{2,1,0:T(8,128)(2,1)S(1)}, bf16[3,192,512]{2,1,0:T(8,128)(2,1)S(1)}, u32[]{:S(2)}, u32[]{:S(2)}) %collective-permute-start.20) | collective-permute-done | bytes 589856 | tf_op jit(solution)/shard_map/ppermute | solution.py:257
  120.5 2.4 %collective-permute-done.21.one = bf16[656,512]{1,0:T(8,128)(2,1)S(1)} collective-permute-done((bf16[656,512]{1,0:T(8,128)(2,1)S(1)}, bf16[656,512]{1,0:T(8,128)(2,1)S(1)}, u32[]{:S(2)}, u32[]{:S(2)}) %collective-permute-start.21) | collective-permute-done | bytes 671776 | tf_op jit(solution)/shard_map/ppermute | solution.py:251
  122.9 3.1 %collective-permute-done.22.three = bf16[656,512]{1,0:T(8,128)(2,1)S(1)} collective-permute-done((bf16[656,512]{1,0:T(8,128)(2,1)S(1)}, bf16[656,512]{1,0:T(8,128)(2,1)S(1)}, u32[]{:S(2)}, u32[]{:S(2)}) %collective-permute-start.22) | collective-permute-done | bytes 671776 | tf_op jit(solution)/shard_map/ppermute | solution.py:251
  126.4 2.6 %collective-permute-start.23 = (bf16[3,192,512]{2,1,0:T(8,128)(2,1)S(1)}, bf16[3,192,512]{2,1,0:T(8,128)(2,1)S(1)}, u32[]{:S(2)}, u32[]{:S(2)}) collective-permute-start(bf16[3,192,512]{2,1,0:T(8,128)(2,1)S(1)} %get-tuple-element.110), channel_id=1, source_target_pairs={{0,192},{64,0},{128,64},{192,128},{1,193},{65,1},{129,65},{193,129... | collective-permute-start | bytes 1769480 | tf_op jit(solution)/shard_map/ppermute | solution.py:251
  129.0 0.8 shard_map.89
  129.9 4.4 %collective-permute-start.28 = (bf16[176,512]{1,0:T(8,128)(2,1)S(1)}, bf16[176,512]{1,0:T(8,128)(2,1)S(1)}, u32[]{:S(2)}, u32[]{:S(2)}) collective-permute-start(bf16[176,512]{1,0:T(8,128)(2,1)S(1)} %get-tuple-element.82), channel_id=1, source_target_pairs={{0,16},{8,24},{16,0},{24,8},{1,17},{9,25},{17,1},{25,9},{2,18},{10... | collective-permute-start | bytes 540680 | tf_op jit(solution)/shard_map/ppermute | solution.py:251
  134.2 5.8 %collective-permute-done.23 = bf16[3,192,512]{2,1,0:T(8,128)(2,1)S(1)} collective-permute-done((bf16[3,192,512]{2,1,0:T(8,128)(2,1)S(1)}, bf16[3,192,512]{2,1,0:T(8,128)(2,1)S(1)}, u32[]{:S(2)}, u32[]{:S(2)}) %collective-permute-start.23) | collective-permute-done | bytes 589856 | tf_op jit(solution)/shard_map/ppermute | solution.py:251
  140.1 3.1 %collective-permute-done.24 = bf16[3,192,512]{2,1,0:T(8,128)(2,1)S(1)} collective-permute-done((bf16[3,192,512]{2,1,0:T(8,128)(2,1)S(1)}, bf16[3,192,512]{2,1,0:T(8,128)(2,1)S(1)}, u32[]{:S(2)}, u32[]{:S(2)}) %collective-permute-start.24) | collective-permute-done | bytes 589856 | tf_op jit(solution)/shard_map/ppermute | solution.py:251
  143.5 6.0 %collective-permute-start.26 = (bf16[288,512]{1,0:T(8,128)(2,1)S(1)}, bf16[288,512]{1,0:T(8,128)(2,1)S(1)}, u32[]{:S(2)}, u32[]{:S(2)}) collective-permute-start(bf16[288,512]{1,0:T(8,128)(2,1)S(1)} %get-tuple-element.108), channel_id=1, source_target_pairs={{0,0},{1,32},{32,1},{33,33},{2,2},{3,34},{34,3},{35,35},{4,4},{5,3... | collective-permute-start | bytes 884744 | tf_op jit(solution)/shard_map/ppermute | solution.py:266
  149.5 1.9 %collective-permute-start.25 = (bf16[288,512]{1,0:T(8,128)(2,1)S(1)}, bf16[288,512]{1,0:T(8,128)(2,1)S(1)}, u32[]{:S(2)}, u32[]{:S(2)}) collective-permute-start(bf16[288,512]{1,0:T(8,128)(2,1)S(1)} %get-tuple-element.109), channel_id=1, source_target_pairs={{0,0},{1,32},{32,1},{33,33},{2,2},{3,34},{34,3},{35,35},{4,4},{5,3... | collective-permute-start | bytes 884744 | tf_op jit(solution)/shard_map/ppermute | solution.py:266
  151.5 1.7 %shard_map.90 = (bf16[128,512]{1,0:T(8,128)(2,1)}, bf16[128,512]{1,0:T(8,128)(2,1)}, f32[8,128]{1,0:T(8,128)S(1)}) custom-call(s32[5]{0:T(128)S(1)} %stack.48.place, f32[4,128]{1,0:T(4,128)S(1)} %pad_maximum_fusion.3.small, bf16[320,128]{1,0:T(8,128)(2,1)S(1)} %get-tuple-element.76.placing, bf16[176,512]{1,0:T(8,128)(2,1)S(1)} %get-tuple-element.80.refs_0_, ...), custom_call_target="tpu_custom_call" | custom-call | tf_op jit(solution)/shard_map/pallas_call | solution.py:31
  154.2 3.4 %collective-permute-done.25 = bf16[288,512]{1,0:T(8,128)(2,1)S(1)} collective-permute-done((bf16[288,512]{1,0:T(8,128)(2,1)S(1)}, bf16[288,512]{1,0:T(8,128)(2,1)S(1)}, u32[]{:S(2)}, u32[]{:S(2)}) %collective-permute-start.25) | collective-permute-done | bytes 294944 | tf_op jit(solution)/shard_map/ppermute | solution.py:266
  157.6 1.2 convert.14
  (58 shorter events, 5.3 us)
Async XLA Ops:
  0.6 24.4 %copy-start.8 = (bf16[1,3,192,512]{3,2,1,0:T(8,128)(2,1)S(1)}, bf16[1,3,192,512]{3,2,1,0:T(8,128)(2,1)}, u32[]{:S(2)}) copy-start(bf16[1,3,192,512]{3,2,1,0:T(8,128)(2,1)} %param.8) | copy-start | bytes 1769476
  4.2 20.8 %collective-permute-start.3 = (bf16[3,192,512]{2,1,0:T(8,128)(2,1)}, bf16[3,192,512]{2,1,0:T(8,128)(2,1)S(1)}, u32[]{:S(2)}, u32[]{:S(2)}) collective-permute-start(bf16[3,192,512]{2,1,0:T(8,128)(2,1)} %bitcast.50), channel_id=1, source_target_pairs={{1,32},{32,1},{3,34},{34,3},{5,36},{36,5},{7,38},{38,7},{9,40},{40... | collective-permute-start | bytes 1769480 | tf_op jit(solution)/shard_map/ppermute | solution.py:292
  9.1 21.5 %collective-permute-start = (bf16[160,512]{1,0:T(8,128)(2,1)S(1)}, bf16[160,512]{1,0:T(8,128)(2,1)}, u32[]{:S(2)}, u32[]{:S(2)}) collective-permute-start(bf16[160,512]{1,0:T(8,128)(2,1)S(1)} %get-tuple-element.49), channel_id=1, source_target_pairs={{0,8},{8,16},{16,24},{24,0},{1,9},{9,17},{17,25},{25,1},{2,10},{10... | collective-permute-start | bytes 491528 | tf_op jit(solution)/shard_map/ppermute | solution.py:251
  12.2 24.1 %collective-permute-start.1 = (bf16[160,512]{1,0:T(8,128)(2,1)S(1)}, bf16[160,512]{1,0:T(8,128)(2,1)S(1)}, u32[]{:S(2)}, u32[]{:S(2)}) collective-permute-start(bf16[160,512]{1,0:T(8,128)(2,1)S(1)} %get-tuple-element.50), channel_id=1, source_target_pairs={{0,16},{8,24},{16,0},{24,8},{1,17},{9,25},{17,1},{25,9},{2,18},{10... | collective-permute-start | bytes 491528 | tf_op jit(solution)/shard_map/ppermute | solution.py:251
  16.4 20.0 %collective-permute-start.2 = (bf16[160,512]{1,0:T(8,128)(2,1)S(1)}, bf16[160,512]{1,0:T(8,128)(2,1)S(1)}, u32[]{:S(2)}, u32[]{:S(2)}) collective-permute-start(bf16[160,512]{1,0:T(8,128)(2,1)S(1)} %get-tuple-element.51), channel_id=1, source_target_pairs={{0,24},{8,0},{16,8},{24,16},{1,25},{9,1},{17,9},{25,17},{2,26},{10... | collective-permute-start | bytes 491528 | tf_op jit(solution)/shard_map/ppermute | solution.py:251
  25.1 14.1 %collective-permute-start.5 = (bf16[3,192,512]{2,1,0:T(8,128)(2,1)S(1)}, bf16[3,192,512]{2,1,0:T(8,128)(2,1)S(1)}, u32[]{:S(2)}, u32[]{:S(2)}) collective-permute-start(bf16[3,192,512]{2,1,0:T(8,128)(2,1)S(1)} %broadcast_select_fusion.2.refs_4_), channel_id=1, source_target_pairs={{0,192},{64,0},{128,64},{192,128},{1,193},{65,1},{129,65},{193,129... | collective-permute-start | bytes 1769480 | tf_op jit(solution)/shard_map/ppermute | solution.py:251
  27.6 11.6 %collective-permute-start.4 = (bf16[3,192,512]{2,1,0:T(8,128)(2,1)S(1)}, bf16[3,192,512]{2,1,0:T(8,128)(2,1)}, u32[]{:S(2)}, u32[]{:S(2)}) collective-permute-start(bf16[3,192,512]{2,1,0:T(8,128)(2,1)S(1)} %broadcast_select_fusion.2.refs_4_), channel_id=1, source_target_pairs={{0,64},{64,128},{128,192},{192,0},{1,65},{65,129},{129,193},{193,1... | collective-permute-start | bytes 1769480 | tf_op jit(solution)/shard_map/ppermute | solution.py:251
  36.4 10.3 %collective-permute-start.7 = (bf16[640,512]{1,0:T(8,128)(2,1)S(1)}, bf16[640,512]{1,0:T(8,128)(2,1)S(1)}, u32[]{:S(2)}, u32[]{:S(2)}) collective-permute-start(bf16[640,512]{1,0:T(8,128)(2,1)S(1)} %constant_dynamic-update-slice_fusion.refs_0_), channel_id=1, source_target_pairs={{0,6},{2,0},{4,2},{6,4},{1,7},{3,1},{5,3},{7,5},{8,14},{10,8},{12,... | collective-permute-start | bytes 1966088 | tf_op jit(solution)/shard_map/ppermute | solution.py:251
  39.2 13.1 %collective-permute-start.6 = (bf16[640,512]{1,0:T(8,128)(2,1)S(1)}, bf16[640,512]{1,0:T(8,128)(2,1)S(1)}, u32[]{:S(2)}, u32[]{:S(2)}) collective-permute-start(bf16[640,512]{1,0:T(8,128)(2,1)S(1)} %constant_dynamic-update-slice_fusion.refs_0_), channel_id=1, source_target_pairs={{0,2},{2,4},{4,6},{6,0},{1,3},{3,5},{5,7},{7,1},{8,10},{10,12},{12... | collective-permute-start | bytes 1966088 | tf_op jit(solution)/shard_map/ppermute | solution.py:251
  39.3 13.9 %collective-permute-start.9 = (bf16[3,192,512]{2,1,0:T(8,128)(2,1)S(1)}, bf16[3,192,512]{2,1,0:T(8,128)(2,1)S(1)}, u32[]{:S(2)}, u32[]{:S(2)}) collective-permute-start(bf16[3,192,512]{2,1,0:T(8,128)(2,1)S(1)} %broadcast_select_fusion.1), channel_id=1, source_target_pairs={{0,64},{64,128},{128,192},{192,0},{32,224},{96,32},{160,96},{224,1... | collective-permute-start | bytes 1769480 | tf_op jit(solution)/shard_map/ppermute | solution.py:257
  46.7 15.2 %copy-start = (bf16[640,512]{1,0:T(8,128)(2,1)}, bf16[640,512]{1,0:T(8,128)(2,1)S(1)}, u32[]{:S(2)}) copy-start(bf16[640,512]{1,0:T(8,128)(2,1)S(1)} %collective-permute-done.7.refs_3_) | copy-start | bytes 1966084
  52.3 9.6 %copy-start.2 = (bf16[640,512]{1,0:T(8,128)(2,1)}, bf16[640,512]{1,0:T(8,128)(2,1)S(1)}, u32[]{:S(2)}) copy-start(bf16[640,512]{1,0:T(8,128)(2,1)S(1)} %collective-permute-done.6.refs_1_) | copy-start | bytes 1966084
  52.4 9.5 %collective-permute-start.8 = (bf16[640,512]{1,0:T(8,128)(2,1)S(1)}, bf16[640,512]{1,0:T(8,128)(2,1)S(1)}, u32[]{:S(2)}, u32[]{:S(2)}) collective-permute-start(bf16[640,512]{1,0:T(8,128)(2,1)S(1)} %broadcast_select_fusion), channel_id=1, source_target_pairs={{0,2},{2,4},{4,6},{6,0},{32,38},{34,32},{36,34},{38,36},{1,3},{3,5... | collective-permute-start | bytes 1966088 | tf_op jit(solution)/shard_map/ppermute | solution.py:258
  52.5 2.1 %collective-permute-start.10 = (bf16[3,192,512]{2,1,0:T(8,128)(2,1)S(1)}, bf16[3,192,512]{2,1,0:T(8,128)(2,1)S(1)}, u32[]{:S(2)}, u32[]{:S(2)}) collective-permute-start(bf16[3,192,512]{2,1,0:T(8,128)(2,1)S(1)} %broadcast_select_fusion.2.refs_4_), channel_id=1, source_target_pairs={{0,32},{32,0},{1,33},{33,1},{2,34},{34,2},{3,35},{35,3},{4,36},{36... | collective-permute-start | bytes 1769480 | tf_op jit(solution)/shard_map/ppermute | solution.py:262
  52.6 3.9 %collective-permute-start.11 = (bf16[3,192,512]{2,1,0:T(8,128)(2,1)}, bf16[3,192,512]{2,1,0:T(8,128)(2,1)S(1)}, u32[]{:S(2)}, u32[]{:S(2)}) collective-permute-start(bf16[3,192,512]{2,1,0:T(8,128)(2,1)} %collective-permute-done.4.refs_5_), channel_id=1, source_target_pairs={{0,32},{32,0},{1,33},{33,1},{2,34},{34,2},{3,35},{35,3},{4,36},{36... | collective-permute-start | bytes 1769480 | tf_op jit(solution)/shard_map/ppermute | solution.py:262
  53.1 3.4 %collective-permute-start.13 = (bf16[3,192,512]{2,1,0:T(8,128)(2,1)S(1)}, bf16[3,192,512]{2,1,0:T(8,128)(2,1)S(1)}, u32[]{:S(2)}, u32[]{:S(2)}) collective-permute-start(bf16[3,192,512]{2,1,0:T(8,128)(2,1)S(1)} %collective-permute-done.5.refs_7_), channel_id=1, source_target_pairs={{0,32},{32,0},{1,33},{33,1},{2,34},{34,2},{3,35},{35,3},{4,36},{36... | collective-permute-start | bytes 1769480 | tf_op jit(solution)/shard_map/ppermute | solution.py:262
  53.2 8.7 %collective-permute-start.12 = (bf16[3,192,512]{2,1,0:T(8,128)(2,1)S(1)}, bf16[3,192,512]{2,1,0:T(8,128)(2,1)S(1)}, u32[]{:S(2)}, u32[]{:S(2)}) collective-permute-start(bf16[3,192,512]{2,1,0:T(8,128)(2,1)S(1)} %collective-permute-done.9.refs_6_), channel_id=1, source_target_pairs={{0,32},{32,0},{1,33},{33,1},{2,34},{34,2},{3,35},{35,3},{4,36},{36... | collective-permute-start | bytes 1769480 | tf_op jit(solution)/shard_map/ppermute | solution.py:262
  61.9 0.8 copy-start.4
  68.6 8.9 %collective-permute-start.14 = (bf16[160,1152]{1,0:T(8,128)(2,1)S(1)}, bf16[160,1152]{1,0:T(8,128)(2,1)S(1)}, u32[]{:S(2)}, u32[]{:S(2)}) collective-permute-start(bf16[160,1152]{1,0:T(8,128)(2,1)S(1)} %get-tuple-element.59), channel_id=1, source_target_pairs={{0,1},{1,0},{2,3},{3,2},{4,5},{5,4},{6,7},{7,6},{8,9},{9,8},{10,11... | collective-permute-start | bytes 1105928 | tf_op jit(solution)/shard_map/ppermute | solution.py:262
  77.5 1.1 copy-start.6
  79.5 11.4 %collective-permute-start.15 = (bf16[176,1152]{1,0:T(8,128)(2,1)S(1)}, bf16[176,1152]{1,0:T(8,128)(2,1)S(1)}, u32[]{:S(2)}, u32[]{:S(2)}) collective-permute-start(bf16[176,1152]{1,0:T(8,128)(2,1)S(1)} %shard_map.86.near), channel_id=1, source_target_pairs={{0,1},{1,0},{2,3},{3,2},{4,5},{5,4},{6,7},{7,6},{8,9},{9,8},{10,11... | collective-permute-start | bytes 1216520 | tf_op jit(solution)/shard_map/ppermute | solution.py:262
  90.9 5.4 %copy-start.1 = (bf16[640,512]{1,0:T(8,128)(2,1)S(1)}, bf16[640,512]{1,0:T(8,128)(2,1)}, u32[]{:S(2)}) copy-start(bf16[640,512]{1,0:T(8,128)(2,1)} %copy-done) | copy-start | bytes 1966084
  90.9 5.4 %copy-start.3 = (bf16[640,512]{1,0:T(8,128)(2,1)S(1)}, bf16[640,512]{1,0:T(8,128)(2,1)}, u32[]{:S(2)}) copy-start(bf16[640,512]{1,0:T(8,128)(2,1)} %copy-done.2) | copy-start | bytes 1966084
  90.9 5.4 %copy-start.5 = (bf16[640,512]{1,0:T(8,128)(2,1)S(1)}, bf16[640,512]{1,0:T(8,128)(2,1)}, u32[]{:S(2)}) copy-start(bf16[640,512]{1,0:T(8,128)(2,1)} %copy-done.4) | copy-start | bytes 1966084
  95.3 10.0 %collective-permute-start.16 = (bf16[656,512]{1,0:T(8,128)(2,1)S(1)}, bf16[656,512]{1,0:T(8,128)(2,1)S(1)}, u32[]{:S(2)}, u32[]{:S(2)}) collective-permute-start(bf16[656,512]{1,0:T(8,128)(2,1)S(1)} %get-tuple-element.65), channel_id=1, source_target_pairs={{0,2},{2,4},{4,6},{6,0},{32,38},{34,32},{36,34},{38,36},{1,3},{3,5... | collective-permute-start | bytes 2015240 | tf_op jit(solution)/shard_map/ppermute | solution.py:258
  101.7 3.9 %collective-permute-start.17 = (bf16[4,192,512]{2,1,0:T(8,128)(2,1)S(1)}, bf16[4,192,512]{2,1,0:T(8,128)(2,1)S(1)}, u32[]{:S(2)}, u32[]{:S(2)}) collective-permute-start(bf16[4,192,512]{2,1,0:T(8,128)(2,1)S(1)} %get-tuple-element.67), channel_id=1, source_target_pairs={{0,32},{32,0},{1,33},{33,1},{2,34},{34,2},{3,35},{35,3},{4,36},{36... | collective-permute-start | bytes 2359304 | tf_op jit(solution)/shard_map/ppermute | solution.py:262
  101.8 3.9 %collective-permute-start.18 = (bf16[4,192,512]{2,1,0:T(8,128)(2,1)S(1)}, bf16[4,192,512]{2,1,0:T(8,128)(2,1)S(1)}, u32[]{:S(2)}, u32[]{:S(2)}) collective-permute-start(bf16[4,192,512]{2,1,0:T(8,128)(2,1)S(1)} %get-tuple-element.68), channel_id=1, source_target_pairs={{0,32},{32,0},{1,33},{33,1},{2,34},{34,2},{3,35},{35,3},{4,36},{36... | collective-permute-start | bytes 2359304 | tf_op jit(solution)/shard_map/ppermute | solution.py:262
  102.2 4.0 %collective-permute-start.19 = (bf16[4,192,512]{2,1,0:T(8,128)(2,1)S(1)}, bf16[4,192,512]{2,1,0:T(8,128)(2,1)S(1)}, u32[]{:S(2)}, u32[]{:S(2)}) collective-permute-start(bf16[4,192,512]{2,1,0:T(8,128)(2,1)S(1)} %get-tuple-element.69), channel_id=1, source_target_pairs={{0,32},{32,0},{1,33},{33,1},{2,34},{34,2},{3,35},{35,3},{4,36},{36... | collective-permute-start | bytes 2359304 | tf_op jit(solution)/shard_map/ppermute | solution.py:262
  105.3 5.2 %copy-start.7 = (f32[4,3,192,512]{3,2,1,0:T(8,128)S(1)}, f32[4,3,192,512]{3,2,1,0:T(8,128)}, u32[]{:S(2)}) copy-start(f32[4,3,192,512]{3,2,1,0:T(8,128)} %get-tuple-element.63) | copy-start | bytes 14155780
  106.2 16.7 %collective-permute-start.21 = (bf16[656,512]{1,0:T(8,128)(2,1)S(1)}, bf16[656,512]{1,0:T(8,128)(2,1)S(1)}, u32[]{:S(2)}, u32[]{:S(2)}) collective-permute-start(bf16[656,512]{1,0:T(8,128)(2,1)S(1)} %get-tuple-element.73), channel_id=1, source_target_pairs={{0,6},{2,0},{4,2},{6,4},{1,7},{3,1},{5,3},{7,5},{8,14},{10,8},{12,... | collective-permute-start | bytes 2015240 | tf_op jit(solution)/shard_map/ppermute | solution.py:251
  108.8 17.2 %collective-permute-start.22 = (bf16[656,512]{1,0:T(8,128)(2,1)S(1)}, bf16[656,512]{1,0:T(8,128)(2,1)S(1)}, u32[]{:S(2)}, u32[]{:S(2)}) collective-permute-start(bf16[656,512]{1,0:T(8,128)(2,1)S(1)} %get-tuple-element.74), channel_id=1, source_target_pairs={{0,2},{2,4},{4,6},{6,0},{1,3},{3,5},{5,7},{7,1},{8,10},{10,12},{12... | collective-permute-start | bytes 2015240 | tf_op jit(solution)/shard_map/ppermute | solution.py:251
  111.2 9.4 %collective-permute-start.20 = (bf16[3,192,512]{2,1,0:T(8,128)(2,1)S(1)}, bf16[3,192,512]{2,1,0:T(8,128)(2,1)S(1)}, u32[]{:S(2)}, u32[]{:S(2)}) collective-permute-start(bf16[3,192,512]{2,1,0:T(8,128)(2,1)S(1)} %pad_maximum_fusion), channel_id=1, source_target_pairs={{0,64},{64,128},{128,192},{192,0},{32,224},{96,32},{160,96},{224,1... | collective-permute-start | bytes 1769480 | tf_op jit(solution)/shard_map/ppermute | solution.py:257
  126.4 13.7 %collective-permute-start.23 = (bf16[3,192,512]{2,1,0:T(8,128)(2,1)S(1)}, bf16[3,192,512]{2,1,0:T(8,128)(2,1)S(1)}, u32[]{:S(2)}, u32[]{:S(2)}) collective-permute-start(bf16[3,192,512]{2,1,0:T(8,128)(2,1)S(1)} %get-tuple-element.110), channel_id=1, source_target_pairs={{0,192},{64,0},{128,64},{192,128},{1,193},{65,1},{129,65},{193,129... | collective-permute-start | bytes 1769480 | tf_op jit(solution)/shard_map/ppermute | solution.py:251
  129.0 14.2 %collective-permute-start.24 = (bf16[3,192,512]{2,1,0:T(8,128)(2,1)S(1)}, bf16[3,192,512]{2,1,0:T(8,128)(2,1)S(1)}, u32[]{:S(2)}, u32[]{:S(2)}) collective-permute-start(bf16[3,192,512]{2,1,0:T(8,128)(2,1)S(1)} %get-tuple-element.111), channel_id=1, source_target_pairs={{0,64},{64,128},{128,192},{192,0},{1,65},{65,129},{129,193},{193,1... | collective-permute-start | bytes 1769480 | tf_op jit(solution)/shard_map/ppermute | solution.py:251
  129.8 21.7 %collective-permute-start.27 = (bf16[176,512]{1,0:T(8,128)(2,1)S(1)}, bf16[176,512]{1,0:T(8,128)(2,1)S(1)}, u32[]{:S(2)}, u32[]{:S(2)}) collective-permute-start(bf16[176,512]{1,0:T(8,128)(2,1)S(1)} %get-tuple-element.81), channel_id=1, source_target_pairs={{0,24},{8,0},{16,8},{24,16},{1,25},{9,1},{17,9},{25,17},{2,26},{10... | collective-permute-start | bytes 540680 | tf_op jit(solution)/shard_map/ppermute | solution.py:251
  129.9 21.6 %collective-permute-start.28 = (bf16[176,512]{1,0:T(8,128)(2,1)S(1)}, bf16[176,512]{1,0:T(8,128)(2,1)S(1)}, u32[]{:S(2)}, u32[]{:S(2)}) collective-permute-start(bf16[176,512]{1,0:T(8,128)(2,1)S(1)} %get-tuple-element.82), channel_id=1, source_target_pairs={{0,16},{8,24},{16,0},{24,8},{1,17},{9,25},{17,1},{25,9},{2,18},{10... | collective-permute-start | bytes 540680 | tf_op jit(solution)/shard_map/ppermute | solution.py:251
  134.2 17.2 %collective-permute-start.29 = (bf16[176,512]{1,0:T(8,128)(2,1)S(1)}, bf16[176,512]{1,0:T(8,128)(2,1)S(1)}, u32[]{:S(2)}, u32[]{:S(2)}) collective-permute-start(bf16[176,512]{1,0:T(8,128)(2,1)S(1)} %get-tuple-element.83), channel_id=1, source_target_pairs={{0,8},{8,16},{16,24},{24,0},{1,9},{9,17},{17,25},{25,1},{2,10},{10... | collective-permute-start | bytes 540680 | tf_op jit(solution)/shard_map/ppermute | solution.py:251
  143.5 10.7 %collective-permute-start.26 = (bf16[288,512]{1,0:T(8,128)(2,1)S(1)}, bf16[288,512]{1,0:T(8,128)(2,1)S(1)}, u32[]{:S(2)}, u32[]{:S(2)}) collective-permute-start(bf16[288,512]{1,0:T(8,128)(2,1)S(1)} %get-tuple-element.108), channel_id=1, source_target_pairs={{0,0},{1,32},{32,1},{33,33},{2,2},{3,34},{34,3},{35,35},{4,4},{5,3... | collective-permute-start | bytes 884744 | tf_op jit(solution)/shard_map/ppermute | solution.py:266
  149.5 8.0 %collective-permute-start.25 = (bf16[288,512]{1,0:T(8,128)(2,1)S(1)}, bf16[288,512]{1,0:T(8,128)(2,1)S(1)}, u32[]{:S(2)}, u32[]{:S(2)}) collective-permute-start(bf16[288,512]{1,0:T(8,128)(2,1)S(1)} %get-tuple-element.109), channel_id=1, source_target_pairs={{0,0},{1,32},{32,1},{33,33},{2,2},{3,34},{34,3},{35,35},{4,4},{5,3... | collective-permute-start | bytes 884744 | tf_op jit(solution)/shard_map/ppermute | solution.py:266

commit v7 on v6

--- a/solution.py
+++ b/solution.py
@@ -1,3 +1,5 @@
+import functools
+
 import functools
 
 import jax
@@ -71,19 +73,19 @@
         outs[k][CAP : 2 * CAP, :] = (scales[k] * nn(hot, wide[:, width:])).astype(BF16)
 
 
-def fetch(own, other, joined, sems, place):
+def fetch(own, other, joined, sems, names, place):
     half, width = own[0].shape[1:]
     copies = []
     for block in range(4):
         spot = lax.rem(place[2] - place[1] + block + 4, 4)
         columns = pl.ds(pl.multiple_of(spot * width, width), width)
-        for m in range(3):
+        for n, m in enumerate(names):
             for h, source in enumerate((own[block], other[block])):
                 copies.append(
                     pltpu.make_async_copy(
                         source.at[m],
-                        joined.at[pl.ds((2 * m + h) * half, half), columns],
-                        sems.at[block, m, h],
+                        joined.at[pl.ds((2 * n + h) * half, half), columns],
+                        sems.at[block, n, h],
                     )
                 )
     for copy in copies:
@@ -97,22 +99,16 @@
         target[k * CAP : (k + 1) * CAP, :] = source[first : first + CAP, :]
 
 
-def project_kernel(place, *refs):
+def project_kernel(names, second, place, *refs):
     rows, own, other = refs[0:4], refs[4:8], refs[8:12]
-    keep, send, joined, wide, total, sems = refs[12:18]
+    out, joined, wide, sems = refs[12:16]
     width = rows[0].shape[1]
-    hidden = keep.shape[1] // 3
-    copies = fetch(own, other, joined, sems, place)
-    for second in range(2):
-        for j in range(4):
-            take_rows(wide.at[second, :, pl.ds(j * width, width)], rows[j], second)
+    copies = fetch(own, other, joined, sems, names, place)
+    for j in range(4):
+        take_rows(wide.at[:, pl.ds(j * width, width)], rows[j], second)
     for copy in copies:
         copy.wait()
-    total[:, 0 : 2 * hidden] = nt(wide[0], joined[0 : 2 * hidden, :])
-    total[:, 2 * hidden :] = nt(wide[1], joined[2 * hidden :, :])
-    part = keep.shape[0]
-    keep[...] = total[pl.ds(pl.multiple_of(place[3] * part, 32), part), :]
-    send[...] = total[pl.ds(pl.multiple_of((1 - place[3]) * part, 32), part), :].astype(BF16)
+    out[...] = nt(wide[...], joined[...]).astype(BF16)
 
 
 def pieces(values):
@@ -131,58 +127,41 @@
     return total
 
 
-def hidden_kernel(place, keep, far, out):
-    part, width = keep.shape[0], keep.shape[1] // 3
-    gate, up, grad = [
-        keep[:, n * width : (n + 1) * width] + far[:, n * width : (n + 1) * width].astype(F32)
-        for n in range(3)
-    ]
+def share_kernel(place, pair, pair_far, down, down_far, pair_weights, down_weights, *refs):
+    outs, hidden = refs[0:4], refs[4]
+    width, step = down.shape[1], outs[0].shape[1]
+
+    def both(near, far, n):
+        columns = slice(n * width, (n + 1) * width)
+        return near[:, columns].astype(F32) + far[:, columns].astype(F32)
+
+    gate, up, grad = both(pair, pair_far, 0), both(pair, pair_far, 1), both(down, down_far, 0)
     sigmoid = 1.0 / (1.0 + jnp.exp(-gate))
     swish = gate * sigmoid
     act = (swish * up).astype(BF16)
-    out[0:part, 0:width] = (
-        grad * up * sigmoid * (1.0 + gate * (1.0 - sigmoid))
-    ).astype(BF16)
-    out[0:part, width : 2 * width] = (grad * swish).astype(BF16)
-    out[0:part, 2 * width :] = act
+    hidden[:, 2 * width :] = act
+    hidden[:, 0:width] = (grad * up * sigmoid * (1.0 + gate * (1.0 - sigmoid))).astype(BF16)
+    hidden[:, width : 2 * width] = (grad * swish).astype(BF16)
     share = jnp.sum(act.astype(F32) * grad, axis=1, keepdims=True)
-    out[part:, :] = jnp.zeros((TILE, out.shape[1]), BF16)
-    marks = jnp.zeros((TILE, 128), F32)
     shape = (CAP, 128)
     same = lax.broadcasted_iota(jnp.int32, shape, 0) == lax.broadcasted_iota(jnp.int32, shape, 1)
-    for n in range(2):
+    marks = jnp.zeros((TILE, 128), F32)
+    for k in range(4):
         row = jnp.sum(
-            jnp.where(same, share[n * CAP : (n + 1) * CAP, :], 0.0), axis=0, keepdims=True
+            jnp.where(same, share[k * CAP : (k + 1) * CAP, :], 0.0), axis=0, keepdims=True
         )
-        marks += marked_rows(row, 6 * place[3] + 3 * n)
-    out[part:, 0:128] = marks.astype(BF16)
-
-
-def join(target, mine, theirs, zl):
-    part = target.shape[0] // 2
-    target[pl.ds(pl.multiple_of(zl * part, 32), part), :] = mine[0:part, :]
-    target[pl.ds(pl.multiple_of((1 - zl) * part, 32), part), :] = theirs[0:part, :]
-
-
-def share_kernel(place, near, far, weights, *refs):
-    outs, joined = refs[0:4], refs[4]
-    part, width = joined.shape[0] // 2, outs[0].shape[1]
-    hidden = near.shape[1] // 3
-    join(joined, near, far, place[3])
-    marks = near[part:, 0:128].astype(F32) + far[part:, 0:128].astype(F32)
+        marks += marked_rows(row, 3 * k)
     unit = 2 * CAP
-    for j in (1, 3, 2, 0):
+    for j in (2, 1, 3, 0):
         kind = outs[j].dtype
-        columns = slice(j * width, (j + 1) * width)
-        out = nn(joined[:, 2 * hidden :], weights[2 * hidden :, columns])
-        back = nn(joined[:, 0 : 2 * hidden], weights[0 : 2 * hidden, columns])
+        columns = slice(j * step, (j + 1) * step)
+        out = nn(hidden[:, 2 * width :], down_weights[:, columns])
+        back = nn(hidden[:, 0 : 2 * width], pair_weights[:, columns])
         for k in range(4):
             start, rows = k * unit, slice(k * CAP, (k + 1) * CAP)
             outs[j][start : start + CAP, :] = out[rows, :].astype(kind)
             outs[j][start + CAP : start + 2 * CAP, :] = back[rows, :].astype(kind)
-    for j in range(4):
-        kind = outs[j].dtype
-        outs[j][4 * unit :, :] = jnp.zeros((TILE, width), kind)
+        outs[j][4 * unit :, :] = jnp.zeros((TILE, step), kind)
         outs[j][4 * unit :, 0:128] = marks.astype(kind)
 
 
@@ -202,11 +181,9 @@
         outs[k][unit:, 0:128] = marked_rows(row, 0).astype(BF16)
 
 
-def weight_kernel(place, near, far, *refs):
-    rows, keep, sends = refs[0:4], refs[4], refs[5:8]
-    joined, chosen = refs[8:10]
+def weight_kernel(place, joined, *refs):
+    rows, keep, sends, chosen = refs[0:4], refs[4], refs[5:8], refs[8]
     half = keep.shape[2]
-    join(joined, near, far, place[3])
     for j in range(4):
         block = lax.rem(place[1] - place[2] + j + 4, 4)
         for m, second in ((2, 1), (0, 0), (1, 0)):
@@ -271,7 +248,6 @@
     half = stacked_weights.shape[2]
     hidden = 2 * half
     slots = 4 * CAP
-    part = slots // 2
     place = jnp.stack(
         [lax.axis_index(name) for name in ("expert", "x", "y", "zl", "core")]
     ).astype(jnp.int32)
@@ -302,25 +278,21 @@
     other = [swap(block, "core") for block in own]
     blocks += [near, relay(jnp.where(first, near, back), "y"), back]
 
-    keep, send, weights = call(
-        project_kernel,
-        place,
-        blocks + own + other,
-        [((part, 3 * hidden), F32), ((part, 3 * hidden), BF16), ((3 * hidden, 4 * width), BF16)],
-        [
-            pltpu.VMEM((2, slots, 4 * width), BF16),
-            pltpu.VMEM((slots, 3 * hidden), F32),
-            pltpu.SemaphoreType.DMA((4, 3, 2)),
-        ],
-        [vmem] * 4 + [hbm] * 8,
-    )
-    hidden_near = call(
-        hidden_kernel,
-        place,
-        [keep, swap(send, "zl")],
-        [((part + TILE, 3 * hidden), BF16)],
-    )[0]
-    hidden_far = swap(hidden_near, "zl")
+    def project(names, second):
+        tall = len(names) * hidden
+        return call(
+            functools.partial(project_kernel, names, second),
+            place,
+            blocks + own + other,
+            [((slots, tall), BF16), ((tall, 4 * width), BF16)],
+            [pltpu.VMEM((slots, 4 * width), BF16), pltpu.SemaphoreType.DMA((4, 2, 2))],
+            [vmem] * 4 + [hbm] * 8,
+        )
+
+    pair, pair_weights = project((0, 1), 0)
+    pair_far = swap(pair, "zl")
+    down, down_weights = project((2,), 1)
+    down_far = swap(down, "zl")
 
     def halfway(passed, near, back):
         passed = passed.astype(F32)
@@ -331,18 +303,18 @@
     shares = call(
         share_kernel,
         place,
-        [hidden_near, hidden_far, weights],
-        [((8 * CAP + TILE, width), F32)] + [((8 * CAP + TILE, width), BF16)] * 3,
-        [pltpu.VMEM((slots, 3 * hidden), BF16)],
+        [pair, pair_far, down, down_far, pair_weights, down_weights],
+        [((8 * CAP + TILE, width), F32)]
+        + [((8 * CAP + TILE, width), BF16)] * 3
+        + [((slots, 3 * hidden), BF16)],
     )
     passed = relay(shares[2], "y")
-    shares[0], hidden_near = lax.optimization_barrier((shares[0], hidden_near))
     keep, *sends = call(
         weight_kernel,
         place,
-        [hidden_near, hidden_far] + blocks,
+        [shares[4]] + blocks,
         [((4, 3, half, width), F32)] + [((4, half, width), BF16)] * 3,
-        [pltpu.VMEM((slots, 3 * hidden), BF16), pltpu.VMEM((slots, width), BF16)],
+        [pltpu.VMEM((slots, width), BF16)],
     )
     moved = [swap(send, "core") for send in sends]
     near, back = halfway(passed, shares[1], shares[3])

time: 159 us -> 152 us (0.956)
  waiting for transfers between devices: 79.4 us -> 74.4 us
  local copies, waits for them, and re-layouts: 3.63 us -> 1.62 us
    ppermute x9, waiting for transfers between devices: 21.5 us -> 14.9 us  [swap(): return lax.ppermute(value, axis, [(0, 1), (1, 0)])]
    unnamed x21 -> x19, local copies, waits for them, and re-layouts: 2.92 us -> 0.92 us
    ppermute x14, waiting for transfers between devices: 32.7 us -> 34.3 us  [shift(): return lax.ppermute(value, axis, [(i, (i + step) % 4) for i in range(4)])]
  transfers between devices with their start and end apart: 30 -> 30, of which waited for: 19 -> 18; matrix products, arithmetic and copies ran while one was open for 3% -> 2% of each run, Pallas kernels for 5% -> 8%
where the time goes in v7:
time: 152 us
  waiting for transfers between devices  74.4 us (49%)
  starting transfers between devices  46.5 us (31%)
  Pallas kernels  21.5 us (14%)
  other arithmetic  7.05 us (5%)
  local copies, waits for them, and re-layouts  1.62 us (1%)
    ppermute x14, waiting for transfers between devices, shift(): return lax.ppermute(value, axis, [(i, (i + step) % 4) for i in range(4)])  34.3 us
    ppermute x14, starting transfers between devices, shift(): return lax.ppermute(value, axis, [(i, (i + step) % 4) for i in range(4)])  23.2 us
    pallas_call x7, Pallas kernels, call(): pl.pallas_call(kernel, out_shape=[jax.ShapeDtypeStruct(shape, kind) for s...  21.5 us
    ppermute x9, waiting for transfers between devices, swap(): return lax.ppermute(value, axis, [(0, 1), (1, 0)])  14.9 us
    ppermute x2, waiting for transfers between devices, relay(): lax.ppermute(value, ('core', axis), [(4 * c + i, 4 * c + j) for c, i, j i...  8.19 us
    ppermute x2, starting transfers between devices, turn(): lax.ppermute(value, ('core', 'zl'), [(2 * c + z, 2 * z + c) for c in rang...  8.18 us
    ppermute x2, waiting for transfers between devices, relay(): lax.ppermute(value, ('x', 'core'), [(2 * i + c, 2 * j + c) for c, i, j in...  6.83 us
    ppermute x1, waiting for transfers between devices, body(): turned = lax.ppermute(own, ('core', 'zl'), [(1, 2), (2, 1)])  6.23 us
  transfers between devices with their start and end apart: 30, of which 18 were waited for; matrix products, arithmetic and copies ran while one was open for 2% of the time, Pallas kernels for 8%

profile of v7, /device:TPU:1, one launch (start us, length us, event | category | flops | bytes accessed | tf_op | source)
XLA Modules:
  0.0 152.0 jit_solution(1735458394094109450)
XLA Ops:
  0.7 0.7 convert_bitcast_fusion
  1.4 0.7 pad_maximum_fusion.3.small
  2.1 1.0 pad_maximum_fusion.2.wide
  3.2 1.0 shard_map.84
  4.2 4.9 %collective-permute-start.3 = (bf16[3,192,512]{2,1,0:T(8,128)(2,1)}, bf16[3,192,512]{2,1,0:T(8,128)(2,1)S(1)}, u32[]{:S(2)}, u32[]{:S(2)}) collective-permute-start(bf16[3,192,512]{2,1,0:T(8,128)(2,1)} %bitcast.50), channel_id=1, source_target_pairs={{1,32},{32,1},{3,34},{34,3},{5,36},{36,5},{7,38},{38,7},{9,40},{40... | collective-permute-start | bytes 1769480 | tf_op jit(solution)/shard_map/ppermute | solution.py:268
  9.1 3.1 %collective-permute-start = (bf16[160,512]{1,0:T(8,128)(2,1)S(1)}, bf16[160,512]{1,0:T(8,128)(2,1)S(1)}, u32[]{:S(2)}, u32[]{:S(2)}) collective-permute-start(bf16[160,512]{1,0:T(8,128)(2,1)S(1)} %get-tuple-element.49), channel_id=1, source_target_pairs={{0,8},{8,16},{16,24},{24,0},{1,9},{9,17},{17,25},{25,1},{2,10},{10... | collective-permute-start | bytes 491528 | tf_op jit(solution)/shard_map/ppermute | solution.py:228
  12.2 4.2 %collective-permute-start.1 = (bf16[160,512]{1,0:T(8,128)(2,1)S(1)}, bf16[160,512]{1,0:T(8,128)(2,1)S(1)}, u32[]{:S(2)}, u32[]{:S(2)}) collective-permute-start(bf16[160,512]{1,0:T(8,128)(2,1)S(1)} %get-tuple-element.50), channel_id=1, source_target_pairs={{0,16},{8,24},{16,0},{24,8},{1,17},{9,25},{17,1},{25,9},{2,18},{10... | collective-permute-start | bytes 491528 | tf_op jit(solution)/shard_map/ppermute | solution.py:228
  16.4 2.4 %collective-permute-start.2 = (bf16[160,512]{1,0:T(8,128)(2,1)S(1)}, bf16[160,512]{1,0:T(8,128)(2,1)S(1)}, u32[]{:S(2)}, u32[]{:S(2)}) collective-permute-start(bf16[160,512]{1,0:T(8,128)(2,1)S(1)} %get-tuple-element.51), channel_id=1, source_target_pairs={{0,24},{8,0},{16,8},{24,16},{1,25},{9,1},{17,9},{25,17},{2,26},{10... | collective-permute-start | bytes 491528 | tf_op jit(solution)/shard_map/ppermute | solution.py:228
  18.8 6.2 %collective-permute-done.3 = bf16[3,192,512]{2,1,0:T(8,128)(2,1)S(1)} collective-permute-done((bf16[3,192,512]{2,1,0:T(8,128)(2,1)}, bf16[3,192,512]{2,1,0:T(8,128)(2,1)S(1)}, u32[]{:S(2)}, u32[]{:S(2)}) %collective-permute-start.3) | collective-permute-done | bytes 589856 | tf_op jit(solution)/shard_map/ppermute | solution.py:268
  25.1 2.6 %collective-permute-start.5 = (bf16[3,192,512]{2,1,0:T(8,128)(2,1)S(1)}, bf16[3,192,512]{2,1,0:T(8,128)(2,1)S(1)}, u32[]{:S(2)}, u32[]{:S(2)}) collective-permute-start(bf16[3,192,512]{2,1,0:T(8,128)(2,1)S(1)} %broadcast_select_fusion.2.refs_4_), channel_id=1, source_target_pairs={{0,192},{64,0},{128,64},{192,128},{1,193},{65,1},{129,65},{193,129... | collective-permute-start | bytes 1769480 | tf_op jit(solution)/shard_map/ppermute | solution.py:228
  27.7 2.8 %collective-permute-done = bf16[160,512]{1,0:T(8,128)(2,1)S(1)} collective-permute-done((bf16[160,512]{1,0:T(8,128)(2,1)S(1)}, bf16[160,512]{1,0:T(8,128)(2,1)S(1)}, u32[]{:S(2)}, u32[]{:S(2)}) %collective-permute-start) | collective-permute-done | bytes 163872 | tf_op jit(solution)/shard_map/ppermute | solution.py:228
  30.5 5.9 %collective-permute-done.1 = bf16[160,512]{1,0:T(8,128)(2,1)S(1)} collective-permute-done((bf16[160,512]{1,0:T(8,128)(2,1)S(1)}, bf16[160,512]{1,0:T(8,128)(2,1)S(1)}, u32[]{:S(2)}, u32[]{:S(2)}) %collective-permute-start.1) | collective-permute-done | bytes 163872 | tf_op jit(solution)/shard_map/ppermute | solution.py:228
  36.4 2.8 %collective-permute-start.7 = (bf16[640,512]{1,0:T(8,128)(2,1)S(1)}, bf16[640,512]{1,0:T(8,128)(2,1)S(1)}, u32[]{:S(2)}, u32[]{:S(2)}) collective-permute-start(bf16[640,512]{1,0:T(8,128)(2,1)S(1)} %constant_dynamic-update-slice_fusion.refs_0_), channel_id=1, source_target_pairs={{0,6},{2,0},{4,2},{6,4},{1,7},{3,1},{5,3},{7,5},{8,14},{10,8},{12,... | collective-permute-start | bytes 1966088 | tf_op jit(solution)/shard_map/ppermute | solution.py:228
  39.3 2.6 %collective-permute-start.9 = (bf16[3,192,512]{2,1,0:T(8,128)(2,1)S(1)}, bf16[3,192,512]{2,1,0:T(8,128)(2,1)S(1)}, u32[]{:S(2)}, u32[]{:S(2)}) collective-permute-start(bf16[3,192,512]{2,1,0:T(8,128)(2,1)S(1)} %broadcast_select_fusion.1), channel_id=1, source_target_pairs={{0,64},{64,128},{128,192},{192,0},{32,224},{96,32},{160,96},{224,1... | collective-permute-start | bytes 1769480 | tf_op jit(solution)/shard_map/ppermute | solution.py:234
  41.9 4.9 %collective-permute-done.7.refs_3_ = bf16[640,512]{1,0:T(8,128)(2,1)S(1)} collective-permute-done((bf16[640,512]{1,0:T(8,128)(2,1)S(1)}, bf16[640,512]{1,0:T(8,128)(2,1)S(1)}, u32[]{:S(2)}, u32[]{:S(2)}) %collective-permute-start.7) | collective-permute-done | bytes 655392 | tf_op jit(solution)/shard_map/ppermute | solution.py:228
  46.7 5.6 %collective-permute-done.6.refs_1_ = bf16[640,512]{1,0:T(8,128)(2,1)S(1)} collective-permute-done((bf16[640,512]{1,0:T(8,128)(2,1)S(1)}, bf16[640,512]{1,0:T(8,128)(2,1)S(1)}, u32[]{:S(2)}, u32[]{:S(2)}) %collective-permute-start.6) | collective-permute-done | bytes 655392 | tf_op jit(solution)/shard_map/ppermute | solution.py:228
  53.6 1.0 collective-permute-done.10.refs_8_
  54.6 1.9 %collective-permute-done.11.refs_9_ = bf16[3,192,512]{2,1,0:T(8,128)(2,1)S(1)} collective-permute-done((bf16[3,192,512]{2,1,0:T(8,128)(2,1)}, bf16[3,192,512]{2,1,0:T(8,128)(2,1)S(1)}, u32[]{:S(2)}, u32[]{:S(2)}) %collective-permute-start.11) | collective-permute-done | bytes 589856 | tf_op jit(solution)/shard_map/ppermute | solution.py:239
  56.5 5.4 %collective-permute-done.8.refs_2_ = bf16[640,512]{1,0:T(8,128)(2,1)S(1)} collective-permute-done((bf16[640,512]{1,0:T(8,128)(2,1)S(1)}, bf16[640,512]{1,0:T(8,128)(2,1)S(1)}, u32[]{:S(2)}, u32[]{:S(2)}) %collective-permute-start.8) | collective-permute-done | bytes 655392 | tf_op jit(solution)/shard_map/ppermute | solution.py:235
  61.9 0.9 copy-done.4
  62.8 4.4 %shard_map.85 = (bf16[320,768]{1,0:T(8,128)(2,1)S(1)}, bf16[768,2048]{1,0:T(8,128)(2,1)}) custom-call(s32[5]{0:T(128)S(1)} %stack.48.place, bf16[640,512]{1,0:T(8,128)(2,1)S(1)} %constant_dynamic-update-slice_fusion.refs_0_, bf16[640,512]{1,0:T(8,128)(2,1)} %copy-done.2, bf16[640,512]{1,0:T(8,128)(2,1)} %copy-done.4, bf16[640,512]{1,0:T(8,128)(2,1)} %copy-done, ...), custom_call_target="tpu_custom_call" | custom-call | tf_op jit(solution)/shard_map/pallas_call | solution.py:33
  67.5 3.8 %shard_map.86 = (bf16[320,384]{1,0:T(8,128)(2,1)S(1)}, bf16[384,2048]{1,0:T(8,128)(2,1)}) custom-call(s32[5]{0:T(128)S(1)} %stack.48.place, bf16[640,512]{1,0:T(8,128)(2,1)S(1)} %constant_dynamic-update-slice_fusion.refs_0_, bf16[640,512]{1,0:T(8,128)(2,1)} %copy-done.2, bf16[640,512]{1,0:T(8,128)(2,1)} %copy-done.4, bf16[640,512]{1,0:T(8,128)(2,1)} %copy-done, ...), custom_call_target="tpu_custom_call" | custom-call | tf_op jit(solution)/shard_map/pallas_call | solution.py:33
  71.3 1.5 %collective-permute-start.15 = (bf16[320,384]{1,0:T(8,128)(2,1)S(1)}, bf16[320,384]{1,0:T(8,128)(2,1)S(1)}, u32[]{:S(2)}, u32[]{:S(2)}) collective-permute-start(bf16[320,384]{1,0:T(8,128)(2,1)S(1)} %get-tuple-element.59.down), channel_id=1, source_target_pairs={{0,1},{1,0},{2,3},{3,2},{4,5},{5,4},{6,7},{7,6},{8,9},{9,8},{10,11... | collective-permute-start | bytes 737288 | tf_op jit(solution)/shard_map/ppermute | solution.py:239
  72.8 11.2 %collective-permute-done.15.down_far = bf16[320,384]{1,0:T(8,128)(2,1)S(1)} collective-permute-done((bf16[320,384]{1,0:T(8,128)(2,1)S(1)}, bf16[320,384]{1,0:T(8,128)(2,1)S(1)}, u32[]{:S(2)}, u32[]{:S(2)}) %collective-permute-start.15) | collective-permute-done | bytes 245792 | tf_op jit(solution)/shard_map/ppermute | solution.py:239
  84.0 4.6 %shard_map.87 = (f32[656,512]{1,0:T(8,128)S(1)}, bf16[656,512]{1,0:T(8,128)(2,1)S(1)}, bf16[656,512]{1,0:T(8,128)(2,1)S(1)}, bf16[656,512]{1,0:T(8,128)(2,1)S(1)}, bf16[320,1152]{1,0:T(8,128)(2,1)S(1)}) custom-call(s32[5]{0:T(128)S(1)} %stack.48.place, bf16[320,768]{1,0:T(8,128)(2,1)S(1)} %get-tuple-element.58.pair, ...), custom_call_target="tpu_custom_call" | custom-call | tf_op jit(solution)/shard_map/pallas_call | solution.py:33
  88.6 1.4 collective-permute-start.16
  90.1 5.3 %shard_map.88 = (f32[4,3,192,512]{3,2,1,0:T(8,128)}, bf16[4,192,512]{2,1,0:T(8,128)(2,1)S(1)}, bf16[4,192,512]{2,1,0:T(8,128)(2,1)S(1)}, bf16[4,192,512]{2,1,0:T(8,128)(2,1)S(1)}) custom-call(s32[5]{0:T(128)S(1)} %stack.48.place, bf16[320,1152]{1,0:T(8,128)(2,1)S(1)} %get-tuple-element.62.joined, ...), custom_call_target="tpu_custom_call" | custom-call | tf_op jit(solution)/shard_map/pallas_call | solution.py:33
  95.9 2.8 %collective-permute-done.16 = bf16[656,512]{1,0:T(8,128)(2,1)S(1)} collective-permute-done((bf16[656,512]{1,0:T(8,128)(2,1)S(1)}, bf16[656,512]{1,0:T(8,128)(2,1)S(1)}, u32[]{:S(2)}, u32[]{:S(2)}) %collective-permute-start.16) | collective-permute-done | bytes 671776 | tf_op jit(solution)/shard_map/ppermute | solution.py:235
  99.0 0.9 collective-permute-done.19
  99.9 1.5 collective-permute-start.21
  101.4 1.6 %bitcast_add_fusion.7 = (f32[1,192,512]{2,1,0:T(8,128)S(1)}, f32[1,192,512]{2,1,0:T(8,128)S(1)}, bf16[1,192,512]{2,1,0:T(8,128)(2,1)S(1)}, f32[1,192,512]{2,1,0:T(8,128)S(1)}) fusion(f32[4,3,192,512]{3,2,1,0:T(8,128)} %get-tuple-element.63, bf16[4,192,512]{2,1,0:T(8,128)(2,1)S(1)} %collective-permute-done.18), kind=kLoop, calls=%fused_computation.30 | loop fusion | flops 884736 | bytes 3735552 | tf_op jit(solution)/shard_map/add | solution.py:325
  103.6 2.7 %collective-permute-start.20 = (bf16[3,192,512]{2,1,0:T(8,128)(2,1)S(1)}, bf16[3,192,512]{2,1,0:T(8,128)(2,1)S(1)}, u32[]{:S(2)}, u32[]{:S(2)}) collective-permute-start(bf16[3,192,512]{2,1,0:T(8,128)(2,1)S(1)} %pad_maximum_fusion), channel_id=1, source_target_pairs={{0,64},{64,128},{128,192},{192,0},{32,224},{96,32},{160,96},{224,1... | collective-permute-start | bytes 1769480 | tf_op jit(solution)/shard_map/ppermute | solution.py:234
  106.2 6.8 %collective-permute-done.20 = bf16[3,192,512]{2,1,0:T(8,128)(2,1)S(1)} collective-permute-done((bf16[3,192,512]{2,1,0:T(8,128)(2,1)S(1)}, bf16[3,192,512]{2,1,0:T(8,128)(2,1)S(1)}, u32[]{:S(2)}, u32[]{:S(2)}) %collective-permute-start.20) | collective-permute-done | bytes 589856 | tf_op jit(solution)/shard_map/ppermute | solution.py:234
  113.1 2.4 %collective-permute-done.21.one = bf16[656,512]{1,0:T(8,128)(2,1)S(1)} collective-permute-done((bf16[656,512]{1,0:T(8,128)(2,1)S(1)}, bf16[656,512]{1,0:T(8,128)(2,1)S(1)}, u32[]{:S(2)}, u32[]{:S(2)}) %collective-permute-start.21) | collective-permute-done | bytes 671776 | tf_op jit(solution)/shard_map/ppermute | solution.py:228
  115.5 3.1 %collective-permute-done.22.three = bf16[656,512]{1,0:T(8,128)(2,1)S(1)} collective-permute-done((bf16[656,512]{1,0:T(8,128)(2,1)S(1)}, bf16[656,512]{1,0:T(8,128)(2,1)S(1)}, u32[]{:S(2)}, u32[]{:S(2)}) %collective-permute-start.22) | collective-permute-done | bytes 671776 | tf_op jit(solution)/shard_map/ppermute | solution.py:228
  119.0 2.8 %collective-permute-start.23 = (bf16[3,192,512]{2,1,0:T(8,128)(2,1)S(1)}, bf16[3,192,512]{2,1,0:T(8,128)(2,1)S(1)}, u32[]{:S(2)}, u32[]{:S(2)}) collective-permute-start(bf16[3,192,512]{2,1,0:T(8,128)(2,1)S(1)} %get-tuple-element.110), channel_id=1, source_target_pairs={{0,192},{64,0},{128,64},{192,128},{1,193},{65,1},{129,65},{193,129... | collective-permute-start | bytes 1769480 | tf_op jit(solution)/shard_map/ppermute | solution.py:228
  121.8 0.8 shard_map.89
  122.5 1.7 %collective-permute-start.27 = (bf16[176,512]{1,0:T(8,128)(2,1)S(1)}, bf16[176,512]{1,0:T(8,128)(2,1)S(1)}, u32[]{:S(2)}, u32[]{:S(2)}) collective-permute-start(bf16[176,512]{1,0:T(8,128)(2,1)S(1)} %get-tuple-element.81), channel_id=1, source_target_pairs={{0,24},{8,0},{16,8},{24,16},{1,25},{9,1},{17,9},{25,17},{2,26},{10... | collective-permute-start | bytes 540680 | tf_op jit(solution)/shard_map/ppermute | solution.py:228
  124.3 1.5 collective-permute-start.28
  125.7 0.7 collective-permute-start.29
  126.4 7.2 %collective-permute-done.23 = bf16[3,192,512]{2,1,0:T(8,128)(2,1)S(1)} collective-permute-done((bf16[3,192,512]{2,1,0:T(8,128)(2,1)S(1)}, bf16[3,192,512]{2,1,0:T(8,128)(2,1)S(1)}, u32[]{:S(2)}, u32[]{:S(2)}) %collective-permute-start.23) | collective-permute-done | bytes 589856 | tf_op jit(solution)/shard_map/ppermute | solution.py:228
  133.7 2.5 %collective-permute-done.24 = bf16[3,192,512]{2,1,0:T(8,128)(2,1)S(1)} collective-permute-done((bf16[3,192,512]{2,1,0:T(8,128)(2,1)S(1)}, bf16[3,192,512]{2,1,0:T(8,128)(2,1)S(1)}, u32[]{:S(2)}, u32[]{:S(2)}) %collective-permute-start.24) | collective-permute-done | bytes 589856 | tf_op jit(solution)/shard_map/ppermute | solution.py:228
  136.4 6.3 %collective-permute-start.26 = (bf16[288,512]{1,0:T(8,128)(2,1)S(1)}, bf16[288,512]{1,0:T(8,128)(2,1)S(1)}, u32[]{:S(2)}, u32[]{:S(2)}) collective-permute-start(bf16[288,512]{1,0:T(8,128)(2,1)S(1)} %get-tuple-element.108), channel_id=1, source_target_pairs={{0,0},{1,32},{32,1},{33,33},{2,2},{3,34},{34,3},{35,35},{4,4},{5,3... | collective-permute-start | bytes 884744 | tf_op jit(solution)/shard_map/ppermute | solution.py:243
  142.7 1.9 %collective-permute-start.25 = (bf16[288,512]{1,0:T(8,128)(2,1)S(1)}, bf16[288,512]{1,0:T(8,128)(2,1)S(1)}, u32[]{:S(2)}, u32[]{:S(2)}) collective-permute-start(bf16[288,512]{1,0:T(8,128)(2,1)S(1)} %get-tuple-element.109), channel_id=1, source_target_pairs={{0,0},{1,32},{32,1},{33,33},{2,2},{3,34},{34,3},{35,35},{4,4},{5,3... | collective-permute-start | bytes 884744 | tf_op jit(solution)/shard_map/ppermute | solution.py:243
  144.7 1.7 %shard_map.90 = (bf16[128,512]{1,0:T(8,128)(2,1)}, bf16[128,512]{1,0:T(8,128)(2,1)}, f32[8,128]{1,0:T(8,128)S(1)}) custom-call(s32[5]{0:T(128)S(1)} %stack.48.place, f32[4,128]{1,0:T(4,128)S(1)} %pad_maximum_fusion.3.small, bf16[320,128]{1,0:T(8,128)(2,1)S(1)} %get-tuple-element.76.placing, bf16[176,512]{1,0:T(8,128)(2,1)S(1)} %get-tuple-element.80.refs_0_, ...), custom_call_target="tpu_custom_call" | custom-call | tf_op jit(solution)/shard_map/pallas_call | solution.py:33
  146.4 0.6 slice_bitcast_fusion.2
  147.1 3.6 %collective-permute-done.25 = bf16[288,512]{1,0:T(8,128)(2,1)S(1)} collective-permute-done((bf16[288,512]{1,0:T(8,128)(2,1)S(1)}, bf16[288,512]{1,0:T(8,128)(2,1)S(1)}, u32[]{:S(2)}, u32[]{:S(2)}) %collective-permute-start.25) | collective-permute-done | bytes 294944 | tf_op jit(solution)/shard_map/ppermute | solution.py:243
  150.8 1.2 convert.14
  (56 shorter events, 4.3 us)
Async XLA Ops:
  0.6 24.4 %copy-start.7 = (bf16[1,3,192,512]{3,2,1,0:T(8,128)(2,1)S(1)}, bf16[1,3,192,512]{3,2,1,0:T(8,128)(2,1)}, u32[]{:S(2)}) copy-start(bf16[1,3,192,512]{3,2,1,0:T(8,128)(2,1)} %param.8) | copy-start | bytes 1769476
  4.2 20.8 %collective-permute-start.3 = (bf16[3,192,512]{2,1,0:T(8,128)(2,1)}, bf16[3,192,512]{2,1,0:T(8,128)(2,1)S(1)}, u32[]{:S(2)}, u32[]{:S(2)}) collective-permute-start(bf16[3,192,512]{2,1,0:T(8,128)(2,1)} %bitcast.50), channel_id=1, source_target_pairs={{1,32},{32,1},{3,34},{34,3},{5,36},{36,5},{7,38},{38,7},{9,40},{40... | collective-permute-start | bytes 1769480 | tf_op jit(solution)/shard_map/ppermute | solution.py:268
  9.1 21.4 %collective-permute-start = (bf16[160,512]{1,0:T(8,128)(2,1)S(1)}, bf16[160,512]{1,0:T(8,128)(2,1)S(1)}, u32[]{:S(2)}, u32[]{:S(2)}) collective-permute-start(bf16[160,512]{1,0:T(8,128)(2,1)S(1)} %get-tuple-element.49), channel_id=1, source_target_pairs={{0,8},{8,16},{16,24},{24,0},{1,9},{9,17},{17,25},{25,1},{2,10},{10... | collective-permute-start | bytes 491528 | tf_op jit(solution)/shard_map/ppermute | solution.py:228
  12.2 24.1 %collective-permute-start.1 = (bf16[160,512]{1,0:T(8,128)(2,1)S(1)}, bf16[160,512]{1,0:T(8,128)(2,1)S(1)}, u32[]{:S(2)}, u32[]{:S(2)}) collective-permute-start(bf16[160,512]{1,0:T(8,128)(2,1)S(1)} %get-tuple-element.50), channel_id=1, source_target_pairs={{0,16},{8,24},{16,0},{24,8},{1,17},{9,25},{17,1},{25,9},{2,18},{10... | collective-permute-start | bytes 491528 | tf_op jit(solution)/shard_map/ppermute | solution.py:228
  16.4 20.0 %collective-permute-start.2 = (bf16[160,512]{1,0:T(8,128)(2,1)S(1)}, bf16[160,512]{1,0:T(8,128)(2,1)S(1)}, u32[]{:S(2)}, u32[]{:S(2)}) collective-permute-start(bf16[160,512]{1,0:T(8,128)(2,1)S(1)} %get-tuple-element.51), channel_id=1, source_target_pairs={{0,24},{8,0},{16,8},{24,16},{1,25},{9,1},{17,9},{25,17},{2,26},{10... | collective-permute-start | bytes 491528 | tf_op jit(solution)/shard_map/ppermute | solution.py:228
  25.1 14.1 %collective-permute-start.5 = (bf16[3,192,512]{2,1,0:T(8,128)(2,1)S(1)}, bf16[3,192,512]{2,1,0:T(8,128)(2,1)S(1)}, u32[]{:S(2)}, u32[]{:S(2)}) collective-permute-start(bf16[3,192,512]{2,1,0:T(8,128)(2,1)S(1)} %broadcast_select_fusion.2.refs_4_), channel_id=1, source_target_pairs={{0,192},{64,0},{128,64},{192,128},{1,193},{65,1},{129,65},{193,129... | collective-permute-start | bytes 1769480 | tf_op jit(solution)/shard_map/ppermute | solution.py:228
  27.6 11.6 %collective-permute-start.4 = (bf16[3,192,512]{2,1,0:T(8,128)(2,1)S(1)}, bf16[3,192,512]{2,1,0:T(8,128)(2,1)}, u32[]{:S(2)}, u32[]{:S(2)}) collective-permute-start(bf16[3,192,512]{2,1,0:T(8,128)(2,1)S(1)} %broadcast_select_fusion.2.refs_4_), channel_id=1, source_target_pairs={{0,64},{64,128},{128,192},{192,0},{1,65},{65,129},{129,193},{193,1... | collective-permute-start | bytes 1769480 | tf_op jit(solution)/shard_map/ppermute | solution.py:228
  36.4 10.3 %collective-permute-start.7 = (bf16[640,512]{1,0:T(8,128)(2,1)S(1)}, bf16[640,512]{1,0:T(8,128)(2,1)S(1)}, u32[]{:S(2)}, u32[]{:S(2)}) collective-permute-start(bf16[640,512]{1,0:T(8,128)(2,1)S(1)} %constant_dynamic-update-slice_fusion.refs_0_), channel_id=1, source_target_pairs={{0,6},{2,0},{4,2},{6,4},{1,7},{3,1},{5,3},{7,5},{8,14},{10,8},{12,... | collective-permute-start | bytes 1966088 | tf_op jit(solution)/shard_map/ppermute | solution.py:228
  39.2 13.1 %collective-permute-start.6 = (bf16[640,512]{1,0:T(8,128)(2,1)S(1)}, bf16[640,512]{1,0:T(8,128)(2,1)S(1)}, u32[]{:S(2)}, u32[]{:S(2)}) collective-permute-start(bf16[640,512]{1,0:T(8,128)(2,1)S(1)} %constant_dynamic-update-slice_fusion.refs_0_), channel_id=1, source_target_pairs={{0,2},{2,4},{4,6},{6,0},{1,3},{3,5},{5,7},{7,1},{8,10},{10,12},{12... | collective-permute-start | bytes 1966088 | tf_op jit(solution)/shard_map/ppermute | solution.py:228
  39.3 13.9 %collective-permute-start.9 = (bf16[3,192,512]{2,1,0:T(8,128)(2,1)S(1)}, bf16[3,192,512]{2,1,0:T(8,128)(2,1)S(1)}, u32[]{:S(2)}, u32[]{:S(2)}) collective-permute-start(bf16[3,192,512]{2,1,0:T(8,128)(2,1)S(1)} %broadcast_select_fusion.1), channel_id=1, source_target_pairs={{0,64},{64,128},{128,192},{192,0},{32,224},{96,32},{160,96},{224,1... | collective-permute-start | bytes 1769480 | tf_op jit(solution)/shard_map/ppermute | solution.py:234
  46.7 15.2 %copy-start = (bf16[640,512]{1,0:T(8,128)(2,1)}, bf16[640,512]{1,0:T(8,128)(2,1)S(1)}, u32[]{:S(2)}) copy-start(bf16[640,512]{1,0:T(8,128)(2,1)S(1)} %collective-permute-done.7.refs_3_) | copy-start | bytes 1966084
  52.3 9.6 %copy-start.2 = (bf16[640,512]{1,0:T(8,128)(2,1)}, bf16[640,512]{1,0:T(8,128)(2,1)S(1)}, u32[]{:S(2)}) copy-start(bf16[640,512]{1,0:T(8,128)(2,1)S(1)} %collective-permute-done.6.refs_1_) | copy-start | bytes 1966084
  52.4 9.5 %collective-permute-start.8 = (bf16[640,512]{1,0:T(8,128)(2,1)S(1)}, bf16[640,512]{1,0:T(8,128)(2,1)S(1)}, u32[]{:S(2)}, u32[]{:S(2)}) collective-permute-start(bf16[640,512]{1,0:T(8,128)(2,1)S(1)} %broadcast_select_fusion), channel_id=1, source_target_pairs={{0,2},{2,4},{4,6},{6,0},{32,38},{34,32},{36,34},{38,36},{1,3},{3,5... | collective-permute-start | bytes 1966088 | tf_op jit(solution)/shard_map/ppermute | solution.py:235
  52.5 2.1 %collective-permute-start.10 = (bf16[3,192,512]{2,1,0:T(8,128)(2,1)S(1)}, bf16[3,192,512]{2,1,0:T(8,128)(2,1)S(1)}, u32[]{:S(2)}, u32[]{:S(2)}) collective-permute-start(bf16[3,192,512]{2,1,0:T(8,128)(2,1)S(1)} %broadcast_select_fusion.2.refs_4_), channel_id=1, source_target_pairs={{0,32},{32,0},{1,33},{33,1},{2,34},{34,2},{3,35},{35,3},{4,36},{36... | collective-permute-start | bytes 1769480 | tf_op jit(solution)/shard_map/ppermute | solution.py:239
  52.6 3.9 %collective-permute-start.11 = (bf16[3,192,512]{2,1,0:T(8,128)(2,1)}, bf16[3,192,512]{2,1,0:T(8,128)(2,1)S(1)}, u32[]{:S(2)}, u32[]{:S(2)}) collective-permute-start(bf16[3,192,512]{2,1,0:T(8,128)(2,1)} %collective-permute-done.4.refs_5_), channel_id=1, source_target_pairs={{0,32},{32,0},{1,33},{33,1},{2,34},{34,2},{3,35},{35,3},{4,36},{36... | collective-permute-start | bytes 1769480 | tf_op jit(solution)/shard_map/ppermute | solution.py:239
  53.1 3.4 %collective-permute-start.13 = (bf16[3,192,512]{2,1,0:T(8,128)(2,1)S(1)}, bf16[3,192,512]{2,1,0:T(8,128)(2,1)S(1)}, u32[]{:S(2)}, u32[]{:S(2)}) collective-permute-start(bf16[3,192,512]{2,1,0:T(8,128)(2,1)S(1)} %collective-permute-done.5.refs_7_), channel_id=1, source_target_pairs={{0,32},{32,0},{1,33},{33,1},{2,34},{34,2},{3,35},{35,3},{4,36},{36... | collective-permute-start | bytes 1769480 | tf_op jit(solution)/shard_map/ppermute | solution.py:239
  53.2 8.7 %collective-permute-start.12 = (bf16[3,192,512]{2,1,0:T(8,128)(2,1)S(1)}, bf16[3,192,512]{2,1,0:T(8,128)(2,1)S(1)}, u32[]{:S(2)}, u32[]{:S(2)}) collective-permute-start(bf16[3,192,512]{2,1,0:T(8,128)(2,1)S(1)} %collective-permute-done.9.refs_6_), channel_id=1, source_target_pairs={{0,32},{32,0},{1,33},{33,1},{2,34},{34,2},{3,35},{35,3},{4,36},{36... | collective-permute-start | bytes 1769480 | tf_op jit(solution)/shard_map/ppermute | solution.py:239
  61.9 0.9 copy-start.4
  67.2 16.8 %collective-permute-start.14 = (bf16[320,768]{1,0:T(8,128)(2,1)S(1)}, bf16[320,768]{1,0:T(8,128)(2,1)S(1)}, u32[]{:S(2)}, u32[]{:S(2)}) collective-permute-start(bf16[320,768]{1,0:T(8,128)(2,1)S(1)} %get-tuple-element.58.pair), channel_id=1, source_target_pairs={{0,1},{1,0},{2,3},{3,2},{4,5},{5,4},{6,7},{7,6},{8,9},{9,8},{10,11... | collective-permute-start | bytes 1474568 | tf_op jit(solution)/shard_map/ppermute | solution.py:239
  71.3 12.7 %collective-permute-start.15 = (bf16[320,384]{1,0:T(8,128)(2,1)S(1)}, bf16[320,384]{1,0:T(8,128)(2,1)S(1)}, u32[]{:S(2)}, u32[]{:S(2)}) collective-permute-start(bf16[320,384]{1,0:T(8,128)(2,1)S(1)} %get-tuple-element.59.down), channel_id=1, source_target_pairs={{0,1},{1,0},{2,3},{3,2},{4,5},{5,4},{6,7},{7,6},{8,9},{9,8},{10,11... | collective-permute-start | bytes 737288 | tf_op jit(solution)/shard_map/ppermute | solution.py:239
  84.0 6.1 %copy-start.1 = (bf16[640,512]{1,0:T(8,128)(2,1)S(1)}, bf16[640,512]{1,0:T(8,128)(2,1)}, u32[]{:S(2)}) copy-start(bf16[640,512]{1,0:T(8,128)(2,1)} %copy-done) | copy-start | bytes 1966084
  84.0 6.1 %copy-start.3 = (bf16[640,512]{1,0:T(8,128)(2,1)S(1)}, bf16[640,512]{1,0:T(8,128)(2,1)}, u32[]{:S(2)}) copy-start(bf16[640,512]{1,0:T(8,128)(2,1)} %copy-done.2) | copy-start | bytes 1966084
  84.0 6.1 %copy-start.5 = (bf16[640,512]{1,0:T(8,128)(2,1)S(1)}, bf16[640,512]{1,0:T(8,128)(2,1)}, u32[]{:S(2)}) copy-start(bf16[640,512]{1,0:T(8,128)(2,1)} %copy-done.4) | copy-start | bytes 1966084
  88.6 10.0 %collective-permute-start.16 = (bf16[656,512]{1,0:T(8,128)(2,1)S(1)}, bf16[656,512]{1,0:T(8,128)(2,1)S(1)}, u32[]{:S(2)}, u32[]{:S(2)}) collective-permute-start(bf16[656,512]{1,0:T(8,128)(2,1)S(1)} %get-tuple-element.65), channel_id=1, source_target_pairs={{0,2},{2,4},{4,6},{6,0},{32,38},{34,32},{36,34},{38,36},{1,3},{3,5... | collective-permute-start | bytes 2015240 | tf_op jit(solution)/shard_map/ppermute | solution.py:235
  95.3 3.6 %collective-permute-start.17 = (bf16[4,192,512]{2,1,0:T(8,128)(2,1)S(1)}, bf16[4,192,512]{2,1,0:T(8,128)(2,1)S(1)}, u32[]{:S(2)}, u32[]{:S(2)}) collective-permute-start(bf16[4,192,512]{2,1,0:T(8,128)(2,1)S(1)} %get-tuple-element.67), channel_id=1, source_target_pairs={{0,32},{32,0},{1,33},{33,1},{2,34},{34,2},{3,35},{35,3},{4,36},{36... | collective-permute-start | bytes 2359304 | tf_op jit(solution)/shard_map/ppermute | solution.py:239
  95.3 3.6 %collective-permute-start.18 = (bf16[4,192,512]{2,1,0:T(8,128)(2,1)S(1)}, bf16[4,192,512]{2,1,0:T(8,128)(2,1)S(1)}, u32[]{:S(2)}, u32[]{:S(2)}) collective-permute-start(bf16[4,192,512]{2,1,0:T(8,128)(2,1)S(1)} %get-tuple-element.68), channel_id=1, source_target_pairs={{0,32},{32,0},{1,33},{33,1},{2,34},{34,2},{3,35},{35,3},{4,36},{36... | collective-permute-start | bytes 2359304 | tf_op jit(solution)/shard_map/ppermute | solution.py:239
  95.9 4.0 %collective-permute-start.19 = (bf16[4,192,512]{2,1,0:T(8,128)(2,1)S(1)}, bf16[4,192,512]{2,1,0:T(8,128)(2,1)S(1)}, u32[]{:S(2)}, u32[]{:S(2)}) collective-permute-start(bf16[4,192,512]{2,1,0:T(8,128)(2,1)S(1)} %get-tuple-element.69), channel_id=1, source_target_pairs={{0,32},{32,0},{1,33},{33,1},{2,34},{34,2},{3,35},{35,3},{4,36},{36... | collective-permute-start | bytes 2359304 | tf_op jit(solution)/shard_map/ppermute | solution.py:239
  98.6 4.3 %copy-start.6 = (f32[4,3,192,512]{3,2,1,0:T(8,128)S(1)}, f32[4,3,192,512]{3,2,1,0:T(8,128)}, u32[]{:S(2)}) copy-start(f32[4,3,192,512]{3,2,1,0:T(8,128)} %get-tuple-element.63) | copy-start | bytes 14155780
  99.9 15.6 %collective-permute-start.21 = (bf16[656,512]{1,0:T(8,128)(2,1)S(1)}, bf16[656,512]{1,0:T(8,128)(2,1)S(1)}, u32[]{:S(2)}, u32[]{:S(2)}) collective-permute-start(bf16[656,512]{1,0:T(8,128)(2,1)S(1)} %get-tuple-element.73), channel_id=1, source_target_pairs={{0,6},{2,0},{4,2},{6,4},{1,7},{3,1},{5,3},{7,5},{8,14},{10,8},{12,... | collective-permute-start | bytes 2015240 | tf_op jit(solution)/shard_map/ppermute | solution.py:228
  101.4 17.2 %collective-permute-start.22 = (bf16[656,512]{1,0:T(8,128)(2,1)S(1)}, bf16[656,512]{1,0:T(8,128)(2,1)S(1)}, u32[]{:S(2)}, u32[]{:S(2)}) collective-permute-start(bf16[656,512]{1,0:T(8,128)(2,1)S(1)} %get-tuple-element.74), channel_id=1, source_target_pairs={{0,2},{2,4},{4,6},{6,0},{1,3},{3,5},{5,7},{7,1},{8,10},{10,12},{12... | collective-permute-start | bytes 2015240 | tf_op jit(solution)/shard_map/ppermute | solution.py:228
  103.6 9.5 %collective-permute-start.20 = (bf16[3,192,512]{2,1,0:T(8,128)(2,1)S(1)}, bf16[3,192,512]{2,1,0:T(8,128)(2,1)S(1)}, u32[]{:S(2)}, u32[]{:S(2)}) collective-permute-start(bf16[3,192,512]{2,1,0:T(8,128)(2,1)S(1)} %pad_maximum_fusion), channel_id=1, source_target_pairs={{0,64},{64,128},{128,192},{192,0},{32,224},{96,32},{160,96},{224,1... | collective-permute-start | bytes 1769480 | tf_op jit(solution)/shard_map/ppermute | solution.py:234
  119.0 14.7 %collective-permute-start.23 = (bf16[3,192,512]{2,1,0:T(8,128)(2,1)S(1)}, bf16[3,192,512]{2,1,0:T(8,128)(2,1)S(1)}, u32[]{:S(2)}, u32[]{:S(2)}) collective-permute-start(bf16[3,192,512]{2,1,0:T(8,128)(2,1)S(1)} %get-tuple-element.110), channel_id=1, source_target_pairs={{0,192},{64,0},{128,64},{192,128},{1,193},{65,1},{129,65},{193,129... | collective-permute-start | bytes 1769480 | tf_op jit(solution)/shard_map/ppermute | solution.py:228
  121.8 14.4 %collective-permute-start.24 = (bf16[3,192,512]{2,1,0:T(8,128)(2,1)S(1)}, bf16[3,192,512]{2,1,0:T(8,128)(2,1)S(1)}, u32[]{:S(2)}, u32[]{:S(2)}) collective-permute-start(bf16[3,192,512]{2,1,0:T(8,128)(2,1)S(1)} %get-tuple-element.111), channel_id=1, source_target_pairs={{0,64},{64,128},{128,192},{192,0},{1,65},{65,129},{129,193},{193,1... | collective-permute-start | bytes 1769480 | tf_op jit(solution)/shard_map/ppermute | solution.py:228
  122.5 22.1 %collective-permute-start.27 = (bf16[176,512]{1,0:T(8,128)(2,1)S(1)}, bf16[176,512]{1,0:T(8,128)(2,1)S(1)}, u32[]{:S(2)}, u32[]{:S(2)}) collective-permute-start(bf16[176,512]{1,0:T(8,128)(2,1)S(1)} %get-tuple-element.81), channel_id=1, source_target_pairs={{0,24},{8,0},{16,8},{24,16},{1,25},{9,1},{17,9},{25,17},{2,26},{10... | collective-permute-start | bytes 540680 | tf_op jit(solution)/shard_map/ppermute | solution.py:228
  124.3 20.4 %collective-permute-start.28 = (bf16[176,512]{1,0:T(8,128)(2,1)S(1)}, bf16[176,512]{1,0:T(8,128)(2,1)S(1)}, u32[]{:S(2)}, u32[]{:S(2)}) collective-permute-start(bf16[176,512]{1,0:T(8,128)(2,1)S(1)} %get-tuple-element.82), channel_id=1, source_target_pairs={{0,16},{8,24},{16,0},{24,8},{1,17},{9,25},{17,1},{25,9},{2,18},{10... | collective-permute-start | bytes 540680 | tf_op jit(solution)/shard_map/ppermute | solution.py:228
  125.7 18.9 %collective-permute-start.29 = (bf16[176,512]{1,0:T(8,128)(2,1)S(1)}, bf16[176,512]{1,0:T(8,128)(2,1)S(1)}, u32[]{:S(2)}, u32[]{:S(2)}) collective-permute-start(bf16[176,512]{1,0:T(8,128)(2,1)S(1)} %get-tuple-element.83), channel_id=1, source_target_pairs={{0,8},{8,16},{16,24},{24,0},{1,9},{9,17},{17,25},{25,1},{2,10},{10... | collective-permute-start | bytes 540680 | tf_op jit(solution)/shard_map/ppermute | solution.py:228
  136.4 10.7 %collective-permute-start.26 = (bf16[288,512]{1,0:T(8,128)(2,1)S(1)}, bf16[288,512]{1,0:T(8,128)(2,1)S(1)}, u32[]{:S(2)}, u32[]{:S(2)}) collective-permute-start(bf16[288,512]{1,0:T(8,128)(2,1)S(1)} %get-tuple-element.108), channel_id=1, source_target_pairs={{0,0},{1,32},{32,1},{33,33},{2,2},{3,34},{34,3},{35,35},{4,4},{5,3... | collective-permute-start | bytes 884744 | tf_op jit(solution)/shard_map/ppermute | solution.py:243
  142.7 8.0 %collective-permute-start.25 = (bf16[288,512]{1,0:T(8,128)(2,1)S(1)}, bf16[288,512]{1,0:T(8,128)(2,1)S(1)}, u32[]{:S(2)}, u32[]{:S(2)}) collective-permute-start(bf16[288,512]{1,0:T(8,128)(2,1)S(1)} %get-tuple-element.109), channel_id=1, source_target_pairs={{0,0},{1,32},{32,1},{33,33},{2,2},{3,34},{34,3},{35,35},{4,4},{5,3... | collective-permute-start | bytes 884744 | tf_op jit(solution)/shard_map/ppermute | solution.py:243

commit v8 on v7

--- a/solution.py
+++ b/solution.py
@@ -182,16 +182,18 @@
 
 
 def weight_kernel(place, joined, *refs):
-    rows, keep, sends, chosen = refs[0:4], refs[4], refs[5:8], refs[8]
-    half = keep.shape[2]
+    rows, keeps, sends, chosen = refs[0:4], refs[4:8], refs[8:12], refs[12]
+    half = keeps[0].shape[1]
     for j in range(4):
-        block = lax.rem(place[1] - place[2] + j + 4, 4)
-        for m, second in ((2, 1), (0, 0), (1, 0)):
-            if m != 1:
-                take_rows(chosen, rows[j], second)
-            total = tn(joined[:, 2 * m * half : 2 * (m + 1) * half], chosen[...])
-            keep[block, m] = total[0:half, :]
-            sends[m][block] = total[half:, :].astype(BF16)
+        spot = lax.rem(place[1] - place[2] + j + 4, 4)
+        for second in range(2):
+            take_rows(chosen.at[second, spot], rows[j], second)
+    for i in (2, 1, 3, 0):
+        for m in range(3):
+            columns = slice(2 * m * half, 2 * (m + 1) * half)
+            total = tn(joined[:, columns], chosen[1 if m == 2 else 0, i])
+            keeps[i][m] = total[0:half, :]
+            sends[i][m] = total[half:, :].astype(BF16)
 
 
 def column(row):
@@ -309,23 +311,23 @@
         + [((slots, 3 * hidden), BF16)],
     )
     passed = relay(shares[2], "y")
-    keep, *sends = call(
+    terms = call(
         weight_kernel,
         place,
         [shares[4]] + blocks,
-        [((4, 3, half, width), F32)] + [((4, half, width), BF16)] * 3,
-        [pltpu.VMEM((slots, width), BF16)],
-    )
+        [((3, half, width), kind) for kind in (F32, BF16) for _ in range(4)],
+        [pltpu.VMEM((2, 4, slots, width), BF16)],
+    )
+    keeps, sends = terms[0:4], terms[4:8]
     moved = [swap(send, "core") for send in sends]
     near, back = halfway(passed, shares[1], shares[3])
     near, back, *moved = lax.optimization_barrier((near, back, *moved))
     arrived = [shift(near, "y", -1), shift(back, "y", 1)]
 
     def both_cores(i):
-        return jnp.stack([keep[i, m] + moved[m][i].astype(F32) for m in range(3)])
+        return keeps[i] + moved[i].astype(F32)
 
     passed = relay(both_cores(2).astype(BF16), "x")
-    passed, *arrived = lax.optimization_barrier((passed, *arrived))
     near, back = halfway(passed, both_cores(1), both_cores(3))
     far_sums = [shift(near, "x", -1), shift(back, "x", 1)]
     totals = call(total_kernel, place, [shares[0]] + arrived, [((unit, width), BF16)] * 4)

time: 152 us -> 150 us (0.987)
  waiting for transfers between devices: 74.4 us -> 69.9 us
  starting transfers between devices: 46.5 us -> 49.2 us
  other arithmetic: 7.05 us -> 5.25 us
  local copies, waits for them, and re-layouts: 1.62 us -> 3.23 us
    ppermute x2, waiting for transfers between devices: 6.83 us -> 4.46 us  [relay(): lax.ppermute(value, ('x', 'core'), [(2 * i + c, 2 * j + c) for c, i, j in...]
    add x2 -> x0, other arithmetic: 2.11 us -> none  [both_cores(): return jnp.stack([keep[i, m] + moved[m][i].astype(F32) for m in range(3)])]
    ppermute x14, waiting for transfers between devices: 34.3 us -> 32.3 us  [shift(): return lax.ppermute(value, axis, [(i, (i + step) % 4) for i in range(4)])]
    ppermute x14, starting transfers between devices: 23.2 us -> 25.1 us  [shift(): return lax.ppermute(value, axis, [(i, (i + step) % 4) for i in range(4)])]
    unnamed x19 -> x25, local copies, waits for them, and re-layouts: 0.92 us -> 2.52 us
    ppermute x9 -> x10, waiting for transfers between devices: 14.9 us -> 14.2 us  [swap(): return lax.ppermute(value, axis, [(0, 1), (1, 0)])]
    ppermute x9 -> x10, starting transfers between devices: 3.42 us -> 3.93 us  [swap(): return lax.ppermute(value, axis, [(0, 1), (1, 0)])]
  transfers between devices with their start and end apart: 30 -> 31, of which waited for: 18 -> 18; matrix products, arithmetic and copies ran while one was open for 2% -> 2% of each run, Pallas kernels for 8% -> 7%
where the time goes in v8:
time: 150 us; the launch traced here: 149 us
  waiting for transfers between devices  69.9 us (47%)
  starting transfers between devices  49.2 us (33%)
  Pallas kernels  20.8 us (14%)
  other arithmetic  5.25 us (4%)
  local copies, waits for them, and re-layouts  3.23 us (2%)
    ppermute x14, waiting for transfers between devices, shift(): return lax.ppermute(value, axis, [(i, (i + step) % 4) for i in range(4)])  32.3 us
    ppermute x14, starting transfers between devices, shift(): return lax.ppermute(value, axis, [(i, (i + step) % 4) for i in range(4)])  25.1 us
    pallas_call x7, Pallas kernels, call(): pl.pallas_call(kernel, out_shape=[jax.ShapeDtypeStruct(shape, kind) for s...  20.8 us
    ppermute x10, waiting for transfers between devices, swap(): return lax.ppermute(value, axis, [(0, 1), (1, 0)])  14.2 us
    ppermute x2, starting transfers between devices, turn(): lax.ppermute(value, ('core', 'zl'), [(2 * c + z, 2 * z + c) for c in rang...  8.64 us
    ppermute x2, waiting for transfers between devices, relay(): lax.ppermute(value, ('core', axis), [(4 * c + i, 4 * c + j) for c, i, j i...  8.37 us
    ppermute x1, waiting for transfers between devices, body(): turned = lax.ppermute(own, ('core', 'zl'), [(1, 2), (2, 1)])  6.23 us
    ppermute x2, starting transfers between devices, relay(): lax.ppermute(value, ('x', 'core'), [(2 * i + c, 2 * j + c) for c, i, j in...  5.11 us
  transfers between devices with their start and end apart: 31, of which 18 were waited for; matrix products, arithmetic and copies ran while one was open for 2% of the time, Pallas kernels for 7%

profile of v8, /device:TPU:1, one launch (start us, length us, event | category | flops | bytes accessed | tf_op | source)
XLA Modules:
  0.0 149.3 jit_solution(5633427957493011738)
XLA Ops:
  0.7 0.7 convert_bitcast_fusion
  1.4 0.7 pad_maximum_fusion.2.small
  2.1 1.0 pad_maximum_fusion.1.wide
  3.2 1.0 shard_map.84
  4.2 4.9 %collective-permute-start.3 = (bf16[3,192,512]{2,1,0:T(8,128)(2,1)}, bf16[3,192,512]{2,1,0:T(8,128)(2,1)S(1)}, u32[]{:S(2)}, u32[]{:S(2)}) collective-permute-start(bf16[3,192,512]{2,1,0:T(8,128)(2,1)} %bitcast.20), channel_id=1, source_target_pairs={{1,32},{32,1},{3,34},{34,3},{5,36},{36,5},{7,38},{38,7},{9,40},{40... | collective-permute-start | bytes 1769480 | tf_op jit(solution)/shard_map/ppermute | solution.py:270
  9.1 3.1 %collective-permute-start = (bf16[160,512]{1,0:T(8,128)(2,1)S(1)}, bf16[160,512]{1,0:T(8,128)(2,1)}, u32[]{:S(2)}, u32[]{:S(2)}) collective-permute-start(bf16[160,512]{1,0:T(8,128)(2,1)S(1)} %get-tuple-element.51), channel_id=1, source_target_pairs={{0,8},{8,16},{16,24},{24,0},{1,9},{9,17},{17,25},{25,1},{2,10},{10... | collective-permute-start | bytes 491528 | tf_op jit(solution)/shard_map/ppermute | solution.py:230
  12.2 4.2 %collective-permute-start.1 = (bf16[160,512]{1,0:T(8,128)(2,1)S(1)}, bf16[160,512]{1,0:T(8,128)(2,1)S(1)}, u32[]{:S(2)}, u32[]{:S(2)}) collective-permute-start(bf16[160,512]{1,0:T(8,128)(2,1)S(1)} %get-tuple-element.52), channel_id=1, source_target_pairs={{0,16},{8,24},{16,0},{24,8},{1,17},{9,25},{17,1},{25,9},{2,18},{10... | collective-permute-start | bytes 491528 | tf_op jit(solution)/shard_map/ppermute | solution.py:230
  16.4 2.4 %collective-permute-start.2 = (bf16[160,512]{1,0:T(8,128)(2,1)S(1)}, bf16[160,512]{1,0:T(8,128)(2,1)S(1)}, u32[]{:S(2)}, u32[]{:S(2)}) collective-permute-start(bf16[160,512]{1,0:T(8,128)(2,1)S(1)} %get-tuple-element.53), channel_id=1, source_target_pairs={{0,24},{8,0},{16,8},{24,16},{1,25},{9,1},{17,9},{25,17},{2,26},{10... | collective-permute-start | bytes 491528 | tf_op jit(solution)/shard_map/ppermute | solution.py:230
  18.8 6.2 %collective-permute-done.3 = bf16[3,192,512]{2,1,0:T(8,128)(2,1)S(1)} collective-permute-done((bf16[3,192,512]{2,1,0:T(8,128)(2,1)}, bf16[3,192,512]{2,1,0:T(8,128)(2,1)S(1)}, u32[]{:S(2)}, u32[]{:S(2)}) %collective-permute-start.3) | collective-permute-done | bytes 589856 | tf_op jit(solution)/shard_map/ppermute | solution.py:270
  25.1 2.6 %collective-permute-start.5 = (bf16[3,192,512]{2,1,0:T(8,128)(2,1)S(1)}, bf16[3,192,512]{2,1,0:T(8,128)(2,1)S(1)}, u32[]{:S(2)}, u32[]{:S(2)}) collective-permute-start(bf16[3,192,512]{2,1,0:T(8,128)(2,1)S(1)} %broadcast_select_fusion.2.refs_4_), channel_id=1, source_target_pairs={{0,192},{64,0},{128,64},{192,128},{1,193},{65,1},{129,65},{193,129... | collective-permute-start | bytes 1769480 | tf_op jit(solution)/shard_map/ppermute | solution.py:230
  27.7 2.9 %collective-permute-done = bf16[160,512]{1,0:T(8,128)(2,1)} collective-permute-done((bf16[160,512]{1,0:T(8,128)(2,1)S(1)}, bf16[160,512]{1,0:T(8,128)(2,1)}, u32[]{:S(2)}, u32[]{:S(2)}) %collective-permute-start) | collective-permute-done | bytes 163872 | tf_op jit(solution)/shard_map/ppermute | solution.py:230
  30.6 0.9 constant_dynamic-update-slice_fusion.2
  31.5 4.8 %collective-permute-done.1 = bf16[160,512]{1,0:T(8,128)(2,1)S(1)} collective-permute-done((bf16[160,512]{1,0:T(8,128)(2,1)S(1)}, bf16[160,512]{1,0:T(8,128)(2,1)S(1)}, u32[]{:S(2)}, u32[]{:S(2)}) %collective-permute-start.1) | collective-permute-done | bytes 163872 | tf_op jit(solution)/shard_map/ppermute | solution.py:230
  36.4 2.8 %collective-permute-start.7 = (bf16[640,512]{1,0:T(8,128)(2,1)S(1)}, bf16[640,512]{1,0:T(8,128)(2,1)S(1)}, u32[]{:S(2)}, u32[]{:S(2)}) collective-permute-start(bf16[640,512]{1,0:T(8,128)(2,1)S(1)} %constant_dynamic-update-slice_fusion.refs_0_), channel_id=1, source_target_pairs={{0,6},{2,0},{4,2},{6,4},{1,7},{3,1},{5,3},{7,5},{8,14},{10,8},{12,... | collective-permute-start | bytes 1966088 | tf_op jit(solution)/shard_map/ppermute | solution.py:230
  39.3 2.6 %collective-permute-start.9 = (bf16[3,192,512]{2,1,0:T(8,128)(2,1)S(1)}, bf16[3,192,512]{2,1,0:T(8,128)(2,1)S(1)}, u32[]{:S(2)}, u32[]{:S(2)}) collective-permute-start(bf16[3,192,512]{2,1,0:T(8,128)(2,1)S(1)} %broadcast_select_fusion.1), channel_id=1, source_target_pairs={{0,64},{64,128},{128,192},{192,0},{32,224},{96,32},{160,96},{224,1... | collective-permute-start | bytes 1769480 | tf_op jit(solution)/shard_map/ppermute | solution.py:236
  41.8 4.9 %collective-permute-done.7.refs_3_ = bf16[640,512]{1,0:T(8,128)(2,1)S(1)} collective-permute-done((bf16[640,512]{1,0:T(8,128)(2,1)S(1)}, bf16[640,512]{1,0:T(8,128)(2,1)S(1)}, u32[]{:S(2)}, u32[]{:S(2)}) %collective-permute-start.7) | collective-permute-done | bytes 655392 | tf_op jit(solution)/shard_map/ppermute | solution.py:230
  46.7 5.6 %collective-permute-done.6.refs_1_ = bf16[640,512]{1,0:T(8,128)(2,1)S(1)} collective-permute-done((bf16[640,512]{1,0:T(8,128)(2,1)S(1)}, bf16[640,512]{1,0:T(8,128)(2,1)S(1)}, u32[]{:S(2)}, u32[]{:S(2)}) %collective-permute-start.6) | collective-permute-done | bytes 655392 | tf_op jit(solution)/shard_map/ppermute | solution.py:230
  53.6 1.0 collective-permute-done.10.refs_8_
  54.6 1.9 %collective-permute-done.11.refs_9_ = bf16[3,192,512]{2,1,0:T(8,128)(2,1)S(1)} collective-permute-done((bf16[3,192,512]{2,1,0:T(8,128)(2,1)}, bf16[3,192,512]{2,1,0:T(8,128)(2,1)S(1)}, u32[]{:S(2)}, u32[]{:S(2)}) %collective-permute-start.11) | collective-permute-done | bytes 589856 | tf_op jit(solution)/shard_map/ppermute | solution.py:241
  56.5 5.4 %collective-permute-done.8.refs_2_ = bf16[640,512]{1,0:T(8,128)(2,1)S(1)} collective-permute-done((bf16[640,512]{1,0:T(8,128)(2,1)S(1)}, bf16[640,512]{1,0:T(8,128)(2,1)S(1)}, u32[]{:S(2)}, u32[]{:S(2)}) %collective-permute-start.8) | collective-permute-done | bytes 655392 | tf_op jit(solution)/shard_map/ppermute | solution.py:237
  61.9 0.8 copy-done.4
  62.8 4.4 %shard_map.85 = (bf16[320,768]{1,0:T(8,128)(2,1)S(1)}, bf16[768,2048]{1,0:T(8,128)(2,1)}) custom-call(s32[5]{0:T(128)S(1)} %stack.23.place, bf16[640,512]{1,0:T(8,128)(2,1)S(1)} %constant_dynamic-update-slice_fusion.refs_0_, bf16[640,512]{1,0:T(8,128)(2,1)} %copy-done.2, bf16[640,512]{1,0:T(8,128)(2,1)} %copy-done.4, bf16[640,512]{1,0:T(8,128)(2,1)} %copy-done, ...), custom_call_target="tpu_custom_call" | custom-call | tf_op jit(solution)/shard_map/pallas_call | solution.py:33
  67.5 3.8 %shard_map.86 = (bf16[320,384]{1,0:T(8,128)(2,1)S(1)}, bf16[384,2048]{1,0:T(8,128)(2,1)}) custom-call(s32[5]{0:T(128)S(1)} %stack.23.place, bf16[640,512]{1,0:T(8,128)(2,1)S(1)} %constant_dynamic-update-slice_fusion.refs_0_, bf16[640,512]{1,0:T(8,128)(2,1)} %copy-done.2, bf16[640,512]{1,0:T(8,128)(2,1)} %copy-done.4, bf16[640,512]{1,0:T(8,128)(2,1)} %copy-done, ...), custom_call_target="tpu_custom_call" | custom-call | tf_op jit(solution)/shard_map/pallas_call | solution.py:33
  71.3 1.5 %collective-permute-start.15 = (bf16[320,384]{1,0:T(8,128)(2,1)S(1)}, bf16[320,384]{1,0:T(8,128)(2,1)S(1)}, u32[]{:S(2)}, u32[]{:S(2)}) collective-permute-start(bf16[320,384]{1,0:T(8,128)(2,1)S(1)} %get-tuple-element.61.down), channel_id=1, source_target_pairs={{0,1},{1,0},{2,3},{3,2},{4,5},{5,4},{6,7},{7,6},{8,9},{9,8},{10,11... | collective-permute-start | bytes 737288 | tf_op jit(solution)/shard_map/ppermute | solution.py:241
  72.8 11.2 %collective-permute-done.15.down_far = bf16[320,384]{1,0:T(8,128)(2,1)S(1)} collective-permute-done((bf16[320,384]{1,0:T(8,128)(2,1)S(1)}, bf16[320,384]{1,0:T(8,128)(2,1)S(1)}, u32[]{:S(2)}, u32[]{:S(2)}) %collective-permute-start.15) | collective-permute-done | bytes 245792 | tf_op jit(solution)/shard_map/ppermute | solution.py:241
  84.0 4.6 %shard_map.87 = (f32[656,512]{1,0:T(8,128)S(1)}, bf16[656,512]{1,0:T(8,128)(2,1)S(1)}, bf16[656,512]{1,0:T(8,128)(2,1)S(1)}, bf16[656,512]{1,0:T(8,128)(2,1)S(1)}, bf16[320,1152]{1,0:T(8,128)(2,1)S(1)}) custom-call(s32[5]{0:T(128)S(1)} %stack.23.place, bf16[320,768]{1,0:T(8,128)(2,1)S(1)} %get-tuple-element.60.pair, ...), custom_call_target="tpu_custom_call" | custom-call | tf_op jit(solution)/shard_map/pallas_call | solution.py:33
  88.6 1.4 collective-permute-start.16
  90.0 4.6 %shard_map.88 = (f32[3,192,512]{2,1,0:T(8,128)}, f32[3,192,512]{2,1,0:T(8,128)}, f32[3,192,512]{2,1,0:T(8,128)}, f32[3,192,512]{2,1,0:T(8,128)}, bf16[3,192,512]...) custom-call(s32[5]{0:T(128)S(1)} %stack.23.place, ...), custom_call_target="tpu_custom_call" | custom-call | tf_op jit(solution)/shard_map/pallas_call | solution.py:33
  95.6 2.9 %collective-permute-done.16 = bf16[656,512]{1,0:T(8,128)(2,1)S(1)} collective-permute-done((bf16[656,512]{1,0:T(8,128)(2,1)S(1)}, bf16[656,512]{1,0:T(8,128)(2,1)S(1)}, u32[]{:S(2)}, u32[]{:S(2)}) %collective-permute-start.16) | collective-permute-done | bytes 671776 | tf_op jit(solution)/shard_map/ppermute | solution.py:237
  99.1 0.7 copy-done.7
  100.0 2.6 %collective-permute-start.21 = (bf16[3,192,512]{2,1,0:T(8,128)(2,1)S(1)}, bf16[3,192,512]{2,1,0:T(8,128)(2,1)S(1)}, u32[]{:S(2)}, u32[]{:S(2)}) collective-permute-start(bf16[3,192,512]{2,1,0:T(8,128)(2,1)S(1)} %add_convert_fusion.1), channel_id=1, source_target_pairs={{0,64},{64,128},{128,192},{192,0},{32,224},{96,32},{160,96},{224,1... | collective-permute-start | bytes 1769480 | tf_op jit(solution)/shard_map/ppermute | solution.py:236
  102.6 2.4 %collective-permute-start.26 = (bf16[656,512]{1,0:T(8,128)(2,1)S(1)}, bf16[656,512]{1,0:T(8,128)(2,1)S(1)}, u32[]{:S(2)}, u32[]{:S(2)}) collective-permute-start(bf16[656,512]{1,0:T(8,128)(2,1)S(1)} %get-tuple-element.82), channel_id=1, source_target_pairs={{0,6},{2,0},{4,2},{6,4},{1,7},{3,1},{5,3},{7,5},{8,14},{10,8},{12,... | collective-permute-start | bytes 2015240 | tf_op jit(solution)/shard_map/ppermute | solution.py:230
  104.9 4.5 %collective-permute-done.21 = bf16[3,192,512]{2,1,0:T(8,128)(2,1)S(1)} collective-permute-done((bf16[3,192,512]{2,1,0:T(8,128)(2,1)S(1)}, bf16[3,192,512]{2,1,0:T(8,128)(2,1)S(1)}, u32[]{:S(2)}, u32[]{:S(2)}) %collective-permute-start.21) | collective-permute-done | bytes 589856 | tf_op jit(solution)/shard_map/ppermute | solution.py:236
  109.9 3.7 %collective-permute-start.22 = (bf16[3,192,512]{2,1,0:T(8,128)(2,1)S(1)}, bf16[3,192,512]{2,1,0:T(8,128)(2,1)S(1)}, u32[]{:S(2)}, u32[]{:S(2)}) collective-permute-start(bf16[3,192,512]{2,1,0:T(8,128)(2,1)S(1)} %get-tuple-element.98), channel_id=1, source_target_pairs={{0,192},{64,0},{128,64},{192,128},{1,193},{65,1},{129,65},{193,129... | collective-permute-start | bytes 1769480 | tf_op jit(solution)/shard_map/ppermute | solution.py:230
  113.7 5.6 %collective-permute-done.26.one = bf16[656,512]{1,0:T(8,128)(2,1)S(1)} collective-permute-done((bf16[656,512]{1,0:T(8,128)(2,1)S(1)}, bf16[656,512]{1,0:T(8,128)(2,1)S(1)}, u32[]{:S(2)}, u32[]{:S(2)}) %collective-permute-start.26) | collective-permute-done | bytes 671776 | tf_op jit(solution)/shard_map/ppermute | solution.py:230
  119.2 3.7 %collective-permute-done.27.three = bf16[656,512]{1,0:T(8,128)(2,1)S(1)} collective-permute-done((bf16[656,512]{1,0:T(8,128)(2,1)S(1)}, bf16[656,512]{1,0:T(8,128)(2,1)S(1)}, u32[]{:S(2)}, u32[]{:S(2)}) %collective-permute-start.27) | collective-permute-done | bytes 671776 | tf_op jit(solution)/shard_map/ppermute | solution.py:230
  122.9 0.8 shard_map.89
  123.7 1.8 %collective-permute-start.28 = (bf16[176,512]{1,0:T(8,128)(2,1)S(1)}, bf16[176,512]{1,0:T(8,128)(2,1)S(1)}, u32[]{:S(2)}, u32[]{:S(2)}) collective-permute-start(bf16[176,512]{1,0:T(8,128)(2,1)S(1)} %get-tuple-element.85), channel_id=1, source_target_pairs={{0,24},{8,0},{16,8},{24,16},{1,25},{9,1},{17,9},{25,17},{2,26},{10... | collective-permute-start | bytes 540680 | tf_op jit(solution)/shard_map/ppermute | solution.py:230
  125.4 2.2 %collective-permute-start.30 = (bf16[176,512]{1,0:T(8,128)(2,1)S(1)}, bf16[176,512]{1,0:T(8,128)(2,1)S(1)}, u32[]{:S(2)}, u32[]{:S(2)}) collective-permute-start(bf16[176,512]{1,0:T(8,128)(2,1)S(1)} %get-tuple-element.87), channel_id=1, source_target_pairs={{0,8},{8,16},{16,24},{24,0},{1,9},{9,17},{17,25},{25,1},{2,10},{10... | collective-permute-start | bytes 540680 | tf_op jit(solution)/shard_map/ppermute | solution.py:230
  128.0 6.7 %collective-permute-start.25 = (bf16[288,512]{1,0:T(8,128)(2,1)S(1)}, bf16[288,512]{1,0:T(8,128)(2,1)S(1)}, u32[]{:S(2)}, u32[]{:S(2)}) collective-permute-start(bf16[288,512]{1,0:T(8,128)(2,1)S(1)} %get-tuple-element.96), channel_id=1, source_target_pairs={{0,0},{1,32},{32,1},{33,33},{2,2},{3,34},{34,3},{35,35},{4,4},{5,3... | collective-permute-start | bytes 884744 | tf_op jit(solution)/shard_map/ppermute | solution.py:245
  134.7 1.9 %collective-permute-start.24 = (bf16[288,512]{1,0:T(8,128)(2,1)S(1)}, bf16[288,512]{1,0:T(8,128)(2,1)S(1)}, u32[]{:S(2)}, u32[]{:S(2)}) collective-permute-start(bf16[288,512]{1,0:T(8,128)(2,1)S(1)} %get-tuple-element.97), channel_id=1, source_target_pairs={{0,0},{1,32},{32,1},{33,33},{2,2},{3,34},{34,3},{35,35},{4,4},{5,3... | collective-permute-start | bytes 884744 | tf_op jit(solution)/shard_map/ppermute | solution.py:245
  136.7 1.2 collective-permute-done.29.refs_2_
  137.9 3.6 %collective-permute-done.30.refs_3_ = bf16[176,512]{1,0:T(8,128)(2,1)S(1)} collective-permute-done((bf16[176,512]{1,0:T(8,128)(2,1)S(1)}, bf16[176,512]{1,0:T(8,128)(2,1)S(1)}, u32[]{:S(2)}, u32[]{:S(2)}) %collective-permute-start.30) | collective-permute-done | bytes 180256 | tf_op jit(solution)/shard_map/ppermute | solution.py:230
  141.5 1.7 %shard_map.90 = (bf16[128,512]{1,0:T(8,128)(2,1)}, bf16[128,512]{1,0:T(8,128)(2,1)}, f32[8,128]{1,0:T(8,128)S(1)}) custom-call(s32[5]{0:T(128)S(1)} %stack.23.place, f32[4,128]{1,0:T(4,128)S(1)} %pad_maximum_fusion.2.small, bf16[320,128]{1,0:T(8,128)(2,1)S(1)} %get-tuple-element.80.placing, bf16[176,512]{1,0:T(8,128)(2,1)S(1)} %get-tuple-element.84.refs_0_, ...), custom_call_target="tpu_custom_call" | custom-call | tf_op jit(solution)/shard_map/pallas_call | solution.py:33
  143.2 0.6 slice_bitcast_fusion.2
  143.8 1.1 collective-permute-done.25
  144.9 3.2 %collective-permute-done.24 = bf16[288,512]{1,0:T(8,128)(2,1)S(1)} collective-permute-done((bf16[288,512]{1,0:T(8,128)(2,1)S(1)}, bf16[288,512]{1,0:T(8,128)(2,1)S(1)}, u32[]{:S(2)}, u32[]{:S(2)}) %collective-permute-start.24) | collective-permute-done | bytes 294944 | tf_op jit(solution)/shard_map/ppermute | solution.py:245
  148.1 1.2 convert.2
  (62 shorter events, 4.6 us)
Async XLA Ops:
  0.6 24.4 %copy-start.10 = (bf16[1,3,192,512]{3,2,1,0:T(8,128)(2,1)S(1)}, bf16[1,3,192,512]{3,2,1,0:T(8,128)(2,1)}, u32[]{:S(2)}) copy-start(bf16[1,3,192,512]{3,2,1,0:T(8,128)(2,1)} %param.8) | copy-start | bytes 1769476
  4.2 20.8 %collective-permute-start.3 = (bf16[3,192,512]{2,1,0:T(8,128)(2,1)}, bf16[3,192,512]{2,1,0:T(8,128)(2,1)S(1)}, u32[]{:S(2)}, u32[]{:S(2)}) collective-permute-start(bf16[3,192,512]{2,1,0:T(8,128)(2,1)} %bitcast.20), channel_id=1, source_target_pairs={{1,32},{32,1},{3,34},{34,3},{5,36},{36,5},{7,38},{38,7},{9,40},{40... | collective-permute-start | bytes 1769480 | tf_op jit(solution)/shard_map/ppermute | solution.py:270
  9.1 21.5 %collective-permute-start = (bf16[160,512]{1,0:T(8,128)(2,1)S(1)}, bf16[160,512]{1,0:T(8,128)(2,1)}, u32[]{:S(2)}, u32[]{:S(2)}) collective-permute-start(bf16[160,512]{1,0:T(8,128)(2,1)S(1)} %get-tuple-element.51), channel_id=1, source_target_pairs={{0,8},{8,16},{16,24},{24,0},{1,9},{9,17},{17,25},{25,1},{2,10},{10... | collective-permute-start | bytes 491528 | tf_op jit(solution)/shard_map/ppermute | solution.py:230
  12.2 24.1 %collective-permute-start.1 = (bf16[160,512]{1,0:T(8,128)(2,1)S(1)}, bf16[160,512]{1,0:T(8,128)(2,1)S(1)}, u32[]{:S(2)}, u32[]{:S(2)}) collective-permute-start(bf16[160,512]{1,0:T(8,128)(2,1)S(1)} %get-tuple-element.52), channel_id=1, source_target_pairs={{0,16},{8,24},{16,0},{24,8},{1,17},{9,25},{17,1},{25,9},{2,18},{10... | collective-permute-start | bytes 491528 | tf_op jit(solution)/shard_map/ppermute | solution.py:230
  16.4 20.0 %collective-permute-start.2 = (bf16[160,512]{1,0:T(8,128)(2,1)S(1)}, bf16[160,512]{1,0:T(8,128)(2,1)S(1)}, u32[]{:S(2)}, u32[]{:S(2)}) collective-permute-start(bf16[160,512]{1,0:T(8,128)(2,1)S(1)} %get-tuple-element.53), channel_id=1, source_target_pairs={{0,24},{8,0},{16,8},{24,16},{1,25},{9,1},{17,9},{25,17},{2,26},{10... | collective-permute-start | bytes 491528 | tf_op jit(solution)/shard_map/ppermute | solution.py:230
  25.1 14.1 %collective-permute-start.5 = (bf16[3,192,512]{2,1,0:T(8,128)(2,1)S(1)}, bf16[3,192,512]{2,1,0:T(8,128)(2,1)S(1)}, u32[]{:S(2)}, u32[]{:S(2)}) collective-permute-start(bf16[3,192,512]{2,1,0:T(8,128)(2,1)S(1)} %broadcast_select_fusion.2.refs_4_), channel_id=1, source_target_pairs={{0,192},{64,0},{128,64},{192,128},{1,193},{65,1},{129,65},{193,129... | collective-permute-start | bytes 1769480 | tf_op jit(solution)/shard_map/ppermute | solution.py:230
  27.6 11.6 %collective-permute-start.4 = (bf16[3,192,512]{2,1,0:T(8,128)(2,1)S(1)}, bf16[3,192,512]{2,1,0:T(8,128)(2,1)}, u32[]{:S(2)}, u32[]{:S(2)}) collective-permute-start(bf16[3,192,512]{2,1,0:T(8,128)(2,1)S(1)} %broadcast_select_fusion.2.refs_4_), channel_id=1, source_target_pairs={{0,64},{64,128},{128,192},{192,0},{1,65},{65,129},{129,193},{193,1... | collective-permute-start | bytes 1769480 | tf_op jit(solution)/shard_map/ppermute | solution.py:230
  36.4 10.3 %collective-permute-start.7 = (bf16[640,512]{1,0:T(8,128)(2,1)S(1)}, bf16[640,512]{1,0:T(8,128)(2,1)S(1)}, u32[]{:S(2)}, u32[]{:S(2)}) collective-permute-start(bf16[640,512]{1,0:T(8,128)(2,1)S(1)} %constant_dynamic-update-slice_fusion.refs_0_), channel_id=1, source_target_pairs={{0,6},{2,0},{4,2},{6,4},{1,7},{3,1},{5,3},{7,5},{8,14},{10,8},{12,... | collective-permute-start | bytes 1966088 | tf_op jit(solution)/shard_map/ppermute | solution.py:230
  39.2 13.1 %collective-permute-start.6 = (bf16[640,512]{1,0:T(8,128)(2,1)S(1)}, bf16[640,512]{1,0:T(8,128)(2,1)S(1)}, u32[]{:S(2)}, u32[]{:S(2)}) collective-permute-start(bf16[640,512]{1,0:T(8,128)(2,1)S(1)} %constant_dynamic-update-slice_fusion.refs_0_), channel_id=1, source_target_pairs={{0,2},{2,4},{4,6},{6,0},{1,3},{3,5},{5,7},{7,1},{8,10},{10,12},{12... | collective-permute-start | bytes 1966088 | tf_op jit(solution)/shard_map/ppermute | solution.py:230
  39.3 13.9 %collective-permute-start.9 = (bf16[3,192,512]{2,1,0:T(8,128)(2,1)S(1)}, bf16[3,192,512]{2,1,0:T(8,128)(2,1)S(1)}, u32[]{:S(2)}, u32[]{:S(2)}) collective-permute-start(bf16[3,192,512]{2,1,0:T(8,128)(2,1)S(1)} %broadcast_select_fusion.1), channel_id=1, source_target_pairs={{0,64},{64,128},{128,192},{192,0},{32,224},{96,32},{160,96},{224,1... | collective-permute-start | bytes 1769480 | tf_op jit(solution)/shard_map/ppermute | solution.py:236
  46.7 15.2 %copy-start = (bf16[640,512]{1,0:T(8,128)(2,1)}, bf16[640,512]{1,0:T(8,128)(2,1)S(1)}, u32[]{:S(2)}) copy-start(bf16[640,512]{1,0:T(8,128)(2,1)S(1)} %collective-permute-done.7.refs_3_) | copy-start | bytes 1966084
  52.3 9.6 %copy-start.2 = (bf16[640,512]{1,0:T(8,128)(2,1)}, bf16[640,512]{1,0:T(8,128)(2,1)S(1)}, u32[]{:S(2)}) copy-start(bf16[640,512]{1,0:T(8,128)(2,1)S(1)} %collective-permute-done.6.refs_1_) | copy-start | bytes 1966084
  52.4 9.5 %collective-permute-start.8 = (bf16[640,512]{1,0:T(8,128)(2,1)S(1)}, bf16[640,512]{1,0:T(8,128)(2,1)S(1)}, u32[]{:S(2)}, u32[]{:S(2)}) collective-permute-start(bf16[640,512]{1,0:T(8,128)(2,1)S(1)} %broadcast_select_fusion), channel_id=1, source_target_pairs={{0,2},{2,4},{4,6},{6,0},{32,38},{34,32},{36,34},{38,36},{1,3},{3,5... | collective-permute-start | bytes 1966088 | tf_op jit(solution)/shard_map/ppermute | solution.py:237
  52.5 2.1 %collective-permute-start.10 = (bf16[3,192,512]{2,1,0:T(8,128)(2,1)S(1)}, bf16[3,192,512]{2,1,0:T(8,128)(2,1)S(1)}, u32[]{:S(2)}, u32[]{:S(2)}) collective-permute-start(bf16[3,192,512]{2,1,0:T(8,128)(2,1)S(1)} %broadcast_select_fusion.2.refs_4_), channel_id=1, source_target_pairs={{0,32},{32,0},{1,33},{33,1},{2,34},{34,2},{3,35},{35,3},{4,36},{36... | collective-permute-start | bytes 1769480 | tf_op jit(solution)/shard_map/ppermute | solution.py:241
  52.6 3.9 %collective-permute-start.11 = (bf16[3,192,512]{2,1,0:T(8,128)(2,1)}, bf16[3,192,512]{2,1,0:T(8,128)(2,1)S(1)}, u32[]{:S(2)}, u32[]{:S(2)}) collective-permute-start(bf16[3,192,512]{2,1,0:T(8,128)(2,1)} %collective-permute-done.4.refs_5_), channel_id=1, source_target_pairs={{0,32},{32,0},{1,33},{33,1},{2,34},{34,2},{3,35},{35,3},{4,36},{36... | collective-permute-start | bytes 1769480 | tf_op jit(solution)/shard_map/ppermute | solution.py:241
  53.1 3.4 %collective-permute-start.13 = (bf16[3,192,512]{2,1,0:T(8,128)(2,1)S(1)}, bf16[3,192,512]{2,1,0:T(8,128)(2,1)S(1)}, u32[]{:S(2)}, u32[]{:S(2)}) collective-permute-start(bf16[3,192,512]{2,1,0:T(8,128)(2,1)S(1)} %collective-permute-done.5.refs_7_), channel_id=1, source_target_pairs={{0,32},{32,0},{1,33},{33,1},{2,34},{34,2},{3,35},{35,3},{4,36},{36... | collective-permute-start | bytes 1769480 | tf_op jit(solution)/shard_map/ppermute | solution.py:241
  53.2 8.7 %collective-permute-start.12 = (bf16[3,192,512]{2,1,0:T(8,128)(2,1)S(1)}, bf16[3,192,512]{2,1,0:T(8,128)(2,1)S(1)}, u32[]{:S(2)}, u32[]{:S(2)}) collective-permute-start(bf16[3,192,512]{2,1,0:T(8,128)(2,1)S(1)} %collective-permute-done.9.refs_6_), channel_id=1, source_target_pairs={{0,32},{32,0},{1,33},{33,1},{2,34},{34,2},{3,35},{35,3},{4,36},{36... | collective-permute-start | bytes 1769480 | tf_op jit(solution)/shard_map/ppermute | solution.py:241
  61.9 0.9 copy-start.4
  67.2 16.8 %collective-permute-start.14 = (bf16[320,768]{1,0:T(8,128)(2,1)S(1)}, bf16[320,768]{1,0:T(8,128)(2,1)S(1)}, u32[]{:S(2)}, u32[]{:S(2)}) collective-permute-start(bf16[320,768]{1,0:T(8,128)(2,1)S(1)} %get-tuple-element.60.pair), channel_id=1, source_target_pairs={{0,1},{1,0},{2,3},{3,2},{4,5},{5,4},{6,7},{7,6},{8,9},{9,8},{10,11... | collective-permute-start | bytes 1474568 | tf_op jit(solution)/shard_map/ppermute | solution.py:241
  71.3 12.7 %collective-permute-start.15 = (bf16[320,384]{1,0:T(8,128)(2,1)S(1)}, bf16[320,384]{1,0:T(8,128)(2,1)S(1)}, u32[]{:S(2)}, u32[]{:S(2)}) collective-permute-start(bf16[320,384]{1,0:T(8,128)(2,1)S(1)} %get-tuple-element.61.down), channel_id=1, source_target_pairs={{0,1},{1,0},{2,3},{3,2},{4,5},{5,4},{6,7},{7,6},{8,9},{9,8},{10,11... | collective-permute-start | bytes 737288 | tf_op jit(solution)/shard_map/ppermute | solution.py:241
  84.0 6.0 %copy-start.1 = (bf16[640,512]{1,0:T(8,128)(2,1)S(1)}, bf16[640,512]{1,0:T(8,128)(2,1)}, u32[]{:S(2)}) copy-start(bf16[640,512]{1,0:T(8,128)(2,1)} %copy-done) | copy-start | bytes 1966084
  84.0 6.0 %copy-start.3 = (bf16[640,512]{1,0:T(8,128)(2,1)S(1)}, bf16[640,512]{1,0:T(8,128)(2,1)}, u32[]{:S(2)}) copy-start(bf16[640,512]{1,0:T(8,128)(2,1)} %copy-done.2) | copy-start | bytes 1966084
  84.0 6.0 %copy-start.5 = (bf16[640,512]{1,0:T(8,128)(2,1)S(1)}, bf16[640,512]{1,0:T(8,128)(2,1)}, u32[]{:S(2)}) copy-start(bf16[640,512]{1,0:T(8,128)(2,1)} %copy-done.4) | copy-start | bytes 1966084
  88.6 10.0 %collective-permute-start.16 = (bf16[656,512]{1,0:T(8,128)(2,1)S(1)}, bf16[656,512]{1,0:T(8,128)(2,1)S(1)}, u32[]{:S(2)}, u32[]{:S(2)}) collective-permute-start(bf16[656,512]{1,0:T(8,128)(2,1)S(1)} %get-tuple-element.67), channel_id=1, source_target_pairs={{0,2},{2,4},{4,6},{6,0},{32,38},{34,32},{36,34},{38,36},{1,3},{3,5... | collective-permute-start | bytes 2015240 | tf_op jit(solution)/shard_map/ppermute | solution.py:237
  94.6 4.4 %collective-permute-start.17 = (bf16[3,192,512]{2,1,0:T(8,128)(2,1)S(1)}, bf16[3,192,512]{2,1,0:T(8,128)(2,1)S(1)}, u32[]{:S(2)}, u32[]{:S(2)}) collective-permute-start(bf16[3,192,512]{2,1,0:T(8,128)(2,1)S(1)} %get-tuple-element.69), channel_id=1, source_target_pairs={{0,32},{32,0},{1,33},{33,1},{2,34},{34,2},{3,35},{35,3},{4,36},{36... | collective-permute-start | bytes 1769480 | tf_op jit(solution)/shard_map/ppermute | solution.py:241
  94.6 4.4 %collective-permute-start.18 = (bf16[3,192,512]{2,1,0:T(8,128)(2,1)S(1)}, bf16[3,192,512]{2,1,0:T(8,128)(2,1)S(1)}, u32[]{:S(2)}, u32[]{:S(2)}) collective-permute-start(bf16[3,192,512]{2,1,0:T(8,128)(2,1)S(1)} %get-tuple-element.70), channel_id=1, source_target_pairs={{0,32},{32,0},{1,33},{33,1},{2,34},{34,2},{3,35},{35,3},{4,36},{36... | collective-permute-start | bytes 1769480 | tf_op jit(solution)/shard_map/ppermute | solution.py:241
  95.1 3.9 %collective-permute-start.19 = (bf16[3,192,512]{2,1,0:T(8,128)(2,1)S(1)}, bf16[3,192,512]{2,1,0:T(8,128)(2,1)S(1)}, u32[]{:S(2)}, u32[]{:S(2)}) collective-permute-start(bf16[3,192,512]{2,1,0:T(8,128)(2,1)S(1)} %get-tuple-element.71), channel_id=1, source_target_pairs={{0,32},{32,0},{1,33},{33,1},{2,34},{34,2},{3,35},{35,3},{4,36},{36... | collective-permute-start | bytes 1769480 | tf_op jit(solution)/shard_map/ppermute | solution.py:241
  95.1 4.0 %collective-permute-start.20 = (bf16[3,192,512]{2,1,0:T(8,128)(2,1)S(1)}, bf16[3,192,512]{2,1,0:T(8,128)(2,1)S(1)}, u32[]{:S(2)}, u32[]{:S(2)}) collective-permute-start(bf16[3,192,512]{2,1,0:T(8,128)(2,1)S(1)} %get-tuple-element.72), channel_id=1, source_target_pairs={{0,32},{32,0},{1,33},{33,1},{2,34},{34,2},{3,35},{35,3},{4,36},{36... | collective-permute-start | bytes 1769480 | tf_op jit(solution)/shard_map/ppermute | solution.py:241
  98.6 1.3 copy-start.7
  99.8 9.6 %copy-start.8 = (f32[3,192,512]{2,1,0:T(8,128)S(1)}, f32[3,192,512]{2,1,0:T(8,128)}, u32[]{:S(2)}) copy-start(f32[3,192,512]{2,1,0:T(8,128)} %get-tuple-element.74) | copy-start | bytes 3538948
  99.8 9.6 %copy-start.9 = (f32[3,192,512]{2,1,0:T(8,128)S(1)}, f32[3,192,512]{2,1,0:T(8,128)}, u32[]{:S(2)}) copy-start(f32[3,192,512]{2,1,0:T(8,128)} %get-tuple-element.78) | copy-start | bytes 3538948
  100.0 9.4 %collective-permute-start.21 = (bf16[3,192,512]{2,1,0:T(8,128)(2,1)S(1)}, bf16[3,192,512]{2,1,0:T(8,128)(2,1)S(1)}, u32[]{:S(2)}, u32[]{:S(2)}) collective-permute-start(bf16[3,192,512]{2,1,0:T(8,128)(2,1)S(1)} %add_convert_fusion.1), channel_id=1, source_target_pairs={{0,64},{64,128},{128,192},{192,0},{32,224},{96,32},{160,96},{224,1... | collective-permute-start | bytes 1769480 | tf_op jit(solution)/shard_map/ppermute | solution.py:236
  102.6 16.6 %collective-permute-start.26 = (bf16[656,512]{1,0:T(8,128)(2,1)S(1)}, bf16[656,512]{1,0:T(8,128)(2,1)S(1)}, u32[]{:S(2)}, u32[]{:S(2)}) collective-permute-start(bf16[656,512]{1,0:T(8,128)(2,1)S(1)} %get-tuple-element.82), channel_id=1, source_target_pairs={{0,6},{2,0},{4,2},{6,4},{1,7},{3,1},{5,3},{7,5},{8,14},{10,8},{12,... | collective-permute-start | bytes 2015240 | tf_op jit(solution)/shard_map/ppermute | solution.py:230
  104.9 18.0 %collective-permute-start.27 = (bf16[656,512]{1,0:T(8,128)(2,1)S(1)}, bf16[656,512]{1,0:T(8,128)(2,1)S(1)}, u32[]{:S(2)}, u32[]{:S(2)}) collective-permute-start(bf16[656,512]{1,0:T(8,128)(2,1)S(1)} %get-tuple-element.83), channel_id=1, source_target_pairs={{0,2},{2,4},{4,6},{6,0},{1,3},{3,5},{5,7},{7,1},{8,10},{10,12},{12... | collective-permute-start | bytes 2015240 | tf_op jit(solution)/shard_map/ppermute | solution.py:230
  109.9 17.7 %collective-permute-start.22 = (bf16[3,192,512]{2,1,0:T(8,128)(2,1)S(1)}, bf16[3,192,512]{2,1,0:T(8,128)(2,1)S(1)}, u32[]{:S(2)}, u32[]{:S(2)}) collective-permute-start(bf16[3,192,512]{2,1,0:T(8,128)(2,1)S(1)} %get-tuple-element.98), channel_id=1, source_target_pairs={{0,192},{64,0},{128,64},{192,128},{1,193},{65,1},{129,65},{193,129... | collective-permute-start | bytes 1769480 | tf_op jit(solution)/shard_map/ppermute | solution.py:230
  113.6 14.0 %collective-permute-start.23 = (bf16[3,192,512]{2,1,0:T(8,128)(2,1)S(1)}, bf16[3,192,512]{2,1,0:T(8,128)(2,1)S(1)}, u32[]{:S(2)}, u32[]{:S(2)}) collective-permute-start(bf16[3,192,512]{2,1,0:T(8,128)(2,1)S(1)} %get-tuple-element.99), channel_id=1, source_target_pairs={{0,64},{64,128},{128,192},{192,0},{1,65},{65,129},{129,193},{193,1... | collective-permute-start | bytes 1769480 | tf_op jit(solution)/shard_map/ppermute | solution.py:230
  122.9 4.7 %copy-start.6 = (f32[3,192,512]{2,1,0:T(8,128)S(1)}, f32[3,192,512]{2,1,0:T(8,128)}, u32[]{:S(2)}) copy-start(f32[3,192,512]{2,1,0:T(8,128)} %get-tuple-element.65) | copy-start | bytes 3538948
  123.7 13.0 %collective-permute-start.28 = (bf16[176,512]{1,0:T(8,128)(2,1)S(1)}, bf16[176,512]{1,0:T(8,128)(2,1)S(1)}, u32[]{:S(2)}, u32[]{:S(2)}) collective-permute-start(bf16[176,512]{1,0:T(8,128)(2,1)S(1)} %get-tuple-element.85), channel_id=1, source_target_pairs={{0,24},{8,0},{16,8},{24,16},{1,25},{9,1},{17,9},{25,17},{2,26},{10... | collective-permute-start | bytes 540680 | tf_op jit(solution)/shard_map/ppermute | solution.py:230
  125.4 12.5 %collective-permute-start.29 = (bf16[176,512]{1,0:T(8,128)(2,1)S(1)}, bf16[176,512]{1,0:T(8,128)(2,1)S(1)}, u32[]{:S(2)}, u32[]{:S(2)}) collective-permute-start(bf16[176,512]{1,0:T(8,128)(2,1)S(1)} %get-tuple-element.86), channel_id=1, source_target_pairs={{0,16},{8,24},{16,0},{24,8},{1,17},{9,25},{17,1},{25,9},{2,18},{10... | collective-permute-start | bytes 540680 | tf_op jit(solution)/shard_map/ppermute | solution.py:230
  125.4 16.1 %collective-permute-start.30 = (bf16[176,512]{1,0:T(8,128)(2,1)S(1)}, bf16[176,512]{1,0:T(8,128)(2,1)S(1)}, u32[]{:S(2)}, u32[]{:S(2)}) collective-permute-start(bf16[176,512]{1,0:T(8,128)(2,1)S(1)} %get-tuple-element.87), channel_id=1, source_target_pairs={{0,8},{8,16},{16,24},{24,0},{1,9},{9,17},{17,25},{25,1},{2,10},{10... | collective-permute-start | bytes 540680 | tf_op jit(solution)/shard_map/ppermute | solution.py:230
  128.0 16.9 %collective-permute-start.25 = (bf16[288,512]{1,0:T(8,128)(2,1)S(1)}, bf16[288,512]{1,0:T(8,128)(2,1)S(1)}, u32[]{:S(2)}, u32[]{:S(2)}) collective-permute-start(bf16[288,512]{1,0:T(8,128)(2,1)S(1)} %get-tuple-element.96), channel_id=1, source_target_pairs={{0,0},{1,32},{32,1},{33,33},{2,2},{3,34},{34,3},{35,35},{4,4},{5,3... | collective-permute-start | bytes 884744 | tf_op jit(solution)/shard_map/ppermute | solution.py:245
  134.7 13.3 %collective-permute-start.24 = (bf16[288,512]{1,0:T(8,128)(2,1)S(1)}, bf16[288,512]{1,0:T(8,128)(2,1)S(1)}, u32[]{:S(2)}, u32[]{:S(2)}) collective-permute-start(bf16[288,512]{1,0:T(8,128)(2,1)S(1)} %get-tuple-element.97), channel_id=1, source_target_pairs={{0,0},{1,32},{32,1},{33,33},{2,2},{3,34},{34,3},{35,35},{4,4},{5,3... | collective-permute-start | bytes 884744 | tf_op jit(solution)/shard_map/ppermute | solution.py:245

commit v9 on v8

--- a/solution.py
+++ b/solution.py
@@ -99,16 +99,27 @@
         target[k * CAP : (k + 1) * CAP, :] = source[first : first + CAP, :]
 
 
-def project_kernel(names, second, place, *refs):
-    rows, own, other = refs[0:4], refs[4:8], refs[8:12]
-    out, joined, wide, sems = refs[12:16]
+def early_kernel(place, *refs):
+    rows, own, other = refs[0:3], refs[3:7], refs[7:11]
+    pair, down, pair_weights, down_weights, wide, pair_sems, down_sems = refs[11:18]
     width = rows[0].shape[1]
-    copies = fetch(own, other, joined, sems, names, place)
-    for j in range(4):
-        take_rows(wide.at[:, pl.ds(j * width, width)], rows[j], second)
-    for copy in copies:
-        copy.wait()
-    out[...] = nt(wide[...], joined[...]).astype(BF16)
+    copies = fetch(own, other, pair_weights, pair_sems, (0, 1), place)
+    more = fetch(own, other, down_weights, down_sems, (2,), place)
+    for second in range(2):
+        for n in range(3):
+            take_rows(wide.at[second, :, pl.ds(n * width, width)], rows[n], second)
+    for second, out, weights in ((0, pair, pair_weights), (1, down, down_weights)):
+        for copy in more if second else copies:
+            copy.wait()
+        low = nt(wide[second, :, 0 : 2 * width], weights[:, 0 : 2 * width])
+        out[...] = low + nt(wide[second, :, 2 * width :], weights[:, 3 * width :])
+
+
+def late_kernel(second, place, early, rows, weights, out, chosen):
+    width = rows.shape[1]
+    take_rows(chosen, rows, second)
+    total = early[...] + nt(chosen[...], weights[:, 2 * width : 3 * width])
+    out[...] = total.astype(BF16)
 
 
 def pieces(values):
@@ -127,9 +138,28 @@
     return total
 
 
-def share_kernel(place, pair, pair_far, down, down_far, pair_weights, down_weights, *refs):
-    outs, hidden = refs[0:4], refs[4]
-    width, step = down.shape[1], outs[0].shape[1]
+def store_shares(outs, order, hidden, marks, pair_weights, down_weights):
+    width, step, unit = hidden.shape[1] // 3, outs[0].shape[1], 2 * CAP
+    for out, j in zip(outs, order):
+        columns = slice(j * step, (j + 1) * step)
+        first = nn(hidden[:, 2 * width :], down_weights[:, columns]).astype(out.dtype)
+        second = nn(hidden[:, 0 : 2 * width], pair_weights[:, columns]).astype(out.dtype)
+        for k in range(4):
+            start, rows = k * unit, slice(k * CAP, (k + 1) * CAP)
+            out[start : start + CAP, :] = first[rows, :]
+            out[start + CAP : start + 2 * CAP, :] = second[rows, :]
+        out[4 * unit :, :] = jnp.zeros((TILE, step), out.dtype)
+        out[4 * unit :, 0:128] = marks.astype(out.dtype)
+
+
+def rest_kernel(place, hidden, marks, pair_weights, down_weights, *outs):
+    store_shares(outs, (1, 3, 0), hidden, marks[...], pair_weights, down_weights)
+
+
+def share_kernel(
+    place, pair, pair_far, down, down_far, pair_weights, down_weights, across, hidden, mark_rows
+):
+    width = down.shape[1]
 
     def both(near, far, n):
         columns = slice(n * width, (n + 1) * width)
@@ -151,18 +181,8 @@
             jnp.where(same, share[k * CAP : (k + 1) * CAP, :], 0.0), axis=0, keepdims=True
         )
         marks += marked_rows(row, 3 * k)
-    unit = 2 * CAP
-    for j in (2, 1, 3, 0):
-        kind = outs[j].dtype
-        columns = slice(j * step, (j + 1) * step)
-        out = nn(hidden[:, 2 * width :], down_weights[:, columns])
-        back = nn(hidden[:, 0 : 2 * width], pair_weights[:, columns])
-        for k in range(4):
-            start, rows = k * unit, slice(k * CAP, (k + 1) * CAP)
-            outs[j][start : start + CAP, :] = out[rows, :].astype(kind)
-            outs[j][start + CAP : start + 2 * CAP, :] = back[rows, :].astype(kind)
-        outs[j][4 * unit :, :] = jnp.zeros((TILE, step), kind)
-        outs[j][4 * unit :, 0:128] = marks.astype(kind)
+    mark_rows[...] = marks
+    store_shares((across,), (2,), hidden, marks, pair_weights, down_weights)
 
 
 def total_kernel(place, own, one, three, *outs):
@@ -280,20 +300,32 @@
     other = [swap(block, "core") for block in own]
     blocks += [near, relay(jnp.where(first, near, back), "y"), back]
 
-    def project(names, second):
-        tall = len(names) * hidden
+    early_pair, early_down, pair_weights, down_weights = call(
+        early_kernel,
+        place,
+        [blocks[0], blocks[1], blocks[3]] + own + other,
+        [((slots, 2 * hidden), F32), ((slots, hidden), F32)]
+        + [((2 * hidden, 4 * width), BF16), ((hidden, 4 * width), BF16)],
+        [
+            pltpu.VMEM((2, slots, 3 * width), BF16),
+            pltpu.SemaphoreType.DMA((4, 2, 2)),
+            pltpu.SemaphoreType.DMA((4, 1, 2)),
+        ],
+        [vmem] * 3 + [hbm] * 8,
+    )
+
+    def late(second, early, weights):
         return call(
-            functools.partial(project_kernel, names, second),
+            functools.partial(late_kernel, second),
             place,
-            blocks + own + other,
-            [((slots, tall), BF16), ((tall, 4 * width), BF16)],
-            [pltpu.VMEM((slots, 4 * width), BF16), pltpu.SemaphoreType.DMA((4, 2, 2))],
-            [vmem] * 4 + [hbm] * 8,
-        )
-
-    pair, pair_weights = project((0, 1), 0)
+            [early, blocks[2], weights],
+            [(early.shape, BF16)],
+            [pltpu.VMEM((slots, width), BF16)],
+        )[0]
+
+    pair = late(0, early_pair, pair_weights)
     pair_far = swap(pair, "zl")
-    down, down_weights = project((2,), 1)
+    down = late(1, early_down, down_weights)
     down_far = swap(down, "zl")
 
     def halfway(passed, near, back):
@@ -302,25 +334,30 @@
         return near, (back + jnp.where(first, passed, 0.0)).astype(BF16)
 
     unit = 2 * CAP + TILE
-    shares = call(
+    tall = (8 * CAP + TILE, width)
+    across, grads, marks = call(
         share_kernel,
         place,
         [pair, pair_far, down, down_far, pair_weights, down_weights],
-        [((8 * CAP + TILE, width), F32)]
-        + [((8 * CAP + TILE, width), BF16)] * 3
-        + [((slots, 3 * hidden), BF16)],
-    )
-    passed = relay(shares[2], "y")
+        [(tall, BF16), ((slots, 3 * hidden), BF16), ((TILE, 128), F32)],
+    )
+    passed = relay(across, "y")
+    near, back, mine = call(
+        rest_kernel,
+        place,
+        [grads, marks, pair_weights, down_weights],
+        [(tall, BF16), (tall, BF16), (tall, F32)],
+    )
     terms = call(
         weight_kernel,
         place,
-        [shares[4]] + blocks,
+        [grads] + blocks,
         [((3, half, width), kind) for kind in (F32, BF16) for _ in range(4)],
         [pltpu.VMEM((2, 4, slots, width), BF16)],
     )
     keeps, sends = terms[0:4], terms[4:8]
     moved = [swap(send, "core") for send in sends]
-    near, back = halfway(passed, shares[1], shares[3])
+    near, back = halfway(passed, near, back)
     near, back, *moved = lax.optimization_barrier((near, back, *moved))
     arrived = [shift(near, "y", -1), shift(back, "y", 1)]
 
@@ -330,7 +367,7 @@
     passed = relay(both_cores(2).astype(BF16), "x")
     near, back = halfway(passed, both_cores(1), both_cores(3))
     far_sums = [shift(near, "x", -1), shift(back, "x", 1)]
-    totals = call(total_kernel, place, [shares[0]] + arrived, [((unit, width), BF16)] * 4)
+    totals = call(total_kernel, place, [mine] + arrived, [((unit, width), BF16)] * 4)
     returned = [totals[0]] + [shift(totals[k], "expert", -k) for k in (1, 2, 3)]
     layer_output, token_grad, prob_grad = call(
         owner_kernel,

time: 150 us -> 156 us (1.040)
  starting transfers between devices: 49.2 us -> 52.7 us
  waiting for transfers between devices: 69.9 us -> 66.9 us
  local copies, waits for them, and re-layouts: 3.23 us -> 5.6 us
  Pallas kernels: 20.8 us -> 22.8 us
    ppermute x2, waiting for transfers between devices: 8.37 us -> 0.01 us  [relay(): lax.ppermute(value, ('core', axis), [(4 * c + i, 4 * c + j) for c, i, j i...]
    ppermute x10, waiting for transfers between devices: 14.2 us -> 19 us  [swap(): return lax.ppermute(value, axis, [(0, 1), (1, 0)])]
    ppermute x14, waiting for transfers between devices: 32.3 us -> 28.3 us  [shift(): return lax.ppermute(value, axis, [(i, (i + step) % 4) for i in range(4)])]
    ppermute x14, starting transfers between devices: 25.1 us -> 29.1 us  [shift(): return lax.ppermute(value, axis, [(i, (i + step) % 4) for i in range(4)])]
    ppermute x2, waiting for transfers between devices: 4.29 us -> 7.72 us  [turn(): lax.ppermute(value, ('core', 'zl'), [(2 * c + z, 2 * z + c) for c in rang...]
    ppermute x2, starting transfers between devices: 1.5 us -> 4.26 us  [relay(): lax.ppermute(value, ('core', axis), [(4 * c + i, 4 * c + j) for c, i, j i...]
    unnamed x25 -> x27, local copies, waits for them, and re-layouts: 2.52 us -> 4.89 us
    ppermute x2, starting transfers between devices: 8.64 us -> 6.51 us  [turn(): lax.ppermute(value, ('core', 'zl'), [(2 * c + z, 2 * z + c) for c in rang...]
  transfers between devices with their start and end apart: 31 -> 31, of which waited for: 18 -> 16; matrix products, arithmetic and copies ran while one was open for 2% -> 3% of each run, Pallas kernels for 7% -> 12%
where the time goes in v9:
time: 156 us; the launch traced here: 155 us
  waiting for transfers between devices  66.9 us (43%)
  starting transfers between devices  52.7 us (34%)
  Pallas kernels  22.8 us (15%)
  other arithmetic  6.32 us (4%)
  local copies, waits for them, and re-layouts  5.6 us (4%)
    ppermute x14, starting transfers between devices, shift(): return lax.ppermute(value, axis, [(i, (i + step) % 4) for i in range(4)])  29.1 us
    ppermute x14, waiting for transfers between devices, shift(): return lax.ppermute(value, axis, [(i, (i + step) % 4) for i in range(4)])  28.3 us
    pallas_call x9, Pallas kernels, call(): pl.pallas_call(kernel, out_shape=[jax.ShapeDtypeStruct(shape, kind) for s...  22.8 us
    ppermute x10, waiting for transfers between devices, swap(): return lax.ppermute(value, axis, [(0, 1), (1, 0)])  19 us
    ppermute x2, waiting for transfers between devices, turn(): lax.ppermute(value, ('core', 'zl'), [(2 * c + z, 2 * z + c) for c in rang...  7.72 us
    ppermute x2, starting transfers between devices, turn(): lax.ppermute(value, ('core', 'zl'), [(2 * c + z, 2 * z + c) for c in rang...  6.51 us
    ppermute x1, waiting for transfers between devices, body(): turned = lax.ppermute(own, ('core', 'zl'), [(1, 2), (2, 1)])  6.23 us
    ppermute x2, waiting for transfers between devices, relay(): lax.ppermute(value, ('x', 'core'), [(2 * i + c, 2 * j + c) for c, i, j in...  5.71 us
  transfers between devices with their start and end apart: 31, of which 16 were waited for; matrix products, arithmetic and copies ran while one was open for 3% of the time, Pallas kernels for 12%

profile of v9, /device:TPU:1, one launch (start us, length us, event | category | flops | bytes accessed | tf_op | source)
XLA Modules:
  0.0 155.3 jit_solution(11044223934601060331)
XLA Ops:
  2.1 1.0 pad_maximum_fusion.1.wide
  3.2 1.0 shard_map.84
  4.2 4.9 %collective-permute-start.3 = (bf16[3,192,512]{2,1,0:T(8,128)(2,1)}, bf16[3,192,512]{2,1,0:T(8,128)(2,1)S(1)}, u32[]{:S(2)}, u32[]{:S(2)}) collective-permute-start(bf16[3,192,512]{2,1,0:T(8,128)(2,1)} %bitcast.20), channel_id=1, source_target_pairs={{1,32},{32,1},{3,34},{34,3},{5,36},{36,5},{7,38},{38,7},{9,40},{40... | collective-permute-start | bytes 1769480 | tf_op jit(solution)/shard_map/ppermute | solution.py:290
  9.1 3.1 %collective-permute-start = (bf16[160,512]{1,0:T(8,128)(2,1)S(1)}, bf16[160,512]{1,0:T(8,128)(2,1)}, u32[]{:S(2)}, u32[]{:S(2)}) collective-permute-start(bf16[160,512]{1,0:T(8,128)(2,1)S(1)} %get-tuple-element.52), channel_id=1, source_target_pairs={{0,8},{8,16},{16,24},{24,0},{1,9},{9,17},{17,25},{25,1},{2,10},{10... | collective-permute-start | bytes 491528 | tf_op jit(solution)/shard_map/ppermute | solution.py:250
  12.2 4.2 %collective-permute-start.1 = (bf16[160,512]{1,0:T(8,128)(2,1)S(1)}, bf16[160,512]{1,0:T(8,128)(2,1)S(1)}, u32[]{:S(2)}, u32[]{:S(2)}) collective-permute-start(bf16[160,512]{1,0:T(8,128)(2,1)S(1)} %get-tuple-element.53), channel_id=1, source_target_pairs={{0,16},{8,24},{16,0},{24,8},{1,17},{9,25},{17,1},{25,9},{2,18},{10... | collective-permute-start | bytes 491528 | tf_op jit(solution)/shard_map/ppermute | solution.py:250
  16.4 2.4 %collective-permute-start.2 = (bf16[160,512]{1,0:T(8,128)(2,1)S(1)}, bf16[160,512]{1,0:T(8,128)(2,1)S(1)}, u32[]{:S(2)}, u32[]{:S(2)}) collective-permute-start(bf16[160,512]{1,0:T(8,128)(2,1)S(1)} %get-tuple-element.54), channel_id=1, source_target_pairs={{0,24},{8,0},{16,8},{24,16},{1,25},{9,1},{17,9},{25,17},{2,26},{10... | collective-permute-start | bytes 491528 | tf_op jit(solution)/shard_map/ppermute | solution.py:250
  18.8 6.2 %collective-permute-done.3 = bf16[3,192,512]{2,1,0:T(8,128)(2,1)S(1)} collective-permute-done((bf16[3,192,512]{2,1,0:T(8,128)(2,1)}, bf16[3,192,512]{2,1,0:T(8,128)(2,1)S(1)}, u32[]{:S(2)}, u32[]{:S(2)}) %collective-permute-start.3) | collective-permute-done | bytes 589856 | tf_op jit(solution)/shard_map/ppermute | solution.py:290
  25.1 1.3 collective-permute-start.4
  26.4 1.5 collective-permute-start.5
  27.8 2.7 %collective-permute-done = bf16[160,512]{1,0:T(8,128)(2,1)} collective-permute-done((bf16[160,512]{1,0:T(8,128)(2,1)S(1)}, bf16[160,512]{1,0:T(8,128)(2,1)}, u32[]{:S(2)}, u32[]{:S(2)}) %collective-permute-start) | collective-permute-done | bytes 163872 | tf_op jit(solution)/shard_map/ppermute | solution.py:250
  30.6 0.9 constant_dynamic-update-slice_fusion.2
  31.5 4.8 %collective-permute-done.1 = bf16[160,512]{1,0:T(8,128)(2,1)S(1)} collective-permute-done((bf16[160,512]{1,0:T(8,128)(2,1)S(1)}, bf16[160,512]{1,0:T(8,128)(2,1)S(1)}, u32[]{:S(2)}, u32[]{:S(2)}) %collective-permute-start.1) | collective-permute-done | bytes 163872 | tf_op jit(solution)/shard_map/ppermute | solution.py:250
  36.4 1.4 collective-permute-start.6
  37.7 1.5 collective-permute-start.7
  39.3 1.1 broadcast_select_fusion.1
  40.4 2.6 %collective-permute-start.8 = (bf16[3,192,512]{2,1,0:T(8,128)(2,1)S(1)}, bf16[3,192,512]{2,1,0:T(8,128)(2,1)S(1)}, u32[]{:S(2)}, u32[]{:S(2)}) collective-permute-start(bf16[3,192,512]{2,1,0:T(8,128)(2,1)S(1)} %broadcast_select_fusion.1), channel_id=1, source_target_pairs={{0,64},{64,128},{128,192},{192,0},{32,224},{96,32},{160,96},{224,1... | collective-permute-start | bytes 1769480 | tf_op jit(solution)/shard_map/ppermute | solution.py:256
  43.0 6.7 %collective-permute-done.6.refs_1_ = bf16[640,512]{1,0:T(8,128)(2,1)S(1)} collective-permute-done((bf16[640,512]{1,0:T(8,128)(2,1)S(1)}, bf16[640,512]{1,0:T(8,128)(2,1)S(1)}, u32[]{:S(2)}, u32[]{:S(2)}) %collective-permute-start.6) | collective-permute-done | bytes 655392 | tf_op jit(solution)/shard_map/ppermute | solution.py:250
  49.7 1.6 %collective-permute-start.13 = (bf16[640,512]{1,0:T(8,128)(2,1)S(1)}, bf16[640,512]{1,0:T(8,128)(2,1)S(1)}, u32[]{:S(2)}, u32[]{:S(2)}) collective-permute-start(bf16[640,512]{1,0:T(8,128)(2,1)S(1)} %broadcast_select_fusion), channel_id=1, source_target_pairs={{0,2},{2,4},{4,6},{6,0},{32,38},{34,32},{36,34},{38,36},{1,3},{3,5... | collective-permute-start | bytes 1966088 | tf_op jit(solution)/shard_map/ppermute | solution.py:257
  52.3 1.8 %collective-permute-done.10.refs_8_ = bf16[3,192,512]{2,1,0:T(8,128)(2,1)S(1)} collective-permute-done((bf16[3,192,512]{2,1,0:T(8,128)(2,1)S(1)}, bf16[3,192,512]{2,1,0:T(8,128)(2,1)S(1)}, u32[]{:S(2)}, u32[]{:S(2)}) %collective-permute-start.10) | collective-permute-done | bytes 589856 | tf_op jit(solution)/shard_map/ppermute | solution.py:261
  55.0 0.8 collective-permute-done.11.refs_9_
  55.9 6.8 %shard_map.85 = (f32[320,768]{1,0:T(8,128)}, f32[320,384]{1,0:T(8,128)S(1)}, bf16[768,2048]{1,0:T(8,128)(2,1)}, bf16[384,2048]{1,0:T(8,128)(2,1)}) custom-call(s32[5]{0:T(128)S(1)} %stack.23.place, bf16[640,512]{1,0:T(8,128)(2,1)S(1)} %constant_dynamic-update-slice_fusion.refs_0_, bf16[640,512]{1,0:T(8,128)(2,1)} %copy-done.2, bf16[640,512]{1,0:T(8,128)(2,1)} %copy-done.4, ...), custom_call_target="tpu_custom_call" | custom-call | tf_op jit(solution)/shard_map/pallas_call | solution.py:33
  62.7 1.9 %copy-done = bf16[768,2048]{1,0:T(8,128)(2,1)S(1)} copy-done((bf16[768,2048]{1,0:T(8,128)(2,1)S(1)}, bf16[768,2048]{1,0:T(8,128)(2,1)}, u32[]{:S(2)}) %copy-start) | copy-done | bytes 3145752
  64.6 1.2 copy-done.6
  65.8 1.0 shard_map.86.pair
  66.8 1.5 collective-permute-start.14
  68.3 0.9 shard_map.87.down
  69.5 15.5 %collective-permute-done.15.down_far = bf16[320,384]{1,0:T(8,128)(2,1)S(1)} collective-permute-done((bf16[320,384]{1,0:T(8,128)(2,1)S(1)}, bf16[320,384]{1,0:T(8,128)(2,1)S(1)}, u32[]{:S(2)}, u32[]{:S(2)}) %collective-permute-start.15) | collective-permute-done | bytes 245792 | tf_op jit(solution)/shard_map/ppermute | solution.py:261
  85.0 2.7 %shard_map.88 = (bf16[656,512]{1,0:T(8,128)(2,1)S(1)}, bf16[320,1152]{1,0:T(8,128)(2,1)S(1)}, f32[16,128]{1,0:T(8,128)S(1)}) custom-call(s32[5]{0:T(128)S(1)} %stack.23.place, bf16[320,768]{1,0:T(8,128)(2,1)S(1)} %shard_map.86.pair, bf16[320,768]{1,0:T(8,128)(2,1)S(1)} %collective-permute-done.14.pair_far, bf16[320,384]{1,0:T(8,128)(2,1)S(1)} %shard_map.87.down, ...), custom_call_target="tpu_custom_call" | custom-call | tf_op jit(solution)/shard_map/pallas_call | solution.py:33
  87.7 2.7 %collective-permute-start.16 = (bf16[656,512]{1,0:T(8,128)(2,1)S(1)}, bf16[656,512]{1,0:T(8,128)(2,1)S(1)}, u32[]{:S(2)}, u32[]{:S(2)}) collective-permute-start(bf16[656,512]{1,0:T(8,128)(2,1)S(1)} %get-tuple-element.69), channel_id=1, source_target_pairs={{0,2},{2,4},{4,6},{6,0},{32,38},{34,32},{36,34},{38,36},{1,3},{3,5... | collective-permute-start | bytes 2015240 | tf_op jit(solution)/shard_map/ppermute | solution.py:257
  90.4 4.6 %shard_map.89 = (f32[3,192,512]{2,1,0:T(8,128)}, f32[3,192,512]{2,1,0:T(8,128)}, f32[3,192,512]{2,1,0:T(8,128)}, f32[3,192,512]{2,1,0:T(8,128)}, bf16[3,192,512]...) custom-call(s32[5]{0:T(128)S(1)} %stack.23.place, ...), custom_call_target="tpu_custom_call" | custom-call | tf_op jit(solution)/shard_map/pallas_call | solution.py:33
  96.0 3.3 %shard_map.90 = (bf16[656,512]{1,0:T(8,128)(2,1)S(1)}, bf16[656,512]{1,0:T(8,128)(2,1)S(1)}, f32[656,512]{1,0:T(8,128)S(1)}) custom-call(s32[5]{0:T(128)S(1)} %stack.23.place, bf16[320,1152]{1,0:T(8,128)(2,1)S(1)} %get-tuple-element.65.joined.hidden, f32[16,128]{1,0:T(8,128)S(1)} %get-tuple-element.67.marks, ...), custom_call_target="tpu_custom_call" | custom-call | tf_op jit(solution)/shard_map/pallas_call | solution.py:33
  99.8 0.8 copy-done.8
  100.8 1.5 collective-permute-start.21
  102.3 1.9 %collective-permute-start.26 = (bf16[656,512]{1,0:T(8,128)(2,1)S(1)}, bf16[656,512]{1,0:T(8,128)(2,1)S(1)}, u32[]{:S(2)}, u32[]{:S(2)}) collective-permute-start(bf16[656,512]{1,0:T(8,128)(2,1)S(1)} %get-tuple-element.84), channel_id=1, source_target_pairs={{0,6},{2,0},{4,2},{6,4},{1,7},{3,1},{5,3},{7,5},{8,14},{10,8},{12,... | collective-permute-start | bytes 2015240 | tf_op jit(solution)/shard_map/ppermute | solution.py:250
  104.2 5.7 %collective-permute-done.21 = bf16[3,192,512]{2,1,0:T(8,128)(2,1)S(1)} collective-permute-done((bf16[3,192,512]{2,1,0:T(8,128)(2,1)S(1)}, bf16[3,192,512]{2,1,0:T(8,128)(2,1)S(1)}, u32[]{:S(2)}, u32[]{:S(2)}) %collective-permute-start.21) | collective-permute-done | bytes 589856 | tf_op jit(solution)/shard_map/ppermute | solution.py:256
  110.4 2.9 %collective-permute-start.22 = (bf16[3,192,512]{2,1,0:T(8,128)(2,1)S(1)}, bf16[3,192,512]{2,1,0:T(8,128)(2,1)S(1)}, u32[]{:S(2)}, u32[]{:S(2)}) collective-permute-start(bf16[3,192,512]{2,1,0:T(8,128)(2,1)S(1)} %get-tuple-element.100), channel_id=1, source_target_pairs={{0,192},{64,0},{128,64},{192,128},{1,193},{65,1},{129,65},{193,129... | collective-permute-start | bytes 1769480 | tf_op jit(solution)/shard_map/ppermute | solution.py:250
  113.4 5.6 %collective-permute-done.26.one = bf16[656,512]{1,0:T(8,128)(2,1)S(1)} collective-permute-done((bf16[656,512]{1,0:T(8,128)(2,1)S(1)}, bf16[656,512]{1,0:T(8,128)(2,1)S(1)}, u32[]{:S(2)}, u32[]{:S(2)}) %collective-permute-start.26) | collective-permute-done | bytes 671776 | tf_op jit(solution)/shard_map/ppermute | solution.py:250
  119.0 3.2 %collective-permute-done.27.three = bf16[656,512]{1,0:T(8,128)(2,1)S(1)} collective-permute-done((bf16[656,512]{1,0:T(8,128)(2,1)S(1)}, bf16[656,512]{1,0:T(8,128)(2,1)S(1)}, u32[]{:S(2)}, u32[]{:S(2)}) %collective-permute-start.27) | collective-permute-done | bytes 671776 | tf_op jit(solution)/shard_map/ppermute | solution.py:250
  122.2 0.8 shard_map.91
  123.0 6.7 %collective-permute-start.28 = (bf16[176,512]{1,0:T(8,128)(2,1)S(1)}, bf16[176,512]{1,0:T(8,128)(2,1)S(1)}, u32[]{:S(2)}, u32[]{:S(2)}) collective-permute-start(bf16[176,512]{1,0:T(8,128)(2,1)S(1)} %get-tuple-element.87), channel_id=1, source_target_pairs={{0,24},{8,0},{16,8},{24,16},{1,25},{9,1},{17,9},{25,17},{2,26},{10... | collective-permute-start | bytes 540680 | tf_op jit(solution)/shard_map/ppermute | solution.py:250
  129.7 2.3 %collective-permute-start.29 = (bf16[176,512]{1,0:T(8,128)(2,1)S(1)}, bf16[176,512]{1,0:T(8,128)(2,1)S(1)}, u32[]{:S(2)}, u32[]{:S(2)}) collective-permute-start(bf16[176,512]{1,0:T(8,128)(2,1)S(1)} %get-tuple-element.88), channel_id=1, source_target_pairs={{0,16},{8,24},{16,0},{24,8},{1,17},{9,25},{17,1},{25,9},{2,18},{10... | collective-permute-start | bytes 540680 | tf_op jit(solution)/shard_map/ppermute | solution.py:250
  132.4 4.6 %collective-permute-start.24 = (bf16[288,512]{1,0:T(8,128)(2,1)S(1)}, bf16[288,512]{1,0:T(8,128)(2,1)S(1)}, u32[]{:S(2)}, u32[]{:S(2)}) collective-permute-start(bf16[288,512]{1,0:T(8,128)(2,1)S(1)} %get-tuple-element.99), channel_id=1, source_target_pairs={{0,0},{1,32},{32,1},{33,33},{2,2},{3,34},{34,3},{35,35},{4,4},{5,3... | collective-permute-start | bytes 884744 | tf_op jit(solution)/shard_map/ppermute | solution.py:265
  137.0 1.9 %collective-permute-start.25 = (bf16[288,512]{1,0:T(8,128)(2,1)S(1)}, bf16[288,512]{1,0:T(8,128)(2,1)S(1)}, u32[]{:S(2)}, u32[]{:S(2)}) collective-permute-start(bf16[288,512]{1,0:T(8,128)(2,1)S(1)} %get-tuple-element.98), channel_id=1, source_target_pairs={{0,0},{1,32},{32,1},{33,33},{2,2},{3,34},{34,3},{35,35},{4,4},{5,3... | collective-permute-start | bytes 884744 | tf_op jit(solution)/shard_map/ppermute | solution.py:265
  138.9 5.0 %collective-permute-done.29.refs_2_ = bf16[176,512]{1,0:T(8,128)(2,1)S(1)} collective-permute-done((bf16[176,512]{1,0:T(8,128)(2,1)S(1)}, bf16[176,512]{1,0:T(8,128)(2,1)S(1)}, u32[]{:S(2)}, u32[]{:S(2)}) %collective-permute-start.29) | collective-permute-done | bytes 180256 | tf_op jit(solution)/shard_map/ppermute | solution.py:250
  144.1 1.7 %shard_map.92 = (bf16[128,512]{1,0:T(8,128)(2,1)}, bf16[128,512]{1,0:T(8,128)(2,1)}, f32[8,128]{1,0:T(8,128)S(1)}) custom-call(s32[5]{0:T(128)S(1)} %stack.23.place, f32[4,128]{1,0:T(4,128)S(1)} %pad_maximum_fusion.2.small, bf16[320,128]{1,0:T(8,128)(2,1)S(1)} %get-tuple-element.82.placing, bf16[176,512]{1,0:T(8,128)(2,1)S(1)} %get-tuple-element.86.refs_0_, ...), custom_call_target="tpu_custom_call" | custom-call | tf_op jit(solution)/shard_map/pallas_call | solution.py:33
  146.4 4.6 %collective-permute-done.24 = bf16[288,512]{1,0:T(8,128)(2,1)S(1)} collective-permute-done((bf16[288,512]{1,0:T(8,128)(2,1)S(1)}, bf16[288,512]{1,0:T(8,128)(2,1)S(1)}, u32[]{:S(2)}, u32[]{:S(2)}) %collective-permute-start.24) | collective-permute-done | bytes 294944 | tf_op jit(solution)/shard_map/ppermute | solution.py:265
  150.9 3.2 %collective-permute-done.25 = bf16[288,512]{1,0:T(8,128)(2,1)S(1)} collective-permute-done((bf16[288,512]{1,0:T(8,128)(2,1)S(1)}, bf16[288,512]{1,0:T(8,128)(2,1)S(1)}, u32[]{:S(2)}, u32[]{:S(2)}) %collective-permute-start.25) | collective-permute-done | bytes 294944 | tf_op jit(solution)/shard_map/ppermute | solution.py:265
  154.1 1.2 convert.2
  (66 shorter events, 7.3 us)
Async XLA Ops:
  0.6 24.4 %copy-start.11 = (bf16[1,3,192,512]{3,2,1,0:T(8,128)(2,1)S(1)}, bf16[1,3,192,512]{3,2,1,0:T(8,128)(2,1)}, u32[]{:S(2)}) copy-start(bf16[1,3,192,512]{3,2,1,0:T(8,128)(2,1)} %param.8) | copy-start | bytes 1769476
  4.2 20.8 %collective-permute-start.3 = (bf16[3,192,512]{2,1,0:T(8,128)(2,1)}, bf16[3,192,512]{2,1,0:T(8,128)(2,1)S(1)}, u32[]{:S(2)}, u32[]{:S(2)}) collective-permute-start(bf16[3,192,512]{2,1,0:T(8,128)(2,1)} %bitcast.20), channel_id=1, source_target_pairs={{1,32},{32,1},{3,34},{34,3},{5,36},{36,5},{7,38},{38,7},{9,40},{40... | collective-permute-start | bytes 1769480 | tf_op jit(solution)/shard_map/ppermute | solution.py:290
  9.1 21.5 %collective-permute-start = (bf16[160,512]{1,0:T(8,128)(2,1)S(1)}, bf16[160,512]{1,0:T(8,128)(2,1)}, u32[]{:S(2)}, u32[]{:S(2)}) collective-permute-start(bf16[160,512]{1,0:T(8,128)(2,1)S(1)} %get-tuple-element.52), channel_id=1, source_target_pairs={{0,8},{8,16},{16,24},{24,0},{1,9},{9,17},{17,25},{25,1},{2,10},{10... | collective-permute-start | bytes 491528 | tf_op jit(solution)/shard_map/ppermute | solution.py:250
  12.2 24.1 %collective-permute-start.1 = (bf16[160,512]{1,0:T(8,128)(2,1)S(1)}, bf16[160,512]{1,0:T(8,128)(2,1)S(1)}, u32[]{:S(2)}, u32[]{:S(2)}) collective-permute-start(bf16[160,512]{1,0:T(8,128)(2,1)S(1)} %get-tuple-element.53), channel_id=1, source_target_pairs={{0,16},{8,24},{16,0},{24,8},{1,17},{9,25},{17,1},{25,9},{2,18},{10... | collective-permute-start | bytes 491528 | tf_op jit(solution)/shard_map/ppermute | solution.py:250
  16.4 20.0 %collective-permute-start.2 = (bf16[160,512]{1,0:T(8,128)(2,1)S(1)}, bf16[160,512]{1,0:T(8,128)(2,1)S(1)}, u32[]{:S(2)}, u32[]{:S(2)}) collective-permute-start(bf16[160,512]{1,0:T(8,128)(2,1)S(1)} %get-tuple-element.54), channel_id=1, source_target_pairs={{0,24},{8,0},{16,8},{24,16},{1,25},{9,1},{17,9},{25,17},{2,26},{10... | collective-permute-start | bytes 491528 | tf_op jit(solution)/shard_map/ppermute | solution.py:250
  25.1 14.2 %collective-permute-start.4 = (bf16[3,192,512]{2,1,0:T(8,128)(2,1)S(1)}, bf16[3,192,512]{2,1,0:T(8,128)(2,1)S(1)}, u32[]{:S(2)}, u32[]{:S(2)}) collective-permute-start(bf16[3,192,512]{2,1,0:T(8,128)(2,1)S(1)} %broadcast_select_fusion.2.refs_3_), channel_id=1, source_target_pairs={{0,64},{64,128},{128,192},{192,0},{1,65},{65,129},{129,193},{193,1... | collective-permute-start | bytes 1769480 | tf_op jit(solution)/shard_map/ppermute | solution.py:250
  26.4 12.9 %collective-permute-start.5 = (bf16[3,192,512]{2,1,0:T(8,128)(2,1)S(1)}, bf16[3,192,512]{2,1,0:T(8,128)(2,1)}, u32[]{:S(2)}, u32[]{:S(2)}) collective-permute-start(bf16[3,192,512]{2,1,0:T(8,128)(2,1)S(1)} %broadcast_select_fusion.2.refs_3_), channel_id=1, source_target_pairs={{0,192},{64,0},{128,64},{192,128},{1,193},{65,1},{129,65},{193,129... | collective-permute-start | bytes 1769480 | tf_op jit(solution)/shard_map/ppermute | solution.py:250
  36.4 13.3 %collective-permute-start.6 = (bf16[640,512]{1,0:T(8,128)(2,1)S(1)}, bf16[640,512]{1,0:T(8,128)(2,1)S(1)}, u32[]{:S(2)}, u32[]{:S(2)}) collective-permute-start(bf16[640,512]{1,0:T(8,128)(2,1)S(1)} %constant_dynamic-update-slice_fusion.refs_0_), channel_id=1, source_target_pairs={{0,2},{2,4},{4,6},{6,0},{1,3},{3,5},{5,7},{7,1},{8,10},{10,12},{12... | collective-permute-start | bytes 1966088 | tf_op jit(solution)/shard_map/ppermute | solution.py:250
  37.7 11.9 %collective-permute-start.7 = (bf16[640,512]{1,0:T(8,128)(2,1)S(1)}, bf16[640,512]{1,0:T(8,128)(2,1)S(1)}, u32[]{:S(2)}, u32[]{:S(2)}) collective-permute-start(bf16[640,512]{1,0:T(8,128)(2,1)S(1)} %constant_dynamic-update-slice_fusion.refs_0_), channel_id=1, source_target_pairs={{0,6},{2,0},{4,2},{6,4},{1,7},{3,1},{5,3},{7,5},{8,14},{10,8},{12,... | collective-permute-start | bytes 1966088 | tf_op jit(solution)/shard_map/ppermute | solution.py:250
  40.4 11.4 %collective-permute-start.8 = (bf16[3,192,512]{2,1,0:T(8,128)(2,1)S(1)}, bf16[3,192,512]{2,1,0:T(8,128)(2,1)S(1)}, u32[]{:S(2)}, u32[]{:S(2)}) collective-permute-start(bf16[3,192,512]{2,1,0:T(8,128)(2,1)S(1)} %broadcast_select_fusion.1), channel_id=1, source_target_pairs={{0,64},{64,128},{128,192},{192,0},{32,224},{96,32},{160,96},{224,1... | collective-permute-start | bytes 1769480 | tf_op jit(solution)/shard_map/ppermute | solution.py:256
  49.6 6.2 %copy-start.2 = (bf16[640,512]{1,0:T(8,128)(2,1)}, bf16[640,512]{1,0:T(8,128)(2,1)S(1)}, u32[]{:S(2)}) copy-start(bf16[640,512]{1,0:T(8,128)(2,1)S(1)} %collective-permute-done.6.refs_1_) | copy-start | bytes 1966084
  49.6 6.2 %copy-start.4 = (bf16[640,512]{1,0:T(8,128)(2,1)}, bf16[640,512]{1,0:T(8,128)(2,1)S(1)}, u32[]{:S(2)}) copy-start(bf16[640,512]{1,0:T(8,128)(2,1)S(1)} %collective-permute-done.7.refs_2_.refs_3_) | copy-start | bytes 1966084
  49.7 13.0 %collective-permute-start.13 = (bf16[640,512]{1,0:T(8,128)(2,1)S(1)}, bf16[640,512]{1,0:T(8,128)(2,1)S(1)}, u32[]{:S(2)}, u32[]{:S(2)}) collective-permute-start(bf16[640,512]{1,0:T(8,128)(2,1)S(1)} %broadcast_select_fusion), channel_id=1, source_target_pairs={{0,2},{2,4},{4,6},{6,0},{32,38},{34,32},{36,34},{38,36},{1,3},{3,5... | collective-permute-start | bytes 1966088 | tf_op jit(solution)/shard_map/ppermute | solution.py:257
  51.3 2.8 %collective-permute-start.10 = (bf16[3,192,512]{2,1,0:T(8,128)(2,1)S(1)}, bf16[3,192,512]{2,1,0:T(8,128)(2,1)S(1)}, u32[]{:S(2)}, u32[]{:S(2)}) collective-permute-start(bf16[3,192,512]{2,1,0:T(8,128)(2,1)S(1)} %collective-permute-done.4.refs_4_), channel_id=1, source_target_pairs={{0,32},{32,0},{1,33},{33,1},{2,34},{34,2},{3,35},{35,3},{4,36},{36... | collective-permute-start | bytes 1769480 | tf_op jit(solution)/shard_map/ppermute | solution.py:261
  51.3 3.5 %collective-permute-start.12 = (bf16[3,192,512]{2,1,0:T(8,128)(2,1)}, bf16[3,192,512]{2,1,0:T(8,128)(2,1)S(1)}, u32[]{:S(2)}, u32[]{:S(2)}) collective-permute-start(bf16[3,192,512]{2,1,0:T(8,128)(2,1)} %collective-permute-done.5.refs_6_), channel_id=1, source_target_pairs={{0,32},{32,0},{1,33},{33,1},{2,34},{34,2},{3,35},{35,3},{4,36},{36... | collective-permute-start | bytes 1769480 | tf_op jit(solution)/shard_map/ppermute | solution.py:261
  51.8 3.2 %collective-permute-start.9 = (bf16[3,192,512]{2,1,0:T(8,128)(2,1)S(1)}, bf16[3,192,512]{2,1,0:T(8,128)(2,1)S(1)}, u32[]{:S(2)}, u32[]{:S(2)}) collective-permute-start(bf16[3,192,512]{2,1,0:T(8,128)(2,1)S(1)} %broadcast_select_fusion.2.refs_3_), channel_id=1, source_target_pairs={{0,32},{32,0},{1,33},{33,1},{2,34},{34,2},{3,35},{35,3},{4,36},{36... | collective-permute-start | bytes 1769480 | tf_op jit(solution)/shard_map/ppermute | solution.py:261
  51.8 4.0 %collective-permute-start.11 = (bf16[3,192,512]{2,1,0:T(8,128)(2,1)S(1)}, bf16[3,192,512]{2,1,0:T(8,128)(2,1)S(1)}, u32[]{:S(2)}, u32[]{:S(2)}) collective-permute-start(bf16[3,192,512]{2,1,0:T(8,128)(2,1)S(1)} %collective-permute-done.8.refs_5_), channel_id=1, source_target_pairs={{0,32},{32,0},{1,33},{33,1},{2,34},{34,2},{3,35},{35,3},{4,36},{36... | collective-permute-start | bytes 1769480 | tf_op jit(solution)/shard_map/ppermute | solution.py:261
  62.7 1.9 %copy-start = (bf16[768,2048]{1,0:T(8,128)(2,1)S(1)}, bf16[768,2048]{1,0:T(8,128)(2,1)}, u32[]{:S(2)}) copy-start(bf16[768,2048]{1,0:T(8,128)(2,1)} %get-tuple-element.62.weights.pair_weights) | copy-start | bytes 9437188
  64.6 1.2 copy-start.6
  65.8 2.5 %copy-start.1 = (bf16[384,2048]{1,0:T(8,128)(2,1)S(1)}, bf16[384,2048]{1,0:T(8,128)(2,1)}, u32[]{:S(2)}) copy-start(bf16[384,2048]{1,0:T(8,128)(2,1)} %get-tuple-element.64.weights.down_weights) | copy-start | bytes 4718596
  66.8 18.2 %collective-permute-start.14 = (bf16[320,768]{1,0:T(8,128)(2,1)S(1)}, bf16[320,768]{1,0:T(8,128)(2,1)S(1)}, u32[]{:S(2)}, u32[]{:S(2)}) collective-permute-start(bf16[320,768]{1,0:T(8,128)(2,1)S(1)} %shard_map.86.pair), channel_id=1, source_target_pairs={{0,1},{1,0},{2,3},{3,2},{4,5},{5,4},{6,7},{7,6},{8,9},{9,8},{10,11... | collective-permute-start | bytes 1474568 | tf_op jit(solution)/shard_map/ppermute | solution.py:261
  69.2 21.1 %copy-start.3 = (bf16[640,512]{1,0:T(8,128)(2,1)S(1)}, bf16[640,512]{1,0:T(8,128)(2,1)}, u32[]{:S(2)}) copy-start(bf16[640,512]{1,0:T(8,128)(2,1)} %copy-done.2) | copy-start | bytes 1966084
  69.2 21.1 %copy-start.5 = (bf16[640,512]{1,0:T(8,128)(2,1)S(1)}, bf16[640,512]{1,0:T(8,128)(2,1)}, u32[]{:S(2)}) copy-start(bf16[640,512]{1,0:T(8,128)(2,1)} %copy-done.4) | copy-start | bytes 1966084
  69.3 15.8 %collective-permute-start.15 = (bf16[320,384]{1,0:T(8,128)(2,1)S(1)}, bf16[320,384]{1,0:T(8,128)(2,1)S(1)}, u32[]{:S(2)}, u32[]{:S(2)}) collective-permute-start(bf16[320,384]{1,0:T(8,128)(2,1)S(1)} %shard_map.87.down), channel_id=1, source_target_pairs={{0,1},{1,0},{2,3},{3,2},{4,5},{5,4},{6,7},{7,6},{8,9},{9,8},{10,11... | collective-permute-start | bytes 737288 | tf_op jit(solution)/shard_map/ppermute | solution.py:261
  87.7 11.6 %collective-permute-start.16 = (bf16[656,512]{1,0:T(8,128)(2,1)S(1)}, bf16[656,512]{1,0:T(8,128)(2,1)S(1)}, u32[]{:S(2)}, u32[]{:S(2)}) collective-permute-start(bf16[656,512]{1,0:T(8,128)(2,1)S(1)} %get-tuple-element.69), channel_id=1, source_target_pairs={{0,2},{2,4},{4,6},{6,0},{32,38},{34,32},{36,34},{38,36},{1,3},{3,5... | collective-permute-start | bytes 2015240 | tf_op jit(solution)/shard_map/ppermute | solution.py:257
  95.0 4.8 %collective-permute-start.17 = (bf16[3,192,512]{2,1,0:T(8,128)(2,1)S(1)}, bf16[3,192,512]{2,1,0:T(8,128)(2,1)S(1)}, u32[]{:S(2)}, u32[]{:S(2)}) collective-permute-start(bf16[3,192,512]{2,1,0:T(8,128)(2,1)S(1)} %get-tuple-element.71), channel_id=1, source_target_pairs={{0,32},{32,0},{1,33},{33,1},{2,34},{34,2},{3,35},{35,3},{4,36},{36... | collective-permute-start | bytes 1769480 | tf_op jit(solution)/shard_map/ppermute | solution.py:261
  95.0 4.8 %collective-permute-start.18 = (bf16[3,192,512]{2,1,0:T(8,128)(2,1)S(1)}, bf16[3,192,512]{2,1,0:T(8,128)(2,1)S(1)}, u32[]{:S(2)}, u32[]{:S(2)}) collective-permute-start(bf16[3,192,512]{2,1,0:T(8,128)(2,1)S(1)} %get-tuple-element.72), channel_id=1, source_target_pairs={{0,32},{32,0},{1,33},{33,1},{2,34},{34,2},{3,35},{35,3},{4,36},{36... | collective-permute-start | bytes 1769480 | tf_op jit(solution)/shard_map/ppermute | solution.py:261
  95.5 4.3 %collective-permute-start.19 = (bf16[3,192,512]{2,1,0:T(8,128)(2,1)S(1)}, bf16[3,192,512]{2,1,0:T(8,128)(2,1)S(1)}, u32[]{:S(2)}, u32[]{:S(2)}) collective-permute-start(bf16[3,192,512]{2,1,0:T(8,128)(2,1)S(1)} %get-tuple-element.73), channel_id=1, source_target_pairs={{0,32},{32,0},{1,33},{33,1},{2,34},{34,2},{3,35},{35,3},{4,36},{36... | collective-permute-start | bytes 1769480 | tf_op jit(solution)/shard_map/ppermute | solution.py:261
  95.5 4.3 %collective-permute-start.20 = (bf16[3,192,512]{2,1,0:T(8,128)(2,1)S(1)}, bf16[3,192,512]{2,1,0:T(8,128)(2,1)S(1)}, u32[]{:S(2)}, u32[]{:S(2)}) collective-permute-start(bf16[3,192,512]{2,1,0:T(8,128)(2,1)S(1)} %get-tuple-element.74), channel_id=1, source_target_pairs={{0,32},{32,0},{1,33},{33,1},{2,34},{34,2},{3,35},{35,3},{4,36},{36... | collective-permute-start | bytes 1769480 | tf_op jit(solution)/shard_map/ppermute | solution.py:261
  99.3 1.3 copy-start.8
  100.6 9.3 %copy-start.9 = (f32[3,192,512]{2,1,0:T(8,128)S(1)}, f32[3,192,512]{2,1,0:T(8,128)}, u32[]{:S(2)}) copy-start(f32[3,192,512]{2,1,0:T(8,128)} %get-tuple-element.76) | copy-start | bytes 3538948
  100.6 9.3 %copy-start.10 = (f32[3,192,512]{2,1,0:T(8,128)S(1)}, f32[3,192,512]{2,1,0:T(8,128)}, u32[]{:S(2)}) copy-start(f32[3,192,512]{2,1,0:T(8,128)} %get-tuple-element.80) | copy-start | bytes 3538948
  100.8 9.1 %collective-permute-start.21 = (bf16[3,192,512]{2,1,0:T(8,128)(2,1)S(1)}, bf16[3,192,512]{2,1,0:T(8,128)(2,1)S(1)}, u32[]{:S(2)}, u32[]{:S(2)}) collective-permute-start(bf16[3,192,512]{2,1,0:T(8,128)(2,1)S(1)} %add_convert_fusion.1), channel_id=1, source_target_pairs={{0,64},{64,128},{128,192},{192,0},{32,224},{96,32},{160,96},{224,1... | collective-permute-start | bytes 1769480 | tf_op jit(solution)/shard_map/ppermute | solution.py:256
  102.3 16.7 %collective-permute-start.26 = (bf16[656,512]{1,0:T(8,128)(2,1)S(1)}, bf16[656,512]{1,0:T(8,128)(2,1)S(1)}, u32[]{:S(2)}, u32[]{:S(2)}) collective-permute-start(bf16[656,512]{1,0:T(8,128)(2,1)S(1)} %get-tuple-element.84), channel_id=1, source_target_pairs={{0,6},{2,0},{4,2},{6,4},{1,7},{3,1},{5,3},{7,5},{8,14},{10,8},{12,... | collective-permute-start | bytes 2015240 | tf_op jit(solution)/shard_map/ppermute | solution.py:250
  104.2 18.0 %collective-permute-start.27 = (bf16[656,512]{1,0:T(8,128)(2,1)S(1)}, bf16[656,512]{1,0:T(8,128)(2,1)S(1)}, u32[]{:S(2)}, u32[]{:S(2)}) collective-permute-start(bf16[656,512]{1,0:T(8,128)(2,1)S(1)} %get-tuple-element.85), channel_id=1, source_target_pairs={{0,2},{2,4},{4,6},{6,0},{1,3},{3,5},{5,7},{7,1},{8,10},{10,12},{12... | collective-permute-start | bytes 2015240 | tf_op jit(solution)/shard_map/ppermute | solution.py:250
  110.4 21.5 %collective-permute-start.22 = (bf16[3,192,512]{2,1,0:T(8,128)(2,1)S(1)}, bf16[3,192,512]{2,1,0:T(8,128)(2,1)S(1)}, u32[]{:S(2)}, u32[]{:S(2)}) collective-permute-start(bf16[3,192,512]{2,1,0:T(8,128)(2,1)S(1)} %get-tuple-element.100), channel_id=1, source_target_pairs={{0,192},{64,0},{128,64},{192,128},{1,193},{65,1},{129,65},{193,129... | collective-permute-start | bytes 1769480 | tf_op jit(solution)/shard_map/ppermute | solution.py:250
  113.4 18.6 %collective-permute-start.23 = (bf16[3,192,512]{2,1,0:T(8,128)(2,1)S(1)}, bf16[3,192,512]{2,1,0:T(8,128)(2,1)S(1)}, u32[]{:S(2)}, u32[]{:S(2)}) collective-permute-start(bf16[3,192,512]{2,1,0:T(8,128)(2,1)S(1)} %get-tuple-element.101), channel_id=1, source_target_pairs={{0,64},{64,128},{128,192},{192,0},{1,65},{65,129},{129,193},{193,1... | collective-permute-start | bytes 1769480 | tf_op jit(solution)/shard_map/ppermute | solution.py:250
  122.2 9.7 %copy-start.7 = (f32[3,192,512]{2,1,0:T(8,128)S(1)}, f32[3,192,512]{2,1,0:T(8,128)}, u32[]{:S(2)}) copy-start(f32[3,192,512]{2,1,0:T(8,128)} %get-tuple-element.66) | copy-start | bytes 3538948
  123.0 15.9 %collective-permute-start.28 = (bf16[176,512]{1,0:T(8,128)(2,1)S(1)}, bf16[176,512]{1,0:T(8,128)(2,1)S(1)}, u32[]{:S(2)}, u32[]{:S(2)}) collective-permute-start(bf16[176,512]{1,0:T(8,128)(2,1)S(1)} %get-tuple-element.87), channel_id=1, source_target_pairs={{0,24},{8,0},{16,8},{24,16},{1,25},{9,1},{17,9},{25,17},{2,26},{10... | collective-permute-start | bytes 540680 | tf_op jit(solution)/shard_map/ppermute | solution.py:250
  129.7 14.2 %collective-permute-start.29 = (bf16[176,512]{1,0:T(8,128)(2,1)S(1)}, bf16[176,512]{1,0:T(8,128)(2,1)S(1)}, u32[]{:S(2)}, u32[]{:S(2)}) collective-permute-start(bf16[176,512]{1,0:T(8,128)(2,1)S(1)} %get-tuple-element.88), channel_id=1, source_target_pairs={{0,16},{8,24},{16,0},{24,8},{1,17},{9,25},{17,1},{25,9},{2,18},{10... | collective-permute-start | bytes 540680 | tf_op jit(solution)/shard_map/ppermute | solution.py:250
  132.0 12.2 %collective-permute-start.30 = (bf16[176,512]{1,0:T(8,128)(2,1)S(1)}, bf16[176,512]{1,0:T(8,128)(2,1)S(1)}, u32[]{:S(2)}, u32[]{:S(2)}) collective-permute-start(bf16[176,512]{1,0:T(8,128)(2,1)S(1)} %get-tuple-element.89), channel_id=1, source_target_pairs={{0,8},{8,16},{16,24},{24,0},{1,9},{9,17},{17,25},{25,1},{2,10},{10... | collective-permute-start | bytes 540680 | tf_op jit(solution)/shard_map/ppermute | solution.py:250
  132.4 18.6 %collective-permute-start.24 = (bf16[288,512]{1,0:T(8,128)(2,1)S(1)}, bf16[288,512]{1,0:T(8,128)(2,1)S(1)}, u32[]{:S(2)}, u32[]{:S(2)}) collective-permute-start(bf16[288,512]{1,0:T(8,128)(2,1)S(1)} %get-tuple-element.99), channel_id=1, source_target_pairs={{0,0},{1,32},{32,1},{33,33},{2,2},{3,34},{34,3},{35,35},{4,4},{5,3... | collective-permute-start | bytes 884744 | tf_op jit(solution)/shard_map/ppermute | solution.py:265
  137.0 17.1 %collective-permute-start.25 = (bf16[288,512]{1,0:T(8,128)(2,1)S(1)}, bf16[288,512]{1,0:T(8,128)(2,1)S(1)}, u32[]{:S(2)}, u32[]{:S(2)}) collective-permute-start(bf16[288,512]{1,0:T(8,128)(2,1)S(1)} %get-tuple-element.98), channel_id=1, source_target_pairs={{0,0},{1,32},{32,1},{33,33},{2,2},{3,34},{34,3},{35,35},{4,4},{5,3... | collective-permute-start | bytes 884744 | tf_op jit(solution)/shard_map/ppermute | solution.py:265

commit v10 on v8

--- a/solution.py
+++ b/solution.py
@@ -253,7 +253,9 @@
     place = jnp.stack(
         [lax.axis_index(name) for name in ("expert", "x", "y", "zl", "core")]
     ).astype(jnp.int32)
-    small = jnp.concatenate([expert_ids.T.astype(F32), gate_probs.T])
+    small = jnp.pad(expert_ids.T.astype(F32), ((0, 2), (0, 0))) + jnp.pad(
+        gate_probs.T, ((2, 0), (0, 0))
+    )
     wide = jnp.concatenate([tokens, out_grad], axis=1)
     vmem = pl.BlockSpec(memory_space=pltpu.VMEM)
     hbm = pl.BlockSpec(memory_space=pl.ANY)
@@ -266,7 +268,7 @@
     )
 
     blocks = [blocks[0]] + [shift(blocks[k], "expert", k) for k in (1, 2, 3)]
-    own, blocks[0] = lax.optimization_barrier((stacked_weights[0], blocks[0]))
+    own = stacked_weights[0]
     turned = lax.ppermute(own, ("core", "zl"), [(1, 2), (2, 1)])
     own = jnp.where(place[4] == place[3], own, turned)
     first = lax.axis_index("core") == 0

time: 150 us -> 151 us (level)
  waiting for transfers between devices: 69.9 us -> 74.3 us
  starting transfers between devices: 49.2 us -> 46.1 us
    ppermute x14, waiting for transfers between devices: 32.3 us -> 44.5 us  [shift(): return lax.ppermute(value, axis, [(i, (i + step) % 4) for i in range(4)])]
    ppermute x1, waiting for transfers between devices: 6.23 us -> 0.01 us  [body(): turned = lax.ppermute(own, ('core', 'zl'), [(1, 2), (2, 1)])]
    ppermute x2, starting transfers between devices: 5.11 us -> 2.8 us  [relay(): lax.ppermute(value, ('x', 'core'), [(2 * i + c, 2 * j + c) for c, i, j in...]
    ppermute x2, waiting for transfers between devices: 4.29 us -> 2.28 us  [turn(): lax.ppermute(value, ('core', 'zl'), [(2 * c + z, 2 * z + c) for c in rang...]
    ppermute x2, starting transfers between devices: 8.64 us -> 6.89 us  [turn(): lax.ppermute(value, ('core', 'zl'), [(2 * c + z, 2 * z + c) for c in rang...]
  transfers between devices with their start and end apart: 31 -> 31, of which waited for: 18 -> 17; matrix products, arithmetic and copies ran while one was open for 2% -> 4% of each run, Pallas kernels for 7% -> 8%
where the time goes in v10:
time: 151 us
  waiting for transfers between devices  74.3 us (49%)
  starting transfers between devices  46.1 us (31%)
  Pallas kernels  20.8 us (14%)
  other arithmetic  5.18 us (3%)
  local copies, waits for them, and re-layouts  3.68 us (2%)
    ppermute x14, waiting for transfers between devices, shift(): return lax.ppermute(value, axis, [(i, (i + step) % 4) for i in range(4)])  44.5 us
    ppermute x14, starting transfers between devices, shift(): return lax.ppermute(value, axis, [(i, (i + step) % 4) for i in range(4)])  25.4 us
    pallas_call x7, Pallas kernels, call(): pl.pallas_call(kernel, out_shape=[jax.ShapeDtypeStruct(shape, kind) for s...  20.8 us
    ppermute x10, waiting for transfers between devices, swap(): return lax.ppermute(value, axis, [(0, 1), (1, 0)])  15.2 us
    ppermute x2, waiting for transfers between devices, relay(): lax.ppermute(value, ('core', axis), [(4 * c + i, 4 * c + j) for c, i, j i...  8.21 us
    ppermute x2, starting transfers between devices, turn(): lax.ppermute(value, ('core', 'zl'), [(2 * c + z, 2 * z + c) for c in rang...  6.89 us
    ppermute x1, starting transfers between devices, body(): turned = lax.ppermute(own, ('core', 'zl'), [(1, 2), (2, 1)])  5.07 us
    ppermute x2, waiting for transfers between devices, relay(): lax.ppermute(value, ('x', 'core'), [(2 * i + c, 2 * j + c) for c, i, j in...  4.07 us
  transfers between devices with their start and end apart: 31, of which 17 were waited for; matrix products, arithmetic and copies ran while one was open for 4% of the time, Pallas kernels for 8%

profile of v10, /device:TPU:1, one launch (start us, length us, event | category | flops | bytes accessed | tf_op | source)
XLA Modules:
  0.0 151.0 jit_solution(5017603158371030096)
XLA Ops:
  0.6 5.1 %collective-permute-start.3 = (bf16[3,192,512]{2,1,0:T(8,128)(2,1)}, bf16[3,192,512]{2,1,0:T(8,128)(2,1)S(1)}, u32[]{:S(2)}, u32[]{:S(2)}) collective-permute-start(bf16[3,192,512]{2,1,0:T(8,128)(2,1)} %bitcast.21), channel_id=1, source_target_pairs={{1,32},{32,1},{3,34},{34,3},{5,36},{36,5},{7,38},{38,7},{9,40},{40... | collective-permute-start | bytes 1769480 | tf_op jit(solution)/shard_map/ppermute | solution.py:272
  5.8 0.7 convert_bitcast_fusion
  6.5 0.7 pad_add_fusion.small
  7.2 1.0 pad_maximum_fusion.1.wide
  8.2 1.0 shard_map.84
  9.2 3.1 %collective-permute-start = (bf16[160,512]{1,0:T(8,128)(2,1)S(1)}, bf16[160,512]{1,0:T(8,128)(2,1)}, u32[]{:S(2)}, u32[]{:S(2)}) collective-permute-start(bf16[160,512]{1,0:T(8,128)(2,1)S(1)} %get-tuple-element.48), channel_id=1, source_target_pairs={{0,8},{8,16},{16,24},{24,0},{1,9},{9,17},{17,25},{25,1},{2,10},{10... | collective-permute-start | bytes 491528 | tf_op jit(solution)/shard_map/ppermute | solution.py:230
  12.2 4.2 %collective-permute-start.1 = (bf16[160,512]{1,0:T(8,128)(2,1)S(1)}, bf16[160,512]{1,0:T(8,128)(2,1)}, u32[]{:S(2)}, u32[]{:S(2)}) collective-permute-start(bf16[160,512]{1,0:T(8,128)(2,1)S(1)} %get-tuple-element.49), channel_id=1, source_target_pairs={{0,16},{8,24},{16,0},{24,8},{1,17},{9,25},{17,1},{25,9},{2,18},{10... | collective-permute-start | bytes 491528 | tf_op jit(solution)/shard_map/ppermute | solution.py:230
  16.5 2.4 %collective-permute-start.2 = (bf16[160,512]{1,0:T(8,128)(2,1)S(1)}, bf16[160,512]{1,0:T(8,128)(2,1)S(1)}, u32[]{:S(2)}, u32[]{:S(2)}) collective-permute-start(bf16[160,512]{1,0:T(8,128)(2,1)S(1)} %get-tuple-element.50), channel_id=1, source_target_pairs={{0,24},{8,0},{16,8},{24,16},{1,25},{9,1},{17,9},{25,17},{2,26},{10... | collective-permute-start | bytes 491528 | tf_op jit(solution)/shard_map/ppermute | solution.py:230
  18.9 2.6 %collective-permute-start.5 = (bf16[3,192,512]{2,1,0:T(8,128)(2,1)S(1)}, bf16[3,192,512]{2,1,0:T(8,128)(2,1)S(1)}, u32[]{:S(2)}, u32[]{:S(2)}) collective-permute-start(bf16[3,192,512]{2,1,0:T(8,128)(2,1)S(1)} %broadcast_select_fusion.2.refs_4_), channel_id=1, source_target_pairs={{0,192},{64,0},{128,64},{192,128},{1,193},{65,1},{129,65},{193,129... | collective-permute-start | bytes 1769480 | tf_op jit(solution)/shard_map/ppermute | solution.py:230
  21.5 7.4 %collective-permute-done = bf16[160,512]{1,0:T(8,128)(2,1)} collective-permute-done((bf16[160,512]{1,0:T(8,128)(2,1)S(1)}, bf16[160,512]{1,0:T(8,128)(2,1)}, u32[]{:S(2)}, u32[]{:S(2)}) %collective-permute-start) | collective-permute-done | bytes 163872 | tf_op jit(solution)/shard_map/ppermute | solution.py:230
  28.9 0.9 constant_dynamic-update-slice_fusion.2
  29.9 1.8 %collective-permute-done.1 = bf16[160,512]{1,0:T(8,128)(2,1)} collective-permute-done((bf16[160,512]{1,0:T(8,128)(2,1)S(1)}, bf16[160,512]{1,0:T(8,128)(2,1)}, u32[]{:S(2)}, u32[]{:S(2)}) %collective-permute-start.1) | collective-permute-done | bytes 163872 | tf_op jit(solution)/shard_map/ppermute | solution.py:230
  31.7 0.9 constant_dynamic-update-slice_fusion.1
  32.6 2.8 %collective-permute-start.7 = (bf16[640,512]{1,0:T(8,128)(2,1)S(1)}, bf16[640,512]{1,0:T(8,128)(2,1)S(1)}, u32[]{:S(2)}, u32[]{:S(2)}) collective-permute-start(bf16[640,512]{1,0:T(8,128)(2,1)S(1)} %constant_dynamic-update-slice_fusion.refs_0_), channel_id=1, source_target_pairs={{0,6},{2,0},{4,2},{6,4},{1,7},{3,1},{5,3},{7,5},{8,14},{10,8},{12,... | collective-permute-start | bytes 1966088 | tf_op jit(solution)/shard_map/ppermute | solution.py:230
  35.5 2.3 %collective-permute-done.4.refs_5_ = bf16[3,192,512]{2,1,0:T(8,128)(2,1)} collective-permute-done((bf16[3,192,512]{2,1,0:T(8,128)(2,1)S(1)}, bf16[3,192,512]{2,1,0:T(8,128)(2,1)}, u32[]{:S(2)}, u32[]{:S(2)}) %collective-permute-start.4) | collective-permute-done | bytes 589856 | tf_op jit(solution)/shard_map/ppermute | solution.py:230
  38.1 9.9 %collective-permute-done.7.refs_3_ = bf16[640,512]{1,0:T(8,128)(2,1)S(1)} collective-permute-done((bf16[640,512]{1,0:T(8,128)(2,1)S(1)}, bf16[640,512]{1,0:T(8,128)(2,1)S(1)}, u32[]{:S(2)}, u32[]{:S(2)}) %collective-permute-start.7) | collective-permute-done | bytes 655392 | tf_op jit(solution)/shard_map/ppermute | solution.py:230
  48.0 3.4 %collective-permute-done.6.refs_1_ = bf16[640,512]{1,0:T(8,128)(2,1)S(1)} collective-permute-done((bf16[640,512]{1,0:T(8,128)(2,1)S(1)}, bf16[640,512]{1,0:T(8,128)(2,1)S(1)}, u32[]{:S(2)}, u32[]{:S(2)}) %collective-permute-start.6) | collective-permute-done | bytes 655392 | tf_op jit(solution)/shard_map/ppermute | solution.py:230
  52.6 1.0 collective-permute-done.10.refs_8_
  53.6 1.9 %collective-permute-done.11.refs_9_ = bf16[3,192,512]{2,1,0:T(8,128)(2,1)S(1)} collective-permute-done((bf16[3,192,512]{2,1,0:T(8,128)(2,1)}, bf16[3,192,512]{2,1,0:T(8,128)(2,1)S(1)}, u32[]{:S(2)}, u32[]{:S(2)}) %collective-permute-start.11) | collective-permute-done | bytes 589856 | tf_op jit(solution)/shard_map/ppermute | solution.py:241
  55.5 5.7 %collective-permute-done.8.refs_2_ = bf16[640,512]{1,0:T(8,128)(2,1)S(1)} collective-permute-done((bf16[640,512]{1,0:T(8,128)(2,1)S(1)}, bf16[640,512]{1,0:T(8,128)(2,1)S(1)}, u32[]{:S(2)}, u32[]{:S(2)}) %collective-permute-start.8) | collective-permute-done | bytes 655392 | tf_op jit(solution)/shard_map/ppermute | solution.py:237
  61.3 0.8 copy-done.4
  62.1 4.4 %shard_map.85 = (bf16[320,768]{1,0:T(8,128)(2,1)S(1)}, bf16[768,2048]{1,0:T(8,128)(2,1)}) custom-call(s32[5]{0:T(128)S(1)} %stack.23.place, bf16[640,512]{1,0:T(8,128)(2,1)S(1)} %constant_dynamic-update-slice_fusion.refs_0_, bf16[640,512]{1,0:T(8,128)(2,1)} %copy-done.2, bf16[640,512]{1,0:T(8,128)(2,1)} %copy-done.4, bf16[640,512]{1,0:T(8,128)(2,1)} %copy-done, ...), custom_call_target="tpu_custom_call" | custom-call | tf_op jit(solution)/shard_map/pallas_call | solution.py:33
  66.8 3.8 %shard_map.86 = (bf16[320,384]{1,0:T(8,128)(2,1)S(1)}, bf16[384,2048]{1,0:T(8,128)(2,1)}) custom-call(s32[5]{0:T(128)S(1)} %stack.23.place, bf16[640,512]{1,0:T(8,128)(2,1)S(1)} %constant_dynamic-update-slice_fusion.refs_0_, bf16[640,512]{1,0:T(8,128)(2,1)} %copy-done.2, bf16[640,512]{1,0:T(8,128)(2,1)} %copy-done.4, bf16[640,512]{1,0:T(8,128)(2,1)} %copy-done, ...), custom_call_target="tpu_custom_call" | custom-call | tf_op jit(solution)/shard_map/pallas_call | solution.py:33
  70.6 1.5 %collective-permute-start.15 = (bf16[320,384]{1,0:T(8,128)(2,1)S(1)}, bf16[320,384]{1,0:T(8,128)(2,1)S(1)}, u32[]{:S(2)}, u32[]{:S(2)}) collective-permute-start(bf16[320,384]{1,0:T(8,128)(2,1)S(1)} %get-tuple-element.57.down), channel_id=1, source_target_pairs={{0,1},{1,0},{2,3},{3,2},{4,5},{5,4},{6,7},{7,6},{8,9},{9,8},{10,11... | collective-permute-start | bytes 737288 | tf_op jit(solution)/shard_map/ppermute | solution.py:241
  72.1 11.7 %collective-permute-done.15.down_far = bf16[320,384]{1,0:T(8,128)(2,1)S(1)} collective-permute-done((bf16[320,384]{1,0:T(8,128)(2,1)S(1)}, bf16[320,384]{1,0:T(8,128)(2,1)S(1)}, u32[]{:S(2)}, u32[]{:S(2)}) %collective-permute-start.15) | collective-permute-done | bytes 245792 | tf_op jit(solution)/shard_map/ppermute | solution.py:241
  83.9 4.6 %shard_map.87 = (f32[656,512]{1,0:T(8,128)S(1)}, bf16[656,512]{1,0:T(8,128)(2,1)S(1)}, bf16[656,512]{1,0:T(8,128)(2,1)S(1)}, bf16[656,512]{1,0:T(8,128)(2,1)S(1)}, bf16[320,1152]{1,0:T(8,128)(2,1)S(1)}) custom-call(s32[5]{0:T(128)S(1)} %stack.23.place, bf16[320,768]{1,0:T(8,128)(2,1)S(1)} %get-tuple-element.56.pair, ...), custom_call_target="tpu_custom_call" | custom-call | tf_op jit(solution)/shard_map/pallas_call | solution.py:33
  88.5 1.9 %collective-permute-start.16 = (bf16[656,512]{1,0:T(8,128)(2,1)S(1)}, bf16[656,512]{1,0:T(8,128)(2,1)S(1)}, u32[]{:S(2)}, u32[]{:S(2)}) collective-permute-start(bf16[656,512]{1,0:T(8,128)(2,1)S(1)} %get-tuple-element.63), channel_id=1, source_target_pairs={{0,2},{2,4},{4,6},{6,0},{32,38},{34,32},{36,34},{38,36},{1,3},{3,5... | collective-permute-start | bytes 2015240 | tf_op jit(solution)/shard_map/ppermute | solution.py:237
  90.3 4.6 %shard_map.88 = (f32[3,192,512]{2,1,0:T(8,128)}, f32[3,192,512]{2,1,0:T(8,128)}, f32[3,192,512]{2,1,0:T(8,128)}, f32[3,192,512]{2,1,0:T(8,128)}, bf16[3,192,512]...) custom-call(s32[5]{0:T(128)S(1)} %stack.23.place, ...), custom_call_target="tpu_custom_call" | custom-call | tf_op jit(solution)/shard_map/pallas_call | solution.py:33
  96.0 2.5 %collective-permute-done.16 = bf16[656,512]{1,0:T(8,128)(2,1)S(1)} collective-permute-done((bf16[656,512]{1,0:T(8,128)(2,1)S(1)}, bf16[656,512]{1,0:T(8,128)(2,1)S(1)}, u32[]{:S(2)}, u32[]{:S(2)}) %collective-permute-start.16) | collective-permute-done | bytes 671776 | tf_op jit(solution)/shard_map/ppermute | solution.py:237
  98.9 0.6 collective-permute-done.20
  99.9 2.5 %collective-permute-start.21 = (bf16[3,192,512]{2,1,0:T(8,128)(2,1)S(1)}, bf16[3,192,512]{2,1,0:T(8,128)(2,1)S(1)}, u32[]{:S(2)}, u32[]{:S(2)}) collective-permute-start(bf16[3,192,512]{2,1,0:T(8,128)(2,1)S(1)} %add_convert_fusion.1), channel_id=1, source_target_pairs={{0,64},{64,128},{128,192},{192,0},{32,224},{96,32},{160,96},{224,1... | collective-permute-start | bytes 1769480 | tf_op jit(solution)/shard_map/ppermute | solution.py:236
  102.5 2.8 %collective-permute-start.26 = (bf16[656,512]{1,0:T(8,128)(2,1)S(1)}, bf16[656,512]{1,0:T(8,128)(2,1)S(1)}, u32[]{:S(2)}, u32[]{:S(2)}) collective-permute-start(bf16[656,512]{1,0:T(8,128)(2,1)S(1)} %get-tuple-element.78), channel_id=1, source_target_pairs={{0,6},{2,0},{4,2},{6,4},{1,7},{3,1},{5,3},{7,5},{8,14},{10,8},{12,... | collective-permute-start | bytes 2015240 | tf_op jit(solution)/shard_map/ppermute | solution.py:230
  105.2 4.1 %collective-permute-done.21 = bf16[3,192,512]{2,1,0:T(8,128)(2,1)S(1)} collective-permute-done((bf16[3,192,512]{2,1,0:T(8,128)(2,1)S(1)}, bf16[3,192,512]{2,1,0:T(8,128)(2,1)S(1)}, u32[]{:S(2)}, u32[]{:S(2)}) %collective-permute-start.21) | collective-permute-done | bytes 589856 | tf_op jit(solution)/shard_map/ppermute | solution.py:236
  109.3 0.5 fusion.5
  109.8 3.7 %collective-permute-start.22 = (bf16[3,192,512]{2,1,0:T(8,128)(2,1)S(1)}, bf16[3,192,512]{2,1,0:T(8,128)(2,1)S(1)}, u32[]{:S(2)}, u32[]{:S(2)}) collective-permute-start(bf16[3,192,512]{2,1,0:T(8,128)(2,1)S(1)} %get-tuple-element.94), channel_id=1, source_target_pairs={{0,192},{64,0},{128,64},{192,128},{1,193},{65,1},{129,65},{193,129... | collective-permute-start | bytes 1769480 | tf_op jit(solution)/shard_map/ppermute | solution.py:230
  113.5 6.3 %collective-permute-done.26.one = bf16[656,512]{1,0:T(8,128)(2,1)S(1)} collective-permute-done((bf16[656,512]{1,0:T(8,128)(2,1)S(1)}, bf16[656,512]{1,0:T(8,128)(2,1)S(1)}, u32[]{:S(2)}, u32[]{:S(2)}) %collective-permute-start.26) | collective-permute-done | bytes 671776 | tf_op jit(solution)/shard_map/ppermute | solution.py:230
  119.9 3.1 %collective-permute-done.27.three = bf16[656,512]{1,0:T(8,128)(2,1)S(1)} collective-permute-done((bf16[656,512]{1,0:T(8,128)(2,1)S(1)}, bf16[656,512]{1,0:T(8,128)(2,1)S(1)}, u32[]{:S(2)}, u32[]{:S(2)}) %collective-permute-start.27) | collective-permute-done | bytes 671776 | tf_op jit(solution)/shard_map/ppermute | solution.py:230
  123.0 0.8 shard_map.89
  123.7 1.3 collective-permute-start.28
  125.1 2.4 %collective-permute-start.29 = (bf16[176,512]{1,0:T(8,128)(2,1)S(1)}, bf16[176,512]{1,0:T(8,128)(2,1)S(1)}, u32[]{:S(2)}, u32[]{:S(2)}) collective-permute-start(bf16[176,512]{1,0:T(8,128)(2,1)S(1)} %get-tuple-element.82), channel_id=1, source_target_pairs={{0,16},{8,24},{16,0},{24,8},{1,17},{9,25},{17,1},{25,9},{2,18},{10... | collective-permute-start | bytes 540680 | tf_op jit(solution)/shard_map/ppermute | solution.py:230
  128.0 5.0 %collective-permute-start.25 = (bf16[288,512]{1,0:T(8,128)(2,1)S(1)}, bf16[288,512]{1,0:T(8,128)(2,1)S(1)}, u32[]{:S(2)}, u32[]{:S(2)}) collective-permute-start(bf16[288,512]{1,0:T(8,128)(2,1)S(1)} %get-tuple-element.92), channel_id=1, source_target_pairs={{0,0},{1,32},{32,1},{33,33},{2,2},{3,34},{34,3},{35,35},{4,4},{5,3... | collective-permute-start | bytes 884744 | tf_op jit(solution)/shard_map/ppermute | solution.py:245
  133.0 1.9 %collective-permute-start.24 = (bf16[288,512]{1,0:T(8,128)(2,1)S(1)}, bf16[288,512]{1,0:T(8,128)(2,1)S(1)}, u32[]{:S(2)}, u32[]{:S(2)}) collective-permute-start(bf16[288,512]{1,0:T(8,128)(2,1)S(1)} %get-tuple-element.93), channel_id=1, source_target_pairs={{0,0},{1,32},{32,1},{33,33},{2,2},{3,34},{34,3},{35,35},{4,4},{5,3... | collective-permute-start | bytes 884744 | tf_op jit(solution)/shard_map/ppermute | solution.py:245
  134.9 4.5 %collective-permute-done.28.refs_1_ = bf16[176,512]{1,0:T(8,128)(2,1)S(1)} collective-permute-done((bf16[176,512]{1,0:T(8,128)(2,1)S(1)}, bf16[176,512]{1,0:T(8,128)(2,1)S(1)}, u32[]{:S(2)}, u32[]{:S(2)}) %collective-permute-start.28) | collective-permute-done | bytes 180256 | tf_op jit(solution)/shard_map/ppermute | solution.py:230
  139.4 5.8 %collective-permute-done.30.refs_3_ = bf16[176,512]{1,0:T(8,128)(2,1)S(1)} collective-permute-done((bf16[176,512]{1,0:T(8,128)(2,1)S(1)}, bf16[176,512]{1,0:T(8,128)(2,1)S(1)}, u32[]{:S(2)}, u32[]{:S(2)}) %collective-permute-start.30) | collective-permute-done | bytes 180256 | tf_op jit(solution)/shard_map/ppermute | solution.py:230
  145.2 1.7 %shard_map.90 = (bf16[128,512]{1,0:T(8,128)(2,1)}, bf16[128,512]{1,0:T(8,128)(2,1)}, f32[8,128]{1,0:T(8,128)S(1)}) custom-call(s32[5]{0:T(128)S(1)} %stack.23.place, f32[4,128]{1,0:T(4,128)S(1)} %pad_add_fusion.small, bf16[320,128]{1,0:T(8,128)(2,1)S(1)} %get-tuple-element.76.placing, bf16[176,512]{1,0:T(8,128)(2,1)S(1)} %get-tuple-element.80.refs_0_, ...), custom_call_target="tpu_custom_call" | custom-call | tf_op jit(solution)/shard_map/pallas_call | solution.py:33
  146.9 0.6 slice_bitcast_fusion.2
  147.5 2.3 %collective-permute-done.24 = bf16[288,512]{1,0:T(8,128)(2,1)S(1)} collective-permute-done((bf16[288,512]{1,0:T(8,128)(2,1)S(1)}, bf16[288,512]{1,0:T(8,128)(2,1)S(1)}, u32[]{:S(2)}, u32[]{:S(2)}) %collective-permute-start.24) | collective-permute-done | bytes 294944 | tf_op jit(solution)/shard_map/ppermute | solution.py:245
  149.8 1.2 convert.2
  (62 shorter events, 4.6 us)
Async XLA Ops:
  0.6 18.2 %copy-start.10 = (bf16[1,3,192,512]{3,2,1,0:T(8,128)(2,1)S(1)}, bf16[1,3,192,512]{3,2,1,0:T(8,128)(2,1)}, u32[]{:S(2)}) copy-start(bf16[1,3,192,512]{3,2,1,0:T(8,128)(2,1)} %param.8) | copy-start | bytes 1769476
  0.6 18.2 %collective-permute-start.3 = (bf16[3,192,512]{2,1,0:T(8,128)(2,1)}, bf16[3,192,512]{2,1,0:T(8,128)(2,1)S(1)}, u32[]{:S(2)}, u32[]{:S(2)}) collective-permute-start(bf16[3,192,512]{2,1,0:T(8,128)(2,1)} %bitcast.21), channel_id=1, source_target_pairs={{1,32},{32,1},{3,34},{34,3},{5,36},{36,5},{7,38},{38,7},{9,40},{40... | collective-permute-start | bytes 1769480 | tf_op jit(solution)/shard_map/ppermute | solution.py:272
  9.2 19.8 %collective-permute-start = (bf16[160,512]{1,0:T(8,128)(2,1)S(1)}, bf16[160,512]{1,0:T(8,128)(2,1)}, u32[]{:S(2)}, u32[]{:S(2)}) collective-permute-start(bf16[160,512]{1,0:T(8,128)(2,1)S(1)} %get-tuple-element.48), channel_id=1, source_target_pairs={{0,8},{8,16},{16,24},{24,0},{1,9},{9,17},{17,25},{25,1},{2,10},{10... | collective-permute-start | bytes 491528 | tf_op jit(solution)/shard_map/ppermute | solution.py:230
  12.2 19.4 %collective-permute-start.1 = (bf16[160,512]{1,0:T(8,128)(2,1)S(1)}, bf16[160,512]{1,0:T(8,128)(2,1)}, u32[]{:S(2)}, u32[]{:S(2)}) collective-permute-start(bf16[160,512]{1,0:T(8,128)(2,1)S(1)} %get-tuple-element.49), channel_id=1, source_target_pairs={{0,16},{8,24},{16,0},{24,8},{1,17},{9,25},{17,1},{25,9},{2,18},{10... | collective-permute-start | bytes 491528 | tf_op jit(solution)/shard_map/ppermute | solution.py:230
  16.5 16.1 %collective-permute-start.2 = (bf16[160,512]{1,0:T(8,128)(2,1)S(1)}, bf16[160,512]{1,0:T(8,128)(2,1)S(1)}, u32[]{:S(2)}, u32[]{:S(2)}) collective-permute-start(bf16[160,512]{1,0:T(8,128)(2,1)S(1)} %get-tuple-element.50), channel_id=1, source_target_pairs={{0,24},{8,0},{16,8},{24,16},{1,25},{9,1},{17,9},{25,17},{2,26},{10... | collective-permute-start | bytes 491528 | tf_op jit(solution)/shard_map/ppermute | solution.py:230
  18.9 16.5 %collective-permute-start.5 = (bf16[3,192,512]{2,1,0:T(8,128)(2,1)S(1)}, bf16[3,192,512]{2,1,0:T(8,128)(2,1)S(1)}, u32[]{:S(2)}, u32[]{:S(2)}) collective-permute-start(bf16[3,192,512]{2,1,0:T(8,128)(2,1)S(1)} %broadcast_select_fusion.2.refs_4_), channel_id=1, source_target_pairs={{0,192},{64,0},{128,64},{192,128},{1,193},{65,1},{129,65},{193,129... | collective-permute-start | bytes 1769480 | tf_op jit(solution)/shard_map/ppermute | solution.py:230
  21.5 16.3 %collective-permute-start.4 = (bf16[3,192,512]{2,1,0:T(8,128)(2,1)S(1)}, bf16[3,192,512]{2,1,0:T(8,128)(2,1)}, u32[]{:S(2)}, u32[]{:S(2)}) collective-permute-start(bf16[3,192,512]{2,1,0:T(8,128)(2,1)S(1)} %broadcast_select_fusion.2.refs_4_), channel_id=1, source_target_pairs={{0,64},{64,128},{128,192},{192,0},{1,65},{65,129},{129,193},{193,1... | collective-permute-start | bytes 1769480 | tf_op jit(solution)/shard_map/ppermute | solution.py:230
  32.6 15.3 %collective-permute-start.7 = (bf16[640,512]{1,0:T(8,128)(2,1)S(1)}, bf16[640,512]{1,0:T(8,128)(2,1)S(1)}, u32[]{:S(2)}, u32[]{:S(2)}) collective-permute-start(bf16[640,512]{1,0:T(8,128)(2,1)S(1)} %constant_dynamic-update-slice_fusion.refs_0_), channel_id=1, source_target_pairs={{0,6},{2,0},{4,2},{6,4},{1,7},{3,1},{5,3},{7,5},{8,14},{10,8},{12,... | collective-permute-start | bytes 1966088 | tf_op jit(solution)/shard_map/ppermute | solution.py:230
  35.4 15.9 %collective-permute-start.6 = (bf16[640,512]{1,0:T(8,128)(2,1)S(1)}, bf16[640,512]{1,0:T(8,128)(2,1)S(1)}, u32[]{:S(2)}, u32[]{:S(2)}) collective-permute-start(bf16[640,512]{1,0:T(8,128)(2,1)S(1)} %constant_dynamic-update-slice_fusion.refs_0_), channel_id=1, source_target_pairs={{0,2},{2,4},{4,6},{6,0},{1,3},{3,5},{5,7},{7,1},{8,10},{10,12},{12... | collective-permute-start | bytes 1966088 | tf_op jit(solution)/shard_map/ppermute | solution.py:230
  37.8 14.4 %collective-permute-start.9 = (bf16[3,192,512]{2,1,0:T(8,128)(2,1)S(1)}, bf16[3,192,512]{2,1,0:T(8,128)(2,1)S(1)}, u32[]{:S(2)}, u32[]{:S(2)}) collective-permute-start(bf16[3,192,512]{2,1,0:T(8,128)(2,1)S(1)} %broadcast_select_fusion.1), channel_id=1, source_target_pairs={{0,64},{64,128},{128,192},{192,0},{32,224},{96,32},{160,96},{224,1... | collective-permute-start | bytes 1769480 | tf_op jit(solution)/shard_map/ppermute | solution.py:236
  48.0 13.3 %copy-start = (bf16[640,512]{1,0:T(8,128)(2,1)}, bf16[640,512]{1,0:T(8,128)(2,1)S(1)}, u32[]{:S(2)}) copy-start(bf16[640,512]{1,0:T(8,128)(2,1)S(1)} %collective-permute-done.7.refs_3_) | copy-start | bytes 1966084
  51.4 9.9 %copy-start.2 = (bf16[640,512]{1,0:T(8,128)(2,1)}, bf16[640,512]{1,0:T(8,128)(2,1)S(1)}, u32[]{:S(2)}) copy-start(bf16[640,512]{1,0:T(8,128)(2,1)S(1)} %collective-permute-done.6.refs_1_) | copy-start | bytes 1966084
  51.4 9.8 %collective-permute-start.8 = (bf16[640,512]{1,0:T(8,128)(2,1)S(1)}, bf16[640,512]{1,0:T(8,128)(2,1)S(1)}, u32[]{:S(2)}, u32[]{:S(2)}) collective-permute-start(bf16[640,512]{1,0:T(8,128)(2,1)S(1)} %broadcast_select_fusion), channel_id=1, source_target_pairs={{0,2},{2,4},{4,6},{6,0},{32,38},{34,32},{36,34},{38,36},{1,3},{3,5... | collective-permute-start | bytes 1966088 | tf_op jit(solution)/shard_map/ppermute | solution.py:237
  51.5 2.1 %collective-permute-start.10 = (bf16[3,192,512]{2,1,0:T(8,128)(2,1)S(1)}, bf16[3,192,512]{2,1,0:T(8,128)(2,1)S(1)}, u32[]{:S(2)}, u32[]{:S(2)}) collective-permute-start(bf16[3,192,512]{2,1,0:T(8,128)(2,1)S(1)} %broadcast_select_fusion.2.refs_4_), channel_id=1, source_target_pairs={{0,32},{32,0},{1,33},{33,1},{2,34},{34,2},{3,35},{35,3},{4,36},{36... | collective-permute-start | bytes 1769480 | tf_op jit(solution)/shard_map/ppermute | solution.py:241
  51.6 3.9 %collective-permute-start.11 = (bf16[3,192,512]{2,1,0:T(8,128)(2,1)}, bf16[3,192,512]{2,1,0:T(8,128)(2,1)S(1)}, u32[]{:S(2)}, u32[]{:S(2)}) collective-permute-start(bf16[3,192,512]{2,1,0:T(8,128)(2,1)} %collective-permute-done.4.refs_5_), channel_id=1, source_target_pairs={{0,32},{32,0},{1,33},{33,1},{2,34},{34,2},{3,35},{35,3},{4,36},{36... | collective-permute-start | bytes 1769480 | tf_op jit(solution)/shard_map/ppermute | solution.py:241
  52.1 3.4 %collective-permute-start.13 = (bf16[3,192,512]{2,1,0:T(8,128)(2,1)S(1)}, bf16[3,192,512]{2,1,0:T(8,128)(2,1)S(1)}, u32[]{:S(2)}, u32[]{:S(2)}) collective-permute-start(bf16[3,192,512]{2,1,0:T(8,128)(2,1)S(1)} %collective-permute-done.5.refs_7_), channel_id=1, source_target_pairs={{0,32},{32,0},{1,33},{33,1},{2,34},{34,2},{3,35},{35,3},{4,36},{36... | collective-permute-start | bytes 1769480 | tf_op jit(solution)/shard_map/ppermute | solution.py:241
  52.2 9.0 %collective-permute-start.12 = (bf16[3,192,512]{2,1,0:T(8,128)(2,1)S(1)}, bf16[3,192,512]{2,1,0:T(8,128)(2,1)S(1)}, u32[]{:S(2)}, u32[]{:S(2)}) collective-permute-start(bf16[3,192,512]{2,1,0:T(8,128)(2,1)S(1)} %collective-permute-done.9.refs_6_), channel_id=1, source_target_pairs={{0,32},{32,0},{1,33},{33,1},{2,34},{34,2},{3,35},{35,3},{4,36},{36... | collective-permute-start | bytes 1769480 | tf_op jit(solution)/shard_map/ppermute | solution.py:241
  61.2 0.9 copy-start.4
  66.5 17.3 %collective-permute-start.14 = (bf16[320,768]{1,0:T(8,128)(2,1)S(1)}, bf16[320,768]{1,0:T(8,128)(2,1)S(1)}, u32[]{:S(2)}, u32[]{:S(2)}) collective-permute-start(bf16[320,768]{1,0:T(8,128)(2,1)S(1)} %get-tuple-element.56.pair), channel_id=1, source_target_pairs={{0,1},{1,0},{2,3},{3,2},{4,5},{5,4},{6,7},{7,6},{8,9},{9,8},{10,11... | collective-permute-start | bytes 1474568 | tf_op jit(solution)/shard_map/ppermute | solution.py:241
  70.6 13.3 %collective-permute-start.15 = (bf16[320,384]{1,0:T(8,128)(2,1)S(1)}, bf16[320,384]{1,0:T(8,128)(2,1)S(1)}, u32[]{:S(2)}, u32[]{:S(2)}) collective-permute-start(bf16[320,384]{1,0:T(8,128)(2,1)S(1)} %get-tuple-element.57.down), channel_id=1, source_target_pairs={{0,1},{1,0},{2,3},{3,2},{4,5},{5,4},{6,7},{7,6},{8,9},{9,8},{10,11... | collective-permute-start | bytes 737288 | tf_op jit(solution)/shard_map/ppermute | solution.py:241
  83.9 6.5 %copy-start.1 = (bf16[640,512]{1,0:T(8,128)(2,1)S(1)}, bf16[640,512]{1,0:T(8,128)(2,1)}, u32[]{:S(2)}) copy-start(bf16[640,512]{1,0:T(8,128)(2,1)} %copy-done) | copy-start | bytes 1966084
  83.9 6.5 %copy-start.3 = (bf16[640,512]{1,0:T(8,128)(2,1)S(1)}, bf16[640,512]{1,0:T(8,128)(2,1)}, u32[]{:S(2)}) copy-start(bf16[640,512]{1,0:T(8,128)(2,1)} %copy-done.2) | copy-start | bytes 1966084
  83.9 6.5 %copy-start.5 = (bf16[640,512]{1,0:T(8,128)(2,1)S(1)}, bf16[640,512]{1,0:T(8,128)(2,1)}, u32[]{:S(2)}) copy-start(bf16[640,512]{1,0:T(8,128)(2,1)} %copy-done.4) | copy-start | bytes 1966084
  88.5 10.0 %collective-permute-start.16 = (bf16[656,512]{1,0:T(8,128)(2,1)S(1)}, bf16[656,512]{1,0:T(8,128)(2,1)S(1)}, u32[]{:S(2)}, u32[]{:S(2)}) collective-permute-start(bf16[656,512]{1,0:T(8,128)(2,1)S(1)} %get-tuple-element.63), channel_id=1, source_target_pairs={{0,2},{2,4},{4,6},{6,0},{32,38},{34,32},{36,34},{38,36},{1,3},{3,5... | collective-permute-start | bytes 2015240 | tf_op jit(solution)/shard_map/ppermute | solution.py:237
  94.9 3.9 %collective-permute-start.17 = (bf16[3,192,512]{2,1,0:T(8,128)(2,1)S(1)}, bf16[3,192,512]{2,1,0:T(8,128)(2,1)S(1)}, u32[]{:S(2)}, u32[]{:S(2)}) collective-permute-start(bf16[3,192,512]{2,1,0:T(8,128)(2,1)S(1)} %get-tuple-element.65), channel_id=1, source_target_pairs={{0,32},{32,0},{1,33},{33,1},{2,34},{34,2},{3,35},{35,3},{4,36},{36... | collective-permute-start | bytes 1769480 | tf_op jit(solution)/shard_map/ppermute | solution.py:241
  95.0 3.8 %collective-permute-start.18 = (bf16[3,192,512]{2,1,0:T(8,128)(2,1)S(1)}, bf16[3,192,512]{2,1,0:T(8,128)(2,1)S(1)}, u32[]{:S(2)}, u32[]{:S(2)}) collective-permute-start(bf16[3,192,512]{2,1,0:T(8,128)(2,1)S(1)} %get-tuple-element.66), channel_id=1, source_target_pairs={{0,32},{32,0},{1,33},{33,1},{2,34},{34,2},{3,35},{35,3},{4,36},{36... | collective-permute-start | bytes 1769480 | tf_op jit(solution)/shard_map/ppermute | solution.py:241
  95.4 3.4 %collective-permute-start.19 = (bf16[3,192,512]{2,1,0:T(8,128)(2,1)S(1)}, bf16[3,192,512]{2,1,0:T(8,128)(2,1)S(1)}, u32[]{:S(2)}, u32[]{:S(2)}) collective-permute-start(bf16[3,192,512]{2,1,0:T(8,128)(2,1)S(1)} %get-tuple-element.67), channel_id=1, source_target_pairs={{0,32},{32,0},{1,33},{33,1},{2,34},{34,2},{3,35},{35,3},{4,36},{36... | collective-permute-start | bytes 1769480 | tf_op jit(solution)/shard_map/ppermute | solution.py:241
  95.5 4.0 %collective-permute-start.20 = (bf16[3,192,512]{2,1,0:T(8,128)(2,1)S(1)}, bf16[3,192,512]{2,1,0:T(8,128)(2,1)S(1)}, u32[]{:S(2)}, u32[]{:S(2)}) collective-permute-start(bf16[3,192,512]{2,1,0:T(8,128)(2,1)S(1)} %get-tuple-element.68), channel_id=1, source_target_pairs={{0,32},{32,0},{1,33},{33,1},{2,34},{34,2},{3,35},{35,3},{4,36},{36... | collective-permute-start | bytes 1769480 | tf_op jit(solution)/shard_map/ppermute | solution.py:241
  98.4 1.3 copy-start.7
  99.7 9.6 %copy-start.8 = (f32[3,192,512]{2,1,0:T(8,128)S(1)}, f32[3,192,512]{2,1,0:T(8,128)}, u32[]{:S(2)}) copy-start(f32[3,192,512]{2,1,0:T(8,128)} %get-tuple-element.70) | copy-start | bytes 3538948
  99.7 9.6 %copy-start.9 = (f32[3,192,512]{2,1,0:T(8,128)S(1)}, f32[3,192,512]{2,1,0:T(8,128)}, u32[]{:S(2)}) copy-start(f32[3,192,512]{2,1,0:T(8,128)} %get-tuple-element.74) | copy-start | bytes 3538948
  99.9 9.4 %collective-permute-start.21 = (bf16[3,192,512]{2,1,0:T(8,128)(2,1)S(1)}, bf16[3,192,512]{2,1,0:T(8,128)(2,1)S(1)}, u32[]{:S(2)}, u32[]{:S(2)}) collective-permute-start(bf16[3,192,512]{2,1,0:T(8,128)(2,1)S(1)} %add_convert_fusion.1), channel_id=1, source_target_pairs={{0,64},{64,128},{128,192},{192,0},{32,224},{96,32},{160,96},{224,1... | collective-permute-start | bytes 1769480 | tf_op jit(solution)/shard_map/ppermute | solution.py:236
  102.5 17.4 %collective-permute-start.26 = (bf16[656,512]{1,0:T(8,128)(2,1)S(1)}, bf16[656,512]{1,0:T(8,128)(2,1)S(1)}, u32[]{:S(2)}, u32[]{:S(2)}) collective-permute-start(bf16[656,512]{1,0:T(8,128)(2,1)S(1)} %get-tuple-element.78), channel_id=1, source_target_pairs={{0,6},{2,0},{4,2},{6,4},{1,7},{3,1},{5,3},{7,5},{8,14},{10,8},{12,... | collective-permute-start | bytes 2015240 | tf_op jit(solution)/shard_map/ppermute | solution.py:230
  105.2 17.7 %collective-permute-start.27 = (bf16[656,512]{1,0:T(8,128)(2,1)S(1)}, bf16[656,512]{1,0:T(8,128)(2,1)S(1)}, u32[]{:S(2)}, u32[]{:S(2)}) collective-permute-start(bf16[656,512]{1,0:T(8,128)(2,1)S(1)} %get-tuple-element.79), channel_id=1, source_target_pairs={{0,2},{2,4},{4,6},{6,0},{1,3},{3,5},{5,7},{7,1},{8,10},{10,12},{12... | collective-permute-start | bytes 2015240 | tf_op jit(solution)/shard_map/ppermute | solution.py:230
  109.8 17.8 %collective-permute-start.22 = (bf16[3,192,512]{2,1,0:T(8,128)(2,1)S(1)}, bf16[3,192,512]{2,1,0:T(8,128)(2,1)S(1)}, u32[]{:S(2)}, u32[]{:S(2)}) collective-permute-start(bf16[3,192,512]{2,1,0:T(8,128)(2,1)S(1)} %get-tuple-element.94), channel_id=1, source_target_pairs={{0,192},{64,0},{128,64},{192,128},{1,193},{65,1},{129,65},{193,129... | collective-permute-start | bytes 1769480 | tf_op jit(solution)/shard_map/ppermute | solution.py:230
  113.5 14.1 %collective-permute-start.23 = (bf16[3,192,512]{2,1,0:T(8,128)(2,1)S(1)}, bf16[3,192,512]{2,1,0:T(8,128)(2,1)S(1)}, u32[]{:S(2)}, u32[]{:S(2)}) collective-permute-start(bf16[3,192,512]{2,1,0:T(8,128)(2,1)S(1)} %get-tuple-element.95), channel_id=1, source_target_pairs={{0,64},{64,128},{128,192},{192,0},{1,65},{65,129},{129,193},{193,1... | collective-permute-start | bytes 1769480 | tf_op jit(solution)/shard_map/ppermute | solution.py:230
  123.0 4.7 %copy-start.6 = (f32[3,192,512]{2,1,0:T(8,128)S(1)}, f32[3,192,512]{2,1,0:T(8,128)}, u32[]{:S(2)}) copy-start(f32[3,192,512]{2,1,0:T(8,128)} %get-tuple-element.61) | copy-start | bytes 3538948
  123.7 15.7 %collective-permute-start.28 = (bf16[176,512]{1,0:T(8,128)(2,1)S(1)}, bf16[176,512]{1,0:T(8,128)(2,1)S(1)}, u32[]{:S(2)}, u32[]{:S(2)}) collective-permute-start(bf16[176,512]{1,0:T(8,128)(2,1)S(1)} %get-tuple-element.81), channel_id=1, source_target_pairs={{0,24},{8,0},{16,8},{24,16},{1,25},{9,1},{17,9},{25,17},{2,26},{10... | collective-permute-start | bytes 540680 | tf_op jit(solution)/shard_map/ppermute | solution.py:230
  125.1 14.4 %collective-permute-start.29 = (bf16[176,512]{1,0:T(8,128)(2,1)S(1)}, bf16[176,512]{1,0:T(8,128)(2,1)S(1)}, u32[]{:S(2)}, u32[]{:S(2)}) collective-permute-start(bf16[176,512]{1,0:T(8,128)(2,1)S(1)} %get-tuple-element.82), channel_id=1, source_target_pairs={{0,16},{8,24},{16,0},{24,8},{1,17},{9,25},{17,1},{25,9},{2,18},{10... | collective-permute-start | bytes 540680 | tf_op jit(solution)/shard_map/ppermute | solution.py:230
  127.4 17.8 %collective-permute-start.30 = (bf16[176,512]{1,0:T(8,128)(2,1)S(1)}, bf16[176,512]{1,0:T(8,128)(2,1)S(1)}, u32[]{:S(2)}, u32[]{:S(2)}) collective-permute-start(bf16[176,512]{1,0:T(8,128)(2,1)S(1)} %get-tuple-element.83), channel_id=1, source_target_pairs={{0,8},{8,16},{16,24},{24,0},{1,9},{9,17},{17,25},{25,1},{2,10},{10... | collective-permute-start | bytes 540680 | tf_op jit(solution)/shard_map/ppermute | solution.py:230
  128.0 19.4 %collective-permute-start.25 = (bf16[288,512]{1,0:T(8,128)(2,1)S(1)}, bf16[288,512]{1,0:T(8,128)(2,1)S(1)}, u32[]{:S(2)}, u32[]{:S(2)}) collective-permute-start(bf16[288,512]{1,0:T(8,128)(2,1)S(1)} %get-tuple-element.92), channel_id=1, source_target_pairs={{0,0},{1,32},{32,1},{33,33},{2,2},{3,34},{34,3},{35,35},{4,4},{5,3... | collective-permute-start | bytes 884744 | tf_op jit(solution)/shard_map/ppermute | solution.py:245
  133.0 16.7 %collective-permute-start.24 = (bf16[288,512]{1,0:T(8,128)(2,1)S(1)}, bf16[288,512]{1,0:T(8,128)(2,1)S(1)}, u32[]{:S(2)}, u32[]{:S(2)}) collective-permute-start(bf16[288,512]{1,0:T(8,128)(2,1)S(1)} %get-tuple-element.93), channel_id=1, source_target_pairs={{0,0},{1,32},{32,1},{33,33},{2,2},{3,34},{34,3},{35,35},{4,4},{5,3... | collective-permute-start | bytes 884744 | tf_op jit(solution)/shard_map/ppermute | solution.py:245

commit v11 on v10

--- a/solution.py
+++ b/solution.py
@@ -242,7 +242,13 @@
 
 
 def turn(value):
-    return lax.ppermute(value, ("core", "zl"), [(2 * c + z, 2 * z + c) for c in range(2) for z in range(2)])
+    return lax.ppermute(value, ("core", "zl"), [(1, 2), (2, 1)])
+
+
+def home(value, step):
+    places = [(x, c, z) for x in range(4) for c in range(2) for z in range(2)]
+    perm = [(4 * x + 2 * c + z, 4 * ((x + step) % 4) + 2 * z + c) for x, c, z in places]
+    return lax.ppermute(value, ("x", "core", "zl"), perm)
 
 
 def body(tokens, expert_ids, gate_probs, stacked_weights, out_grad):
@@ -269,7 +275,7 @@
 
     blocks = [blocks[0]] + [shift(blocks[k], "expert", k) for k in (1, 2, 3)]
     own = stacked_weights[0]
-    turned = lax.ppermute(own, ("core", "zl"), [(1, 2), (2, 1)])
+    turned = turn(own)
     own = jnp.where(place[4] == place[3], own, turned)
     first = lax.axis_index("core") == 0
     near, back = shift(own, "x", 1), shift(own, "x", 3)
@@ -331,7 +337,10 @@
 
     passed = relay(both_cores(2).astype(BF16), "x")
     near, back = halfway(passed, both_cores(1), both_cores(3))
-    far_sums = [shift(near, "x", -1), shift(back, "x", 1)]
+    far_sums = [home(near, -1), home(back, 1)]
+    mine_sum = both_cores(0)
+    turned_sum = turn(mine_sum.astype(BF16))
+    turned_sum, *arrived = lax.optimization_barrier((turned_sum, *arrived))
     totals = call(total_kernel, place, [shares[0]] + arrived, [((unit, width), BF16)] * 4)
     returned = [totals[0]] + [shift(totals[k], "expert", -k) for k in (1, 2, 3)]
     layer_output, token_grad, prob_grad = call(
@@ -340,14 +349,10 @@
         [small, placing] + returned,
         [((rows, width), BF16), ((rows, width), BF16), ((8, rows), F32)],
     )
-    weight_total = both_cores(0)
+    weight_total = jnp.where(place[4] == place[3], mine_sum, turned_sum.astype(F32))
     for block in far_sums:
         weight_total = weight_total + block.astype(F32)
-    weight_total = weight_total.astype(BF16).reshape(2, 3 * half // 2, width)
-    parts = [turn(weight_total[n]) for n in range(2)]
-    *parts, layer_output = lax.optimization_barrier((*parts, layer_output))
-    weight_grad = jnp.concatenate([part.astype(F32) for part in parts])
-    weight_grad = weight_grad.reshape(stacked_weights.shape)
+    weight_grad = weight_total[None]
     return layer_output, token_grad, prob_grad[0:2].T, weight_grad
 
 

time: 151 us -> 152 us (level)
    ppermute x14 -> x12, waiting for transfers between devices: 44.5 us -> 50.3 us  [shift(): return lax.ppermute(value, axis, [(i, (i + step) % 4) for i in range(4)])]
    ppermute x2, waiting for transfers between devices: 4.07 us -> 0.01 us  [relay(): lax.ppermute(value, ('x', 'core'), [(2 * i + c, 2 * j + c) for c, i, j in...]
    ppermute x3 -> x4, starting transfers between devices: 12 us -> 15.8 us  [the longest x2 9.18 us: turn(): return lax.ppermute(value, ('core', 'zl'), [(1, 2), (2, 1)])]
    ppermute x14 -> x12, starting transfers between devices: 25.4 us -> 21.7 us  [shift(): return lax.ppermute(value, axis, [(i, (i + step) % 4) for i in range(4)])]
    ppermute x3 -> x4, waiting for transfers between devices: 2.29 us -> 0.71 us  [the longest x2 0.71 us: turn(): return lax.ppermute(value, ('core', 'zl'), [(1, 2), (2, 1)])]
  transfers between devices with their start and end apart: 31 -> 30, of which waited for: 17 -> 17; matrix products, arithmetic and copies ran while one was open for 4% -> 4% of each run, Pallas kernels for 8% -> 8%
where the time goes in v11:
time: 152 us; the launch traced here: 151 us
  waiting for transfers between devices  74.5 us (49%)
  starting transfers between devices  46.2 us (30%)
  Pallas kernels  20.8 us (14%)
  other arithmetic  5.25 us (3%)
  local copies, waits for them, and re-layouts  3.65 us (2%)
    ppermute x12, waiting for transfers between devices, shift(): return lax.ppermute(value, axis, [(i, (i + step) % 4) for i in range(4)])  50.3 us
    ppermute x12, starting transfers between devices, shift(): return lax.ppermute(value, axis, [(i, (i + step) % 4) for i in range(4)])  21.7 us
    pallas_call x7, Pallas kernels, call(): pl.pallas_call(kernel, out_shape=[jax.ShapeDtypeStruct(shape, kind) for s...  20.8 us
    ppermute x10, waiting for transfers between devices, swap(): return lax.ppermute(value, axis, [(0, 1), (1, 0)])  15.2 us
    ppermute x2, starting transfers between devices, turn(): return lax.ppermute(value, ('core', 'zl'), [(1, 2), (2, 1)])  9.18 us
    ppermute x2, waiting for transfers between devices, relay(): lax.ppermute(value, ('core', axis), [(4 * c + i, 4 * c + j) for c, i, j i...  8.2 us
    ppermute x2, starting transfers between devices, home(): return lax.ppermute(value, ('x', 'core', 'zl'), perm)  6.58 us
    ppermute x10, starting transfers between devices, swap(): return lax.ppermute(value, axis, [(0, 1), (1, 0)])  3.92 us
  transfers between devices with their start and end apart: 30, of which 17 were waited for; matrix products, arithmetic and copies ran while one was open for 4% of the time, Pallas kernels for 8%

profile of v11, /device:TPU:1, one launch (start us, length us, event | category | flops | bytes accessed | tf_op | source)
XLA Modules:
  0.0 151.2 jit_solution(17372787148633790123)
XLA Ops:
  0.6 5.1 %collective-permute-start.3 = (bf16[3,192,512]{2,1,0:T(8,128)(2,1)}, bf16[3,192,512]{2,1,0:T(8,128)(2,1)S(1)}, u32[]{:S(2)}, u32[]{:S(2)}) collective-permute-start(bf16[3,192,512]{2,1,0:T(8,128)(2,1)} %bitcast.14), channel_id=1, source_target_pairs={{1,32},{32,1},{3,34},{34,3},{5,36},{36,5},{7,38},{38,7},{9,40},{40... | collective-permute-start | bytes 1769480 | tf_op jit(solution)/shard_map/ppermute | solution.py:245
  5.8 0.7 convert_bitcast_fusion
  6.5 0.7 pad_add_fusion.small
  7.2 1.0 pad_maximum_fusion.wide
  8.2 1.0 shard_map.84
  9.2 3.1 %collective-permute-start = (bf16[160,512]{1,0:T(8,128)(2,1)S(1)}, bf16[160,512]{1,0:T(8,128)(2,1)}, u32[]{:S(2)}, u32[]{:S(2)}) collective-permute-start(bf16[160,512]{1,0:T(8,128)(2,1)S(1)} %get-tuple-element.49), channel_id=1, source_target_pairs={{0,8},{8,16},{16,24},{24,0},{1,9},{9,17},{17,25},{25,1},{2,10},{10... | collective-permute-start | bytes 491528 | tf_op jit(solution)/shard_map/ppermute | solution.py:230
  12.2 4.2 %collective-permute-start.1 = (bf16[160,512]{1,0:T(8,128)(2,1)S(1)}, bf16[160,512]{1,0:T(8,128)(2,1)}, u32[]{:S(2)}, u32[]{:S(2)}) collective-permute-start(bf16[160,512]{1,0:T(8,128)(2,1)S(1)} %get-tuple-element.50), channel_id=1, source_target_pairs={{0,16},{8,24},{16,0},{24,8},{1,17},{9,25},{17,1},{25,9},{2,18},{10... | collective-permute-start | bytes 491528 | tf_op jit(solution)/shard_map/ppermute | solution.py:230
  16.5 2.4 %collective-permute-start.2 = (bf16[160,512]{1,0:T(8,128)(2,1)S(1)}, bf16[160,512]{1,0:T(8,128)(2,1)S(1)}, u32[]{:S(2)}, u32[]{:S(2)}) collective-permute-start(bf16[160,512]{1,0:T(8,128)(2,1)S(1)} %get-tuple-element.51), channel_id=1, source_target_pairs={{0,24},{8,0},{16,8},{24,16},{1,25},{9,1},{17,9},{25,17},{2,26},{10... | collective-permute-start | bytes 491528 | tf_op jit(solution)/shard_map/ppermute | solution.py:230
  18.9 2.6 %collective-permute-start.5 = (bf16[3,192,512]{2,1,0:T(8,128)(2,1)S(1)}, bf16[3,192,512]{2,1,0:T(8,128)(2,1)S(1)}, u32[]{:S(2)}, u32[]{:S(2)}) collective-permute-start(bf16[3,192,512]{2,1,0:T(8,128)(2,1)S(1)} %broadcast_select_fusion.2.refs_4_), channel_id=1, source_target_pairs={{0,192},{64,0},{128,64},{192,128},{1,193},{65,1},{129,65},{193,129... | collective-permute-start | bytes 1769480 | tf_op jit(solution)/shard_map/ppermute | solution.py:230
  21.5 7.4 %collective-permute-done = bf16[160,512]{1,0:T(8,128)(2,1)} collective-permute-done((bf16[160,512]{1,0:T(8,128)(2,1)S(1)}, bf16[160,512]{1,0:T(8,128)(2,1)}, u32[]{:S(2)}, u32[]{:S(2)}) %collective-permute-start) | collective-permute-done | bytes 163872 | tf_op jit(solution)/shard_map/ppermute | solution.py:230
  28.9 0.9 constant_dynamic-update-slice_fusion.2
  29.9 1.8 %collective-permute-done.1 = bf16[160,512]{1,0:T(8,128)(2,1)} collective-permute-done((bf16[160,512]{1,0:T(8,128)(2,1)S(1)}, bf16[160,512]{1,0:T(8,128)(2,1)}, u32[]{:S(2)}, u32[]{:S(2)}) %collective-permute-start.1) | collective-permute-done | bytes 163872 | tf_op jit(solution)/shard_map/ppermute | solution.py:230
  31.7 0.9 constant_dynamic-update-slice_fusion.1
  32.6 2.8 %collective-permute-start.7 = (bf16[640,512]{1,0:T(8,128)(2,1)S(1)}, bf16[640,512]{1,0:T(8,128)(2,1)S(1)}, u32[]{:S(2)}, u32[]{:S(2)}) collective-permute-start(bf16[640,512]{1,0:T(8,128)(2,1)S(1)} %constant_dynamic-update-slice_fusion.refs_0_), channel_id=1, source_target_pairs={{0,6},{2,0},{4,2},{6,4},{1,7},{3,1},{5,3},{7,5},{8,14},{10,8},{12,... | collective-permute-start | bytes 1966088 | tf_op jit(solution)/shard_map/ppermute | solution.py:230
  35.5 2.3 %collective-permute-done.4.refs_5_ = bf16[3,192,512]{2,1,0:T(8,128)(2,1)} collective-permute-done((bf16[3,192,512]{2,1,0:T(8,128)(2,1)S(1)}, bf16[3,192,512]{2,1,0:T(8,128)(2,1)}, u32[]{:S(2)}, u32[]{:S(2)}) %collective-permute-start.4) | collective-permute-done | bytes 589856 | tf_op jit(solution)/shard_map/ppermute | solution.py:230
  38.1 9.9 %collective-permute-done.7.refs_3_ = bf16[640,512]{1,0:T(8,128)(2,1)S(1)} collective-permute-done((bf16[640,512]{1,0:T(8,128)(2,1)S(1)}, bf16[640,512]{1,0:T(8,128)(2,1)S(1)}, u32[]{:S(2)}, u32[]{:S(2)}) %collective-permute-start.7) | collective-permute-done | bytes 655392 | tf_op jit(solution)/shard_map/ppermute | solution.py:230
  48.0 3.4 %collective-permute-done.6.refs_1_ = bf16[640,512]{1,0:T(8,128)(2,1)S(1)} collective-permute-done((bf16[640,512]{1,0:T(8,128)(2,1)S(1)}, bf16[640,512]{1,0:T(8,128)(2,1)S(1)}, u32[]{:S(2)}, u32[]{:S(2)}) %collective-permute-start.6) | collective-permute-done | bytes 655392 | tf_op jit(solution)/shard_map/ppermute | solution.py:230
  51.6 0.5 collective-permute-start.11
  52.6 1.0 collective-permute-done.10.refs_8_
  53.6 1.9 %collective-permute-done.11.refs_9_ = bf16[3,192,512]{2,1,0:T(8,128)(2,1)S(1)} collective-permute-done((bf16[3,192,512]{2,1,0:T(8,128)(2,1)}, bf16[3,192,512]{2,1,0:T(8,128)(2,1)S(1)}, u32[]{:S(2)}, u32[]{:S(2)}) %collective-permute-start.11) | collective-permute-done | bytes 589856 | tf_op jit(solution)/shard_map/ppermute | solution.py:241
  55.5 5.7 %collective-permute-done.8.refs_2_ = bf16[640,512]{1,0:T(8,128)(2,1)S(1)} collective-permute-done((bf16[640,512]{1,0:T(8,128)(2,1)S(1)}, bf16[640,512]{1,0:T(8,128)(2,1)S(1)}, u32[]{:S(2)}, u32[]{:S(2)}) %collective-permute-start.8) | collective-permute-done | bytes 655392 | tf_op jit(solution)/shard_map/ppermute | solution.py:237
  61.3 0.9 copy-done.4
  62.1 4.4 %shard_map.85 = (bf16[320,768]{1,0:T(8,128)(2,1)S(1)}, bf16[768,2048]{1,0:T(8,128)(2,1)}) custom-call(s32[5]{0:T(128)S(1)} %stack.23.place, bf16[640,512]{1,0:T(8,128)(2,1)S(1)} %constant_dynamic-update-slice_fusion.refs_0_, bf16[640,512]{1,0:T(8,128)(2,1)} %copy-done.2, bf16[640,512]{1,0:T(8,128)(2,1)} %copy-done.4, bf16[640,512]{1,0:T(8,128)(2,1)} %copy-done, ...), custom_call_target="tpu_custom_call" | custom-call | tf_op jit(solution)/shard_map/pallas_call | solution.py:33
  66.8 3.8 %shard_map.86 = (bf16[320,384]{1,0:T(8,128)(2,1)S(1)}, bf16[384,2048]{1,0:T(8,128)(2,1)}) custom-call(s32[5]{0:T(128)S(1)} %stack.23.place, bf16[640,512]{1,0:T(8,128)(2,1)S(1)} %constant_dynamic-update-slice_fusion.refs_0_, bf16[640,512]{1,0:T(8,128)(2,1)} %copy-done.2, bf16[640,512]{1,0:T(8,128)(2,1)} %copy-done.4, bf16[640,512]{1,0:T(8,128)(2,1)} %copy-done, ...), custom_call_target="tpu_custom_call" | custom-call | tf_op jit(solution)/shard_map/pallas_call | solution.py:33
  70.6 1.5 %collective-permute-start.15 = (bf16[320,384]{1,0:T(8,128)(2,1)S(1)}, bf16[320,384]{1,0:T(8,128)(2,1)S(1)}, u32[]{:S(2)}, u32[]{:S(2)}) collective-permute-start(bf16[320,384]{1,0:T(8,128)(2,1)S(1)} %get-tuple-element.58.down), channel_id=1, source_target_pairs={{0,1},{1,0},{2,3},{3,2},{4,5},{5,4},{6,7},{7,6},{8,9},{9,8},{10,11... | collective-permute-start | bytes 737288 | tf_op jit(solution)/shard_map/ppermute | solution.py:241
  72.2 11.7 %collective-permute-done.15.down_far = bf16[320,384]{1,0:T(8,128)(2,1)S(1)} collective-permute-done((bf16[320,384]{1,0:T(8,128)(2,1)S(1)}, bf16[320,384]{1,0:T(8,128)(2,1)S(1)}, u32[]{:S(2)}, u32[]{:S(2)}) %collective-permute-start.15) | collective-permute-done | bytes 245792 | tf_op jit(solution)/shard_map/ppermute | solution.py:241
  83.9 4.6 %shard_map.87 = (f32[656,512]{1,0:T(8,128)S(1)}, bf16[656,512]{1,0:T(8,128)(2,1)S(1)}, bf16[656,512]{1,0:T(8,128)(2,1)S(1)}, bf16[656,512]{1,0:T(8,128)(2,1)S(1)}, bf16[320,1152]{1,0:T(8,128)(2,1)S(1)}) custom-call(s32[5]{0:T(128)S(1)} %stack.23.place, bf16[320,768]{1,0:T(8,128)(2,1)S(1)} %get-tuple-element.57.pair, ...), custom_call_target="tpu_custom_call" | custom-call | tf_op jit(solution)/shard_map/pallas_call | solution.py:33
  88.5 1.9 %collective-permute-start.16 = (bf16[656,512]{1,0:T(8,128)(2,1)S(1)}, bf16[656,512]{1,0:T(8,128)(2,1)S(1)}, u32[]{:S(2)}, u32[]{:S(2)}) collective-permute-start(bf16[656,512]{1,0:T(8,128)(2,1)S(1)} %get-tuple-element.65), channel_id=1, source_target_pairs={{0,2},{2,4},{4,6},{6,0},{32,38},{34,32},{36,34},{38,36},{1,3},{3,5... | collective-permute-start | bytes 2015240 | tf_op jit(solution)/shard_map/ppermute | solution.py:237
  90.4 4.6 %shard_map.88 = (f32[3,192,512]{2,1,0:T(8,128)}, f32[3,192,512]{2,1,0:T(8,128)}, f32[3,192,512]{2,1,0:T(8,128)}, f32[3,192,512]{2,1,0:T(8,128)}, bf16[3,192,512]...) custom-call(s32[5]{0:T(128)S(1)} %stack.23.place, ...), custom_call_target="tpu_custom_call" | custom-call | tf_op jit(solution)/shard_map/pallas_call | solution.py:33
  96.0 2.5 %collective-permute-done.16 = bf16[656,512]{1,0:T(8,128)(2,1)S(1)} collective-permute-done((bf16[656,512]{1,0:T(8,128)(2,1)S(1)}, bf16[656,512]{1,0:T(8,128)(2,1)S(1)}, u32[]{:S(2)}, u32[]{:S(2)}) %collective-permute-start.16) | collective-permute-done | bytes 671776 | tf_op jit(solution)/shard_map/ppermute | solution.py:237
  98.9 0.6 collective-permute-done.20
  99.9 2.6 %collective-permute-start.27 = (bf16[3,192,512]{2,1,0:T(8,128)(2,1)S(1)}, bf16[3,192,512]{2,1,0:T(8,128)(2,1)S(1)}, u32[]{:S(2)}, u32[]{:S(2)}) collective-permute-start(bf16[3,192,512]{2,1,0:T(8,128)(2,1)S(1)} %add_convert_fusion), channel_id=1, source_target_pairs={{0,64},{64,128},{128,192},{192,0},{32,224},{96,32},{160,96},{224,1... | collective-permute-start | bytes 1769480 | tf_op jit(solution)/shard_map/ppermute | solution.py:236
  102.5 2.8 %collective-permute-start.22 = (bf16[656,512]{1,0:T(8,128)(2,1)S(1)}, bf16[656,512]{1,0:T(8,128)(2,1)S(1)}, u32[]{:S(2)}, u32[]{:S(2)}) collective-permute-start(bf16[656,512]{1,0:T(8,128)(2,1)S(1)} %get-tuple-element.72), channel_id=1, source_target_pairs={{0,6},{2,0},{4,2},{6,4},{1,7},{3,1},{5,3},{7,5},{8,14},{10,8},{12,... | collective-permute-start | bytes 2015240 | tf_op jit(solution)/shard_map/ppermute | solution.py:230
  105.4 4.1 %collective-permute-start.21 = (bf16[3,192,512]{2,1,0:T(8,128)(2,1)S(1)}, bf16[3,192,512]{2,1,0:T(8,128)(2,1)S(1)}, u32[]{:S(2)}, u32[]{:S(2)}) collective-permute-start(bf16[3,192,512]{2,1,0:T(8,128)(2,1)S(1)} %fusion.8), channel_id=1, source_target_pairs={{1,32},{32,1},{3,34},{34,3},{5,36},{36,5},{7,38},{38,7},{9,40},{40... | collective-permute-start | bytes 1769480 | tf_op jit(solution)/shard_map/ppermute | solution.py:245
  109.6 0.5 fusion.5
  110.1 6.6 %collective-permute-start.28 = (bf16[3,192,512]{2,1,0:T(8,128)(2,1)S(1)}, bf16[3,192,512]{2,1,0:T(8,128)(2,1)S(1)}, u32[]{:S(2)}, u32[]{:S(2)}) collective-permute-start(bf16[3,192,512]{2,1,0:T(8,128)(2,1)S(1)} %get-tuple-element.92), channel_id=1, source_target_pairs={{0,192},{1,224},{32,193},{33,225},{64,0},{65,32},{96,1},{97,33},{1... | collective-permute-start | bytes 1769480 | tf_op jit(solution)/shard_map/ppermute | solution.py:251
  116.7 0.7 collective-permute-done.21
  117.4 2.5 %collective-permute-done.22.one = bf16[656,512]{1,0:T(8,128)(2,1)S(1)} collective-permute-done((bf16[656,512]{1,0:T(8,128)(2,1)S(1)}, bf16[656,512]{1,0:T(8,128)(2,1)S(1)}, u32[]{:S(2)}, u32[]{:S(2)}) %collective-permute-start.22) | collective-permute-done | bytes 671776 | tf_op jit(solution)/shard_map/ppermute | solution.py:230
  119.9 3.1 %collective-permute-done.23.three = bf16[656,512]{1,0:T(8,128)(2,1)S(1)} collective-permute-done((bf16[656,512]{1,0:T(8,128)(2,1)S(1)}, bf16[656,512]{1,0:T(8,128)(2,1)S(1)}, u32[]{:S(2)}, u32[]{:S(2)}) %collective-permute-start.23) | collective-permute-done | bytes 671776 | tf_op jit(solution)/shard_map/ppermute | solution.py:230
  123.0 0.8 shard_map.89
  123.7 1.3 collective-permute-start.24
  125.1 2.4 %collective-permute-start.25 = (bf16[176,512]{1,0:T(8,128)(2,1)S(1)}, bf16[176,512]{1,0:T(8,128)(2,1)S(1)}, u32[]{:S(2)}, u32[]{:S(2)}) collective-permute-start(bf16[176,512]{1,0:T(8,128)(2,1)S(1)} %get-tuple-element.78), channel_id=1, source_target_pairs={{0,16},{8,24},{16,0},{24,8},{1,17},{9,25},{17,1},{25,9},{2,18},{10... | collective-permute-start | bytes 540680 | tf_op jit(solution)/shard_map/ppermute | solution.py:230
  127.7 3.8 %collective-permute-done.24.refs_1_ = bf16[176,512]{1,0:T(8,128)(2,1)S(1)} collective-permute-done((bf16[176,512]{1,0:T(8,128)(2,1)S(1)}, bf16[176,512]{1,0:T(8,128)(2,1)S(1)}, u32[]{:S(2)}, u32[]{:S(2)}) %collective-permute-start.24) | collective-permute-done | bytes 180256 | tf_op jit(solution)/shard_map/ppermute | solution.py:230
  131.5 9.9 %collective-permute-done.25.refs_2_ = bf16[176,512]{1,0:T(8,128)(2,1)S(1)} collective-permute-done((bf16[176,512]{1,0:T(8,128)(2,1)S(1)}, bf16[176,512]{1,0:T(8,128)(2,1)S(1)}, u32[]{:S(2)}, u32[]{:S(2)}) %collective-permute-start.25) | collective-permute-done | bytes 180256 | tf_op jit(solution)/shard_map/ppermute | solution.py:230
  141.4 6.2 %collective-permute-done.26.refs_3_ = bf16[176,512]{1,0:T(8,128)(2,1)S(1)} collective-permute-done((bf16[176,512]{1,0:T(8,128)(2,1)S(1)}, bf16[176,512]{1,0:T(8,128)(2,1)S(1)}, u32[]{:S(2)}, u32[]{:S(2)}) %collective-permute-start.26) | collective-permute-done | bytes 180256 | tf_op jit(solution)/shard_map/ppermute | solution.py:230
  147.6 1.7 %shard_map.90 = (bf16[128,512]{1,0:T(8,128)(2,1)}, bf16[128,512]{1,0:T(8,128)(2,1)}, f32[8,128]{1,0:T(8,128)S(1)}) custom-call(s32[5]{0:T(128)S(1)} %stack.23.place, f32[4,128]{1,0:T(4,128)S(1)} %pad_add_fusion.small, bf16[320,128]{1,0:T(8,128)(2,1)S(1)} %get-tuple-element.47.placing, bf16[176,512]{1,0:T(8,128)(2,1)S(1)} %get-tuple-element.76.refs_0_, ...), custom_call_target="tpu_custom_call" | custom-call | tf_op jit(solution)/shard_map/pallas_call | solution.py:33
  149.2 0.6 slice_bitcast_fusion
  149.8 1.4 add_bitcast_fusion
  (58 shorter events, 3.8 us)
Async XLA Ops:
  0.6 18.2 %copy-start.10 = (bf16[1,3,192,512]{3,2,1,0:T(8,128)(2,1)S(1)}, bf16[1,3,192,512]{3,2,1,0:T(8,128)(2,1)}, u32[]{:S(2)}) copy-start(bf16[1,3,192,512]{3,2,1,0:T(8,128)(2,1)} %param.8) | copy-start | bytes 1769476
  0.6 18.2 %collective-permute-start.3 = (bf16[3,192,512]{2,1,0:T(8,128)(2,1)}, bf16[3,192,512]{2,1,0:T(8,128)(2,1)S(1)}, u32[]{:S(2)}, u32[]{:S(2)}) collective-permute-start(bf16[3,192,512]{2,1,0:T(8,128)(2,1)} %bitcast.14), channel_id=1, source_target_pairs={{1,32},{32,1},{3,34},{34,3},{5,36},{36,5},{7,38},{38,7},{9,40},{40... | collective-permute-start | bytes 1769480 | tf_op jit(solution)/shard_map/ppermute | solution.py:245
  9.2 19.8 %collective-permute-start = (bf16[160,512]{1,0:T(8,128)(2,1)S(1)}, bf16[160,512]{1,0:T(8,128)(2,1)}, u32[]{:S(2)}, u32[]{:S(2)}) collective-permute-start(bf16[160,512]{1,0:T(8,128)(2,1)S(1)} %get-tuple-element.49), channel_id=1, source_target_pairs={{0,8},{8,16},{16,24},{24,0},{1,9},{9,17},{17,25},{25,1},{2,10},{10... | collective-permute-start | bytes 491528 | tf_op jit(solution)/shard_map/ppermute | solution.py:230
  12.2 19.4 %collective-permute-start.1 = (bf16[160,512]{1,0:T(8,128)(2,1)S(1)}, bf16[160,512]{1,0:T(8,128)(2,1)}, u32[]{:S(2)}, u32[]{:S(2)}) collective-permute-start(bf16[160,512]{1,0:T(8,128)(2,1)S(1)} %get-tuple-element.50), channel_id=1, source_target_pairs={{0,16},{8,24},{16,0},{24,8},{1,17},{9,25},{17,1},{25,9},{2,18},{10... | collective-permute-start | bytes 491528 | tf_op jit(solution)/shard_map/ppermute | solution.py:230
  16.5 16.1 %collective-permute-start.2 = (bf16[160,512]{1,0:T(8,128)(2,1)S(1)}, bf16[160,512]{1,0:T(8,128)(2,1)S(1)}, u32[]{:S(2)}, u32[]{:S(2)}) collective-permute-start(bf16[160,512]{1,0:T(8,128)(2,1)S(1)} %get-tuple-element.51), channel_id=1, source_target_pairs={{0,24},{8,0},{16,8},{24,16},{1,25},{9,1},{17,9},{25,17},{2,26},{10... | collective-permute-start | bytes 491528 | tf_op jit(solution)/shard_map/ppermute | solution.py:230
  18.9 16.5 %collective-permute-start.5 = (bf16[3,192,512]{2,1,0:T(8,128)(2,1)S(1)}, bf16[3,192,512]{2,1,0:T(8,128)(2,1)S(1)}, u32[]{:S(2)}, u32[]{:S(2)}) collective-permute-start(bf16[3,192,512]{2,1,0:T(8,128)(2,1)S(1)} %broadcast_select_fusion.2.refs_4_), channel_id=1, source_target_pairs={{0,192},{64,0},{128,64},{192,128},{1,193},{65,1},{129,65},{193,129... | collective-permute-start | bytes 1769480 | tf_op jit(solution)/shard_map/ppermute | solution.py:230
  21.5 16.3 %collective-permute-start.4 = (bf16[3,192,512]{2,1,0:T(8,128)(2,1)S(1)}, bf16[3,192,512]{2,1,0:T(8,128)(2,1)}, u32[]{:S(2)}, u32[]{:S(2)}) collective-permute-start(bf16[3,192,512]{2,1,0:T(8,128)(2,1)S(1)} %broadcast_select_fusion.2.refs_4_), channel_id=1, source_target_pairs={{0,64},{64,128},{128,192},{192,0},{1,65},{65,129},{129,193},{193,1... | collective-permute-start | bytes 1769480 | tf_op jit(solution)/shard_map/ppermute | solution.py:230
  32.6 15.3 %collective-permute-start.7 = (bf16[640,512]{1,0:T(8,128)(2,1)S(1)}, bf16[640,512]{1,0:T(8,128)(2,1)S(1)}, u32[]{:S(2)}, u32[]{:S(2)}) collective-permute-start(bf16[640,512]{1,0:T(8,128)(2,1)S(1)} %constant_dynamic-update-slice_fusion.refs_0_), channel_id=1, source_target_pairs={{0,6},{2,0},{4,2},{6,4},{1,7},{3,1},{5,3},{7,5},{8,14},{10,8},{12,... | collective-permute-start | bytes 1966088 | tf_op jit(solution)/shard_map/ppermute | solution.py:230
  35.4 15.9 %collective-permute-start.6 = (bf16[640,512]{1,0:T(8,128)(2,1)S(1)}, bf16[640,512]{1,0:T(8,128)(2,1)S(1)}, u32[]{:S(2)}, u32[]{:S(2)}) collective-permute-start(bf16[640,512]{1,0:T(8,128)(2,1)S(1)} %constant_dynamic-update-slice_fusion.refs_0_), channel_id=1, source_target_pairs={{0,2},{2,4},{4,6},{6,0},{1,3},{3,5},{5,7},{7,1},{8,10},{10,12},{12... | collective-permute-start | bytes 1966088 | tf_op jit(solution)/shard_map/ppermute | solution.py:230
  37.8 14.4 %collective-permute-start.9 = (bf16[3,192,512]{2,1,0:T(8,128)(2,1)S(1)}, bf16[3,192,512]{2,1,0:T(8,128)(2,1)S(1)}, u32[]{:S(2)}, u32[]{:S(2)}) collective-permute-start(bf16[3,192,512]{2,1,0:T(8,128)(2,1)S(1)} %broadcast_select_fusion.1), channel_id=1, source_target_pairs={{0,64},{64,128},{128,192},{192,0},{32,224},{96,32},{160,96},{224,1... | collective-permute-start | bytes 1769480 | tf_op jit(solution)/shard_map/ppermute | solution.py:236
  48.0 13.3 %copy-start = (bf16[640,512]{1,0:T(8,128)(2,1)}, bf16[640,512]{1,0:T(8,128)(2,1)S(1)}, u32[]{:S(2)}) copy-start(bf16[640,512]{1,0:T(8,128)(2,1)S(1)} %collective-permute-done.7.refs_3_) | copy-start | bytes 1966084
  51.4 9.9 %copy-start.2 = (bf16[640,512]{1,0:T(8,128)(2,1)}, bf16[640,512]{1,0:T(8,128)(2,1)S(1)}, u32[]{:S(2)}) copy-start(bf16[640,512]{1,0:T(8,128)(2,1)S(1)} %collective-permute-done.6.refs_1_) | copy-start | bytes 1966084
  51.4 9.8 %collective-permute-start.8 = (bf16[640,512]{1,0:T(8,128)(2,1)S(1)}, bf16[640,512]{1,0:T(8,128)(2,1)S(1)}, u32[]{:S(2)}, u32[]{:S(2)}) collective-permute-start(bf16[640,512]{1,0:T(8,128)(2,1)S(1)} %broadcast_select_fusion), channel_id=1, source_target_pairs={{0,2},{2,4},{4,6},{6,0},{32,38},{34,32},{36,34},{38,36},{1,3},{3,5... | collective-permute-start | bytes 1966088 | tf_op jit(solution)/shard_map/ppermute | solution.py:237
  51.5 2.1 %collective-permute-start.10 = (bf16[3,192,512]{2,1,0:T(8,128)(2,1)S(1)}, bf16[3,192,512]{2,1,0:T(8,128)(2,1)S(1)}, u32[]{:S(2)}, u32[]{:S(2)}) collective-permute-start(bf16[3,192,512]{2,1,0:T(8,128)(2,1)S(1)} %broadcast_select_fusion.2.refs_4_), channel_id=1, source_target_pairs={{0,32},{32,0},{1,33},{33,1},{2,34},{34,2},{3,35},{35,3},{4,36},{36... | collective-permute-start | bytes 1769480 | tf_op jit(solution)/shard_map/ppermute | solution.py:241
  51.6 3.9 %collective-permute-start.11 = (bf16[3,192,512]{2,1,0:T(8,128)(2,1)}, bf16[3,192,512]{2,1,0:T(8,128)(2,1)S(1)}, u32[]{:S(2)}, u32[]{:S(2)}) collective-permute-start(bf16[3,192,512]{2,1,0:T(8,128)(2,1)} %collective-permute-done.4.refs_5_), channel_id=1, source_target_pairs={{0,32},{32,0},{1,33},{33,1},{2,34},{34,2},{3,35},{35,3},{4,36},{36... | collective-permute-start | bytes 1769480 | tf_op jit(solution)/shard_map/ppermute | solution.py:241
  52.1 3.4 %collective-permute-start.13 = (bf16[3,192,512]{2,1,0:T(8,128)(2,1)S(1)}, bf16[3,192,512]{2,1,0:T(8,128)(2,1)S(1)}, u32[]{:S(2)}, u32[]{:S(2)}) collective-permute-start(bf16[3,192,512]{2,1,0:T(8,128)(2,1)S(1)} %collective-permute-done.5.refs_7_), channel_id=1, source_target_pairs={{0,32},{32,0},{1,33},{33,1},{2,34},{34,2},{3,35},{35,3},{4,36},{36... | collective-permute-start | bytes 1769480 | tf_op jit(solution)/shard_map/ppermute | solution.py:241
  52.2 9.0 %collective-permute-start.12 = (bf16[3,192,512]{2,1,0:T(8,128)(2,1)S(1)}, bf16[3,192,512]{2,1,0:T(8,128)(2,1)S(1)}, u32[]{:S(2)}, u32[]{:S(2)}) collective-permute-start(bf16[3,192,512]{2,1,0:T(8,128)(2,1)S(1)} %collective-permute-done.9.refs_6_), channel_id=1, source_target_pairs={{0,32},{32,0},{1,33},{33,1},{2,34},{34,2},{3,35},{35,3},{4,36},{36... | collective-permute-start | bytes 1769480 | tf_op jit(solution)/shard_map/ppermute | solution.py:241
  61.2 0.9 copy-start.4
  66.5 17.3 %collective-permute-start.14 = (bf16[320,768]{1,0:T(8,128)(2,1)S(1)}, bf16[320,768]{1,0:T(8,128)(2,1)S(1)}, u32[]{:S(2)}, u32[]{:S(2)}) collective-permute-start(bf16[320,768]{1,0:T(8,128)(2,1)S(1)} %get-tuple-element.57.pair), channel_id=1, source_target_pairs={{0,1},{1,0},{2,3},{3,2},{4,5},{5,4},{6,7},{7,6},{8,9},{9,8},{10,11... | collective-permute-start | bytes 1474568 | tf_op jit(solution)/shard_map/ppermute | solution.py:241
  70.6 13.3 %collective-permute-start.15 = (bf16[320,384]{1,0:T(8,128)(2,1)S(1)}, bf16[320,384]{1,0:T(8,128)(2,1)S(1)}, u32[]{:S(2)}, u32[]{:S(2)}) collective-permute-start(bf16[320,384]{1,0:T(8,128)(2,1)S(1)} %get-tuple-element.58.down), channel_id=1, source_target_pairs={{0,1},{1,0},{2,3},{3,2},{4,5},{5,4},{6,7},{7,6},{8,9},{9,8},{10,11... | collective-permute-start | bytes 737288 | tf_op jit(solution)/shard_map/ppermute | solution.py:241
  83.9 6.5 %copy-start.1 = (bf16[640,512]{1,0:T(8,128)(2,1)S(1)}, bf16[640,512]{1,0:T(8,128)(2,1)}, u32[]{:S(2)}) copy-start(bf16[640,512]{1,0:T(8,128)(2,1)} %copy-done) | copy-start | bytes 1966084
  83.9 6.5 %copy-start.3 = (bf16[640,512]{1,0:T(8,128)(2,1)S(1)}, bf16[640,512]{1,0:T(8,128)(2,1)}, u32[]{:S(2)}) copy-start(bf16[640,512]{1,0:T(8,128)(2,1)} %copy-done.2) | copy-start | bytes 1966084
  83.9 6.5 %copy-start.5 = (bf16[640,512]{1,0:T(8,128)(2,1)S(1)}, bf16[640,512]{1,0:T(8,128)(2,1)}, u32[]{:S(2)}) copy-start(bf16[640,512]{1,0:T(8,128)(2,1)} %copy-done.4) | copy-start | bytes 1966084
  88.5 10.0 %collective-permute-start.16 = (bf16[656,512]{1,0:T(8,128)(2,1)S(1)}, bf16[656,512]{1,0:T(8,128)(2,1)S(1)}, u32[]{:S(2)}, u32[]{:S(2)}) collective-permute-start(bf16[656,512]{1,0:T(8,128)(2,1)S(1)} %get-tuple-element.65), channel_id=1, source_target_pairs={{0,2},{2,4},{4,6},{6,0},{32,38},{34,32},{36,34},{38,36},{1,3},{3,5... | collective-permute-start | bytes 2015240 | tf_op jit(solution)/shard_map/ppermute | solution.py:237
  95.0 3.9 %collective-permute-start.17 = (bf16[3,192,512]{2,1,0:T(8,128)(2,1)S(1)}, bf16[3,192,512]{2,1,0:T(8,128)(2,1)S(1)}, u32[]{:S(2)}, u32[]{:S(2)}) collective-permute-start(bf16[3,192,512]{2,1,0:T(8,128)(2,1)S(1)} %get-tuple-element.67), channel_id=1, source_target_pairs={{0,32},{32,0},{1,33},{33,1},{2,34},{34,2},{3,35},{35,3},{4,36},{36... | collective-permute-start | bytes 1769480 | tf_op jit(solution)/shard_map/ppermute | solution.py:241
  95.0 3.8 %collective-permute-start.18 = (bf16[3,192,512]{2,1,0:T(8,128)(2,1)S(1)}, bf16[3,192,512]{2,1,0:T(8,128)(2,1)S(1)}, u32[]{:S(2)}, u32[]{:S(2)}) collective-permute-start(bf16[3,192,512]{2,1,0:T(8,128)(2,1)S(1)} %get-tuple-element.68), channel_id=1, source_target_pairs={{0,32},{32,0},{1,33},{33,1},{2,34},{34,2},{3,35},{35,3},{4,36},{36... | collective-permute-start | bytes 1769480 | tf_op jit(solution)/shard_map/ppermute | solution.py:241
  95.5 3.4 %collective-permute-start.19 = (bf16[3,192,512]{2,1,0:T(8,128)(2,1)S(1)}, bf16[3,192,512]{2,1,0:T(8,128)(2,1)S(1)}, u32[]{:S(2)}, u32[]{:S(2)}) collective-permute-start(bf16[3,192,512]{2,1,0:T(8,128)(2,1)S(1)} %get-tuple-element.69), channel_id=1, source_target_pairs={{0,32},{32,0},{1,33},{33,1},{2,34},{34,2},{3,35},{35,3},{4,36},{36... | collective-permute-start | bytes 1769480 | tf_op jit(solution)/shard_map/ppermute | solution.py:241
  95.5 4.0 %collective-permute-start.20 = (bf16[3,192,512]{2,1,0:T(8,128)(2,1)S(1)}, bf16[3,192,512]{2,1,0:T(8,128)(2,1)S(1)}, u32[]{:S(2)}, u32[]{:S(2)}) collective-permute-start(bf16[3,192,512]{2,1,0:T(8,128)(2,1)S(1)} %get-tuple-element.70), channel_id=1, source_target_pairs={{0,32},{32,0},{1,33},{33,1},{2,34},{34,2},{3,35},{35,3},{4,36},{36... | collective-permute-start | bytes 1769480 | tf_op jit(solution)/shard_map/ppermute | solution.py:241
  98.5 1.3 copy-start.7
  99.7 5.5 %copy-start.6 = (f32[3,192,512]{2,1,0:T(8,128)S(1)}, f32[3,192,512]{2,1,0:T(8,128)}, u32[]{:S(2)}) copy-start(f32[3,192,512]{2,1,0:T(8,128)} %get-tuple-element.63) | copy-start | bytes 3538948
  99.9 9.6 %collective-permute-start.27 = (bf16[3,192,512]{2,1,0:T(8,128)(2,1)S(1)}, bf16[3,192,512]{2,1,0:T(8,128)(2,1)S(1)}, u32[]{:S(2)}, u32[]{:S(2)}) collective-permute-start(bf16[3,192,512]{2,1,0:T(8,128)(2,1)S(1)} %add_convert_fusion), channel_id=1, source_target_pairs={{0,64},{64,128},{128,192},{192,0},{32,224},{96,32},{160,96},{224,1... | collective-permute-start | bytes 1769480 | tf_op jit(solution)/shard_map/ppermute | solution.py:236
  102.5 17.4 %collective-permute-start.22 = (bf16[656,512]{1,0:T(8,128)(2,1)S(1)}, bf16[656,512]{1,0:T(8,128)(2,1)S(1)}, u32[]{:S(2)}, u32[]{:S(2)}) collective-permute-start(bf16[656,512]{1,0:T(8,128)(2,1)S(1)} %get-tuple-element.72), channel_id=1, source_target_pairs={{0,6},{2,0},{4,2},{6,4},{1,7},{3,1},{5,3},{7,5},{8,14},{10,8},{12,... | collective-permute-start | bytes 2015240 | tf_op jit(solution)/shard_map/ppermute | solution.py:230
  105.2 17.7 %collective-permute-start.23 = (bf16[656,512]{1,0:T(8,128)(2,1)S(1)}, bf16[656,512]{1,0:T(8,128)(2,1)S(1)}, u32[]{:S(2)}, u32[]{:S(2)}) collective-permute-start(bf16[656,512]{1,0:T(8,128)(2,1)S(1)} %get-tuple-element.73), channel_id=1, source_target_pairs={{0,2},{2,4},{4,6},{6,0},{1,3},{3,5},{5,7},{7,1},{8,10},{10,12},{12... | collective-permute-start | bytes 2015240 | tf_op jit(solution)/shard_map/ppermute | solution.py:230
  105.2 4.3 %copy-start.8 = (f32[3,192,512]{2,1,0:T(8,128)S(1)}, f32[3,192,512]{2,1,0:T(8,128)}, u32[]{:S(2)}) copy-start(f32[3,192,512]{2,1,0:T(8,128)} %get-tuple-element.84) | copy-start | bytes 3538948
  105.2 4.3 %copy-start.9 = (f32[3,192,512]{2,1,0:T(8,128)S(1)}, f32[3,192,512]{2,1,0:T(8,128)}, u32[]{:S(2)}) copy-start(f32[3,192,512]{2,1,0:T(8,128)} %get-tuple-element.88) | copy-start | bytes 3538948
  105.4 12.0 %collective-permute-start.21 = (bf16[3,192,512]{2,1,0:T(8,128)(2,1)S(1)}, bf16[3,192,512]{2,1,0:T(8,128)(2,1)S(1)}, u32[]{:S(2)}, u32[]{:S(2)}) collective-permute-start(bf16[3,192,512]{2,1,0:T(8,128)(2,1)S(1)} %fusion.8), channel_id=1, source_target_pairs={{1,32},{32,1},{3,34},{34,3},{5,36},{36,5},{7,38},{38,7},{9,40},{40... | collective-permute-start | bytes 1769480 | tf_op jit(solution)/shard_map/ppermute | solution.py:245
  110.1 39.7 %collective-permute-start.28 = (bf16[3,192,512]{2,1,0:T(8,128)(2,1)S(1)}, bf16[3,192,512]{2,1,0:T(8,128)(2,1)S(1)}, u32[]{:S(2)}, u32[]{:S(2)}) collective-permute-start(bf16[3,192,512]{2,1,0:T(8,128)(2,1)S(1)} %get-tuple-element.92), channel_id=1, source_target_pairs={{0,192},{1,224},{32,193},{33,225},{64,0},{65,32},{96,1},{97,33},{1... | collective-permute-start | bytes 1769480 | tf_op jit(solution)/shard_map/ppermute | solution.py:251
  116.7 33.1 %collective-permute-start.29 = (bf16[3,192,512]{2,1,0:T(8,128)(2,1)S(1)}, bf16[3,192,512]{2,1,0:T(8,128)(2,1)S(1)}, u32[]{:S(2)}, u32[]{:S(2)}) collective-permute-start(bf16[3,192,512]{2,1,0:T(8,128)(2,1)S(1)} %get-tuple-element.93), channel_id=1, source_target_pairs={{0,64},{1,96},{32,65},{33,97},{64,128},{65,160},{96,129},{97,161},... | collective-permute-start | bytes 1769480 | tf_op jit(solution)/shard_map/ppermute | solution.py:251
  123.7 7.7 %collective-permute-start.24 = (bf16[176,512]{1,0:T(8,128)(2,1)S(1)}, bf16[176,512]{1,0:T(8,128)(2,1)S(1)}, u32[]{:S(2)}, u32[]{:S(2)}) collective-permute-start(bf16[176,512]{1,0:T(8,128)(2,1)S(1)} %get-tuple-element.77), channel_id=1, source_target_pairs={{0,24},{8,0},{16,8},{24,16},{1,25},{9,1},{17,9},{25,17},{2,26},{10... | collective-permute-start | bytes 540680 | tf_op jit(solution)/shard_map/ppermute | solution.py:230
  125.1 16.3 %collective-permute-start.25 = (bf16[176,512]{1,0:T(8,128)(2,1)S(1)}, bf16[176,512]{1,0:T(8,128)(2,1)S(1)}, u32[]{:S(2)}, u32[]{:S(2)}) collective-permute-start(bf16[176,512]{1,0:T(8,128)(2,1)S(1)} %get-tuple-element.78), channel_id=1, source_target_pairs={{0,16},{8,24},{16,0},{24,8},{1,17},{9,25},{17,1},{25,9},{2,18},{10... | collective-permute-start | bytes 540680 | tf_op jit(solution)/shard_map/ppermute | solution.py:230
  127.4 20.1 %collective-permute-start.26 = (bf16[176,512]{1,0:T(8,128)(2,1)S(1)}, bf16[176,512]{1,0:T(8,128)(2,1)S(1)}, u32[]{:S(2)}, u32[]{:S(2)}) collective-permute-start(bf16[176,512]{1,0:T(8,128)(2,1)S(1)} %get-tuple-element.79), channel_id=1, source_target_pairs={{0,8},{8,16},{16,24},{24,0},{1,9},{9,17},{17,25},{25,1},{2,10},{10... | collective-permute-start | bytes 540680 | tf_op jit(solution)/shard_map/ppermute | solution.py:230

commit v12 on v8

--- a/solution.py
+++ b/solution.py
@@ -106,9 +106,18 @@
     copies = fetch(own, other, joined, sems, names, place)
     for j in range(4):
         take_rows(wide.at[:, pl.ds(j * width, width)], rows[j], second)
-    for copy in copies:
+    late = 2 * len(copies) // 4
+    for copy in copies[:late]:
         copy.wait()
-    out[...] = nt(wide[...], joined[...]).astype(BF16)
+    total = jnp.zeros(out.shape, F32)
+    for block in range(4):
+        if block == 2:
+            for copy in copies[late:]:
+                copy.wait()
+        spot = lax.rem(place[2] - place[1] + block + 4, 4)
+        columns = pl.ds(pl.multiple_of(spot * width, width), width)
+        total += nt(wide[:, columns], joined[:, columns])
+    out[...] = total.astype(BF16)
 
 
 def pieces(values):
@@ -192,7 +201,7 @@
         for m in range(3):
             columns = slice(2 * m * half, 2 * (m + 1) * half)
             total = tn(joined[:, columns], chosen[1 if m == 2 else 0, i])
-            keeps[i][m] = total[0:half, :]
+            keeps[i][m] = total[0:half, :].astype(BF16)
             sends[i][m] = total[half:, :].astype(BF16)
 
 
@@ -315,7 +324,7 @@
         weight_kernel,
         place,
         [shares[4]] + blocks,
-        [((3, half, width), kind) for kind in (F32, BF16) for _ in range(4)],
+        [((3, half, width), BF16)] * 8,
         [pltpu.VMEM((2, 4, slots, width), BF16)],
     )
     keeps, sends = terms[0:4], terms[4:8]
@@ -325,7 +334,7 @@
     arrived = [shift(near, "y", -1), shift(back, "y", 1)]
 
     def both_cores(i):
-        return keeps[i] + moved[i].astype(F32)
+        return keeps[i].astype(F32) + moved[i].astype(F32)
 
     passed = relay(both_cores(2).astype(BF16), "x")
     near, back = halfway(passed, both_cores(1), both_cores(3))

time: 150 us -> 152 us (1.013)
    ppermute x2, waiting for transfers between devices: 4.29 us -> 7.82 us  [turn(): lax.ppermute(value, ('core', 'zl'), [(2 * c + z, 2 * z + c) for c in rang...]
    ppermute x14, waiting for transfers between devices: 32.3 us -> 29.8 us  [shift(): return lax.ppermute(value, axis, [(i, (i + step) % 4) for i in range(4)])]
    ppermute x14, starting transfers between devices: 25.1 us -> 27.1 us  [shift(): return lax.ppermute(value, axis, [(i, (i + step) % 4) for i in range(4)])]
    ppermute x10, waiting for transfers between devices: 14.2 us -> 12.6 us  [swap(): return lax.ppermute(value, axis, [(0, 1), (1, 0)])]
    ppermute x2, starting transfers between devices: 8.64 us -> 7.01 us  [turn(): lax.ppermute(value, ('core', 'zl'), [(2 * c + z, 2 * z + c) for c in rang...]
    unnamed x25 -> x13, local copies, waits for them, and re-layouts: 2.52 us -> 3.57 us
  transfers between devices with their start and end apart: 31 -> 31, of which waited for: 18 -> 20; matrix products, arithmetic and copies ran while one was open for 2% -> 3% of each run, Pallas kernels for 7% -> 7%
where the time goes in v12:
time: 152 us
  waiting for transfers between devices  70.4 us (46%)
  starting transfers between devices  49.4 us (32%)
  Pallas kernels  20.4 us (13%)
  other arithmetic  6.52 us (4%)
  local copies, waits for them, and re-layouts  4.28 us (3%)
    ppermute x14, waiting for transfers between devices, shift(): return lax.ppermute(value, axis, [(i, (i + step) % 4) for i in range(4)])  29.8 us
    ppermute x14, starting transfers between devices, shift(): return lax.ppermute(value, axis, [(i, (i + step) % 4) for i in range(4)])  27.1 us
    pallas_call x7, Pallas kernels, call(): pl.pallas_call(kernel, out_shape=[jax.ShapeDtypeStruct(shape, kind) for s...  20.4 us
    ppermute x10, waiting for transfers between devices, swap(): return lax.ppermute(value, axis, [(0, 1), (1, 0)])  12.6 us
    ppermute x2, waiting for transfers between devices, relay(): lax.ppermute(value, ('core', axis), [(4 * c + i, 4 * c + j) for c, i, j i...  9.06 us
    ppermute x2, waiting for transfers between devices, turn(): lax.ppermute(value, ('core', 'zl'), [(2 * c + z, 2 * z + c) for c in rang...  7.82 us
    ppermute x2, starting transfers between devices, turn(): lax.ppermute(value, ('core', 'zl'), [(2 * c + z, 2 * z + c) for c in rang...  7.01 us
    ppermute x1, waiting for transfers between devices, body(): turned = lax.ppermute(own, ('core', 'zl'), [(1, 2), (2, 1)])  6.23 us
  transfers between devices with their start and end apart: 31, of which 20 were waited for; matrix products, arithmetic and copies ran while one was open for 3% of the time, Pallas kernels for 7%

profile of v12, /device:TPU:1, one launch (start us, length us, event | category | flops | bytes accessed | tf_op | source)
XLA Modules:
  0.0 151.8 jit_solution(16816730746353818807)
XLA Ops:
  2.1 1.0 pad_maximum_fusion.1.wide
  3.2 1.0 shard_map.84
  4.2 4.9 %collective-permute-start.3 = (bf16[3,192,512]{2,1,0:T(8,128)(2,1)}, bf16[3,192,512]{2,1,0:T(8,128)(2,1)S(1)}, u32[]{:S(2)}, u32[]{:S(2)}) collective-permute-start(bf16[3,192,512]{2,1,0:T(8,128)(2,1)} %bitcast.20), channel_id=1, source_target_pairs={{1,32},{32,1},{3,34},{34,3},{5,36},{36,5},{7,38},{38,7},{9,40},{40... | collective-permute-start | bytes 1769480 | tf_op jit(solution)/shard_map/ppermute | solution.py:279
  9.1 3.1 %collective-permute-start = (bf16[160,512]{1,0:T(8,128)(2,1)S(1)}, bf16[160,512]{1,0:T(8,128)(2,1)}, u32[]{:S(2)}, u32[]{:S(2)}) collective-permute-start(bf16[160,512]{1,0:T(8,128)(2,1)S(1)} %get-tuple-element.51), channel_id=1, source_target_pairs={{0,8},{8,16},{16,24},{24,0},{1,9},{9,17},{17,25},{25,1},{2,10},{10... | collective-permute-start | bytes 491528 | tf_op jit(solution)/shard_map/ppermute | solution.py:239
  12.2 4.2 %collective-permute-start.1 = (bf16[160,512]{1,0:T(8,128)(2,1)S(1)}, bf16[160,512]{1,0:T(8,128)(2,1)}, u32[]{:S(2)}, u32[]{:S(2)}) collective-permute-start(bf16[160,512]{1,0:T(8,128)(2,1)S(1)} %get-tuple-element.52), channel_id=1, source_target_pairs={{0,16},{8,24},{16,0},{24,8},{1,17},{9,25},{17,1},{25,9},{2,18},{10... | collective-permute-start | bytes 491528 | tf_op jit(solution)/shard_map/ppermute | solution.py:239
  16.4 2.4 %collective-permute-start.2 = (bf16[160,512]{1,0:T(8,128)(2,1)S(1)}, bf16[160,512]{1,0:T(8,128)(2,1)S(1)}, u32[]{:S(2)}, u32[]{:S(2)}) collective-permute-start(bf16[160,512]{1,0:T(8,128)(2,1)S(1)} %get-tuple-element.53), channel_id=1, source_target_pairs={{0,24},{8,0},{16,8},{24,16},{1,25},{9,1},{17,9},{25,17},{2,26},{10... | collective-permute-start | bytes 491528 | tf_op jit(solution)/shard_map/ppermute | solution.py:239
  18.8 6.2 %collective-permute-done.3 = bf16[3,192,512]{2,1,0:T(8,128)(2,1)S(1)} collective-permute-done((bf16[3,192,512]{2,1,0:T(8,128)(2,1)}, bf16[3,192,512]{2,1,0:T(8,128)(2,1)S(1)}, u32[]{:S(2)}, u32[]{:S(2)}) %collective-permute-start.3) | collective-permute-done | bytes 589856 | tf_op jit(solution)/shard_map/ppermute | solution.py:279
  25.1 2.6 %collective-permute-start.5 = (bf16[3,192,512]{2,1,0:T(8,128)(2,1)S(1)}, bf16[3,192,512]{2,1,0:T(8,128)(2,1)S(1)}, u32[]{:S(2)}, u32[]{:S(2)}) collective-permute-start(bf16[3,192,512]{2,1,0:T(8,128)(2,1)S(1)} %broadcast_select_fusion.2.refs_4_), channel_id=1, source_target_pairs={{0,192},{64,0},{128,64},{192,128},{1,193},{65,1},{129,65},{193,129... | collective-permute-start | bytes 1769480 | tf_op jit(solution)/shard_map/ppermute | solution.py:239
  27.7 2.9 %collective-permute-done = bf16[160,512]{1,0:T(8,128)(2,1)} collective-permute-done((bf16[160,512]{1,0:T(8,128)(2,1)S(1)}, bf16[160,512]{1,0:T(8,128)(2,1)}, u32[]{:S(2)}, u32[]{:S(2)}) %collective-permute-start) | collective-permute-done | bytes 163872 | tf_op jit(solution)/shard_map/ppermute | solution.py:239
  30.6 0.9 constant_dynamic-update-slice_fusion.2
  31.5 4.9 %collective-permute-done.1 = bf16[160,512]{1,0:T(8,128)(2,1)} collective-permute-done((bf16[160,512]{1,0:T(8,128)(2,1)S(1)}, bf16[160,512]{1,0:T(8,128)(2,1)}, u32[]{:S(2)}, u32[]{:S(2)}) %collective-permute-start.1) | collective-permute-done | bytes 163872 | tf_op jit(solution)/shard_map/ppermute | solution.py:239
  36.4 0.9 constant_dynamic-update-slice_fusion.1
  37.4 2.8 %collective-permute-start.7 = (bf16[640,512]{1,0:T(8,128)(2,1)S(1)}, bf16[640,512]{1,0:T(8,128)(2,1)}, u32[]{:S(2)}, u32[]{:S(2)}) collective-permute-start(bf16[640,512]{1,0:T(8,128)(2,1)S(1)} %constant_dynamic-update-slice_fusion.refs_0_), channel_id=1, source_target_pairs={{0,6},{2,0},{4,2},{6,4},{1,7},{3,1},{5,3},{7,5},{8,14},{10,8},{12,... | collective-permute-start | bytes 1966088 | tf_op jit(solution)/shard_map/ppermute | solution.py:239
  40.3 2.6 %collective-permute-start.9 = (bf16[3,192,512]{2,1,0:T(8,128)(2,1)S(1)}, bf16[3,192,512]{2,1,0:T(8,128)(2,1)S(1)}, u32[]{:S(2)}, u32[]{:S(2)}) collective-permute-start(bf16[3,192,512]{2,1,0:T(8,128)(2,1)S(1)} %broadcast_select_fusion.1), channel_id=1, source_target_pairs={{0,64},{64,128},{128,192},{192,0},{32,224},{96,32},{160,96},{224,1... | collective-permute-start | bytes 1769480 | tf_op jit(solution)/shard_map/ppermute | solution.py:245
  42.8 4.9 %collective-permute-done.7.refs_3_ = bf16[640,512]{1,0:T(8,128)(2,1)} collective-permute-done((bf16[640,512]{1,0:T(8,128)(2,1)S(1)}, bf16[640,512]{1,0:T(8,128)(2,1)}, u32[]{:S(2)}, u32[]{:S(2)}) %collective-permute-start.7) | collective-permute-done | bytes 655392 | tf_op jit(solution)/shard_map/ppermute | solution.py:239
  47.7 5.6 %collective-permute-done.6.refs_1_ = bf16[640,512]{1,0:T(8,128)(2,1)S(1)} collective-permute-done((bf16[640,512]{1,0:T(8,128)(2,1)S(1)}, bf16[640,512]{1,0:T(8,128)(2,1)S(1)}, u32[]{:S(2)}, u32[]{:S(2)}) %collective-permute-start.6) | collective-permute-done | bytes 655392 | tf_op jit(solution)/shard_map/ppermute | solution.py:239
  53.3 1.4 broadcast_select_fusion
  55.9 1.0 collective-permute-done.10.refs_8_
  56.9 0.8 collective-permute-done.11.refs_9_
  57.8 0.8 collective-permute-done.13.refs_11_
  58.6 5.6 %collective-permute-done.8.refs_2_ = bf16[640,512]{1,0:T(8,128)(2,1)S(1)} collective-permute-done((bf16[640,512]{1,0:T(8,128)(2,1)S(1)}, bf16[640,512]{1,0:T(8,128)(2,1)S(1)}, u32[]{:S(2)}, u32[]{:S(2)}) %collective-permute-start.8) | collective-permute-done | bytes 655392 | tf_op jit(solution)/shard_map/ppermute | solution.py:246
  64.3 0.8 copy-done.3
  65.1 4.6 %shard_map.85 = (bf16[320,768]{1,0:T(8,128)(2,1)S(1)}, bf16[768,2048]{1,0:T(8,128)(2,1)}) custom-call(s32[5]{0:T(128)S(1)} %stack.23.place, bf16[640,512]{1,0:T(8,128)(2,1)S(1)} %constant_dynamic-update-slice_fusion.refs_0_, bf16[640,512]{1,0:T(8,128)(2,1)} %copy-done, bf16[640,512]{1,0:T(8,128)(2,1)} %copy-done.3, ...), custom_call_target="tpu_custom_call" | custom-call | tf_op jit(solution)/shard_map/pallas_call | solution.py:33
  70.0 3.5 %shard_map.86 = (bf16[320,384]{1,0:T(8,128)(2,1)S(1)}, bf16[384,2048]{1,0:T(8,128)(2,1)}) custom-call(s32[5]{0:T(128)S(1)} %stack.23.place, bf16[640,512]{1,0:T(8,128)(2,1)S(1)} %constant_dynamic-update-slice_fusion.refs_0_, bf16[640,512]{1,0:T(8,128)(2,1)} %copy-done, bf16[640,512]{1,0:T(8,128)(2,1)} %copy-done.3, ...), custom_call_target="tpu_custom_call" | custom-call | tf_op jit(solution)/shard_map/pallas_call | solution.py:33
  73.5 1.5 %collective-permute-start.15 = (bf16[320,384]{1,0:T(8,128)(2,1)S(1)}, bf16[320,384]{1,0:T(8,128)(2,1)S(1)}, u32[]{:S(2)}, u32[]{:S(2)}) collective-permute-start(bf16[320,384]{1,0:T(8,128)(2,1)S(1)} %get-tuple-element.61.down), channel_id=1, source_target_pairs={{0,1},{1,0},{2,3},{3,2},{4,5},{5,4},{6,7},{7,6},{8,9},{9,8},{10,11... | collective-permute-start | bytes 737288 | tf_op jit(solution)/shard_map/ppermute | solution.py:250
  75.0 9.9 %collective-permute-done.15.down_far = bf16[320,384]{1,0:T(8,128)(2,1)S(1)} collective-permute-done((bf16[320,384]{1,0:T(8,128)(2,1)S(1)}, bf16[320,384]{1,0:T(8,128)(2,1)S(1)}, u32[]{:S(2)}, u32[]{:S(2)}) %collective-permute-start.15) | collective-permute-done | bytes 245792 | tf_op jit(solution)/shard_map/ppermute | solution.py:250
  84.9 4.5 %shard_map.87 = (f32[656,512]{1,0:T(8,128)S(1)}, bf16[656,512]{1,0:T(8,128)(2,1)S(1)}, bf16[656,512]{1,0:T(8,128)(2,1)S(1)}, bf16[656,512]{1,0:T(8,128)(2,1)S(1)}, bf16[320,1152]{1,0:T(8,128)(2,1)S(1)}) custom-call(s32[5]{0:T(128)S(1)} %stack.23.place, bf16[320,768]{1,0:T(8,128)(2,1)S(1)} %get-tuple-element.60.pair, ...), custom_call_target="tpu_custom_call" | custom-call | tf_op jit(solution)/shard_map/pallas_call | solution.py:33
  89.5 0.9 copy-done.2
  90.3 1.1 collective-permute-start.16
  91.4 4.3 %shard_map.88 = (bf16[3,192,512]{2,1,0:T(8,128)(2,1)S(1)}, bf16[3,192,512]{2,1,0:T(8,128)(2,1)S(1)}, bf16[3,192,512]{2,1,0:T(8,128)(2,1)S(1)}, bf16[3,192,512]{2...) custom-call(s32[5]{0:T(128)S(1)} %stack.23.place, ...), custom_call_target="tpu_custom_call" | custom-call | tf_op jit(solution)/shard_map/pallas_call | solution.py:33
  96.8 3.4 %collective-permute-done.16 = bf16[656,512]{1,0:T(8,128)(2,1)S(1)} collective-permute-done((bf16[656,512]{1,0:T(8,128)(2,1)S(1)}, bf16[656,512]{1,0:T(8,128)(2,1)S(1)}, u32[]{:S(2)}, u32[]{:S(2)}) %collective-permute-start.16) | collective-permute-done | bytes 671776 | tf_op jit(solution)/shard_map/ppermute | solution.py:246
  100.8 2.6 %collective-permute-start.21 = (bf16[3,192,512]{2,1,0:T(8,128)(2,1)S(1)}, bf16[3,192,512]{2,1,0:T(8,128)(2,1)S(1)}, u32[]{:S(2)}, u32[]{:S(2)}) collective-permute-start(bf16[3,192,512]{2,1,0:T(8,128)(2,1)S(1)} %add_convert_fusion.1), channel_id=1, source_target_pairs={{0,64},{64,128},{128,192},{192,0},{32,224},{96,32},{160,96},{224,1... | collective-permute-start | bytes 1769480 | tf_op jit(solution)/shard_map/ppermute | solution.py:245
  103.4 2.0 %collective-permute-start.26 = (bf16[656,512]{1,0:T(8,128)(2,1)S(1)}, bf16[656,512]{1,0:T(8,128)(2,1)S(1)}, u32[]{:S(2)}, u32[]{:S(2)}) collective-permute-start(bf16[656,512]{1,0:T(8,128)(2,1)S(1)} %get-tuple-element.82), channel_id=1, source_target_pairs={{0,6},{2,0},{4,2},{6,4},{1,7},{3,1},{5,3},{7,5},{8,14},{10,8},{12,... | collective-permute-start | bytes 2015240 | tf_op jit(solution)/shard_map/ppermute | solution.py:239
  105.4 4.9 %collective-permute-done.21 = bf16[3,192,512]{2,1,0:T(8,128)(2,1)S(1)} collective-permute-done((bf16[3,192,512]{2,1,0:T(8,128)(2,1)S(1)}, bf16[3,192,512]{2,1,0:T(8,128)(2,1)S(1)}, u32[]{:S(2)}, u32[]{:S(2)}) %collective-permute-start.21) | collective-permute-done | bytes 589856 | tf_op jit(solution)/shard_map/ppermute | solution.py:245
  110.7 3.7 %collective-permute-start.22 = (bf16[3,192,512]{2,1,0:T(8,128)(2,1)S(1)}, bf16[3,192,512]{2,1,0:T(8,128)(2,1)S(1)}, u32[]{:S(2)}, u32[]{:S(2)}) collective-permute-start(bf16[3,192,512]{2,1,0:T(8,128)(2,1)S(1)} %get-tuple-element.98), channel_id=1, source_target_pairs={{0,192},{64,0},{128,64},{192,128},{1,193},{65,1},{129,65},{193,129... | collective-permute-start | bytes 1769480 | tf_op jit(solution)/shard_map/ppermute | solution.py:239
  114.5 5.8 %collective-permute-done.26.one = bf16[656,512]{1,0:T(8,128)(2,1)S(1)} collective-permute-done((bf16[656,512]{1,0:T(8,128)(2,1)S(1)}, bf16[656,512]{1,0:T(8,128)(2,1)S(1)}, u32[]{:S(2)}, u32[]{:S(2)}) %collective-permute-start.26) | collective-permute-done | bytes 671776 | tf_op jit(solution)/shard_map/ppermute | solution.py:239
  120.3 2.0 %collective-permute-done.27.three = bf16[656,512]{1,0:T(8,128)(2,1)S(1)} collective-permute-done((bf16[656,512]{1,0:T(8,128)(2,1)S(1)}, bf16[656,512]{1,0:T(8,128)(2,1)S(1)}, u32[]{:S(2)}, u32[]{:S(2)}) %collective-permute-start.27) | collective-permute-done | bytes 671776 | tf_op jit(solution)/shard_map/ppermute | solution.py:239
  123.0 3.5 %collective-permute-start.28 = (bf16[176,512]{1,0:T(8,128)(2,1)S(1)}, bf16[176,512]{1,0:T(8,128)(2,1)S(1)}, u32[]{:S(2)}, u32[]{:S(2)}) collective-permute-start(bf16[176,512]{1,0:T(8,128)(2,1)S(1)} %get-tuple-element.85), channel_id=1, source_target_pairs={{0,24},{8,0},{16,8},{24,16},{1,25},{9,1},{17,9},{25,17},{2,26},{10... | collective-permute-start | bytes 540680 | tf_op jit(solution)/shard_map/ppermute | solution.py:239
  126.5 1.8 %collective-permute-start.29 = (bf16[176,512]{1,0:T(8,128)(2,1)S(1)}, bf16[176,512]{1,0:T(8,128)(2,1)S(1)}, u32[]{:S(2)}, u32[]{:S(2)}) collective-permute-start(bf16[176,512]{1,0:T(8,128)(2,1)S(1)} %get-tuple-element.86), channel_id=1, source_target_pairs={{0,16},{8,24},{16,0},{24,8},{1,17},{9,25},{17,1},{25,9},{2,18},{10... | collective-permute-start | bytes 540680 | tf_op jit(solution)/shard_map/ppermute | solution.py:239
  128.3 1.2 collective-permute-start.30
  130.2 5.1 %collective-permute-start.25 = (bf16[288,512]{1,0:T(8,128)(2,1)S(1)}, bf16[288,512]{1,0:T(8,128)(2,1)S(1)}, u32[]{:S(2)}, u32[]{:S(2)}) collective-permute-start(bf16[288,512]{1,0:T(8,128)(2,1)S(1)} %get-tuple-element.96), channel_id=1, source_target_pairs={{0,0},{1,32},{32,1},{33,33},{2,2},{3,34},{34,3},{35,35},{4,4},{5,3... | collective-permute-start | bytes 884744 | tf_op jit(solution)/shard_map/ppermute | solution.py:254
  135.3 1.9 %collective-permute-start.24 = (bf16[288,512]{1,0:T(8,128)(2,1)S(1)}, bf16[288,512]{1,0:T(8,128)(2,1)S(1)}, u32[]{:S(2)}, u32[]{:S(2)}) collective-permute-start(bf16[288,512]{1,0:T(8,128)(2,1)S(1)} %get-tuple-element.97), channel_id=1, source_target_pairs={{0,0},{1,32},{32,1},{33,33},{2,2},{3,34},{34,3},{35,35},{4,4},{5,3... | collective-permute-start | bytes 884744 | tf_op jit(solution)/shard_map/ppermute | solution.py:254
  137.3 1.0 collective-permute-done.28.refs_1_
  138.3 1.7 %collective-permute-done.29.refs_2_ = bf16[176,512]{1,0:T(8,128)(2,1)S(1)} collective-permute-done((bf16[176,512]{1,0:T(8,128)(2,1)S(1)}, bf16[176,512]{1,0:T(8,128)(2,1)S(1)}, u32[]{:S(2)}, u32[]{:S(2)}) %collective-permute-start.29) | collective-permute-done | bytes 180256 | tf_op jit(solution)/shard_map/ppermute | solution.py:239
  140.5 1.7 %shard_map.90 = (bf16[128,512]{1,0:T(8,128)(2,1)}, bf16[128,512]{1,0:T(8,128)(2,1)}, f32[8,128]{1,0:T(8,128)S(1)}) custom-call(s32[5]{0:T(128)S(1)} %stack.23.place, f32[4,128]{1,0:T(4,128)S(1)} %pad_maximum_fusion.2.small, bf16[320,128]{1,0:T(8,128)(2,1)S(1)} %get-tuple-element.80.placing, bf16[176,512]{1,0:T(8,128)(2,1)S(1)} %get-tuple-element.84.refs_0_, ...), custom_call_target="tpu_custom_call" | custom-call | tf_op jit(solution)/shard_map/pallas_call | solution.py:33
  142.8 4.7 %collective-permute-done.25 = bf16[288,512]{1,0:T(8,128)(2,1)S(1)} collective-permute-done((bf16[288,512]{1,0:T(8,128)(2,1)S(1)}, bf16[288,512]{1,0:T(8,128)(2,1)S(1)}, u32[]{:S(2)}, u32[]{:S(2)}) %collective-permute-start.25) | collective-permute-done | bytes 294944 | tf_op jit(solution)/shard_map/ppermute | solution.py:254
  147.4 3.2 %collective-permute-done.24 = bf16[288,512]{1,0:T(8,128)(2,1)S(1)} collective-permute-done((bf16[288,512]{1,0:T(8,128)(2,1)S(1)}, bf16[288,512]{1,0:T(8,128)(2,1)S(1)}, u32[]{:S(2)}, u32[]{:S(2)}) %collective-permute-start.24) | collective-permute-done | bytes 294944 | tf_op jit(solution)/shard_map/ppermute | solution.py:254
  150.6 1.2 convert.2
  (50 shorter events, 8.0 us)
Async XLA Ops:
  0.6 24.4 %copy-start.4 = (bf16[1,3,192,512]{3,2,1,0:T(8,128)(2,1)S(1)}, bf16[1,3,192,512]{3,2,1,0:T(8,128)(2,1)}, u32[]{:S(2)}) copy-start(bf16[1,3,192,512]{3,2,1,0:T(8,128)(2,1)} %param.8) | copy-start | bytes 1769476
  4.2 20.8 %collective-permute-start.3 = (bf16[3,192,512]{2,1,0:T(8,128)(2,1)}, bf16[3,192,512]{2,1,0:T(8,128)(2,1)S(1)}, u32[]{:S(2)}, u32[]{:S(2)}) collective-permute-start(bf16[3,192,512]{2,1,0:T(8,128)(2,1)} %bitcast.20), channel_id=1, source_target_pairs={{1,32},{32,1},{3,34},{34,3},{5,36},{36,5},{7,38},{38,7},{9,40},{40... | collective-permute-start | bytes 1769480 | tf_op jit(solution)/shard_map/ppermute | solution.py:279
  9.1 21.5 %collective-permute-start = (bf16[160,512]{1,0:T(8,128)(2,1)S(1)}, bf16[160,512]{1,0:T(8,128)(2,1)}, u32[]{:S(2)}, u32[]{:S(2)}) collective-permute-start(bf16[160,512]{1,0:T(8,128)(2,1)S(1)} %get-tuple-element.51), channel_id=1, source_target_pairs={{0,8},{8,16},{16,24},{24,0},{1,9},{9,17},{17,25},{25,1},{2,10},{10... | collective-permute-start | bytes 491528 | tf_op jit(solution)/shard_map/ppermute | solution.py:239
  12.2 24.3 %collective-permute-start.1 = (bf16[160,512]{1,0:T(8,128)(2,1)S(1)}, bf16[160,512]{1,0:T(8,128)(2,1)}, u32[]{:S(2)}, u32[]{:S(2)}) collective-permute-start(bf16[160,512]{1,0:T(8,128)(2,1)S(1)} %get-tuple-element.52), channel_id=1, source_target_pairs={{0,16},{8,24},{16,0},{24,8},{1,17},{9,25},{17,1},{25,9},{2,18},{10... | collective-permute-start | bytes 491528 | tf_op jit(solution)/shard_map/ppermute | solution.py:239
  16.4 21.0 %collective-permute-start.2 = (bf16[160,512]{1,0:T(8,128)(2,1)S(1)}, bf16[160,512]{1,0:T(8,128)(2,1)S(1)}, u32[]{:S(2)}, u32[]{:S(2)}) collective-permute-start(bf16[160,512]{1,0:T(8,128)(2,1)S(1)} %get-tuple-element.53), channel_id=1, source_target_pairs={{0,24},{8,0},{16,8},{24,16},{1,25},{9,1},{17,9},{25,17},{2,26},{10... | collective-permute-start | bytes 491528 | tf_op jit(solution)/shard_map/ppermute | solution.py:239
  25.1 15.1 %collective-permute-start.5 = (bf16[3,192,512]{2,1,0:T(8,128)(2,1)S(1)}, bf16[3,192,512]{2,1,0:T(8,128)(2,1)S(1)}, u32[]{:S(2)}, u32[]{:S(2)}) collective-permute-start(bf16[3,192,512]{2,1,0:T(8,128)(2,1)S(1)} %broadcast_select_fusion.2.refs_4_), channel_id=1, source_target_pairs={{0,192},{64,0},{128,64},{192,128},{1,193},{65,1},{129,65},{193,129... | collective-permute-start | bytes 1769480 | tf_op jit(solution)/shard_map/ppermute | solution.py:239
  27.6 12.6 %collective-permute-start.4 = (bf16[3,192,512]{2,1,0:T(8,128)(2,1)S(1)}, bf16[3,192,512]{2,1,0:T(8,128)(2,1)S(1)}, u32[]{:S(2)}, u32[]{:S(2)}) collective-permute-start(bf16[3,192,512]{2,1,0:T(8,128)(2,1)S(1)} %broadcast_select_fusion.2.refs_4_), channel_id=1, source_target_pairs={{0,64},{64,128},{128,192},{192,0},{1,65},{65,129},{129,193},{193,1... | collective-permute-start | bytes 1769480 | tf_op jit(solution)/shard_map/ppermute | solution.py:239
  37.4 10.3 %collective-permute-start.7 = (bf16[640,512]{1,0:T(8,128)(2,1)S(1)}, bf16[640,512]{1,0:T(8,128)(2,1)}, u32[]{:S(2)}, u32[]{:S(2)}) collective-permute-start(bf16[640,512]{1,0:T(8,128)(2,1)S(1)} %constant_dynamic-update-slice_fusion.refs_0_), channel_id=1, source_target_pairs={{0,6},{2,0},{4,2},{6,4},{1,7},{3,1},{5,3},{7,5},{8,14},{10,8},{12,... | collective-permute-start | bytes 1966088 | tf_op jit(solution)/shard_map/ppermute | solution.py:239
  40.2 13.1 %collective-permute-start.6 = (bf16[640,512]{1,0:T(8,128)(2,1)S(1)}, bf16[640,512]{1,0:T(8,128)(2,1)S(1)}, u32[]{:S(2)}, u32[]{:S(2)}) collective-permute-start(bf16[640,512]{1,0:T(8,128)(2,1)S(1)} %constant_dynamic-update-slice_fusion.refs_0_), channel_id=1, source_target_pairs={{0,2},{2,4},{4,6},{6,0},{1,3},{3,5},{5,7},{7,1},{8,10},{10,12},{12... | collective-permute-start | bytes 1966088 | tf_op jit(solution)/shard_map/ppermute | solution.py:239
  40.3 15.2 %collective-permute-start.9 = (bf16[3,192,512]{2,1,0:T(8,128)(2,1)S(1)}, bf16[3,192,512]{2,1,0:T(8,128)(2,1)S(1)}, u32[]{:S(2)}, u32[]{:S(2)}) collective-permute-start(bf16[3,192,512]{2,1,0:T(8,128)(2,1)S(1)} %broadcast_select_fusion.1), channel_id=1, source_target_pairs={{0,64},{64,128},{128,192},{192,0},{32,224},{96,32},{160,96},{224,1... | collective-permute-start | bytes 1769480 | tf_op jit(solution)/shard_map/ppermute | solution.py:245
  53.3 10.9 %copy-start = (bf16[640,512]{1,0:T(8,128)(2,1)}, bf16[640,512]{1,0:T(8,128)(2,1)S(1)}, u32[]{:S(2)}) copy-start(bf16[640,512]{1,0:T(8,128)(2,1)S(1)} %collective-permute-done.6.refs_1_) | copy-start | bytes 1966084
  54.7 9.5 %collective-permute-start.8 = (bf16[640,512]{1,0:T(8,128)(2,1)S(1)}, bf16[640,512]{1,0:T(8,128)(2,1)S(1)}, u32[]{:S(2)}, u32[]{:S(2)}) collective-permute-start(bf16[640,512]{1,0:T(8,128)(2,1)S(1)} %broadcast_select_fusion), channel_id=1, source_target_pairs={{0,2},{2,4},{4,6},{6,0},{32,38},{34,32},{36,34},{38,36},{1,3},{3,5... | collective-permute-start | bytes 1966088 | tf_op jit(solution)/shard_map/ppermute | solution.py:246
  54.8 2.1 %collective-permute-start.10 = (bf16[3,192,512]{2,1,0:T(8,128)(2,1)S(1)}, bf16[3,192,512]{2,1,0:T(8,128)(2,1)S(1)}, u32[]{:S(2)}, u32[]{:S(2)}) collective-permute-start(bf16[3,192,512]{2,1,0:T(8,128)(2,1)S(1)} %broadcast_select_fusion.2.refs_4_), channel_id=1, source_target_pairs={{0,32},{32,0},{1,33},{33,1},{2,34},{34,2},{3,35},{35,3},{4,36},{36... | collective-permute-start | bytes 1769480 | tf_op jit(solution)/shard_map/ppermute | solution.py:250
  54.9 2.8 %collective-permute-start.11 = (bf16[3,192,512]{2,1,0:T(8,128)(2,1)S(1)}, bf16[3,192,512]{2,1,0:T(8,128)(2,1)S(1)}, u32[]{:S(2)}, u32[]{:S(2)}) collective-permute-start(bf16[3,192,512]{2,1,0:T(8,128)(2,1)S(1)} %collective-permute-done.4.refs_5_), channel_id=1, source_target_pairs={{0,32},{32,0},{1,33},{33,1},{2,34},{34,2},{3,35},{35,3},{4,36},{36... | collective-permute-start | bytes 1769480 | tf_op jit(solution)/shard_map/ppermute | solution.py:250
  55.4 3.2 %collective-permute-start.13 = (bf16[3,192,512]{2,1,0:T(8,128)(2,1)S(1)}, bf16[3,192,512]{2,1,0:T(8,128)(2,1)S(1)}, u32[]{:S(2)}, u32[]{:S(2)}) collective-permute-start(bf16[3,192,512]{2,1,0:T(8,128)(2,1)S(1)} %collective-permute-done.5.refs_7_), channel_id=1, source_target_pairs={{0,32},{32,0},{1,33},{33,1},{2,34},{34,2},{3,35},{35,3},{4,36},{36... | collective-permute-start | bytes 1769480 | tf_op jit(solution)/shard_map/ppermute | solution.py:250
  55.5 8.7 %collective-permute-start.12 = (bf16[3,192,512]{2,1,0:T(8,128)(2,1)S(1)}, bf16[3,192,512]{2,1,0:T(8,128)(2,1)S(1)}, u32[]{:S(2)}, u32[]{:S(2)}) collective-permute-start(bf16[3,192,512]{2,1,0:T(8,128)(2,1)S(1)} %collective-permute-done.9.refs_6_), channel_id=1, source_target_pairs={{0,32},{32,0},{1,33},{33,1},{2,34},{34,2},{3,35},{35,3},{4,36},{36... | collective-permute-start | bytes 1769480 | tf_op jit(solution)/shard_map/ppermute | solution.py:250
  64.2 0.8 copy-start.3
  69.7 15.3 %collective-permute-start.14 = (bf16[320,768]{1,0:T(8,128)(2,1)S(1)}, bf16[320,768]{1,0:T(8,128)(2,1)S(1)}, u32[]{:S(2)}, u32[]{:S(2)}) collective-permute-start(bf16[320,768]{1,0:T(8,128)(2,1)S(1)} %get-tuple-element.60.pair), channel_id=1, source_target_pairs={{0,1},{1,0},{2,3},{3,2},{4,5},{5,4},{6,7},{7,6},{8,9},{9,8},{10,11... | collective-permute-start | bytes 1474568 | tf_op jit(solution)/shard_map/ppermute | solution.py:250
  73.5 11.4 %collective-permute-start.15 = (bf16[320,384]{1,0:T(8,128)(2,1)S(1)}, bf16[320,384]{1,0:T(8,128)(2,1)S(1)}, u32[]{:S(2)}, u32[]{:S(2)}) collective-permute-start(bf16[320,384]{1,0:T(8,128)(2,1)S(1)} %get-tuple-element.61.down), channel_id=1, source_target_pairs={{0,1},{1,0},{2,3},{3,2},{4,5},{5,4},{6,7},{7,6},{8,9},{9,8},{10,11... | collective-permute-start | bytes 737288 | tf_op jit(solution)/shard_map/ppermute | solution.py:250
  84.9 6.4 %copy-start.1 = (bf16[640,512]{1,0:T(8,128)(2,1)S(1)}, bf16[640,512]{1,0:T(8,128)(2,1)}, u32[]{:S(2)}) copy-start(bf16[640,512]{1,0:T(8,128)(2,1)} %copy-done) | copy-start | bytes 1966084
  89.5 0.9 copy-start.2
  90.3 9.9 %collective-permute-start.16 = (bf16[656,512]{1,0:T(8,128)(2,1)S(1)}, bf16[656,512]{1,0:T(8,128)(2,1)S(1)}, u32[]{:S(2)}, u32[]{:S(2)}) collective-permute-start(bf16[656,512]{1,0:T(8,128)(2,1)S(1)} %get-tuple-element.67), channel_id=1, source_target_pairs={{0,2},{2,4},{4,6},{6,0},{32,38},{34,32},{36,34},{38,36},{1,3},{3,5... | collective-permute-start | bytes 2015240 | tf_op jit(solution)/shard_map/ppermute | solution.py:246
  95.7 4.9 %collective-permute-start.17 = (bf16[3,192,512]{2,1,0:T(8,128)(2,1)S(1)}, bf16[3,192,512]{2,1,0:T(8,128)(2,1)S(1)}, u32[]{:S(2)}, u32[]{:S(2)}) collective-permute-start(bf16[3,192,512]{2,1,0:T(8,128)(2,1)S(1)} %get-tuple-element.69), channel_id=1, source_target_pairs={{0,32},{32,0},{1,33},{33,1},{2,34},{34,2},{3,35},{35,3},{4,36},{36... | collective-permute-start | bytes 1769480 | tf_op jit(solution)/shard_map/ppermute | solution.py:250
  95.8 4.8 %collective-permute-start.18 = (bf16[3,192,512]{2,1,0:T(8,128)(2,1)S(1)}, bf16[3,192,512]{2,1,0:T(8,128)(2,1)S(1)}, u32[]{:S(2)}, u32[]{:S(2)}) collective-permute-start(bf16[3,192,512]{2,1,0:T(8,128)(2,1)S(1)} %get-tuple-element.70), channel_id=1, source_target_pairs={{0,32},{32,0},{1,33},{33,1},{2,34},{34,2},{3,35},{35,3},{4,36},{36... | collective-permute-start | bytes 1769480 | tf_op jit(solution)/shard_map/ppermute | solution.py:250
  96.3 4.3 %collective-permute-start.19 = (bf16[3,192,512]{2,1,0:T(8,128)(2,1)S(1)}, bf16[3,192,512]{2,1,0:T(8,128)(2,1)S(1)}, u32[]{:S(2)}, u32[]{:S(2)}) collective-permute-start(bf16[3,192,512]{2,1,0:T(8,128)(2,1)S(1)} %get-tuple-element.71), channel_id=1, source_target_pairs={{0,32},{32,0},{1,33},{33,1},{2,34},{34,2},{3,35},{35,3},{4,36},{36... | collective-permute-start | bytes 1769480 | tf_op jit(solution)/shard_map/ppermute | solution.py:250
  96.4 4.3 %collective-permute-start.20 = (bf16[3,192,512]{2,1,0:T(8,128)(2,1)S(1)}, bf16[3,192,512]{2,1,0:T(8,128)(2,1)S(1)}, u32[]{:S(2)}, u32[]{:S(2)}) collective-permute-start(bf16[3,192,512]{2,1,0:T(8,128)(2,1)S(1)} %get-tuple-element.72), channel_id=1, source_target_pairs={{0,32},{32,0},{1,33},{33,1},{2,34},{34,2},{3,35},{35,3},{4,36},{36... | collective-permute-start | bytes 1769480 | tf_op jit(solution)/shard_map/ppermute | solution.py:250
  100.8 9.4 %collective-permute-start.21 = (bf16[3,192,512]{2,1,0:T(8,128)(2,1)S(1)}, bf16[3,192,512]{2,1,0:T(8,128)(2,1)S(1)}, u32[]{:S(2)}, u32[]{:S(2)}) collective-permute-start(bf16[3,192,512]{2,1,0:T(8,128)(2,1)S(1)} %add_convert_fusion.1), channel_id=1, source_target_pairs={{0,64},{64,128},{128,192},{192,0},{32,224},{96,32},{160,96},{224,1... | collective-permute-start | bytes 1769480 | tf_op jit(solution)/shard_map/ppermute | solution.py:245
  103.4 16.9 %collective-permute-start.26 = (bf16[656,512]{1,0:T(8,128)(2,1)S(1)}, bf16[656,512]{1,0:T(8,128)(2,1)S(1)}, u32[]{:S(2)}, u32[]{:S(2)}) collective-permute-start(bf16[656,512]{1,0:T(8,128)(2,1)S(1)} %get-tuple-element.82), channel_id=1, source_target_pairs={{0,6},{2,0},{4,2},{6,4},{1,7},{3,1},{5,3},{7,5},{8,14},{10,8},{12,... | collective-permute-start | bytes 2015240 | tf_op jit(solution)/shard_map/ppermute | solution.py:239
  105.4 16.9 %collective-permute-start.27 = (bf16[656,512]{1,0:T(8,128)(2,1)S(1)}, bf16[656,512]{1,0:T(8,128)(2,1)S(1)}, u32[]{:S(2)}, u32[]{:S(2)}) collective-permute-start(bf16[656,512]{1,0:T(8,128)(2,1)S(1)} %get-tuple-element.83), channel_id=1, source_target_pairs={{0,2},{2,4},{4,6},{6,0},{1,3},{3,5},{5,7},{7,1},{8,10},{10,12},{12... | collective-permute-start | bytes 2015240 | tf_op jit(solution)/shard_map/ppermute | solution.py:239
  110.7 18.7 %collective-permute-start.22 = (bf16[3,192,512]{2,1,0:T(8,128)(2,1)S(1)}, bf16[3,192,512]{2,1,0:T(8,128)(2,1)S(1)}, u32[]{:S(2)}, u32[]{:S(2)}) collective-permute-start(bf16[3,192,512]{2,1,0:T(8,128)(2,1)S(1)} %get-tuple-element.98), channel_id=1, source_target_pairs={{0,192},{64,0},{128,64},{192,128},{1,193},{65,1},{129,65},{193,129... | collective-permute-start | bytes 1769480 | tf_op jit(solution)/shard_map/ppermute | solution.py:239
  114.4 15.4 %collective-permute-start.23 = (bf16[3,192,512]{2,1,0:T(8,128)(2,1)S(1)}, bf16[3,192,512]{2,1,0:T(8,128)(2,1)S(1)}, u32[]{:S(2)}, u32[]{:S(2)}) collective-permute-start(bf16[3,192,512]{2,1,0:T(8,128)(2,1)S(1)} %get-tuple-element.99), channel_id=1, source_target_pairs={{0,64},{64,128},{128,192},{192,0},{1,65},{65,129},{129,193},{193,1... | collective-permute-start | bytes 1769480 | tf_op jit(solution)/shard_map/ppermute | solution.py:239
  123.0 15.2 %collective-permute-start.28 = (bf16[176,512]{1,0:T(8,128)(2,1)S(1)}, bf16[176,512]{1,0:T(8,128)(2,1)S(1)}, u32[]{:S(2)}, u32[]{:S(2)}) collective-permute-start(bf16[176,512]{1,0:T(8,128)(2,1)S(1)} %get-tuple-element.85), channel_id=1, source_target_pairs={{0,24},{8,0},{16,8},{24,16},{1,25},{9,1},{17,9},{25,17},{2,26},{10... | collective-permute-start | bytes 540680 | tf_op jit(solution)/shard_map/ppermute | solution.py:239
  126.5 13.4 %collective-permute-start.29 = (bf16[176,512]{1,0:T(8,128)(2,1)S(1)}, bf16[176,512]{1,0:T(8,128)(2,1)S(1)}, u32[]{:S(2)}, u32[]{:S(2)}) collective-permute-start(bf16[176,512]{1,0:T(8,128)(2,1)S(1)} %get-tuple-element.86), channel_id=1, source_target_pairs={{0,16},{8,24},{16,0},{24,8},{1,17},{9,25},{17,1},{25,9},{2,18},{10... | collective-permute-start | bytes 540680 | tf_op jit(solution)/shard_map/ppermute | solution.py:239
  128.3 12.2 %collective-permute-start.30 = (bf16[176,512]{1,0:T(8,128)(2,1)S(1)}, bf16[176,512]{1,0:T(8,128)(2,1)S(1)}, u32[]{:S(2)}, u32[]{:S(2)}) collective-permute-start(bf16[176,512]{1,0:T(8,128)(2,1)S(1)} %get-tuple-element.87), channel_id=1, source_target_pairs={{0,8},{8,16},{16,24},{24,0},{1,9},{9,17},{17,25},{25,1},{2,10},{10... | collective-permute-start | bytes 540680 | tf_op jit(solution)/shard_map/ppermute | solution.py:239
  130.2 17.2 %collective-permute-start.25 = (bf16[288,512]{1,0:T(8,128)(2,1)S(1)}, bf16[288,512]{1,0:T(8,128)(2,1)S(1)}, u32[]{:S(2)}, u32[]{:S(2)}) collective-permute-start(bf16[288,512]{1,0:T(8,128)(2,1)S(1)} %get-tuple-element.96), channel_id=1, source_target_pairs={{0,0},{1,32},{32,1},{33,33},{2,2},{3,34},{34,3},{35,35},{4,4},{5,3... | collective-permute-start | bytes 884744 | tf_op jit(solution)/shard_map/ppermute | solution.py:254
  135.3 15.3 %collective-permute-start.24 = (bf16[288,512]{1,0:T(8,128)(2,1)S(1)}, bf16[288,512]{1,0:T(8,128)(2,1)S(1)}, u32[]{:S(2)}, u32[]{:S(2)}) collective-permute-start(bf16[288,512]{1,0:T(8,128)(2,1)S(1)} %get-tuple-element.97), channel_id=1, source_target_pairs={{0,0},{1,32},{32,1},{33,33},{2,2},{3,34},{34,3},{35,35},{4,4},{5,3... | collective-permute-start | bytes 884744 | tf_op jit(solution)/shard_map/ppermute | solution.py:254

commit v13 on v8

--- a/solution.py
+++ b/solution.py
@@ -192,7 +192,7 @@
         for m in range(3):
             columns = slice(2 * m * half, 2 * (m + 1) * half)
             total = tn(joined[:, columns], chosen[1 if m == 2 else 0, i])
-            keeps[i][m] = total[0:half, :]
+            keeps[i][m] = total[0:half, :].astype(BF16)
             sends[i][m] = total[half:, :].astype(BF16)
 
 
@@ -315,7 +315,7 @@
         weight_kernel,
         place,
         [shares[4]] + blocks,
-        [((3, half, width), kind) for kind in (F32, BF16) for _ in range(4)],
+        [((3, half, width), BF16)] * 8,
         [pltpu.VMEM((2, 4, slots, width), BF16)],
     )
     keeps, sends = terms[0:4], terms[4:8]
@@ -325,27 +325,25 @@
     arrived = [shift(near, "y", -1), shift(back, "y", 1)]
 
     def both_cores(i):
-        return keeps[i] + moved[i].astype(F32)
+        return keeps[i].astype(F32) + moved[i].astype(F32)
 
     passed = relay(both_cores(2).astype(BF16), "x")
     near, back = halfway(passed, both_cores(1), both_cores(3))
     far_sums = [shift(near, "x", -1), shift(back, "x", 1)]
     totals = call(total_kernel, place, [shares[0]] + arrived, [((unit, width), BF16)] * 4)
     returned = [totals[0]] + [shift(totals[k], "expert", -k) for k in (1, 2, 3)]
+    weight_total = both_cores(0)
+    for block in far_sums:
+        weight_total = weight_total + block.astype(F32)
+    weight_total = weight_total.astype(BF16)
+    weight_total, *returned[1:] = lax.optimization_barrier((weight_total, *returned[1:]))
     layer_output, token_grad, prob_grad = call(
         owner_kernel,
         place,
         [small, placing] + returned,
         [((rows, width), BF16), ((rows, width), BF16), ((8, rows), F32)],
     )
-    weight_total = both_cores(0)
-    for block in far_sums:
-        weight_total = weight_total + block.astype(F32)
-    weight_total = weight_total.astype(BF16).reshape(2, 3 * half // 2, width)
-    parts = [turn(weight_total[n]) for n in range(2)]
-    *parts, layer_output = lax.optimization_barrier((*parts, layer_output))
-    weight_grad = jnp.concatenate([part.astype(F32) for part in parts])
-    weight_grad = weight_grad.reshape(stacked_weights.shape)
+    weight_grad = turn(weight_total).astype(F32)[None]
     return layer_output, token_grad, prob_grad[0:2].T, weight_grad
 
 

time: 150 us -> 157 us (1.047)
  waiting for transfers between devices: 69.9 us -> 75.4 us
  Pallas kernels: 20.8 us -> 19.1 us
    ppermute x14, waiting for transfers between devices: 32.3 us -> 36.9 us  [shift(): return lax.ppermute(value, axis, [(i, (i + step) % 4) for i in range(4)])]
    ppermute x14, starting transfers between devices: 25.1 us -> 27.2 us  [shift(): return lax.ppermute(value, axis, [(i, (i + step) % 4) for i in range(4)])]
    pallas_call x7, Pallas kernels: 20.8 us -> 19.1 us  [call(): pl.pallas_call(kernel, out_shape=[jax.ShapeDtypeStruct(shape, kind) for s...]
    unnamed x25 -> x13, local copies, waits for them, and re-layouts: 2.52 us -> 3.57 us
    ppermute x2 -> x1, waiting for transfers between devices: 4.29 us -> 5.29 us  [turn(): lax.ppermute(value, ('core', 'zl'), [(2 * c + z, 2 * z + c) for c in rang...]
    ppermute x2 -> x1, starting transfers between devices: 8.64 us -> 8.39 us  [turn(): lax.ppermute(value, ('core', 'zl'), [(2 * c + z, 2 * z + c) for c in rang...]
  transfers between devices with their start and end apart: 31 -> 30, of which waited for: 18 -> 19; matrix products, arithmetic and copies ran while one was open for 2% -> 3% of each run, Pallas kernels for 7% -> 6%
where the time goes in v13:
time: 157 us
  waiting for transfers between devices  75.4 us (48%)
  starting transfers between devices  50.7 us (32%)
  Pallas kernels  19.1 us (12%)
  other arithmetic  6.48 us (4%)
  local copies, waits for them, and re-layouts  4.23 us (3%)
    ppermute x14, waiting for transfers between devices, shift(): return lax.ppermute(value, axis, [(i, (i + step) % 4) for i in range(4)])  36.9 us
    ppermute x14, starting transfers between devices, shift(): return lax.ppermute(value, axis, [(i, (i + step) % 4) for i in range(4)])  27.2 us
    pallas_call x7, Pallas kernels, call(): pl.pallas_call(kernel, out_shape=[jax.ShapeDtypeStruct(shape, kind) for s...  19.1 us
    ppermute x10, waiting for transfers between devices, swap(): return lax.ppermute(value, axis, [(0, 1), (1, 0)])  13.1 us
    ppermute x2, waiting for transfers between devices, relay(): lax.ppermute(value, ('core', axis), [(4 * c + i, 4 * c + j) for c, i, j i...  9.07 us
    ppermute x1, starting transfers between devices, turn(): lax.ppermute(value, ('core', 'zl'), [(2 * c + z, 2 * z + c) for c in rang...  8.39 us
    ppermute x1, waiting for transfers between devices, body(): turned = lax.ppermute(own, ('core', 'zl'), [(1, 2), (2, 1)])  6.23 us
    ppermute x1, waiting for transfers between devices, turn(): lax.ppermute(value, ('core', 'zl'), [(2 * c + z, 2 * z + c) for c in rang...  5.29 us
  transfers between devices with their start and end apart: 30, of which 19 were waited for; matrix products, arithmetic and copies ran while one was open for 3% of the time, Pallas kernels for 6%

profile of v13, /device:TPU:1, one launch (start us, length us, event | category | flops | bytes accessed | tf_op | source)
XLA Modules:
  0.0 156.8 jit_solution(8237206555506235801)
XLA Ops:
  0.7 0.7 convert_bitcast_fusion
  2.1 1.0 pad_maximum_fusion.wide
  3.2 1.0 shard_map.84
  4.2 4.9 %collective-permute-start.3 = (bf16[3,192,512]{2,1,0:T(8,128)(2,1)}, bf16[3,192,512]{2,1,0:T(8,128)(2,1)S(1)}, u32[]{:S(2)}, u32[]{:S(2)}) collective-permute-start(bf16[3,192,512]{2,1,0:T(8,128)(2,1)} %bitcast.14), channel_id=1, source_target_pairs={{1,32},{32,1},{3,34},{34,3},{5,36},{36,5},{7,38},{38,7},{9,40},{40... | collective-permute-start | bytes 1769480 | tf_op jit(solution)/shard_map/ppermute | solution.py:270
  9.1 3.1 %collective-permute-start = (bf16[160,512]{1,0:T(8,128)(2,1)S(1)}, bf16[160,512]{1,0:T(8,128)(2,1)}, u32[]{:S(2)}, u32[]{:S(2)}) collective-permute-start(bf16[160,512]{1,0:T(8,128)(2,1)S(1)} %get-tuple-element.53), channel_id=1, source_target_pairs={{0,8},{8,16},{16,24},{24,0},{1,9},{9,17},{17,25},{25,1},{2,10},{10... | collective-permute-start | bytes 491528 | tf_op jit(solution)/shard_map/ppermute | solution.py:230
  12.2 4.2 %collective-permute-start.1 = (bf16[160,512]{1,0:T(8,128)(2,1)S(1)}, bf16[160,512]{1,0:T(8,128)(2,1)}, u32[]{:S(2)}, u32[]{:S(2)}) collective-permute-start(bf16[160,512]{1,0:T(8,128)(2,1)S(1)} %get-tuple-element.54), channel_id=1, source_target_pairs={{0,16},{8,24},{16,0},{24,8},{1,17},{9,25},{17,1},{25,9},{2,18},{10... | collective-permute-start | bytes 491528 | tf_op jit(solution)/shard_map/ppermute | solution.py:230
  16.4 2.4 %collective-permute-start.2 = (bf16[160,512]{1,0:T(8,128)(2,1)S(1)}, bf16[160,512]{1,0:T(8,128)(2,1)S(1)}, u32[]{:S(2)}, u32[]{:S(2)}) collective-permute-start(bf16[160,512]{1,0:T(8,128)(2,1)S(1)} %get-tuple-element.55), channel_id=1, source_target_pairs={{0,24},{8,0},{16,8},{24,16},{1,25},{9,1},{17,9},{25,17},{2,26},{10... | collective-permute-start | bytes 491528 | tf_op jit(solution)/shard_map/ppermute | solution.py:230
  18.8 6.2 %collective-permute-done.3 = bf16[3,192,512]{2,1,0:T(8,128)(2,1)S(1)} collective-permute-done((bf16[3,192,512]{2,1,0:T(8,128)(2,1)}, bf16[3,192,512]{2,1,0:T(8,128)(2,1)S(1)}, u32[]{:S(2)}, u32[]{:S(2)}) %collective-permute-start.3) | collective-permute-done | bytes 589856 | tf_op jit(solution)/shard_map/ppermute | solution.py:270
  25.1 2.6 %collective-permute-start.5 = (bf16[3,192,512]{2,1,0:T(8,128)(2,1)S(1)}, bf16[3,192,512]{2,1,0:T(8,128)(2,1)S(1)}, u32[]{:S(2)}, u32[]{:S(2)}) collective-permute-start(bf16[3,192,512]{2,1,0:T(8,128)(2,1)S(1)} %broadcast_select_fusion.2.refs_4_), channel_id=1, source_target_pairs={{0,192},{64,0},{128,64},{192,128},{1,193},{65,1},{129,65},{193,129... | collective-permute-start | bytes 1769480 | tf_op jit(solution)/shard_map/ppermute | solution.py:230
  27.7 2.9 %collective-permute-done = bf16[160,512]{1,0:T(8,128)(2,1)} collective-permute-done((bf16[160,512]{1,0:T(8,128)(2,1)S(1)}, bf16[160,512]{1,0:T(8,128)(2,1)}, u32[]{:S(2)}, u32[]{:S(2)}) %collective-permute-start) | collective-permute-done | bytes 163872 | tf_op jit(solution)/shard_map/ppermute | solution.py:230
  30.6 0.9 constant_dynamic-update-slice_fusion.2
  31.5 4.9 %collective-permute-done.1 = bf16[160,512]{1,0:T(8,128)(2,1)} collective-permute-done((bf16[160,512]{1,0:T(8,128)(2,1)S(1)}, bf16[160,512]{1,0:T(8,128)(2,1)}, u32[]{:S(2)}, u32[]{:S(2)}) %collective-permute-start.1) | collective-permute-done | bytes 163872 | tf_op jit(solution)/shard_map/ppermute | solution.py:230
  36.4 0.9 constant_dynamic-update-slice_fusion.1
  37.4 2.8 %collective-permute-start.7 = (bf16[640,512]{1,0:T(8,128)(2,1)S(1)}, bf16[640,512]{1,0:T(8,128)(2,1)}, u32[]{:S(2)}, u32[]{:S(2)}) collective-permute-start(bf16[640,512]{1,0:T(8,128)(2,1)S(1)} %constant_dynamic-update-slice_fusion.refs_0_), channel_id=1, source_target_pairs={{0,6},{2,0},{4,2},{6,4},{1,7},{3,1},{5,3},{7,5},{8,14},{10,8},{12,... | collective-permute-start | bytes 1966088 | tf_op jit(solution)/shard_map/ppermute | solution.py:230
  40.3 2.6 %collective-permute-start.9 = (bf16[3,192,512]{2,1,0:T(8,128)(2,1)S(1)}, bf16[3,192,512]{2,1,0:T(8,128)(2,1)S(1)}, u32[]{:S(2)}, u32[]{:S(2)}) collective-permute-start(bf16[3,192,512]{2,1,0:T(8,128)(2,1)S(1)} %broadcast_select_fusion.1), channel_id=1, source_target_pairs={{0,64},{64,128},{128,192},{192,0},{32,224},{96,32},{160,96},{224,1... | collective-permute-start | bytes 1769480 | tf_op jit(solution)/shard_map/ppermute | solution.py:236
  42.8 4.9 %collective-permute-done.7.refs_3_ = bf16[640,512]{1,0:T(8,128)(2,1)} collective-permute-done((bf16[640,512]{1,0:T(8,128)(2,1)S(1)}, bf16[640,512]{1,0:T(8,128)(2,1)}, u32[]{:S(2)}, u32[]{:S(2)}) %collective-permute-start.7) | collective-permute-done | bytes 655392 | tf_op jit(solution)/shard_map/ppermute | solution.py:230
  47.7 5.6 %collective-permute-done.6.refs_1_ = bf16[640,512]{1,0:T(8,128)(2,1)S(1)} collective-permute-done((bf16[640,512]{1,0:T(8,128)(2,1)S(1)}, bf16[640,512]{1,0:T(8,128)(2,1)S(1)}, u32[]{:S(2)}, u32[]{:S(2)}) %collective-permute-start.6) | collective-permute-done | bytes 655392 | tf_op jit(solution)/shard_map/ppermute | solution.py:230
  53.3 1.4 broadcast_select_fusion
  55.9 1.0 collective-permute-done.10.refs_8_
  56.9 0.8 collective-permute-done.11.refs_9_
  57.8 0.8 collective-permute-done.13.refs_11_
  58.6 5.6 %collective-permute-done.8.refs_2_ = bf16[640,512]{1,0:T(8,128)(2,1)S(1)} collective-permute-done((bf16[640,512]{1,0:T(8,128)(2,1)S(1)}, bf16[640,512]{1,0:T(8,128)(2,1)S(1)}, u32[]{:S(2)}, u32[]{:S(2)}) %collective-permute-start.8) | collective-permute-done | bytes 655392 | tf_op jit(solution)/shard_map/ppermute | solution.py:237
  64.3 0.8 copy-done.3
  65.1 3.8 %shard_map.85 = (bf16[320,768]{1,0:T(8,128)(2,1)S(1)}, bf16[768,2048]{1,0:T(8,128)(2,1)}) custom-call(s32[5]{0:T(128)S(1)} %stack.23.place, bf16[640,512]{1,0:T(8,128)(2,1)S(1)} %constant_dynamic-update-slice_fusion.refs_0_, bf16[640,512]{1,0:T(8,128)(2,1)} %copy-done, bf16[640,512]{1,0:T(8,128)(2,1)} %copy-done.3, ...), custom_call_target="tpu_custom_call" | custom-call | tf_op jit(solution)/shard_map/pallas_call | solution.py:33
  69.2 3.1 %shard_map.86 = (bf16[320,384]{1,0:T(8,128)(2,1)S(1)}, bf16[384,2048]{1,0:T(8,128)(2,1)}) custom-call(s32[5]{0:T(128)S(1)} %stack.23.place, bf16[640,512]{1,0:T(8,128)(2,1)S(1)} %constant_dynamic-update-slice_fusion.refs_0_, bf16[640,512]{1,0:T(8,128)(2,1)} %copy-done, bf16[640,512]{1,0:T(8,128)(2,1)} %copy-done.3, ...), custom_call_target="tpu_custom_call" | custom-call | tf_op jit(solution)/shard_map/pallas_call | solution.py:33
  72.2 1.5 collective-permute-start.15
  73.8 10.4 %collective-permute-done.15.down_far = bf16[320,384]{1,0:T(8,128)(2,1)S(1)} collective-permute-done((bf16[320,384]{1,0:T(8,128)(2,1)S(1)}, bf16[320,384]{1,0:T(8,128)(2,1)S(1)}, u32[]{:S(2)}, u32[]{:S(2)}) %collective-permute-start.15) | collective-permute-done | bytes 245792 | tf_op jit(solution)/shard_map/ppermute | solution.py:241
  84.2 4.5 %shard_map.87 = (f32[656,512]{1,0:T(8,128)S(1)}, bf16[656,512]{1,0:T(8,128)(2,1)S(1)}, bf16[656,512]{1,0:T(8,128)(2,1)S(1)}, bf16[656,512]{1,0:T(8,128)(2,1)S(1)}, bf16[320,1152]{1,0:T(8,128)(2,1)S(1)}) custom-call(s32[5]{0:T(128)S(1)} %stack.23.place, bf16[320,768]{1,0:T(8,128)(2,1)S(1)} %get-tuple-element.62.pair, ...), custom_call_target="tpu_custom_call" | custom-call | tf_op jit(solution)/shard_map/pallas_call | solution.py:33
  88.7 0.9 copy-done.2
  89.5 1.1 collective-permute-start.16
  90.6 4.3 %shard_map.88 = (bf16[3,192,512]{2,1,0:T(8,128)(2,1)S(1)}, bf16[3,192,512]{2,1,0:T(8,128)(2,1)S(1)}, bf16[3,192,512]{2,1,0:T(8,128)(2,1)S(1)}, bf16[3,192,512]{2...) custom-call(s32[5]{0:T(128)S(1)} %stack.23.place, ...), custom_call_target="tpu_custom_call" | custom-call | tf_op jit(solution)/shard_map/pallas_call | solution.py:33
  96.0 3.4 %collective-permute-done.16 = bf16[656,512]{1,0:T(8,128)(2,1)S(1)} collective-permute-done((bf16[656,512]{1,0:T(8,128)(2,1)S(1)}, bf16[656,512]{1,0:T(8,128)(2,1)S(1)}, u32[]{:S(2)}, u32[]{:S(2)}) %collective-permute-start.16) | collective-permute-done | bytes 671776 | tf_op jit(solution)/shard_map/ppermute | solution.py:237
  100.0 2.6 %collective-permute-start.23 = (bf16[3,192,512]{2,1,0:T(8,128)(2,1)S(1)}, bf16[3,192,512]{2,1,0:T(8,128)(2,1)S(1)}, u32[]{:S(2)}, u32[]{:S(2)}) collective-permute-start(bf16[3,192,512]{2,1,0:T(8,128)(2,1)S(1)} %add_convert_fusion.1), channel_id=1, source_target_pairs={{0,64},{64,128},{128,192},{192,0},{32,224},{96,32},{160,96},{224,1... | collective-permute-start | bytes 1769480 | tf_op jit(solution)/shard_map/ppermute | solution.py:236
  102.6 2.0 %collective-permute-start.21 = (bf16[656,512]{1,0:T(8,128)(2,1)S(1)}, bf16[656,512]{1,0:T(8,128)(2,1)S(1)}, u32[]{:S(2)}, u32[]{:S(2)}) collective-permute-start(bf16[656,512]{1,0:T(8,128)(2,1)S(1)} %get-tuple-element.75), channel_id=1, source_target_pairs={{0,6},{2,0},{4,2},{6,4},{1,7},{3,1},{5,3},{7,5},{8,14},{10,8},{12,... | collective-permute-start | bytes 2015240 | tf_op jit(solution)/shard_map/ppermute | solution.py:230
  104.6 4.8 %collective-permute-done.23 = bf16[3,192,512]{2,1,0:T(8,128)(2,1)S(1)} collective-permute-done((bf16[3,192,512]{2,1,0:T(8,128)(2,1)S(1)}, bf16[3,192,512]{2,1,0:T(8,128)(2,1)S(1)}, u32[]{:S(2)}, u32[]{:S(2)}) %collective-permute-start.23) | collective-permute-done | bytes 589856 | tf_op jit(solution)/shard_map/ppermute | solution.py:236
  109.9 3.7 %collective-permute-start.24 = (bf16[3,192,512]{2,1,0:T(8,128)(2,1)S(1)}, bf16[3,192,512]{2,1,0:T(8,128)(2,1)S(1)}, u32[]{:S(2)}, u32[]{:S(2)}) collective-permute-start(bf16[3,192,512]{2,1,0:T(8,128)(2,1)S(1)} %get-tuple-element.98), channel_id=1, source_target_pairs={{0,192},{64,0},{128,64},{192,128},{1,193},{65,1},{129,65},{193,129... | collective-permute-start | bytes 1769480 | tf_op jit(solution)/shard_map/ppermute | solution.py:230
  113.7 5.8 %collective-permute-done.21.one = bf16[656,512]{1,0:T(8,128)(2,1)S(1)} collective-permute-done((bf16[656,512]{1,0:T(8,128)(2,1)S(1)}, bf16[656,512]{1,0:T(8,128)(2,1)S(1)}, u32[]{:S(2)}, u32[]{:S(2)}) %collective-permute-start.21) | collective-permute-done | bytes 671776 | tf_op jit(solution)/shard_map/ppermute | solution.py:230
  119.5 2.0 %collective-permute-done.22.three = bf16[656,512]{1,0:T(8,128)(2,1)S(1)} collective-permute-done((bf16[656,512]{1,0:T(8,128)(2,1)S(1)}, bf16[656,512]{1,0:T(8,128)(2,1)S(1)}, u32[]{:S(2)}, u32[]{:S(2)}) %collective-permute-start.22) | collective-permute-done | bytes 671776 | tf_op jit(solution)/shard_map/ppermute | solution.py:230
  121.5 0.8 shard_map.89
  122.3 3.4 %collective-permute-start.26 = (bf16[176,512]{1,0:T(8,128)(2,1)S(1)}, bf16[176,512]{1,0:T(8,128)(2,1)S(1)}, u32[]{:S(2)}, u32[]{:S(2)}) collective-permute-start(bf16[176,512]{1,0:T(8,128)(2,1)S(1)} %get-tuple-element.86), channel_id=1, source_target_pairs={{0,24},{8,0},{16,8},{24,16},{1,25},{9,1},{17,9},{25,17},{2,26},{10... | collective-permute-start | bytes 540680 | tf_op jit(solution)/shard_map/ppermute | solution.py:230
  125.7 1.8 %collective-permute-start.27 = (bf16[176,512]{1,0:T(8,128)(2,1)S(1)}, bf16[176,512]{1,0:T(8,128)(2,1)S(1)}, u32[]{:S(2)}, u32[]{:S(2)}) collective-permute-start(bf16[176,512]{1,0:T(8,128)(2,1)S(1)} %get-tuple-element.87), channel_id=1, source_target_pairs={{0,16},{8,24},{16,0},{24,8},{1,17},{9,25},{17,1},{25,9},{2,18},{10... | collective-permute-start | bytes 540680 | tf_op jit(solution)/shard_map/ppermute | solution.py:230
  127.5 1.2 collective-permute-start.28
  129.4 8.2 %collective-permute-done.26.refs_1_ = bf16[176,512]{1,0:T(8,128)(2,1)S(1)} collective-permute-done((bf16[176,512]{1,0:T(8,128)(2,1)S(1)}, bf16[176,512]{1,0:T(8,128)(2,1)S(1)}, u32[]{:S(2)}, u32[]{:S(2)}) %collective-permute-start.26) | collective-permute-done | bytes 180256 | tf_op jit(solution)/shard_map/ppermute | solution.py:230
  137.6 1.5 collective-permute-done.27.refs_2_
  139.7 8.4 %collective-permute-start.29 = (bf16[3,192,512]{2,1,0:T(8,128)(2,1)S(1)}, bf16[3,192,512]{2,1,0:T(8,128)(2,1)S(1)}, u32[]{:S(2)}, u32[]{:S(2)}) collective-permute-start(bf16[3,192,512]{2,1,0:T(8,128)(2,1)S(1)} %add_convert_fusion), channel_id=1, source_target_pairs={{0,0},{1,32},{32,1},{33,33},{2,2},{3,34},{34,3},{35,35},{4,4},{5,3... | collective-permute-start | bytes 1769480 | tf_op jit(solution)/shard_map/ppermute | solution.py:245
  148.1 1.7 %shard_map.90 = (bf16[128,512]{1,0:T(8,128)(2,1)}, bf16[128,512]{1,0:T(8,128)(2,1)}, f32[8,128]{1,0:T(8,128)S(1)}) custom-call(s32[5]{0:T(128)S(1)} %stack.23.place, f32[4,128]{1,0:T(4,128)S(1)} %pad_maximum_fusion.1.small, bf16[320,128]{1,0:T(8,128)(2,1)S(1)} %get-tuple-element.50.placing, bf16[176,512]{1,0:T(8,128)(2,1)S(1)} %get-tuple-element.77.refs_0_, ...), custom_call_target="tpu_custom_call" | custom-call | tf_op jit(solution)/shard_map/pallas_call | solution.py:33
  150.4 5.3 %collective-permute-done.29 = bf16[3,192,512]{2,1,0:T(8,128)(2,1)S(1)} collective-permute-done((bf16[3,192,512]{2,1,0:T(8,128)(2,1)S(1)}, bf16[3,192,512]{2,1,0:T(8,128)(2,1)S(1)}, u32[]{:S(2)}, u32[]{:S(2)}) %collective-permute-start.29) | collective-permute-done | bytes 589856 | tf_op jit(solution)/shard_map/ppermute | solution.py:245
  155.7 1.2 bitcast_convert_fusion
  (46 shorter events, 6.5 us)
Async XLA Ops:
  0.6 24.4 %copy-start.4 = (bf16[1,3,192,512]{3,2,1,0:T(8,128)(2,1)S(1)}, bf16[1,3,192,512]{3,2,1,0:T(8,128)(2,1)}, u32[]{:S(2)}) copy-start(bf16[1,3,192,512]{3,2,1,0:T(8,128)(2,1)} %param.8) | copy-start | bytes 1769476
  4.2 20.8 %collective-permute-start.3 = (bf16[3,192,512]{2,1,0:T(8,128)(2,1)}, bf16[3,192,512]{2,1,0:T(8,128)(2,1)S(1)}, u32[]{:S(2)}, u32[]{:S(2)}) collective-permute-start(bf16[3,192,512]{2,1,0:T(8,128)(2,1)} %bitcast.14), channel_id=1, source_target_pairs={{1,32},{32,1},{3,34},{34,3},{5,36},{36,5},{7,38},{38,7},{9,40},{40... | collective-permute-start | bytes 1769480 | tf_op jit(solution)/shard_map/ppermute | solution.py:270
  9.1 21.5 %collective-permute-start = (bf16[160,512]{1,0:T(8,128)(2,1)S(1)}, bf16[160,512]{1,0:T(8,128)(2,1)}, u32[]{:S(2)}, u32[]{:S(2)}) collective-permute-start(bf16[160,512]{1,0:T(8,128)(2,1)S(1)} %get-tuple-element.53), channel_id=1, source_target_pairs={{0,8},{8,16},{16,24},{24,0},{1,9},{9,17},{17,25},{25,1},{2,10},{10... | collective-permute-start | bytes 491528 | tf_op jit(solution)/shard_map/ppermute | solution.py:230
  12.2 24.3 %collective-permute-start.1 = (bf16[160,512]{1,0:T(8,128)(2,1)S(1)}, bf16[160,512]{1,0:T(8,128)(2,1)}, u32[]{:S(2)}, u32[]{:S(2)}) collective-permute-start(bf16[160,512]{1,0:T(8,128)(2,1)S(1)} %get-tuple-element.54), channel_id=1, source_target_pairs={{0,16},{8,24},{16,0},{24,8},{1,17},{9,25},{17,1},{25,9},{2,18},{10... | collective-permute-start | bytes 491528 | tf_op jit(solution)/shard_map/ppermute | solution.py:230
  16.4 21.0 %collective-permute-start.2 = (bf16[160,512]{1,0:T(8,128)(2,1)S(1)}, bf16[160,512]{1,0:T(8,128)(2,1)S(1)}, u32[]{:S(2)}, u32[]{:S(2)}) collective-permute-start(bf16[160,512]{1,0:T(8,128)(2,1)S(1)} %get-tuple-element.55), channel_id=1, source_target_pairs={{0,24},{8,0},{16,8},{24,16},{1,25},{9,1},{17,9},{25,17},{2,26},{10... | collective-permute-start | bytes 491528 | tf_op jit(solution)/shard_map/ppermute | solution.py:230
  25.1 15.1 %collective-permute-start.5 = (bf16[3,192,512]{2,1,0:T(8,128)(2,1)S(1)}, bf16[3,192,512]{2,1,0:T(8,128)(2,1)S(1)}, u32[]{:S(2)}, u32[]{:S(2)}) collective-permute-start(bf16[3,192,512]{2,1,0:T(8,128)(2,1)S(1)} %broadcast_select_fusion.2.refs_4_), channel_id=1, source_target_pairs={{0,192},{64,0},{128,64},{192,128},{1,193},{65,1},{129,65},{193,129... | collective-permute-start | bytes 1769480 | tf_op jit(solution)/shard_map/ppermute | solution.py:230
  27.6 12.6 %collective-permute-start.4 = (bf16[3,192,512]{2,1,0:T(8,128)(2,1)S(1)}, bf16[3,192,512]{2,1,0:T(8,128)(2,1)S(1)}, u32[]{:S(2)}, u32[]{:S(2)}) collective-permute-start(bf16[3,192,512]{2,1,0:T(8,128)(2,1)S(1)} %broadcast_select_fusion.2.refs_4_), channel_id=1, source_target_pairs={{0,64},{64,128},{128,192},{192,0},{1,65},{65,129},{129,193},{193,1... | collective-permute-start | bytes 1769480 | tf_op jit(solution)/shard_map/ppermute | solution.py:230
  37.4 10.3 %collective-permute-start.7 = (bf16[640,512]{1,0:T(8,128)(2,1)S(1)}, bf16[640,512]{1,0:T(8,128)(2,1)}, u32[]{:S(2)}, u32[]{:S(2)}) collective-permute-start(bf16[640,512]{1,0:T(8,128)(2,1)S(1)} %constant_dynamic-update-slice_fusion.refs_0_), channel_id=1, source_target_pairs={{0,6},{2,0},{4,2},{6,4},{1,7},{3,1},{5,3},{7,5},{8,14},{10,8},{12,... | collective-permute-start | bytes 1966088 | tf_op jit(solution)/shard_map/ppermute | solution.py:230
  40.2 13.1 %collective-permute-start.6 = (bf16[640,512]{1,0:T(8,128)(2,1)S(1)}, bf16[640,512]{1,0:T(8,128)(2,1)S(1)}, u32[]{:S(2)}, u32[]{:S(2)}) collective-permute-start(bf16[640,512]{1,0:T(8,128)(2,1)S(1)} %constant_dynamic-update-slice_fusion.refs_0_), channel_id=1, source_target_pairs={{0,2},{2,4},{4,6},{6,0},{1,3},{3,5},{5,7},{7,1},{8,10},{10,12},{12... | collective-permute-start | bytes 1966088 | tf_op jit(solution)/shard_map/ppermute | solution.py:230
  40.3 15.2 %collective-permute-start.9 = (bf16[3,192,512]{2,1,0:T(8,128)(2,1)S(1)}, bf16[3,192,512]{2,1,0:T(8,128)(2,1)S(1)}, u32[]{:S(2)}, u32[]{:S(2)}) collective-permute-start(bf16[3,192,512]{2,1,0:T(8,128)(2,1)S(1)} %broadcast_select_fusion.1), channel_id=1, source_target_pairs={{0,64},{64,128},{128,192},{192,0},{32,224},{96,32},{160,96},{224,1... | collective-permute-start | bytes 1769480 | tf_op jit(solution)/shard_map/ppermute | solution.py:236
  53.3 10.9 %copy-start = (bf16[640,512]{1,0:T(8,128)(2,1)}, bf16[640,512]{1,0:T(8,128)(2,1)S(1)}, u32[]{:S(2)}) copy-start(bf16[640,512]{1,0:T(8,128)(2,1)S(1)} %collective-permute-done.6.refs_1_) | copy-start | bytes 1966084
  54.7 9.5 %collective-permute-start.8 = (bf16[640,512]{1,0:T(8,128)(2,1)S(1)}, bf16[640,512]{1,0:T(8,128)(2,1)S(1)}, u32[]{:S(2)}, u32[]{:S(2)}) collective-permute-start(bf16[640,512]{1,0:T(8,128)(2,1)S(1)} %broadcast_select_fusion), channel_id=1, source_target_pairs={{0,2},{2,4},{4,6},{6,0},{32,38},{34,32},{36,34},{38,36},{1,3},{3,5... | collective-permute-start | bytes 1966088 | tf_op jit(solution)/shard_map/ppermute | solution.py:237
  54.8 2.1 %collective-permute-start.10 = (bf16[3,192,512]{2,1,0:T(8,128)(2,1)S(1)}, bf16[3,192,512]{2,1,0:T(8,128)(2,1)S(1)}, u32[]{:S(2)}, u32[]{:S(2)}) collective-permute-start(bf16[3,192,512]{2,1,0:T(8,128)(2,1)S(1)} %broadcast_select_fusion.2.refs_4_), channel_id=1, source_target_pairs={{0,32},{32,0},{1,33},{33,1},{2,34},{34,2},{3,35},{35,3},{4,36},{36... | collective-permute-start | bytes 1769480 | tf_op jit(solution)/shard_map/ppermute | solution.py:241
  54.9 2.8 %collective-permute-start.11 = (bf16[3,192,512]{2,1,0:T(8,128)(2,1)S(1)}, bf16[3,192,512]{2,1,0:T(8,128)(2,1)S(1)}, u32[]{:S(2)}, u32[]{:S(2)}) collective-permute-start(bf16[3,192,512]{2,1,0:T(8,128)(2,1)S(1)} %collective-permute-done.4.refs_5_), channel_id=1, source_target_pairs={{0,32},{32,0},{1,33},{33,1},{2,34},{34,2},{3,35},{35,3},{4,36},{36... | collective-permute-start | bytes 1769480 | tf_op jit(solution)/shard_map/ppermute | solution.py:241
  55.4 3.2 %collective-permute-start.13 = (bf16[3,192,512]{2,1,0:T(8,128)(2,1)S(1)}, bf16[3,192,512]{2,1,0:T(8,128)(2,1)S(1)}, u32[]{:S(2)}, u32[]{:S(2)}) collective-permute-start(bf16[3,192,512]{2,1,0:T(8,128)(2,1)S(1)} %collective-permute-done.5.refs_7_), channel_id=1, source_target_pairs={{0,32},{32,0},{1,33},{33,1},{2,34},{34,2},{3,35},{35,3},{4,36},{36... | collective-permute-start | bytes 1769480 | tf_op jit(solution)/shard_map/ppermute | solution.py:241
  55.5 8.7 %collective-permute-start.12 = (bf16[3,192,512]{2,1,0:T(8,128)(2,1)S(1)}, bf16[3,192,512]{2,1,0:T(8,128)(2,1)S(1)}, u32[]{:S(2)}, u32[]{:S(2)}) collective-permute-start(bf16[3,192,512]{2,1,0:T(8,128)(2,1)S(1)} %collective-permute-done.9.refs_6_), channel_id=1, source_target_pairs={{0,32},{32,0},{1,33},{33,1},{2,34},{34,2},{3,35},{35,3},{4,36},{36... | collective-permute-start | bytes 1769480 | tf_op jit(solution)/shard_map/ppermute | solution.py:241
  64.2 0.8 copy-start.3
  68.9 15.3 %collective-permute-start.14 = (bf16[320,768]{1,0:T(8,128)(2,1)S(1)}, bf16[320,768]{1,0:T(8,128)(2,1)S(1)}, u32[]{:S(2)}, u32[]{:S(2)}) collective-permute-start(bf16[320,768]{1,0:T(8,128)(2,1)S(1)} %get-tuple-element.62.pair), channel_id=1, source_target_pairs={{0,1},{1,0},{2,3},{3,2},{4,5},{5,4},{6,7},{7,6},{8,9},{9,8},{10,11... | collective-permute-start | bytes 1474568 | tf_op jit(solution)/shard_map/ppermute | solution.py:241
  72.2 11.9 %collective-permute-start.15 = (bf16[320,384]{1,0:T(8,128)(2,1)S(1)}, bf16[320,384]{1,0:T(8,128)(2,1)S(1)}, u32[]{:S(2)}, u32[]{:S(2)}) collective-permute-start(bf16[320,384]{1,0:T(8,128)(2,1)S(1)} %get-tuple-element.63.down), channel_id=1, source_target_pairs={{0,1},{1,0},{2,3},{3,2},{4,5},{5,4},{6,7},{7,6},{8,9},{9,8},{10,11... | collective-permute-start | bytes 737288 | tf_op jit(solution)/shard_map/ppermute | solution.py:241
  84.2 6.4 %copy-start.1 = (bf16[640,512]{1,0:T(8,128)(2,1)S(1)}, bf16[640,512]{1,0:T(8,128)(2,1)}, u32[]{:S(2)}) copy-start(bf16[640,512]{1,0:T(8,128)(2,1)} %copy-done) | copy-start | bytes 1966084
  88.7 0.9 copy-start.2
  89.5 9.9 %collective-permute-start.16 = (bf16[656,512]{1,0:T(8,128)(2,1)S(1)}, bf16[656,512]{1,0:T(8,128)(2,1)S(1)}, u32[]{:S(2)}, u32[]{:S(2)}) collective-permute-start(bf16[656,512]{1,0:T(8,128)(2,1)S(1)} %get-tuple-element.68), channel_id=1, source_target_pairs={{0,2},{2,4},{4,6},{6,0},{32,38},{34,32},{36,34},{38,36},{1,3},{3,5... | collective-permute-start | bytes 2015240 | tf_op jit(solution)/shard_map/ppermute | solution.py:237
  94.9 4.9 %collective-permute-start.17 = (bf16[3,192,512]{2,1,0:T(8,128)(2,1)S(1)}, bf16[3,192,512]{2,1,0:T(8,128)(2,1)S(1)}, u32[]{:S(2)}, u32[]{:S(2)}) collective-permute-start(bf16[3,192,512]{2,1,0:T(8,128)(2,1)S(1)} %get-tuple-element.71), channel_id=1, source_target_pairs={{0,32},{32,0},{1,33},{33,1},{2,34},{34,2},{3,35},{35,3},{4,36},{36... | collective-permute-start | bytes 1769480 | tf_op jit(solution)/shard_map/ppermute | solution.py:241
  95.0 4.8 %collective-permute-start.18 = (bf16[3,192,512]{2,1,0:T(8,128)(2,1)S(1)}, bf16[3,192,512]{2,1,0:T(8,128)(2,1)S(1)}, u32[]{:S(2)}, u32[]{:S(2)}) collective-permute-start(bf16[3,192,512]{2,1,0:T(8,128)(2,1)S(1)} %get-tuple-element.72), channel_id=1, source_target_pairs={{0,32},{32,0},{1,33},{33,1},{2,34},{34,2},{3,35},{35,3},{4,36},{36... | collective-permute-start | bytes 1769480 | tf_op jit(solution)/shard_map/ppermute | solution.py:241
  95.5 4.3 %collective-permute-start.19 = (bf16[3,192,512]{2,1,0:T(8,128)(2,1)S(1)}, bf16[3,192,512]{2,1,0:T(8,128)(2,1)S(1)}, u32[]{:S(2)}, u32[]{:S(2)}) collective-permute-start(bf16[3,192,512]{2,1,0:T(8,128)(2,1)S(1)} %get-tuple-element.73), channel_id=1, source_target_pairs={{0,32},{32,0},{1,33},{33,1},{2,34},{34,2},{3,35},{35,3},{4,36},{36... | collective-permute-start | bytes 1769480 | tf_op jit(solution)/shard_map/ppermute | solution.py:241
  95.6 4.3 %collective-permute-start.20 = (bf16[3,192,512]{2,1,0:T(8,128)(2,1)S(1)}, bf16[3,192,512]{2,1,0:T(8,128)(2,1)S(1)}, u32[]{:S(2)}, u32[]{:S(2)}) collective-permute-start(bf16[3,192,512]{2,1,0:T(8,128)(2,1)S(1)} %get-tuple-element.74), channel_id=1, source_target_pairs={{0,32},{32,0},{1,33},{33,1},{2,34},{34,2},{3,35},{35,3},{4,36},{36... | collective-permute-start | bytes 1769480 | tf_op jit(solution)/shard_map/ppermute | solution.py:241
  100.0 9.4 %collective-permute-start.23 = (bf16[3,192,512]{2,1,0:T(8,128)(2,1)S(1)}, bf16[3,192,512]{2,1,0:T(8,128)(2,1)S(1)}, u32[]{:S(2)}, u32[]{:S(2)}) collective-permute-start(bf16[3,192,512]{2,1,0:T(8,128)(2,1)S(1)} %add_convert_fusion.1), channel_id=1, source_target_pairs={{0,64},{64,128},{128,192},{192,0},{32,224},{96,32},{160,96},{224,1... | collective-permute-start | bytes 1769480 | tf_op jit(solution)/shard_map/ppermute | solution.py:236
  102.6 16.9 %collective-permute-start.21 = (bf16[656,512]{1,0:T(8,128)(2,1)S(1)}, bf16[656,512]{1,0:T(8,128)(2,1)S(1)}, u32[]{:S(2)}, u32[]{:S(2)}) collective-permute-start(bf16[656,512]{1,0:T(8,128)(2,1)S(1)} %get-tuple-element.75), channel_id=1, source_target_pairs={{0,6},{2,0},{4,2},{6,4},{1,7},{3,1},{5,3},{7,5},{8,14},{10,8},{12,... | collective-permute-start | bytes 2015240 | tf_op jit(solution)/shard_map/ppermute | solution.py:230
  104.6 16.9 %collective-permute-start.22 = (bf16[656,512]{1,0:T(8,128)(2,1)S(1)}, bf16[656,512]{1,0:T(8,128)(2,1)S(1)}, u32[]{:S(2)}, u32[]{:S(2)}) collective-permute-start(bf16[656,512]{1,0:T(8,128)(2,1)S(1)} %get-tuple-element.76), channel_id=1, source_target_pairs={{0,2},{2,4},{4,6},{6,0},{1,3},{3,5},{5,7},{7,1},{8,10},{10,12},{12... | collective-permute-start | bytes 2015240 | tf_op jit(solution)/shard_map/ppermute | solution.py:230
  109.9 18.8 %collective-permute-start.24 = (bf16[3,192,512]{2,1,0:T(8,128)(2,1)S(1)}, bf16[3,192,512]{2,1,0:T(8,128)(2,1)S(1)}, u32[]{:S(2)}, u32[]{:S(2)}) collective-permute-start(bf16[3,192,512]{2,1,0:T(8,128)(2,1)S(1)} %get-tuple-element.98), channel_id=1, source_target_pairs={{0,192},{64,0},{128,64},{192,128},{1,193},{65,1},{129,65},{193,129... | collective-permute-start | bytes 1769480 | tf_op jit(solution)/shard_map/ppermute | solution.py:230
  113.6 15.4 %collective-permute-start.25 = (bf16[3,192,512]{2,1,0:T(8,128)(2,1)S(1)}, bf16[3,192,512]{2,1,0:T(8,128)(2,1)S(1)}, u32[]{:S(2)}, u32[]{:S(2)}) collective-permute-start(bf16[3,192,512]{2,1,0:T(8,128)(2,1)S(1)} %get-tuple-element.99), channel_id=1, source_target_pairs={{0,64},{64,128},{128,192},{192,0},{1,65},{65,129},{129,193},{193,1... | collective-permute-start | bytes 1769480 | tf_op jit(solution)/shard_map/ppermute | solution.py:230
  122.3 15.3 %collective-permute-start.26 = (bf16[176,512]{1,0:T(8,128)(2,1)S(1)}, bf16[176,512]{1,0:T(8,128)(2,1)S(1)}, u32[]{:S(2)}, u32[]{:S(2)}) collective-permute-start(bf16[176,512]{1,0:T(8,128)(2,1)S(1)} %get-tuple-element.86), channel_id=1, source_target_pairs={{0,24},{8,0},{16,8},{24,16},{1,25},{9,1},{17,9},{25,17},{2,26},{10... | collective-permute-start | bytes 540680 | tf_op jit(solution)/shard_map/ppermute | solution.py:230
  125.7 13.4 %collective-permute-start.27 = (bf16[176,512]{1,0:T(8,128)(2,1)S(1)}, bf16[176,512]{1,0:T(8,128)(2,1)S(1)}, u32[]{:S(2)}, u32[]{:S(2)}) collective-permute-start(bf16[176,512]{1,0:T(8,128)(2,1)S(1)} %get-tuple-element.87), channel_id=1, source_target_pairs={{0,16},{8,24},{16,0},{24,8},{1,17},{9,25},{17,1},{25,9},{2,18},{10... | collective-permute-start | bytes 540680 | tf_op jit(solution)/shard_map/ppermute | solution.py:230
  127.5 12.2 %collective-permute-start.28 = (bf16[176,512]{1,0:T(8,128)(2,1)S(1)}, bf16[176,512]{1,0:T(8,128)(2,1)S(1)}, u32[]{:S(2)}, u32[]{:S(2)}) collective-permute-start(bf16[176,512]{1,0:T(8,128)(2,1)S(1)} %get-tuple-element.88), channel_id=1, source_target_pairs={{0,8},{8,16},{16,24},{24,0},{1,9},{9,17},{17,25},{25,1},{2,10},{10... | collective-permute-start | bytes 540680 | tf_op jit(solution)/shard_map/ppermute | solution.py:230
  139.7 15.9 %collective-permute-start.29 = (bf16[3,192,512]{2,1,0:T(8,128)(2,1)S(1)}, bf16[3,192,512]{2,1,0:T(8,128)(2,1)S(1)}, u32[]{:S(2)}, u32[]{:S(2)}) collective-permute-start(bf16[3,192,512]{2,1,0:T(8,128)(2,1)S(1)} %add_convert_fusion), channel_id=1, source_target_pairs={{0,0},{1,32},{32,1},{33,33},{2,2},{3,34},{34,3},{35,35},{4,4},{5,3... | collective-permute-start | bytes 1769480 | tf_op jit(solution)/shard_map/ppermute | solution.py:245

commit v14 on v8

--- a/solution.py
+++ b/solution.py
@@ -77,7 +77,7 @@
     half, width = own[0].shape[1:]
     copies = []
     for block in range(4):
-        spot = lax.rem(place[2] - place[1] + block + 4, 4)
+        spot = lax.rem(block + (1 - 2 * place[4]) * (place[2] - place[1]) + 8, 4)
         columns = pl.ds(pl.multiple_of(spot * width, width), width)
         for n, m in enumerate(names):
             for h, source in enumerate((own[block], other[block])):
@@ -185,14 +185,14 @@
     rows, keeps, sends, chosen = refs[0:4], refs[4:8], refs[8:12], refs[12]
     half = keeps[0].shape[1]
     for j in range(4):
-        spot = lax.rem(place[1] - place[2] + j + 4, 4)
+        spot = lax.rem(j + (1 - 2 * place[4]) * (place[1] - place[2]) + 8, 4)
         for second in range(2):
             take_rows(chosen.at[second, spot], rows[j], second)
     for i in (2, 1, 3, 0):
         for m in range(3):
             columns = slice(2 * m * half, 2 * (m + 1) * half)
             total = tn(joined[:, columns], chosen[1 if m == 2 else 0, i])
-            keeps[i][m] = total[0:half, :]
+            keeps[i][m] = total[0:half, :].astype(BF16)
             sends[i][m] = total[half:, :].astype(BF16)
 
 
@@ -230,8 +230,8 @@
     return lax.ppermute(value, axis, [(i, (i + step) % 4) for i in range(4)])
 
 
-def relay(value, axis):
-    steps = [(c, i, (i + (3 if c else 1)) % 4) for c in range(2) for i in range(4)]
+def relay(value, axis, sign=1):
+    steps = [(c, i, (i + (-sign if c else sign)) % 4) for c in range(2) for i in range(4)]
     if axis == "x":
         return lax.ppermute(value, ("x", "core"), [(2 * i + c, 2 * j + c) for c, i, j in steps])
     return lax.ppermute(value, ("core", axis), [(4 * c + i, 4 * c + j) for c, i, j in steps])
@@ -269,16 +269,15 @@
     own, blocks[0] = lax.optimization_barrier((stacked_weights[0], blocks[0]))
     turned = lax.ppermute(own, ("core", "zl"), [(1, 2), (2, 1)])
     own = jnp.where(place[4] == place[3], own, turned)
-    first = lax.axis_index("core") == 0
-    near, back = shift(own, "x", 1), shift(own, "x", 3)
-    own = [own, near, relay(jnp.where(first, near, back), "x"), back]
+    near, back = relay(own, "x"), relay(own, "x", -1)
+    own = [own, near, relay(near, "x"), back]
     blocks = [jnp.concatenate(blocks, axis=0)]
-    near, back = shift(blocks[0], "y", 1), shift(blocks[0], "y", 3)
+    near, back = relay(blocks[0], "y"), relay(blocks[0], "y", -1)
     own[0], own[1], own[3], near, back = lax.optimization_barrier(
         (own[0], own[1], own[3], near, back)
     )
-    other = [swap(block, "core") for block in own]
-    blocks += [near, relay(jnp.where(first, near, back), "y"), back]
+    other = [swap(own[(4 - i) % 4], "core") for i in range(4)]
+    blocks += [near, relay(near, "y"), back]
 
     def project(names, second):
         tall = len(names) * hidden
@@ -297,9 +296,8 @@
     down_far = swap(down, "zl")
 
     def halfway(passed, near, back):
-        passed = passed.astype(F32)
-        near = (near + jnp.where(first, 0.0, passed)).astype(BF16)
-        return near, (back + jnp.where(first, passed, 0.0)).astype(BF16)
+        passed, near = lax.optimization_barrier((passed, near))
+        return near.astype(BF16), (back + passed.astype(F32)).astype(BF16)
 
     unit = 2 * CAP + TILE
     shares = call(
@@ -315,21 +313,21 @@
         weight_kernel,
         place,
         [shares[4]] + blocks,
-        [((3, half, width), kind) for kind in (F32, BF16) for _ in range(4)],
+        [((3, half, width), BF16)] * 8,
         [pltpu.VMEM((2, 4, slots, width), BF16)],
     )
     keeps, sends = terms[0:4], terms[4:8]
-    moved = [swap(send, "core") for send in sends]
+    moved = [swap(sends[(4 - i) % 4], "core") for i in range(4)]
     near, back = halfway(passed, shares[1], shares[3])
     near, back, *moved = lax.optimization_barrier((near, back, *moved))
-    arrived = [shift(near, "y", -1), shift(back, "y", 1)]
+    arrived = [relay(near, "y", -1), relay(back, "y")]
 
     def both_cores(i):
-        return keeps[i] + moved[i].astype(F32)
+        return keeps[i].astype(F32) + moved[i].astype(F32)
 
     passed = relay(both_cores(2).astype(BF16), "x")
     near, back = halfway(passed, both_cores(1), both_cores(3))
-    far_sums = [shift(near, "x", -1), shift(back, "x", 1)]
+    far_sums = [relay(near, "x", -1), relay(back, "x")]
     totals = call(total_kernel, place, [shares[0]] + arrived, [((unit, width), BF16)] * 4)
     returned = [totals[0]] + [shift(totals[k], "expert", -k) for k in (1, 2, 3)]
     layer_output, token_grad, prob_grad = call(

time: 150 us -> 146 us (0.973)
  waiting for transfers between devices: 69.9 us -> 68.2 us
  Pallas kernels: 20.8 us -> 19.1 us
    ppermute x14 -> x6, waiting for transfers between devices: 32.3 us -> 14.5 us  [shift(): return lax.ppermute(value, axis, [(i, (i + step) % 4) for i in range(4)])]
    ppermute x2 -> x6, waiting for transfers between devices: 8.37 us -> 21.9 us  [relay(): lax.ppermute(value, ('core', axis), [(4 * c + i, 4 * c + j) for c, i, j i...]
    ppermute x14 -> x6, starting transfers between devices: 25.1 us -> 14.4 us  [shift(): return lax.ppermute(value, axis, [(i, (i + step) % 4) for i in range(4)])]
    ppermute x2 -> x6, starting transfers between devices: 1.5 us -> 8.34 us  [relay(): lax.ppermute(value, ('core', axis), [(4 * c + i, 4 * c + j) for c, i, j i...]
    ppermute x2 -> x6, starting transfers between devices: 5.11 us -> 11.3 us  [relay(): lax.ppermute(value, ('x', 'core'), [(2 * i + c, 2 * j + c) for c, i, j in...]
    pallas_call x7, Pallas kernels: 20.8 us -> 19.1 us  [call(): pl.pallas_call(kernel, out_shape=[jax.ShapeDtypeStruct(shape, kind) for s...]
    ppermute x2, starting transfers between devices: 8.64 us -> 7.06 us  [turn(): lax.ppermute(value, ('core', 'zl'), [(2 * c + z, 2 * z + c) for c in rang...]
    ppermute x2 -> x6, waiting for transfers between devices: 4.46 us -> 5.72 us  [relay(): lax.ppermute(value, ('x', 'core'), [(2 * i + c, 2 * j + c) for c, i, j in...]
  transfers between devices with their start and end apart: 31 -> 31, of which waited for: 18 -> 17; matrix products, arithmetic and copies ran while one was open for 2% -> 1% of each run, Pallas kernels for 7% -> 7%
where the time goes in v14:
time: 146 us; the launch traced here: 145 us
  waiting for transfers between devices  68.2 us (47%)
  starting transfers between devices  50 us (34%)
  Pallas kernels  19.1 us (13%)
  other arithmetic  4.77 us (3%)
  local copies, waits for them, and re-layouts  2.45 us (2%)
    ppermute x6, waiting for transfers between devices, relay(): lax.ppermute(value, ('core', axis), [(4 * c + i, 4 * c + j) for c, i, j i...  21.9 us
    pallas_call x7, Pallas kernels, call(): pl.pallas_call(kernel, out_shape=[jax.ShapeDtypeStruct(shape, kind) for s...  19.1 us
    ppermute x10, waiting for transfers between devices, swap(): return lax.ppermute(value, axis, [(0, 1), (1, 0)])  14.8 us
    ppermute x6, waiting for transfers between devices, shift(): return lax.ppermute(value, axis, [(i, (i + step) % 4) for i in range(4)])  14.5 us
    ppermute x6, starting transfers between devices, shift(): return lax.ppermute(value, axis, [(i, (i + step) % 4) for i in range(4)])  14.4 us
    ppermute x6, starting transfers between devices, relay(): lax.ppermute(value, ('x', 'core'), [(2 * i + c, 2 * j + c) for c, i, j in...  11.3 us
    ppermute x6, starting transfers between devices, relay(): lax.ppermute(value, ('core', axis), [(4 * c + i, 4 * c + j) for c, i, j i...  8.34 us
    ppermute x2, starting transfers between devices, turn(): lax.ppermute(value, ('core', 'zl'), [(2 * c + z, 2 * z + c) for c in rang...  7.06 us
  transfers between devices with their start and end apart: 31, of which 17 were waited for; matrix products, arithmetic and copies ran while one was open for 1% of the time, Pallas kernels for 7%

profile of v14, /device:TPU:1, one launch (start us, length us, event | category | flops | bytes accessed | tf_op | source)
XLA Modules:
  0.0 145.4 jit_solution(8083537592900799053)
XLA Ops:
  0.7 0.7 convert_bitcast_fusion
  1.4 0.7 pad_maximum_fusion.2.small
  2.1 1.0 pad_maximum_fusion.1.wide
  3.2 1.0 shard_map.84
  4.2 4.9 %collective-permute-start.3 = (bf16[3,192,512]{2,1,0:T(8,128)(2,1)}, bf16[3,192,512]{2,1,0:T(8,128)(2,1)S(1)}, u32[]{:S(2)}, u32[]{:S(2)}) collective-permute-start(bf16[3,192,512]{2,1,0:T(8,128)(2,1)} %bitcast.20), channel_id=1, source_target_pairs={{1,32},{32,1},{3,34},{34,3},{5,36},{36,5},{7,38},{38,7},{9,40},{40... | collective-permute-start | bytes 1769480 | tf_op jit(solution)/shard_map/ppermute | solution.py:270
  9.1 3.1 %collective-permute-start = (bf16[160,512]{1,0:T(8,128)(2,1)S(1)}, bf16[160,512]{1,0:T(8,128)(2,1)S(1)}, u32[]{:S(2)}, u32[]{:S(2)}) collective-permute-start(bf16[160,512]{1,0:T(8,128)(2,1)S(1)} %get-tuple-element.55), channel_id=1, source_target_pairs={{0,8},{8,16},{16,24},{24,0},{1,9},{9,17},{17,25},{25,1},{2,10},{10... | collective-permute-start | bytes 491528 | tf_op jit(solution)/shard_map/ppermute | solution.py:230
  12.2 4.2 %collective-permute-start.1 = (bf16[160,512]{1,0:T(8,128)(2,1)S(1)}, bf16[160,512]{1,0:T(8,128)(2,1)S(1)}, u32[]{:S(2)}, u32[]{:S(2)}) collective-permute-start(bf16[160,512]{1,0:T(8,128)(2,1)S(1)} %get-tuple-element.56), channel_id=1, source_target_pairs={{0,16},{8,24},{16,0},{24,8},{1,17},{9,25},{17,1},{25,9},{2,18},{10... | collective-permute-start | bytes 491528 | tf_op jit(solution)/shard_map/ppermute | solution.py:230
  16.4 2.4 %collective-permute-start.2 = (bf16[160,512]{1,0:T(8,128)(2,1)S(1)}, bf16[160,512]{1,0:T(8,128)(2,1)S(1)}, u32[]{:S(2)}, u32[]{:S(2)}) collective-permute-start(bf16[160,512]{1,0:T(8,128)(2,1)S(1)} %get-tuple-element.57), channel_id=1, source_target_pairs={{0,24},{8,0},{16,8},{24,16},{1,25},{9,1},{17,9},{25,17},{2,26},{10... | collective-permute-start | bytes 491528 | tf_op jit(solution)/shard_map/ppermute | solution.py:230
  18.8 6.2 %collective-permute-done.3 = bf16[3,192,512]{2,1,0:T(8,128)(2,1)S(1)} collective-permute-done((bf16[3,192,512]{2,1,0:T(8,128)(2,1)}, bf16[3,192,512]{2,1,0:T(8,128)(2,1)S(1)}, u32[]{:S(2)}, u32[]{:S(2)}) %collective-permute-start.3) | collective-permute-done | bytes 589856 | tf_op jit(solution)/shard_map/ppermute | solution.py:270
  25.1 2.6 %collective-permute-start.4 = (bf16[3,192,512]{2,1,0:T(8,128)(2,1)S(1)}, bf16[3,192,512]{2,1,0:T(8,128)(2,1)S(1)}, u32[]{:S(2)}, u32[]{:S(2)}) collective-permute-start(bf16[3,192,512]{2,1,0:T(8,128)(2,1)S(1)} %broadcast_select_fusion.refs_4_), channel_id=1, source_target_pairs={{0,64},{64,128},{128,192},{192,0},{32,224},{96,32},{160,96},{224,1... | collective-permute-start | bytes 1769480 | tf_op jit(solution)/shard_map/ppermute | solution.py:236
  27.6 2.8 %collective-permute-done = bf16[160,512]{1,0:T(8,128)(2,1)S(1)} collective-permute-done((bf16[160,512]{1,0:T(8,128)(2,1)S(1)}, bf16[160,512]{1,0:T(8,128)(2,1)S(1)}, u32[]{:S(2)}, u32[]{:S(2)}) %collective-permute-start) | collective-permute-done | bytes 163872 | tf_op jit(solution)/shard_map/ppermute | solution.py:230
  30.5 5.9 %collective-permute-done.1 = bf16[160,512]{1,0:T(8,128)(2,1)S(1)} collective-permute-done((bf16[160,512]{1,0:T(8,128)(2,1)S(1)}, bf16[160,512]{1,0:T(8,128)(2,1)S(1)}, u32[]{:S(2)}, u32[]{:S(2)}) %collective-permute-start.1) | collective-permute-done | bytes 163872 | tf_op jit(solution)/shard_map/ppermute | solution.py:230
  36.4 1.4 collective-permute-start.7
  37.7 1.5 %collective-permute-start.6 = (bf16[640,512]{1,0:T(8,128)(2,1)S(1)}, bf16[640,512]{1,0:T(8,128)(2,1)S(1)}, u32[]{:S(2)}, u32[]{:S(2)}) collective-permute-start(bf16[640,512]{1,0:T(8,128)(2,1)S(1)} %constant_dynamic-update-slice_fusion.refs_0_), channel_id=1, source_target_pairs={{0,2},{2,4},{4,6},{6,0},{32,38},{34,32},{36,34},{38,36},{1,3},{3,5... | collective-permute-start | bytes 1966088 | tf_op jit(solution)/shard_map/ppermute | solution.py:237
  39.3 1.2 collective-permute-start.5
  40.5 1.5 %collective-permute-start.9 = (bf16[3,192,512]{2,1,0:T(8,128)(2,1)S(1)}, bf16[3,192,512]{2,1,0:T(8,128)(2,1)S(1)}, u32[]{:S(2)}, u32[]{:S(2)}) collective-permute-start(bf16[3,192,512]{2,1,0:T(8,128)(2,1)S(1)} %collective-permute-done.4.refs_5_), channel_id=1, source_target_pairs={{0,64},{64,128},{128,192},{192,0},{32,224},{96,32},{160,96},{224,1... | collective-permute-start | bytes 1769480 | tf_op jit(solution)/shard_map/ppermute | solution.py:236
  42.0 7.7 %collective-permute-done.7.refs_3_ = bf16[640,512]{1,0:T(8,128)(2,1)S(1)} collective-permute-done((bf16[640,512]{1,0:T(8,128)(2,1)S(1)}, bf16[640,512]{1,0:T(8,128)(2,1)S(1)}, u32[]{:S(2)}, u32[]{:S(2)}) %collective-permute-start.7) | collective-permute-done | bytes 655392 | tf_op jit(solution)/shard_map/ppermute | solution.py:237
  49.7 1.6 %collective-permute-done.5.refs_7_ = bf16[3,192,512]{2,1,0:T(8,128)(2,1)S(1)} collective-permute-done((bf16[3,192,512]{2,1,0:T(8,128)(2,1)S(1)}, bf16[3,192,512]{2,1,0:T(8,128)(2,1)S(1)}, u32[]{:S(2)}, u32[]{:S(2)}) %collective-permute-start.5) | collective-permute-done | bytes 589856 | tf_op jit(solution)/shard_map/ppermute | solution.py:236
  51.3 2.7 %collective-permute-start.8 = (bf16[640,512]{1,0:T(8,128)(2,1)S(1)}, bf16[640,512]{1,0:T(8,128)(2,1)S(1)}, u32[]{:S(2)}, u32[]{:S(2)}) collective-permute-start(bf16[640,512]{1,0:T(8,128)(2,1)S(1)} %collective-permute-done.6.refs_1_), channel_id=1, source_target_pairs={{0,2},{2,4},{4,6},{6,0},{32,38},{34,32},{36,34},{38,36},{1,3},{3,5... | collective-permute-start | bytes 1966088 | tf_op jit(solution)/shard_map/ppermute | solution.py:237
  55.0 1.0 collective-permute-done.10.refs_8_
  56.0 0.8 collective-permute-done.13.refs_11_
  56.8 0.8 collective-permute-done.11.refs_9_
  57.7 3.8 %collective-permute-done.8.refs_2_ = bf16[640,512]{1,0:T(8,128)(2,1)S(1)} collective-permute-done((bf16[640,512]{1,0:T(8,128)(2,1)S(1)}, bf16[640,512]{1,0:T(8,128)(2,1)S(1)}, u32[]{:S(2)}, u32[]{:S(2)}) %collective-permute-start.8) | collective-permute-done | bytes 655392 | tf_op jit(solution)/shard_map/ppermute | solution.py:237
  61.5 0.8 copy-done.4
  62.4 3.8 %shard_map.85 = (bf16[320,768]{1,0:T(8,128)(2,1)S(1)}, bf16[768,2048]{1,0:T(8,128)(2,1)}) custom-call(s32[5]{0:T(128)S(1)} %stack.23.place, bf16[640,512]{1,0:T(8,128)(2,1)S(1)} %constant_dynamic-update-slice_fusion.refs_0_, bf16[640,512]{1,0:T(8,128)(2,1)} %copy-done, bf16[640,512]{1,0:T(8,128)(2,1)} %copy-done.4, bf16[640,512]{1,0:T(8,128)(2,1)} %copy-done.3, ...), custom_call_target="tpu_custom_call" | custom-call | tf_op jit(solution)/shard_map/pallas_call | solution.py:33
  66.4 3.1 %shard_map.86 = (bf16[320,384]{1,0:T(8,128)(2,1)S(1)}, bf16[384,2048]{1,0:T(8,128)(2,1)}) custom-call(s32[5]{0:T(128)S(1)} %stack.23.place, bf16[640,512]{1,0:T(8,128)(2,1)S(1)} %constant_dynamic-update-slice_fusion.refs_0_, bf16[640,512]{1,0:T(8,128)(2,1)} %copy-done, bf16[640,512]{1,0:T(8,128)(2,1)} %copy-done.4, bf16[640,512]{1,0:T(8,128)(2,1)} %copy-done.3, ...), custom_call_target="tpu_custom_call" | custom-call | tf_op jit(solution)/shard_map/pallas_call | solution.py:33
  69.5 1.5 %collective-permute-start.15 = (bf16[320,384]{1,0:T(8,128)(2,1)S(1)}, bf16[320,384]{1,0:T(8,128)(2,1)S(1)}, u32[]{:S(2)}, u32[]{:S(2)}) collective-permute-start(bf16[320,384]{1,0:T(8,128)(2,1)S(1)} %get-tuple-element.65.down), channel_id=1, source_target_pairs={{0,1},{1,0},{2,3},{3,2},{4,5},{5,4},{6,7},{7,6},{8,9},{9,8},{10,11... | collective-permute-start | bytes 737288 | tf_op jit(solution)/shard_map/ppermute | solution.py:241
  71.0 12.1 %collective-permute-done.15.down_far = bf16[320,384]{1,0:T(8,128)(2,1)S(1)} collective-permute-done((bf16[320,384]{1,0:T(8,128)(2,1)S(1)}, bf16[320,384]{1,0:T(8,128)(2,1)S(1)}, u32[]{:S(2)}, u32[]{:S(2)}) %collective-permute-start.15) | collective-permute-done | bytes 245792 | tf_op jit(solution)/shard_map/ppermute | solution.py:241
  83.2 4.5 %shard_map.87 = (f32[656,512]{1,0:T(8,128)S(1)}, bf16[656,512]{1,0:T(8,128)(2,1)S(1)}, bf16[656,512]{1,0:T(8,128)(2,1)S(1)}, bf16[656,512]{1,0:T(8,128)(2,1)S(1)}, bf16[320,1152]{1,0:T(8,128)(2,1)S(1)}) custom-call(s32[5]{0:T(128)S(1)} %stack.23.place, bf16[320,768]{1,0:T(8,128)(2,1)S(1)} %get-tuple-element.64.pair, ...), custom_call_target="tpu_custom_call" | custom-call | tf_op jit(solution)/shard_map/pallas_call | solution.py:33
  87.7 0.9 copy-done.2
  88.7 4.3 %shard_map.88 = (bf16[3,192,512]{2,1,0:T(8,128)(2,1)S(1)}, bf16[3,192,512]{2,1,0:T(8,128)(2,1)S(1)}, bf16[3,192,512]{2,1,0:T(8,128)(2,1)S(1)}, bf16[3,192,512]{2...) custom-call(s32[5]{0:T(128)S(1)} %stack.23.place, ...), custom_call_target="tpu_custom_call" | custom-call | tf_op jit(solution)/shard_map/pallas_call | solution.py:33
  94.1 4.4 %collective-permute-done.16 = bf16[656,512]{1,0:T(8,128)(2,1)S(1)} collective-permute-done((bf16[656,512]{1,0:T(8,128)(2,1)S(1)}, bf16[656,512]{1,0:T(8,128)(2,1)S(1)}, u32[]{:S(2)}, u32[]{:S(2)}) %collective-permute-start.16) | collective-permute-done | bytes 671776 | tf_op jit(solution)/shard_map/ppermute | solution.py:237
  98.9 2.4 %collective-permute-start.21 = (bf16[3,192,512]{2,1,0:T(8,128)(2,1)S(1)}, bf16[3,192,512]{2,1,0:T(8,128)(2,1)S(1)}, u32[]{:S(2)}, u32[]{:S(2)}) collective-permute-start(bf16[3,192,512]{2,1,0:T(8,128)(2,1)S(1)} %add_convert_fusion.3), channel_id=1, source_target_pairs={{0,64},{64,128},{128,192},{192,0},{32,224},{96,32},{160,96},{224,1... | collective-permute-start | bytes 1769480 | tf_op jit(solution)/shard_map/ppermute | solution.py:236
  101.3 2.7 %collective-permute-start.27 = (bf16[656,512]{1,0:T(8,128)(2,1)S(1)}, bf16[656,512]{1,0:T(8,128)(2,1)S(1)}, u32[]{:S(2)}, u32[]{:S(2)}) collective-permute-start(bf16[656,512]{1,0:T(8,128)(2,1)S(1)} %add_convert_fusion), channel_id=1, source_target_pairs={{0,2},{2,4},{4,6},{6,0},{32,38},{34,32},{36,34},{38,36},{1,3},{3,5... | collective-permute-start | bytes 2015240 | tf_op jit(solution)/shard_map/ppermute | solution.py:237
  104.1 4.0 %collective-permute-done.21 = bf16[3,192,512]{2,1,0:T(8,128)(2,1)S(1)} collective-permute-done((bf16[3,192,512]{2,1,0:T(8,128)(2,1)S(1)}, bf16[3,192,512]{2,1,0:T(8,128)(2,1)S(1)}, u32[]{:S(2)}, u32[]{:S(2)}) %collective-permute-start.21) | collective-permute-done | bytes 589856 | tf_op jit(solution)/shard_map/ppermute | solution.py:236
  108.3 3.7 %collective-permute-start.23 = (bf16[3,192,512]{2,1,0:T(8,128)(2,1)S(1)}, bf16[3,192,512]{2,1,0:T(8,128)(2,1)S(1)}, u32[]{:S(2)}, u32[]{:S(2)}) collective-permute-start(bf16[3,192,512]{2,1,0:T(8,128)(2,1)S(1)} %add_convert_fusion.2), channel_id=1, source_target_pairs={{0,64},{64,128},{128,192},{192,0},{32,224},{96,32},{160,96},{224,1... | collective-permute-start | bytes 1769480 | tf_op jit(solution)/shard_map/ppermute | solution.py:236
  112.0 5.9 %collective-permute-done.26.one = bf16[656,512]{1,0:T(8,128)(2,1)S(1)} collective-permute-done((bf16[656,512]{1,0:T(8,128)(2,1)S(1)}, bf16[656,512]{1,0:T(8,128)(2,1)S(1)}, u32[]{:S(2)}, u32[]{:S(2)}) %collective-permute-start.26) | collective-permute-done | bytes 671776 | tf_op jit(solution)/shard_map/ppermute | solution.py:237
  118.0 0.8 shard_map.89
  118.8 2.5 %collective-permute-start.28 = (bf16[176,512]{1,0:T(8,128)(2,1)S(1)}, bf16[176,512]{1,0:T(8,128)(2,1)S(1)}, u32[]{:S(2)}, u32[]{:S(2)}) collective-permute-start(bf16[176,512]{1,0:T(8,128)(2,1)S(1)} %get-tuple-element.93), channel_id=1, source_target_pairs={{0,24},{8,0},{16,8},{24,16},{1,25},{9,1},{17,9},{25,17},{2,26},{10... | collective-permute-start | bytes 540680 | tf_op jit(solution)/shard_map/ppermute | solution.py:230
  121.3 2.2 %collective-permute-start.30 = (bf16[176,512]{1,0:T(8,128)(2,1)S(1)}, bf16[176,512]{1,0:T(8,128)(2,1)S(1)}, u32[]{:S(2)}, u32[]{:S(2)}) collective-permute-start(bf16[176,512]{1,0:T(8,128)(2,1)S(1)} %get-tuple-element.95), channel_id=1, source_target_pairs={{0,8},{8,16},{16,24},{24,0},{1,9},{9,17},{17,25},{25,1},{2,10},{10... | collective-permute-start | bytes 540680 | tf_op jit(solution)/shard_map/ppermute | solution.py:230
  123.9 5.1 %collective-permute-start.25 = (bf16[288,512]{1,0:T(8,128)(2,1)S(1)}, bf16[288,512]{1,0:T(8,128)(2,1)S(1)}, u32[]{:S(2)}, u32[]{:S(2)}) collective-permute-start(bf16[288,512]{1,0:T(8,128)(2,1)S(1)} %get-tuple-element.102), channel_id=1, source_target_pairs={{0,0},{1,32},{32,1},{33,33},{2,2},{3,34},{34,3},{35,35},{4,4},{5,3... | collective-permute-start | bytes 884744 | tf_op jit(solution)/shard_map/ppermute | solution.py:245
  129.1 1.9 %collective-permute-start.24 = (bf16[288,512]{1,0:T(8,128)(2,1)S(1)}, bf16[288,512]{1,0:T(8,128)(2,1)S(1)}, u32[]{:S(2)}, u32[]{:S(2)}) collective-permute-start(bf16[288,512]{1,0:T(8,128)(2,1)S(1)} %get-tuple-element.103), channel_id=1, source_target_pairs={{0,0},{1,32},{32,1},{33,33},{2,2},{3,34},{34,3},{35,35},{4,4},{5,3... | collective-permute-start | bytes 884744 | tf_op jit(solution)/shard_map/ppermute | solution.py:245
  131.0 5.9 %collective-permute-done.30.refs_3_ = bf16[176,512]{1,0:T(8,128)(2,1)S(1)} collective-permute-done((bf16[176,512]{1,0:T(8,128)(2,1)S(1)}, bf16[176,512]{1,0:T(8,128)(2,1)S(1)}, u32[]{:S(2)}, u32[]{:S(2)}) %collective-permute-start.30) | collective-permute-done | bytes 180256 | tf_op jit(solution)/shard_map/ppermute | solution.py:230
  136.9 1.7 %shard_map.90 = (bf16[128,512]{1,0:T(8,128)(2,1)}, bf16[128,512]{1,0:T(8,128)(2,1)}, f32[8,128]{1,0:T(8,128)S(1)}) custom-call(s32[5]{0:T(128)S(1)} %stack.23.place, f32[4,128]{1,0:T(4,128)S(1)} %pad_maximum_fusion.2.small, bf16[320,128]{1,0:T(8,128)(2,1)S(1)} %get-tuple-element.88.placing, bf16[176,512]{1,0:T(8,128)(2,1)S(1)} %get-tuple-element.92.refs_0_, ...), custom_call_target="tpu_custom_call" | custom-call | tf_op jit(solution)/shard_map/pallas_call | solution.py:33
  138.6 0.6 slice_bitcast_fusion.2
  139.1 2.2 %collective-permute-done.25 = bf16[288,512]{1,0:T(8,128)(2,1)S(1)} collective-permute-done((bf16[288,512]{1,0:T(8,128)(2,1)S(1)}, bf16[288,512]{1,0:T(8,128)(2,1)S(1)}, u32[]{:S(2)}, u32[]{:S(2)}) %collective-permute-start.25) | collective-permute-done | bytes 294944 | tf_op jit(solution)/shard_map/ppermute | solution.py:245
  141.4 2.9 %collective-permute-done.24 = bf16[288,512]{1,0:T(8,128)(2,1)S(1)} collective-permute-done((bf16[288,512]{1,0:T(8,128)(2,1)S(1)}, bf16[288,512]{1,0:T(8,128)(2,1)S(1)}, u32[]{:S(2)}, u32[]{:S(2)}) %collective-permute-start.24) | collective-permute-done | bytes 294944 | tf_op jit(solution)/shard_map/ppermute | solution.py:245
  144.3 1.2 convert.2
  (51 shorter events, 4.0 us)
Async XLA Ops:
  0.6 24.4 %copy-start.5 = (bf16[1,3,192,512]{3,2,1,0:T(8,128)(2,1)S(1)}, bf16[1,3,192,512]{3,2,1,0:T(8,128)(2,1)}, u32[]{:S(2)}) copy-start(bf16[1,3,192,512]{3,2,1,0:T(8,128)(2,1)} %param.8) | copy-start | bytes 1769476
  4.2 20.8 %collective-permute-start.3 = (bf16[3,192,512]{2,1,0:T(8,128)(2,1)}, bf16[3,192,512]{2,1,0:T(8,128)(2,1)S(1)}, u32[]{:S(2)}, u32[]{:S(2)}) collective-permute-start(bf16[3,192,512]{2,1,0:T(8,128)(2,1)} %bitcast.20), channel_id=1, source_target_pairs={{1,32},{32,1},{3,34},{34,3},{5,36},{36,5},{7,38},{38,7},{9,40},{40... | collective-permute-start | bytes 1769480 | tf_op jit(solution)/shard_map/ppermute | solution.py:270
  9.1 21.4 %collective-permute-start = (bf16[160,512]{1,0:T(8,128)(2,1)S(1)}, bf16[160,512]{1,0:T(8,128)(2,1)S(1)}, u32[]{:S(2)}, u32[]{:S(2)}) collective-permute-start(bf16[160,512]{1,0:T(8,128)(2,1)S(1)} %get-tuple-element.55), channel_id=1, source_target_pairs={{0,8},{8,16},{16,24},{24,0},{1,9},{9,17},{17,25},{25,1},{2,10},{10... | collective-permute-start | bytes 491528 | tf_op jit(solution)/shard_map/ppermute | solution.py:230
  12.2 24.1 %collective-permute-start.1 = (bf16[160,512]{1,0:T(8,128)(2,1)S(1)}, bf16[160,512]{1,0:T(8,128)(2,1)S(1)}, u32[]{:S(2)}, u32[]{:S(2)}) collective-permute-start(bf16[160,512]{1,0:T(8,128)(2,1)S(1)} %get-tuple-element.56), channel_id=1, source_target_pairs={{0,16},{8,24},{16,0},{24,8},{1,17},{9,25},{17,1},{25,9},{2,18},{10... | collective-permute-start | bytes 491528 | tf_op jit(solution)/shard_map/ppermute | solution.py:230
  16.4 20.0 %collective-permute-start.2 = (bf16[160,512]{1,0:T(8,128)(2,1)S(1)}, bf16[160,512]{1,0:T(8,128)(2,1)S(1)}, u32[]{:S(2)}, u32[]{:S(2)}) collective-permute-start(bf16[160,512]{1,0:T(8,128)(2,1)S(1)} %get-tuple-element.57), channel_id=1, source_target_pairs={{0,24},{8,0},{16,8},{24,16},{1,25},{9,1},{17,9},{25,17},{2,26},{10... | collective-permute-start | bytes 491528 | tf_op jit(solution)/shard_map/ppermute | solution.py:230
  25.1 15.4 %collective-permute-start.4 = (bf16[3,192,512]{2,1,0:T(8,128)(2,1)S(1)}, bf16[3,192,512]{2,1,0:T(8,128)(2,1)S(1)}, u32[]{:S(2)}, u32[]{:S(2)}) collective-permute-start(bf16[3,192,512]{2,1,0:T(8,128)(2,1)S(1)} %broadcast_select_fusion.refs_4_), channel_id=1, source_target_pairs={{0,64},{64,128},{128,192},{192,0},{32,224},{96,32},{160,96},{224,1... | collective-permute-start | bytes 1769480 | tf_op jit(solution)/shard_map/ppermute | solution.py:236
  36.4 13.3 %collective-permute-start.7 = (bf16[640,512]{1,0:T(8,128)(2,1)S(1)}, bf16[640,512]{1,0:T(8,128)(2,1)S(1)}, u32[]{:S(2)}, u32[]{:S(2)}) collective-permute-start(bf16[640,512]{1,0:T(8,128)(2,1)S(1)} %constant_dynamic-update-slice_fusion.refs_0_), channel_id=1, source_target_pairs={{0,6},{2,0},{4,2},{6,4},{32,34},{34,36},{36,38},{38,32},{1,7},{3,1... | collective-permute-start | bytes 1966088 | tf_op jit(solution)/shard_map/ppermute | solution.py:237
  37.7 11.9 %collective-permute-start.6 = (bf16[640,512]{1,0:T(8,128)(2,1)S(1)}, bf16[640,512]{1,0:T(8,128)(2,1)S(1)}, u32[]{:S(2)}, u32[]{:S(2)}) collective-permute-start(bf16[640,512]{1,0:T(8,128)(2,1)S(1)} %constant_dynamic-update-slice_fusion.refs_0_), channel_id=1, source_target_pairs={{0,2},{2,4},{4,6},{6,0},{32,38},{34,32},{36,34},{38,36},{1,3},{3,5... | collective-permute-start | bytes 1966088 | tf_op jit(solution)/shard_map/ppermute | solution.py:237
  39.3 12.0 %collective-permute-start.5 = (bf16[3,192,512]{2,1,0:T(8,128)(2,1)S(1)}, bf16[3,192,512]{2,1,0:T(8,128)(2,1)S(1)}, u32[]{:S(2)}, u32[]{:S(2)}) collective-permute-start(bf16[3,192,512]{2,1,0:T(8,128)(2,1)S(1)} %broadcast_select_fusion.refs_4_), channel_id=1, source_target_pairs={{0,192},{64,0},{128,64},{192,128},{32,96},{96,160},{160,224},{224,... | collective-permute-start | bytes 1769480 | tf_op jit(solution)/shard_map/ppermute | solution.py:236
  40.5 14.0 %collective-permute-start.9 = (bf16[3,192,512]{2,1,0:T(8,128)(2,1)S(1)}, bf16[3,192,512]{2,1,0:T(8,128)(2,1)S(1)}, u32[]{:S(2)}, u32[]{:S(2)}) collective-permute-start(bf16[3,192,512]{2,1,0:T(8,128)(2,1)S(1)} %collective-permute-done.4.refs_5_), channel_id=1, source_target_pairs={{0,64},{64,128},{128,192},{192,0},{32,224},{96,32},{160,96},{224,1... | collective-permute-start | bytes 1769480 | tf_op jit(solution)/shard_map/ppermute | solution.py:236
  49.7 11.9 %copy-start.3 = (bf16[640,512]{1,0:T(8,128)(2,1)}, bf16[640,512]{1,0:T(8,128)(2,1)S(1)}, u32[]{:S(2)}) copy-start(bf16[640,512]{1,0:T(8,128)(2,1)S(1)} %collective-permute-done.7.refs_3_) | copy-start | bytes 1966084
  49.7 11.9 %copy-start = (bf16[640,512]{1,0:T(8,128)(2,1)}, bf16[640,512]{1,0:T(8,128)(2,1)S(1)}, u32[]{:S(2)}) copy-start(bf16[640,512]{1,0:T(8,128)(2,1)S(1)} %collective-permute-done.6.refs_1_) | copy-start | bytes 1966084
  51.3 10.2 %collective-permute-start.8 = (bf16[640,512]{1,0:T(8,128)(2,1)S(1)}, bf16[640,512]{1,0:T(8,128)(2,1)S(1)}, u32[]{:S(2)}, u32[]{:S(2)}) collective-permute-start(bf16[640,512]{1,0:T(8,128)(2,1)S(1)} %collective-permute-done.6.refs_1_), channel_id=1, source_target_pairs={{0,2},{2,4},{4,6},{6,0},{32,38},{34,32},{36,34},{38,36},{1,3},{3,5... | collective-permute-start | bytes 1966088 | tf_op jit(solution)/shard_map/ppermute | solution.py:237
  54.0 2.0 %collective-permute-start.10 = (bf16[3,192,512]{2,1,0:T(8,128)(2,1)S(1)}, bf16[3,192,512]{2,1,0:T(8,128)(2,1)S(1)}, u32[]{:S(2)}, u32[]{:S(2)}) collective-permute-start(bf16[3,192,512]{2,1,0:T(8,128)(2,1)S(1)} %broadcast_select_fusion.refs_4_), channel_id=1, source_target_pairs={{0,32},{32,0},{1,33},{33,1},{2,34},{34,2},{3,35},{35,3},{4,36},{36... | collective-permute-start | bytes 1769480 | tf_op jit(solution)/shard_map/ppermute | solution.py:241
  54.0 2.8 %collective-permute-start.13 = (bf16[3,192,512]{2,1,0:T(8,128)(2,1)S(1)}, bf16[3,192,512]{2,1,0:T(8,128)(2,1)S(1)}, u32[]{:S(2)}, u32[]{:S(2)}) collective-permute-start(bf16[3,192,512]{2,1,0:T(8,128)(2,1)S(1)} %collective-permute-done.4.refs_5_), channel_id=1, source_target_pairs={{0,32},{32,0},{1,33},{33,1},{2,34},{34,2},{3,35},{35,3},{4,36},{36... | collective-permute-start | bytes 1769480 | tf_op jit(solution)/shard_map/ppermute | solution.py:241
  54.5 3.2 %collective-permute-start.11 = (bf16[3,192,512]{2,1,0:T(8,128)(2,1)S(1)}, bf16[3,192,512]{2,1,0:T(8,128)(2,1)S(1)}, u32[]{:S(2)}, u32[]{:S(2)}) collective-permute-start(bf16[3,192,512]{2,1,0:T(8,128)(2,1)S(1)} %collective-permute-done.5.refs_7_), channel_id=1, source_target_pairs={{0,32},{32,0},{1,33},{33,1},{2,34},{34,2},{3,35},{35,3},{4,36},{36... | collective-permute-start | bytes 1769480 | tf_op jit(solution)/shard_map/ppermute | solution.py:241
  54.5 7.0 %collective-permute-start.12 = (bf16[3,192,512]{2,1,0:T(8,128)(2,1)S(1)}, bf16[3,192,512]{2,1,0:T(8,128)(2,1)S(1)}, u32[]{:S(2)}, u32[]{:S(2)}) collective-permute-start(bf16[3,192,512]{2,1,0:T(8,128)(2,1)S(1)} %collective-permute-done.9.refs_6_), channel_id=1, source_target_pairs={{0,32},{32,0},{1,33},{33,1},{2,34},{34,2},{3,35},{35,3},{4,36},{36... | collective-permute-start | bytes 1769480 | tf_op jit(solution)/shard_map/ppermute | solution.py:241
  61.5 0.9 copy-start.4
  66.1 17.0 %collective-permute-start.14 = (bf16[320,768]{1,0:T(8,128)(2,1)S(1)}, bf16[320,768]{1,0:T(8,128)(2,1)S(1)}, u32[]{:S(2)}, u32[]{:S(2)}) collective-permute-start(bf16[320,768]{1,0:T(8,128)(2,1)S(1)} %get-tuple-element.64.pair), channel_id=1, source_target_pairs={{0,1},{1,0},{2,3},{3,2},{4,5},{5,4},{6,7},{7,6},{8,9},{9,8},{10,11... | collective-permute-start | bytes 1474568 | tf_op jit(solution)/shard_map/ppermute | solution.py:241
  69.5 13.7 %collective-permute-start.15 = (bf16[320,384]{1,0:T(8,128)(2,1)S(1)}, bf16[320,384]{1,0:T(8,128)(2,1)S(1)}, u32[]{:S(2)}, u32[]{:S(2)}) collective-permute-start(bf16[320,384]{1,0:T(8,128)(2,1)S(1)} %get-tuple-element.65.down), channel_id=1, source_target_pairs={{0,1},{1,0},{2,3},{3,2},{4,5},{5,4},{6,7},{7,6},{8,9},{9,8},{10,11... | collective-permute-start | bytes 737288 | tf_op jit(solution)/shard_map/ppermute | solution.py:241
  83.2 5.5 %copy-start.1 = (bf16[640,512]{1,0:T(8,128)(2,1)S(1)}, bf16[640,512]{1,0:T(8,128)(2,1)}, u32[]{:S(2)}) copy-start(bf16[640,512]{1,0:T(8,128)(2,1)} %copy-done) | copy-start | bytes 1966084
  87.7 0.9 copy-start.2
  88.6 9.9 %collective-permute-start.16 = (bf16[656,512]{1,0:T(8,128)(2,1)S(1)}, bf16[656,512]{1,0:T(8,128)(2,1)S(1)}, u32[]{:S(2)}, u32[]{:S(2)}) collective-permute-start(bf16[656,512]{1,0:T(8,128)(2,1)S(1)} %get-tuple-element.70), channel_id=1, source_target_pairs={{0,2},{2,4},{4,6},{6,0},{32,38},{34,32},{36,34},{38,36},{1,3},{3,5... | collective-permute-start | bytes 2015240 | tf_op jit(solution)/shard_map/ppermute | solution.py:237
  93.0 5.7 %collective-permute-start.17 = (bf16[3,192,512]{2,1,0:T(8,128)(2,1)S(1)}, bf16[3,192,512]{2,1,0:T(8,128)(2,1)S(1)}, u32[]{:S(2)}, u32[]{:S(2)}) collective-permute-start(bf16[3,192,512]{2,1,0:T(8,128)(2,1)S(1)} %get-tuple-element.75), channel_id=1, source_target_pairs={{0,32},{32,0},{1,33},{33,1},{2,34},{34,2},{3,35},{35,3},{4,36},{36... | collective-permute-start | bytes 1769480 | tf_op jit(solution)/shard_map/ppermute | solution.py:241
  93.1 5.6 %collective-permute-start.18 = (bf16[3,192,512]{2,1,0:T(8,128)(2,1)S(1)}, bf16[3,192,512]{2,1,0:T(8,128)(2,1)S(1)}, u32[]{:S(2)}, u32[]{:S(2)}) collective-permute-start(bf16[3,192,512]{2,1,0:T(8,128)(2,1)S(1)} %get-tuple-element.76), channel_id=1, source_target_pairs={{0,32},{32,0},{1,33},{33,1},{2,34},{34,2},{3,35},{35,3},{4,36},{36... | collective-permute-start | bytes 1769480 | tf_op jit(solution)/shard_map/ppermute | solution.py:241
  93.6 5.1 %collective-permute-start.19 = (bf16[3,192,512]{2,1,0:T(8,128)(2,1)S(1)}, bf16[3,192,512]{2,1,0:T(8,128)(2,1)S(1)}, u32[]{:S(2)}, u32[]{:S(2)}) collective-permute-start(bf16[3,192,512]{2,1,0:T(8,128)(2,1)S(1)} %get-tuple-element.77), channel_id=1, source_target_pairs={{0,32},{32,0},{1,33},{33,1},{2,34},{34,2},{3,35},{35,3},{4,36},{36... | collective-permute-start | bytes 1769480 | tf_op jit(solution)/shard_map/ppermute | solution.py:241
  93.7 5.0 %collective-permute-start.20 = (bf16[3,192,512]{2,1,0:T(8,128)(2,1)S(1)}, bf16[3,192,512]{2,1,0:T(8,128)(2,1)S(1)}, u32[]{:S(2)}, u32[]{:S(2)}) collective-permute-start(bf16[3,192,512]{2,1,0:T(8,128)(2,1)S(1)} %get-tuple-element.78), channel_id=1, source_target_pairs={{0,32},{32,0},{1,33},{33,1},{2,34},{34,2},{3,35},{35,3},{4,36},{36... | collective-permute-start | bytes 1769480 | tf_op jit(solution)/shard_map/ppermute | solution.py:241
  98.9 9.2 %collective-permute-start.21 = (bf16[3,192,512]{2,1,0:T(8,128)(2,1)S(1)}, bf16[3,192,512]{2,1,0:T(8,128)(2,1)S(1)}, u32[]{:S(2)}, u32[]{:S(2)}) collective-permute-start(bf16[3,192,512]{2,1,0:T(8,128)(2,1)S(1)} %add_convert_fusion.3), channel_id=1, source_target_pairs={{0,64},{64,128},{128,192},{192,0},{32,224},{96,32},{160,96},{224,1... | collective-permute-start | bytes 1769480 | tf_op jit(solution)/shard_map/ppermute | solution.py:236
  101.3 16.7 %collective-permute-start.26 = (bf16[656,512]{1,0:T(8,128)(2,1)S(1)}, bf16[656,512]{1,0:T(8,128)(2,1)S(1)}, u32[]{:S(2)}, u32[]{:S(2)}) collective-permute-start(bf16[656,512]{1,0:T(8,128)(2,1)S(1)} %get-tuple-element.90), channel_id=1, source_target_pairs={{0,6},{2,0},{4,2},{6,4},{32,34},{34,36},{36,38},{38,32},{1,7},{3,1... | collective-permute-start | bytes 2015240 | tf_op jit(solution)/shard_map/ppermute | solution.py:237
  101.3 16.7 %collective-permute-start.27 = (bf16[656,512]{1,0:T(8,128)(2,1)S(1)}, bf16[656,512]{1,0:T(8,128)(2,1)S(1)}, u32[]{:S(2)}, u32[]{:S(2)}) collective-permute-start(bf16[656,512]{1,0:T(8,128)(2,1)S(1)} %add_convert_fusion), channel_id=1, source_target_pairs={{0,2},{2,4},{4,6},{6,0},{32,38},{34,32},{36,34},{38,36},{1,3},{3,5... | collective-permute-start | bytes 2015240 | tf_op jit(solution)/shard_map/ppermute | solution.py:237
  108.1 15.4 %collective-permute-start.22 = (bf16[3,192,512]{2,1,0:T(8,128)(2,1)S(1)}, bf16[3,192,512]{2,1,0:T(8,128)(2,1)S(1)}, u32[]{:S(2)}, u32[]{:S(2)}) collective-permute-start(bf16[3,192,512]{2,1,0:T(8,128)(2,1)S(1)} %convert_add_fusion), channel_id=1, source_target_pairs={{0,192},{64,0},{128,64},{192,128},{32,96},{96,160},{160,224},{224,... | collective-permute-start | bytes 1769480 | tf_op jit(solution)/shard_map/ppermute | solution.py:236
  108.3 15.2 %collective-permute-start.23 = (bf16[3,192,512]{2,1,0:T(8,128)(2,1)S(1)}, bf16[3,192,512]{2,1,0:T(8,128)(2,1)S(1)}, u32[]{:S(2)}, u32[]{:S(2)}) collective-permute-start(bf16[3,192,512]{2,1,0:T(8,128)(2,1)S(1)} %add_convert_fusion.2), channel_id=1, source_target_pairs={{0,64},{64,128},{128,192},{192,0},{32,224},{96,32},{160,96},{224,1... | collective-permute-start | bytes 1769480 | tf_op jit(solution)/shard_map/ppermute | solution.py:236
  118.8 12.2 %collective-permute-start.28 = (bf16[176,512]{1,0:T(8,128)(2,1)S(1)}, bf16[176,512]{1,0:T(8,128)(2,1)S(1)}, u32[]{:S(2)}, u32[]{:S(2)}) collective-permute-start(bf16[176,512]{1,0:T(8,128)(2,1)S(1)} %get-tuple-element.93), channel_id=1, source_target_pairs={{0,24},{8,0},{16,8},{24,16},{1,25},{9,1},{17,9},{25,17},{2,26},{10... | collective-permute-start | bytes 540680 | tf_op jit(solution)/shard_map/ppermute | solution.py:230
  121.3 9.7 %collective-permute-start.29 = (bf16[176,512]{1,0:T(8,128)(2,1)S(1)}, bf16[176,512]{1,0:T(8,128)(2,1)S(1)}, u32[]{:S(2)}, u32[]{:S(2)}) collective-permute-start(bf16[176,512]{1,0:T(8,128)(2,1)S(1)} %get-tuple-element.94), channel_id=1, source_target_pairs={{0,16},{8,24},{16,0},{24,8},{1,17},{9,25},{17,1},{25,9},{2,18},{10... | collective-permute-start | bytes 540680 | tf_op jit(solution)/shard_map/ppermute | solution.py:230
  121.3 15.6 %collective-permute-start.30 = (bf16[176,512]{1,0:T(8,128)(2,1)S(1)}, bf16[176,512]{1,0:T(8,128)(2,1)S(1)}, u32[]{:S(2)}, u32[]{:S(2)}) collective-permute-start(bf16[176,512]{1,0:T(8,128)(2,1)S(1)} %get-tuple-element.95), channel_id=1, source_target_pairs={{0,8},{8,16},{16,24},{24,0},{1,9},{9,17},{17,25},{25,1},{2,10},{10... | collective-permute-start | bytes 540680 | tf_op jit(solution)/shard_map/ppermute | solution.py:230
  123.9 17.4 %collective-permute-start.25 = (bf16[288,512]{1,0:T(8,128)(2,1)S(1)}, bf16[288,512]{1,0:T(8,128)(2,1)S(1)}, u32[]{:S(2)}, u32[]{:S(2)}) collective-permute-start(bf16[288,512]{1,0:T(8,128)(2,1)S(1)} %get-tuple-element.102), channel_id=1, source_target_pairs={{0,0},{1,32},{32,1},{33,33},{2,2},{3,34},{34,3},{35,35},{4,4},{5,3... | collective-permute-start | bytes 884744 | tf_op jit(solution)/shard_map/ppermute | solution.py:245
  129.1 15.2 %collective-permute-start.24 = (bf16[288,512]{1,0:T(8,128)(2,1)S(1)}, bf16[288,512]{1,0:T(8,128)(2,1)S(1)}, u32[]{:S(2)}, u32[]{:S(2)}) collective-permute-start(bf16[288,512]{1,0:T(8,128)(2,1)S(1)} %get-tuple-element.103), channel_id=1, source_target_pairs={{0,0},{1,32},{32,1},{33,33},{2,2},{3,34},{34,3},{35,35},{4,4},{5,3... | collective-permute-start | bytes 884744 | tf_op jit(solution)/shard_map/ppermute | solution.py:245

commit v15 on v14

--- a/solution.py
+++ b/solution.py
@@ -266,7 +266,7 @@
     )
 
     blocks = [blocks[0]] + [shift(blocks[k], "expert", k) for k in (1, 2, 3)]
-    own, blocks[0] = lax.optimization_barrier((stacked_weights[0], blocks[0]))
+    own = stacked_weights[0]
     turned = lax.ppermute(own, ("core", "zl"), [(1, 2), (2, 1)])
     own = jnp.where(place[4] == place[3], own, turned)
     near, back = relay(own, "x"), relay(own, "x", -1)

time: 146 us -> 147 us (level)
    ppermute x1, waiting for transfers between devices: 6.23 us -> 0.01 us  [body(): turned = lax.ppermute(own, ('core', 'zl'), [(1, 2), (2, 1)])]
    ppermute x6, waiting for transfers between devices: 21.9 us -> 26.4 us  [relay(): lax.ppermute(value, ('core', axis), [(4 * c + i, 4 * c + j) for c, i, j i...]
    ppermute x6, waiting for transfers between devices: 14.5 us -> 18.5 us  [shift(): return lax.ppermute(value, axis, [(i, (i + step) % 4) for i in range(4)])]
  transfers between devices with their start and end apart: 31 -> 31, of which waited for: 17 -> 20; matrix products, arithmetic and copies ran while one was open for 1% -> 3% of each run, Pallas kernels for 7% -> 7%
where the time goes in v15:
time: 147 us
  waiting for transfers between devices  69.2 us (47%)
  starting transfers between devices  50.2 us (34%)
  Pallas kernels  19.1 us (13%)
  other arithmetic  4.71 us (3%)
  local copies, waits for them, and re-layouts  2.44 us (2%)
    ppermute x6, waiting for transfers between devices, relay(): lax.ppermute(value, ('core', axis), [(4 * c + i, 4 * c + j) for c, i, j i...  26.4 us
    pallas_call x7, Pallas kernels, call(): pl.pallas_call(kernel, out_shape=[jax.ShapeDtypeStruct(shape, kind) for s...  19.1 us
    ppermute x6, waiting for transfers between devices, shift(): return lax.ppermute(value, axis, [(i, (i + step) % 4) for i in range(4)])  18.5 us
    ppermute x10, waiting for transfers between devices, swap(): return lax.ppermute(value, axis, [(0, 1), (1, 0)])  15.2 us
    ppermute x6, starting transfers between devices, shift(): return lax.ppermute(value, axis, [(i, (i + step) % 4) for i in range(4)])  14.3 us
    ppermute x6, starting transfers between devices, relay(): lax.ppermute(value, ('x', 'core'), [(2 * i + c, 2 * j + c) for c, i, j in...  11.1 us
    ppermute x6, starting transfers between devices, relay(): lax.ppermute(value, ('core', axis), [(4 * c + i, 4 * c + j) for c, i, j i...  8.12 us
    ppermute x2, starting transfers between devices, turn(): lax.ppermute(value, ('core', 'zl'), [(2 * c + z, 2 * z + c) for c in rang...  7.32 us
  transfers between devices with their start and end apart: 31, of which 20 were waited for; matrix products, arithmetic and copies ran while one was open for 3% of the time, Pallas kernels for 7%

profile of v15, /device:TPU:1, one launch (start us, length us, event | category | flops | bytes accessed | tf_op | source)
XLA Modules:
  0.0 146.5 jit_solution(6945581024977584736)
XLA Ops:
  0.6 5.1 %collective-permute-start.3 = (bf16[3,192,512]{2,1,0:T(8,128)(2,1)}, bf16[3,192,512]{2,1,0:T(8,128)(2,1)S(1)}, u32[]{:S(2)}, u32[]{:S(2)}) collective-permute-start(bf16[3,192,512]{2,1,0:T(8,128)(2,1)} %bitcast.21), channel_id=1, source_target_pairs={{1,32},{32,1},{3,34},{34,3},{5,36},{36,5},{7,38},{38,7},{9,40},{40... | collective-permute-start | bytes 1769480 | tf_op jit(solution)/shard_map/ppermute | solution.py:270
  7.2 1.0 pad_maximum_fusion.1.wide
  8.2 1.0 shard_map.84
  9.2 3.1 %collective-permute-start = (bf16[160,512]{1,0:T(8,128)(2,1)S(1)}, bf16[160,512]{1,0:T(8,128)(2,1)S(1)}, u32[]{:S(2)}, u32[]{:S(2)}) collective-permute-start(bf16[160,512]{1,0:T(8,128)(2,1)S(1)} %get-tuple-element.52), channel_id=1, source_target_pairs={{0,8},{8,16},{16,24},{24,0},{1,9},{9,17},{17,25},{25,1},{2,10},{10... | collective-permute-start | bytes 491528 | tf_op jit(solution)/shard_map/ppermute | solution.py:230
  12.2 4.2 %collective-permute-start.1 = (bf16[160,512]{1,0:T(8,128)(2,1)S(1)}, bf16[160,512]{1,0:T(8,128)(2,1)S(1)}, u32[]{:S(2)}, u32[]{:S(2)}) collective-permute-start(bf16[160,512]{1,0:T(8,128)(2,1)S(1)} %get-tuple-element.53), channel_id=1, source_target_pairs={{0,16},{8,24},{16,0},{24,8},{1,17},{9,25},{17,1},{25,9},{2,18},{10... | collective-permute-start | bytes 491528 | tf_op jit(solution)/shard_map/ppermute | solution.py:230
  16.5 2.4 %collective-permute-start.2 = (bf16[160,512]{1,0:T(8,128)(2,1)S(1)}, bf16[160,512]{1,0:T(8,128)(2,1)S(1)}, u32[]{:S(2)}, u32[]{:S(2)}) collective-permute-start(bf16[160,512]{1,0:T(8,128)(2,1)S(1)} %get-tuple-element.54), channel_id=1, source_target_pairs={{0,24},{8,0},{16,8},{24,16},{1,25},{9,1},{17,9},{25,17},{2,26},{10... | collective-permute-start | bytes 491528 | tf_op jit(solution)/shard_map/ppermute | solution.py:230
  18.9 2.6 %collective-permute-start.4 = (bf16[3,192,512]{2,1,0:T(8,128)(2,1)S(1)}, bf16[3,192,512]{2,1,0:T(8,128)(2,1)S(1)}, u32[]{:S(2)}, u32[]{:S(2)}) collective-permute-start(bf16[3,192,512]{2,1,0:T(8,128)(2,1)S(1)} %broadcast_select_fusion.refs_4_), channel_id=1, source_target_pairs={{0,64},{64,128},{128,192},{192,0},{32,224},{96,32},{160,96},{224,1... | collective-permute-start | bytes 1769480 | tf_op jit(solution)/shard_map/ppermute | solution.py:236
  21.5 7.3 %collective-permute-done = bf16[160,512]{1,0:T(8,128)(2,1)S(1)} collective-permute-done((bf16[160,512]{1,0:T(8,128)(2,1)S(1)}, bf16[160,512]{1,0:T(8,128)(2,1)S(1)}, u32[]{:S(2)}, u32[]{:S(2)}) %collective-permute-start) | collective-permute-done | bytes 163872 | tf_op jit(solution)/shard_map/ppermute | solution.py:230
  28.8 2.7 %collective-permute-done.1 = bf16[160,512]{1,0:T(8,128)(2,1)S(1)} collective-permute-done((bf16[160,512]{1,0:T(8,128)(2,1)S(1)}, bf16[160,512]{1,0:T(8,128)(2,1)S(1)}, u32[]{:S(2)}, u32[]{:S(2)}) %collective-permute-start.1) | collective-permute-done | bytes 163872 | tf_op jit(solution)/shard_map/ppermute | solution.py:230
  31.6 1.4 collective-permute-start.7
  33.0 1.5 %collective-permute-start.6 = (bf16[640,512]{1,0:T(8,128)(2,1)S(1)}, bf16[640,512]{1,0:T(8,128)(2,1)S(1)}, u32[]{:S(2)}, u32[]{:S(2)}) collective-permute-start(bf16[640,512]{1,0:T(8,128)(2,1)S(1)} %constant_dynamic-update-slice_fusion.refs_0_), channel_id=1, source_target_pairs={{0,2},{2,4},{4,6},{6,0},{32,38},{34,32},{36,34},{38,36},{1,3},{3,5... | collective-permute-start | bytes 1966088 | tf_op jit(solution)/shard_map/ppermute | solution.py:237
  34.5 1.2 collective-permute-start.5
  35.7 1.5 %collective-permute-start.9 = (bf16[3,192,512]{2,1,0:T(8,128)(2,1)S(1)}, bf16[3,192,512]{2,1,0:T(8,128)(2,1)S(1)}, u32[]{:S(2)}, u32[]{:S(2)}) collective-permute-start(bf16[3,192,512]{2,1,0:T(8,128)(2,1)S(1)} %collective-permute-done.4.refs_5_), channel_id=1, source_target_pairs={{0,64},{64,128},{128,192},{192,0},{32,224},{96,32},{160,96},{224,1... | collective-permute-start | bytes 1769480 | tf_op jit(solution)/shard_map/ppermute | solution.py:236
  37.2 11.6 %collective-permute-done.7.refs_3_ = bf16[640,512]{1,0:T(8,128)(2,1)S(1)} collective-permute-done((bf16[640,512]{1,0:T(8,128)(2,1)S(1)}, bf16[640,512]{1,0:T(8,128)(2,1)S(1)}, u32[]{:S(2)}, u32[]{:S(2)}) %collective-permute-start.7) | collective-permute-done | bytes 655392 | tf_op jit(solution)/shard_map/ppermute | solution.py:237
  48.8 1.3 collective-permute-done.5.refs_7_
  51.5 0.9 collective-permute-done.10.refs_8_
  52.4 0.8 collective-permute-done.13.refs_11_
  53.2 0.8 collective-permute-done.11.refs_9_
  54.1 5.8 %collective-permute-done.8.refs_2_ = bf16[640,512]{1,0:T(8,128)(2,1)S(1)} collective-permute-done((bf16[640,512]{1,0:T(8,128)(2,1)S(1)}, bf16[640,512]{1,0:T(8,128)(2,1)S(1)}, u32[]{:S(2)}, u32[]{:S(2)}) %collective-permute-start.8) | collective-permute-done | bytes 655392 | tf_op jit(solution)/shard_map/ppermute | solution.py:237
  59.9 0.8 copy-done.4
  60.7 3.8 %shard_map.85 = (bf16[320,768]{1,0:T(8,128)(2,1)S(1)}, bf16[768,2048]{1,0:T(8,128)(2,1)}) custom-call(s32[5]{0:T(128)S(1)} %stack.23.place, bf16[640,512]{1,0:T(8,128)(2,1)S(1)} %constant_dynamic-update-slice_fusion.refs_0_, bf16[640,512]{1,0:T(8,128)(2,1)} %copy-done, bf16[640,512]{1,0:T(8,128)(2,1)} %copy-done.4, bf16[640,512]{1,0:T(8,128)(2,1)} %copy-done.3, ...), custom_call_target="tpu_custom_call" | custom-call | tf_op jit(solution)/shard_map/pallas_call | solution.py:33
  64.8 3.1 %shard_map.86 = (bf16[320,384]{1,0:T(8,128)(2,1)S(1)}, bf16[384,2048]{1,0:T(8,128)(2,1)}) custom-call(s32[5]{0:T(128)S(1)} %stack.23.place, bf16[640,512]{1,0:T(8,128)(2,1)S(1)} %constant_dynamic-update-slice_fusion.refs_0_, bf16[640,512]{1,0:T(8,128)(2,1)} %copy-done, bf16[640,512]{1,0:T(8,128)(2,1)} %copy-done.4, bf16[640,512]{1,0:T(8,128)(2,1)} %copy-done.3, ...), custom_call_target="tpu_custom_call" | custom-call | tf_op jit(solution)/shard_map/pallas_call | solution.py:33
  67.9 1.5 %collective-permute-start.15 = (bf16[320,384]{1,0:T(8,128)(2,1)S(1)}, bf16[320,384]{1,0:T(8,128)(2,1)S(1)}, u32[]{:S(2)}, u32[]{:S(2)}) collective-permute-start(bf16[320,384]{1,0:T(8,128)(2,1)S(1)} %get-tuple-element.61.down), channel_id=1, source_target_pairs={{0,1},{1,0},{2,3},{3,2},{4,5},{5,4},{6,7},{7,6},{8,9},{9,8},{10,11... | collective-permute-start | bytes 737288 | tf_op jit(solution)/shard_map/ppermute | solution.py:241
  69.4 11.3 %collective-permute-done.15.down_far = bf16[320,384]{1,0:T(8,128)(2,1)S(1)} collective-permute-done((bf16[320,384]{1,0:T(8,128)(2,1)S(1)}, bf16[320,384]{1,0:T(8,128)(2,1)S(1)}, u32[]{:S(2)}, u32[]{:S(2)}) %collective-permute-start.15) | collective-permute-done | bytes 245792 | tf_op jit(solution)/shard_map/ppermute | solution.py:241
  80.7 4.5 %shard_map.87 = (f32[656,512]{1,0:T(8,128)S(1)}, bf16[656,512]{1,0:T(8,128)(2,1)S(1)}, bf16[656,512]{1,0:T(8,128)(2,1)S(1)}, bf16[656,512]{1,0:T(8,128)(2,1)S(1)}, bf16[320,1152]{1,0:T(8,128)(2,1)S(1)}) custom-call(s32[5]{0:T(128)S(1)} %stack.23.place, bf16[320,768]{1,0:T(8,128)(2,1)S(1)} %get-tuple-element.60.pair, ...), custom_call_target="tpu_custom_call" | custom-call | tf_op jit(solution)/shard_map/pallas_call | solution.py:33
  85.3 0.9 copy-done.2
  86.1 2.3 %collective-permute-start.16 = (bf16[656,512]{1,0:T(8,128)(2,1)S(1)}, bf16[656,512]{1,0:T(8,128)(2,1)S(1)}, u32[]{:S(2)}, u32[]{:S(2)}) collective-permute-start(bf16[656,512]{1,0:T(8,128)(2,1)S(1)} %get-tuple-element.66), channel_id=1, source_target_pairs={{0,2},{2,4},{4,6},{6,0},{32,38},{34,32},{36,34},{38,36},{1,3},{3,5... | collective-permute-start | bytes 2015240 | tf_op jit(solution)/shard_map/ppermute | solution.py:237
  88.5 4.3 %shard_map.88 = (bf16[3,192,512]{2,1,0:T(8,128)(2,1)S(1)}, bf16[3,192,512]{2,1,0:T(8,128)(2,1)S(1)}, bf16[3,192,512]{2,1,0:T(8,128)(2,1)S(1)}, bf16[3,192,512]{2...) custom-call(s32[5]{0:T(128)S(1)} %stack.23.place, ...), custom_call_target="tpu_custom_call" | custom-call | tf_op jit(solution)/shard_map/pallas_call | solution.py:33
  94.1 2.1 %collective-permute-done.16 = bf16[656,512]{1,0:T(8,128)(2,1)S(1)} collective-permute-done((bf16[656,512]{1,0:T(8,128)(2,1)S(1)}, bf16[656,512]{1,0:T(8,128)(2,1)S(1)}, u32[]{:S(2)}, u32[]{:S(2)}) %collective-permute-start.16) | collective-permute-done | bytes 671776 | tf_op jit(solution)/shard_map/ppermute | solution.py:237
  96.8 0.8 collective-permute-done.20
  97.8 2.2 %collective-permute-start.21 = (bf16[3,192,512]{2,1,0:T(8,128)(2,1)S(1)}, bf16[3,192,512]{2,1,0:T(8,128)(2,1)S(1)}, u32[]{:S(2)}, u32[]{:S(2)}) collective-permute-start(bf16[3,192,512]{2,1,0:T(8,128)(2,1)S(1)} %add_convert_fusion.3), channel_id=1, source_target_pairs={{0,64},{64,128},{128,192},{192,0},{32,224},{96,32},{160,96},{224,1... | collective-permute-start | bytes 1769480 | tf_op jit(solution)/shard_map/ppermute | solution.py:236
  100.4 2.3 %collective-permute-start.27 = (bf16[656,512]{1,0:T(8,128)(2,1)S(1)}, bf16[656,512]{1,0:T(8,128)(2,1)S(1)}, u32[]{:S(2)}, u32[]{:S(2)}) collective-permute-start(bf16[656,512]{1,0:T(8,128)(2,1)S(1)} %add_convert_fusion), channel_id=1, source_target_pairs={{0,2},{2,4},{4,6},{6,0},{32,38},{34,32},{36,34},{38,36},{1,3},{3,5... | collective-permute-start | bytes 2015240 | tf_op jit(solution)/shard_map/ppermute | solution.py:237
  102.9 4.0 %collective-permute-done.21 = bf16[3,192,512]{2,1,0:T(8,128)(2,1)S(1)} collective-permute-done((bf16[3,192,512]{2,1,0:T(8,128)(2,1)S(1)}, bf16[3,192,512]{2,1,0:T(8,128)(2,1)S(1)}, u32[]{:S(2)}, u32[]{:S(2)}) %collective-permute-start.21) | collective-permute-done | bytes 589856 | tf_op jit(solution)/shard_map/ppermute | solution.py:236
  106.9 2.6 %collective-permute-start.22 = (bf16[3,192,512]{2,1,0:T(8,128)(2,1)S(1)}, bf16[3,192,512]{2,1,0:T(8,128)(2,1)S(1)}, u32[]{:S(2)}, u32[]{:S(2)}) collective-permute-start(bf16[3,192,512]{2,1,0:T(8,128)(2,1)S(1)} %convert_add_fusion), channel_id=1, source_target_pairs={{0,192},{64,0},{128,64},{192,128},{32,96},{96,160},{160,224},{224,... | collective-permute-start | bytes 1769480 | tf_op jit(solution)/shard_map/ppermute | solution.py:236
  109.8 1.0 collective-permute-start.23
  110.8 3.9 %collective-permute-done.26.one = bf16[656,512]{1,0:T(8,128)(2,1)S(1)} collective-permute-done((bf16[656,512]{1,0:T(8,128)(2,1)S(1)}, bf16[656,512]{1,0:T(8,128)(2,1)S(1)}, u32[]{:S(2)}, u32[]{:S(2)}) %collective-permute-start.26) | collective-permute-done | bytes 671776 | tf_op jit(solution)/shard_map/ppermute | solution.py:237
  114.8 2.9 %collective-permute-done.27.three = bf16[656,512]{1,0:T(8,128)(2,1)S(1)} collective-permute-done((bf16[656,512]{1,0:T(8,128)(2,1)S(1)}, bf16[656,512]{1,0:T(8,128)(2,1)S(1)}, u32[]{:S(2)}, u32[]{:S(2)}) %collective-permute-start.27) | collective-permute-done | bytes 671776 | tf_op jit(solution)/shard_map/ppermute | solution.py:237
  117.7 0.8 shard_map.89
  118.4 2.5 %collective-permute-start.28 = (bf16[176,512]{1,0:T(8,128)(2,1)S(1)}, bf16[176,512]{1,0:T(8,128)(2,1)S(1)}, u32[]{:S(2)}, u32[]{:S(2)}) collective-permute-start(bf16[176,512]{1,0:T(8,128)(2,1)S(1)} %get-tuple-element.89), channel_id=1, source_target_pairs={{0,24},{8,0},{16,8},{24,16},{1,25},{9,1},{17,9},{25,17},{2,26},{10... | collective-permute-start | bytes 540680 | tf_op jit(solution)/shard_map/ppermute | solution.py:230
  120.9 2.0 %collective-permute-start.29 = (bf16[176,512]{1,0:T(8,128)(2,1)S(1)}, bf16[176,512]{1,0:T(8,128)(2,1)S(1)}, u32[]{:S(2)}, u32[]{:S(2)}) collective-permute-start(bf16[176,512]{1,0:T(8,128)(2,1)S(1)} %get-tuple-element.90), channel_id=1, source_target_pairs={{0,16},{8,24},{16,0},{24,8},{1,17},{9,25},{17,1},{25,9},{2,18},{10... | collective-permute-start | bytes 540680 | tf_op jit(solution)/shard_map/ppermute | solution.py:230
  123.5 5.4 %collective-permute-start.25 = (bf16[288,512]{1,0:T(8,128)(2,1)S(1)}, bf16[288,512]{1,0:T(8,128)(2,1)S(1)}, u32[]{:S(2)}, u32[]{:S(2)}) collective-permute-start(bf16[288,512]{1,0:T(8,128)(2,1)S(1)} %get-tuple-element.98), channel_id=1, source_target_pairs={{0,0},{1,32},{32,1},{33,33},{2,2},{3,34},{34,3},{35,35},{4,4},{5,3... | collective-permute-start | bytes 884744 | tf_op jit(solution)/shard_map/ppermute | solution.py:245
  128.9 1.9 %collective-permute-start.24 = (bf16[288,512]{1,0:T(8,128)(2,1)S(1)}, bf16[288,512]{1,0:T(8,128)(2,1)S(1)}, u32[]{:S(2)}, u32[]{:S(2)}) collective-permute-start(bf16[288,512]{1,0:T(8,128)(2,1)S(1)} %get-tuple-element.99), channel_id=1, source_target_pairs={{0,0},{1,32},{32,1},{33,33},{2,2},{3,34},{34,3},{35,35},{4,4},{5,3... | collective-permute-start | bytes 884744 | tf_op jit(solution)/shard_map/ppermute | solution.py:245
  130.8 4.1 %collective-permute-done.28.refs_1_ = bf16[176,512]{1,0:T(8,128)(2,1)S(1)} collective-permute-done((bf16[176,512]{1,0:T(8,128)(2,1)S(1)}, bf16[176,512]{1,0:T(8,128)(2,1)S(1)}, u32[]{:S(2)}, u32[]{:S(2)}) %collective-permute-start.28) | collective-permute-done | bytes 180256 | tf_op jit(solution)/shard_map/ppermute | solution.py:230
  134.9 0.9 collective-permute-done.29.refs_2_
  135.8 3.4 %collective-permute-done.30.refs_3_ = bf16[176,512]{1,0:T(8,128)(2,1)S(1)} collective-permute-done((bf16[176,512]{1,0:T(8,128)(2,1)S(1)}, bf16[176,512]{1,0:T(8,128)(2,1)S(1)}, u32[]{:S(2)}, u32[]{:S(2)}) %collective-permute-start.30) | collective-permute-done | bytes 180256 | tf_op jit(solution)/shard_map/ppermute | solution.py:230
  139.3 1.7 %shard_map.90 = (bf16[128,512]{1,0:T(8,128)(2,1)}, bf16[128,512]{1,0:T(8,128)(2,1)}, f32[8,128]{1,0:T(8,128)S(1)}) custom-call(s32[5]{0:T(128)S(1)} %stack.23.place, f32[4,128]{1,0:T(4,128)S(1)} %pad_maximum_fusion.2.small, bf16[320,128]{1,0:T(8,128)(2,1)S(1)} %get-tuple-element.84.placing, bf16[176,512]{1,0:T(8,128)(2,1)S(1)} %get-tuple-element.88.refs_0_, ...), custom_call_target="tpu_custom_call" | custom-call | tf_op jit(solution)/shard_map/pallas_call | solution.py:33
  142.2 3.2 %collective-permute-done.24 = bf16[288,512]{1,0:T(8,128)(2,1)S(1)} collective-permute-done((bf16[288,512]{1,0:T(8,128)(2,1)S(1)}, bf16[288,512]{1,0:T(8,128)(2,1)S(1)}, u32[]{:S(2)}, u32[]{:S(2)}) %collective-permute-start.24) | collective-permute-done | bytes 294944 | tf_op jit(solution)/shard_map/ppermute | solution.py:245
  145.4 1.2 convert.2
  (51 shorter events, 7.9 us)
Async XLA Ops:
  0.6 18.2 %copy-start.5 = (bf16[1,3,192,512]{3,2,1,0:T(8,128)(2,1)S(1)}, bf16[1,3,192,512]{3,2,1,0:T(8,128)(2,1)}, u32[]{:S(2)}) copy-start(bf16[1,3,192,512]{3,2,1,0:T(8,128)(2,1)} %param.8) | copy-start | bytes 1769476
  0.6 18.2 %collective-permute-start.3 = (bf16[3,192,512]{2,1,0:T(8,128)(2,1)}, bf16[3,192,512]{2,1,0:T(8,128)(2,1)S(1)}, u32[]{:S(2)}, u32[]{:S(2)}) collective-permute-start(bf16[3,192,512]{2,1,0:T(8,128)(2,1)} %bitcast.21), channel_id=1, source_target_pairs={{1,32},{32,1},{3,34},{34,3},{5,36},{36,5},{7,38},{38,7},{9,40},{40... | collective-permute-start | bytes 1769480 | tf_op jit(solution)/shard_map/ppermute | solution.py:270
  9.2 19.6 %collective-permute-start = (bf16[160,512]{1,0:T(8,128)(2,1)S(1)}, bf16[160,512]{1,0:T(8,128)(2,1)S(1)}, u32[]{:S(2)}, u32[]{:S(2)}) collective-permute-start(bf16[160,512]{1,0:T(8,128)(2,1)S(1)} %get-tuple-element.52), channel_id=1, source_target_pairs={{0,8},{8,16},{16,24},{24,0},{1,9},{9,17},{17,25},{25,1},{2,10},{10... | collective-permute-start | bytes 491528 | tf_op jit(solution)/shard_map/ppermute | solution.py:230
  12.2 19.3 %collective-permute-start.1 = (bf16[160,512]{1,0:T(8,128)(2,1)S(1)}, bf16[160,512]{1,0:T(8,128)(2,1)S(1)}, u32[]{:S(2)}, u32[]{:S(2)}) collective-permute-start(bf16[160,512]{1,0:T(8,128)(2,1)S(1)} %get-tuple-element.53), channel_id=1, source_target_pairs={{0,16},{8,24},{16,0},{24,8},{1,17},{9,25},{17,1},{25,9},{2,18},{10... | collective-permute-start | bytes 491528 | tf_op jit(solution)/shard_map/ppermute | solution.py:230
  16.5 15.1 %collective-permute-start.2 = (bf16[160,512]{1,0:T(8,128)(2,1)S(1)}, bf16[160,512]{1,0:T(8,128)(2,1)S(1)}, u32[]{:S(2)}, u32[]{:S(2)}) collective-permute-start(bf16[160,512]{1,0:T(8,128)(2,1)S(1)} %get-tuple-element.54), channel_id=1, source_target_pairs={{0,24},{8,0},{16,8},{24,16},{1,25},{9,1},{17,9},{25,17},{2,26},{10... | collective-permute-start | bytes 491528 | tf_op jit(solution)/shard_map/ppermute | solution.py:230
  18.9 16.8 %collective-permute-start.4 = (bf16[3,192,512]{2,1,0:T(8,128)(2,1)S(1)}, bf16[3,192,512]{2,1,0:T(8,128)(2,1)S(1)}, u32[]{:S(2)}, u32[]{:S(2)}) collective-permute-start(bf16[3,192,512]{2,1,0:T(8,128)(2,1)S(1)} %broadcast_select_fusion.refs_4_), channel_id=1, source_target_pairs={{0,64},{64,128},{128,192},{192,0},{32,224},{96,32},{160,96},{224,1... | collective-permute-start | bytes 1769480 | tf_op jit(solution)/shard_map/ppermute | solution.py:236
  31.6 17.2 %collective-permute-start.7 = (bf16[640,512]{1,0:T(8,128)(2,1)S(1)}, bf16[640,512]{1,0:T(8,128)(2,1)S(1)}, u32[]{:S(2)}, u32[]{:S(2)}) collective-permute-start(bf16[640,512]{1,0:T(8,128)(2,1)S(1)} %constant_dynamic-update-slice_fusion.refs_0_), channel_id=1, source_target_pairs={{0,6},{2,0},{4,2},{6,4},{32,34},{34,36},{36,38},{38,32},{1,7},{3,1... | collective-permute-start | bytes 1966088 | tf_op jit(solution)/shard_map/ppermute | solution.py:237
  33.0 15.8 %collective-permute-start.6 = (bf16[640,512]{1,0:T(8,128)(2,1)S(1)}, bf16[640,512]{1,0:T(8,128)(2,1)S(1)}, u32[]{:S(2)}, u32[]{:S(2)}) collective-permute-start(bf16[640,512]{1,0:T(8,128)(2,1)S(1)} %constant_dynamic-update-slice_fusion.refs_0_), channel_id=1, source_target_pairs={{0,2},{2,4},{4,6},{6,0},{32,38},{34,32},{36,34},{38,36},{1,3},{3,5... | collective-permute-start | bytes 1966088 | tf_op jit(solution)/shard_map/ppermute | solution.py:237
  34.5 15.6 %collective-permute-start.5 = (bf16[3,192,512]{2,1,0:T(8,128)(2,1)S(1)}, bf16[3,192,512]{2,1,0:T(8,128)(2,1)S(1)}, u32[]{:S(2)}, u32[]{:S(2)}) collective-permute-start(bf16[3,192,512]{2,1,0:T(8,128)(2,1)S(1)} %broadcast_select_fusion.refs_4_), channel_id=1, source_target_pairs={{0,192},{64,0},{128,64},{192,128},{32,96},{96,160},{160,224},{224,... | collective-permute-start | bytes 1769480 | tf_op jit(solution)/shard_map/ppermute | solution.py:236
  35.7 15.1 %collective-permute-start.9 = (bf16[3,192,512]{2,1,0:T(8,128)(2,1)S(1)}, bf16[3,192,512]{2,1,0:T(8,128)(2,1)S(1)}, u32[]{:S(2)}, u32[]{:S(2)}) collective-permute-start(bf16[3,192,512]{2,1,0:T(8,128)(2,1)S(1)} %collective-permute-done.4.refs_5_), channel_id=1, source_target_pairs={{0,64},{64,128},{128,192},{192,0},{32,224},{96,32},{160,96},{224,1... | collective-permute-start | bytes 1769480 | tf_op jit(solution)/shard_map/ppermute | solution.py:236
  48.8 11.1 %copy-start.3 = (bf16[640,512]{1,0:T(8,128)(2,1)}, bf16[640,512]{1,0:T(8,128)(2,1)S(1)}, u32[]{:S(2)}) copy-start(bf16[640,512]{1,0:T(8,128)(2,1)S(1)} %collective-permute-done.7.refs_3_) | copy-start | bytes 1966084
  48.8 11.1 %copy-start = (bf16[640,512]{1,0:T(8,128)(2,1)}, bf16[640,512]{1,0:T(8,128)(2,1)S(1)}, u32[]{:S(2)}) copy-start(bf16[640,512]{1,0:T(8,128)(2,1)S(1)} %collective-permute-done.6.refs_1_) | copy-start | bytes 1966084
  50.2 9.7 %collective-permute-start.8 = (bf16[640,512]{1,0:T(8,128)(2,1)S(1)}, bf16[640,512]{1,0:T(8,128)(2,1)S(1)}, u32[]{:S(2)}, u32[]{:S(2)}) collective-permute-start(bf16[640,512]{1,0:T(8,128)(2,1)S(1)} %collective-permute-done.6.refs_1_), channel_id=1, source_target_pairs={{0,2},{2,4},{4,6},{6,0},{32,38},{34,32},{36,34},{38,36},{1,3},{3,5... | collective-permute-start | bytes 1966088 | tf_op jit(solution)/shard_map/ppermute | solution.py:237
  50.4 2.0 %collective-permute-start.10 = (bf16[3,192,512]{2,1,0:T(8,128)(2,1)S(1)}, bf16[3,192,512]{2,1,0:T(8,128)(2,1)S(1)}, u32[]{:S(2)}, u32[]{:S(2)}) collective-permute-start(bf16[3,192,512]{2,1,0:T(8,128)(2,1)S(1)} %broadcast_select_fusion.refs_4_), channel_id=1, source_target_pairs={{0,32},{32,0},{1,33},{33,1},{2,34},{34,2},{3,35},{35,3},{4,36},{36... | collective-permute-start | bytes 1769480 | tf_op jit(solution)/shard_map/ppermute | solution.py:241
  50.4 2.8 %collective-permute-start.13 = (bf16[3,192,512]{2,1,0:T(8,128)(2,1)S(1)}, bf16[3,192,512]{2,1,0:T(8,128)(2,1)S(1)}, u32[]{:S(2)}, u32[]{:S(2)}) collective-permute-start(bf16[3,192,512]{2,1,0:T(8,128)(2,1)S(1)} %collective-permute-done.4.refs_5_), channel_id=1, source_target_pairs={{0,32},{32,0},{1,33},{33,1},{2,34},{34,2},{3,35},{35,3},{4,36},{36... | collective-permute-start | bytes 1769480 | tf_op jit(solution)/shard_map/ppermute | solution.py:241
  50.9 3.2 %collective-permute-start.11 = (bf16[3,192,512]{2,1,0:T(8,128)(2,1)S(1)}, bf16[3,192,512]{2,1,0:T(8,128)(2,1)S(1)}, u32[]{:S(2)}, u32[]{:S(2)}) collective-permute-start(bf16[3,192,512]{2,1,0:T(8,128)(2,1)S(1)} %collective-permute-done.5.refs_7_), channel_id=1, source_target_pairs={{0,32},{32,0},{1,33},{33,1},{2,34},{34,2},{3,35},{35,3},{4,36},{36... | collective-permute-start | bytes 1769480 | tf_op jit(solution)/shard_map/ppermute | solution.py:241
  50.9 9.0 %collective-permute-start.12 = (bf16[3,192,512]{2,1,0:T(8,128)(2,1)S(1)}, bf16[3,192,512]{2,1,0:T(8,128)(2,1)S(1)}, u32[]{:S(2)}, u32[]{:S(2)}) collective-permute-start(bf16[3,192,512]{2,1,0:T(8,128)(2,1)S(1)} %collective-permute-done.9.refs_6_), channel_id=1, source_target_pairs={{0,32},{32,0},{1,33},{33,1},{2,34},{34,2},{3,35},{35,3},{4,36},{36... | collective-permute-start | bytes 1769480 | tf_op jit(solution)/shard_map/ppermute | solution.py:241
  59.9 0.9 copy-start.4
  64.5 16.2 %collective-permute-start.14 = (bf16[320,768]{1,0:T(8,128)(2,1)S(1)}, bf16[320,768]{1,0:T(8,128)(2,1)S(1)}, u32[]{:S(2)}, u32[]{:S(2)}) collective-permute-start(bf16[320,768]{1,0:T(8,128)(2,1)S(1)} %get-tuple-element.60.pair), channel_id=1, source_target_pairs={{0,1},{1,0},{2,3},{3,2},{4,5},{5,4},{6,7},{7,6},{8,9},{9,8},{10,11... | collective-permute-start | bytes 1474568 | tf_op jit(solution)/shard_map/ppermute | solution.py:241
  67.9 12.8 %collective-permute-start.15 = (bf16[320,384]{1,0:T(8,128)(2,1)S(1)}, bf16[320,384]{1,0:T(8,128)(2,1)S(1)}, u32[]{:S(2)}, u32[]{:S(2)}) collective-permute-start(bf16[320,384]{1,0:T(8,128)(2,1)S(1)} %get-tuple-element.61.down), channel_id=1, source_target_pairs={{0,1},{1,0},{2,3},{3,2},{4,5},{5,4},{6,7},{7,6},{8,9},{9,8},{10,11... | collective-permute-start | bytes 737288 | tf_op jit(solution)/shard_map/ppermute | solution.py:241
  80.7 7.7 %copy-start.1 = (bf16[640,512]{1,0:T(8,128)(2,1)S(1)}, bf16[640,512]{1,0:T(8,128)(2,1)}, u32[]{:S(2)}) copy-start(bf16[640,512]{1,0:T(8,128)(2,1)} %copy-done) | copy-start | bytes 1966084
  85.3 0.9 copy-start.2
  86.1 10.0 %collective-permute-start.16 = (bf16[656,512]{1,0:T(8,128)(2,1)S(1)}, bf16[656,512]{1,0:T(8,128)(2,1)S(1)}, u32[]{:S(2)}, u32[]{:S(2)}) collective-permute-start(bf16[656,512]{1,0:T(8,128)(2,1)S(1)} %get-tuple-element.66), channel_id=1, source_target_pairs={{0,2},{2,4},{4,6},{6,0},{32,38},{34,32},{36,34},{38,36},{1,3},{3,5... | collective-permute-start | bytes 2015240 | tf_op jit(solution)/shard_map/ppermute | solution.py:237
  92.8 3.6 %collective-permute-start.17 = (bf16[3,192,512]{2,1,0:T(8,128)(2,1)S(1)}, bf16[3,192,512]{2,1,0:T(8,128)(2,1)S(1)}, u32[]{:S(2)}, u32[]{:S(2)}) collective-permute-start(bf16[3,192,512]{2,1,0:T(8,128)(2,1)S(1)} %get-tuple-element.71), channel_id=1, source_target_pairs={{0,32},{32,0},{1,33},{33,1},{2,34},{34,2},{3,35},{35,3},{4,36},{36... | collective-permute-start | bytes 1769480 | tf_op jit(solution)/shard_map/ppermute | solution.py:241
  93.5 2.9 %collective-permute-start.18 = (bf16[3,192,512]{2,1,0:T(8,128)(2,1)S(1)}, bf16[3,192,512]{2,1,0:T(8,128)(2,1)S(1)}, u32[]{:S(2)}, u32[]{:S(2)}) collective-permute-start(bf16[3,192,512]{2,1,0:T(8,128)(2,1)S(1)} %get-tuple-element.72), channel_id=1, source_target_pairs={{0,32},{32,0},{1,33},{33,1},{2,34},{34,2},{3,35},{35,3},{4,36},{36... | collective-permute-start | bytes 1769480 | tf_op jit(solution)/shard_map/ppermute | solution.py:241
  93.6 3.2 %collective-permute-start.19 = (bf16[3,192,512]{2,1,0:T(8,128)(2,1)S(1)}, bf16[3,192,512]{2,1,0:T(8,128)(2,1)S(1)}, u32[]{:S(2)}, u32[]{:S(2)}) collective-permute-start(bf16[3,192,512]{2,1,0:T(8,128)(2,1)S(1)} %get-tuple-element.73), channel_id=1, source_target_pairs={{0,32},{32,0},{1,33},{33,1},{2,34},{34,2},{3,35},{35,3},{4,36},{36... | collective-permute-start | bytes 1769480 | tf_op jit(solution)/shard_map/ppermute | solution.py:241
  94.0 3.7 %collective-permute-start.20 = (bf16[3,192,512]{2,1,0:T(8,128)(2,1)S(1)}, bf16[3,192,512]{2,1,0:T(8,128)(2,1)S(1)}, u32[]{:S(2)}, u32[]{:S(2)}) collective-permute-start(bf16[3,192,512]{2,1,0:T(8,128)(2,1)S(1)} %get-tuple-element.74), channel_id=1, source_target_pairs={{0,32},{32,0},{1,33},{33,1},{2,34},{34,2},{3,35},{35,3},{4,36},{36... | collective-permute-start | bytes 1769480 | tf_op jit(solution)/shard_map/ppermute | solution.py:241
  97.8 9.1 %collective-permute-start.21 = (bf16[3,192,512]{2,1,0:T(8,128)(2,1)S(1)}, bf16[3,192,512]{2,1,0:T(8,128)(2,1)S(1)}, u32[]{:S(2)}, u32[]{:S(2)}) collective-permute-start(bf16[3,192,512]{2,1,0:T(8,128)(2,1)S(1)} %add_convert_fusion.3), channel_id=1, source_target_pairs={{0,64},{64,128},{128,192},{192,0},{32,224},{96,32},{160,96},{224,1... | collective-permute-start | bytes 1769480 | tf_op jit(solution)/shard_map/ppermute | solution.py:236
  100.0 14.7 %collective-permute-start.26 = (bf16[656,512]{1,0:T(8,128)(2,1)S(1)}, bf16[656,512]{1,0:T(8,128)(2,1)S(1)}, u32[]{:S(2)}, u32[]{:S(2)}) collective-permute-start(bf16[656,512]{1,0:T(8,128)(2,1)S(1)} %get-tuple-element.86), channel_id=1, source_target_pairs={{0,6},{2,0},{4,2},{6,4},{32,34},{34,36},{36,38},{38,32},{1,7},{3,1... | collective-permute-start | bytes 2015240 | tf_op jit(solution)/shard_map/ppermute | solution.py:237
  100.4 17.2 %collective-permute-start.27 = (bf16[656,512]{1,0:T(8,128)(2,1)S(1)}, bf16[656,512]{1,0:T(8,128)(2,1)S(1)}, u32[]{:S(2)}, u32[]{:S(2)}) collective-permute-start(bf16[656,512]{1,0:T(8,128)(2,1)S(1)} %add_convert_fusion), channel_id=1, source_target_pairs={{0,2},{2,4},{4,6},{6,0},{32,38},{34,32},{36,34},{38,36},{1,3},{3,5... | collective-permute-start | bytes 2015240 | tf_op jit(solution)/shard_map/ppermute | solution.py:237
  106.9 16.2 %collective-permute-start.22 = (bf16[3,192,512]{2,1,0:T(8,128)(2,1)S(1)}, bf16[3,192,512]{2,1,0:T(8,128)(2,1)S(1)}, u32[]{:S(2)}, u32[]{:S(2)}) collective-permute-start(bf16[3,192,512]{2,1,0:T(8,128)(2,1)S(1)} %convert_add_fusion), channel_id=1, source_target_pairs={{0,192},{64,0},{128,64},{192,128},{32,96},{96,160},{160,224},{224,... | collective-permute-start | bytes 1769480 | tf_op jit(solution)/shard_map/ppermute | solution.py:236
  109.8 13.3 %collective-permute-start.23 = (bf16[3,192,512]{2,1,0:T(8,128)(2,1)S(1)}, bf16[3,192,512]{2,1,0:T(8,128)(2,1)S(1)}, u32[]{:S(2)}, u32[]{:S(2)}) collective-permute-start(bf16[3,192,512]{2,1,0:T(8,128)(2,1)S(1)} %add_convert_fusion.2), channel_id=1, source_target_pairs={{0,64},{64,128},{128,192},{192,0},{32,224},{96,32},{160,96},{224,1... | collective-permute-start | bytes 1769480 | tf_op jit(solution)/shard_map/ppermute | solution.py:236
  118.4 16.5 %collective-permute-start.28 = (bf16[176,512]{1,0:T(8,128)(2,1)S(1)}, bf16[176,512]{1,0:T(8,128)(2,1)S(1)}, u32[]{:S(2)}, u32[]{:S(2)}) collective-permute-start(bf16[176,512]{1,0:T(8,128)(2,1)S(1)} %get-tuple-element.89), channel_id=1, source_target_pairs={{0,24},{8,0},{16,8},{24,16},{1,25},{9,1},{17,9},{25,17},{2,26},{10... | collective-permute-start | bytes 540680 | tf_op jit(solution)/shard_map/ppermute | solution.py:230
  120.9 14.9 %collective-permute-start.29 = (bf16[176,512]{1,0:T(8,128)(2,1)S(1)}, bf16[176,512]{1,0:T(8,128)(2,1)S(1)}, u32[]{:S(2)}, u32[]{:S(2)}) collective-permute-start(bf16[176,512]{1,0:T(8,128)(2,1)S(1)} %get-tuple-element.90), channel_id=1, source_target_pairs={{0,16},{8,24},{16,0},{24,8},{1,17},{9,25},{17,1},{25,9},{2,18},{10... | collective-permute-start | bytes 540680 | tf_op jit(solution)/shard_map/ppermute | solution.py:230
  123.0 16.3 %collective-permute-start.30 = (bf16[176,512]{1,0:T(8,128)(2,1)S(1)}, bf16[176,512]{1,0:T(8,128)(2,1)S(1)}, u32[]{:S(2)}, u32[]{:S(2)}) collective-permute-start(bf16[176,512]{1,0:T(8,128)(2,1)S(1)} %get-tuple-element.91), channel_id=1, source_target_pairs={{0,8},{8,16},{16,24},{24,0},{1,9},{9,17},{17,25},{25,1},{2,10},{10... | collective-permute-start | bytes 540680 | tf_op jit(solution)/shard_map/ppermute | solution.py:230
  123.5 18.7 %collective-permute-start.25 = (bf16[288,512]{1,0:T(8,128)(2,1)S(1)}, bf16[288,512]{1,0:T(8,128)(2,1)S(1)}, u32[]{:S(2)}, u32[]{:S(2)}) collective-permute-start(bf16[288,512]{1,0:T(8,128)(2,1)S(1)} %get-tuple-element.98), channel_id=1, source_target_pairs={{0,0},{1,32},{32,1},{33,33},{2,2},{3,34},{34,3},{35,35},{4,4},{5,3... | collective-permute-start | bytes 884744 | tf_op jit(solution)/shard_map/ppermute | solution.py:245
  128.9 16.4 %collective-permute-start.24 = (bf16[288,512]{1,0:T(8,128)(2,1)S(1)}, bf16[288,512]{1,0:T(8,128)(2,1)S(1)}, u32[]{:S(2)}, u32[]{:S(2)}) collective-permute-start(bf16[288,512]{1,0:T(8,128)(2,1)S(1)} %get-tuple-element.99), channel_id=1, source_target_pairs={{0,0},{1,32},{32,1},{33,33},{2,2},{3,34},{34,3},{35,35},{4,4},{5,3... | collective-permute-start | bytes 884744 | tf_op jit(solution)/shard_map/ppermute | solution.py:245

commit v16 on v14

--- a/solution.py
+++ b/solution.py
@@ -326,7 +326,8 @@
         return keeps[i].astype(F32) + moved[i].astype(F32)
 
     passed = relay(both_cores(2).astype(BF16), "x")
-    near, back = halfway(passed, both_cores(1), both_cores(3))
+    near = both_cores(1).astype(BF16)
+    back = (both_cores(3) + passed.astype(F32)).astype(BF16)
     far_sums = [relay(near, "x", -1), relay(back, "x")]
     totals = call(total_kernel, place, [shares[0]] + arrived, [((unit, width), BF16)] * 4)
     returned = [totals[0]] + [shift(totals[k], "expert", -k) for k in (1, 2, 3)]

time: 146 us -> 146 us (level)
  starting transfers between devices: 50 us -> 52.5 us
  waiting for transfers between devices: 68.2 us -> 65.7 us
    ppermute x2, waiting for transfers between devices: 5.09 us -> 0.39 us  [turn(): lax.ppermute(value, ('core', 'zl'), [(2 * c + z, 2 * z + c) for c in rang...]
    ppermute x2, starting transfers between devices: 7.06 us -> 10.7 us  [turn(): lax.ppermute(value, ('core', 'zl'), [(2 * c + z, 2 * z + c) for c in rang...]
    ppermute x6, waiting for transfers between devices: 5.72 us -> 8.4 us  [relay(): lax.ppermute(value, ('x', 'core'), [(2 * i + c, 2 * j + c) for c, i, j in...]
    ppermute x6, waiting for transfers between devices: 21.9 us -> 19.8 us  [relay(): lax.ppermute(value, ('core', axis), [(4 * c + i, 4 * c + j) for c, i, j i...]
    ppermute x6, waiting for transfers between devices: 14.5 us -> 16.1 us  [shift(): return lax.ppermute(value, axis, [(i, (i + step) % 4) for i in range(4)])]
  transfers between devices with their start and end apart: 31 -> 31, of which waited for: 17 -> 16; matrix products, arithmetic and copies ran while one was open for 1% -> 1% of each run, Pallas kernels for 7% -> 7%
where the time goes in v16:
time: 146 us; the launch traced here: 145 us
  waiting for transfers between devices  65.7 us (45%)
  starting transfers between devices  52.5 us (36%)
  Pallas kernels  19.1 us (13%)
  other arithmetic  4.77 us (3%)
  local copies, waits for them, and re-layouts  2.45 us (2%)
    ppermute x6, waiting for transfers between devices, relay(): lax.ppermute(value, ('core', axis), [(4 * c + i, 4 * c + j) for c, i, j i...  19.8 us
    pallas_call x7, Pallas kernels, call(): pl.pallas_call(kernel, out_shape=[jax.ShapeDtypeStruct(shape, kind) for s...  19.1 us
    ppermute x6, waiting for transfers between devices, shift(): return lax.ppermute(value, axis, [(i, (i + step) % 4) for i in range(4)])  16.1 us
    ppermute x10, waiting for transfers between devices, swap(): return lax.ppermute(value, axis, [(0, 1), (1, 0)])  14.8 us
    ppermute x6, starting transfers between devices, shift(): return lax.ppermute(value, axis, [(i, (i + step) % 4) for i in range(4)])  13.1 us
    ppermute x6, starting transfers between devices, relay(): lax.ppermute(value, ('x', 'core'), [(2 * i + c, 2 * j + c) for c, i, j in...  11.4 us
    ppermute x2, starting transfers between devices, turn(): lax.ppermute(value, ('core', 'zl'), [(2 * c + z, 2 * z + c) for c in rang...  10.7 us
    ppermute x6, starting transfers between devices, relay(): lax.ppermute(value, ('core', axis), [(4 * c + i, 4 * c + j) for c, i, j i...  8.41 us
  transfers between devices with their start and end apart: 31, of which 16 were waited for; matrix products, arithmetic and copies ran while one was open for 1% of the time, Pallas kernels for 7%

profile of v16, /device:TPU:1, one launch (start us, length us, event | category | flops | bytes accessed | tf_op | source)
XLA Modules:
  0.0 145.4 jit_solution(1271709560649504425)
XLA Ops:
  0.7 0.7 convert_bitcast_fusion
  1.4 0.7 pad_maximum_fusion.2.small
  2.1 1.0 pad_maximum_fusion.1.wide
  3.2 1.0 shard_map.84
  4.2 4.9 %collective-permute-start.3 = (bf16[3,192,512]{2,1,0:T(8,128)(2,1)}, bf16[3,192,512]{2,1,0:T(8,128)(2,1)S(1)}, u32[]{:S(2)}, u32[]{:S(2)}) collective-permute-start(bf16[3,192,512]{2,1,0:T(8,128)(2,1)} %bitcast.20), channel_id=1, source_target_pairs={{1,32},{32,1},{3,34},{34,3},{5,36},{36,5},{7,38},{38,7},{9,40},{40... | collective-permute-start | bytes 1769480 | tf_op jit(solution)/shard_map/ppermute | solution.py:270
  9.1 3.1 %collective-permute-start = (bf16[160,512]{1,0:T(8,128)(2,1)S(1)}, bf16[160,512]{1,0:T(8,128)(2,1)S(1)}, u32[]{:S(2)}, u32[]{:S(2)}) collective-permute-start(bf16[160,512]{1,0:T(8,128)(2,1)S(1)} %get-tuple-element.53), channel_id=1, source_target_pairs={{0,8},{8,16},{16,24},{24,0},{1,9},{9,17},{17,25},{25,1},{2,10},{10... | collective-permute-start | bytes 491528 | tf_op jit(solution)/shard_map/ppermute | solution.py:230
  12.2 4.2 %collective-permute-start.1 = (bf16[160,512]{1,0:T(8,128)(2,1)S(1)}, bf16[160,512]{1,0:T(8,128)(2,1)S(1)}, u32[]{:S(2)}, u32[]{:S(2)}) collective-permute-start(bf16[160,512]{1,0:T(8,128)(2,1)S(1)} %get-tuple-element.54), channel_id=1, source_target_pairs={{0,16},{8,24},{16,0},{24,8},{1,17},{9,25},{17,1},{25,9},{2,18},{10... | collective-permute-start | bytes 491528 | tf_op jit(solution)/shard_map/ppermute | solution.py:230
  16.4 2.4 %collective-permute-start.2 = (bf16[160,512]{1,0:T(8,128)(2,1)S(1)}, bf16[160,512]{1,0:T(8,128)(2,1)S(1)}, u32[]{:S(2)}, u32[]{:S(2)}) collective-permute-start(bf16[160,512]{1,0:T(8,128)(2,1)S(1)} %get-tuple-element.55), channel_id=1, source_target_pairs={{0,24},{8,0},{16,8},{24,16},{1,25},{9,1},{17,9},{25,17},{2,26},{10... | collective-permute-start | bytes 491528 | tf_op jit(solution)/shard_map/ppermute | solution.py:230
  18.8 6.2 %collective-permute-done.3 = bf16[3,192,512]{2,1,0:T(8,128)(2,1)S(1)} collective-permute-done((bf16[3,192,512]{2,1,0:T(8,128)(2,1)}, bf16[3,192,512]{2,1,0:T(8,128)(2,1)S(1)}, u32[]{:S(2)}, u32[]{:S(2)}) %collective-permute-start.3) | collective-permute-done | bytes 589856 | tf_op jit(solution)/shard_map/ppermute | solution.py:270
  25.1 2.6 %collective-permute-start.4 = (bf16[3,192,512]{2,1,0:T(8,128)(2,1)S(1)}, bf16[3,192,512]{2,1,0:T(8,128)(2,1)S(1)}, u32[]{:S(2)}, u32[]{:S(2)}) collective-permute-start(bf16[3,192,512]{2,1,0:T(8,128)(2,1)S(1)} %broadcast_select_fusion.refs_4_), channel_id=1, source_target_pairs={{0,64},{64,128},{128,192},{192,0},{32,224},{96,32},{160,96},{224,1... | collective-permute-start | bytes 1769480 | tf_op jit(solution)/shard_map/ppermute | solution.py:236
  27.6 2.8 %collective-permute-done = bf16[160,512]{1,0:T(8,128)(2,1)S(1)} collective-permute-done((bf16[160,512]{1,0:T(8,128)(2,1)S(1)}, bf16[160,512]{1,0:T(8,128)(2,1)S(1)}, u32[]{:S(2)}, u32[]{:S(2)}) %collective-permute-start) | collective-permute-done | bytes 163872 | tf_op jit(solution)/shard_map/ppermute | solution.py:230
  30.5 5.9 %collective-permute-done.1 = bf16[160,512]{1,0:T(8,128)(2,1)S(1)} collective-permute-done((bf16[160,512]{1,0:T(8,128)(2,1)S(1)}, bf16[160,512]{1,0:T(8,128)(2,1)S(1)}, u32[]{:S(2)}, u32[]{:S(2)}) %collective-permute-start.1) | collective-permute-done | bytes 163872 | tf_op jit(solution)/shard_map/ppermute | solution.py:230
  36.4 1.4 collective-permute-start.7
  37.7 1.5 %collective-permute-start.6 = (bf16[640,512]{1,0:T(8,128)(2,1)S(1)}, bf16[640,512]{1,0:T(8,128)(2,1)S(1)}, u32[]{:S(2)}, u32[]{:S(2)}) collective-permute-start(bf16[640,512]{1,0:T(8,128)(2,1)S(1)} %constant_dynamic-update-slice_fusion.refs_0_), channel_id=1, source_target_pairs={{0,2},{2,4},{4,6},{6,0},{32,38},{34,32},{36,34},{38,36},{1,3},{3,5... | collective-permute-start | bytes 1966088 | tf_op jit(solution)/shard_map/ppermute | solution.py:237
  39.3 1.2 collective-permute-start.5
  40.5 1.5 %collective-permute-start.9 = (bf16[3,192,512]{2,1,0:T(8,128)(2,1)S(1)}, bf16[3,192,512]{2,1,0:T(8,128)(2,1)S(1)}, u32[]{:S(2)}, u32[]{:S(2)}) collective-permute-start(bf16[3,192,512]{2,1,0:T(8,128)(2,1)S(1)} %collective-permute-done.4.refs_5_), channel_id=1, source_target_pairs={{0,64},{64,128},{128,192},{192,0},{32,224},{96,32},{160,96},{224,1... | collective-permute-start | bytes 1769480 | tf_op jit(solution)/shard_map/ppermute | solution.py:236
  42.0 7.7 %collective-permute-done.7.refs_3_ = bf16[640,512]{1,0:T(8,128)(2,1)S(1)} collective-permute-done((bf16[640,512]{1,0:T(8,128)(2,1)S(1)}, bf16[640,512]{1,0:T(8,128)(2,1)S(1)}, u32[]{:S(2)}, u32[]{:S(2)}) %collective-permute-start.7) | collective-permute-done | bytes 655392 | tf_op jit(solution)/shard_map/ppermute | solution.py:237
  49.7 1.6 %collective-permute-done.5.refs_7_ = bf16[3,192,512]{2,1,0:T(8,128)(2,1)S(1)} collective-permute-done((bf16[3,192,512]{2,1,0:T(8,128)(2,1)S(1)}, bf16[3,192,512]{2,1,0:T(8,128)(2,1)S(1)}, u32[]{:S(2)}, u32[]{:S(2)}) %collective-permute-start.5) | collective-permute-done | bytes 589856 | tf_op jit(solution)/shard_map/ppermute | solution.py:236
  51.3 2.7 %collective-permute-start.8 = (bf16[640,512]{1,0:T(8,128)(2,1)S(1)}, bf16[640,512]{1,0:T(8,128)(2,1)S(1)}, u32[]{:S(2)}, u32[]{:S(2)}) collective-permute-start(bf16[640,512]{1,0:T(8,128)(2,1)S(1)} %collective-permute-done.6.refs_1_), channel_id=1, source_target_pairs={{0,2},{2,4},{4,6},{6,0},{32,38},{34,32},{36,34},{38,36},{1,3},{3,5... | collective-permute-start | bytes 1966088 | tf_op jit(solution)/shard_map/ppermute | solution.py:237
  54.5 0.5 collective-permute-start.12
  55.0 1.0 collective-permute-done.10.refs_8_
  56.0 0.8 collective-permute-done.13.refs_11_
  56.8 0.8 collective-permute-done.11.refs_9_
  57.7 3.8 %collective-permute-done.8.refs_2_ = bf16[640,512]{1,0:T(8,128)(2,1)S(1)} collective-permute-done((bf16[640,512]{1,0:T(8,128)(2,1)S(1)}, bf16[640,512]{1,0:T(8,128)(2,1)S(1)}, u32[]{:S(2)}, u32[]{:S(2)}) %collective-permute-start.8) | collective-permute-done | bytes 655392 | tf_op jit(solution)/shard_map/ppermute | solution.py:237
  61.5 0.8 copy-done.4
  62.4 3.8 %shard_map.85 = (bf16[320,768]{1,0:T(8,128)(2,1)S(1)}, bf16[768,2048]{1,0:T(8,128)(2,1)}) custom-call(s32[5]{0:T(128)S(1)} %stack.23.place, bf16[640,512]{1,0:T(8,128)(2,1)S(1)} %constant_dynamic-update-slice_fusion.refs_0_, bf16[640,512]{1,0:T(8,128)(2,1)} %copy-done, bf16[640,512]{1,0:T(8,128)(2,1)} %copy-done.4, bf16[640,512]{1,0:T(8,128)(2,1)} %copy-done.3, ...), custom_call_target="tpu_custom_call" | custom-call | tf_op jit(solution)/shard_map/pallas_call | solution.py:33
  66.4 3.1 %shard_map.86 = (bf16[320,384]{1,0:T(8,128)(2,1)S(1)}, bf16[384,2048]{1,0:T(8,128)(2,1)}) custom-call(s32[5]{0:T(128)S(1)} %stack.23.place, bf16[640,512]{1,0:T(8,128)(2,1)S(1)} %constant_dynamic-update-slice_fusion.refs_0_, bf16[640,512]{1,0:T(8,128)(2,1)} %copy-done, bf16[640,512]{1,0:T(8,128)(2,1)} %copy-done.4, bf16[640,512]{1,0:T(8,128)(2,1)} %copy-done.3, ...), custom_call_target="tpu_custom_call" | custom-call | tf_op jit(solution)/shard_map/pallas_call | solution.py:33
  69.5 1.5 %collective-permute-start.15 = (bf16[320,384]{1,0:T(8,128)(2,1)S(1)}, bf16[320,384]{1,0:T(8,128)(2,1)S(1)}, u32[]{:S(2)}, u32[]{:S(2)}) collective-permute-start(bf16[320,384]{1,0:T(8,128)(2,1)S(1)} %get-tuple-element.63.down), channel_id=1, source_target_pairs={{0,1},{1,0},{2,3},{3,2},{4,5},{5,4},{6,7},{7,6},{8,9},{9,8},{10,11... | collective-permute-start | bytes 737288 | tf_op jit(solution)/shard_map/ppermute | solution.py:241
  71.0 12.1 %collective-permute-done.15.down_far = bf16[320,384]{1,0:T(8,128)(2,1)S(1)} collective-permute-done((bf16[320,384]{1,0:T(8,128)(2,1)S(1)}, bf16[320,384]{1,0:T(8,128)(2,1)S(1)}, u32[]{:S(2)}, u32[]{:S(2)}) %collective-permute-start.15) | collective-permute-done | bytes 245792 | tf_op jit(solution)/shard_map/ppermute | solution.py:241
  83.2 4.5 %shard_map.87 = (f32[656,512]{1,0:T(8,128)S(1)}, bf16[656,512]{1,0:T(8,128)(2,1)S(1)}, bf16[656,512]{1,0:T(8,128)(2,1)S(1)}, bf16[656,512]{1,0:T(8,128)(2,1)S(1)}, bf16[320,1152]{1,0:T(8,128)(2,1)S(1)}) custom-call(s32[5]{0:T(128)S(1)} %stack.23.place, bf16[320,768]{1,0:T(8,128)(2,1)S(1)} %get-tuple-element.62.pair, ...), custom_call_target="tpu_custom_call" | custom-call | tf_op jit(solution)/shard_map/pallas_call | solution.py:33
  87.7 0.9 copy-done.2
  88.7 4.3 %shard_map.88 = (bf16[3,192,512]{2,1,0:T(8,128)(2,1)S(1)}, bf16[3,192,512]{2,1,0:T(8,128)(2,1)S(1)}, bf16[3,192,512]{2,1,0:T(8,128)(2,1)S(1)}, bf16[3,192,512]{2...) custom-call(s32[5]{0:T(128)S(1)} %stack.23.place, ...), custom_call_target="tpu_custom_call" | custom-call | tf_op jit(solution)/shard_map/pallas_call | solution.py:33
  94.1 4.4 %collective-permute-done.16 = bf16[656,512]{1,0:T(8,128)(2,1)S(1)} collective-permute-done((bf16[656,512]{1,0:T(8,128)(2,1)S(1)}, bf16[656,512]{1,0:T(8,128)(2,1)S(1)}, u32[]{:S(2)}, u32[]{:S(2)}) %collective-permute-start.16) | collective-permute-done | bytes 671776 | tf_op jit(solution)/shard_map/ppermute | solution.py:237
  98.9 2.4 %collective-permute-start.22 = (bf16[3,192,512]{2,1,0:T(8,128)(2,1)S(1)}, bf16[3,192,512]{2,1,0:T(8,128)(2,1)S(1)}, u32[]{:S(2)}, u32[]{:S(2)}) collective-permute-start(bf16[3,192,512]{2,1,0:T(8,128)(2,1)S(1)} %add_convert_fusion.3), channel_id=1, source_target_pairs={{0,64},{64,128},{128,192},{192,0},{32,224},{96,32},{160,96},{224,1... | collective-permute-start | bytes 1769480 | tf_op jit(solution)/shard_map/ppermute | solution.py:236
  101.6 2.7 %collective-permute-start.27 = (bf16[656,512]{1,0:T(8,128)(2,1)S(1)}, bf16[656,512]{1,0:T(8,128)(2,1)S(1)}, u32[]{:S(2)}, u32[]{:S(2)}) collective-permute-start(bf16[656,512]{1,0:T(8,128)(2,1)S(1)} %add_convert_fusion), channel_id=1, source_target_pairs={{0,2},{2,4},{4,6},{6,0},{32,38},{34,32},{36,34},{38,36},{1,3},{3,5... | collective-permute-start | bytes 2015240 | tf_op jit(solution)/shard_map/ppermute | solution.py:237
  104.3 6.7 %collective-permute-done.22 = bf16[3,192,512]{2,1,0:T(8,128)(2,1)S(1)} collective-permute-done((bf16[3,192,512]{2,1,0:T(8,128)(2,1)S(1)}, bf16[3,192,512]{2,1,0:T(8,128)(2,1)S(1)}, u32[]{:S(2)}, u32[]{:S(2)}) %collective-permute-start.22) | collective-permute-done | bytes 589856 | tf_op jit(solution)/shard_map/ppermute | solution.py:236
  111.3 3.7 %collective-permute-start.23 = (bf16[3,192,512]{2,1,0:T(8,128)(2,1)S(1)}, bf16[3,192,512]{2,1,0:T(8,128)(2,1)S(1)}, u32[]{:S(2)}, u32[]{:S(2)}) collective-permute-start(bf16[3,192,512]{2,1,0:T(8,128)(2,1)S(1)} %add_convert_fusion.2), channel_id=1, source_target_pairs={{0,64},{64,128},{128,192},{192,0},{32,224},{96,32},{160,96},{224,1... | collective-permute-start | bytes 1769480 | tf_op jit(solution)/shard_map/ppermute | solution.py:236
  115.0 1.6 %collective-permute-done.26.one = bf16[656,512]{1,0:T(8,128)(2,1)S(1)} collective-permute-done((bf16[656,512]{1,0:T(8,128)(2,1)S(1)}, bf16[656,512]{1,0:T(8,128)(2,1)S(1)}, u32[]{:S(2)}, u32[]{:S(2)}) %collective-permute-start.26) | collective-permute-done | bytes 671776 | tf_op jit(solution)/shard_map/ppermute | solution.py:237
  116.6 2.3 %collective-permute-done.27.three = bf16[656,512]{1,0:T(8,128)(2,1)S(1)} collective-permute-done((bf16[656,512]{1,0:T(8,128)(2,1)S(1)}, bf16[656,512]{1,0:T(8,128)(2,1)S(1)}, u32[]{:S(2)}, u32[]{:S(2)}) %collective-permute-start.27) | collective-permute-done | bytes 671776 | tf_op jit(solution)/shard_map/ppermute | solution.py:237
  118.8 0.8 shard_map.89
  119.6 1.1 collective-permute-start.28
  120.7 2.3 %collective-permute-start.30 = (bf16[176,512]{1,0:T(8,128)(2,1)S(1)}, bf16[176,512]{1,0:T(8,128)(2,1)S(1)}, u32[]{:S(2)}, u32[]{:S(2)}) collective-permute-start(bf16[176,512]{1,0:T(8,128)(2,1)S(1)} %get-tuple-element.91), channel_id=1, source_target_pairs={{0,8},{8,16},{16,24},{24,0},{1,9},{9,17},{17,25},{25,1},{2,10},{10... | collective-permute-start | bytes 540680 | tf_op jit(solution)/shard_map/ppermute | solution.py:230
  123.4 8.8 %collective-permute-start.25 = (bf16[288,512]{1,0:T(8,128)(2,1)S(1)}, bf16[288,512]{1,0:T(8,128)(2,1)S(1)}, u32[]{:S(2)}, u32[]{:S(2)}) collective-permute-start(bf16[288,512]{1,0:T(8,128)(2,1)S(1)} %get-tuple-element.98), channel_id=1, source_target_pairs={{0,0},{1,32},{32,1},{33,33},{2,2},{3,34},{34,3},{35,35},{4,4},{5,3... | collective-permute-start | bytes 884744 | tf_op jit(solution)/shard_map/ppermute | solution.py:245
  132.2 1.9 %collective-permute-start.24 = (bf16[288,512]{1,0:T(8,128)(2,1)S(1)}, bf16[288,512]{1,0:T(8,128)(2,1)S(1)}, u32[]{:S(2)}, u32[]{:S(2)}) collective-permute-start(bf16[288,512]{1,0:T(8,128)(2,1)S(1)} %get-tuple-element.99), channel_id=1, source_target_pairs={{0,0},{1,32},{32,1},{33,33},{2,2},{3,34},{34,3},{35,35},{4,4},{5,3... | collective-permute-start | bytes 884744 | tf_op jit(solution)/shard_map/ppermute | solution.py:245
  134.2 7.4 %collective-permute-done.30.refs_3_ = bf16[176,512]{1,0:T(8,128)(2,1)S(1)} collective-permute-done((bf16[176,512]{1,0:T(8,128)(2,1)S(1)}, bf16[176,512]{1,0:T(8,128)(2,1)S(1)}, u32[]{:S(2)}, u32[]{:S(2)}) %collective-permute-start.30) | collective-permute-done | bytes 180256 | tf_op jit(solution)/shard_map/ppermute | solution.py:230
  141.5 1.7 %shard_map.90 = (bf16[128,512]{1,0:T(8,128)(2,1)}, bf16[128,512]{1,0:T(8,128)(2,1)}, f32[8,128]{1,0:T(8,128)S(1)}) custom-call(s32[5]{0:T(128)S(1)} %stack.23.place, f32[4,128]{1,0:T(4,128)S(1)} %pad_maximum_fusion.2.small, bf16[320,128]{1,0:T(8,128)(2,1)S(1)} %get-tuple-element.84.placing, bf16[176,512]{1,0:T(8,128)(2,1)S(1)} %get-tuple-element.88.refs_0_, ...), custom_call_target="tpu_custom_call" | custom-call | tf_op jit(solution)/shard_map/pallas_call | solution.py:33
  143.2 0.6 slice_bitcast_fusion.2
  144.2 1.2 convert.2
  (51 shorter events, 4.0 us)
Async XLA Ops:
  0.6 24.4 %copy-start.5 = (bf16[1,3,192,512]{3,2,1,0:T(8,128)(2,1)S(1)}, bf16[1,3,192,512]{3,2,1,0:T(8,128)(2,1)}, u32[]{:S(2)}) copy-start(bf16[1,3,192,512]{3,2,1,0:T(8,128)(2,1)} %param.8) | copy-start | bytes 1769476
  4.2 20.8 %collective-permute-start.3 = (bf16[3,192,512]{2,1,0:T(8,128)(2,1)}, bf16[3,192,512]{2,1,0:T(8,128)(2,1)S(1)}, u32[]{:S(2)}, u32[]{:S(2)}) collective-permute-start(bf16[3,192,512]{2,1,0:T(8,128)(2,1)} %bitcast.20), channel_id=1, source_target_pairs={{1,32},{32,1},{3,34},{34,3},{5,36},{36,5},{7,38},{38,7},{9,40},{40... | collective-permute-start | bytes 1769480 | tf_op jit(solution)/shard_map/ppermute | solution.py:270
  9.1 21.4 %collective-permute-start = (bf16[160,512]{1,0:T(8,128)(2,1)S(1)}, bf16[160,512]{1,0:T(8,128)(2,1)S(1)}, u32[]{:S(2)}, u32[]{:S(2)}) collective-permute-start(bf16[160,512]{1,0:T(8,128)(2,1)S(1)} %get-tuple-element.53), channel_id=1, source_target_pairs={{0,8},{8,16},{16,24},{24,0},{1,9},{9,17},{17,25},{25,1},{2,10},{10... | collective-permute-start | bytes 491528 | tf_op jit(solution)/shard_map/ppermute | solution.py:230
  12.2 24.1 %collective-permute-start.1 = (bf16[160,512]{1,0:T(8,128)(2,1)S(1)}, bf16[160,512]{1,0:T(8,128)(2,1)S(1)}, u32[]{:S(2)}, u32[]{:S(2)}) collective-permute-start(bf16[160,512]{1,0:T(8,128)(2,1)S(1)} %get-tuple-element.54), channel_id=1, source_target_pairs={{0,16},{8,24},{16,0},{24,8},{1,17},{9,25},{17,1},{25,9},{2,18},{10... | collective-permute-start | bytes 491528 | tf_op jit(solution)/shard_map/ppermute | solution.py:230
  16.4 20.0 %collective-permute-start.2 = (bf16[160,512]{1,0:T(8,128)(2,1)S(1)}, bf16[160,512]{1,0:T(8,128)(2,1)S(1)}, u32[]{:S(2)}, u32[]{:S(2)}) collective-permute-start(bf16[160,512]{1,0:T(8,128)(2,1)S(1)} %get-tuple-element.55), channel_id=1, source_target_pairs={{0,24},{8,0},{16,8},{24,16},{1,25},{9,1},{17,9},{25,17},{2,26},{10... | collective-permute-start | bytes 491528 | tf_op jit(solution)/shard_map/ppermute | solution.py:230
  25.1 15.4 %collective-permute-start.4 = (bf16[3,192,512]{2,1,0:T(8,128)(2,1)S(1)}, bf16[3,192,512]{2,1,0:T(8,128)(2,1)S(1)}, u32[]{:S(2)}, u32[]{:S(2)}) collective-permute-start(bf16[3,192,512]{2,1,0:T(8,128)(2,1)S(1)} %broadcast_select_fusion.refs_4_), channel_id=1, source_target_pairs={{0,64},{64,128},{128,192},{192,0},{32,224},{96,32},{160,96},{224,1... | collective-permute-start | bytes 1769480 | tf_op jit(solution)/shard_map/ppermute | solution.py:236
  36.4 13.3 %collective-permute-start.7 = (bf16[640,512]{1,0:T(8,128)(2,1)S(1)}, bf16[640,512]{1,0:T(8,128)(2,1)S(1)}, u32[]{:S(2)}, u32[]{:S(2)}) collective-permute-start(bf16[640,512]{1,0:T(8,128)(2,1)S(1)} %constant_dynamic-update-slice_fusion.refs_0_), channel_id=1, source_target_pairs={{0,6},{2,0},{4,2},{6,4},{32,34},{34,36},{36,38},{38,32},{1,7},{3,1... | collective-permute-start | bytes 1966088 | tf_op jit(solution)/shard_map/ppermute | solution.py:237
  37.7 11.9 %collective-permute-start.6 = (bf16[640,512]{1,0:T(8,128)(2,1)S(1)}, bf16[640,512]{1,0:T(8,128)(2,1)S(1)}, u32[]{:S(2)}, u32[]{:S(2)}) collective-permute-start(bf16[640,512]{1,0:T(8,128)(2,1)S(1)} %constant_dynamic-update-slice_fusion.refs_0_), channel_id=1, source_target_pairs={{0,2},{2,4},{4,6},{6,0},{32,38},{34,32},{36,34},{38,36},{1,3},{3,5... | collective-permute-start | bytes 1966088 | tf_op jit(solution)/shard_map/ppermute | solution.py:237
  39.3 12.0 %collective-permute-start.5 = (bf16[3,192,512]{2,1,0:T(8,128)(2,1)S(1)}, bf16[3,192,512]{2,1,0:T(8,128)(2,1)S(1)}, u32[]{:S(2)}, u32[]{:S(2)}) collective-permute-start(bf16[3,192,512]{2,1,0:T(8,128)(2,1)S(1)} %broadcast_select_fusion.refs_4_), channel_id=1, source_target_pairs={{0,192},{64,0},{128,64},{192,128},{32,96},{96,160},{160,224},{224,... | collective-permute-start | bytes 1769480 | tf_op jit(solution)/shard_map/ppermute | solution.py:236
  40.5 14.0 %collective-permute-start.9 = (bf16[3,192,512]{2,1,0:T(8,128)(2,1)S(1)}, bf16[3,192,512]{2,1,0:T(8,128)(2,1)S(1)}, u32[]{:S(2)}, u32[]{:S(2)}) collective-permute-start(bf16[3,192,512]{2,1,0:T(8,128)(2,1)S(1)} %collective-permute-done.4.refs_5_), channel_id=1, source_target_pairs={{0,64},{64,128},{128,192},{192,0},{32,224},{96,32},{160,96},{224,1... | collective-permute-start | bytes 1769480 | tf_op jit(solution)/shard_map/ppermute | solution.py:236
  49.7 11.9 %copy-start.3 = (bf16[640,512]{1,0:T(8,128)(2,1)}, bf16[640,512]{1,0:T(8,128)(2,1)S(1)}, u32[]{:S(2)}) copy-start(bf16[640,512]{1,0:T(8,128)(2,1)S(1)} %collective-permute-done.7.refs_3_) | copy-start | bytes 1966084
  49.7 11.9 %copy-start = (bf16[640,512]{1,0:T(8,128)(2,1)}, bf16[640,512]{1,0:T(8,128)(2,1)S(1)}, u32[]{:S(2)}) copy-start(bf16[640,512]{1,0:T(8,128)(2,1)S(1)} %collective-permute-done.6.refs_1_) | copy-start | bytes 1966084
  51.3 10.2 %collective-permute-start.8 = (bf16[640,512]{1,0:T(8,128)(2,1)S(1)}, bf16[640,512]{1,0:T(8,128)(2,1)S(1)}, u32[]{:S(2)}, u32[]{:S(2)}) collective-permute-start(bf16[640,512]{1,0:T(8,128)(2,1)S(1)} %collective-permute-done.6.refs_1_), channel_id=1, source_target_pairs={{0,2},{2,4},{4,6},{6,0},{32,38},{34,32},{36,34},{38,36},{1,3},{3,5... | collective-permute-start | bytes 1966088 | tf_op jit(solution)/shard_map/ppermute | solution.py:237
  54.0 2.0 %collective-permute-start.10 = (bf16[3,192,512]{2,1,0:T(8,128)(2,1)S(1)}, bf16[3,192,512]{2,1,0:T(8,128)(2,1)S(1)}, u32[]{:S(2)}, u32[]{:S(2)}) collective-permute-start(bf16[3,192,512]{2,1,0:T(8,128)(2,1)S(1)} %broadcast_select_fusion.refs_4_), channel_id=1, source_target_pairs={{0,32},{32,0},{1,33},{33,1},{2,34},{34,2},{3,35},{35,3},{4,36},{36... | collective-permute-start | bytes 1769480 | tf_op jit(solution)/shard_map/ppermute | solution.py:241
  54.0 2.8 %collective-permute-start.13 = (bf16[3,192,512]{2,1,0:T(8,128)(2,1)S(1)}, bf16[3,192,512]{2,1,0:T(8,128)(2,1)S(1)}, u32[]{:S(2)}, u32[]{:S(2)}) collective-permute-start(bf16[3,192,512]{2,1,0:T(8,128)(2,1)S(1)} %collective-permute-done.4.refs_5_), channel_id=1, source_target_pairs={{0,32},{32,0},{1,33},{33,1},{2,34},{34,2},{3,35},{35,3},{4,36},{36... | collective-permute-start | bytes 1769480 | tf_op jit(solution)/shard_map/ppermute | solution.py:241
  54.5 3.2 %collective-permute-start.11 = (bf16[3,192,512]{2,1,0:T(8,128)(2,1)S(1)}, bf16[3,192,512]{2,1,0:T(8,128)(2,1)S(1)}, u32[]{:S(2)}, u32[]{:S(2)}) collective-permute-start(bf16[3,192,512]{2,1,0:T(8,128)(2,1)S(1)} %collective-permute-done.5.refs_7_), channel_id=1, source_target_pairs={{0,32},{32,0},{1,33},{33,1},{2,34},{34,2},{3,35},{35,3},{4,36},{36... | collective-permute-start | bytes 1769480 | tf_op jit(solution)/shard_map/ppermute | solution.py:241
  54.5 7.0 %collective-permute-start.12 = (bf16[3,192,512]{2,1,0:T(8,128)(2,1)S(1)}, bf16[3,192,512]{2,1,0:T(8,128)(2,1)S(1)}, u32[]{:S(2)}, u32[]{:S(2)}) collective-permute-start(bf16[3,192,512]{2,1,0:T(8,128)(2,1)S(1)} %collective-permute-done.9.refs_6_), channel_id=1, source_target_pairs={{0,32},{32,0},{1,33},{33,1},{2,34},{34,2},{3,35},{35,3},{4,36},{36... | collective-permute-start | bytes 1769480 | tf_op jit(solution)/shard_map/ppermute | solution.py:241
  61.5 0.9 copy-start.4
  66.1 17.0 %collective-permute-start.14 = (bf16[320,768]{1,0:T(8,128)(2,1)S(1)}, bf16[320,768]{1,0:T(8,128)(2,1)S(1)}, u32[]{:S(2)}, u32[]{:S(2)}) collective-permute-start(bf16[320,768]{1,0:T(8,128)(2,1)S(1)} %get-tuple-element.62.pair), channel_id=1, source_target_pairs={{0,1},{1,0},{2,3},{3,2},{4,5},{5,4},{6,7},{7,6},{8,9},{9,8},{10,11... | collective-permute-start | bytes 1474568 | tf_op jit(solution)/shard_map/ppermute | solution.py:241
  69.5 13.7 %collective-permute-start.15 = (bf16[320,384]{1,0:T(8,128)(2,1)S(1)}, bf16[320,384]{1,0:T(8,128)(2,1)S(1)}, u32[]{:S(2)}, u32[]{:S(2)}) collective-permute-start(bf16[320,384]{1,0:T(8,128)(2,1)S(1)} %get-tuple-element.63.down), channel_id=1, source_target_pairs={{0,1},{1,0},{2,3},{3,2},{4,5},{5,4},{6,7},{7,6},{8,9},{9,8},{10,11... | collective-permute-start | bytes 737288 | tf_op jit(solution)/shard_map/ppermute | solution.py:241
  83.2 5.5 %copy-start.1 = (bf16[640,512]{1,0:T(8,128)(2,1)S(1)}, bf16[640,512]{1,0:T(8,128)(2,1)}, u32[]{:S(2)}) copy-start(bf16[640,512]{1,0:T(8,128)(2,1)} %copy-done) | copy-start | bytes 1966084
  87.7 0.9 copy-start.2
  88.6 9.9 %collective-permute-start.16 = (bf16[656,512]{1,0:T(8,128)(2,1)S(1)}, bf16[656,512]{1,0:T(8,128)(2,1)S(1)}, u32[]{:S(2)}, u32[]{:S(2)}) collective-permute-start(bf16[656,512]{1,0:T(8,128)(2,1)S(1)} %get-tuple-element.68), channel_id=1, source_target_pairs={{0,2},{2,4},{4,6},{6,0},{32,38},{34,32},{36,34},{38,36},{1,3},{3,5... | collective-permute-start | bytes 2015240 | tf_op jit(solution)/shard_map/ppermute | solution.py:237
  93.0 5.7 %collective-permute-start.17 = (bf16[3,192,512]{2,1,0:T(8,128)(2,1)S(1)}, bf16[3,192,512]{2,1,0:T(8,128)(2,1)S(1)}, u32[]{:S(2)}, u32[]{:S(2)}) collective-permute-start(bf16[3,192,512]{2,1,0:T(8,128)(2,1)S(1)} %get-tuple-element.73), channel_id=1, source_target_pairs={{0,32},{32,0},{1,33},{33,1},{2,34},{34,2},{3,35},{35,3},{4,36},{36... | collective-permute-start | bytes 1769480 | tf_op jit(solution)/shard_map/ppermute | solution.py:241
  93.1 5.6 %collective-permute-start.18 = (bf16[3,192,512]{2,1,0:T(8,128)(2,1)S(1)}, bf16[3,192,512]{2,1,0:T(8,128)(2,1)S(1)}, u32[]{:S(2)}, u32[]{:S(2)}) collective-permute-start(bf16[3,192,512]{2,1,0:T(8,128)(2,1)S(1)} %get-tuple-element.74), channel_id=1, source_target_pairs={{0,32},{32,0},{1,33},{33,1},{2,34},{34,2},{3,35},{35,3},{4,36},{36... | collective-permute-start | bytes 1769480 | tf_op jit(solution)/shard_map/ppermute | solution.py:241
  93.6 5.1 %collective-permute-start.19 = (bf16[3,192,512]{2,1,0:T(8,128)(2,1)S(1)}, bf16[3,192,512]{2,1,0:T(8,128)(2,1)S(1)}, u32[]{:S(2)}, u32[]{:S(2)}) collective-permute-start(bf16[3,192,512]{2,1,0:T(8,128)(2,1)S(1)} %get-tuple-element.75), channel_id=1, source_target_pairs={{0,32},{32,0},{1,33},{33,1},{2,34},{34,2},{3,35},{35,3},{4,36},{36... | collective-permute-start | bytes 1769480 | tf_op jit(solution)/shard_map/ppermute | solution.py:241
  93.7 5.0 %collective-permute-start.20 = (bf16[3,192,512]{2,1,0:T(8,128)(2,1)S(1)}, bf16[3,192,512]{2,1,0:T(8,128)(2,1)S(1)}, u32[]{:S(2)}, u32[]{:S(2)}) collective-permute-start(bf16[3,192,512]{2,1,0:T(8,128)(2,1)S(1)} %get-tuple-element.76), channel_id=1, source_target_pairs={{0,32},{32,0},{1,33},{33,1},{2,34},{34,2},{3,35},{35,3},{4,36},{36... | collective-permute-start | bytes 1769480 | tf_op jit(solution)/shard_map/ppermute | solution.py:241
  98.9 12.1 %collective-permute-start.22 = (bf16[3,192,512]{2,1,0:T(8,128)(2,1)S(1)}, bf16[3,192,512]{2,1,0:T(8,128)(2,1)S(1)}, u32[]{:S(2)}, u32[]{:S(2)}) collective-permute-start(bf16[3,192,512]{2,1,0:T(8,128)(2,1)S(1)} %add_convert_fusion.3), channel_id=1, source_target_pairs={{0,64},{64,128},{128,192},{192,0},{32,224},{96,32},{160,96},{224,1... | collective-permute-start | bytes 1769480 | tf_op jit(solution)/shard_map/ppermute | solution.py:236
  101.4 21.6 %collective-permute-start.21 = (bf16[3,192,512]{2,1,0:T(8,128)(2,1)S(1)}, bf16[3,192,512]{2,1,0:T(8,128)(2,1)S(1)}, u32[]{:S(2)}, u32[]{:S(2)}) collective-permute-start(bf16[3,192,512]{2,1,0:T(8,128)(2,1)S(1)} %add_convert_fusion.4), channel_id=1, source_target_pairs={{0,192},{64,0},{128,64},{192,128},{32,96},{96,160},{160,224},{224,... | collective-permute-start | bytes 1769480 | tf_op jit(solution)/shard_map/ppermute | solution.py:236
  101.5 15.0 %collective-permute-start.26 = (bf16[656,512]{1,0:T(8,128)(2,1)S(1)}, bf16[656,512]{1,0:T(8,128)(2,1)S(1)}, u32[]{:S(2)}, u32[]{:S(2)}) collective-permute-start(bf16[656,512]{1,0:T(8,128)(2,1)S(1)} %get-tuple-element.86), channel_id=1, source_target_pairs={{0,6},{2,0},{4,2},{6,4},{32,34},{34,36},{36,38},{38,32},{1,7},{3,1... | collective-permute-start | bytes 2015240 | tf_op jit(solution)/shard_map/ppermute | solution.py:237
  101.6 17.2 %collective-permute-start.27 = (bf16[656,512]{1,0:T(8,128)(2,1)S(1)}, bf16[656,512]{1,0:T(8,128)(2,1)S(1)}, u32[]{:S(2)}, u32[]{:S(2)}) collective-permute-start(bf16[656,512]{1,0:T(8,128)(2,1)S(1)} %add_convert_fusion), channel_id=1, source_target_pairs={{0,2},{2,4},{4,6},{6,0},{32,38},{34,32},{36,34},{38,36},{1,3},{3,5... | collective-permute-start | bytes 2015240 | tf_op jit(solution)/shard_map/ppermute | solution.py:237
  111.3 11.7 %collective-permute-start.23 = (bf16[3,192,512]{2,1,0:T(8,128)(2,1)S(1)}, bf16[3,192,512]{2,1,0:T(8,128)(2,1)S(1)}, u32[]{:S(2)}, u32[]{:S(2)}) collective-permute-start(bf16[3,192,512]{2,1,0:T(8,128)(2,1)S(1)} %add_convert_fusion.2), channel_id=1, source_target_pairs={{0,64},{64,128},{128,192},{192,0},{32,224},{96,32},{160,96},{224,1... | collective-permute-start | bytes 1769480 | tf_op jit(solution)/shard_map/ppermute | solution.py:236
  119.6 14.5 %collective-permute-start.28 = (bf16[176,512]{1,0:T(8,128)(2,1)S(1)}, bf16[176,512]{1,0:T(8,128)(2,1)S(1)}, u32[]{:S(2)}, u32[]{:S(2)}) collective-permute-start(bf16[176,512]{1,0:T(8,128)(2,1)S(1)} %get-tuple-element.89), channel_id=1, source_target_pairs={{0,24},{8,0},{16,8},{24,16},{1,25},{9,1},{17,9},{25,17},{2,26},{10... | collective-permute-start | bytes 540680 | tf_op jit(solution)/shard_map/ppermute | solution.py:230
  120.7 13.4 %collective-permute-start.29 = (bf16[176,512]{1,0:T(8,128)(2,1)S(1)}, bf16[176,512]{1,0:T(8,128)(2,1)S(1)}, u32[]{:S(2)}, u32[]{:S(2)}) collective-permute-start(bf16[176,512]{1,0:T(8,128)(2,1)S(1)} %get-tuple-element.90), channel_id=1, source_target_pairs={{0,16},{8,24},{16,0},{24,8},{1,17},{9,25},{17,1},{25,9},{2,18},{10... | collective-permute-start | bytes 540680 | tf_op jit(solution)/shard_map/ppermute | solution.py:230
  120.7 20.8 %collective-permute-start.30 = (bf16[176,512]{1,0:T(8,128)(2,1)S(1)}, bf16[176,512]{1,0:T(8,128)(2,1)S(1)}, u32[]{:S(2)}, u32[]{:S(2)}) collective-permute-start(bf16[176,512]{1,0:T(8,128)(2,1)S(1)} %get-tuple-element.91), channel_id=1, source_target_pairs={{0,8},{8,16},{16,24},{24,0},{1,9},{9,17},{17,25},{25,1},{2,10},{10... | collective-permute-start | bytes 540680 | tf_op jit(solution)/shard_map/ppermute | solution.py:230
  123.4 20.4 %collective-permute-start.25 = (bf16[288,512]{1,0:T(8,128)(2,1)S(1)}, bf16[288,512]{1,0:T(8,128)(2,1)S(1)}, u32[]{:S(2)}, u32[]{:S(2)}) collective-permute-start(bf16[288,512]{1,0:T(8,128)(2,1)S(1)} %get-tuple-element.98), channel_id=1, source_target_pairs={{0,0},{1,32},{32,1},{33,33},{2,2},{3,34},{34,3},{35,35},{4,4},{5,3... | collective-permute-start | bytes 884744 | tf_op jit(solution)/shard_map/ppermute | solution.py:245
  132.2 12.0 %collective-permute-start.24 = (bf16[288,512]{1,0:T(8,128)(2,1)S(1)}, bf16[288,512]{1,0:T(8,128)(2,1)S(1)}, u32[]{:S(2)}, u32[]{:S(2)}) collective-permute-start(bf16[288,512]{1,0:T(8,128)(2,1)S(1)} %get-tuple-element.99), channel_id=1, source_target_pairs={{0,0},{1,32},{32,1},{33,33},{2,2},{3,34},{34,3},{35,35},{4,4},{5,3... | collective-permute-start | bytes 884744 | tf_op jit(solution)/shard_map/ppermute | solution.py:245
